TPU v7x, 32 devices: a whole 2x2x4 slice. The times are simulated.
32 devices in a mesh: batch: 2 (over x), space: 16 (over z, y, core).
Axes of the slice: x: 2, y: 2, z: 4, core: 2. Of those that a mesh axis runs over, the one named last changes fastest.
Arguments:
- snapshots: bfloat16 [2, 64, 32, 1024], P('batch', None, 'space'), may hold values from -6 to 6
- cotangent: bfloat16 [2, 64, 32, 1024], P('batch', None, 'space'), may hold values from -6 to 6
- mode_weight: bfloat16 [16, 16, 24, 64, 64], P('batch', 'space'), may hold values from -0.75 to 0.75
- conv_weight: bfloat16 [3, 3, 3, 64, 64], replicated, may hold values from -0.15625 to 0.15625
Outputs:
- activated: bfloat16 [2, 64, 32, 1024], P('batch', None, 'space')
- input_gradient: bfloat16 [2, 64, 32, 1024], P('batch', None, 'space')
- mode_gradient: float32 [16, 16, 24, 64, 64], P('batch', 'space')
- conv_gradient: float32 [3, 3, 3, 64, 64], replicated
All inputs are finite; a program needn't handle non-finite values.
Results may differ from a plain program's by a relative error of at most 0.02.
Values may be sent and summed in bfloat16 or wider, within the bound.
No kernel may reach another device: no remote copies, remote signals or barrier semaphores. Data moves between devices by JAX's collectives and lax.ppermute only.
A program may use at most 128 MiB of HBM per device.

v0:
```python
import math

import jax
import jax.numpy as jnp
from jax import lax
from jax.sharding import PartitionSpec as P

KX = 8
KY = 8
KZ = 12
NX = 32
NY = 32


inv_root_two = 1.0 / math.sqrt(2.0)
inv_root_two_pi = 1.0 / math.sqrt(2.0 * math.pi)


def extended_2(cells, sides, width):
    for axis, dim in sides:
        count = lax.axis_size(axis)
        ends = count - 1
        head = lax.slice_in_dim(cells, 0, width, axis=dim)
        tail = lax.slice_in_dim(cells, cells.shape[dim] - width, cells.shape[dim], axis=dim)
        cells = jnp.concatenate(
            [
                lax.ppermute(tail, axis, [(i, (i + 1) % count) for i in range(ends)]),
                cells,
                lax.ppermute(head, axis, [((i + 1) % count, i) for i in range(ends)]),
            ],
            axis=dim,
        )
    return cells


def basis_rows(half_count, length):
    row_index = lax.broadcasted_iota(jnp.int32, (2 * half_count, length), 0)
    cell_index = lax.broadcasted_iota(jnp.int32, (2 * half_count, length), 1)
    frequency = jnp.where(row_index < half_count, row_index, row_index - half_count + 1)
    phases = (frequency * cell_index % length).astype(jnp.float32) * (2.0 * math.pi / length)
    return jnp.where(row_index < half_count, jnp.cos(phases), jnp.sin(phases))


def make_tables(count_x, count_y, count_z, length_x, length_y, length_z):
    across = basis_rows(count_x, length_x)
    along_y = basis_rows(count_y, length_y)
    depth_rows = basis_rows(count_z, length_z)
    modes_x = 2 * count_x
    modes_y = 2 * count_y
    outer_table = (across[:, None, :, None] * along_y[None, :, None, :]).reshape(
        modes_x * modes_y, length_x * length_y
    )
    plane_analysis = (outer_table * (2.0 / math.sqrt(length_x * length_y))).astype(jnp.bfloat16)
    plane_synthesis = (outer_table.T * (2.0 / math.sqrt(modes_x * modes_y))).astype(jnp.bfloat16)
    depth_analysis = (depth_rows * math.sqrt(2.0 / length_z)).astype(jnp.bfloat16)
    depth_synthesis = (depth_rows.T * math.sqrt(2.0 / (2 * count_z))).astype(jnp.bfloat16)
    return (plane_analysis, plane_synthesis, depth_analysis, depth_synthesis)


def rim(values):
    return extended_2(values, (("space", 1),), 1)


def widen(values):
    channels, depth_cells, plane = values.shape
    extended = rim(values)
    return jnp.pad(
        extended.reshape(channels, depth_cells + 2, NX, NY), ((0, 0), (0, 0), (1, 1), (1, 1))
    )


def to_pencils(values):
    return lax.all_to_all(values, "space", split_axis=3, concat_axis=1, tiled=True)


def to_slabs(values):
    return lax.all_to_all(values, "space", split_axis=1, concat_axis=3, tiled=True)


def stacked_window(padded, offset_x, offset_y):
    channels = padded.shape[0]
    depth_cells = padded.shape[1] - 2
    window = padded[:, :, offset_x : offset_x + NX, offset_y : offset_y + NY]
    stacked = jnp.stack([window[:, offset_z : offset_z + depth_cells] for offset_z in range(3)], 0)
    return stacked.reshape(3, channels, depth_cells * NX * NY)


def stencil(padded, kernel):
    depth_cells = padded.shape[1] - 2
    summed = jnp.zeros((kernel.shape[4], depth_cells * NX * NY), jnp.float32)
    for offset_x in range(3):
        for offset_y in range(3):
            stacked = stacked_window(padded, offset_x, offset_y)
            summed = summed + lax.dot_general(
                kernel[:, offset_x, offset_y],
                stacked,
                (((0, 1), (0, 1)), ((), ())),
                preferred_element_type=jnp.float32,
            )
    return summed


def kernel_terms(padded, pre_flat):
    pieces = []
    for offset_x in range(3):
        row_pieces = []
        for offset_y in range(3):
            stacked = stacked_window(padded, offset_x, offset_y)
            row_pieces.append(
                lax.dot_general(
                    stacked, pre_flat, (((2,), (1,)), ((), ())), preferred_element_type=jnp.float32
                )
            )
        pieces.append(jnp.stack(row_pieces, 1))
    return jnp.stack(pieces, 1)


def shards(snapshots, cotangent, mode_weight, conv_weight):
    local_field = snapshots[0]
    channels, depth_cells, plane = local_field.shape
    total_depth = depth_cells * lax.axis_size("space")
    modes_x = 2 * KX
    modes_y = 2 * KY
    plane_analysis, plane_synthesis, depth_analysis, depth_synthesis = make_tables(
        KX, KY, KZ, NX, NY, total_depth
    )
    padded = widen(local_field)
    plane_coef = lax.dot_general(
        local_field.reshape(channels * depth_cells, plane),
        plane_analysis,
        (((1,), (1,)), ((), ())),
        preferred_element_type=jnp.float32,
    )
    plane_coef = plane_coef.astype(jnp.bfloat16).reshape(channels, depth_cells, modes_x, modes_y)
    coef = jnp.einsum(
        "czxy,pz->cpxy", to_pencils(plane_coef), depth_analysis, preferred_element_type=jnp.float32
    ).astype(jnp.bfloat16)
    full_weight = lax.all_gather(mode_weight, "batch", axis=0, tiled=True)
    mixed = jnp.einsum(
        "ipxy,xypio->opxy", coef, full_weight, preferred_element_type=jnp.float32
    ).astype(jnp.bfloat16)
    depth_back = jnp.einsum(
        "opxy,zp->ozxy", mixed, depth_synthesis, preferred_element_type=jnp.float32
    ).astype(jnp.bfloat16)
    slab_back = to_slabs(depth_back)
    spectral = lax.dot_general(
        slab_back.reshape(channels * depth_cells, modes_x * modes_y),
        plane_synthesis,
        (((1,), (1,)), ((), ())),
        preferred_element_type=jnp.float32,
    )
    pre = spectral.reshape(channels, depth_cells * plane) + stencil(padded, conv_weight)
    normal_cdf = 0.5 * (1.0 + lax.erf(pre * inv_root_two))
    density = jnp.exp(-0.5 * pre * pre) * inv_root_two_pi
    activated = (pre * normal_cdf).astype(jnp.bfloat16).reshape(channels, depth_cells, plane)
    pre_grad = (
        cotangent[0].reshape(channels, depth_cells * plane).astype(jnp.float32)
        * (normal_cdf + pre * density)
    ).astype(jnp.bfloat16)
    back_plane = jnp.dot(
        pre_grad.reshape(channels * depth_cells, plane),
        plane_synthesis,
        preferred_element_type=jnp.float32,
    )
    back_plane = back_plane.astype(jnp.bfloat16).reshape(channels, depth_cells, modes_x, modes_y)
    mixed_grad = jnp.einsum(
        "ozxy,zp->opxy", to_pencils(back_plane), depth_synthesis, preferred_element_type=jnp.float32
    ).astype(jnp.bfloat16)
    coef_grad = jnp.einsum(
        "opxy,xypio->ipxy", mixed_grad, full_weight, preferred_element_type=jnp.float32
    ).astype(jnp.bfloat16)
    mode_gradient = lax.psum_scatter(
        jnp.einsum("ipxy,opxy->xypio", coef, mixed_grad, preferred_element_type=jnp.float32).astype(
            jnp.bfloat16
        ),
        "batch",
        scatter_dimension=0,
        tiled=True,
    ).astype(jnp.float32)
    depth_grad = jnp.einsum(
        "ipxy,pz->izxy", coef_grad, depth_analysis, preferred_element_type=jnp.float32
    ).astype(jnp.bfloat16)
    slab_grad = to_slabs(depth_grad)
    spectral_grad = jnp.dot(
        slab_grad.reshape(channels * depth_cells, modes_x * modes_y),
        plane_analysis,
        preferred_element_type=jnp.float32,
    )
    flipped = jnp.transpose(conv_weight[::-1, ::-1, ::-1], (0, 1, 2, 4, 3))
    local_grad = stencil(widen(pre_grad.reshape(channels, depth_cells, plane)), flipped)
    input_gradient = (
        (spectral_grad.reshape(channels, depth_cells * plane) + local_grad)
        .astype(jnp.bfloat16)
        .reshape(channels, depth_cells, plane)
    )
    kernel_local = kernel_terms(padded, pre_grad)
    kernel_total = lax.psum(kernel_local, ("batch", "space"))
    conv_gradient = kernel_total / math.sqrt(lax.axis_size("batch") * total_depth * plane)
    return (activated[None], input_gradient[None], mode_gradient, conv_gradient)


def solution(mesh):
    in_specs = (
        P("batch", None, "space", None),
        P("batch", None, "space", None),
        P("batch", "space", None, None, None),
        P(),
    )
    out_specs = (
        P("batch", None, "space", None),
        P("batch", None, "space", None),
        P("batch", "space", None, None, None),
        P(),
    )
    return jax.shard_map(shards, mesh=mesh, in_specs=in_specs, out_specs=out_specs, check_vma=False)
```

profile of v0, /device:TPU:0, one launch (start us, length us, event | category | flops | bytes accessed | tf_op | source)
XLA Modules:
  0.0 361.3 jit_solution(15835471398676052375)
XLA Ops:
  9.3 3.1 collective-permute-start
  12.4 1.3 collective-permute-start.1
  14.6 2.1 fusion.6
  16.7 3.6 convert_element_type.165
  20.3 1.3 fusion.34
  22.9 1.8 copy.99
  25.4 8.9 %all-to-all-start = ((bf16[16,2,1024]{2,1,0:T(2,128)(2,1)}), bf16[16,2,1024]{2,1,0:T(2,128)(2,1)S(1)}, u32[]{:S(2)}, u32[]{:S(2)}) async-start(bf16[16,2,1024]{2,1,0:T(2,128)(2,1)} %reshape.401), calls=%async_computation | async-start | bytes 131072 | tf_op jit(solution)/shard_map/all_to_all | solution.py:73
  35.2 1.8 copy.190
  37.0 2.9 convert_element_type.178
  39.9 1.3 all-to-all-done
  45.4 1.6 select_maximum_fusion.2
  47.0 1.5 fusion.196
  48.5 1.9 copy.109
  50.4 1.9 copy.107
  54.2 3.9 %fusion.195 = (bf16[64,2,32,32]{0,3,2,1:T(8,128)(2,1)}, bf16[64,2,32,32]{0,3,2,1:T(8,128)(2,1)S(1)}, bf16[64,2,32,32]{0,3,2,1:T(8,128)(2,1)}, bf16[64,2,32,32]{0...) fusion(bf16[64,4,34,34]{0,3,2,1:T(8,128)(2,1)S(1)} %select_maxi, ...), kind=kLoop, calls=%fused_computation.284 | loop fusion | bytes 9961472 | tf_op jit(solution)/shard_map/slice | solution.py:84
  58.1 2.0 copy.134
  60.1 1.9 copy.133
  62.0 1.9 copy.132
  64.0 1.9 copy.130
  65.9 1.9 copy.129
  67.8 1.9 copy.128
  71.6 2.0 copy.124
  73.5 1.9 copy.119
  75.5 2.0 copy.118
  77.4 1.9 copy.117
  79.4 1.9 copy.115
  81.3 1.9 copy.114
  86.0 1.4 convolution_bitcast_fusion.17
  87.5 1.5 fusion.19
  92.7 4.5 %fusion.3 = bf16[24,16,1,64]{3,2,1,0:T(2,128)(2,1)S(1)} fusion(bf16[64,24,16,1]{0,1,2,3:T(8,128)(2,1)S(1)} %bitcast.458, bf16[16,1,24,64,64]{4,3,2,1,0:T(8,128)(2,1)} %all-gather.2.cloned.1.call-done), kind=kOutput, calls=%fused_computation.6 | convolution fusion | flops 3145728 | bytes 3244032 | tf_op jit(solution)/shard_map/ipxy,xypio->opxy/dot_general | solution.py:139
  98.4 5.9 %all-to-all-start.1 = ((bf16[16,2,1024]{2,1,0:T(2,128)(2,1)}), bf16[16,2,1024]{2,1,0:T(2,128)(2,1)}, u32[]{:S(2)}, u32[]{:S(2)}) async-start(bf16[16,2,1024]{2,1,0:T(2,128)(2,1)} %reshape.403), calls=%async_computation.1 | async-start | bytes 131072 | tf_op jit(solution)/shard_map/all_to_all | solution.py:77
  104.3 2.5 fusion.13
  109.5 1.7 all-to-all-done.1
  113.9 2.6 fusion.85
  116.5 2.1 convolution_bitcast_fusion.25
  128.6 4.4 %all-to-all-start.2 = ((bf16[16,2,1024]{2,1,0:T(2,128)(2,1)}), bf16[16,2,1024]{2,1,0:T(2,128)(2,1)S(1)}, u32[]{:S(2)}, u32[]{:S(2)}) async-start(bf16[16,2,1024]{2,1,0:T(2,128)(2,1)} %reshape.405), calls=%async_computation.2 | async-start | bytes 131072 | tf_op jit(solution)/shard_map/all_to_all | solution.py:73
  134.3 5.6 %all-to-all-done.2 = bf16[16,2,1024]{2,1,0:T(2,128)(2,1)S(1)} async-done(((bf16[16,2,1024]{2,1,0:T(2,128)(2,1)}), bf16[16,2,1024]{2,1,0:T(2,128)(2,1)S(1)}, u32[]{:S(2)}, u32[]{:S(2)}) %all-to-all-start.2) | async-done | bytes 65568 | tf_op jit(solution)/shard_map/all_to_all | solution.py:73
  140.5 5.6 %fusion = bf16[16,1,24,64,64]{4,3,2,1,0:T(8,128)(2,1)} fusion(f32[16,24,64]{2,1,0:T(8,128)S(1)} %get-tuple-element.76, f32[16,24,64]{2,1,0:T(8,128)S(1)} %get-tuple-element.77), kind=kLoop, calls=%fused_computation.1 | loop fusion | flops 3145728 | bytes 3342336 | tf_op jit(solution)/shard_map/convert_element_type | solution.py:173
  149.1 1.5 collective-permute-start.2
  150.6 1.3 collective-permute-start.3
  151.9 6.2 %fusion.1 = bf16[24,16,1,64]{3,2,1,0:T(2,128)(2,1)S(1)} fusion(bf16[64,24,16,1]{0,1,2,3:T(8,128)(2,1)S(1)} %bitcast.459, bf16[16,1,24,64,64]{4,3,2,1,0:T(8,128)(2,1)} %all-gather.2.cloned.1.call-done), kind=kOutput, calls=%fused_computation.4 | convolution fusion | flops 3145728 | bytes 3244032 | tf_op jit(solution)/shard_map/opxy,xypio->ipxy/dot_general | solution.py:169
  159.3 5.9 %all-to-all-start.3 = ((bf16[16,2,1024]{2,1,0:T(2,128)(2,1)}), bf16[16,2,1024]{2,1,0:T(2,128)(2,1)S(1)}, u32[]{:S(2)}, u32[]{:S(2)}) async-start(bf16[16,2,1024]{2,1,0:T(2,128)(2,1)} %reshape.407), calls=%async_computation.3 | async-start | bytes 131072 | tf_op jit(solution)/shard_map/all_to_all | solution.py:77
  167.3 1.6 select_maximum_fusion
  168.9 1.5 fusion.194
  170.3 1.9 copy.148
  172.2 1.9 copy.152
  176.9 3.8 %fusion.193 = (bf16[64,2,32,32]{0,3,2,1:T(8,128)(2,1)}, bf16[64,2,32,32]{0,3,2,1:T(8,128)(2,1)}, bf16[64,2,32,32]{0,3,2,1:T(8,128)(2,1)}, bf16[64,2,32,32]{0,3,2...) fusion(bf16[64,4,34,34]{0,3,2,1:T(8,128)(2,1)S(1)} %select_maxi, ...), kind=kLoop, calls=%fused_computation.282 | loop fusion | bytes 9961472 | tf_op jit(solution)/shard_map/slice | solution.py:84
  180.8 1.3 copy.147
  182.1 1.9 copy.172
  184.0 1.9 copy.171
  185.9 1.9 copy.170
  187.9 1.9 copy.169
  189.8 1.9 copy.168
  193.6 2.0 copy.165
  195.6 1.9 copy.164
  197.5 1.9 copy.163
  199.4 2.0 copy.162
  201.4 2.0 copy.159
  203.3 1.9 copy.158
  209.8 2.2 convolution_bitcast_fusion.4
  219.9 49.5 %all-reduce.4.cloned.1.call-done = f32[3,3,3,64,64]{4,3,0,2,1:T(8,128)} async-done(((f32[3,3,3,64,64]{4,3,0,2,1:T(8,128)}), f32[3,3,3,64,64]{4,3,0,2,1:T(8,128)}) %all-reduce.4.cloned.1.call-update) | async-done | bytes 442384 | tf_op jit(solution)/shard_map/psum | solution.py:197
  273.5 2.4 fusion.30
  276.8 72.1 %reduce-scatter.2.cloned.1.call-done = bf16[8,1,24,64,64]{4,3,2,1,0:T(8,128)(2,1)} async-done(((bf16[16,1,24,64,64]{4,3,2,1,0:T(8,128)(2,1)}), bf16[8,1,24,64,64]{4,3,2,1,0:T(8,128)(2,1)}) %reduce-scatter.2.cloned.1.call-update) | async-done | bytes 1572880 | tf_op jit(solution)/shard_map/reduce_scatter | solution.py:172
  349.0 5.3 %convert_element_type.196 = f32[8,1,24,64,64]{4,3,2,1,0:T(8,128)} convert(bf16[8,1,24,64,64]{4,3,2,1,0:T(8,128)(2,1)} %reduce-scatter.2.cloned.1.call-done) | non-fusion elementwise | flops 786432 | bytes 4718592 | tf_op jit(solution)/shard_map/convert_element_type | solution.py:179
  (299 shorter events, 66.2 us)
Async XLA Ops:
  7.2 85.5 %all-gather.2.cloned.1.call-start = ((), (), s32[]{:S(2)}) async-start(), calls=%async_computation.5 | async-start | bytes 9437184 | tf_op jit(solution)/shard_map/all_gather | solution.py:138
  9.3 33.1 %collective-permute-start = (bf16[64,1,1024]{0,2,1:T(8,128)(2,1)}, bf16[64,1,1024]{0,2,1:T(8,128)(2,1)}, u32[]{:S(2)}, u32[]{:S(2)}) collective-permute-start(bf16[64,1,1024]{0,2,1:T(8,128)(2,1)} %get-tuple-element.72), channel_id=1, source_target_pairs={{0,1},{1,2},{2,3},{3,4},{4,5},{5,6},{6,7},{7,8},{8,9},{9,10},{10,1... | collective-permute-start | bytes 393224 | tf_op jit(solution)/shard_map/ppermute | solution.py:27
  12.4 30.0 %collective-permute-start.1 = (bf16[64,1,1024]{0,2,1:T(8,128)(2,1)}, bf16[64,1,1024]{0,2,1:T(8,128)(2,1)}, u32[]{:S(2)}, u32[]{:S(2)}) collective-permute-start(bf16[64,1,1024]{0,2,1:T(8,128)(2,1)} %get-tuple-element.73), channel_id=1, source_target_pairs={{1,0},{2,1},{3,2},{4,3},{5,4},{6,5},{7,6},{8,7},{9,8},{10,9},{11,1... | collective-permute-start | bytes 393224 | tf_op jit(solution)/shard_map/ppermute | solution.py:29
  25.4 15.7 %all-to-all-start = ((bf16[16,2,1024]{2,1,0:T(2,128)(2,1)}), bf16[16,2,1024]{2,1,0:T(2,128)(2,1)S(1)}, u32[]{:S(2)}, u32[]{:S(2)}) async-start(bf16[16,2,1024]{2,1,0:T(2,128)(2,1)} %reshape.401), calls=%async_computation | async-start | bytes 131072 | tf_op jit(solution)/shard_map/all_to_all | solution.py:73
  58.1 11.7 %copy-start.9 = (bf16[64,2,32,32]{0,3,2,1:T(8,128)(2,1)S(1)}, bf16[64,2,32,32]{0,3,2,1:T(8,128)(2,1)}, u32[]{:S(2)}) copy-start(bf16[64,2,32,32]{0,3,2,1:T(8,128)(2,1)} %get-tuple-element.48) | copy-start | bytes 786436
  58.1 12.6 %copy-start.7 = (bf16[64,2,32,32]{0,3,2,1:T(8,128)(2,1)S(1)}, bf16[64,2,32,32]{0,3,2,1:T(8,128)(2,1)}, u32[]{:S(2)}) copy-start(bf16[64,2,32,32]{0,3,2,1:T(8,128)(2,1)} %get-tuple-element.49) | copy-start | bytes 786436
  70.7 12.6 %copy-start.5 = (bf16[64,2,32,32]{0,3,2,1:T(8,128)(2,1)S(1)}, bf16[64,2,32,32]{0,3,2,1:T(8,128)(2,1)}, u32[]{:S(2)}) copy-start(bf16[64,2,32,32]{0,3,2,1:T(8,128)(2,1)} %get-tuple-element.56) | copy-start | bytes 786436
  71.6 12.6 %copy-start.3 = (bf16[64,2,32,32]{0,3,2,1:T(8,128)(2,1)S(1)}, bf16[64,2,32,32]{0,3,2,1:T(8,128)(2,1)}, u32[]{:S(2)}) copy-start(bf16[64,2,32,32]{0,3,2,1:T(8,128)(2,1)} %get-tuple-element.57) | copy-start | bytes 786436
  75.5 10.5 %copy-start.23 = (bf16[1,64,2048]{2,1,0:T(8,128)(2,1)S(1)}, bf16[1,64,2048]{2,1,0:T(8,128)(2,1)}, u32[]{:S(2)}) copy-start(bf16[1,64,2048]{2,1,0:T(8,128)(2,1)} %copy.107) | copy-start | bytes 786436
  84.1 3.3 copy-start.20
  85.0 3.9 %copy-start.55 = (bf16[1,64,2048]{2,1,0:T(8,128)(2,1)S(1)}, bf16[1,64,2048]{2,1,0:T(8,128)(2,1)}, u32[]{:S(2)}) copy-start(bf16[1,64,2048]{2,1,0:T(8,128)(2,1)} %copy.115) | copy-start | bytes 786436
  85.0 3.9 %copy-start.57 = (bf16[1,64,2048]{2,1,0:T(8,128)(2,1)S(1)}, bf16[1,64,2048]{2,1,0:T(8,128)(2,1)}, u32[]{:S(2)}) copy-start(bf16[1,64,2048]{2,1,0:T(8,128)(2,1)} %copy.114) | copy-start | bytes 786436
  86.0 3.3 copy-start.49
  86.0 3.3 copy-start.51
  86.0 3.4 copy-start.53
  97.2 10.5 %copy-start.2 = (bf16[64,2,32,32]{0,3,2,1:T(8,128)(2,1)S(1)}, bf16[64,2,32,32]{0,3,2,1:T(8,128)(2,1)}, u32[]{:S(2)}) copy-start(bf16[64,2,32,32]{0,3,2,1:T(8,128)(2,1)} %get-tuple-element.40) | copy-start | bytes 786436
  98.4 12.8 %all-to-all-start.1 = ((bf16[16,2,1024]{2,1,0:T(2,128)(2,1)}), bf16[16,2,1024]{2,1,0:T(2,128)(2,1)}, u32[]{:S(2)}, u32[]{:S(2)}) async-start(bf16[16,2,1024]{2,1,0:T(2,128)(2,1)} %reshape.403), calls=%async_computation.1 | async-start | bytes 131072 | tf_op jit(solution)/shard_map/all_to_all | solution.py:77
  104.3 9.2 %copy-start = (bf16[256,1024]{1,0:T(8,128)(2,1)S(1)}, bf16[256,1024]{1,0:T(8,128)(2,1)}, u32[]{:S(2)}) copy-start(bf16[256,1024]{1,0:T(8,128)(2,1)} %convert_element_type.178) | copy-start | bytes 1572868
  107.7 6.2 %copy-start.18 = (f32[8,8,2,1024]{3,1,2,0:T(8,128)S(1)}, f32[8,8,2,1024]{3,1,2,0:T(8,128)}, u32[]{:S(2)}) copy-start(f32[8,8,2,1024]{3,1,2,0:T(8,128)} %copy.190) | copy-start | bytes 1572868
  113.9 4.7 %copy-start.56 = (bf16[1,64,2048]{2,1,0:T(8,128)(2,1)S(1)}, bf16[1,64,2048]{2,1,0:T(8,128)(2,1)}, u32[]{:S(2)}) copy-start(bf16[1,64,2048]{2,1,0:T(8,128)(2,1)} %copy.115) | copy-start | bytes 786436
  113.9 4.7 %copy-start.58 = (bf16[1,64,2048]{2,1,0:T(8,128)(2,1)S(1)}, bf16[1,64,2048]{2,1,0:T(8,128)(2,1)}, u32[]{:S(2)}) copy-start(bf16[1,64,2048]{2,1,0:T(8,128)(2,1)} %copy.114) | copy-start | bytes 786436
  113.9 4.7 %copy-start.60 = (bf16[1,64,2048]{2,1,0:T(8,128)(2,1)S(1)}, bf16[1,64,2048]{2,1,0:T(8,128)(2,1)}, u32[]{:S(2)}) copy-start(bf16[1,64,2048]{2,1,0:T(8,128)(2,1)} %copy.113) | copy-start | bytes 786436
  116.5 31.5 %copy-start.13 = (bf16[64,2048]{1,0:T(8,128)(2,1)}, bf16[64,2048]{1,0:T(8,128)(2,1)S(1)}, u32[]{:S(2)}) copy-start(bf16[64,2048]{1,0:T(8,128)(2,1)S(1)} %get-tuple-element.68) | copy-start | bytes 786436
  125.9 7.1 %copy-start.91 = (f32[3,1,64,64]{3,2,0,1:T(8,128)S(1)}, f32[3,1,64,64]{3,2,0,1:T(8,128)}, u32[]{:S(2)}) copy-start(f32[3,1,64,64]{3,2,0,1:T(8,128)} %convolution_bitcast_fusion.20) | copy-start | bytes 147460
  125.9 7.2 %copy-start.92 = (f32[3,1,64,64]{3,2,0,1:T(8,128)S(1)}, f32[3,1,64,64]{3,2,0,1:T(8,128)}, u32[]{:S(2)}) copy-start(f32[3,1,64,64]{3,2,0,1:T(8,128)} %convolution_bitcast_fusion.19) | copy-start | bytes 147460
  125.9 7.2 %copy-start.86 = (f32[3,1,64,64]{3,2,0,1:T(8,128)S(1)}, f32[3,1,64,64]{3,2,0,1:T(8,128)}, u32[]{:S(2)}) copy-start(f32[3,1,64,64]{3,2,0,1:T(8,128)} %convolution_bitcast_fusion.25) | copy-start | bytes 147460
  125.9 7.2 %copy-start.87 = (f32[3,1,64,64]{3,2,0,1:T(8,128)S(1)}, f32[3,1,64,64]{3,2,0,1:T(8,128)}, u32[]{:S(2)}) copy-start(f32[3,1,64,64]{3,2,0,1:T(8,128)} %convolution_bitcast_fusion.24) | copy-start | bytes 147460
  125.9 7.2 %copy-start.88 = (f32[3,1,64,64]{3,2,0,1:T(8,128)S(1)}, f32[3,1,64,64]{3,2,0,1:T(8,128)}, u32[]{:S(2)}) copy-start(f32[3,1,64,64]{3,2,0,1:T(8,128)} %convolution_bitcast_fusion.23) | copy-start | bytes 147460
  126.0 7.2 %copy-start.89 = (f32[3,1,64,64]{3,2,0,1:T(8,128)S(1)}, f32[3,1,64,64]{3,2,0,1:T(8,128)}, u32[]{:S(2)}) copy-start(f32[3,1,64,64]{3,2,0,1:T(8,128)} %convolution_bitcast_fusion.22) | copy-start | bytes 147460
  126.0 7.2 %copy-start.90 = (f32[3,1,64,64]{3,2,0,1:T(8,128)S(1)}, f32[3,1,64,64]{3,2,0,1:T(8,128)}, u32[]{:S(2)}) copy-start(f32[3,1,64,64]{3,2,0,1:T(8,128)} %convolution_bitcast_fusion.21) | copy-start | bytes 147460
  126.3 6.7 %copy-start.93 = (f32[3,1,64,64]{3,2,0,1:T(8,128)S(1)}, f32[3,1,64,64]{3,2,0,1:T(8,128)}, u32[]{:S(2)}) copy-start(f32[3,1,64,64]{3,2,0,1:T(8,128)} %convolution_bitcast_fusion.18) | copy-start | bytes 147460
  128.6 11.3 %all-to-all-start.2 = ((bf16[16,2,1024]{2,1,0:T(2,128)(2,1)}), bf16[16,2,1024]{2,1,0:T(2,128)(2,1)S(1)}, u32[]{:S(2)}, u32[]{:S(2)}) async-start(bf16[16,2,1024]{2,1,0:T(2,128)(2,1)} %reshape.405), calls=%async_computation.2 | async-start | bytes 131072 | tf_op jit(solution)/shard_map/all_to_all | solution.py:73
  133.0 136.4 %all-reduce.4.cloned.1.call-start = ((), (), s32[]{:S(2)}) async-start(), calls=%async_computation.7 | async-start | bytes 1769472 | tf_op jit(solution)/shard_map/psum | solution.py:197
  134.3 214.7 %reduce-scatter.2.cloned.1.call-start = ((), (), s32[]{:S(2)}) async-start(), calls=%async_computation.6 | async-start | bytes 9437184 | tf_op jit(solution)/shard_map/reduce_scatter | solution.py:172
  149.1 16.1 %collective-permute-start.2 = (bf16[64,1,1024]{0,2,1:T(8,128)(2,1)S(1)}, bf16[64,1,1024]{0,2,1:T(8,128)(2,1)S(1)}, u32[]{:S(2)}, u32[]{:S(2)}) collective-permute-start(bf16[64,1,1024]{0,2,1:T(8,128)(2,1)S(1)} %get-tuple-element.66), channel_id=1, source_target_pairs={{0,1},{1,2},{2,3},{3,4},{4,5},{5,6},{6,7},{7,8},{8,9},{9,10},{10,1... | collective-permute-start | bytes 393224 | tf_op jit(solution)/shard_map/ppermute | solution.py:27
  150.6 14.6 %collective-permute-start.3 = (bf16[64,1,1024]{0,2,1:T(8,128)(2,1)S(1)}, bf16[64,1,1024]{0,2,1:T(8,128)(2,1)S(1)}, u32[]{:S(2)}, u32[]{:S(2)}) collective-permute-start(bf16[64,1,1024]{0,2,1:T(8,128)(2,1)S(1)} %get-tuple-element.67), channel_id=1, source_target_pairs={{1,0},{2,1},{3,2},{4,3},{5,4},{6,5},{7,6},{8,7},{9,8},{10,9},{11,1... | collective-permute-start | bytes 393224 | tf_op jit(solution)/shard_map/ppermute | solution.py:29
  159.3 112.4 %all-to-all-start.3 = ((bf16[16,2,1024]{2,1,0:T(2,128)(2,1)}), bf16[16,2,1024]{2,1,0:T(2,128)(2,1)S(1)}, u32[]{:S(2)}, u32[]{:S(2)}) async-start(bf16[16,2,1024]{2,1,0:T(2,128)(2,1)} %reshape.407), calls=%async_computation.3 | async-start | bytes 131072 | tf_op jit(solution)/shard_map/all_to_all | solution.py:77
  180.7 11.0 %copy-start.10 = (bf16[64,2,32,32]{0,3,2,1:T(8,128)(2,1)S(1)}, bf16[64,2,32,32]{0,3,2,1:T(8,128)(2,1)}, u32[]{:S(2)}) copy-start(bf16[64,2,32,32]{0,3,2,1:T(8,128)(2,1)} %get-tuple-element.22) | copy-start | bytes 786436
  180.8 11.9 %copy-start.8 = (bf16[64,2,32,32]{0,3,2,1:T(8,128)(2,1)S(1)}, bf16[64,2,32,32]{0,3,2,1:T(8,128)(2,1)}, u32[]{:S(2)}) copy-start(bf16[64,2,32,32]{0,3,2,1:T(8,128)(2,1)} %get-tuple-element.23) | copy-start | bytes 786436
  192.7 12.6 %copy-start.6 = (bf16[64,2,32,32]{0,3,2,1:T(8,128)(2,1)S(1)}, bf16[64,2,32,32]{0,3,2,1:T(8,128)(2,1)}, u32[]{:S(2)}) copy-start(bf16[64,2,32,32]{0,3,2,1:T(8,128)(2,1)} %get-tuple-element.30) | copy-start | bytes 786436
  193.6 12.6 %copy-start.4 = (bf16[64,2,32,32]{0,3,2,1:T(8,128)(2,1)S(1)}, bf16[64,2,32,32]{0,3,2,1:T(8,128)(2,1)}, u32[]{:S(2)}) copy-start(bf16[64,2,32,32]{0,3,2,1:T(8,128)(2,1)} %get-tuple-element.31) | copy-start | bytes 786436
  206.2 3.6 %copy-start.14 = (bf16[64,2048]{1,0:T(8,128)(2,1)S(1)}, bf16[64,2048]{1,0:T(8,128)(2,1)}, u32[]{:S(2)}) copy-start(bf16[64,2048]{1,0:T(8,128)(2,1)} %copy-done.13) | copy-start | bytes 786436
  206.2 3.6 %copy-start.48 = (bf16[1,64,2048]{2,1,0:T(8,128)(2,1)S(1)}, bf16[1,64,2048]{2,1,0:T(8,128)(2,1)}, u32[]{:S(2)}) copy-start(bf16[1,64,2048]{2,1,0:T(8,128)(2,1)} %copy.160) | copy-start | bytes 786436
  207.1 4.9 %copy-start.17 = (bf16[3,3,3,64,64]{3,4,0,2,1:T(8,128)(2,1)S(1)}, bf16[3,3,3,64,64]{3,4,0,2,1:T(8,128)(2,1)}, u32[]{:S(2)}) copy-start(bf16[3,3,3,64,64]{3,4,0,2,1:T(8,128)(2,1)} %reverse_bitcast_fusion) | copy-start | bytes 663556
  208.0 4.0 %copy-start.61 = (bf16[1,64,2048]{2,1,0:T(8,128)(2,1)S(1)}, bf16[1,64,2048]{2,1,0:T(8,128)(2,1)}, u32[]{:S(2)}) copy-start(bf16[1,64,2048]{2,1,0:T(8,128)(2,1)} %copy.173) | copy-start | bytes 786436
  208.0 4.0 %copy-start.65 = (bf16[1,64,2048]{2,1,0:T(8,128)(2,1)S(1)}, bf16[1,64,2048]{2,1,0:T(8,128)(2,1)}, u32[]{:S(2)}) copy-start(bf16[1,64,2048]{2,1,0:T(8,128)(2,1)} %copy.172) | copy-start | bytes 786436
  208.9 4.3 %copy-start.67 = (bf16[1,64,2048]{2,1,0:T(8,128)(2,1)S(1)}, bf16[1,64,2048]{2,1,0:T(8,128)(2,1)}, u32[]{:S(2)}) copy-start(bf16[1,64,2048]{2,1,0:T(8,128)(2,1)} %copy.170) | copy-start | bytes 786436
  209.8 3.4 copy-start.68
  209.8 3.4 copy-start.69
  209.8 4.5 %copy-start.70 = (bf16[1,64,2048]{2,1,0:T(8,128)(2,1)S(1)}, bf16[1,64,2048]{2,1,0:T(8,128)(2,1)}, u32[]{:S(2)}) copy-start(bf16[1,64,2048]{2,1,0:T(8,128)(2,1)} %copy.167) | copy-start | bytes 786436
  209.8 4.5 %copy-start.71 = (bf16[1,64,2048]{2,1,0:T(8,128)(2,1)S(1)}, bf16[1,64,2048]{2,1,0:T(8,128)(2,1)}, u32[]{:S(2)}) copy-start(bf16[1,64,2048]{2,1,0:T(8,128)(2,1)} %copy.166) | copy-start | bytes 786436
  209.8 4.5 %copy-start.72 = (bf16[1,64,2048]{2,1,0:T(8,128)(2,1)S(1)}, bf16[1,64,2048]{2,1,0:T(8,128)(2,1)}, u32[]{:S(2)}) copy-start(bf16[1,64,2048]{2,1,0:T(8,128)(2,1)} %copy.165) | copy-start | bytes 786436
  212.0 3.4 copy-start.73
  212.1 3.4 copy-start.74
  212.1 3.4 copy-start.75
  213.2 3.4 copy-start.76
  213.2 3.4 copy-start.77
  213.2 3.4 copy-start.78
  214.3 3.4 copy-start.79
  214.3 3.4 copy-start.80
  214.3 3.4 copy-start.82
  215.5 3.4 copy-start.42
  215.5 3.4 copy-start.45
  215.5 3.3 copy-start.81
  (41 other events, 85.0 us)
Sparse Core Ops, SparseCore 0:
  9.5 83.0 all-gather.1
  139.7 129.6 all-reduce.3
  272.3 76.6 reduce-scatter.1
where the time goes:
time: 367 us; the launch traced here: 361 us
  waiting for transfers between devices  132 us (36%)
  local copies, waits for them, and re-layouts  115 us (31%)
  matrix products  46.9 us (13%)
  starting transfers between devices  32.3 us (9%)
  other arithmetic  20.1 us (5%)
  between operations  15.4 us (4%)
    another operation x53, local copies, waits for them, and re-layouts, stacked_window(): jnp.stack([window[:, offset_z:offset_z + depth_cells] for offset_z in ran...  76.3 us
    reduce_scatter x1, waiting for transfers between devices, shards(): lax.psum_scatter(jnp.einsum('ipxy,opxy->xypio', coef, mixed_grad, preferr...  72.1 us
    psum x1, waiting for transfers between devices, shards(): kernel_total = lax.psum(kernel_local, ('batch', 'space'))  49.5 us
    dot_general x18, matrix products, stencil(): lax.dot_general(kernel[:, offset_x, offset_y], stacked, (((0, 1), (0, 1))...  22.6 us
    all_to_all x2, starting transfers between devices, to_pencils(): lax.all_to_all(values, 'space', split_axis=3, concat_axis=1, tiled=True)  13.3 us
    all_to_all x2, starting transfers between devices, to_slabs(): lax.all_to_all(values, 'space', split_axis=1, concat_axis=3, tiled=True)  11.8 us
    slice x4, local copies, waits for them, and re-layouts, stacked_window(): window[:, offset_z:offset_z + depth_cells]  10.7 us
    dot_general x9, matrix products, kernel_terms(): lax.dot_general(stacked, pre_flat, (((2,), (1,)), ((), ())), preferred_el...  9.54 us
  transfers between devices with their start and end apart: 11, of which 6 were waited for; matrix products, arithmetic and copies ran while one was open for 42% of the time, Pallas kernels for 0%

commit v1 on v0

v1 whole, which is shorter than its diff:
```python
import functools
import math

import jax
import jax.numpy as jnp
import ml_dtypes
import numpy as np
from jax import lax
from jax.experimental import pallas as pl
from jax.experimental.pallas import tpu as pltpu
from jax.sharding import PartitionSpec as P

KX = 8
KY = 8
KZ = 12
NX = 32
NY = 32
CELLS = NX * NY
LANES = 128
GROUP = 8
OFFSETS = 27
TERM_ROWS = 1024

F32 = jnp.float32
BF16 = jnp.bfloat16
inv_root_two = 1.0 / math.sqrt(2.0)
inv_root_two_pi = 1.0 / math.sqrt(2.0 * math.pi)


def basis_rows(half_count, length):
    row = np.arange(2 * half_count)[:, None]
    cell = np.arange(length)[None, :]
    frequency = np.where(row < half_count, row, row - half_count + 1)
    phases = (frequency * cell % length).astype(np.float32) * np.float32(2.0 * math.pi / length)
    return np.where(row < half_count, np.cos(phases), np.sin(phases)).astype(np.float32)


def plane_tables(batches, slabs):
    outer = (basis_rows(KX, NX)[:, None, :, None] * basis_rows(KY, NY)[None, :, None, :]).reshape(
        2 * KX, 2 * KY, CELLS
    )
    outer = outer.reshape(batches, 2 * KX // batches, slabs, 2 * KY // slabs, CELLS)
    outer = outer.transpose(0, 2, 1, 3, 4).reshape(4 * KX * KY, CELLS)
    analysis = (outer * np.float32(2.0 / math.sqrt(CELLS))).astype(ml_dtypes.bfloat16)
    synthesis = (outer * np.float32(2.0 / math.sqrt(4 * KX * KY))).astype(ml_dtypes.bfloat16)
    return analysis, synthesis


def depth_tables(batches, slabs, layers, modes):
    rows = basis_rows(KZ, slabs * layers)
    analysis = (rows * np.float32(math.sqrt(2.0 / (slabs * layers)))).astype(ml_dtypes.bfloat16)
    synthesis = (rows * np.float32(math.sqrt(2.0 / (2 * KZ)))).astype(ml_dtypes.bfloat16)

    def spread(table):
        table = table.astype(np.float32).reshape(2 * KZ, slabs, layers)
        full = np.einsum("psz,bc,mn->mpbzcsn", table, np.eye(batches), np.eye(modes))
        return full.reshape(modes * 2 * KZ * batches, layers * batches * slabs * modes)

    def gathered(table):
        return spread(table).astype(ml_dtypes.bfloat16)

    def scattered(table):
        full = spread(table)
        count = full.shape[0]
        full = full.reshape(count, layers, -1).transpose(2, 1, 0)
        return full.reshape(-1, layers * count).astype(ml_dtypes.bfloat16)

    return gathered(analysis), scattered(synthesis), gathered(synthesis), scattered(analysis)


def interleave_table(channels, layers):
    table = np.zeros((channels, layers, layers, channels), np.float32)
    for layer in range(layers):
        table[np.arange(channels), layer, layer, np.arange(channels)] = 1.0
    return table.reshape(channels * layers, channels * layers).astype(ml_dtypes.bfloat16)


def dot(left, right, contract=(1, 0)):
    return lax.dot_general(
        left, right, (((contract[0],), (contract[1],)), ((), ())), preferred_element_type=F32
    )


def low_lanes(rows):
    return lax.broadcasted_iota(jnp.int32, (rows, LANES), 1) < LANES // 2


def swap_halves(values):
    return pltpu.roll(values, LANES // 2, 1)


def doubled(values):
    low = low_lanes(values.shape[0])
    swapped = swap_halves(values)
    return jnp.concatenate(
        [jnp.where(low, values, swapped), jnp.where(low, swapped, values)], axis=0
    )


def halved(values):
    low = low_lanes(values.shape[0])
    return jnp.concatenate([jnp.where(low, values, 0.0), jnp.where(low, 0.0, values)], axis=0)


def edge_layers(cells_first):
    top = cells_first[: CELLS // 2]
    bottom = cells_first[CELLS // 2 :]
    low = low_lanes(CELLS // 2)
    first = jnp.where(low, top, swap_halves(bottom))
    last = jnp.where(low, swap_halves(top), bottom)
    return first.astype(BF16), last.astype(BF16)


def beside_layers(before, after):
    before = before.astype(F32)
    after = after.astype(F32)
    low = low_lanes(CELLS // 2)
    top = jnp.where(low, before, swap_halves(after))
    bottom = jnp.where(low, swap_halves(before), after)
    return jnp.concatenate([top, bottom], axis=0).astype(BF16)


def y_cells(rows):
    return lax.broadcasted_iota(jnp.int32, (rows, LANES), 0) % NY


def from_below(values):
    return jnp.where(y_cells(values.shape[0]) == 0, 0.0, pltpu.roll(values, 1, 0))


def from_above(values):
    rows = values.shape[0]
    return jnp.where(y_cells(rows) == NY - 1, 0.0, pltpu.roll(values, rows - 1, 0))


def pad_cells(padded, own, beside):
    width = own.shape[1] + beside.shape[1]
    padded[0:NY, :] = jnp.zeros((NY, width), BF16)
    padded[NY + CELLS : 2 * NY + CELLS, :] = jnp.zeros((NY, width), BF16)
    padded[NY : NY + CELLS, 0 : own.shape[1]] = own
    padded[NY : NY + CELLS, own.shape[1] :] = beside


BLOCK_OF_DEPTH = {-1: 2, 0: 0, 1: 1, 2: 3}
STEP = 256


def stencil(padded, table, transposed, store):
    for start in range(0, CELLS, STEP):
        total = None
        for b in range(3):
            cells = padded[start + NY * b : start + NY * b + STEP, :]
            term = dot(cells, table[b], (1, 1) if transposed else (1, 0))
            total = term if total is None else total + term
        result = (
            from_below(total[:, 0:LANES])
            + total[:, LANES : 2 * LANES]
            + from_above(total[:, 2 * LANES :])
        )
        store(start, result)


def banded_forward(weights, table):
    half = LANES // 2
    for b in range(3):
        for c in range(3):
            for depth, block in BLOCK_OF_DEPTH.items():
                parts = []
                for out in range(2):
                    a = depth - out + 1
                    if 0 <= a < 3:
                        parts.append(weights[a * 9 + b * 3 + c])
                    else:
                        parts.append(jnp.zeros((half, half), BF16))
                table[b, block * half : (block + 1) * half, c * LANES : (c + 1) * LANES] = (
                    jnp.concatenate(parts, axis=1)
                )


def banded_backward(weights, table):
    half = LANES // 2
    for b in range(3):
        for c in range(3):
            for out in range(2):
                for pair in ((0, 1), (-1, 2)):
                    parts = []
                    for depth in pair:
                        a = depth - out + 1
                        if 0 <= a < 3:
                            parts.append(weights[(2 - a) * 9 + (2 - b) * 3 + 2 - c])
                        else:
                            parts.append(jnp.zeros((half, half), BF16))
                    row = c * LANES + out * half
                    column = BLOCK_OF_DEPTH[pair[0]] * half
                    table[b, row : row + half, column : column + LANES] = jnp.concatenate(
                        parts, axis=1
                    )


def analyse_kernel(field, turn, analysis, cells_out, coef_out, first_out, last_out):
    cells = dot(field[...], turn[...], (0, 0))
    rounded = cells.astype(BF16)
    coef_out[...] = dot(analysis[...], rounded).astype(BF16)
    cells_out[...] = rounded
    first, last = edge_layers(cells)
    first_out[...] = first
    last_out[...] = last


def local_kernel(
    cells, before, after, cotangent, turn, weights, local_out, lanes_out, cotangent_out, padded, table
):
    banded_forward(weights, table)
    beside = beside_layers(before[...], after[...])
    pad_cells(padded, cells[...], beside)

    def store(start, result):
        local_out[start : start + STEP, :] = result

    stencil(padded, table, False, store)
    whole = jnp.concatenate([cells[...].astype(F32), beside.astype(F32)], axis=1)
    lanes_out[...] = whole.T.astype(BF16)
    cotangent_out[...] = dot(cotangent[...], turn[...], (0, 0))


def diagonal_mask(rows, snaps):
    width = GROUP * LANES // 2
    row = lax.broadcasted_iota(jnp.int32, (rows, width), 0)
    lane = lax.broadcasted_iota(jnp.int32, (rows, width), 1)
    return (row // snaps) % GROUP == lane // (LANES // 2)


def mix_kernel(snaps, received, gather, weights, scatter, back_out, diagonal_out):
    both = doubled(received[...].astype(F32)).astype(BF16)
    coef = dot(gather[...], both)
    count = coef.shape[0]
    wide = jnp.concatenate([coef] * (GROUP // 2), axis=1)
    diagonal_out[...] = jnp.where(diagonal_mask(count, snaps), wide, 0.0).astype(BF16)
    rows = GROUP * snaps
    depth = GROUP * LANES // 2
    mixed = jnp.concatenate(
        [
            dot(
                diagonal_out[g * rows : (g + 1) * rows, :],
                weights[g * depth : (g + 1) * depth, :],
            )
            for g in range(count // rows)
        ],
        axis=0,
    )
    mixed = halved(jnp.concatenate([mixed, mixed], axis=1)).astype(BF16)
    back_out[...] = dot(scatter[...], mixed).astype(BF16)


def activate_kernel(
    terms_in_slab,
    received,
    synthesis,
    synthesis_rows,
    local,
    cotangent,
    lanes,
    activated_out,
    grad_out,
    first_out,
    last_out,
    back_out,
    terms_out,
    spread,
):
    pre = dot(synthesis[...], received[...]) + local[...]
    cdf = 0.5 * (1.0 + lax.erf(pre * inv_root_two))
    density = jnp.exp(-0.5 * pre * pre) * inv_root_two_pi
    activated_out[...] = (pre * cdf).astype(BF16)
    grad = (cotangent[...] * (cdf + pre * density)).astype(BF16)
    grad_out[...] = grad
    back = dot(synthesis_rows[...], grad)
    grad = grad.astype(F32)
    first, last = edge_layers(grad)
    first_out[...] = first
    last_out[...] = last
    spread[0:NY, :] = jnp.zeros((NY, 3 * LANES), BF16)
    spread[NY + CELLS : 2 * NY + CELLS, :] = jnp.zeros((NY, 3 * LANES), BF16)
    spread[NY : NY + CELLS, 0:LANES] = from_above(grad).astype(BF16)
    spread[NY : NY + CELLS, LANES : 2 * LANES] = grad.astype(BF16)
    spread[NY : NY + CELLS, 2 * LANES :] = from_below(grad).astype(BF16)
    half = LANES // 2
    low = low_lanes(half)
    twice = {}
    for b in range(3):
        product = dot(lanes[...], spread[NY * (2 - b) : NY * (2 - b) + CELLS, :])
        for c in range(3):
            for a in range(3):
                blocks = [BLOCK_OF_DEPTH[out + a - 1] * half for out in range(2)]
                columns = slice(c * LANES, (c + 1) * LANES)
                both = jnp.where(
                    low,
                    product[blocks[0] : blocks[0] + half, columns],
                    product[blocks[1] : blocks[1] + half, columns],
                )
                twice[a * 9 + b * 3 + c] = both + swap_halves(both)
    pairs = []
    for k in range(0, OFFSETS, 2):
        pairs.append(jnp.where(low, twice[k], twice.get(k + 1, 0.0)))
    pairs.append(jnp.zeros((TERM_ROWS - half * len(pairs), LANES), F32))
    terms = jnp.concatenate(pairs, axis=0)
    if terms_in_slab:
        slab_store(back_out, back, terms)
    else:
        back_out[...] = back.astype(BF16)
        terms_out[...] = terms.astype(BF16)


def slab_store(slab, modes, terms):
    owners = slab.shape[0]
    modes = modes.reshape(owners, 8, LANES)
    slab[:, 0:16, :] = jnp.concatenate([modes, jnp.zeros_like(modes)], axis=1).astype(BF16)
    slab[:, 16:, :] = terms.reshape(owners, -1, LANES).astype(BF16)


def slab_modes(slab):
    owners = slab.shape[0]
    return slab[:, 0:16, :].astype(F32)[:, 0:8, :].reshape(owners * 8, LANES)


def unmix_kernel(snaps, scale, received, terms, gather, weights, scatter, grad_out, mixed_out, sums_out):
    in_slab = terms is None
    modes = slab_modes(received) if in_slab else received[...].astype(F32)
    mixed = dot(gather[...], doubled(modes).astype(BF16)).astype(BF16)
    mixed_out[...] = mixed
    count = mixed.shape[0]
    rows = GROUP * snaps
    depth = GROUP * LANES // 2
    own = diagonal_mask(rows, snaps)
    narrow = mixed[:, 0 : LANES // 2]
    pieces = []
    for g in range(count // rows):
        full = dot(
            narrow[g * rows : (g + 1) * rows, :], weights[g * depth : (g + 1) * depth, :], (1, 1)
        )
        full = jnp.where(own, full, 0.0)
        pieces.append(sum(full[:, k : k + LANES] for k in range(0, depth, LANES)))
    coef = jnp.concatenate(pieces, axis=0)
    coef = coef + swap_halves(coef)
    grad = dot(scatter[...], halved(coef).astype(BF16))
    if in_slab:
        owners = received.shape[0]
        sums = jnp.sum(received[:, 16:, :].astype(F32), axis=0) * scale
        share = sums.shape[0]
        slab_store(
            grad_out, grad, jnp.broadcast_to(sums[None], (owners, share, LANES)).reshape(-1, LANES)
        )
    else:
        grad_out[...] = grad.astype(BF16)
        sums_out[...] = jnp.sum(terms[...].astype(F32), axis=0) * scale


def weight_kernel(snaps, diagonal, mixed, out):
    rows = GROUP * snaps
    depth = GROUP * LANES // 2
    half = LANES // 2
    for g in range(diagonal.shape[0] // rows):
        span = slice(g * rows, (g + 1) * rows)
        out[g * depth : (g + 1) * depth, :] = dot(diagonal[span, :], mixed[span, 0:half], (0, 0))


def output_kernel(cells, turn, out):
    out[...] = dot(turn[...], cells[...], (1, 1)).astype(BF16)


def local_grad_kernel(grad, before, after, weights, out, padded, table):
    banded_backward(weights, table)
    pad_cells(padded, grad[...], beside_layers(before[...], after[...]))

    def store(start, result):
        out[start : start + STEP, :] = result

    stencil(padded, table, True, store)


def finish_kernel(received, sums, synthesis, local, turn, grad_out, stencil_out):
    in_slab = sums is None
    modes = slab_modes(received).astype(BF16) if in_slab else received[...]
    cells = (dot(synthesis[...], modes) + local[...]).astype(BF16)
    grad_out[...] = dot(turn[...], cells, (1, 1)).astype(BF16)
    if in_slab:
        terms = received[:, 16:, :].astype(F32).reshape(TERM_ROWS, LANES)
    else:
        terms = sums[...].astype(F32)
    half = LANES // 2
    for k in range(OFFSETS):
        row = (k // 2) * half
        lane = (k % 2) * half
        stencil_out[k] = terms[row : row + half, lane : lane + half]


def shape(dims, dtype):
    return jax.ShapeDtypeStruct(dims, dtype)


def run(body, outs, *operands, scratch=(), flops=0):
    given = [operand for operand in operands if operand is not None]

    def kernel(*refs):
        refs = list(refs)
        filled = [None if operand is None else refs.pop(0) for operand in operands]
        kept = [None if out is None else refs.pop(0) for out in outs]
        body(*filled, *kept, *refs)

    made = [out for out in outs if out is not None]
    size = sum(x.size * x.dtype.itemsize for x in (*given, *made))
    results = pl.pallas_call(
        kernel,
        out_shape=made,
        in_specs=[pl.BlockSpec(memory_space=pltpu.VMEM)] * len(given),
        out_specs=[pl.BlockSpec(memory_space=pltpu.VMEM)] * len(made),
        scratch_shapes=list(scratch),
        compiler_params=pltpu.CompilerParams(vmem_limit_bytes=40 * 1024 * 1024),
        cost_estimate=pl.CostEstimate(flops=flops, bytes_accessed=size, transcendentals=0),
        name=body.__name__ if hasattr(body, "__name__") else body.func.__name__,
    )(*given)
    results = list(results)
    return [None if out is None else results.pop(0) for out in outs]


def exchange(values):
    return lax.all_to_all(values, ("batch", "space"), split_axis=0, concat_axis=0, tiled=True)


def neighbours(first, last):
    ends = lax.axis_size("space") - 1
    before = lax.ppermute(last, "space", [(i, i + 1) for i in range(ends)])
    after = lax.ppermute(first, "space", [(i + 1, i) for i in range(ends)])
    return before, after


def shards(snapshots, cotangent, mode_weight, conv_weight):
    batches = lax.axis_size("batch")
    slabs = lax.axis_size("space")
    devices = batches * slabs
    _, channels, layers, plane = snapshots.shape
    modes = mode_weight.shape[0] * mode_weight.shape[1]
    half = LANES // 2
    assert channels == half and layers == 2 and plane == CELLS
    plane_rows = devices * modes
    count = modes * 2 * KZ * batches
    in_slab = modes == 8 and devices * 32 == TERM_ROWS

    analysis, synthesis = plane_tables(batches, slabs)
    gather, scatter, gather_back, scatter_back = depth_tables(batches, slabs, layers, modes)
    turn = interleave_table(channels, layers)

    weights = mode_weight.reshape(modes * 2 * KZ * channels, channels)
    taps = conv_weight.reshape(OFFSETS, channels, channels)
    field = snapshots.reshape(channels * layers, plane)
    outer = cotangent.reshape(channels * layers, plane)
    wide = shape((CELLS, LANES), BF16)
    edge = shape((CELLS // 2, LANES), BF16)
    plane_modes = shape((plane_rows, LANES), BF16)
    padded = pltpu.VMEM((CELLS + 2 * NY, 2 * LANES), BF16)

    def send(values):
        return exchange(values.reshape(devices, modes, LANES)).reshape(plane_rows, LANES)

    cells, coef, first, last = run(
        analyse_kernel, [wide, plane_modes, edge, edge], field, turn, analysis, flops=10**8
    )
    coef = send(coef)
    before, after = neighbours(first, last)
    local, lanes, outer_cells = run(
        local_kernel,
        [shape((CELLS, LANES), F32), shape((2 * LANES, CELLS), BF16), shape((CELLS, LANES), F32)],
        cells,
        before,
        after,
        outer,
        turn,
        taps,
        scratch=[padded, pltpu.VMEM((3, 2 * LANES, 3 * LANES), BF16)],
        flops=7 * 10**8,
    )
    back, diagonal = run(
        functools.partial(mix_kernel, batches),
        [plane_modes, shape((count, GROUP * half), BF16)],
        coef,
        gather,
        weights,
        scatter,
        flops=4 * 10**8,
    )
    back = send(back)
    slab = shape((devices, 16 + TERM_ROWS // devices, LANES), BF16)
    activated, grad, first, last, back, terms = run(
        functools.partial(activate_kernel, in_slab),
        [
            wide,
            wide,
            edge,
            edge,
            slab if in_slab else plane_modes,
            None if in_slab else shape((TERM_ROWS, LANES), BF16),
        ],
        back,
        np.ascontiguousarray(synthesis.T),
        synthesis,
        local,
        outer_cells,
        lanes,
        scratch=[pltpu.VMEM((CELLS + 2 * NY, 3 * LANES), BF16)],
        flops=10**9,
    )
    if in_slab:
        back = exchange(back)
    else:
        back = send(back)
        terms = exchange(terms.reshape(devices, TERM_ROWS // devices, LANES))
    before, after = neighbours(first, last)
    (activated,) = run(
        output_kernel, [shape((channels * layers, plane), BF16)], activated, turn, flops=10**8
    )
    (local,) = run(
        local_grad_kernel,
        [shape((CELLS, LANES), F32)],
        grad,
        before,
        after,
        taps,
        scratch=[padded, pltpu.VMEM((3, 3 * LANES, 2 * LANES), BF16)],
        flops=7 * 10**8,
    )
    scale = 1.0 / math.sqrt(batches * slabs * layers * plane)
    grad_modes, mixed_grad, sums = run(
        functools.partial(unmix_kernel, batches, scale),
        [
            slab if in_slab else plane_modes,
            shape((count, LANES), BF16),
            None if in_slab else shape((TERM_ROWS // devices, LANES), F32),
        ],
        back,
        None if in_slab else terms,
        gather_back,
        weights,
        scatter_back,
        flops=4 * 10**8,
    )
    if in_slab:
        grad_modes = exchange(grad_modes)
    else:
        grad_modes = send(grad_modes)
        sums = lax.all_gather(sums, ("batch", "space"), axis=0, tiled=True)
    (mode_gradient,) = run(
        functools.partial(weight_kernel, batches),
        [shape((modes * 2 * KZ * channels, channels), F32)],
        diagonal,
        mixed_grad,
        flops=4 * 10**8,
    )
    input_gradient, conv_gradient = run(
        finish_kernel,
        [shape((channels * layers, plane), BF16), shape((OFFSETS, channels, channels), F32)],
        grad_modes,
        sums,
        np.ascontiguousarray(analysis.T),
        local,
        turn,
        flops=10**8,
    )
    return (
        activated.reshape(snapshots.shape),
        input_gradient.reshape(snapshots.shape),
        mode_gradient.reshape(mode_weight.shape),
        conv_gradient.reshape(conv_weight.shape),
    )


def solution(mesh):
    in_specs = (
        P("batch", None, "space", None),
        P("batch", None, "space", None),
        P("batch", "space", None, None, None),
        P(),
    )
    out_specs = (
        P("batch", None, "space", None),
        P("batch", None, "space", None),
        P("batch", "space", None, None, None),
        P(),
    )
    return jax.shard_map(shards, mesh=mesh, in_specs=in_specs, out_specs=out_specs, check_vma=False)
```

time: 367 us -> 98.4 us (0.27)
  the two profiles are of different devices: /device:TPU:0 before, /device:TPU:17 now
where the time goes in v1:
time: 98.4 us; the launch traced here: 96.9 us
  local copies, waits for them, and re-layouts  32.1 us (33%)
  starting transfers between devices  27.9 us (28%)
  blocking collectives  16.6 us (17%)
  Pallas kernels  15.1 us (15%)
  waiting for transfers between devices  4.44 us (5%)
    unnamed x74, local copies, waits for them, and re-layouts  27.7 us
    all_to_all x3, starting transfers between devices, exchange(): lax.all_to_all(values, ('batch', 'space'), split_axis=0, concat_axis=0, t...  17.3 us
    all_to_all x1, blocking collectives, exchange(): lax.all_to_all(values, ('batch', 'space'), split_axis=0, concat_axis=0, t...  16.6 us
    pallas_call x9, Pallas kernels, run(): pl.pallas_call(kernel, out_shape=made, in_specs=[pl.BlockSpec(memory_spac...  15.1 us
    ppermute x2, starting transfers between devices, neighbours(): before = lax.ppermute(last, 'space', [(i, i + 1) for i in range(ends)])  6.72 us
    ppermute x2, waiting for transfers between devices, neighbours(): after = lax.ppermute(first, 'space', [(i + 1, i) for i in range(ends)])  4.43 us
    ppermute x2, starting transfers between devices, neighbours(): after = lax.ppermute(first, 'space', [(i + 1, i) for i in range(ends)])  3.84 us
  transfers between devices with their start and end apart: 7, of which 1 were waited for; matrix products, arithmetic and copies ran while one was open for 3% of the time, Pallas kernels for 9%

profile of v1, /device:TPU:17, one launch (start us, length us, event | category | flops | bytes accessed | tf_op | source)
XLA Modules:
  0.0 96.9 jit_solution(8107142535011397495)
XLA Ops:
  0.6 1.0 %reshape.44.refs_0_ = bf16[128,1024]{1,0:T(8,128)(2,1)S(1)} reshape(bf16[1,64,2,1024]{3,2,1,0:T(2,128)(2,1)} %param.13) | data formatting | bytes 524288 | tf_op jit(solution)/shard_map/reshape | solution.py:455
  1.7 0.0 copy-start.3
  1.7 1.0 %copy-done.3 = bf16[256,1024]{1,0:T(8,128)(2,1)S(1)} copy-done((bf16[256,1024]{1,0:T(8,128)(2,1)S(1)}, bf16[256,1024]{1,0:T(8,128)(2,1)}, u32[]{:S(2)}) %copy-start.3) | copy-done | bytes 524312
  2.7 0.8 copy-done.9
  3.5 1.2 %analyse_kernel.1 = (bf16[1024,128]{1,0:T(8,128)(2,1)S(1)}, bf16[256,128]{1,0:T(8,128)(2,1)}, bf16[512,128]{1,0:T(8,128)(2,1)}, bf16[512,128]{1,0:T(8,128)(2,1)}) custom-call(bf16[128,1024]{1,0:T(8,128)(2,1)S(1)} %reshape.44.refs_0_, bf16[128,128]{1,0:T(8,128)(2,1)S(1)} %copy-done.9, bf16[256,1024]{1,0:T(8,128)(2,1)S(1)} %copy-done.3), custom_call_target="tpu_custom_call" | custom-call | flops 100000000 | bytes 1409024 | tf_op jit(solution)/shard_map/analyse_kernel/pallas_call | solution.py:412
  4.7 0.7 copy-done.23
  5.4 6.2 %all-to-all-start = ((bf16[32,8,128]{2,1,0:T(8,128)(2,1)}), bf16[32,8,128]{2,1,0:T(8,128)(2,1)S(1)}, u32[]{:S(2)}, u32[]{:S(2)}) async-start(bf16[32,8,128]{2,1,0:T(8,128)(2,1)} %bitcast), calls=%async_computation | async-start | bytes 131072 | tf_op jit(solution)/shard_map/all_to_all | solution.py:427
  11.6 3.4 %collective-permute-start = (bf16[512,128]{1,0:T(8,128)(2,1)}, bf16[512,128]{1,0:T(8,128)(2,1)}, u32[]{:S(2)}, u32[]{:S(2)}) collective-permute-start(bf16[512,128]{1,0:T(8,128)(2,1)} %get-tuple-element.25), channel_id=1, source_target_pairs={{0,1},{1,2},{2,3},{3,4},{4,5},{5,6},{6,7},{7,8},{8,9},{9,10},{10,1... | collective-permute-start | bytes 393224 | tf_op jit(solution)/shard_map/ppermute | solution.py:432
  15.0 1.9 %collective-permute-start.1 = (bf16[512,128]{1,0:T(8,128)(2,1)}, bf16[512,128]{1,0:T(8,128)(2,1)}, u32[]{:S(2)}, u32[]{:S(2)}) collective-permute-start(bf16[512,128]{1,0:T(8,128)(2,1)} %get-tuple-element.26), channel_id=1, source_target_pairs={{1,0},{2,1},{3,2},{4,3},{5,4},{6,5},{7,6},{8,7},{9,8},{10,9},{11,1... | collective-permute-start | bytes 393224 | tf_op jit(solution)/shard_map/ppermute | solution.py:433
  16.9 0.0 all-to-all-done
  16.9 0.0 copy-start.13
  16.9 0.6 copy-done.13
  17.5 1.9 %copy-done = bf16[8,1,24,64,64]{4,3,2,1,0:T(8,128)(2,1)S(1)} copy-done((bf16[8,1,24,64,64]{4,3,2,1,0:T(8,128)(2,1)S(1)}, bf16[8,1,24,64,64]{4,3,2,1,0:T(8,128)(2,1)}, u32[]{:S(2)}) %copy-start) | copy-done | bytes 1572888
  19.4 1.0 %copy-done.7 = bf16[256,768]{1,0:T(8,128)(2,1)S(1)} copy-done((bf16[256,768]{1,0:T(8,128)(2,1)S(1)}, bf16[256,768]{1,0:T(8,128)(2,1)}, u32[]{:S(2)}) %copy-start.7) | copy-done | bytes 393240
  20.4 1.0 %copy-done.8 = bf16[384,512]{1,0:T(8,128)(2,1)S(1)} copy-done((bf16[384,512]{1,0:T(8,128)(2,1)S(1)}, bf16[384,512]{1,0:T(8,128)(2,1)}, u32[]{:S(2)}) %copy-start.8) | copy-done | bytes 393240
  21.4 0.8 copy-done.14
  22.3 1.2 %mix_kernel.1 = (bf16[256,128]{1,0:T(8,128)(2,1)S(1)}, bf16[384,512]{1,0:T(8,128)(2,1)S(1)}) custom-call(bf16[256,128]{1,0:T(8,128)(2,1)S(1)} %bitcast.12, bf16[384,512]{1,0:T(8,128)(2,1)S(1)} %copy-done.8, bf16[12288,64]{1,0:T(8,128)(2,1)S(1)} %bitcast.10, bf16[256,768]{1,0:T(8,128)(2,1)S(1)} %copy-done.7), custom_call_target="tpu_custom_call" | custom-call | flops 400000000 | bytes 2883584 | tf_op jit(solution)/shard_map/mix_kernel/pallas_call | solution.py:412
  23.5 0.6 copy-done.20
  24.1 6.2 %all-to-all-start.1 = ((bf16[32,8,128]{2,1,0:T(8,128)(2,1)}), bf16[32,8,128]{2,1,0:T(8,128)(2,1)}, u32[]{:S(2)}, u32[]{:S(2)}) async-start(bf16[32,8,128]{2,1,0:T(8,128)(2,1)} %bitcast.13), calls=%async_computation.1 | async-start | bytes 131072 | tf_op jit(solution)/shard_map/all_to_all | solution.py:427
  30.3 1.8 %reshape.50.refs_3_ = bf16[128,1024]{1,0:T(8,128)(2,1)} reshape(bf16[1,64,2,1024]{3,2,1,0:T(2,128)(2,1)} %param.14) | data formatting | bytes 524288 | tf_op jit(solution)/shard_map/reshape | solution.py:456
  32.1 0.0 collective-permute-done.refs_1_
  32.1 0.0 collective-permute-done.1.refs_2_
  32.1 0.8 copy-done.10
  32.8 0.9 copy-done.17
  33.8 1.0 %copy-done.21 = bf16[3,3,3,64,64]{4,3,2,1,0:T(8,128)(2,1)S(1)} copy-done((bf16[3,3,3,64,64]{4,3,2,1,0:T(8,128)(2,1)S(1)}, bf16[3,3,3,64,64]{4,3,2,1,0:T(8,128)(2,1)}, u32[]{:S(2)}) %copy-start.21) | copy-done | bytes 221208
  34.8 0.9 copy-done.24
  35.7 2.1 %local_kernel.1 = (f32[1024,128]{1,0:T(8,128)S(1)}, bf16[256,1024]{1,0:T(8,128)(2,1)S(1)}, f32[1024,128]{1,0:T(8,128)S(1)}) custom-call(bf16[1024,128]{1,0:T(8,128)(2,1)S(1)} %copy-done.24, bf16[512,128]{1,0:T(8,128)(2,1)} %collective-permute-done.refs_1_, bf16[512,128]{1,0:T(8,128)(2,1)} %collective-permute-done.1.refs_2_, ...), custom_call_target="tpu_custom_call" | custom-call | flops 700000000 | bytes 2613248 | tf_op jit(solution)/shard_map/local_kernel/pallas_call | solution.py:412
  37.9 0.0 copy-start.29
  37.9 0.8 copy-done.29
  38.7 0.8 copy-done.31
  39.5 0.8 copy-done.33
  40.3 0.0 all-to-all-done.1
  40.3 1.0 %copy-done.27 = bf16[256,1024]{1,0:T(8,128)(2,1)S(1)} copy-done((bf16[256,1024]{1,0:T(8,128)(2,1)S(1)}, bf16[256,1024]{1,0:T(8,128)(2,1)}, u32[]{:S(2)}) %copy-start.27) | copy-done | bytes 524312
  41.3 1.0 %copy-done.28 = bf16[1024,256]{1,0:T(8,128)(2,1)S(1)} copy-done((bf16[1024,256]{1,0:T(8,128)(2,1)S(1)}, bf16[1024,256]{1,0:T(8,128)(2,1)}, u32[]{:S(2)}) %copy-start.28) | copy-done | bytes 524312
  42.4 1.0 %copy-done.30 = f32[1024,128]{1,0:T(8,128)S(1)} copy-done((f32[1024,128]{1,0:T(8,128)S(1)}, f32[1024,128]{1,0:T(8,128)}, u32[]{:S(2)}) %copy-start.30) | copy-done | bytes 524312
  43.4 1.0 %copy-done.32 = bf16[256,1024]{1,0:T(8,128)(2,1)S(1)} copy-done((bf16[256,1024]{1,0:T(8,128)(2,1)S(1)}, bf16[256,1024]{1,0:T(8,128)(2,1)}, u32[]{:S(2)}) %copy-start.32) | copy-done | bytes 524312
  44.4 1.0 %copy-done.34 = f32[1024,128]{1,0:T(8,128)S(1)} copy-done((f32[1024,128]{1,0:T(8,128)S(1)}, f32[1024,128]{1,0:T(8,128)}, u32[]{:S(2)}) %copy-start.34) | copy-done | bytes 524312
  45.5 2.6 %activate_kernel.1 = (bf16[1024,128]{1,0:T(8,128)(2,1)S(1)}, bf16[1024,128]{1,0:T(8,128)(2,1)S(1)}, bf16[512,128]{1,0:T(8,128)(2,1)S(1)}, bf16[512,128]{1,0:T(8,128)(2,1)S(1)}, bf16[32,48,128]{2,1,0:T(8,128)(2,1)S(1)}) custom-call(bf16[256,128]{1,0:T(8,128)(2,1)} %bitcast.4.refs_0_, bf16[1024,256]{1,0:T(8,128)(2,1)S(1)} %copy-done.28, ...), custom_call_target="tpu_custom_call" | custom-call | flops 1000000000 | bytes 3866624 | tf_op jit(solution)/shard_map/activate_kernel/pallas_call | solution.py:412
  48.1 0.0 copy-start.15
  48.1 0.0 copy-start.35
  48.1 16.6 %all_to_all.20.refs_0_ = bf16[32,48,128]{2,1,0:T(8,128)(2,1)S(1)} all-to-all(bf16[32,48,128]{2,1,0:T(8,128)(2,1)S(1)} %get-tuple-element.31), channel_id=1, replica_groups=mesh['batch'=2,'space'=16] {'batch','space'}, dimensions={0} | all-to-all | bytes 786432 | tf_op jit(solution)/shard_map/all_to_all | solution.py:427
  64.7 1.0 %copy-done.4 = bf16[256,768]{1,0:T(8,128)(2,1)S(1)} copy-done((bf16[256,768]{1,0:T(8,128)(2,1)S(1)}, bf16[256,768]{1,0:T(8,128)(2,1)}, u32[]{:S(2)}) %copy-start.4) | copy-done | bytes 393240
  65.7 1.0 %copy-done.5 = bf16[384,512]{1,0:T(8,128)(2,1)S(1)} copy-done((bf16[384,512]{1,0:T(8,128)(2,1)S(1)}, bf16[384,512]{1,0:T(8,128)(2,1)}, u32[]{:S(2)}) %copy-start.5) | copy-done | bytes 393240
  66.7 1.6 %unmix_kernel.1 = (bf16[32,48,128]{2,1,0:T(8,128)(2,1)S(1)}, bf16[384,128]{1,0:T(8,128)(2,1)S(1)}) custom-call(bf16[32,48,128]{2,1,0:T(8,128)(2,1)S(1)} %all_to_all.20.refs_0_, bf16[384,512]{1,0:T(8,128)(2,1)S(1)} %copy-done.5, bf16[12288,64]{1,0:T(8,128)(2,1)S(1)} %bitcast.11, bf16[256,768]{1,0:T(8,128)(2,1)S(1)} %copy-done.4), custom_call_target="tpu_custom_call" | custom-call | flops 400000000 | bytes 3244032 | tf_op jit(solution)/shard_map/unmix_kernel/pallas_call | solution.py:412
  68.3 0.0 copy-start.6
  68.3 0.7 copy-done.6
  69.1 0.6 copy-done.18
  69.7 4.9 %all-to-all-start.3 = ((bf16[32,48,128]{2,1,0:T(8,128)(2,1)}), bf16[32,48,128]{2,1,0:T(8,128)(2,1)S(1)}, u32[]{:S(2)}, u32[]{:S(2)}) async-start(bf16[32,48,128]{2,1,0:T(8,128)(2,1)} %copy-done.6), calls=%async_computation.3 | async-start | bytes 786432 | tf_op jit(solution)/shard_map/all_to_all | solution.py:427
  74.6 3.4 %collective-permute-start.2 = (bf16[512,128]{1,0:T(8,128)(2,1)}, bf16[512,128]{1,0:T(8,128)(2,1)S(1)}, u32[]{:S(2)}, u32[]{:S(2)}) collective-permute-start(bf16[512,128]{1,0:T(8,128)(2,1)} %copy-done.26), channel_id=1, source_target_pairs={{0,1},{1,2},{2,3},{3,4},{4,5},{5,6},{6,7},{7,8},{8,9},{9,10},{10,1... | collective-permute-start | bytes 393224 | tf_op jit(solution)/shard_map/ppermute | solution.py:432
  78.0 1.9 %collective-permute-start.3 = (bf16[512,128]{1,0:T(8,128)(2,1)}, bf16[512,128]{1,0:T(8,128)(2,1)S(1)}, u32[]{:S(2)}, u32[]{:S(2)}) collective-permute-start(bf16[512,128]{1,0:T(8,128)(2,1)} %copy-done.25), channel_id=1, source_target_pairs={{1,0},{2,1},{3,2},{4,3},{5,4},{6,5},{7,6},{8,7},{9,8},{10,9},{11,1... | collective-permute-start | bytes 393224 | tf_op jit(solution)/shard_map/ppermute | solution.py:433
  79.9 0.0 copy-start.11
  79.9 0.7 copy-done.11
  80.6 0.9 copy-done.16
  81.6 0.2 output_kernel.1
  81.8 0.8 reshape.52
  82.6 4.4 %collective-permute-done.3.refs_2_ = bf16[512,128]{1,0:T(8,128)(2,1)S(1)} collective-permute-done((bf16[512,128]{1,0:T(8,128)(2,1)}, bf16[512,128]{1,0:T(8,128)(2,1)S(1)}, u32[]{:S(2)}, u32[]{:S(2)}) %collective-permute-start.3) | collective-permute-done | bytes 131104 | tf_op jit(solution)/shard_map/ppermute | solution.py:433
  87.1 1.0 %copy-done.22 = bf16[3,3,3,64,64]{4,3,2,1,0:T(8,128)(2,1)S(1)} copy-done((bf16[3,3,3,64,64]{4,3,2,1,0:T(8,128)(2,1)S(1)}, bf16[3,3,3,64,64]{4,3,2,1,0:T(8,128)(2,1)}, u32[]{:S(2)}) %copy-start.22) | copy-done | bytes 221208
  88.1 0.9 copy-done.36
  89.0 1.1 %local_grad_kernel.1.refs_2_ = f32[1024,128]{1,0:T(8,128)S(1)} custom-call(bf16[1024,128]{1,0:T(8,128)(2,1)S(1)} %copy-done.36, bf16[512,128]{1,0:T(8,128)(2,1)S(1)} %collective-permute-done.2.refs_1_, bf16[512,128]{1,0:T(8,128)(2,1)S(1)} %collective-permute-done.3.refs_2_, bf16[27,64,64]{2,1,0:T(8,128)(2,1)S(1)} %bitcast.15), custom_call_target="tpu_custom_call" | custom-call | flops 700000000 | bytes 1269760 | tf_op jit(solution)/shard_map/local_grad_kernel/pallas_call | solution.py:412
  90.1 0.9 copy-done.19
  91.0 3.7 %weight_kernel.1 = f32[12288,64]{1,0:T(8,128)} custom-call(bf16[384,512]{1,0:T(8,128)(2,1)S(1)} %get-tuple-element.37.refs_0_, bf16[384,128]{1,0:T(8,128)(2,1)S(1)} %copy-done.19), custom_call_target="tpu_custom_call" | custom-call | flops 400000000 | bytes 3637248 | tf_op jit(solution)/shard_map/weight_kernel/pallas_call | solution.py:412
  94.7 0.0 all-to-all-done.3.refs_0_
  94.7 1.4 %finish_kernel.1 = (bf16[128,1024]{1,0:T(8,128)(2,1)S(1)}, f32[27,64,64]{2,1,0:T(8,128)}) custom-call(bf16[32,48,128]{2,1,0:T(8,128)(2,1)S(1)} %all-to-all-done.3.refs_0_, bf16[1024,256]{1,0:T(8,128)(2,1)S(1)} %copy-done.2, f32[1024,128]{1,0:T(8,128)S(1)} %local_grad_kernel.1.refs_2_, bf16[128,128]{1,0:T(8,128)(2,1)S(1)} %copy-done.12), custom_call_target="tpu_custom_call" | custom-call | flops 100000000 | bytes 2179072 | tf_op jit(solution)/shard_map/finish_kernel/pallas_call | solution.py:412
  96.1 0.8 reshape.53
  (38 shorter events, 0.1 us)
Async XLA Ops:
  1.7 1.0 %copy-start.3 = (bf16[256,1024]{1,0:T(8,128)(2,1)S(1)}, bf16[256,1024]{1,0:T(8,128)(2,1)}, u32[]{:S(2)}) copy-start(bf16[256,1024]{1,0:T(8,128)(2,1)} %constant.19.clone.refs_2_) | copy-start | bytes 1572868
  2.7 0.8 copy-start.9
  4.7 0.7 copy-start.23
  5.4 11.6 %all-to-all-start = ((bf16[32,8,128]{2,1,0:T(8,128)(2,1)}), bf16[32,8,128]{2,1,0:T(8,128)(2,1)S(1)}, u32[]{:S(2)}, u32[]{:S(2)}) async-start(bf16[32,8,128]{2,1,0:T(8,128)(2,1)} %bitcast), calls=%async_computation | async-start | bytes 131072 | tf_op jit(solution)/shard_map/all_to_all | solution.py:427
  11.6 20.4 %collective-permute-start = (bf16[512,128]{1,0:T(8,128)(2,1)}, bf16[512,128]{1,0:T(8,128)(2,1)}, u32[]{:S(2)}, u32[]{:S(2)}) collective-permute-start(bf16[512,128]{1,0:T(8,128)(2,1)} %get-tuple-element.25), channel_id=1, source_target_pairs={{0,1},{1,2},{2,3},{3,4},{4,5},{5,6},{6,7},{7,8},{8,9},{9,10},{10,1... | collective-permute-start | bytes 393224 | tf_op jit(solution)/shard_map/ppermute | solution.py:432
  15.0 17.1 %collective-permute-start.1 = (bf16[512,128]{1,0:T(8,128)(2,1)}, bf16[512,128]{1,0:T(8,128)(2,1)}, u32[]{:S(2)}, u32[]{:S(2)}) collective-permute-start(bf16[512,128]{1,0:T(8,128)(2,1)} %get-tuple-element.26), channel_id=1, source_target_pairs={{1,0},{2,1},{3,2},{4,3},{5,4},{6,5},{7,6},{8,7},{9,8},{10,9},{11,1... | collective-permute-start | bytes 393224 | tf_op jit(solution)/shard_map/ppermute | solution.py:433
  16.9 0.6 copy-start.13
  17.5 1.9 %copy-start = (bf16[8,1,24,64,64]{4,3,2,1,0:T(8,128)(2,1)S(1)}, bf16[8,1,24,64,64]{4,3,2,1,0:T(8,128)(2,1)}, u32[]{:S(2)}) copy-start(bf16[8,1,24,64,64]{4,3,2,1,0:T(8,128)(2,1)} %param.15) | copy-start | bytes 4718596
  19.4 1.0 %copy-start.7 = (bf16[256,768]{1,0:T(8,128)(2,1)S(1)}, bf16[256,768]{1,0:T(8,128)(2,1)}, u32[]{:S(2)}) copy-start(bf16[256,768]{1,0:T(8,128)(2,1)} %constant.21.clone.refs_3_) | copy-start | bytes 1179652
  20.4 1.0 %copy-start.8 = (bf16[384,512]{1,0:T(8,128)(2,1)S(1)}, bf16[384,512]{1,0:T(8,128)(2,1)}, u32[]{:S(2)}) copy-start(bf16[384,512]{1,0:T(8,128)(2,1)} %constant.20.clone.refs_1_) | copy-start | bytes 1179652
  21.4 0.8 copy-start.14
  22.3 42.4 %copy-start.1 = (bf16[8,1,24,64,64]{4,3,2,1,0:T(8,128)(2,1)S(1)}, bf16[8,1,24,64,64]{4,3,2,1,0:T(8,128)(2,1)}, u32[]{:S(2)}) copy-start(bf16[8,1,24,64,64]{4,3,2,1,0:T(8,128)(2,1)} %param.15) | copy-start | bytes 4718596
  23.5 0.6 copy-start.20
  24.1 16.1 %all-to-all-start.1 = ((bf16[32,8,128]{2,1,0:T(8,128)(2,1)}), bf16[32,8,128]{2,1,0:T(8,128)(2,1)}, u32[]{:S(2)}, u32[]{:S(2)}) async-start(bf16[32,8,128]{2,1,0:T(8,128)(2,1)} %bitcast.13), calls=%async_computation.1 | async-start | bytes 131072 | tf_op jit(solution)/shard_map/all_to_all | solution.py:427
  32.1 0.8 copy-start.10
  32.8 0.9 copy-start.17
  33.8 1.0 %copy-start.21 = (bf16[3,3,3,64,64]{4,3,2,1,0:T(8,128)(2,1)S(1)}, bf16[3,3,3,64,64]{4,3,2,1,0:T(8,128)(2,1)}, u32[]{:S(2)}) copy-start(bf16[3,3,3,64,64]{4,3,2,1,0:T(8,128)(2,1)} %param.16) | copy-start | bytes 663556
  34.8 0.9 copy-start.24
  37.9 0.8 copy-start.29
  38.7 0.8 copy-start.31
  39.5 0.8 copy-start.33
  40.3 1.0 %copy-start.27 = (bf16[256,1024]{1,0:T(8,128)(2,1)S(1)}, bf16[256,1024]{1,0:T(8,128)(2,1)}, u32[]{:S(2)}) copy-start(bf16[256,1024]{1,0:T(8,128)(2,1)} %constant.23.clone.refs_2_) | copy-start | bytes 1572868
  41.3 1.0 %copy-start.28 = (bf16[1024,256]{1,0:T(8,128)(2,1)S(1)}, bf16[1024,256]{1,0:T(8,128)(2,1)}, u32[]{:S(2)}) copy-start(bf16[1024,256]{1,0:T(8,128)(2,1)} %constant.22.clone.refs_1_) | copy-start | bytes 1572868
  42.3 1.0 %copy-start.30 = (f32[1024,128]{1,0:T(8,128)S(1)}, f32[1024,128]{1,0:T(8,128)}, u32[]{:S(2)}) copy-start(f32[1024,128]{1,0:T(8,128)} %copy-done.29) | copy-start | bytes 1572868
  43.4 1.0 %copy-start.32 = (bf16[256,1024]{1,0:T(8,128)(2,1)S(1)}, bf16[256,1024]{1,0:T(8,128)(2,1)}, u32[]{:S(2)}) copy-start(bf16[256,1024]{1,0:T(8,128)(2,1)} %copy-done.31) | copy-start | bytes 1572868
  44.4 1.0 %copy-start.34 = (f32[1024,128]{1,0:T(8,128)S(1)}, f32[1024,128]{1,0:T(8,128)}, u32[]{:S(2)}) copy-start(f32[1024,128]{1,0:T(8,128)} %copy-done.33) | copy-start | bytes 1572868
  48.1 20.2 %copy-start.15 = (bf16[1024,128]{1,0:T(8,128)(2,1)}, bf16[1024,128]{1,0:T(8,128)(2,1)S(1)}, u32[]{:S(2)}) copy-start(bf16[1024,128]{1,0:T(8,128)(2,1)S(1)} %get-tuple-element.30.refs_0_) | copy-start | bytes 786436
  48.1 20.2 %copy-start.25 = (bf16[512,128]{1,0:T(8,128)(2,1)}, bf16[512,128]{1,0:T(8,128)(2,1)S(1)}, u32[]{:S(2)}) copy-start(bf16[512,128]{1,0:T(8,128)(2,1)S(1)} %get-tuple-element.35) | copy-start | bytes 393220
  48.1 20.2 %copy-start.26 = (bf16[512,128]{1,0:T(8,128)(2,1)}, bf16[512,128]{1,0:T(8,128)(2,1)S(1)}, u32[]{:S(2)}) copy-start(bf16[512,128]{1,0:T(8,128)(2,1)S(1)} %get-tuple-element.34) | copy-start | bytes 393220
  48.1 20.2 %copy-start.35 = (bf16[1024,128]{1,0:T(8,128)(2,1)}, bf16[1024,128]{1,0:T(8,128)(2,1)S(1)}, u32[]{:S(2)}) copy-start(bf16[1024,128]{1,0:T(8,128)(2,1)S(1)} %get-tuple-element.33.refs_0_) | copy-start | bytes 786436
  64.7 1.0 %copy-start.4 = (bf16[256,768]{1,0:T(8,128)(2,1)S(1)}, bf16[256,768]{1,0:T(8,128)(2,1)}, u32[]{:S(2)}) copy-start(bf16[256,768]{1,0:T(8,128)(2,1)} %constant.25.clone.refs_3_) | copy-start | bytes 1179652
  65.7 1.0 %copy-start.5 = (bf16[384,512]{1,0:T(8,128)(2,1)S(1)}, bf16[384,512]{1,0:T(8,128)(2,1)}, u32[]{:S(2)}) copy-start(bf16[384,512]{1,0:T(8,128)(2,1)} %constant.24.clone.refs_1_) | copy-start | bytes 1179652
  68.3 0.7 copy-start.6
  69.1 0.6 copy-start.18
  69.7 25.0 %copy-start.2 = (bf16[1024,256]{1,0:T(8,128)(2,1)S(1)}, bf16[1024,256]{1,0:T(8,128)(2,1)}, u32[]{:S(2)}) copy-start(bf16[1024,256]{1,0:T(8,128)(2,1)} %constant.26.clone.refs_1_) | copy-start | bytes 1572868
  69.7 25.0 %copy-start.12 = (bf16[128,128]{1,0:T(8,128)(2,1)S(1)}, bf16[128,128]{1,0:T(8,128)(2,1)}, u32[]{:S(2)}) copy-start(bf16[128,128]{1,0:T(8,128)(2,1)} %constant.18.clone.refs_1_.refs_4_.refs_3_) | copy-start | bytes 98308
  69.7 25.0 %all-to-all-start.3 = ((bf16[32,48,128]{2,1,0:T(8,128)(2,1)}), bf16[32,48,128]{2,1,0:T(8,128)(2,1)S(1)}, u32[]{:S(2)}, u32[]{:S(2)}) async-start(bf16[32,48,128]{2,1,0:T(8,128)(2,1)} %copy-done.6), calls=%async_computation.3 | async-start | bytes 786432 | tf_op jit(solution)/shard_map/all_to_all | solution.py:427
  74.6 8.1 %collective-permute-start.2 = (bf16[512,128]{1,0:T(8,128)(2,1)}, bf16[512,128]{1,0:T(8,128)(2,1)S(1)}, u32[]{:S(2)}, u32[]{:S(2)}) collective-permute-start(bf16[512,128]{1,0:T(8,128)(2,1)} %copy-done.26), channel_id=1, source_target_pairs={{0,1},{1,2},{2,3},{3,4},{4,5},{5,6},{6,7},{7,8},{8,9},{9,10},{10,1... | collective-permute-start | bytes 393224 | tf_op jit(solution)/shard_map/ppermute | solution.py:432
  78.0 9.1 %collective-permute-start.3 = (bf16[512,128]{1,0:T(8,128)(2,1)}, bf16[512,128]{1,0:T(8,128)(2,1)S(1)}, u32[]{:S(2)}, u32[]{:S(2)}) collective-permute-start(bf16[512,128]{1,0:T(8,128)(2,1)} %copy-done.25), channel_id=1, source_target_pairs={{1,0},{2,1},{3,2},{4,3},{5,4},{6,5},{7,6},{8,7},{9,8},{10,9},{11,1... | collective-permute-start | bytes 393224 | tf_op jit(solution)/shard_map/ppermute | solution.py:433
  79.9 0.8 copy-start.11
  80.6 0.9 copy-start.16
  87.1 1.0 %copy-start.22 = (bf16[3,3,3,64,64]{4,3,2,1,0:T(8,128)(2,1)S(1)}, bf16[3,3,3,64,64]{4,3,2,1,0:T(8,128)(2,1)}, u32[]{:S(2)}) copy-start(bf16[3,3,3,64,64]{4,3,2,1,0:T(8,128)(2,1)} %param.16) | copy-start | bytes 663556
  88.1 0.9 copy-start.36
  90.1 0.9 copy-start.19

commit v2 on v1

--- a/solution.py
+++ b/solution.py
@@ -220,7 +220,7 @@
     stencil(padded, table, False, store)
     whole = jnp.concatenate([cells[...].astype(F32), beside.astype(F32)], axis=1)
     lanes_out[...] = whole.T.astype(BF16)
-    cotangent_out[...] = dot(cotangent[...], turn[...], (0, 0))
+    cotangent_out[...] = dot(cotangent[...], turn[...], (0, 0)).astype(BF16)
 
 
 def diagonal_mask(rows, snaps):
@@ -272,7 +272,7 @@
     cdf = 0.5 * (1.0 + lax.erf(pre * inv_root_two))
     density = jnp.exp(-0.5 * pre * pre) * inv_root_two_pi
     activated_out[...] = (pre * cdf).astype(BF16)
-    grad = (cotangent[...] * (cdf + pre * density)).astype(BF16)
+    grad = (cotangent[...].astype(F32) * (cdf + pre * density)).astype(BF16)
     grad_out[...] = grad
     back = dot(synthesis_rows[...], grad)
     grad = grad.astype(F32)
@@ -314,18 +314,21 @@
 def slab_store(slab, modes, terms):
     owners = slab.shape[0]
     modes = modes.reshape(owners, 8, LANES)
-    slab[:, 0:16, :] = jnp.concatenate([modes, jnp.zeros_like(modes)], axis=1).astype(BF16)
-    slab[:, 16:, :] = terms.reshape(owners, -1, LANES).astype(BF16)
-
-
-def slab_modes(slab):
-    owners = slab.shape[0]
-    return slab[:, 0:16, :].astype(F32)[:, 0:8, :].reshape(owners * 8, LANES)
+    terms = terms.reshape(owners, -1, LANES)
+    slab[...] = jnp.concatenate([modes, terms], axis=1).astype(BF16)
+
+
+def slab_load(slab):
+    whole = slab[...].astype(F32)
+    return whole[:, 0:8, :].reshape(-1, LANES), whole[:, 8:, :]
 
 
 def unmix_kernel(snaps, scale, received, terms, gather, weights, scatter, grad_out, mixed_out, sums_out):
     in_slab = terms is None
-    modes = slab_modes(received) if in_slab else received[...].astype(F32)
+    if in_slab:
+        modes, terms = slab_load(received)
+    else:
+        modes, terms = received[...].astype(F32), terms[...].astype(F32)
     mixed = dot(gather[...], doubled(modes).astype(BF16)).astype(BF16)
     mixed_out[...] = mixed
     count = mixed.shape[0]
@@ -333,6 +336,7 @@
     depth = GROUP * LANES // 2
     own = diagonal_mask(rows, snaps)
     narrow = mixed[:, 0 : LANES // 2]
+    sums = jnp.sum(terms, axis=0) * scale
     pieces = []
     for g in range(count // rows):
         full = dot(
@@ -345,14 +349,13 @@
     grad = dot(scatter[...], halved(coef).astype(BF16))
     if in_slab:
         owners = received.shape[0]
-        sums = jnp.sum(received[:, 16:, :].astype(F32), axis=0) * scale
         share = sums.shape[0]
         slab_store(
             grad_out, grad, jnp.broadcast_to(sums[None], (owners, share, LANES)).reshape(-1, LANES)
         )
     else:
         grad_out[...] = grad.astype(BF16)
-        sums_out[...] = jnp.sum(terms[...].astype(F32), axis=0) * scale
+        sums_out[...] = sums
 
 
 def weight_kernel(snaps, diagonal, mixed, out):
@@ -380,13 +383,13 @@
 
 def finish_kernel(received, sums, synthesis, local, turn, grad_out, stencil_out):
     in_slab = sums is None
-    modes = slab_modes(received).astype(BF16) if in_slab else received[...]
-    cells = (dot(synthesis[...], modes) + local[...]).astype(BF16)
+    if in_slab:
+        modes, terms = slab_load(received)
+        terms = terms.reshape(TERM_ROWS, LANES)
+    else:
+        modes, terms = received[...], sums[...].astype(F32)
+    cells = (dot(synthesis[...], modes.astype(BF16)) + local[...]).astype(BF16)
     grad_out[...] = dot(turn[...], cells, (1, 1)).astype(BF16)
-    if in_slab:
-        terms = received[:, 16:, :].astype(F32).reshape(TERM_ROWS, LANES)
-    else:
-        terms = sums[...].astype(F32)
     half = LANES // 2
     for k in range(OFFSETS):
         row = (k // 2) * half
@@ -398,29 +401,95 @@
     return jax.ShapeDtypeStruct(dims, dtype)
 
 
-def run(body, outs, *operands, scratch=(), flops=0):
-    given = [operand for operand in operands if operand is not None]
+class Staged:
+    def __init__(self, source, buffer, semaphore):
+        self.copy = pltpu.make_async_copy(source, buffer, semaphore)
+        self.buffer = buffer
+        self.copy.start()
+        self.ready = False
+
+    def load(self):
+        if not self.ready:
+            self.copy.wait()
+            self.ready = True
+        return self.buffer
+
+    def __getitem__(self, index):
+        return self.load()[index]
+
+    @property
+    def shape(self):
+        return self.buffer.shape
+
+
+class Sent:
+    def __init__(self, target, buffer, semaphore):
+        self.copy = pltpu.make_async_copy(buffer, target, semaphore)
+        self.buffer = buffer
+
+    def __setitem__(self, index, value):
+        self.buffer[index] = value
+        self.copy.start()
+
+    @property
+    def shape(self):
+        return self.buffer.shape
+
+
+def run(body, outs, *operands, staged=(), sent=(), after=(), scratch=(), flops=0):
+    given = [k for k, operand in enumerate(operands) if operand is not None]
+    made = [k for k, out in enumerate(outs) if out is not None]
+    staged = [k for k in given if k in staged]
+    sent = [k for k in made if k in sent]
 
     def kernel(*refs):
         refs = list(refs)
-        filled = [None if operand is None else refs.pop(0) for operand in operands]
-        kept = [None if out is None else refs.pop(0) for out in outs]
-        body(*filled, *kept, *refs)
-
-    made = [out for out in outs if out is not None]
-    size = sum(x.size * x.dtype.itemsize for x in (*given, *made))
+
+        def take(count):
+            taken = refs[:count]
+            del refs[:count]
+            return taken
+
+        filled = dict(zip(given, take(len(given))))
+        take(len(after))
+        kept = dict(zip(made, take(len(made))))
+        own = take(len(scratch))
+        for place, (k, buffer) in enumerate(zip(staged, take(len(staged)))):
+            filled[k] = Staged(filled[k], buffer, refs[-1].at[place])
+        for place, (k, buffer) in enumerate(zip(sent, take(len(sent)))):
+            kept[k] = Sent(kept[k], buffer, refs[-1].at[len(staged) + place])
+        body(
+            *[filled.get(k) for k in range(len(operands))],
+            *[kept.get(k) for k in range(len(outs))],
+            *own,
+        )
+        for k in staged:
+            filled[k].load()
+        for k in sent:
+            kept[k].copy.wait()
+
+    arrays = [operands[k] for k in given]
+    results = [outs[k] for k in made]
+    size = sum(x.size * x.dtype.itemsize for x in (*arrays, *results))
+    in_vmem = pl.BlockSpec(memory_space=pltpu.VMEM)
+    anywhere = pl.BlockSpec(memory_space=pl.ANY)
+    in_hbm = pl.BlockSpec(memory_space=pltpu.HBM)
+    buffers = [operands[k] for k in staged] + [outs[k] for k in sent]
+    buffers = [pltpu.VMEM(x.shape, x.dtype) for x in buffers]
+    if buffers:
+        buffers.append(pltpu.SemaphoreType.DMA((len(buffers),)))
     results = pl.pallas_call(
         kernel,
-        out_shape=made,
-        in_specs=[pl.BlockSpec(memory_space=pltpu.VMEM)] * len(given),
-        out_specs=[pl.BlockSpec(memory_space=pltpu.VMEM)] * len(made),
-        scratch_shapes=list(scratch),
-        compiler_params=pltpu.CompilerParams(vmem_limit_bytes=40 * 1024 * 1024),
+        out_shape=results,
+        in_specs=[in_hbm if k in staged else in_vmem for k in given] + [anywhere] * len(after),
+        out_specs=[in_hbm if k in sent else in_vmem for k in made],
+        scratch_shapes=[*scratch, *buffers],
+        compiler_params=pltpu.CompilerParams(vmem_limit_bytes=24 * 1024 * 1024),
         cost_estimate=pl.CostEstimate(flops=flops, bytes_accessed=size, transcendentals=0),
         name=body.__name__ if hasattr(body, "__name__") else body.func.__name__,
-    )(*given)
-    results = list(results)
-    return [None if out is None else results.pop(0) for out in outs]
+    )(*arrays, *after)
+    results = dict(zip(made, results))
+    return [results.get(k) for k in range(len(outs))]
 
 
 def exchange(values):
@@ -463,19 +532,27 @@
         return exchange(values.reshape(devices, modes, LANES)).reshape(plane_rows, LANES)
 
     cells, coef, first, last = run(
-        analyse_kernel, [wide, plane_modes, edge, edge], field, turn, analysis, flops=10**8
+        analyse_kernel,
+        [wide, plane_modes, edge, edge],
+        field,
+        turn,
+        analysis,
+        staged=(1, 2),
+        sent=(1, 2, 3),
+        flops=10**8,
     )
     coef = send(coef)
     before, after = neighbours(first, last)
     local, lanes, outer_cells = run(
         local_kernel,
-        [shape((CELLS, LANES), F32), shape((2 * LANES, CELLS), BF16), shape((CELLS, LANES), F32)],
+        [shape((CELLS, LANES), F32), shape((2 * LANES, CELLS), BF16), wide],
         cells,
         before,
         after,
         outer,
         turn,
         taps,
+        staged=(4, 5),
         scratch=[padded, pltpu.VMEM((3, 2 * LANES, 3 * LANES), BF16)],
         flops=7 * 10**8,
     )
@@ -486,10 +563,12 @@
         gather,
         weights,
         scatter,
+        staged=(1, 2, 3),
+        sent=(0,),
         flops=4 * 10**8,
     )
     back = send(back)
-    slab = shape((devices, 16 + TERM_ROWS // devices, LANES), BF16)
+    slab = shape((devices, 8 + TERM_ROWS // devices, LANES), BF16)
     activated, grad, first, last, back, terms = run(
         functools.partial(activate_kernel, in_slab),
         [
@@ -506,6 +585,8 @@
         local,
         outer_cells,
         lanes,
+        staged=(1, 2),
+        sent=(2, 3, 4),
         scratch=[pltpu.VMEM((CELLS + 2 * NY, 3 * LANES), BF16)],
         flops=10**9,
     )
@@ -516,17 +597,12 @@
         terms = exchange(terms.reshape(devices, TERM_ROWS // devices, LANES))
     before, after = neighbours(first, last)
     (activated,) = run(
-        output_kernel, [shape((channels * layers, plane), BF16)], activated, turn, flops=10**8
-    )
-    (local,) = run(
-        local_grad_kernel,
-        [shape((CELLS, LANES), F32)],
-        grad,
-        before,
-        after,
-        taps,
-        scratch=[padded, pltpu.VMEM((3, 3 * LANES, 2 * LANES), BF16)],
-        flops=7 * 10**8,
+        output_kernel,
+        [shape((channels * layers, plane), BF16)],
+        activated,
+        turn,
+        staged=(1,),
+        flops=10**8,
     )
     scale = 1.0 / math.sqrt(batches * slabs * layers * plane)
     grad_modes, mixed_grad, sums = run(
@@ -541,6 +617,9 @@
         gather_back,
         weights,
         scatter_back,
+        staged=(2, 3, 4),
+        sent=(0,),
+        after=(before, after, activated),
         flops=4 * 10**8,
     )
     if in_slab:
@@ -548,6 +627,17 @@
     else:
         grad_modes = send(grad_modes)
         sums = lax.all_gather(sums, ("batch", "space"), axis=0, tiled=True)
+    (local,) = run(
+        local_grad_kernel,
+        [shape((CELLS, LANES), F32)],
+        grad,
+        before,
+        after,
+        taps,
+        staged=(3,),
+        scratch=[padded, pltpu.VMEM((3, 3 * LANES, 2 * LANES), BF16)],
+        flops=7 * 10**8,
+    )
     (mode_gradient,) = run(
         functools.partial(weight_kernel, batches),
         [shape((modes * 2 * KZ * channels, channels), F32)],
@@ -563,6 +653,7 @@
         np.ascontiguousarray(analysis.T),
         local,
         turn,
+        staged=(2, 4),
         flops=10**8,
     )
     return (

time: 98.4 us -> 95.3 us (0.968)
  the two profiles are of different devices: /device:TPU:17 before, /device:TPU:0 now
where the time goes in v2:
time: 95.3 us; the launch traced here: 93.9 us
  local copies, waits for them, and re-layouts  33.9 us (36%)
  starting transfers between devices  29.2 us (31%)
  Pallas kernels  19.8 us (21%)
  waiting for transfers between devices  10.1 us (11%)
    unnamed x72, local copies, waits for them, and re-layouts  30.2 us
    all_to_all x4, starting transfers between devices, exchange(): lax.all_to_all(values, ('batch', 'space'), split_axis=0, concat_axis=0, t...  21.8 us
    pallas_call x9, Pallas kernels, run(): pl.pallas_call(kernel, out_shape=results, in_specs=[in_hbm if k in staged...  19.8 us
    all_to_all x4, waiting for transfers between devices, exchange(): lax.all_to_all(values, ('batch', 'space'), split_axis=0, concat_axis=0, t...  8.7 us
    ppermute x2, starting transfers between devices, neighbours(): before = lax.ppermute(last, 'space', [(i, i + 1) for i in range(ends)])  4.91 us
    ppermute x2, starting transfers between devices, neighbours(): after = lax.ppermute(first, 'space', [(i + 1, i) for i in range(ends)])  2.57 us
  transfers between devices with their start and end apart: 8, of which 4 were waited for; matrix products, arithmetic and copies ran while one was open for 2% of the time, Pallas kernels for 11%

profile of v2, /device:TPU:0, one launch (start us, length us, event | category | flops | bytes accessed | tf_op | source)
XLA Modules:
  0.0 93.9 jit_solution(1526474571405570176)
XLA Ops:
  0.6 1.0 %reshape.44.refs_0_ = bf16[128,1024]{1,0:T(8,128)(2,1)S(1)} reshape(bf16[1,64,2,1024]{3,2,1,0:T(2,128)(2,1)} %param.13) | data formatting | bytes 524288 | tf_op jit(solution)/shard_map/reshape | solution.py:524
  1.7 0.0 copy-start.2
  1.7 1.0 %copy-done.2 = bf16[256,1024]{1,0:T(8,128)(2,1)S(1)} copy-done((bf16[256,1024]{1,0:T(8,128)(2,1)S(1)}, bf16[256,1024]{1,0:T(8,128)(2,1)}, u32[]{:S(2)}) %copy-start.2) | copy-done | bytes 524312
  2.7 0.8 copy-done.11
  3.5 1.5 %analyse_kernel.1 = (bf16[1024,128]{1,0:T(8,128)(2,1)S(1)}, bf16[256,128]{1,0:T(8,128)(2,1)}, bf16[512,128]{1,0:T(8,128)(2,1)}, bf16[512,128]{1,0:T(8,128)(2,1)}) custom-call(bf16[128,1024]{1,0:T(8,128)(2,1)S(1)} %reshape.44.refs_0_, bf16[128,128]{1,0:T(8,128)(2,1)S(1)} %copy-done.11, bf16[256,1024]{1,0:T(8,128)(2,1)S(1)} %copy-done.2), custom_call_target="tpu_custom_call" | custom-call | flops 100000000 | bytes 1409024 | tf_op jit(solution)/shard_map/analyse_kernel/pallas_call | solution.py:481
  5.0 0.0 copy-start.24
  5.0 0.7 copy-done.24
  5.7 7.3 %all-to-all-start = ((bf16[32,8,128]{2,1,0:T(8,128)(2,1)}), bf16[32,8,128]{2,1,0:T(8,128)(2,1)S(1)}, u32[]{:S(2)}, u32[]{:S(2)}) async-start(bf16[32,8,128]{2,1,0:T(8,128)(2,1)} %bitcast), calls=%async_computation | async-start | bytes 131072 | tf_op jit(solution)/shard_map/all_to_all | solution.py:496
  13.0 2.8 %collective-permute-start = (bf16[512,128]{1,0:T(8,128)(2,1)}, bf16[512,128]{1,0:T(8,128)(2,1)}, u32[]{:S(2)}, u32[]{:S(2)}) collective-permute-start(bf16[512,128]{1,0:T(8,128)(2,1)} %get-tuple-element.25), channel_id=1, source_target_pairs={{0,1},{1,2},{2,3},{3,4},{4,5},{5,6},{6,7},{7,8},{8,9},{9,10},{10,1... | collective-permute-start | bytes 393224 | tf_op jit(solution)/shard_map/ppermute | solution.py:501
  15.8 1.3 %collective-permute-start.1 = (bf16[512,128]{1,0:T(8,128)(2,1)}, bf16[512,128]{1,0:T(8,128)(2,1)}, u32[]{:S(2)}, u32[]{:S(2)}) collective-permute-start(bf16[512,128]{1,0:T(8,128)(2,1)} %get-tuple-element.26), channel_id=1, source_target_pairs={{1,0},{2,1},{3,2},{4,3},{5,4},{6,5},{7,6},{8,7},{9,8},{10,9},{11,1... | collective-permute-start | bytes 393224 | tf_op jit(solution)/shard_map/ppermute | solution.py:502
  17.1 3.3 %all-to-all-done = bf16[32,8,128]{2,1,0:T(8,128)(2,1)S(1)} async-done(((bf16[32,8,128]{2,1,0:T(8,128)(2,1)}), bf16[32,8,128]{2,1,0:T(8,128)(2,1)S(1)}, u32[]{:S(2)}, u32[]{:S(2)}) %all-to-all-start) | async-done | bytes 65568 | tf_op jit(solution)/shard_map/all_to_all | solution.py:496
  20.4 1.9 %copy-done = bf16[8,1,24,64,64]{4,3,2,1,0:T(8,128)(2,1)S(1)} copy-done((bf16[8,1,24,64,64]{4,3,2,1,0:T(8,128)(2,1)S(1)}, bf16[8,1,24,64,64]{4,3,2,1,0:T(8,128)(2,1)}, u32[]{:S(2)}) %copy-start) | copy-done | bytes 1572888
  22.3 1.0 %copy-done.8 = bf16[256,768]{1,0:T(8,128)(2,1)S(1)} copy-done((bf16[256,768]{1,0:T(8,128)(2,1)S(1)}, bf16[256,768]{1,0:T(8,128)(2,1)}, u32[]{:S(2)}) %copy-start.8) | copy-done | bytes 393240
  23.3 1.0 %copy-done.9 = bf16[384,512]{1,0:T(8,128)(2,1)S(1)} copy-done((bf16[384,512]{1,0:T(8,128)(2,1)S(1)}, bf16[384,512]{1,0:T(8,128)(2,1)}, u32[]{:S(2)}) %copy-start.9) | copy-done | bytes 393240
  24.3 2.6 %mix_kernel.1 = (bf16[256,128]{1,0:T(8,128)(2,1)}, bf16[384,512]{1,0:T(8,128)(2,1)S(1)}) custom-call(bf16[256,128]{1,0:T(8,128)(2,1)S(1)} %bitcast.12, bf16[384,512]{1,0:T(8,128)(2,1)S(1)} %copy-done.9, bf16[12288,64]{1,0:T(8,128)(2,1)S(1)} %bitcast.10, bf16[256,768]{1,0:T(8,128)(2,1)S(1)} %copy-done.8), custom_call_target="tpu_custom_call" | custom-call | flops 400000000 | bytes 2883584 | tf_op jit(solution)/shard_map/mix_kernel/pallas_call | solution.py:481
  27.0 0.7 copy-done.6
  27.7 4.0 %all-to-all-start.1 = ((bf16[32,8,128]{2,1,0:T(8,128)(2,1)}), bf16[32,8,128]{2,1,0:T(8,128)(2,1)S(1)}, u32[]{:S(2)}, u32[]{:S(2)}) async-start(bf16[32,8,128]{2,1,0:T(8,128)(2,1)} %bitcast.3), calls=%async_computation.1 | async-start | bytes 131072 | tf_op jit(solution)/shard_map/all_to_all | solution.py:496
  31.7 1.1 %reshape.50.refs_3_ = bf16[128,1024]{1,0:T(8,128)(2,1)S(1)} reshape(bf16[1,64,2,1024]{3,2,1,0:T(2,128)(2,1)} %param.14) | data formatting | bytes 524288 | tf_op jit(solution)/shard_map/reshape | solution.py:525
  32.8 0.0 copy-start.12
  32.8 0.7 copy-done.12
  33.6 1.0 %copy-done.22 = bf16[3,3,3,64,64]{4,3,2,1,0:T(8,128)(2,1)S(1)} copy-done((bf16[3,3,3,64,64]{4,3,2,1,0:T(8,128)(2,1)S(1)}, bf16[3,3,3,64,64]{4,3,2,1,0:T(8,128)(2,1)}, u32[]{:S(2)}) %copy-start.22) | copy-done | bytes 221208
  34.6 0.9 %copy-done.25 = bf16[1024,128]{1,0:T(8,128)(2,1)S(1)} copy-done((bf16[1024,128]{1,0:T(8,128)(2,1)S(1)}, bf16[1024,128]{1,0:T(8,128)(2,1)}, u32[]{:S(2)}) %copy-start.25) | copy-done | bytes 262168
  35.5 2.6 %local_kernel.1 = (f32[1024,128]{1,0:T(8,128)S(1)}, bf16[256,1024]{1,0:T(8,128)(2,1)S(1)}, bf16[1024,128]{1,0:T(8,128)(2,1)S(1)}) custom-call(bf16[1024,128]{1,0:T(8,128)(2,1)S(1)} %copy-done.25, bf16[512,128]{1,0:T(8,128)(2,1)} %collective-permute-done.refs_1_, bf16[512,128]{1,0:T(8,128)(2,1)} %collective-permute-done.1.refs_2_, ...), custom_call_target="tpu_custom_call" | custom-call | flops 700000000 | bytes 2351104 | tf_op jit(solution)/shard_map/local_kernel/pallas_call | solution.py:481
  38.2 0.0 copy-start.28
  38.2 0.8 copy-done.28
  39.0 0.8 copy-done.30
  39.8 0.7 copy-done.34
  40.5 1.0 %copy-done.26 = bf16[256,1024]{1,0:T(8,128)(2,1)S(1)} copy-done((bf16[256,1024]{1,0:T(8,128)(2,1)S(1)}, bf16[256,1024]{1,0:T(8,128)(2,1)}, u32[]{:S(2)}) %copy-start.26) | copy-done | bytes 524312
  41.5 1.0 %copy-done.27 = bf16[1024,256]{1,0:T(8,128)(2,1)S(1)} copy-done((bf16[1024,256]{1,0:T(8,128)(2,1)S(1)}, bf16[1024,256]{1,0:T(8,128)(2,1)}, u32[]{:S(2)}) %copy-start.27) | copy-done | bytes 524312
  42.6 1.0 %copy-done.29 = f32[1024,128]{1,0:T(8,128)S(1)} copy-done((f32[1024,128]{1,0:T(8,128)S(1)}, f32[1024,128]{1,0:T(8,128)}, u32[]{:S(2)}) %copy-start.29) | copy-done | bytes 524312
  43.6 1.0 %copy-done.31 = bf16[256,1024]{1,0:T(8,128)(2,1)S(1)} copy-done((bf16[256,1024]{1,0:T(8,128)(2,1)S(1)}, bf16[256,1024]{1,0:T(8,128)(2,1)}, u32[]{:S(2)}) %copy-start.31) | copy-done | bytes 524312
  44.6 0.9 %copy-done.35 = bf16[1024,128]{1,0:T(8,128)(2,1)S(1)} copy-done((bf16[1024,128]{1,0:T(8,128)(2,1)S(1)}, bf16[1024,128]{1,0:T(8,128)(2,1)}, u32[]{:S(2)}) %copy-start.35) | copy-done | bytes 262168
  45.6 2.6 %activate_kernel.1 = (bf16[1024,128]{1,0:T(8,128)(2,1)S(1)}, bf16[1024,128]{1,0:T(8,128)(2,1)S(1)}, bf16[512,128]{1,0:T(8,128)(2,1)}, bf16[512,128]{1,0:T(8,128)(2,1)}, bf16[32,40,128]{2,1,0:T(8,128)(2,1)}) custom-call(bf16[256,128]{1,0:T(8,128)(2,1)S(1)} %bitcast.13, bf16[1024,256]{1,0:T(8,128)(2,1)S(1)} %copy-done.27, bf16[256,1024]{1,0:T(8,128)(2,1)S(1)} %copy-done.26, ...), custom_call_target="tpu_custom_call" | custom-call | flops 1000000000 | bytes 3538944 | tf_op jit(solution)/shard_map/activate_kernel/pallas_call | solution.py:481
  48.2 0.0 copy-start.14
  48.2 0.7 copy-done.14
  48.9 0.7 copy-done.32
  49.6 5.9 %all-to-all-start.2 = ((bf16[32,40,128]{2,1,0:T(8,128)(2,1)}), bf16[32,40,128]{2,1,0:T(8,128)(2,1)}, u32[]{:S(2)}, u32[]{:S(2)}) async-start(bf16[32,40,128]{2,1,0:T(8,128)(2,1)} %get-tuple-element.31), calls=%async_computation.2 | async-start | bytes 655360 | tf_op jit(solution)/shard_map/all_to_all | solution.py:496
  55.6 2.1 %collective-permute-start.2 = (bf16[512,128]{1,0:T(8,128)(2,1)}, bf16[512,128]{1,0:T(8,128)(2,1)S(1)}, u32[]{:S(2)}, u32[]{:S(2)}) collective-permute-start(bf16[512,128]{1,0:T(8,128)(2,1)} %get-tuple-element.32), channel_id=1, source_target_pairs={{0,1},{1,2},{2,3},{3,4},{4,5},{5,6},{6,7},{7,8},{8,9},{9,10},{10,1... | collective-permute-start | bytes 393224 | tf_op jit(solution)/shard_map/ppermute | solution.py:501
  57.7 1.3 %collective-permute-start.3 = (bf16[512,128]{1,0:T(8,128)(2,1)}, bf16[512,128]{1,0:T(8,128)(2,1)S(1)}, u32[]{:S(2)}, u32[]{:S(2)}) collective-permute-start(bf16[512,128]{1,0:T(8,128)(2,1)} %get-tuple-element.33), channel_id=1, source_target_pairs={{1,0},{2,1},{3,2},{4,3},{5,4},{6,5},{7,6},{8,7},{9,8},{10,9},{11,1... | collective-permute-start | bytes 393224 | tf_op jit(solution)/shard_map/ppermute | solution.py:502
  59.0 0.0 copy-start.15
  59.0 0.9 %copy-done.15 = bf16[1024,128]{1,0:T(8,128)(2,1)S(1)} copy-done((bf16[1024,128]{1,0:T(8,128)(2,1)S(1)}, bf16[1024,128]{1,0:T(8,128)(2,1)}, u32[]{:S(2)}) %copy-start.15) | copy-done | bytes 262168
  59.9 0.2 output_kernel.1.refs_6_
  60.2 0.6 copy-done.16
  60.9 1.4 %collective-permute-done.3.refs_5_.refs_2_ = bf16[512,128]{1,0:T(8,128)(2,1)S(1)} collective-permute-done((bf16[512,128]{1,0:T(8,128)(2,1)}, bf16[512,128]{1,0:T(8,128)(2,1)S(1)}, u32[]{:S(2)}, u32[]{:S(2)}) %collective-permute-start.3) | collective-permute-done | bytes 131104 | tf_op jit(solution)/shard_map/ppermute | solution.py:502
  62.3 0.6 copy-done.19
  62.9 4.3 %all-to-all-done.2.refs_0_ = bf16[32,40,128]{2,1,0:T(8,128)(2,1)} async-done(((bf16[32,40,128]{2,1,0:T(8,128)(2,1)}), bf16[32,40,128]{2,1,0:T(8,128)(2,1)}, u32[]{:S(2)}, u32[]{:S(2)}) %all-to-all-start.2) | async-done | bytes 327712 | tf_op jit(solution)/shard_map/all_to_all | solution.py:496
  67.3 1.0 %copy-done.4 = bf16[256,768]{1,0:T(8,128)(2,1)S(1)} copy-done((bf16[256,768]{1,0:T(8,128)(2,1)S(1)}, bf16[256,768]{1,0:T(8,128)(2,1)}, u32[]{:S(2)}) %copy-start.4) | copy-done | bytes 393240
  68.2 1.0 %copy-done.5 = bf16[384,512]{1,0:T(8,128)(2,1)S(1)} copy-done((bf16[384,512]{1,0:T(8,128)(2,1)S(1)}, bf16[384,512]{1,0:T(8,128)(2,1)}, u32[]{:S(2)}) %copy-start.5) | copy-done | bytes 393240
  69.2 0.9 copy-done.17
  70.2 0.9 copy-done.20
  71.1 3.5 %unmix_kernel.1 = (bf16[32,40,128]{2,1,0:T(8,128)(2,1)S(1)}, bf16[384,128]{1,0:T(8,128)(2,1)S(1)}) custom-call(bf16[32,40,128]{2,1,0:T(8,128)(2,1)} %all-to-all-done.2.refs_0_, bf16[384,512]{1,0:T(8,128)(2,1)S(1)} %copy-done.5, bf16[12288,64]{1,0:T(8,128)(2,1)S(1)} %bitcast.11, bf16[256,768]{1,0:T(8,128)(2,1)S(1)} %copy-done.4, ...), custom_call_target="tpu_custom_call" | custom-call | flops 400000000 | bytes 3112960 | tf_op jit(solution)/shard_map/unmix_kernel/pallas_call | solution.py:481
  74.6 0.7 copy-done.10
  75.3 4.5 %all-to-all-start.3 = ((bf16[32,40,128]{2,1,0:T(8,128)(2,1)}), bf16[32,40,128]{2,1,0:T(8,128)(2,1)S(1)}, u32[]{:S(2)}, u32[]{:S(2)}) async-start(bf16[32,40,128]{2,1,0:T(8,128)(2,1)} %copy-done.10), calls=%async_computation.3 | async-start | bytes 655360 | tf_op jit(solution)/shard_map/all_to_all | solution.py:496
  79.8 0.8 reshape.52
  80.6 0.9 copy-done.18
  81.5 0.9 copy-done.21
  82.4 1.0 %copy-done.23 = bf16[3,3,3,64,64]{4,3,2,1,0:T(8,128)(2,1)S(1)} copy-done((bf16[3,3,3,64,64]{4,3,2,1,0:T(8,128)(2,1)S(1)}, bf16[3,3,3,64,64]{4,3,2,1,0:T(8,128)(2,1)}, u32[]{:S(2)}) %copy-start.23) | copy-done | bytes 221208
  83.4 0.9 %copy-done.33 = bf16[1024,128]{1,0:T(8,128)(2,1)S(1)} copy-done((bf16[1024,128]{1,0:T(8,128)(2,1)S(1)}, bf16[1024,128]{1,0:T(8,128)(2,1)}, u32[]{:S(2)}) %copy-start.33) | copy-done | bytes 262168
  84.4 1.3 %local_grad_kernel.1.refs_2_ = f32[1024,128]{1,0:T(8,128)S(1)} custom-call(bf16[1024,128]{1,0:T(8,128)(2,1)S(1)} %copy-done.33, bf16[512,128]{1,0:T(8,128)(2,1)S(1)} %copy-done.18, bf16[512,128]{1,0:T(8,128)(2,1)S(1)} %copy-done.21, bf16[27,64,64]{2,1,0:T(8,128)(2,1)S(1)} %bitcast.15), custom_call_target="tpu_custom_call" | custom-call | flops 700000000 | bytes 1269760 | tf_op jit(solution)/shard_map/local_grad_kernel/pallas_call | solution.py:481
  85.7 1.0 %copy-done.7 = bf16[384,512]{1,0:T(8,128)(2,1)S(1)} copy-done((bf16[384,512]{1,0:T(8,128)(2,1)S(1)}, bf16[384,512]{1,0:T(8,128)(2,1)}, u32[]{:S(2)}) %copy-start.7) | copy-done | bytes 393240
  86.7 3.7 %weight_kernel.1 = f32[12288,64]{1,0:T(8,128)} custom-call(bf16[384,512]{1,0:T(8,128)(2,1)S(1)} %copy-done.7, bf16[384,128]{1,0:T(8,128)(2,1)S(1)} %get-tuple-element.38.refs_1_), custom_call_target="tpu_custom_call" | custom-call | flops 400000000 | bytes 3637248 | tf_op jit(solution)/shard_map/weight_kernel/pallas_call | solution.py:481
  90.4 1.0 %all-to-all-done.3.refs_0_ = bf16[32,40,128]{2,1,0:T(8,128)(2,1)S(1)} async-done(((bf16[32,40,128]{2,1,0:T(8,128)(2,1)}), bf16[32,40,128]{2,1,0:T(8,128)(2,1)S(1)}, u32[]{:S(2)}, u32[]{:S(2)}) %all-to-all-start.3) | async-done | bytes 327712 | tf_op jit(solution)/shard_map/all_to_all | solution.py:496
  91.5 1.6 %finish_kernel.1 = (bf16[128,1024]{1,0:T(8,128)(2,1)S(1)}, f32[27,64,64]{2,1,0:T(8,128)}) custom-call(bf16[32,40,128]{2,1,0:T(8,128)(2,1)S(1)} %all-to-all-done.3.refs_0_, bf16[1024,256]{1,0:T(8,128)(2,1)S(1)} %copy-done.3, f32[1024,128]{1,0:T(8,128)S(1)} %local_grad_kernel.1.refs_2_, bf16[128,128]{1,0:T(8,128)(2,1)S(1)} %copy-done.13), custom_call_target="tpu_custom_call" | custom-call | flops 100000000 | bytes 2113536 | tf_op jit(solution)/shard_map/finish_kernel/pallas_call | solution.py:481
  93.1 0.8 reshape.53
  (37 shorter events, 0.1 us)
Async XLA Ops:
  1.7 1.0 %copy-start.2 = (bf16[256,1024]{1,0:T(8,128)(2,1)S(1)}, bf16[256,1024]{1,0:T(8,128)(2,1)}, u32[]{:S(2)}) copy-start(bf16[256,1024]{1,0:T(8,128)(2,1)} %constant.19.clone.refs_2_) | copy-start | bytes 1572868
  2.7 0.8 copy-start.11
  3.5 55.5 %copy-start.13 = (bf16[128,128]{1,0:T(8,128)(2,1)S(1)}, bf16[128,128]{1,0:T(8,128)(2,1)}, u32[]{:S(2)}) copy-start(bf16[128,128]{1,0:T(8,128)(2,1)} %constant.18.clone.refs_1_.refs_4_.refs_3_) | copy-start | bytes 98308
  5.0 0.7 copy-start.24
  5.7 14.7 %all-to-all-start = ((bf16[32,8,128]{2,1,0:T(8,128)(2,1)}), bf16[32,8,128]{2,1,0:T(8,128)(2,1)S(1)}, u32[]{:S(2)}, u32[]{:S(2)}) async-start(bf16[32,8,128]{2,1,0:T(8,128)(2,1)} %bitcast), calls=%async_computation | async-start | bytes 131072 | tf_op jit(solution)/shard_map/all_to_all | solution.py:496
  13.0 19.8 %collective-permute-start = (bf16[512,128]{1,0:T(8,128)(2,1)}, bf16[512,128]{1,0:T(8,128)(2,1)}, u32[]{:S(2)}, u32[]{:S(2)}) collective-permute-start(bf16[512,128]{1,0:T(8,128)(2,1)} %get-tuple-element.25), channel_id=1, source_target_pairs={{0,1},{1,2},{2,3},{3,4},{4,5},{5,6},{6,7},{7,8},{8,9},{9,10},{10,1... | collective-permute-start | bytes 393224 | tf_op jit(solution)/shard_map/ppermute | solution.py:501
  15.8 17.0 %collective-permute-start.1 = (bf16[512,128]{1,0:T(8,128)(2,1)}, bf16[512,128]{1,0:T(8,128)(2,1)}, u32[]{:S(2)}, u32[]{:S(2)}) collective-permute-start(bf16[512,128]{1,0:T(8,128)(2,1)} %get-tuple-element.26), channel_id=1, source_target_pairs={{1,0},{2,1},{3,2},{4,3},{5,4},{6,5},{7,6},{8,7},{9,8},{10,9},{11,1... | collective-permute-start | bytes 393224 | tf_op jit(solution)/shard_map/ppermute | solution.py:502
  20.4 1.9 %copy-start = (bf16[8,1,24,64,64]{4,3,2,1,0:T(8,128)(2,1)S(1)}, bf16[8,1,24,64,64]{4,3,2,1,0:T(8,128)(2,1)}, u32[]{:S(2)}) copy-start(bf16[8,1,24,64,64]{4,3,2,1,0:T(8,128)(2,1)} %param.15) | copy-start | bytes 4718596
  22.3 1.0 %copy-start.8 = (bf16[256,768]{1,0:T(8,128)(2,1)S(1)}, bf16[256,768]{1,0:T(8,128)(2,1)}, u32[]{:S(2)}) copy-start(bf16[256,768]{1,0:T(8,128)(2,1)} %constant.21.clone.refs_3_) | copy-start | bytes 1179652
  23.3 1.0 %copy-start.9 = (bf16[384,512]{1,0:T(8,128)(2,1)S(1)}, bf16[384,512]{1,0:T(8,128)(2,1)}, u32[]{:S(2)}) copy-start(bf16[384,512]{1,0:T(8,128)(2,1)} %constant.20.clone.refs_1_) | copy-start | bytes 1179652
  24.3 43.0 %copy-start.1 = (bf16[8,1,24,64,64]{4,3,2,1,0:T(8,128)(2,1)S(1)}, bf16[8,1,24,64,64]{4,3,2,1,0:T(8,128)(2,1)}, u32[]{:S(2)}) copy-start(bf16[8,1,24,64,64]{4,3,2,1,0:T(8,128)(2,1)} %param.15) | copy-start | bytes 4718596
  26.9 0.8 copy-start.6
  27.7 12.8 %all-to-all-start.1 = ((bf16[32,8,128]{2,1,0:T(8,128)(2,1)}), bf16[32,8,128]{2,1,0:T(8,128)(2,1)S(1)}, u32[]{:S(2)}, u32[]{:S(2)}) async-start(bf16[32,8,128]{2,1,0:T(8,128)(2,1)} %bitcast.3), calls=%async_computation.1 | async-start | bytes 131072 | tf_op jit(solution)/shard_map/all_to_all | solution.py:496
  32.8 0.8 copy-start.12
  33.6 1.0 %copy-start.22 = (bf16[3,3,3,64,64]{4,3,2,1,0:T(8,128)(2,1)S(1)}, bf16[3,3,3,64,64]{4,3,2,1,0:T(8,128)(2,1)}, u32[]{:S(2)}) copy-start(bf16[3,3,3,64,64]{4,3,2,1,0:T(8,128)(2,1)} %param.16) | copy-start | bytes 663556
  34.6 0.9 %copy-start.25 = (bf16[1024,128]{1,0:T(8,128)(2,1)S(1)}, bf16[1024,128]{1,0:T(8,128)(2,1)}, u32[]{:S(2)}) copy-start(bf16[1024,128]{1,0:T(8,128)(2,1)} %copy-done.24) | copy-start | bytes 786436
  38.2 0.8 copy-start.28
  39.0 0.8 copy-start.30
  39.8 0.7 copy-start.34
  40.5 1.0 %copy-start.26 = (bf16[256,1024]{1,0:T(8,128)(2,1)S(1)}, bf16[256,1024]{1,0:T(8,128)(2,1)}, u32[]{:S(2)}) copy-start(bf16[256,1024]{1,0:T(8,128)(2,1)} %constant.23.clone.refs_2_) | copy-start | bytes 1572868
  41.5 1.0 %copy-start.27 = (bf16[1024,256]{1,0:T(8,128)(2,1)S(1)}, bf16[1024,256]{1,0:T(8,128)(2,1)}, u32[]{:S(2)}) copy-start(bf16[1024,256]{1,0:T(8,128)(2,1)} %constant.22.clone.refs_1_) | copy-start | bytes 1572868
  42.5 1.0 %copy-start.29 = (f32[1024,128]{1,0:T(8,128)S(1)}, f32[1024,128]{1,0:T(8,128)}, u32[]{:S(2)}) copy-start(f32[1024,128]{1,0:T(8,128)} %copy-done.28) | copy-start | bytes 1572868
  43.6 1.0 %copy-start.31 = (bf16[256,1024]{1,0:T(8,128)(2,1)S(1)}, bf16[256,1024]{1,0:T(8,128)(2,1)}, u32[]{:S(2)}) copy-start(bf16[256,1024]{1,0:T(8,128)(2,1)} %copy-done.30) | copy-start | bytes 1572868
  44.6 0.9 %copy-start.35 = (bf16[1024,128]{1,0:T(8,128)(2,1)S(1)}, bf16[1024,128]{1,0:T(8,128)(2,1)}, u32[]{:S(2)}) copy-start(bf16[1024,128]{1,0:T(8,128)(2,1)} %copy-done.34) | copy-start | bytes 786436
  48.2 0.7 copy-start.14
  48.9 0.7 copy-start.32
  49.6 17.6 %all-to-all-start.2 = ((bf16[32,40,128]{2,1,0:T(8,128)(2,1)}), bf16[32,40,128]{2,1,0:T(8,128)(2,1)}, u32[]{:S(2)}, u32[]{:S(2)}) async-start(bf16[32,40,128]{2,1,0:T(8,128)(2,1)} %get-tuple-element.31), calls=%async_computation.2 | async-start | bytes 655360 | tf_op jit(solution)/shard_map/all_to_all | solution.py:496
  55.6 4.6 %collective-permute-start.2 = (bf16[512,128]{1,0:T(8,128)(2,1)}, bf16[512,128]{1,0:T(8,128)(2,1)S(1)}, u32[]{:S(2)}, u32[]{:S(2)}) collective-permute-start(bf16[512,128]{1,0:T(8,128)(2,1)} %get-tuple-element.32), channel_id=1, source_target_pairs={{0,1},{1,2},{2,3},{3,4},{4,5},{5,6},{6,7},{7,8},{8,9},{9,10},{10,1... | collective-permute-start | bytes 393224 | tf_op jit(solution)/shard_map/ppermute | solution.py:501
  57.7 4.6 %collective-permute-start.3 = (bf16[512,128]{1,0:T(8,128)(2,1)}, bf16[512,128]{1,0:T(8,128)(2,1)S(1)}, u32[]{:S(2)}, u32[]{:S(2)}) collective-permute-start(bf16[512,128]{1,0:T(8,128)(2,1)} %get-tuple-element.33), channel_id=1, source_target_pairs={{1,0},{2,1},{3,2},{4,3},{5,4},{6,5},{7,6},{8,7},{9,8},{10,9},{11,1... | collective-permute-start | bytes 393224 | tf_op jit(solution)/shard_map/ppermute | solution.py:502
  59.0 1.0 %copy-start.15 = (bf16[1024,128]{1,0:T(8,128)(2,1)S(1)}, bf16[1024,128]{1,0:T(8,128)(2,1)}, u32[]{:S(2)}) copy-start(bf16[1024,128]{1,0:T(8,128)(2,1)} %copy-done.14) | copy-start | bytes 786436
  60.2 0.7 copy-start.16
  62.3 0.7 copy-start.19
  67.2 1.0 %copy-start.4 = (bf16[256,768]{1,0:T(8,128)(2,1)S(1)}, bf16[256,768]{1,0:T(8,128)(2,1)}, u32[]{:S(2)}) copy-start(bf16[256,768]{1,0:T(8,128)(2,1)} %constant.25.clone.refs_3_) | copy-start | bytes 1179652
  68.2 1.0 %copy-start.5 = (bf16[384,512]{1,0:T(8,128)(2,1)S(1)}, bf16[384,512]{1,0:T(8,128)(2,1)}, u32[]{:S(2)}) copy-start(bf16[384,512]{1,0:T(8,128)(2,1)} %constant.24.clone.refs_1_) | copy-start | bytes 1179652
  69.2 0.9 copy-start.17
  70.1 0.9 copy-start.20
  74.6 0.7 copy-start.10
  75.3 16.2 %copy-start.3 = (bf16[1024,256]{1,0:T(8,128)(2,1)S(1)}, bf16[1024,256]{1,0:T(8,128)(2,1)}, u32[]{:S(2)}) copy-start(bf16[1024,256]{1,0:T(8,128)(2,1)} %constant.26.clone.refs_1_) | copy-start | bytes 1572868
  75.3 16.2 %all-to-all-start.3 = ((bf16[32,40,128]{2,1,0:T(8,128)(2,1)}), bf16[32,40,128]{2,1,0:T(8,128)(2,1)S(1)}, u32[]{:S(2)}, u32[]{:S(2)}) async-start(bf16[32,40,128]{2,1,0:T(8,128)(2,1)} %copy-done.10), calls=%async_computation.3 | async-start | bytes 655360 | tf_op jit(solution)/shard_map/all_to_all | solution.py:496
  80.6 0.9 copy-start.18
  81.5 0.9 copy-start.21
  82.4 1.0 %copy-start.23 = (bf16[3,3,3,64,64]{4,3,2,1,0:T(8,128)(2,1)S(1)}, bf16[3,3,3,64,64]{4,3,2,1,0:T(8,128)(2,1)}, u32[]{:S(2)}) copy-start(bf16[3,3,3,64,64]{4,3,2,1,0:T(8,128)(2,1)} %param.16) | copy-start | bytes 663556
  83.4 0.9 %copy-start.33 = (bf16[1024,128]{1,0:T(8,128)(2,1)S(1)}, bf16[1024,128]{1,0:T(8,128)(2,1)}, u32[]{:S(2)}) copy-start(bf16[1024,128]{1,0:T(8,128)(2,1)} %copy-done.32) | copy-start | bytes 786436
  85.7 1.0 %copy-start.7 = (bf16[384,512]{1,0:T(8,128)(2,1)S(1)}, bf16[384,512]{1,0:T(8,128)(2,1)}, u32[]{:S(2)}) copy-start(bf16[384,512]{1,0:T(8,128)(2,1)} %copy-done.6) | copy-start | bytes 1179652

commit v3 on v2

--- a/solution.py
+++ b/solution.py
@@ -20,6 +20,7 @@
 GROUP = 8
 OFFSETS = 27
 TERM_ROWS = 1024
+VMEM_BYTES = 65000 * 1024
 
 F32 = jnp.float32
 BF16 = jnp.bfloat16
@@ -484,7 +485,7 @@
         in_specs=[in_hbm if k in staged else in_vmem for k in given] + [anywhere] * len(after),
         out_specs=[in_hbm if k in sent else in_vmem for k in made],
         scratch_shapes=[*scratch, *buffers],
-        compiler_params=pltpu.CompilerParams(vmem_limit_bytes=24 * 1024 * 1024),
+        compiler_params=pltpu.CompilerParams(vmem_limit_bytes=VMEM_BYTES),
         cost_estimate=pl.CostEstimate(flops=flops, bytes_accessed=size, transcendentals=0),
         name=body.__name__ if hasattr(body, "__name__") else body.func.__name__,
     )(*arrays, *after)
@@ -537,8 +538,8 @@
         field,
         turn,
         analysis,
-        staged=(1, 2),
-        sent=(1, 2, 3),
+        staged=(0, 1, 2),
+        sent=(0, 1, 2, 3),
         flops=10**8,
     )
     coef = send(coef)
@@ -552,7 +553,8 @@
         outer,
         turn,
         taps,
-        staged=(4, 5),
+        staged=(0, 1, 2, 3, 4, 5),
+        sent=(1, 2),
         scratch=[padded, pltpu.VMEM((3, 2 * LANES, 3 * LANES), BF16)],
         flops=7 * 10**8,
     )
@@ -585,8 +587,8 @@
         local,
         outer_cells,
         lanes,
-        staged=(1, 2),
-        sent=(2, 3, 4),
+        staged=(1, 2, 3, 4, 5),
+        sent=(0, 1, 2, 3, 4),
         scratch=[pltpu.VMEM((CELLS + 2 * NY, 3 * LANES), BF16)],
         flops=10**9,
     )
@@ -601,7 +603,8 @@
         [shape((channels * layers, plane), BF16)],
         activated,
         turn,
-        staged=(1,),
+        staged=(0, 1),
+        sent=(0,),
         flops=10**8,
     )
     scale = 1.0 / math.sqrt(batches * slabs * layers * plane)
@@ -618,7 +621,7 @@
         weights,
         scatter_back,
         staged=(2, 3, 4),
-        sent=(0,),
+        sent=(0, 1),
         after=(before, after, activated),
         flops=4 * 10**8,
     )
@@ -634,7 +637,7 @@
         before,
         after,
         taps,
-        staged=(3,),
+        staged=(0, 1, 2, 3),
         scratch=[padded, pltpu.VMEM((3, 3 * LANES, 2 * LANES), BF16)],
         flops=7 * 10**8,
     )
@@ -643,6 +646,7 @@
         [shape((modes * 2 * KZ * channels, channels), F32)],
         diagonal,
         mixed_grad,
+        staged=(0, 1),
         flops=4 * 10**8,
     )
     input_gradient, conv_gradient = run(
@@ -653,7 +657,8 @@
         np.ascontiguousarray(analysis.T),
         local,
         turn,
-        staged=(2, 4),
+        staged=(2, 3, 4),
+        sent=(0,),
         flops=10**8,
     )
     return (

time: 95.3 us -> 89.2 us (0.936)
  local copies, waits for them, and re-layouts: 33.9 us -> 10.4 us
  Pallas kernels: 19.8 us -> 37.1 us
  waiting for transfers between devices: 10.1 us -> 12.4 us
  starting transfers between devices: 29.2 us -> 27.6 us
    unnamed x72 -> x14, local copies, waits for them, and re-layouts: 30.2 us -> 3.42 us
    pallas_call x9, Pallas kernels: 19.8 us -> 37.1 us  [run(): pl.pallas_call(kernel, out_shape=results, in_specs=[in_hbm if k in staged...]
    all_to_all x4, waiting for transfers between devices: 8.7 us -> 10.9 us  [exchange(): lax.all_to_all(values, ('batch', 'space'), split_axis=0, concat_axis=0, t...]
    all_to_all x4, starting transfers between devices: 21.8 us -> 20.7 us  [exchange(): lax.all_to_all(values, ('batch', 'space'), split_axis=0, concat_axis=0, t...]
  transfers between devices with their start and end apart: 8 -> 8, of which waited for: 4 -> 5; matrix products, arithmetic and copies ran while one was open for 2% -> 4% of each run, Pallas kernels for 11% -> 22%
where the time goes in v3:
time: 89.2 us; the launch traced here: 88.3 us
  Pallas kernels  37.1 us (42%)
  starting transfers between devices  27.6 us (31%)
  waiting for transfers between devices  12.4 us (14%)
  local copies, waits for them, and re-layouts  10.4 us (12%)
    pallas_call x9, Pallas kernels, run(): pl.pallas_call(kernel, out_shape=results, in_specs=[in_hbm if k in staged...  37.1 us
    all_to_all x4, starting transfers between devices, exchange(): lax.all_to_all(values, ('batch', 'space'), split_axis=0, concat_axis=0, t...  20.7 us
    all_to_all x4, waiting for transfers between devices, exchange(): lax.all_to_all(values, ('batch', 'space'), split_axis=0, concat_axis=0, t...  10.9 us
    ppermute x2, starting transfers between devices, neighbours(): before = lax.ppermute(last, 'space', [(i, i + 1) for i in range(ends)])  4.32 us
    unnamed x14, local copies, waits for them, and re-layouts  3.42 us
    ppermute x2, starting transfers between devices, neighbours(): after = lax.ppermute(first, 'space', [(i + 1, i) for i in range(ends)])  2.58 us
  transfers between devices with their start and end apart: 8, of which 5 were waited for; matrix products, arithmetic and copies ran while one was open for 4% of the time, Pallas kernels for 22%

profile of v3, /device:TPU:0, one launch (start us, length us, event | category | flops | bytes accessed | tf_op | source)
XLA Modules:
  0.0 88.3 jit_solution(18252301261866862720)
XLA Ops:
  0.6 1.8 %reshape.44.refs_0_ = bf16[128,1024]{1,0:T(8,128)(2,1)} reshape(bf16[1,64,2,1024]{3,2,1,0:T(2,128)(2,1)} %param.13) | data formatting | bytes 524288 | tf_op jit(solution)/shard_map/reshape | solution.py:525
  2.4 2.5 %analyse_kernel.1 = (bf16[1024,128]{1,0:T(8,128)(2,1)}, bf16[256,128]{1,0:T(8,128)(2,1)}, bf16[512,128]{1,0:T(8,128)(2,1)}, bf16[512,128]{1,0:T(8,128)(2,1)}) custom-call(bf16[128,1024]{1,0:T(8,128)(2,1)} %reshape.44.refs_0_, bf16[128,128]{1,0:T(8,128)(2,1)} %constant.18.clone.refs_1_.refs_4_.refs_3_, bf16[256,1024]{1,0:T(8,128)(2,1)} %constant.19.clone.refs_2_), custom_call_target="tpu_custom_call" | custom-call | flops 100000000 | bytes 1409024 | tf_op jit(solution)/shard_map/analyse_kernel/pallas_call | solution.py:482
  4.9 7.3 %all-to-all-start = ((bf16[32,8,128]{2,1,0:T(8,128)(2,1)}), bf16[32,8,128]{2,1,0:T(8,128)(2,1)S(1)}, u32[]{:S(2)}, u32[]{:S(2)}) async-start(bf16[32,8,128]{2,1,0:T(8,128)(2,1)} %bitcast.16), calls=%async_computation | async-start | bytes 131072 | tf_op jit(solution)/shard_map/all_to_all | solution.py:497
  12.2 2.2 %collective-permute-start = (bf16[512,128]{1,0:T(8,128)(2,1)}, bf16[512,128]{1,0:T(8,128)(2,1)S(1)}, u32[]{:S(2)}, u32[]{:S(2)}) collective-permute-start(bf16[512,128]{1,0:T(8,128)(2,1)} %get-tuple-element.25), channel_id=1, source_target_pairs={{0,1},{1,2},{2,3},{3,4},{4,5},{5,6},{6,7},{7,8},{8,9},{9,10},{10,1... | collective-permute-start | bytes 393224 | tf_op jit(solution)/shard_map/ppermute | solution.py:502
  14.4 1.3 %collective-permute-start.1 = (bf16[512,128]{1,0:T(8,128)(2,1)}, bf16[512,128]{1,0:T(8,128)(2,1)S(1)}, u32[]{:S(2)}, u32[]{:S(2)}) collective-permute-start(bf16[512,128]{1,0:T(8,128)(2,1)} %get-tuple-element.26), channel_id=1, source_target_pairs={{1,0},{2,1},{3,2},{4,3},{5,4},{6,5},{7,6},{8,7},{9,8},{10,9},{11,1... | collective-permute-start | bytes 393224 | tf_op jit(solution)/shard_map/ppermute | solution.py:503
  15.7 3.9 %all-to-all-done = bf16[32,8,128]{2,1,0:T(8,128)(2,1)S(1)} async-done(((bf16[32,8,128]{2,1,0:T(8,128)(2,1)}), bf16[32,8,128]{2,1,0:T(8,128)(2,1)S(1)}, u32[]{:S(2)}, u32[]{:S(2)}) %all-to-all-start) | async-done | bytes 65568 | tf_op jit(solution)/shard_map/all_to_all | solution.py:497
  19.6 0.0 copy-start.2
  19.6 0.6 copy-done.2
  20.2 5.2 %mix_kernel.1 = (bf16[256,128]{1,0:T(8,128)(2,1)}, bf16[384,512]{1,0:T(8,128)(2,1)}) custom-call(bf16[256,128]{1,0:T(8,128)(2,1)} %bitcast.13, bf16[384,512]{1,0:T(8,128)(2,1)} %constant.20.clone.refs_1_, bf16[12288,64]{1,0:T(8,128)(2,1)} %bitcast.10, bf16[256,768]{1,0:T(8,128)(2,1)} %constant.21.clone.refs_3_), custom_call_target="tpu_custom_call" | custom-call | flops 400000000 | bytes 2883584 | tf_op jit(solution)/shard_map/mix_kernel/pallas_call | solution.py:482
  25.5 4.0 %all-to-all-start.1 = ((bf16[32,8,128]{2,1,0:T(8,128)(2,1)}), bf16[32,8,128]{2,1,0:T(8,128)(2,1)S(1)}, u32[]{:S(2)}, u32[]{:S(2)}) async-start(bf16[32,8,128]{2,1,0:T(8,128)(2,1)} %bitcast.15), calls=%async_computation.1 | async-start | bytes 131072 | tf_op jit(solution)/shard_map/all_to_all | solution.py:497
  29.5 1.8 %reshape.50.refs_3_ = bf16[128,1024]{1,0:T(8,128)(2,1)} reshape(bf16[1,64,2,1024]{3,2,1,0:T(2,128)(2,1)} %param.14) | data formatting | bytes 524288 | tf_op jit(solution)/shard_map/reshape | solution.py:526
  31.2 0.0 collective-permute-done.refs_1_
  31.2 0.0 copy-start.5
  31.3 0.0 collective-permute-done.1.refs_2_
  31.3 0.0 copy-start.6
  31.3 0.6 copy-done.5
  31.9 0.1 copy-done.6
  32.0 4.5 %local_kernel.1 = (f32[1024,128]{1,0:T(8,128)}, bf16[256,1024]{1,0:T(8,128)(2,1)}, bf16[1024,128]{1,0:T(8,128)(2,1)}) custom-call(bf16[1024,128]{1,0:T(8,128)(2,1)} %get-tuple-element.24.refs_0_, bf16[512,128]{1,0:T(8,128)(2,1)} %copy-done.5, bf16[512,128]{1,0:T(8,128)(2,1)} %copy-done.6, bf16[128,1024]{1,0:T(8,128)(2,1)} %reshape.50.refs_3_, ...), custom_call_target="tpu_custom_call" | custom-call | flops 700000000 | bytes 2351104 | tf_op jit(solution)/shard_map/local_kernel/pallas_call | solution.py:482
  36.5 0.4 all-to-all-done.1
  36.9 0.0 copy-start.4
  36.9 0.6 copy-done.4
  37.5 5.1 %activate_kernel.1 = (bf16[1024,128]{1,0:T(8,128)(2,1)}, bf16[1024,128]{1,0:T(8,128)(2,1)}, bf16[512,128]{1,0:T(8,128)(2,1)}, bf16[512,128]{1,0:T(8,128)(2,1)}, bf16[32,40,128]{2,1,0:T(8,128)(2,1)}) custom-call(bf16[256,128]{1,0:T(8,128)(2,1)} %bitcast.14, bf16[1024,256]{1,0:T(8,128)(2,1)} %constant.22.clone.refs_1_, ...), custom_call_target="tpu_custom_call" | custom-call | flops 1000000000 | bytes 3538944 | tf_op jit(solution)/shard_map/activate_kernel/pallas_call | solution.py:482
  42.6 5.4 %all-to-all-start.2 = ((bf16[32,40,128]{2,1,0:T(8,128)(2,1)}), bf16[32,40,128]{2,1,0:T(8,128)(2,1)S(1)}, u32[]{:S(2)}, u32[]{:S(2)}) async-start(bf16[32,40,128]{2,1,0:T(8,128)(2,1)} %get-tuple-element.31), calls=%async_computation.2 | async-start | bytes 655360 | tf_op jit(solution)/shard_map/all_to_all | solution.py:497
  48.1 2.2 %collective-permute-start.2 = (bf16[512,128]{1,0:T(8,128)(2,1)}, bf16[512,128]{1,0:T(8,128)(2,1)S(1)}, u32[]{:S(2)}, u32[]{:S(2)}) collective-permute-start(bf16[512,128]{1,0:T(8,128)(2,1)} %get-tuple-element.32), channel_id=1, source_target_pairs={{0,1},{1,2},{2,3},{3,4},{4,5},{5,6},{6,7},{7,8},{8,9},{9,10},{10,1... | collective-permute-start | bytes 393224 | tf_op jit(solution)/shard_map/ppermute | solution.py:502
  50.3 1.3 %collective-permute-start.3 = (bf16[512,128]{1,0:T(8,128)(2,1)}, bf16[512,128]{1,0:T(8,128)(2,1)}, u32[]{:S(2)}, u32[]{:S(2)}) collective-permute-start(bf16[512,128]{1,0:T(8,128)(2,1)} %get-tuple-element.33), channel_id=1, source_target_pairs={{1,0},{2,1},{3,2},{4,3},{5,4},{6,5},{7,6},{8,7},{9,8},{10,9},{11,1... | collective-permute-start | bytes 393224 | tf_op jit(solution)/shard_map/ppermute | solution.py:503
  51.6 1.9 %output_kernel.1.refs_6_ = bf16[128,1024]{1,0:T(8,128)(2,1)} custom-call(bf16[1024,128]{1,0:T(8,128)(2,1)} %get-tuple-element.30.refs_0_, bf16[128,128]{1,0:T(8,128)(2,1)} %constant.18.clone.refs_1_.refs_4_.refs_3_), custom_call_target="tpu_custom_call" | custom-call | flops 100000000 | bytes 557056 | tf_op jit(solution)/shard_map/output_kernel/pallas_call | solution.py:482
  53.5 0.0 collective-permute-done.2.refs_4_.refs_1_
  53.5 0.0 copy-start.3
  53.5 1.5 %collective-permute-done.3.refs_5_.refs_2_ = bf16[512,128]{1,0:T(8,128)(2,1)} collective-permute-done((bf16[512,128]{1,0:T(8,128)(2,1)}, bf16[512,128]{1,0:T(8,128)(2,1)}, u32[]{:S(2)}, u32[]{:S(2)}) %collective-permute-start.3) | collective-permute-done | bytes 131104 | tf_op jit(solution)/shard_map/ppermute | solution.py:503
  55.0 4.8 %all-to-all-done.2.refs_0_ = bf16[32,40,128]{2,1,0:T(8,128)(2,1)S(1)} async-done(((bf16[32,40,128]{2,1,0:T(8,128)(2,1)}), bf16[32,40,128]{2,1,0:T(8,128)(2,1)S(1)}, u32[]{:S(2)}, u32[]{:S(2)}) %all-to-all-start.2) | async-done | bytes 327712 | tf_op jit(solution)/shard_map/all_to_all | solution.py:497
  59.8 0.0 copy-done.3
  59.8 0.0 copy-start
  59.8 0.7 copy-done
  60.5 5.2 %unmix_kernel.1 = (bf16[32,40,128]{2,1,0:T(8,128)(2,1)}, bf16[384,128]{1,0:T(8,128)(2,1)}) custom-call(bf16[32,40,128]{2,1,0:T(8,128)(2,1)} %copy-done, bf16[384,512]{1,0:T(8,128)(2,1)} %constant.24.clone.refs_1_, bf16[12288,64]{1,0:T(8,128)(2,1)} %bitcast.11, bf16[256,768]{1,0:T(8,128)(2,1)} %constant.25.clone.refs_3_, bf16[512,128]{1,0:T(8,128)(2,1)} %copy-done.3, ...), custom_call_target="tpu_custom_call" | custom-call | flops 400000000 | bytes 3112960 | tf_op jit(solution)/shard_map/unmix_kernel/pallas_call | solution.py:482
  65.7 3.9 %all-to-all-start.3 = ((bf16[32,40,128]{2,1,0:T(8,128)(2,1)}), bf16[32,40,128]{2,1,0:T(8,128)(2,1)S(1)}, u32[]{:S(2)}, u32[]{:S(2)}) async-start(bf16[32,40,128]{2,1,0:T(8,128)(2,1)} %get-tuple-element.34), calls=%async_computation.3 | async-start | bytes 655360 | tf_op jit(solution)/shard_map/all_to_all | solution.py:497
  69.6 1.8 %reshape.52 = bf16[1,64,2,1024]{3,2,1,0:T(2,128)(2,1)} reshape(bf16[128,1024]{1,0:T(8,128)(2,1)} %output_kernel.1.refs_6_) | data formatting | bytes 524288 | tf_op jit(solution)/shard_map/reshape | solution.py:665
  71.4 3.4 %local_grad_kernel.1.refs_2_ = f32[1024,128]{1,0:T(8,128)} custom-call(bf16[1024,128]{1,0:T(8,128)(2,1)} %get-tuple-element.35.refs_0_, bf16[512,128]{1,0:T(8,128)(2,1)} %copy-done.3, bf16[512,128]{1,0:T(8,128)(2,1)} %collective-permute-done.3.refs_5_.refs_2_, bf16[27,64,64]{2,1,0:T(8,128)(2,1)} %bitcast.19), custom_call_target="tpu_custom_call" | custom-call | flops 700000000 | bytes 1269760 | tf_op jit(solution)/shard_map/local_grad_kernel/pallas_call | solution.py:482
  74.8 4.8 %weight_kernel.1 = f32[12288,64]{1,0:T(8,128)} custom-call(bf16[384,512]{1,0:T(8,128)(2,1)} %get-tuple-element.37.refs_0_, bf16[384,128]{1,0:T(8,128)(2,1)} %get-tuple-element.38.refs_1_), custom_call_target="tpu_custom_call" | custom-call | flops 400000000 | bytes 3637248 | tf_op jit(solution)/shard_map/weight_kernel/pallas_call | solution.py:482
  79.5 1.8 %all-to-all-done.3.refs_0_ = bf16[32,40,128]{2,1,0:T(8,128)(2,1)S(1)} async-done(((bf16[32,40,128]{2,1,0:T(8,128)(2,1)}), bf16[32,40,128]{2,1,0:T(8,128)(2,1)S(1)}, u32[]{:S(2)}, u32[]{:S(2)}) %all-to-all-start.3) | async-done | bytes 327712 | tf_op jit(solution)/shard_map/all_to_all | solution.py:497
  81.3 0.0 copy-start.1
  81.3 0.7 copy-done.1
  82.1 4.5 %finish_kernel.1 = (bf16[128,1024]{1,0:T(8,128)(2,1)}, f32[27,64,64]{2,1,0:T(8,128)}) custom-call(bf16[32,40,128]{2,1,0:T(8,128)(2,1)} %copy-done.1, bf16[1024,256]{1,0:T(8,128)(2,1)} %constant.26.clone.refs_1_, f32[1024,128]{1,0:T(8,128)} %local_grad_kernel.1.refs_2_, bf16[128,128]{1,0:T(8,128)(2,1)} %constant.18.clone.refs_1_.refs_4_.refs_3_), custom_call_target="tpu_custom_call" | custom-call | flops 100000000 | bytes 2113536 | tf_op jit(solution)/shard_map/finish_kernel/pallas_call | solution.py:482
  86.6 1.8 %reshape.53 = bf16[1,64,2,1024]{3,2,1,0:T(2,128)(2,1)} reshape(bf16[128,1024]{1,0:T(8,128)(2,1)} %get-tuple-element.36) | data formatting | bytes 524288 | tf_op jit(solution)/shard_map/reshape | solution.py:666
Async XLA Ops:
  4.9 14.7 %all-to-all-start = ((bf16[32,8,128]{2,1,0:T(8,128)(2,1)}), bf16[32,8,128]{2,1,0:T(8,128)(2,1)S(1)}, u32[]{:S(2)}, u32[]{:S(2)}) async-start(bf16[32,8,128]{2,1,0:T(8,128)(2,1)} %bitcast.16), calls=%async_computation | async-start | bytes 131072 | tf_op jit(solution)/shard_map/all_to_all | solution.py:497
  12.2 19.1 %collective-permute-start = (bf16[512,128]{1,0:T(8,128)(2,1)}, bf16[512,128]{1,0:T(8,128)(2,1)S(1)}, u32[]{:S(2)}, u32[]{:S(2)}) collective-permute-start(bf16[512,128]{1,0:T(8,128)(2,1)} %get-tuple-element.25), channel_id=1, source_target_pairs={{0,1},{1,2},{2,3},{3,4},{4,5},{5,6},{6,7},{7,8},{8,9},{9,10},{10,1... | collective-permute-start | bytes 393224 | tf_op jit(solution)/shard_map/ppermute | solution.py:502
  14.4 16.9 %collective-permute-start.1 = (bf16[512,128]{1,0:T(8,128)(2,1)}, bf16[512,128]{1,0:T(8,128)(2,1)S(1)}, u32[]{:S(2)}, u32[]{:S(2)}) collective-permute-start(bf16[512,128]{1,0:T(8,128)(2,1)} %get-tuple-element.26), channel_id=1, source_target_pairs={{1,0},{2,1},{3,2},{4,3},{5,4},{6,5},{7,6},{8,7},{9,8},{10,9},{11,1... | collective-permute-start | bytes 393224 | tf_op jit(solution)/shard_map/ppermute | solution.py:503
  19.6 0.6 copy-start.2
  25.5 11.4 %all-to-all-start.1 = ((bf16[32,8,128]{2,1,0:T(8,128)(2,1)}), bf16[32,8,128]{2,1,0:T(8,128)(2,1)S(1)}, u32[]{:S(2)}, u32[]{:S(2)}) async-start(bf16[32,8,128]{2,1,0:T(8,128)(2,1)} %bitcast.15), calls=%async_computation.1 | async-start | bytes 131072 | tf_op jit(solution)/shard_map/all_to_all | solution.py:497
  31.2 0.6 copy-start.5
  31.3 0.7 copy-start.6
  36.9 0.6 copy-start.4
  42.6 17.1 %all-to-all-start.2 = ((bf16[32,40,128]{2,1,0:T(8,128)(2,1)}), bf16[32,40,128]{2,1,0:T(8,128)(2,1)S(1)}, u32[]{:S(2)}, u32[]{:S(2)}) async-start(bf16[32,40,128]{2,1,0:T(8,128)(2,1)} %get-tuple-element.31), calls=%async_computation.2 | async-start | bytes 655360 | tf_op jit(solution)/shard_map/all_to_all | solution.py:497
  48.1 5.4 %collective-permute-start.2 = (bf16[512,128]{1,0:T(8,128)(2,1)}, bf16[512,128]{1,0:T(8,128)(2,1)S(1)}, u32[]{:S(2)}, u32[]{:S(2)}) collective-permute-start(bf16[512,128]{1,0:T(8,128)(2,1)} %get-tuple-element.32), channel_id=1, source_target_pairs={{0,1},{1,2},{2,3},{3,4},{4,5},{5,6},{6,7},{7,8},{8,9},{9,10},{10,1... | collective-permute-start | bytes 393224 | tf_op jit(solution)/shard_map/ppermute | solution.py:502
  50.3 4.7 %collective-permute-start.3 = (bf16[512,128]{1,0:T(8,128)(2,1)}, bf16[512,128]{1,0:T(8,128)(2,1)}, u32[]{:S(2)}, u32[]{:S(2)}) collective-permute-start(bf16[512,128]{1,0:T(8,128)(2,1)} %get-tuple-element.33), channel_id=1, source_target_pairs={{1,0},{2,1},{3,2},{4,3},{5,4},{6,5},{7,6},{8,7},{9,8},{10,9},{11,1... | collective-permute-start | bytes 393224 | tf_op jit(solution)/shard_map/ppermute | solution.py:503
  53.5 6.3 %copy-start.3 = (bf16[512,128]{1,0:T(8,128)(2,1)}, bf16[512,128]{1,0:T(8,128)(2,1)S(1)}, u32[]{:S(2)}) copy-start(bf16[512,128]{1,0:T(8,128)(2,1)S(1)} %collective-permute-done.2.refs_4_.refs_1_) | copy-start | bytes 393220
  59.8 0.7 copy-start
  65.7 15.6 %all-to-all-start.3 = ((bf16[32,40,128]{2,1,0:T(8,128)(2,1)}), bf16[32,40,128]{2,1,0:T(8,128)(2,1)S(1)}, u32[]{:S(2)}, u32[]{:S(2)}) async-start(bf16[32,40,128]{2,1,0:T(8,128)(2,1)} %get-tuple-element.34), calls=%async_computation.3 | async-start | bytes 655360 | tf_op jit(solution)/shard_map/all_to_all | solution.py:497
  81.3 0.7 copy-start.1

commit v4 on v2

--- a/solution.py
+++ b/solution.py
@@ -20,6 +20,7 @@
 GROUP = 8
 OFFSETS = 27
 TERM_ROWS = 1024
+VMEM_BYTES = 63000 * 1024
 
 F32 = jnp.float32
 BF16 = jnp.bfloat16
@@ -73,6 +74,47 @@
     for layer in range(layers):
         table[np.arange(channels), layer, layer, np.arange(channels)] = 1.0
     return table.reshape(channels * layers, channels * layers).astype(ml_dtypes.bfloat16)
+
+
+class Piece:
+    def __init__(self, row, column, values):
+        self.index = (slice(row, row + values.shape[0]), slice(column, column + values.shape[1]))
+        self.shape = values.shape
+        self.dtype = BF16
+        self.values = values
+
+
+def join_tables(batches, slabs, layers, modes, channels):
+    analysis, synthesis = plane_tables(batches, slabs)
+    gather, scatter, gather_back, scatter_back = depth_tables(batches, slabs, layers, modes)
+    turn = interleave_table(channels, layers)
+    parts = {}
+    rows = [0]
+
+    def shelf(**named):
+        column = 0
+        for name, values in named.items():
+            parts[name] = Piece(rows[0], column, values)
+            column += values.shape[1]
+        rows[0] += max(values.shape[0] for values in named.values())
+
+    shelf(analysis=analysis)
+    shelf(synthesis=synthesis)
+    shelf(
+        synthesis_cells=synthesis.T,
+        analysis_cells=analysis.T,
+        gather=np.concatenate([gather, gather_back], axis=0),
+    )
+    both = parts.pop("gather")
+    first, column = both.index[0].start, both.index[1].start
+    parts["gather"] = Piece(first, column, gather)
+    parts["gather_back"] = Piece(first + gather.shape[0], column, gather_back)
+    shelf(scatter=scatter, turn=turn)
+    shelf(scatter_back=scatter_back)
+    joined = np.zeros((rows[0], 1024), ml_dtypes.bfloat16)
+    for part in parts.values():
+        joined[part.index] = part.values
+    return joined, parts
 
 
 def dot(left, right, contract=(1, 0)):
@@ -436,10 +478,11 @@
         return self.buffer.shape
 
 
-def run(body, outs, *operands, staged=(), sent=(), after=(), scratch=(), flops=0):
-    given = [k for k, operand in enumerate(operands) if operand is not None]
+def run(body, outs, *operands, tables=None, staged=(), sent=(), after=(), scratch=(), flops=0):
+    pieces = [k for k, operand in enumerate(operands) if isinstance(operand, Piece)]
+    given = [k for k, operand in enumerate(operands) if operand is not None and k not in pieces]
     made = [k for k, out in enumerate(outs) if out is not None]
-    staged = [k for k in given if k in staged]
+    staged = [k for k in range(len(operands)) if k in pieces or (k in given and k in staged)]
     sent = [k for k in made if k in sent]
 
     def kernel(*refs):
@@ -451,6 +494,10 @@
             return taken
 
         filled = dict(zip(given, take(len(given))))
+        if pieces:
+            joined = take(1)[0]
+            for k in pieces:
+                filled[k] = joined.at[operands[k].index]
         take(len(after))
         kept = dict(zip(made, take(len(made))))
         own = take(len(scratch))
@@ -481,13 +528,15 @@
     results = pl.pallas_call(
         kernel,
         out_shape=results,
-        in_specs=[in_hbm if k in staged else in_vmem for k in given] + [anywhere] * len(after),
+        in_specs=[in_hbm if k in staged else in_vmem for k in given]
+        + [in_hbm] * len(pieces[:1])
+        + [anywhere] * len(after),
         out_specs=[in_hbm if k in sent else in_vmem for k in made],
         scratch_shapes=[*scratch, *buffers],
-        compiler_params=pltpu.CompilerParams(vmem_limit_bytes=24 * 1024 * 1024),
+        compiler_params=pltpu.CompilerParams(vmem_limit_bytes=VMEM_BYTES),
         cost_estimate=pl.CostEstimate(flops=flops, bytes_accessed=size, transcendentals=0),
         name=body.__name__ if hasattr(body, "__name__") else body.func.__name__,
-    )(*arrays, *after)
+    )(*arrays, *([tables] if pieces else []), *after)
     results = dict(zip(made, results))
     return [results.get(k) for k in range(len(outs))]
 
@@ -515,10 +564,8 @@
     count = modes * 2 * KZ * batches
     in_slab = modes == 8 and devices * 32 == TERM_ROWS
 
-    analysis, synthesis = plane_tables(batches, slabs)
-    gather, scatter, gather_back, scatter_back = depth_tables(batches, slabs, layers, modes)
-    turn = interleave_table(channels, layers)
-
+    tables, parts = join_tables(batches, slabs, layers, modes, channels)
+    call = functools.partial(run, tables=tables)
     weights = mode_weight.reshape(modes * 2 * KZ * channels, channels)
     taps = conv_weight.reshape(OFFSETS, channels, channels)
     field = snapshots.reshape(channels * layers, plane)
@@ -531,45 +578,44 @@
     def send(values):
         return exchange(values.reshape(devices, modes, LANES)).reshape(plane_rows, LANES)
 
-    cells, coef, first, last = run(
+    cells, coef, first, last = call(
         analyse_kernel,
         [wide, plane_modes, edge, edge],
         field,
-        turn,
-        analysis,
-        staged=(1, 2),
+        parts["turn"],
+        parts["analysis"],
         sent=(1, 2, 3),
         flops=10**8,
     )
     coef = send(coef)
     before, after = neighbours(first, last)
-    local, lanes, outer_cells = run(
+    local, lanes, outer_cells = call(
         local_kernel,
         [shape((CELLS, LANES), F32), shape((2 * LANES, CELLS), BF16), wide],
         cells,
         before,
         after,
         outer,
-        turn,
+        parts["turn"],
         taps,
-        staged=(4, 5),
+        staged=(5,),
         scratch=[padded, pltpu.VMEM((3, 2 * LANES, 3 * LANES), BF16)],
         flops=7 * 10**8,
     )
-    back, diagonal = run(
+    back, diagonal = call(
         functools.partial(mix_kernel, batches),
         [plane_modes, shape((count, GROUP * half), BF16)],
         coef,
-        gather,
+        parts["gather"],
         weights,
-        scatter,
-        staged=(1, 2, 3),
+        parts["scatter"],
+        staged=(2,),
         sent=(0,),
         flops=4 * 10**8,
     )
     back = send(back)
     slab = shape((devices, 8 + TERM_ROWS // devices, LANES), BF16)
-    activated, grad, first, last, back, terms = run(
+    activated, grad, first, last, back, terms = call(
         functools.partial(activate_kernel, in_slab),
         [
             wide,
@@ -580,12 +626,11 @@
             None if in_slab else shape((TERM_ROWS, LANES), BF16),
         ],
         back,
-        np.ascontiguousarray(synthesis.T),
-        synthesis,
+        parts["synthesis_cells"],
+        parts["synthesis"],
         local,
         outer_cells,
         lanes,
-        staged=(1, 2),
         sent=(2, 3, 4),
         scratch=[pltpu.VMEM((CELLS + 2 * NY, 3 * LANES), BF16)],
         flops=10**9,
@@ -596,16 +641,16 @@
         back = send(back)
         terms = exchange(terms.reshape(devices, TERM_ROWS // devices, LANES))
     before, after = neighbours(first, last)
-    (activated,) = run(
+    (activated,) = call(
         output_kernel,
         [shape((channels * layers, plane), BF16)],
         activated,
-        turn,
-        staged=(1,),
+        parts["turn"],
         flops=10**8,
     )
+    back, before, after, activated = lax.optimization_barrier((back, before, after, activated))
     scale = 1.0 / math.sqrt(batches * slabs * layers * plane)
-    grad_modes, mixed_grad, sums = run(
+    grad_modes, mixed_grad, sums = call(
         functools.partial(unmix_kernel, batches, scale),
         [
             slab if in_slab else plane_modes,
@@ -614,12 +659,11 @@
         ],
         back,
         None if in_slab else terms,
-        gather_back,
+        parts["gather_back"],
         weights,
-        scatter_back,
-        staged=(2, 3, 4),
+        parts["scatter_back"],
+        staged=(3,),
         sent=(0,),
-        after=(before, after, activated),
         flops=4 * 10**8,
     )
     if in_slab:
@@ -627,7 +671,7 @@
     else:
         grad_modes = send(grad_modes)
         sums = lax.all_gather(sums, ("batch", "space"), axis=0, tiled=True)
-    (local,) = run(
+    (local,) = call(
         local_grad_kernel,
         [shape((CELLS, LANES), F32)],
         grad,
@@ -638,22 +682,21 @@
         scratch=[padded, pltpu.VMEM((3, 3 * LANES, 2 * LANES), BF16)],
         flops=7 * 10**8,
     )
-    (mode_gradient,) = run(
+    (mode_gradient,) = call(
         functools.partial(weight_kernel, batches),
         [shape((modes * 2 * KZ * channels, channels), F32)],
         diagonal,
         mixed_grad,
         flops=4 * 10**8,
     )
-    input_gradient, conv_gradient = run(
+    input_gradient, conv_gradient = call(
         finish_kernel,
         [shape((channels * layers, plane), BF16), shape((OFFSETS, channels, channels), F32)],
         grad_modes,
         sums,
-        np.ascontiguousarray(analysis.T),
+        parts["analysis_cells"],
         local,
-        turn,
-        staged=(2, 4),
+        parts["turn"],
         flops=10**8,
     )
     return (

time: 95.3 us -> 89.8 us (0.942)
  local copies, waits for them, and re-layouts: 33.9 us -> 8.53 us
  Pallas kernels: 19.8 us -> 40 us
  waiting for transfers between devices: 10.1 us -> 13.1 us
  starting transfers between devices: 29.2 us -> 26.3 us
    unnamed x72 -> x20, local copies, waits for them, and re-layouts: 30.2 us -> 3.42 us
    pallas_call x9, Pallas kernels: 19.8 us -> 40 us  [run(): pl.pallas_call(kernel, out_shape=results, in_specs=[in_hbm if k in staged...]
    all_to_all x4, waiting for transfers between devices: 8.7 us -> 12.5 us  [exchange(): lax.all_to_all(values, ('batch', 'space'), split_axis=0, concat_axis=0, t...]
    all_to_all x4, starting transfers between devices: 21.8 us -> 19.4 us  [exchange(): lax.all_to_all(values, ('batch', 'space'), split_axis=0, concat_axis=0, t...]
  transfers between devices with their start and end apart: 8 -> 8, of which waited for: 4 -> 5; matrix products, arithmetic and copies ran while one was open for 2% -> 2% of each run, Pallas kernels for 11% -> 24%
where the time goes in v4:
time: 89.8 us; the launch traced here: 88.8 us
  Pallas kernels  40 us (45%)
  starting transfers between devices  26.3 us (29%)
  waiting for transfers between devices  13.1 us (15%)
  local copies, waits for them, and re-layouts  8.53 us (9%)
    pallas_call x9, Pallas kernels, run(): pl.pallas_call(kernel, out_shape=results, in_specs=[in_hbm if k in staged...  40 us
    all_to_all x4, starting transfers between devices, exchange(): lax.all_to_all(values, ('batch', 'space'), split_axis=0, concat_axis=0, t...  19.4 us
    all_to_all x4, waiting for transfers between devices, exchange(): lax.all_to_all(values, ('batch', 'space'), split_axis=0, concat_axis=0, t...  12.5 us
    ppermute x2, starting transfers between devices, neighbours(): before = lax.ppermute(last, 'space', [(i, i + 1) for i in range(ends)])  4.32 us
    unnamed x20, local copies, waits for them, and re-layouts  3.42 us
    ppermute x2, starting transfers between devices, neighbours(): after = lax.ppermute(first, 'space', [(i + 1, i) for i in range(ends)])  2.58 us
  transfers between devices with their start and end apart: 8, of which 5 were waited for; matrix products, arithmetic and copies ran while one was open for 2% of the time, Pallas kernels for 24%

profile of v4, /device:TPU:0, one launch (start us, length us, event | category | flops | bytes accessed | tf_op | source)
XLA Modules:
  0.0 88.8 jit_solution(16676902686977113963)
XLA Ops:
  0.6 1.8 %reshape.44.refs_0_ = bf16[128,1024]{1,0:T(8,128)(2,1)} reshape(bf16[1,64,2,1024]{3,2,1,0:T(2,128)(2,1)} %param.5) | data formatting | bytes 524288 | tf_op jit(solution)/shard_map/reshape | solution.py:571
  2.4 3.8 %analyse_kernel.1 = (bf16[1024,128]{1,0:T(8,128)(2,1)}, bf16[256,128]{1,0:T(8,128)(2,1)}, bf16[512,128]{1,0:T(8,128)(2,1)}, bf16[512,128]{1,0:T(8,128)(2,1)}) custom-call(bf16[128,1024]{1,0:T(8,128)(2,1)} %reshape.44.refs_0_, bf16[2048,1024]{1,0:T(8,128)(2,1)} %constant.2.clone.refs_1_.refs_2_.refs_5_.refs_4_), custom_call_target="tpu_custom_call" | custom-call | flops 100000000 | bytes 851968 | tf_op jit(solution)/shard_map/analyse_kernel/pallas_call | solution.py:528
  6.2 0.0 copy-start.5
  6.2 7.3 %all-to-all-start = ((bf16[32,8,128]{2,1,0:T(8,128)(2,1)}), bf16[32,8,128]{2,1,0:T(8,128)(2,1)S(1)}, u32[]{:S(2)}, u32[]{:S(2)}) async-start(bf16[32,8,128]{2,1,0:T(8,128)(2,1)} %bitcast.18), calls=%async_computation | async-start | bytes 131072 | tf_op jit(solution)/shard_map/all_to_all | solution.py:545
  13.5 2.2 %collective-permute-start = (bf16[512,128]{1,0:T(8,128)(2,1)}, bf16[512,128]{1,0:T(8,128)(2,1)S(1)}, u32[]{:S(2)}, u32[]{:S(2)}) collective-permute-start(bf16[512,128]{1,0:T(8,128)(2,1)} %get-tuple-element.29), channel_id=1, source_target_pairs={{0,1},{1,2},{2,3},{3,4},{4,5},{5,6},{6,7},{7,8},{8,9},{9,10},{10,1... | collective-permute-start | bytes 393224 | tf_op jit(solution)/shard_map/ppermute | solution.py:550
  15.7 1.3 %collective-permute-start.1 = (bf16[512,128]{1,0:T(8,128)(2,1)}, bf16[512,128]{1,0:T(8,128)(2,1)S(1)}, u32[]{:S(2)}, u32[]{:S(2)}) collective-permute-start(bf16[512,128]{1,0:T(8,128)(2,1)} %get-tuple-element.30), channel_id=1, source_target_pairs={{1,0},{2,1},{3,2},{4,3},{5,4},{6,5},{7,6},{8,7},{9,8},{10,9},{11,1... | collective-permute-start | bytes 393224 | tf_op jit(solution)/shard_map/ppermute | solution.py:551
  17.0 3.9 %all-to-all-done = bf16[32,8,128]{2,1,0:T(8,128)(2,1)S(1)} async-done(((bf16[32,8,128]{2,1,0:T(8,128)(2,1)}), bf16[32,8,128]{2,1,0:T(8,128)(2,1)S(1)}, u32[]{:S(2)}, u32[]{:S(2)}) %all-to-all-start) | async-done | bytes 65568 | tf_op jit(solution)/shard_map/all_to_all | solution.py:545
  20.9 0.0 copy-start.4
  21.0 0.6 copy-done.4
  21.6 5.2 %mix_kernel.1 = (bf16[256,128]{1,0:T(8,128)(2,1)}, bf16[384,512]{1,0:T(8,128)(2,1)}) custom-call(bf16[256,128]{1,0:T(8,128)(2,1)} %bitcast.16, bf16[12288,64]{1,0:T(8,128)(2,1)} %bitcast.10, bf16[2048,1024]{1,0:T(8,128)(2,1)} %constant.2.clone.refs_1_.refs_2_.refs_5_.refs_4_), custom_call_target="tpu_custom_call" | custom-call | flops 400000000 | bytes 2097152 | tf_op jit(solution)/shard_map/mix_kernel/pallas_call | solution.py:528
  26.8 4.0 %all-to-all-start.1 = ((bf16[32,8,128]{2,1,0:T(8,128)(2,1)}), bf16[32,8,128]{2,1,0:T(8,128)(2,1)S(1)}, u32[]{:S(2)}, u32[]{:S(2)}) async-start(bf16[32,8,128]{2,1,0:T(8,128)(2,1)} %bitcast.17), calls=%async_computation.1 | async-start | bytes 131072 | tf_op jit(solution)/shard_map/all_to_all | solution.py:545
  30.8 0.0 copy-done.5
  30.8 0.8 reshape.50.refs_3_
  31.6 0.0 collective-permute-done.refs_1_
  31.6 0.0 copy-start.6
  31.6 0.0 collective-permute-done.1.refs_2_
  31.6 0.0 copy-start.7
  31.7 0.6 copy-done.6
  32.3 0.0 copy-done.7
  32.3 4.4 %local_kernel.1 = (f32[1024,128]{1,0:T(8,128)}, bf16[256,1024]{1,0:T(8,128)(2,1)}, bf16[1024,128]{1,0:T(8,128)(2,1)}) custom-call(bf16[1024,128]{1,0:T(8,128)(2,1)} %get-tuple-element.28.refs_0_, bf16[512,128]{1,0:T(8,128)(2,1)} %copy-done.6, bf16[512,128]{1,0:T(8,128)(2,1)} %copy-done.7, bf16[128,1024]{1,0:T(8,128)(2,1)} %reshape.50.refs_3_, ...), custom_call_target="tpu_custom_call" | custom-call | flops 700000000 | bytes 2318336 | tf_op jit(solution)/shard_map/local_kernel/pallas_call | solution.py:528
  36.7 1.5 %all-to-all-done.1 = bf16[32,8,128]{2,1,0:T(8,128)(2,1)S(1)} async-done(((bf16[32,8,128]{2,1,0:T(8,128)(2,1)}), bf16[32,8,128]{2,1,0:T(8,128)(2,1)S(1)}, u32[]{:S(2)}, u32[]{:S(2)}) %all-to-all-start.1) | async-done | bytes 65568 | tf_op jit(solution)/shard_map/all_to_all | solution.py:545
  38.2 0.0 copy-start.3
  38.2 0.6 copy-done.3
  38.9 5.7 %activate_kernel.1 = (bf16[1024,128]{1,0:T(8,128)(2,1)}, bf16[1024,128]{1,0:T(8,128)(2,1)}, bf16[512,128]{1,0:T(8,128)(2,1)}, bf16[512,128]{1,0:T(8,128)(2,1)}, bf16[32,40,128]{2,1,0:T(8,128)(2,1)}) custom-call(bf16[256,128]{1,0:T(8,128)(2,1)} %bitcast.15, f32[1024,128]{1,0:T(8,128)} %get-tuple-element.31.refs_1_, ...), custom_call_target="tpu_custom_call" | custom-call | flops 1000000000 | bytes 2490368 | tf_op jit(solution)/shard_map/activate_kernel/pallas_call | solution.py:528
  44.5 4.3 %all-to-all-start.2 = ((bf16[32,40,128]{2,1,0:T(8,128)(2,1)}), bf16[32,40,128]{2,1,0:T(8,128)(2,1)S(1)}, u32[]{:S(2)}, u32[]{:S(2)}) async-start(bf16[32,40,128]{2,1,0:T(8,128)(2,1)} %get-tuple-element.34), calls=%async_computation.2 | async-start | bytes 655360 | tf_op jit(solution)/shard_map/all_to_all | solution.py:545
  48.9 2.2 %collective-permute-start.2 = (bf16[512,128]{1,0:T(8,128)(2,1)}, bf16[512,128]{1,0:T(8,128)(2,1)S(1)}, u32[]{:S(2)}, u32[]{:S(2)}) collective-permute-start(bf16[512,128]{1,0:T(8,128)(2,1)} %get-tuple-element.35), channel_id=1, source_target_pairs={{0,1},{1,2},{2,3},{3,4},{4,5},{5,6},{6,7},{7,8},{8,9},{9,10},{10,1... | collective-permute-start | bytes 393224 | tf_op jit(solution)/shard_map/ppermute | solution.py:550
  51.1 1.3 %collective-permute-start.3 = (bf16[512,128]{1,0:T(8,128)(2,1)}, bf16[512,128]{1,0:T(8,128)(2,1)S(1)}, u32[]{:S(2)}, u32[]{:S(2)}) collective-permute-start(bf16[512,128]{1,0:T(8,128)(2,1)} %get-tuple-element.36), channel_id=1, source_target_pairs={{1,0},{2,1},{3,2},{4,3},{5,4},{6,5},{7,6},{8,7},{9,8},{10,9},{11,1... | collective-permute-start | bytes 393224 | tf_op jit(solution)/shard_map/ppermute | solution.py:551
  52.4 2.6 %output_kernel.1 = bf16[128,1024]{1,0:T(8,128)(2,1)} custom-call(bf16[1024,128]{1,0:T(8,128)(2,1)} %get-tuple-element.37.refs_0_, bf16[2048,1024]{1,0:T(8,128)(2,1)} %constant.2.clone.refs_1_.refs_2_.refs_5_.refs_4_), custom_call_target="tpu_custom_call" | custom-call | flops 100000000 | bytes 524288 | tf_op jit(solution)/shard_map/output_kernel/pallas_call | solution.py:528
  55.0 0.0 copy-start.2
  55.0 0.0 collective-permute-done.2.refs_1_
  55.0 0.0 copy-start.8
  55.1 0.6 collective-permute-done.3.refs_2_
  55.6 0.0 copy-start.9
  55.7 4.9 %all-to-all-done.2.refs_0_ = bf16[32,40,128]{2,1,0:T(8,128)(2,1)S(1)} async-done(((bf16[32,40,128]{2,1,0:T(8,128)(2,1)}), bf16[32,40,128]{2,1,0:T(8,128)(2,1)S(1)}, u32[]{:S(2)}, u32[]{:S(2)}) %all-to-all-start.2) | async-done | bytes 327712 | tf_op jit(solution)/shard_map/all_to_all | solution.py:545
  60.6 0.0 copy-start.1
  60.6 0.7 copy-done.1
  61.3 5.8 %unmix_kernel.1 = (bf16[32,40,128]{2,1,0:T(8,128)(2,1)}, bf16[384,128]{1,0:T(8,128)(2,1)}) custom-call(bf16[32,40,128]{2,1,0:T(8,128)(2,1)} %copy-done.1, bf16[12288,64]{1,0:T(8,128)(2,1)} %bitcast.11, bf16[2048,1024]{1,0:T(8,128)(2,1)} %constant.2.clone.refs_1_.refs_2_.refs_5_.refs_4_), custom_call_target="tpu_custom_call" | custom-call | flops 400000000 | bytes 2326528 | tf_op jit(solution)/shard_map/unmix_kernel/pallas_call | solution.py:528
  67.1 3.8 %all-to-all-start.3 = ((bf16[32,40,128]{2,1,0:T(8,128)(2,1)}), bf16[32,40,128]{2,1,0:T(8,128)(2,1)S(1)}, u32[]{:S(2)}, u32[]{:S(2)}) async-start(bf16[32,40,128]{2,1,0:T(8,128)(2,1)} %get-tuple-element.40), calls=%async_computation.3 | async-start | bytes 655360 | tf_op jit(solution)/shard_map/all_to_all | solution.py:545
  70.9 0.0 copy-done.2
  70.9 0.8 reshape.52
  71.7 4.7 %weight_kernel.1 = f32[12288,64]{1,0:T(8,128)} custom-call(bf16[384,512]{1,0:T(8,128)(2,1)} %get-tuple-element.45.refs_0_, bf16[384,128]{1,0:T(8,128)(2,1)} %get-tuple-element.46.refs_1_), custom_call_target="tpu_custom_call" | custom-call | flops 400000000 | bytes 3637248 | tf_op jit(solution)/shard_map/weight_kernel/pallas_call | solution.py:528
  76.4 0.0 copy-done.8
  76.4 0.0 copy-done.9
  76.4 4.0 %local_grad_kernel.1.refs_1_ = f32[1024,128]{1,0:T(8,128)} custom-call(bf16[1024,128]{1,0:T(8,128)(2,1)} %get-tuple-element.41.refs_0_, bf16[512,128]{1,0:T(8,128)(2,1)} %copy-done.8, bf16[512,128]{1,0:T(8,128)(2,1)} %copy-done.9, bf16[27,64,64]{2,1,0:T(8,128)(2,1)} %bitcast.14), custom_call_target="tpu_custom_call" | custom-call | flops 700000000 | bytes 1269760 | tf_op jit(solution)/shard_map/local_grad_kernel/pallas_call | solution.py:528
  80.4 2.2 %all-to-all-done.3.refs_0_ = bf16[32,40,128]{2,1,0:T(8,128)(2,1)S(1)} async-done(((bf16[32,40,128]{2,1,0:T(8,128)(2,1)}), bf16[32,40,128]{2,1,0:T(8,128)(2,1)S(1)}, u32[]{:S(2)}, u32[]{:S(2)}) %all-to-all-start.3) | async-done | bytes 327712 | tf_op jit(solution)/shard_map/all_to_all | solution.py:545
  82.6 0.0 copy-start
  82.6 0.7 copy-done
  83.3 3.8 %finish_kernel.1 = (bf16[128,1024]{1,0:T(8,128)(2,1)}, f32[27,64,64]{2,1,0:T(8,128)}) custom-call(bf16[32,40,128]{2,1,0:T(8,128)(2,1)} %copy-done, f32[1024,128]{1,0:T(8,128)} %local_grad_kernel.1.refs_1_, bf16[2048,1024]{1,0:T(8,128)(2,1)} %constant.2.clone.refs_1_.refs_2_.refs_5_.refs_4_), custom_call_target="tpu_custom_call" | custom-call | flops 100000000 | bytes 1556480 | tf_op jit(solution)/shard_map/finish_kernel/pallas_call | solution.py:528
  87.1 1.8 %reshape.53 = bf16[1,64,2,1024]{3,2,1,0:T(2,128)(2,1)} reshape(bf16[128,1024]{1,0:T(8,128)(2,1)} %get-tuple-element.44) | data formatting | bytes 524288 | tf_op jit(solution)/shard_map/reshape | solution.py:704
Async XLA Ops:
  6.2 24.6 %copy-start.5 = (bf16[1,64,2,1024]{3,2,1,0:T(2,128)(2,1)S(1)}, bf16[1,64,2,1024]{3,2,1,0:T(2,128)(2,1)}, u32[]{:S(2)}) copy-start(bf16[1,64,2,1024]{3,2,1,0:T(2,128)(2,1)} %param.6) | copy-start | bytes 786436
  6.2 14.7 %all-to-all-start = ((bf16[32,8,128]{2,1,0:T(8,128)(2,1)}), bf16[32,8,128]{2,1,0:T(8,128)(2,1)S(1)}, u32[]{:S(2)}, u32[]{:S(2)}) async-start(bf16[32,8,128]{2,1,0:T(8,128)(2,1)} %bitcast.18), calls=%async_computation | async-start | bytes 131072 | tf_op jit(solution)/shard_map/all_to_all | solution.py:545
  13.5 18.1 %collective-permute-start = (bf16[512,128]{1,0:T(8,128)(2,1)}, bf16[512,128]{1,0:T(8,128)(2,1)S(1)}, u32[]{:S(2)}, u32[]{:S(2)}) collective-permute-start(bf16[512,128]{1,0:T(8,128)(2,1)} %get-tuple-element.29), channel_id=1, source_target_pairs={{0,1},{1,2},{2,3},{3,4},{4,5},{5,6},{6,7},{7,8},{8,9},{9,10},{10,1... | collective-permute-start | bytes 393224 | tf_op jit(solution)/shard_map/ppermute | solution.py:550
  15.7 15.9 %collective-permute-start.1 = (bf16[512,128]{1,0:T(8,128)(2,1)}, bf16[512,128]{1,0:T(8,128)(2,1)S(1)}, u32[]{:S(2)}, u32[]{:S(2)}) collective-permute-start(bf16[512,128]{1,0:T(8,128)(2,1)} %get-tuple-element.30), channel_id=1, source_target_pairs={{1,0},{2,1},{3,2},{4,3},{5,4},{6,5},{7,6},{8,7},{9,8},{10,9},{11,1... | collective-permute-start | bytes 393224 | tf_op jit(solution)/shard_map/ppermute | solution.py:551
  20.9 0.6 copy-start.4
  26.8 11.4 %all-to-all-start.1 = ((bf16[32,8,128]{2,1,0:T(8,128)(2,1)}), bf16[32,8,128]{2,1,0:T(8,128)(2,1)S(1)}, u32[]{:S(2)}, u32[]{:S(2)}) async-start(bf16[32,8,128]{2,1,0:T(8,128)(2,1)} %bitcast.17), calls=%async_computation.1 | async-start | bytes 131072 | tf_op jit(solution)/shard_map/all_to_all | solution.py:545
  31.6 0.6 copy-start.6
  31.6 0.7 copy-start.7
  38.2 0.6 copy-start.3
  44.5 16.0 %all-to-all-start.2 = ((bf16[32,40,128]{2,1,0:T(8,128)(2,1)}), bf16[32,40,128]{2,1,0:T(8,128)(2,1)S(1)}, u32[]{:S(2)}, u32[]{:S(2)}) async-start(bf16[32,40,128]{2,1,0:T(8,128)(2,1)} %get-tuple-element.34), calls=%async_computation.2 | async-start | bytes 655360 | tf_op jit(solution)/shard_map/all_to_all | solution.py:545
  48.9 6.1 %collective-permute-start.2 = (bf16[512,128]{1,0:T(8,128)(2,1)}, bf16[512,128]{1,0:T(8,128)(2,1)S(1)}, u32[]{:S(2)}, u32[]{:S(2)}) collective-permute-start(bf16[512,128]{1,0:T(8,128)(2,1)} %get-tuple-element.35), channel_id=1, source_target_pairs={{0,1},{1,2},{2,3},{3,4},{4,5},{5,6},{6,7},{7,8},{8,9},{9,10},{10,1... | collective-permute-start | bytes 393224 | tf_op jit(solution)/shard_map/ppermute | solution.py:550
  51.1 4.6 %collective-permute-start.3 = (bf16[512,128]{1,0:T(8,128)(2,1)}, bf16[512,128]{1,0:T(8,128)(2,1)S(1)}, u32[]{:S(2)}, u32[]{:S(2)}) collective-permute-start(bf16[512,128]{1,0:T(8,128)(2,1)} %get-tuple-element.36), channel_id=1, source_target_pairs={{1,0},{2,1},{3,2},{4,3},{5,4},{6,5},{7,6},{8,7},{9,8},{10,9},{11,1... | collective-permute-start | bytes 393224 | tf_op jit(solution)/shard_map/ppermute | solution.py:551
  55.0 15.8 %copy-start.2 = (bf16[128,1024]{1,0:T(8,128)(2,1)S(1)}, bf16[128,1024]{1,0:T(8,128)(2,1)}, u32[]{:S(2)}) copy-start(bf16[128,1024]{1,0:T(8,128)(2,1)} %output_kernel.1) | copy-start | bytes 786436
  55.0 21.4 %copy-start.8 = (bf16[512,128]{1,0:T(8,128)(2,1)}, bf16[512,128]{1,0:T(8,128)(2,1)S(1)}, u32[]{:S(2)}) copy-start(bf16[512,128]{1,0:T(8,128)(2,1)S(1)} %collective-permute-done.2.refs_1_) | copy-start | bytes 393220
  55.6 20.8 %copy-start.9 = (bf16[512,128]{1,0:T(8,128)(2,1)}, bf16[512,128]{1,0:T(8,128)(2,1)S(1)}, u32[]{:S(2)}) copy-start(bf16[512,128]{1,0:T(8,128)(2,1)S(1)} %collective-permute-done.3.refs_2_) | copy-start | bytes 393220
  60.6 0.7 copy-start.1
  67.1 15.5 %all-to-all-start.3 = ((bf16[32,40,128]{2,1,0:T(8,128)(2,1)}), bf16[32,40,128]{2,1,0:T(8,128)(2,1)S(1)}, u32[]{:S(2)}, u32[]{:S(2)}) async-start(bf16[32,40,128]{2,1,0:T(8,128)(2,1)} %get-tuple-element.40), calls=%async_computation.3 | async-start | bytes 655360 | tf_op jit(solution)/shard_map/all_to_all | solution.py:545
  82.6 0.7 copy-start

commit v5 on v2

--- a/solution.py
+++ b/solution.py
@@ -20,6 +20,7 @@
 GROUP = 8
 OFFSETS = 27
 TERM_ROWS = 1024
+VMEM_BYTES = 40 * 1024 * 1024
 
 F32 = jnp.float32
 BF16 = jnp.bfloat16
@@ -223,21 +224,36 @@
     cotangent_out[...] = dot(cotangent[...], turn[...], (0, 0)).astype(BF16)
 
 
-def diagonal_mask(rows, snaps):
-    width = GROUP * LANES // 2
-    row = lax.broadcasted_iota(jnp.int32, (rows, width), 0)
+def pack_kernel(weights, out):
+    rows = GROUP * LANES // 4
+    for g in range(out.shape[0] // rows):
+        first = weights[2 * g * rows : (2 * g + 1) * rows, :]
+        second = weights[(2 * g + 1) * rows : (2 * g + 2) * rows, :]
+        out[g * rows : (g + 1) * rows, :] = jnp.concatenate([first, second], axis=1)
+
+
+def mode_in_group(rows, lanes, snaps):
+    return (lax.broadcasted_iota(jnp.int32, (rows, lanes), 0) // snaps) % GROUP
+
+
+def own_block(rows, snaps):
+    width = GROUP * LANES // 4
     lane = lax.broadcasted_iota(jnp.int32, (rows, width), 1)
-    return (row // snaps) % GROUP == lane // (LANES // 2)
+    return mode_in_group(rows, width, snaps) % (GROUP // 2) == lane // (LANES // 2)
+
+
+def own_half(rows, snaps):
+    return (mode_in_group(rows, LANES, snaps) < GROUP // 2) == low_lanes(rows)
 
 
 def mix_kernel(snaps, received, gather, weights, scatter, back_out, diagonal_out):
     both = doubled(received[...].astype(F32)).astype(BF16)
     coef = dot(gather[...], both)
     count = coef.shape[0]
-    wide = jnp.concatenate([coef] * (GROUP // 2), axis=1)
-    diagonal_out[...] = jnp.where(diagonal_mask(count, snaps), wide, 0.0).astype(BF16)
+    wide = jnp.concatenate([coef] * (GROUP // 4), axis=1)
+    diagonal_out[...] = jnp.where(own_block(count, snaps), wide, 0.0).astype(BF16)
     rows = GROUP * snaps
-    depth = GROUP * LANES // 2
+    depth = GROUP * LANES // 4
     mixed = jnp.concatenate(
         [
             dot(
@@ -248,8 +264,8 @@
         ],
         axis=0,
     )
-    mixed = halved(jnp.concatenate([mixed, mixed], axis=1)).astype(BF16)
-    back_out[...] = dot(scatter[...], mixed).astype(BF16)
+    mixed = jnp.where(own_half(count, snaps), mixed, swap_halves(mixed))
+    back_out[...] = dot(scatter[...], halved(mixed).astype(BF16)).astype(BF16)
 
 
 def activate_kernel(
@@ -329,18 +345,18 @@
         modes, terms = slab_load(received)
     else:
         modes, terms = received[...].astype(F32), terms[...].astype(F32)
-    mixed = dot(gather[...], doubled(modes).astype(BF16)).astype(BF16)
-    mixed_out[...] = mixed
+    mixed = dot(gather[...], doubled(modes).astype(BF16))
+    mixed_out[...] = mixed.astype(BF16)
     count = mixed.shape[0]
     rows = GROUP * snaps
-    depth = GROUP * LANES // 2
-    own = diagonal_mask(rows, snaps)
-    narrow = mixed[:, 0 : LANES // 2]
+    depth = GROUP * LANES // 4
     sums = jnp.sum(terms, axis=0) * scale
+    own = own_block(rows, snaps)
+    placed = jnp.where(own_half(count, snaps), mixed, 0.0).astype(BF16)
     pieces = []
     for g in range(count // rows):
         full = dot(
-            narrow[g * rows : (g + 1) * rows, :], weights[g * depth : (g + 1) * depth, :], (1, 1)
+            placed[g * rows : (g + 1) * rows, :], weights[g * depth : (g + 1) * depth, :], (1, 1)
         )
         full = jnp.where(own, full, 0.0)
         pieces.append(sum(full[:, k : k + LANES] for k in range(0, depth, LANES)))
@@ -360,11 +376,15 @@
 
 def weight_kernel(snaps, diagonal, mixed, out):
     rows = GROUP * snaps
-    depth = GROUP * LANES // 2
+    depth = GROUP * LANES // 4
     half = LANES // 2
+    first = mode_in_group(rows, depth, snaps) < GROUP // 2
     for g in range(diagonal.shape[0] // rows):
         span = slice(g * rows, (g + 1) * rows)
-        out[g * depth : (g + 1) * depth, :] = dot(diagonal[span, :], mixed[span, 0:half], (0, 0))
+        blocks = diagonal[span, :].astype(F32)
+        blocks = [jnp.where(first, blocks, 0.0), jnp.where(first, 0.0, blocks)]
+        blocks = jnp.concatenate(blocks, axis=1).astype(BF16)
+        out[2 * g * depth : 2 * (g + 1) * depth, :] = dot(blocks, mixed[span, 0:half], (0, 0))
 
 
 def output_kernel(cells, turn, out):
@@ -401,27 +421,6 @@
     return jax.ShapeDtypeStruct(dims, dtype)
 
 
-class Staged:
-    def __init__(self, source, buffer, semaphore):
-        self.copy = pltpu.make_async_copy(source, buffer, semaphore)
-        self.buffer = buffer
-        self.copy.start()
-        self.ready = False
-
-    def load(self):
-        if not self.ready:
-            self.copy.wait()
-            self.ready = True
-        return self.buffer
-
-    def __getitem__(self, index):
-        return self.load()[index]
-
-    @property
-    def shape(self):
-        return self.buffer.shape
-
-
 class Sent:
     def __init__(self, target, buffer, semaphore):
         self.copy = pltpu.make_async_copy(buffer, target, semaphore)
@@ -436,10 +435,9 @@
         return self.buffer.shape
 
 
-def run(body, outs, *operands, staged=(), sent=(), after=(), scratch=(), flops=0):
+def run(body, outs, *operands, sent=(), scratch=(), flops=0):
     given = [k for k, operand in enumerate(operands) if operand is not None]
     made = [k for k, out in enumerate(outs) if out is not None]
-    staged = [k for k in given if k in staged]
     sent = [k for k in made if k in sent]
 
     def kernel(*refs):
@@ -451,20 +449,15 @@
             return taken
 
         filled = dict(zip(given, take(len(given))))
-        take(len(after))
         kept = dict(zip(made, take(len(made))))
         own = take(len(scratch))
-        for place, (k, buffer) in enumerate(zip(staged, take(len(staged)))):
-            filled[k] = Staged(filled[k], buffer, refs[-1].at[place])
         for place, (k, buffer) in enumerate(zip(sent, take(len(sent)))):
-            kept[k] = Sent(kept[k], buffer, refs[-1].at[len(staged) + place])
+            kept[k] = Sent(kept[k], buffer, refs[-1].at[place])
         body(
             *[filled.get(k) for k in range(len(operands))],
             *[kept.get(k) for k in range(len(outs))],
             *own,
         )
-        for k in staged:
-            filled[k].load()
         for k in sent:
             kept[k].copy.wait()
 
@@ -472,22 +465,20 @@
     results = [outs[k] for k in made]
     size = sum(x.size * x.dtype.itemsize for x in (*arrays, *results))
     in_vmem = pl.BlockSpec(memory_space=pltpu.VMEM)
-    anywhere = pl.BlockSpec(memory_space=pl.ANY)
     in_hbm = pl.BlockSpec(memory_space=pltpu.HBM)
-    buffers = [operands[k] for k in staged] + [outs[k] for k in sent]
-    buffers = [pltpu.VMEM(x.shape, x.dtype) for x in buffers]
+    buffers = [pltpu.VMEM(outs[k].shape, outs[k].dtype) for k in sent]
     if buffers:
         buffers.append(pltpu.SemaphoreType.DMA((len(buffers),)))
     results = pl.pallas_call(
         kernel,
         out_shape=results,
-        in_specs=[in_hbm if k in staged else in_vmem for k in given] + [anywhere] * len(after),
+        in_specs=[in_vmem] * len(given),
         out_specs=[in_hbm if k in sent else in_vmem for k in made],
         scratch_shapes=[*scratch, *buffers],
-        compiler_params=pltpu.CompilerParams(vmem_limit_bytes=24 * 1024 * 1024),
+        compiler_params=pltpu.CompilerParams(vmem_limit_bytes=VMEM_BYTES),
         cost_estimate=pl.CostEstimate(flops=flops, bytes_accessed=size, transcendentals=0),
         name=body.__name__ if hasattr(body, "__name__") else body.func.__name__,
-    )(*arrays, *after)
+    )(*arrays)
     results = dict(zip(made, results))
     return [results.get(k) for k in range(len(outs))]
 
@@ -518,7 +509,6 @@
     analysis, synthesis = plane_tables(batches, slabs)
     gather, scatter, gather_back, scatter_back = depth_tables(batches, slabs, layers, modes)
     turn = interleave_table(channels, layers)
-
     weights = mode_weight.reshape(modes * 2 * KZ * channels, channels)
     taps = conv_weight.reshape(OFFSETS, channels, channels)
     field = snapshots.reshape(channels * layers, plane)
@@ -537,11 +527,12 @@
         field,
         turn,
         analysis,
-        staged=(1, 2),
         sent=(1, 2, 3),
         flops=10**8,
     )
+    weights, coef = lax.optimization_barrier((weights, coef))
     coef = send(coef)
+    (weights,) = run(pack_kernel, [shape((weights.shape[0] // 2, LANES), BF16)], weights)
     before, after = neighbours(first, last)
     local, lanes, outer_cells = run(
         local_kernel,
@@ -552,18 +543,16 @@
         outer,
         turn,
         taps,
-        staged=(4, 5),
         scratch=[padded, pltpu.VMEM((3, 2 * LANES, 3 * LANES), BF16)],
         flops=7 * 10**8,
     )
     back, diagonal = run(
         functools.partial(mix_kernel, batches),
-        [plane_modes, shape((count, GROUP * half), BF16)],
+        [plane_modes, shape((count, GROUP * half // 2), BF16)],
         coef,
         gather,
         weights,
         scatter,
-        staged=(1, 2, 3),
         sent=(0,),
         flops=4 * 10**8,
     )
@@ -585,7 +574,6 @@
         local,
         outer_cells,
         lanes,
-        staged=(1, 2),
         sent=(2, 3, 4),
         scratch=[pltpu.VMEM((CELLS + 2 * NY, 3 * LANES), BF16)],
         flops=10**9,
@@ -601,9 +589,9 @@
         [shape((channels * layers, plane), BF16)],
         activated,
         turn,
-        staged=(1,),
         flops=10**8,
     )
+    back, before, after, activated = lax.optimization_barrier((back, before, after, activated))
     scale = 1.0 / math.sqrt(batches * slabs * layers * plane)
     grad_modes, mixed_grad, sums = run(
         functools.partial(unmix_kernel, batches, scale),
@@ -617,9 +605,7 @@
         gather_back,
         weights,
         scatter_back,
-        staged=(2, 3, 4),
         sent=(0,),
-        after=(before, after, activated),
         flops=4 * 10**8,
     )
     if in_slab:
@@ -634,7 +620,6 @@
         before,
         after,
         taps,
-        staged=(3,),
         scratch=[padded, pltpu.VMEM((3, 3 * LANES, 2 * LANES), BF16)],
         flops=7 * 10**8,
     )
@@ -653,7 +638,6 @@
         np.ascontiguousarray(analysis.T),
         local,
         turn,
-        staged=(2, 4),
         flops=10**8,
     )
     return (

time: 95.3 us -> 81.7 us (0.86)
  local copies, waits for them, and re-layouts: 33.9 us -> 19.3 us
  Pallas kernels: 19.8 us -> 15.3 us
  waiting for transfers between devices: 10.1 us -> 14.3 us
  starting transfers between devices: 29.2 us -> 31 us
    unnamed x72 -> x54, local copies, waits for them, and re-layouts: 30.2 us -> 15.6 us
    pallas_call x9 -> x10, Pallas kernels: 19.8 us -> 15.3 us  [run(): pl.pallas_call(kernel, out_shape=results, in_specs=[in_vmem] * len(given)...]
    all_to_all x4, waiting for transfers between devices: 8.7 us -> 11.9 us  [exchange(): lax.all_to_all(values, ('batch', 'space'), split_axis=0, concat_axis=0, t...]
    all_to_all x4, starting transfers between devices: 21.8 us -> 24.1 us  [exchange(): lax.all_to_all(values, ('batch', 'space'), split_axis=0, concat_axis=0, t...]
    ppermute x2, waiting for transfers between devices: 1.4 us -> 2.38 us  [neighbours(): after = lax.ppermute(first, 'space', [(i + 1, i) for i in range(ends)])]
  transfers between devices with their start and end apart: 8 -> 8, of which waited for: 4 -> 4; matrix products, arithmetic and copies ran while one was open for 2% -> 2% of each run, Pallas kernels for 11% -> 10%
where the time goes in v5:
time: 81.7 us; the launch traced here: 80.8 us
  starting transfers between devices  31 us (38%)
  local copies, waits for them, and re-layouts  19.3 us (24%)
  Pallas kernels  15.3 us (19%)
  waiting for transfers between devices  14.3 us (18%)
  between operations  0.87 us (1%)
    all_to_all x4, starting transfers between devices, exchange(): lax.all_to_all(values, ('batch', 'space'), split_axis=0, concat_axis=0, t...  24.1 us
    unnamed x54, local copies, waits for them, and re-layouts  15.6 us
    pallas_call x10, Pallas kernels, run(): pl.pallas_call(kernel, out_shape=results, in_specs=[in_vmem] * len(given)...  15.3 us
    all_to_all x4, waiting for transfers between devices, exchange(): lax.all_to_all(values, ('batch', 'space'), split_axis=0, concat_axis=0, t...  11.9 us
    ppermute x2, starting transfers between devices, neighbours(): before = lax.ppermute(last, 'space', [(i, i + 1) for i in range(ends)])  4.32 us
    ppermute x2, starting transfers between devices, neighbours(): after = lax.ppermute(first, 'space', [(i + 1, i) for i in range(ends)])  2.58 us
    ppermute x2, waiting for transfers between devices, neighbours(): after = lax.ppermute(first, 'space', [(i + 1, i) for i in range(ends)])  2.38 us
  transfers between devices with their start and end apart: 8, of which 4 were waited for; matrix products, arithmetic and copies ran while one was open for 2% of the time, Pallas kernels for 10%

profile of v5, /device:TPU:0, one launch (start us, length us, event | category | flops | bytes accessed | tf_op | source)
XLA Modules:
  0.0 80.8 jit_solution(5198812336112329733)
XLA Ops:
  0.6 0.0 copy-start.3
  0.6 1.1 %reshape.45.refs_0_ = bf16[128,1024]{1,0:T(8,128)(2,1)S(1)} reshape(bf16[1,64,2,1024]{3,2,1,0:T(2,128)(2,1)} %param.13) | data formatting | bytes 524288 | tf_op jit(solution)/shard_map/reshape | solution.py:514
  1.7 0.0 copy-start.1
  1.8 1.0 %copy-done.1 = bf16[256,1024]{1,0:T(8,128)(2,1)S(1)} copy-done((bf16[256,1024]{1,0:T(8,128)(2,1)S(1)}, bf16[256,1024]{1,0:T(8,128)(2,1)}, u32[]{:S(2)}) %copy-start.1) | copy-done | bytes 524312
  2.8 0.8 copy-done.7
  3.6 1.2 %analyse_kernel.1 = (bf16[1024,128]{1,0:T(8,128)(2,1)S(1)}, bf16[256,128]{1,0:T(8,128)(2,1)}, bf16[512,128]{1,0:T(8,128)(2,1)S(1)}, bf16[512,128]{1,0:T(8,128)(2,1)S(1)}) custom-call(bf16[128,1024]{1,0:T(8,128)(2,1)S(1)} %reshape.45.refs_0_, bf16[128,128]{1,0:T(8,128)(2,1)S(1)} %copy-done.7, bf16[256,1024]{1,0:T(8,128)(2,1)S(1)} %copy-done.1), custom_call_target="tpu_custom_call" | custom-call | flops 100000000 | bytes 1409024 | tf_op jit(solution)/shard_map/analyse_kernel/pallas_call | solution.py:472
  4.7 7.3 %all-to-all-start = ((bf16[32,8,128]{2,1,0:T(8,128)(2,1)}), bf16[32,8,128]{2,1,0:T(8,128)(2,1)S(1)}, u32[]{:S(2)}, u32[]{:S(2)}) async-start(bf16[32,8,128]{2,1,0:T(8,128)(2,1)} %bitcast.1), calls=%async_computation | async-start | bytes 131072 | tf_op jit(solution)/shard_map/all_to_all | solution.py:487
  12.1 2.2 %collective-permute-start = (bf16[512,128]{1,0:T(8,128)(2,1)S(1)}, bf16[512,128]{1,0:T(8,128)(2,1)S(1)}, u32[]{:S(2)}, u32[]{:S(2)}) collective-permute-start(bf16[512,128]{1,0:T(8,128)(2,1)S(1)} %get-tuple-element.33), channel_id=1, source_target_pairs={{0,1},{1,2},{2,3},{3,4},{4,5},{5,6},{6,7},{7,8},{8,9},{9,10},{10,1... | collective-permute-start | bytes 393224 | tf_op jit(solution)/shard_map/ppermute | solution.py:492
  14.2 1.3 %collective-permute-start.1 = (bf16[512,128]{1,0:T(8,128)(2,1)S(1)}, bf16[512,128]{1,0:T(8,128)(2,1)S(1)}, u32[]{:S(2)}, u32[]{:S(2)}) collective-permute-start(bf16[512,128]{1,0:T(8,128)(2,1)S(1)} %get-tuple-element.34), channel_id=1, source_target_pairs={{1,0},{2,1},{3,2},{4,3},{5,4},{6,5},{7,6},{8,7},{9,8},{10,9},{11,1... | collective-permute-start | bytes 393224 | tf_op jit(solution)/shard_map/ppermute | solution.py:493
  15.5 0.0 copy-start
  15.5 1.9 %copy-done = bf16[8,1,24,64,64]{4,3,2,1,0:T(8,128)(2,1)S(1)} copy-done((bf16[8,1,24,64,64]{4,3,2,1,0:T(8,128)(2,1)S(1)}, bf16[8,1,24,64,64]{4,3,2,1,0:T(8,128)(2,1)}, u32[]{:S(2)}) %copy-start) | copy-done | bytes 1572888
  17.4 0.5 pack_kernel.1.refs_2_
  17.9 1.6 %all-to-all-done = bf16[32,8,128]{2,1,0:T(8,128)(2,1)S(1)} async-done(((bf16[32,8,128]{2,1,0:T(8,128)(2,1)}), bf16[32,8,128]{2,1,0:T(8,128)(2,1)S(1)}, u32[]{:S(2)}, u32[]{:S(2)}) %all-to-all-start) | async-done | bytes 65568 | tf_op jit(solution)/shard_map/all_to_all | solution.py:487
  19.5 0.0 copy-done.3
  19.5 0.0 copy-done.4
  19.5 1.6 %mix_kernel.1 = (bf16[256,128]{1,0:T(8,128)(2,1)}, bf16[384,256]{1,0:T(8,128)(2,1)S(1)}) custom-call(bf16[256,128]{1,0:T(8,128)(2,1)S(1)} %bitcast.11, bf16[384,512]{1,0:T(8,128)(2,1)S(1)} %copy-done.4, bf16[6144,128]{1,0:T(8,128)(2,1)S(1)} %pack_kernel.1.refs_2_, bf16[256,768]{1,0:T(8,128)(2,1)S(1)} %copy-done.3), custom_call_target="tpu_custom_call" | custom-call | flops 400000000 | bytes 2686976 | tf_op jit(solution)/shard_map/mix_kernel/pallas_call | solution.py:472
  21.1 6.4 %all-to-all-start.1 = ((bf16[32,8,128]{2,1,0:T(8,128)(2,1)}), bf16[32,8,128]{2,1,0:T(8,128)(2,1)S(1)}, u32[]{:S(2)}, u32[]{:S(2)}) async-start(bf16[32,8,128]{2,1,0:T(8,128)(2,1)} %bitcast.3), calls=%async_computation.1 | async-start | bytes 131072 | tf_op jit(solution)/shard_map/all_to_all | solution.py:487
  27.5 1.1 %reshape.50.refs_3_ = bf16[128,1024]{1,0:T(8,128)(2,1)S(1)} reshape(bf16[1,64,2,1024]{3,2,1,0:T(2,128)(2,1)} %param.14) | data formatting | bytes 524288 | tf_op jit(solution)/shard_map/reshape | solution.py:515
  28.6 0.0 collective-permute-done.refs_1_
  28.6 0.0 copy-start.15
  28.6 0.6 copy-done.15
  29.3 0.0 collective-permute-done.1.refs_2_
  29.3 0.7 copy-done.17
  29.9 0.0 copy-done.8
  29.9 1.0 %copy-done.9 = bf16[3,3,3,64,64]{4,3,2,1,0:T(8,128)(2,1)S(1)} copy-done((bf16[3,3,3,64,64]{4,3,2,1,0:T(8,128)(2,1)S(1)}, bf16[3,3,3,64,64]{4,3,2,1,0:T(8,128)(2,1)}, u32[]{:S(2)}) %copy-start.9) | copy-done | bytes 221208
  30.9 0.9 %copy-done.16 = bf16[512,128]{1,0:T(8,128)(2,1)S(1)} copy-done((bf16[512,128]{1,0:T(8,128)(2,1)S(1)}, bf16[512,128]{1,0:T(8,128)(2,1)}, u32[]{:S(2)}) %copy-start.16) | copy-done | bytes 131096
  31.8 0.9 %copy-done.18 = bf16[512,128]{1,0:T(8,128)(2,1)S(1)} copy-done((bf16[512,128]{1,0:T(8,128)(2,1)S(1)}, bf16[512,128]{1,0:T(8,128)(2,1)}, u32[]{:S(2)}) %copy-start.18) | copy-done | bytes 131096
  32.7 1.2 %local_kernel.1 = (f32[1024,128]{1,0:T(8,128)S(1)}, bf16[256,1024]{1,0:T(8,128)(2,1)S(1)}, bf16[1024,128]{1,0:T(8,128)(2,1)S(1)}) custom-call(bf16[1024,128]{1,0:T(8,128)(2,1)S(1)} %get-tuple-element.32.refs_0_, bf16[512,128]{1,0:T(8,128)(2,1)S(1)} %copy-done.16, bf16[512,128]{1,0:T(8,128)(2,1)S(1)} %copy-done.18, bf16[128,1024]{1,0:T(8,128)(2,1)S(1)} %reshape.50.refs_3_, ...), custom_call_target="tpu_custom_call" | custom-call | flops 700000000 | bytes 2351104 | tf_op jit(solution)/shard_map/local_kernel/pallas_call | solution.py:472
  33.9 0.0 copy-start.21
  33.9 0.8 copy-done.21
  34.7 0.8 copy-done.23
  35.5 0.0 all-to-all-done.1
  35.5 1.0 %copy-done.19 = bf16[256,1024]{1,0:T(8,128)(2,1)S(1)} copy-done((bf16[256,1024]{1,0:T(8,128)(2,1)S(1)}, bf16[256,1024]{1,0:T(8,128)(2,1)}, u32[]{:S(2)}) %copy-start.19) | copy-done | bytes 524312
  36.6 1.0 %copy-done.20 = bf16[1024,256]{1,0:T(8,128)(2,1)S(1)} copy-done((bf16[1024,256]{1,0:T(8,128)(2,1)S(1)}, bf16[1024,256]{1,0:T(8,128)(2,1)}, u32[]{:S(2)}) %copy-start.20) | copy-done | bytes 524312
  37.6 1.0 %copy-done.22 = f32[1024,128]{1,0:T(8,128)S(1)} copy-done((f32[1024,128]{1,0:T(8,128)S(1)}, f32[1024,128]{1,0:T(8,128)}, u32[]{:S(2)}) %copy-start.22) | copy-done | bytes 524312
  38.6 1.0 %copy-done.24 = bf16[256,1024]{1,0:T(8,128)(2,1)S(1)} copy-done((bf16[256,1024]{1,0:T(8,128)(2,1)S(1)}, bf16[256,1024]{1,0:T(8,128)(2,1)}, u32[]{:S(2)}) %copy-start.24) | copy-done | bytes 524312
  39.7 2.5 %activate_kernel.1 = (bf16[1024,128]{1,0:T(8,128)(2,1)S(1)}, bf16[1024,128]{1,0:T(8,128)(2,1)S(1)}, bf16[512,128]{1,0:T(8,128)(2,1)}, bf16[512,128]{1,0:T(8,128)(2,1)}, bf16[32,40,128]{2,1,0:T(8,128)(2,1)}) custom-call(bf16[256,128]{1,0:T(8,128)(2,1)S(1)} %bitcast.12, bf16[1024,256]{1,0:T(8,128)(2,1)S(1)} %copy-done.20, bf16[256,1024]{1,0:T(8,128)(2,1)S(1)} %copy-done.19, ...), custom_call_target="tpu_custom_call" | custom-call | flops 1000000000 | bytes 3538944 | tf_op jit(solution)/shard_map/activate_kernel/pallas_call | solution.py:472
  42.2 0.0 copy-start.25
  42.2 0.7 copy-done.25
  42.9 5.8 %all-to-all-start.2 = ((bf16[32,40,128]{2,1,0:T(8,128)(2,1)}), bf16[32,40,128]{2,1,0:T(8,128)(2,1)S(1)}, u32[]{:S(2)}, u32[]{:S(2)}) async-start(bf16[32,40,128]{2,1,0:T(8,128)(2,1)} %get-tuple-element.38), calls=%async_computation.2 | async-start | bytes 655360 | tf_op jit(solution)/shard_map/all_to_all | solution.py:487
  48.7 2.2 %collective-permute-start.2 = (bf16[512,128]{1,0:T(8,128)(2,1)}, bf16[512,128]{1,0:T(8,128)(2,1)S(1)}, u32[]{:S(2)}, u32[]{:S(2)}) collective-permute-start(bf16[512,128]{1,0:T(8,128)(2,1)} %get-tuple-element.39), channel_id=1, source_target_pairs={{0,1},{1,2},{2,3},{3,4},{4,5},{5,6},{6,7},{7,8},{8,9},{9,10},{10,1... | collective-permute-start | bytes 393224 | tf_op jit(solution)/shard_map/ppermute | solution.py:492
  50.9 1.3 %collective-permute-start.3 = (bf16[512,128]{1,0:T(8,128)(2,1)}, bf16[512,128]{1,0:T(8,128)(2,1)S(1)}, u32[]{:S(2)}, u32[]{:S(2)}) collective-permute-start(bf16[512,128]{1,0:T(8,128)(2,1)} %get-tuple-element.40), channel_id=1, source_target_pairs={{1,0},{2,1},{3,2},{4,3},{5,4},{6,5},{7,6},{8,7},{9,8},{10,9},{11,1... | collective-permute-start | bytes 393224 | tf_op jit(solution)/shard_map/ppermute | solution.py:493
  52.2 0.2 output_kernel.1
  52.5 0.0 collective-permute-done.2.refs_1_
  52.5 0.0 copy-start.11
  52.5 0.6 copy-done.11
  53.1 2.4 %collective-permute-done.3.refs_2_ = bf16[512,128]{1,0:T(8,128)(2,1)S(1)} collective-permute-done((bf16[512,128]{1,0:T(8,128)(2,1)}, bf16[512,128]{1,0:T(8,128)(2,1)S(1)}, u32[]{:S(2)}, u32[]{:S(2)}) %collective-permute-start.3) | collective-permute-done | bytes 131104 | tf_op jit(solution)/shard_map/ppermute | solution.py:493
  55.5 0.6 copy-done.13
  56.1 4.3 %all-to-all-done.2.refs_0_ = bf16[32,40,128]{2,1,0:T(8,128)(2,1)S(1)} async-done(((bf16[32,40,128]{2,1,0:T(8,128)(2,1)}), bf16[32,40,128]{2,1,0:T(8,128)(2,1)S(1)}, u32[]{:S(2)}, u32[]{:S(2)}) %all-to-all-start.2) | async-done | bytes 327712 | tf_op jit(solution)/shard_map/all_to_all | solution.py:487
  60.4 0.0 copy-done.5
  60.4 0.0 copy-done.6
  60.4 1.9 %unmix_kernel.1 = (bf16[32,40,128]{2,1,0:T(8,128)(2,1)}, bf16[384,128]{1,0:T(8,128)(2,1)S(1)}) custom-call(bf16[32,40,128]{2,1,0:T(8,128)(2,1)S(1)} %all-to-all-done.2.refs_0_, bf16[384,512]{1,0:T(8,128)(2,1)S(1)} %copy-done.6, bf16[6144,128]{1,0:T(8,128)(2,1)S(1)} %pack_kernel.1.refs_2_, bf16[256,768]{1,0:T(8,128)(2,1)S(1)} %copy-done.5), custom_call_target="tpu_custom_call" | custom-call | flops 400000000 | bytes 3112960 | tf_op jit(solution)/shard_map/unmix_kernel/pallas_call | solution.py:472
  62.4 4.6 %all-to-all-start.3 = ((bf16[32,40,128]{2,1,0:T(8,128)(2,1)}), bf16[32,40,128]{2,1,0:T(8,128)(2,1)S(1)}, u32[]{:S(2)}, u32[]{:S(2)}) async-start(bf16[32,40,128]{2,1,0:T(8,128)(2,1)} %get-tuple-element.44), calls=%async_computation.3 | async-start | bytes 655360 | tf_op jit(solution)/shard_map/all_to_all | solution.py:487
  67.0 0.8 reshape.52
  67.8 0.0 copy-start.2
  67.8 3.7 %weight_kernel.1 = f32[12288,64]{1,0:T(8,128)} custom-call(bf16[384,256]{1,0:T(8,128)(2,1)S(1)} %get-tuple-element.49.refs_0_, bf16[384,128]{1,0:T(8,128)(2,1)S(1)} %get-tuple-element.50.refs_1_), custom_call_target="tpu_custom_call" | custom-call | flops 400000000 | bytes 3440640 | tf_op jit(solution)/shard_map/weight_kernel/pallas_call | solution.py:472
  71.5 0.0 copy-done.10
  71.5 0.0 copy-done.12
  71.5 0.0 copy-done.14
  71.5 0.0 copy-done.26
  71.6 1.1 %local_grad_kernel.1.refs_2_ = f32[1024,128]{1,0:T(8,128)S(1)} custom-call(bf16[1024,128]{1,0:T(8,128)(2,1)S(1)} %copy-done.26, bf16[512,128]{1,0:T(8,128)(2,1)S(1)} %copy-done.12, bf16[512,128]{1,0:T(8,128)(2,1)S(1)} %copy-done.14, bf16[27,64,64]{2,1,0:T(8,128)(2,1)S(1)} %bitcast.14), custom_call_target="tpu_custom_call" | custom-call | flops 700000000 | bytes 1269760 | tf_op jit(solution)/shard_map/local_grad_kernel/pallas_call | solution.py:472
  72.6 6.0 %all-to-all-done.3.refs_0_ = bf16[32,40,128]{2,1,0:T(8,128)(2,1)S(1)} async-done(((bf16[32,40,128]{2,1,0:T(8,128)(2,1)}), bf16[32,40,128]{2,1,0:T(8,128)(2,1)S(1)}, u32[]{:S(2)}, u32[]{:S(2)}) %all-to-all-start.3) | async-done | bytes 327712 | tf_op jit(solution)/shard_map/all_to_all | solution.py:487
  78.7 1.4 %finish_kernel.1 = (bf16[128,1024]{1,0:T(8,128)(2,1)S(1)}, f32[27,64,64]{2,1,0:T(8,128)}) custom-call(bf16[32,40,128]{2,1,0:T(8,128)(2,1)S(1)} %all-to-all-done.3.refs_0_, bf16[1024,256]{1,0:T(8,128)(2,1)S(1)} %copy-done.2, f32[1024,128]{1,0:T(8,128)S(1)} %local_grad_kernel.1.refs_2_, bf16[128,128]{1,0:T(8,128)(2,1)S(1)} %copy-done.8), custom_call_target="tpu_custom_call" | custom-call | flops 100000000 | bytes 2113536 | tf_op jit(solution)/shard_map/finish_kernel/pallas_call | solution.py:472
  80.0 0.8 reshape.53
  (20 shorter events, 0.0 us)
Async XLA Ops:
  0.6 18.8 %copy-start.3 = (bf16[256,768]{1,0:T(8,128)(2,1)S(1)}, bf16[256,768]{1,0:T(8,128)(2,1)}, u32[]{:S(2)}) copy-start(bf16[256,768]{1,0:T(8,128)(2,1)} %constant.21.clone.refs_3_) | copy-start | bytes 1179652
  1.7 1.0 %copy-start.1 = (bf16[256,1024]{1,0:T(8,128)(2,1)S(1)}, bf16[256,1024]{1,0:T(8,128)(2,1)}, u32[]{:S(2)}) copy-start(bf16[256,1024]{1,0:T(8,128)(2,1)} %constant.19.clone.refs_2_) | copy-start | bytes 1572868
  2.8 0.8 copy-start.7
  3.5 15.9 %copy-start.4 = (bf16[384,512]{1,0:T(8,128)(2,1)S(1)}, bf16[384,512]{1,0:T(8,128)(2,1)}, u32[]{:S(2)}) copy-start(bf16[384,512]{1,0:T(8,128)(2,1)} %constant.20.clone.refs_1_) | copy-start | bytes 1179652
  4.7 14.7 %all-to-all-start = ((bf16[32,8,128]{2,1,0:T(8,128)(2,1)}), bf16[32,8,128]{2,1,0:T(8,128)(2,1)S(1)}, u32[]{:S(2)}, u32[]{:S(2)}) async-start(bf16[32,8,128]{2,1,0:T(8,128)(2,1)} %bitcast.1), calls=%async_computation | async-start | bytes 131072 | tf_op jit(solution)/shard_map/all_to_all | solution.py:487
  12.1 16.5 %collective-permute-start = (bf16[512,128]{1,0:T(8,128)(2,1)S(1)}, bf16[512,128]{1,0:T(8,128)(2,1)S(1)}, u32[]{:S(2)}, u32[]{:S(2)}) collective-permute-start(bf16[512,128]{1,0:T(8,128)(2,1)S(1)} %get-tuple-element.33), channel_id=1, source_target_pairs={{0,1},{1,2},{2,3},{3,4},{4,5},{5,6},{6,7},{7,8},{8,9},{9,10},{10,1... | collective-permute-start | bytes 393224 | tf_op jit(solution)/shard_map/ppermute | solution.py:492
  14.2 15.0 %collective-permute-start.1 = (bf16[512,128]{1,0:T(8,128)(2,1)S(1)}, bf16[512,128]{1,0:T(8,128)(2,1)S(1)}, u32[]{:S(2)}, u32[]{:S(2)}) collective-permute-start(bf16[512,128]{1,0:T(8,128)(2,1)S(1)} %get-tuple-element.34), channel_id=1, source_target_pairs={{1,0},{2,1},{3,2},{4,3},{5,4},{6,5},{7,6},{8,7},{9,8},{10,9},{11,1... | collective-permute-start | bytes 393224 | tf_op jit(solution)/shard_map/ppermute | solution.py:493
  15.5 1.9 %copy-start = (bf16[8,1,24,64,64]{4,3,2,1,0:T(8,128)(2,1)S(1)}, bf16[8,1,24,64,64]{4,3,2,1,0:T(8,128)(2,1)}, u32[]{:S(2)}) copy-start(bf16[8,1,24,64,64]{4,3,2,1,0:T(8,128)(2,1)} %param.15) | copy-start | bytes 4718596
  17.4 12.5 %copy-start.8 = (bf16[128,128]{1,0:T(8,128)(2,1)S(1)}, bf16[128,128]{1,0:T(8,128)(2,1)}, u32[]{:S(2)}) copy-start(bf16[128,128]{1,0:T(8,128)(2,1)} %constant.18.clone.refs_1_.refs_4_.refs_3_) | copy-start | bytes 98308
  21.1 14.4 %all-to-all-start.1 = ((bf16[32,8,128]{2,1,0:T(8,128)(2,1)}), bf16[32,8,128]{2,1,0:T(8,128)(2,1)S(1)}, u32[]{:S(2)}, u32[]{:S(2)}) async-start(bf16[32,8,128]{2,1,0:T(8,128)(2,1)} %bitcast.3), calls=%async_computation.1 | async-start | bytes 131072 | tf_op jit(solution)/shard_map/all_to_all | solution.py:487
  28.6 0.7 copy-start.15
  29.3 0.7 copy-start.17
  29.9 1.0 %copy-start.9 = (bf16[3,3,3,64,64]{4,3,2,1,0:T(8,128)(2,1)S(1)}, bf16[3,3,3,64,64]{4,3,2,1,0:T(8,128)(2,1)}, u32[]{:S(2)}) copy-start(bf16[3,3,3,64,64]{4,3,2,1,0:T(8,128)(2,1)} %param.16) | copy-start | bytes 663556
  30.9 0.9 %copy-start.16 = (bf16[512,128]{1,0:T(8,128)(2,1)S(1)}, bf16[512,128]{1,0:T(8,128)(2,1)}, u32[]{:S(2)}) copy-start(bf16[512,128]{1,0:T(8,128)(2,1)} %copy-done.15) | copy-start | bytes 393220
  31.8 0.9 %copy-start.18 = (bf16[512,128]{1,0:T(8,128)(2,1)S(1)}, bf16[512,128]{1,0:T(8,128)(2,1)}, u32[]{:S(2)}) copy-start(bf16[512,128]{1,0:T(8,128)(2,1)} %copy-done.17) | copy-start | bytes 393220
  32.7 27.7 %copy-start.5 = (bf16[256,768]{1,0:T(8,128)(2,1)S(1)}, bf16[256,768]{1,0:T(8,128)(2,1)}, u32[]{:S(2)}) copy-start(bf16[256,768]{1,0:T(8,128)(2,1)} %constant.25.clone.refs_3_) | copy-start | bytes 1179652
  32.7 27.7 %copy-start.6 = (bf16[384,512]{1,0:T(8,128)(2,1)S(1)}, bf16[384,512]{1,0:T(8,128)(2,1)}, u32[]{:S(2)}) copy-start(bf16[384,512]{1,0:T(8,128)(2,1)} %constant.24.clone.refs_1_) | copy-start | bytes 1179652
  33.9 0.8 copy-start.21
  34.7 0.8 copy-start.23
  35.5 1.0 %copy-start.19 = (bf16[256,1024]{1,0:T(8,128)(2,1)S(1)}, bf16[256,1024]{1,0:T(8,128)(2,1)}, u32[]{:S(2)}) copy-start(bf16[256,1024]{1,0:T(8,128)(2,1)} %constant.23.clone.refs_2_) | copy-start | bytes 1572868
  36.6 1.0 %copy-start.20 = (bf16[1024,256]{1,0:T(8,128)(2,1)S(1)}, bf16[1024,256]{1,0:T(8,128)(2,1)}, u32[]{:S(2)}) copy-start(bf16[1024,256]{1,0:T(8,128)(2,1)} %constant.22.clone.refs_1_) | copy-start | bytes 1572868
  37.6 1.0 %copy-start.22 = (f32[1024,128]{1,0:T(8,128)S(1)}, f32[1024,128]{1,0:T(8,128)}, u32[]{:S(2)}) copy-start(f32[1024,128]{1,0:T(8,128)} %copy-done.21) | copy-start | bytes 1572868
  38.6 1.0 %copy-start.24 = (bf16[256,1024]{1,0:T(8,128)(2,1)S(1)}, bf16[256,1024]{1,0:T(8,128)(2,1)}, u32[]{:S(2)}) copy-start(bf16[256,1024]{1,0:T(8,128)(2,1)} %copy-done.23) | copy-start | bytes 1572868
  42.2 0.7 copy-start.25
  42.9 17.5 %all-to-all-start.2 = ((bf16[32,40,128]{2,1,0:T(8,128)(2,1)}), bf16[32,40,128]{2,1,0:T(8,128)(2,1)S(1)}, u32[]{:S(2)}, u32[]{:S(2)}) async-start(bf16[32,40,128]{2,1,0:T(8,128)(2,1)} %get-tuple-element.38), calls=%async_computation.2 | async-start | bytes 655360 | tf_op jit(solution)/shard_map/all_to_all | solution.py:487
  48.7 3.7 %collective-permute-start.2 = (bf16[512,128]{1,0:T(8,128)(2,1)}, bf16[512,128]{1,0:T(8,128)(2,1)S(1)}, u32[]{:S(2)}, u32[]{:S(2)}) collective-permute-start(bf16[512,128]{1,0:T(8,128)(2,1)} %get-tuple-element.39), channel_id=1, source_target_pairs={{0,1},{1,2},{2,3},{3,4},{4,5},{5,6},{6,7},{7,8},{8,9},{9,10},{10,1... | collective-permute-start | bytes 393224 | tf_op jit(solution)/shard_map/ppermute | solution.py:492
  50.9 4.6 %collective-permute-start.3 = (bf16[512,128]{1,0:T(8,128)(2,1)}, bf16[512,128]{1,0:T(8,128)(2,1)S(1)}, u32[]{:S(2)}, u32[]{:S(2)}) collective-permute-start(bf16[512,128]{1,0:T(8,128)(2,1)} %get-tuple-element.40), channel_id=1, source_target_pairs={{1,0},{2,1},{3,2},{4,3},{5,4},{6,5},{7,6},{8,7},{9,8},{10,9},{11,1... | collective-permute-start | bytes 393224 | tf_op jit(solution)/shard_map/ppermute | solution.py:493
  52.5 0.7 copy-start.11
  55.5 0.7 copy-start.13
  62.4 16.3 %all-to-all-start.3 = ((bf16[32,40,128]{2,1,0:T(8,128)(2,1)}), bf16[32,40,128]{2,1,0:T(8,128)(2,1)S(1)}, u32[]{:S(2)}, u32[]{:S(2)}) async-start(bf16[32,40,128]{2,1,0:T(8,128)(2,1)} %get-tuple-element.44), calls=%async_computation.3 | async-start | bytes 655360 | tf_op jit(solution)/shard_map/all_to_all | solution.py:487
  67.8 3.8 %copy-start.10 = (bf16[3,3,3,64,64]{4,3,2,1,0:T(8,128)(2,1)S(1)}, bf16[3,3,3,64,64]{4,3,2,1,0:T(8,128)(2,1)}, u32[]{:S(2)}) copy-start(bf16[3,3,3,64,64]{4,3,2,1,0:T(8,128)(2,1)} %param.16) | copy-start | bytes 663556
  67.8 3.8 %copy-start.12 = (bf16[512,128]{1,0:T(8,128)(2,1)S(1)}, bf16[512,128]{1,0:T(8,128)(2,1)}, u32[]{:S(2)}) copy-start(bf16[512,128]{1,0:T(8,128)(2,1)} %copy-done.11) | copy-start | bytes 393220
  67.8 3.8 %copy-start.14 = (bf16[512,128]{1,0:T(8,128)(2,1)S(1)}, bf16[512,128]{1,0:T(8,128)(2,1)}, u32[]{:S(2)}) copy-start(bf16[512,128]{1,0:T(8,128)(2,1)} %copy-done.13) | copy-start | bytes 393220
  67.8 3.8 %copy-start.26 = (bf16[1024,128]{1,0:T(8,128)(2,1)S(1)}, bf16[1024,128]{1,0:T(8,128)(2,1)}, u32[]{:S(2)}) copy-start(bf16[1024,128]{1,0:T(8,128)(2,1)} %copy-done.25) | copy-start | bytes 786436
  67.8 10.9 %copy-start.2 = (bf16[1024,256]{1,0:T(8,128)(2,1)S(1)}, bf16[1024,256]{1,0:T(8,128)(2,1)}, u32[]{:S(2)}) copy-start(bf16[1024,256]{1,0:T(8,128)(2,1)} %constant.26.clone.refs_1_) | copy-start | bytes 1572868

commit v6 on v5

--- a/solution.py
+++ b/solution.py
@@ -21,6 +21,7 @@
 OFFSETS = 27
 TERM_ROWS = 1024
 VMEM_BYTES = 40 * 1024 * 1024
+WHOLE_VMEM = 65000 * 1024
 
 F32 = jnp.float32
 BF16 = jnp.bfloat16
@@ -69,17 +70,24 @@
     return gathered(analysis), scattered(synthesis), gathered(synthesis), scattered(analysis)
 
 
-def interleave_table(channels, layers):
-    table = np.zeros((channels, layers, layers, channels), np.float32)
-    for layer in range(layers):
-        table[np.arange(channels), layer, layer, np.arange(channels)] = 1.0
-    return table.reshape(channels * layers, channels * layers).astype(ml_dtypes.bfloat16)
-
-
 def dot(left, right, contract=(1, 0)):
     return lax.dot_general(
         left, right, (((contract[0],), (contract[1],)), ((), ())), preferred_element_type=F32
     )
+
+
+def turn_table():
+    row = lax.broadcasted_iota(jnp.int32, (LANES, LANES), 0)
+    column = lax.broadcasted_iota(jnp.int32, (LANES, LANES), 1)
+    return jnp.where(column == row % 2 * (LANES // 2) + row // 2, 1.0, 0.0).astype(BF16)
+
+
+def to_cells(field):
+    return dot(field.reshape(LANES, CELLS), turn_table(), (0, 0))
+
+
+def to_field(cells):
+    return dot(turn_table(), cells, (1, 1)).astype(BF16).reshape(LANES // 2, 2, CELLS)
 
 
 def low_lanes(rows):
@@ -198,8 +206,8 @@
                     )
 
 
-def analyse_kernel(field, turn, analysis, cells_out, coef_out, first_out, last_out):
-    cells = dot(field[...], turn[...], (0, 0))
+def analyse_kernel(field, analysis, cells_out, coef_out, first_out, last_out):
+    cells = to_cells(field[...])
     rounded = cells.astype(BF16)
     coef_out[...] = dot(analysis[...], rounded).astype(BF16)
     cells_out[...] = rounded
@@ -209,7 +217,7 @@
 
 
 def local_kernel(
-    cells, before, after, cotangent, turn, weights, local_out, lanes_out, cotangent_out, padded, table
+    cells, before, after, cotangent, weights, local_out, lanes_out, cotangent_out, padded, table
 ):
     banded_forward(weights, table)
     beside = beside_layers(before[...], after[...])
@@ -221,7 +229,7 @@
     stencil(padded, table, False, store)
     whole = jnp.concatenate([cells[...].astype(F32), beside.astype(F32)], axis=1)
     lanes_out[...] = whole.T.astype(BF16)
-    cotangent_out[...] = dot(cotangent[...], turn[...], (0, 0)).astype(BF16)
+    cotangent_out[...] = to_cells(cotangent[...]).astype(BF16)
 
 
 def pack_kernel(weights, out):
@@ -387,8 +395,8 @@
         out[2 * g * depth : 2 * (g + 1) * depth, :] = dot(blocks, mixed[span, 0:half], (0, 0))
 
 
-def output_kernel(cells, turn, out):
-    out[...] = dot(turn[...], cells[...], (1, 1)).astype(BF16)
+def output_kernel(cells, out):
+    out[...] = to_field(cells[...])
 
 
 def local_grad_kernel(grad, before, after, weights, out, padded, table):
@@ -401,7 +409,7 @@
     stencil(padded, table, True, store)
 
 
-def finish_kernel(received, sums, synthesis, local, turn, grad_out, stencil_out):
+def finish_kernel(received, sums, synthesis, local, grad_out, stencil_out):
     in_slab = sums is None
     if in_slab:
         modes, terms = slab_load(received)
@@ -409,7 +417,7 @@
     else:
         modes, terms = received[...], sums[...].astype(F32)
     cells = (dot(synthesis[...], modes.astype(BF16)) + local[...]).astype(BF16)
-    grad_out[...] = dot(turn[...], cells, (1, 1)).astype(BF16)
+    grad_out[...] = to_field(cells)
     half = LANES // 2
     for k in range(OFFSETS):
         row = (k // 2) * half
@@ -421,6 +429,23 @@
     return jax.ShapeDtypeStruct(dims, dtype)
 
 
+class Staged:
+    def __init__(self, source, buffer, semaphore):
+        self.copy = pltpu.make_async_copy(source, buffer, semaphore)
+        self.buffer = buffer
+        self.copy.start()
+        self.ready = False
+
+    def load(self):
+        if not self.ready:
+            self.copy.wait()
+            self.ready = True
+
+    def __getitem__(self, index):
+        self.load()
+        return self.buffer[index]
+
+
 class Sent:
     def __init__(self, target, buffer, semaphore):
         self.copy = pltpu.make_async_copy(buffer, target, semaphore)
@@ -435,7 +460,7 @@
         return self.buffer.shape
 
 
-def run(body, outs, *operands, sent=(), scratch=(), flops=0):
+def run(body, outs, *operands, staged=(), sent=(), scratch=(), flops=0, limit=VMEM_BYTES):
     given = [k for k, operand in enumerate(operands) if operand is not None]
     made = [k for k, out in enumerate(outs) if out is not None]
     sent = [k for k in made if k in sent]
@@ -451,13 +476,17 @@
         filled = dict(zip(given, take(len(given))))
         kept = dict(zip(made, take(len(made))))
         own = take(len(scratch))
+        for place, (k, buffer) in enumerate(zip(staged, take(len(staged)))):
+            filled[k] = Staged(filled[k], buffer, refs[-1].at[place])
         for place, (k, buffer) in enumerate(zip(sent, take(len(sent)))):
-            kept[k] = Sent(kept[k], buffer, refs[-1].at[place])
+            kept[k] = Sent(kept[k], buffer, refs[-1].at[len(staged) + place])
         body(
             *[filled.get(k) for k in range(len(operands))],
             *[kept.get(k) for k in range(len(outs))],
             *own,
         )
+        for k in staged:
+            filled[k].load()
         for k in sent:
             kept[k].copy.wait()
 
@@ -466,16 +495,17 @@
     size = sum(x.size * x.dtype.itemsize for x in (*arrays, *results))
     in_vmem = pl.BlockSpec(memory_space=pltpu.VMEM)
     in_hbm = pl.BlockSpec(memory_space=pltpu.HBM)
-    buffers = [pltpu.VMEM(outs[k].shape, outs[k].dtype) for k in sent]
+    buffers = [operands[k] for k in staged] + [outs[k] for k in sent]
+    buffers = [pltpu.VMEM(x.shape, x.dtype) for x in buffers]
     if buffers:
         buffers.append(pltpu.SemaphoreType.DMA((len(buffers),)))
     results = pl.pallas_call(
         kernel,
         out_shape=results,
-        in_specs=[in_vmem] * len(given),
+        in_specs=[in_hbm if k in staged else in_vmem for k in given],
         out_specs=[in_hbm if k in sent else in_vmem for k in made],
         scratch_shapes=[*scratch, *buffers],
-        compiler_params=pltpu.CompilerParams(vmem_limit_bytes=VMEM_BYTES),
+        compiler_params=pltpu.CompilerParams(vmem_limit_bytes=limit),
         cost_estimate=pl.CostEstimate(flops=flops, bytes_accessed=size, transcendentals=0),
         name=body.__name__ if hasattr(body, "__name__") else body.func.__name__,
     )(*arrays)
@@ -508,11 +538,9 @@
 
     analysis, synthesis = plane_tables(batches, slabs)
     gather, scatter, gather_back, scatter_back = depth_tables(batches, slabs, layers, modes)
-    turn = interleave_table(channels, layers)
     weights = mode_weight.reshape(modes * 2 * KZ * channels, channels)
     taps = conv_weight.reshape(OFFSETS, channels, channels)
-    field = snapshots.reshape(channels * layers, plane)
-    outer = cotangent.reshape(channels * layers, plane)
+    field = shape((channels, layers, plane), BF16)
     wide = shape((CELLS, LANES), BF16)
     edge = shape((CELLS // 2, LANES), BF16)
     plane_modes = shape((plane_rows, LANES), BF16)
@@ -524,15 +552,17 @@
     cells, coef, first, last = run(
         analyse_kernel,
         [wide, plane_modes, edge, edge],
-        field,
-        turn,
+        snapshots.reshape(field.shape),
         analysis,
-        sent=(1, 2, 3),
+        staged=(0, 1),
+        sent=(0, 1, 2, 3),
+        limit=WHOLE_VMEM,
         flops=10**8,
     )
+    packed = shape((weights.shape[0] // 2, LANES), BF16)
     weights, coef = lax.optimization_barrier((weights, coef))
     coef = send(coef)
-    (weights,) = run(pack_kernel, [shape((weights.shape[0] // 2, LANES), BF16)], weights)
+    (packed_weights,) = run(pack_kernel, [packed], weights)
     before, after = neighbours(first, last)
     local, lanes, outer_cells = run(
         local_kernel,
@@ -540,8 +570,7 @@
         cells,
         before,
         after,
-        outer,
-        turn,
+        cotangent.reshape(field.shape),
         taps,
         scratch=[padded, pltpu.VMEM((3, 2 * LANES, 3 * LANES), BF16)],
         flops=7 * 10**8,
@@ -551,7 +580,7 @@
         [plane_modes, shape((count, GROUP * half // 2), BF16)],
         coef,
         gather,
-        weights,
+        packed_weights,
         scatter,
         sent=(0,),
         flops=4 * 10**8,
@@ -574,10 +603,12 @@
         local,
         outer_cells,
         lanes,
-        sent=(2, 3, 4),
+        sent=(0, 1, 2, 3, 4),
         scratch=[pltpu.VMEM((CELLS + 2 * NY, 3 * LANES), BF16)],
         flops=10**9,
     )
+    weights, back = lax.optimization_barrier((weights, back))
+    (packed_weights,) = run(pack_kernel, [packed], weights)
     if in_slab:
         back = exchange(back)
     else:
@@ -586,12 +617,13 @@
     before, after = neighbours(first, last)
     (activated,) = run(
         output_kernel,
-        [shape((channels * layers, plane), BF16)],
+        [field],
         activated,
-        turn,
         flops=10**8,
     )
-    back, before, after, activated = lax.optimization_barrier((back, before, after, activated))
+    back, before, after, activated, packed_weights = lax.optimization_barrier(
+        (back, before, after, activated, packed_weights)
+    )
     scale = 1.0 / math.sqrt(batches * slabs * layers * plane)
     grad_modes, mixed_grad, sums = run(
         functools.partial(unmix_kernel, batches, scale),
@@ -603,7 +635,7 @@
         back,
         None if in_slab else terms,
         gather_back,
-        weights,
+        packed_weights,
         scatter_back,
         sent=(0,),
         flops=4 * 10**8,
@@ -632,12 +664,11 @@
     )
     input_gradient, conv_gradient = run(
         finish_kernel,
-        [shape((channels * layers, plane), BF16), shape((OFFSETS, channels, channels), F32)],
+        [field, shape((OFFSETS, channels, channels), F32)],
         grad_modes,
         sums,
         np.ascontiguousarray(analysis.T),
         local,
-        turn,
         flops=10**8,
     )
     return (

time: 81.7 us -> 87.8 us (1.075)
  local copies, waits for them, and re-layouts: 19.3 us -> 24.6 us
  Pallas kernels: 15.3 us -> 18 us
  waiting for transfers between devices: 14.3 us -> 11.7 us
    unnamed x54 -> x72, local copies, waits for them, and re-layouts: 15.6 us -> 24.6 us
    reshape x4 -> x0, local copies, waits for them, and re-layouts: 3.75 us -> none  [the longest x1 1.1 us: shards(): field = snapshots.reshape(channels * layers, plane)]
    pallas_call x10 -> x11, Pallas kernels: 15.3 us -> 18 us  [run(): pl.pallas_call(kernel, out_shape=results, in_specs=[in_hbm if k in staged...]
    ppermute x2, waiting for transfers between devices: 2.38 us -> 0.05 us  [neighbours(): after = lax.ppermute(first, 'space', [(i + 1, i) for i in range(ends)])]
  transfers between devices with their start and end apart: 8 -> 8, of which waited for: 4 -> 3; matrix products, arithmetic and copies ran while one was open for 2% -> 0% of each run, Pallas kernels for 10% -> 11%
where the time goes in v6:
time: 87.8 us; the launch traced here: 86.8 us
  starting transfers between devices  31.7 us (36%)
  local copies, waits for them, and re-layouts  24.6 us (28%)
  Pallas kernels  18 us (21%)
  waiting for transfers between devices  11.7 us (13%)
  between operations  0.89 us (1%)
    all_to_all x4, starting transfers between devices, exchange(): lax.all_to_all(values, ('batch', 'space'), split_axis=0, concat_axis=0, t...  24.6 us
    unnamed x72, local copies, waits for them, and re-layouts  24.6 us
    pallas_call x11, Pallas kernels, run(): pl.pallas_call(kernel, out_shape=results, in_specs=[in_hbm if k in staged...  18 us
    all_to_all x4, waiting for transfers between devices, exchange(): lax.all_to_all(values, ('batch', 'space'), split_axis=0, concat_axis=0, t...  11.6 us
    ppermute x2, starting transfers between devices, neighbours(): before = lax.ppermute(last, 'space', [(i, i + 1) for i in range(ends)])  4.46 us
    ppermute x2, starting transfers between devices, neighbours(): after = lax.ppermute(first, 'space', [(i + 1, i) for i in range(ends)])  2.58 us
  transfers between devices with their start and end apart: 8, of which 3 were waited for; matrix products, arithmetic and copies ran while one was open for 0% of the time, Pallas kernels for 11%

profile of v6, /device:TPU:0, one launch (start us, length us, event | category | flops | bytes accessed | tf_op | source)
XLA Modules:
  0.0 86.8 jit_solution(11596258091384197633)
XLA Ops:
  0.6 0.0 copy-start.5
  0.6 2.5 %analyse_kernel.1 = (bf16[1024,128]{1,0:T(8,128)(2,1)}, bf16[256,128]{1,0:T(8,128)(2,1)}, bf16[512,128]{1,0:T(8,128)(2,1)}, bf16[512,128]{1,0:T(8,128)(2,1)}) custom-call(bf16[64,2,1024]{2,1,0:T(2,128)(2,1)} %bitcast.22, bf16[256,1024]{1,0:T(8,128)(2,1)} %constant.16.clone.refs_1_), custom_call_target="tpu_custom_call" | custom-call | flops 100000000 | bytes 1376256 | tf_op jit(solution)/shard_map/analyse_kernel/pallas_call | solution.py:502
  3.2 7.3 %all-to-all-start = ((bf16[32,8,128]{2,1,0:T(8,128)(2,1)}), bf16[32,8,128]{2,1,0:T(8,128)(2,1)S(1)}, u32[]{:S(2)}, u32[]{:S(2)}) async-start(bf16[32,8,128]{2,1,0:T(8,128)(2,1)} %bitcast.24), calls=%async_computation | async-start | bytes 131072 | tf_op jit(solution)/shard_map/all_to_all | solution.py:517
  10.5 2.2 %collective-permute-start = (bf16[512,128]{1,0:T(8,128)(2,1)}, bf16[512,128]{1,0:T(8,128)(2,1)S(1)}, u32[]{:S(2)}, u32[]{:S(2)}) collective-permute-start(bf16[512,128]{1,0:T(8,128)(2,1)} %get-tuple-element.36), channel_id=1, source_target_pairs={{0,1},{1,2},{2,3},{3,4},{4,5},{5,6},{6,7},{7,8},{8,9},{9,10},{10,1... | collective-permute-start | bytes 393224 | tf_op jit(solution)/shard_map/ppermute | solution.py:522
  12.7 1.3 %collective-permute-start.1 = (bf16[512,128]{1,0:T(8,128)(2,1)}, bf16[512,128]{1,0:T(8,128)(2,1)S(1)}, u32[]{:S(2)}, u32[]{:S(2)}) collective-permute-start(bf16[512,128]{1,0:T(8,128)(2,1)} %get-tuple-element.37), channel_id=1, source_target_pairs={{1,0},{2,1},{3,2},{4,3},{5,4},{6,5},{7,6},{8,7},{9,8},{10,9},{11,1... | collective-permute-start | bytes 393224 | tf_op jit(solution)/shard_map/ppermute | solution.py:523
  14.0 0.0 copy-start
  14.0 1.9 %copy-done = bf16[8,1,24,64,64]{4,3,2,1,0:T(8,128)(2,1)S(1)} copy-done((bf16[8,1,24,64,64]{4,3,2,1,0:T(8,128)(2,1)S(1)}, bf16[8,1,24,64,64]{4,3,2,1,0:T(8,128)(2,1)}, u32[]{:S(2)}) %copy-start) | copy-done | bytes 1572888
  15.9 0.5 pack_kernel.2.refs_2_
  16.3 1.6 %all-to-all-done = bf16[32,8,128]{2,1,0:T(8,128)(2,1)S(1)} async-done(((bf16[32,8,128]{2,1,0:T(8,128)(2,1)}), bf16[32,8,128]{2,1,0:T(8,128)(2,1)S(1)}, u32[]{:S(2)}, u32[]{:S(2)}) %all-to-all-start) | async-done | bytes 65568 | tf_op jit(solution)/shard_map/all_to_all | solution.py:517
  17.9 0.0 copy-done.6
  17.9 1.6 %mix_kernel.1 = (bf16[256,128]{1,0:T(8,128)(2,1)}, bf16[384,256]{1,0:T(8,128)(2,1)S(1)}) custom-call(bf16[256,128]{1,0:T(8,128)(2,1)S(1)} %bitcast.16, bf16[384,512]{1,0:T(8,128)(2,1)S(1)} %copy-done.6, bf16[6144,128]{1,0:T(8,128)(2,1)S(1)} %pack_kernel.2.refs_2_, bf16[256,768]{1,0:T(8,128)(2,1)S(1)} %copy-done.5), custom_call_target="tpu_custom_call" | custom-call | flops 400000000 | bytes 2686976 | tf_op jit(solution)/shard_map/mix_kernel/pallas_call | solution.py:502
  19.6 0.7 copy-done.12
  20.2 6.9 %all-to-all-start.1 = ((bf16[32,8,128]{2,1,0:T(8,128)(2,1)}), bf16[32,8,128]{2,1,0:T(8,128)(2,1)S(1)}, u32[]{:S(2)}, u32[]{:S(2)}) async-start(bf16[32,8,128]{2,1,0:T(8,128)(2,1)} %bitcast.4), calls=%async_computation.1 | async-start | bytes 131072 | tf_op jit(solution)/shard_map/all_to_all | solution.py:517
  27.1 0.0 collective-permute-done.refs_1_
  27.1 0.0 copy-start.22
  27.1 0.6 copy-done.22
  27.8 0.0 collective-permute-done.1.refs_2_
  27.8 0.7 copy-done.24
  28.4 1.0 %copy-done.14 = bf16[3,3,3,64,64]{4,3,2,1,0:T(8,128)(2,1)S(1)} copy-done((bf16[3,3,3,64,64]{4,3,2,1,0:T(8,128)(2,1)S(1)}, bf16[3,3,3,64,64]{4,3,2,1,0:T(8,128)(2,1)}, u32[]{:S(2)}) %copy-start.14) | copy-done | bytes 221208
  29.5 0.9 %copy-done.16 = bf16[1,64,2,1024]{3,2,1,0:T(2,128)(2,1)S(1)} copy-done((bf16[1,64,2,1024]{3,2,1,0:T(2,128)(2,1)S(1)}, bf16[1,64,2,1024]{3,2,1,0:T(2,128)(2,1)}, u32[]{:S(2)}) %copy-start.16) | copy-done | bytes 262168
  30.4 0.9 %copy-done.17 = bf16[1024,128]{1,0:T(8,128)(2,1)S(1)} copy-done((bf16[1024,128]{1,0:T(8,128)(2,1)S(1)}, bf16[1024,128]{1,0:T(8,128)(2,1)}, u32[]{:S(2)}) %copy-start.17) | copy-done | bytes 262168
  31.4 0.9 %copy-done.23 = bf16[512,128]{1,0:T(8,128)(2,1)S(1)} copy-done((bf16[512,128]{1,0:T(8,128)(2,1)S(1)}, bf16[512,128]{1,0:T(8,128)(2,1)}, u32[]{:S(2)}) %copy-start.23) | copy-done | bytes 131096
  32.3 0.9 %copy-done.25 = bf16[512,128]{1,0:T(8,128)(2,1)S(1)} copy-done((bf16[512,128]{1,0:T(8,128)(2,1)S(1)}, bf16[512,128]{1,0:T(8,128)(2,1)}, u32[]{:S(2)}) %copy-start.25) | copy-done | bytes 131096
  33.2 1.2 %local_kernel.1 = (f32[1024,128]{1,0:T(8,128)S(1)}, bf16[256,1024]{1,0:T(8,128)(2,1)S(1)}, bf16[1024,128]{1,0:T(8,128)(2,1)S(1)}) custom-call(bf16[1024,128]{1,0:T(8,128)(2,1)S(1)} %copy-done.17, bf16[512,128]{1,0:T(8,128)(2,1)S(1)} %copy-done.23, bf16[512,128]{1,0:T(8,128)(2,1)S(1)} %copy-done.25, bf16[64,2,1024]{2,1,0:T(2,128)(2,1)S(1)} %bitcast.20, ...), custom_call_target="tpu_custom_call" | custom-call | flops 700000000 | bytes 2318336 | tf_op jit(solution)/shard_map/local_kernel/pallas_call | solution.py:502
  34.4 0.0 copy-start.30
  34.4 0.8 copy-done.30
  35.2 0.8 copy-done.32
  35.9 0.0 all-to-all-done.1
  35.9 1.0 %copy-done.28 = bf16[256,1024]{1,0:T(8,128)(2,1)S(1)} copy-done((bf16[256,1024]{1,0:T(8,128)(2,1)S(1)}, bf16[256,1024]{1,0:T(8,128)(2,1)}, u32[]{:S(2)}) %copy-start.28) | copy-done | bytes 524312
  37.0 1.0 %copy-done.29 = bf16[1024,256]{1,0:T(8,128)(2,1)S(1)} copy-done((bf16[1024,256]{1,0:T(8,128)(2,1)S(1)}, bf16[1024,256]{1,0:T(8,128)(2,1)}, u32[]{:S(2)}) %copy-start.29) | copy-done | bytes 524312
  38.0 1.0 %copy-done.31 = f32[1024,128]{1,0:T(8,128)S(1)} copy-done((f32[1024,128]{1,0:T(8,128)S(1)}, f32[1024,128]{1,0:T(8,128)}, u32[]{:S(2)}) %copy-start.31) | copy-done | bytes 524312
  39.1 1.0 %copy-done.33 = bf16[256,1024]{1,0:T(8,128)(2,1)S(1)} copy-done((bf16[256,1024]{1,0:T(8,128)(2,1)S(1)}, bf16[256,1024]{1,0:T(8,128)(2,1)}, u32[]{:S(2)}) %copy-start.33) | copy-done | bytes 524312
  40.1 2.6 %activate_kernel.1 = (bf16[1024,128]{1,0:T(8,128)(2,1)S(1)}, bf16[1024,128]{1,0:T(8,128)(2,1)S(1)}, bf16[512,128]{1,0:T(8,128)(2,1)S(1)}, bf16[512,128]{1,0:T(8,128)(2,1)S(1)}, bf16[32,40,128]{2,1,0:T(8,128)(2,1)S(1)}) custom-call(bf16[256,128]{1,0:T(8,128)(2,1)S(1)} %bitcast.17, bf16[1024,256]{1,0:T(8,128)(2,1)S(1)} %copy-done.29, ...), custom_call_target="tpu_custom_call" | custom-call | flops 1000000000 | bytes 3538944 | tf_op jit(solution)/shard_map/activate_kernel/pallas_call | solution.py:502
  42.7 0.0 copy-start.9
  42.7 0.7 copy-done.9
  43.4 0.7 copy-done.10
  44.1 0.6 copy-done.26
  44.8 0.6 copy-done.27
  45.5 0.7 copy-done.34
  46.2 5.8 %all-to-all-start.2 = ((bf16[32,40,128]{2,1,0:T(8,128)(2,1)}), bf16[32,40,128]{2,1,0:T(8,128)(2,1)S(1)}, u32[]{:S(2)}, u32[]{:S(2)}) async-start(bf16[32,40,128]{2,1,0:T(8,128)(2,1)} %copy-done.9), calls=%async_computation.2 | async-start | bytes 655360 | tf_op jit(solution)/shard_map/all_to_all | solution.py:517
  52.0 0.0 copy-start.11
  52.0 2.3 %collective-permute-start.2 = (bf16[512,128]{1,0:T(8,128)(2,1)}, bf16[512,128]{1,0:T(8,128)(2,1)S(1)}, u32[]{:S(2)}, u32[]{:S(2)}) collective-permute-start(bf16[512,128]{1,0:T(8,128)(2,1)} %copy-done.27), channel_id=1, source_target_pairs={{0,1},{1,2},{2,3},{3,4},{4,5},{5,6},{6,7},{7,8},{8,9},{9,10},{10,1... | collective-permute-start | bytes 393224 | tf_op jit(solution)/shard_map/ppermute | solution.py:522
  54.3 1.3 %collective-permute-start.3 = (bf16[512,128]{1,0:T(8,128)(2,1)}, bf16[512,128]{1,0:T(8,128)(2,1)S(1)}, u32[]{:S(2)}, u32[]{:S(2)}) collective-permute-start(bf16[512,128]{1,0:T(8,128)(2,1)} %copy-done.26), channel_id=1, source_target_pairs={{1,0},{2,1},{3,2},{4,3},{5,4},{6,5},{7,6},{8,7},{9,8},{10,9},{11,1... | collective-permute-start | bytes 393224 | tf_op jit(solution)/shard_map/ppermute | solution.py:523
  55.6 0.5 pack_kernel.3.refs_2_
  56.1 0.0 copy-start.2
  56.1 1.1 %copy-done.2 = bf16[6144,128]{1,0:T(8,128)(2,1)} copy-done((bf16[6144,128]{1,0:T(8,128)(2,1)}, bf16[6144,128]{1,0:T(8,128)(2,1)S(1)}, u32[]{:S(2)}) %copy-start.2) | copy-done | bytes 1572888
  57.2 0.0 copy-done.11
  57.2 0.9 %output_kernel.1 = bf16[64,2,1024]{2,1,0:T(2,128)(2,1)} custom-call(bf16[1024,128]{1,0:T(8,128)(2,1)S(1)} %copy-done.11), custom_call_target="tpu_custom_call" | custom-call | flops 100000000 | bytes 524288 | tf_op jit(solution)/shard_map/output_kernel/pallas_call | solution.py:502
  58.2 0.0 collective-permute-done.2.refs_1_
  58.2 0.7 copy-done.18
  58.8 0.1 collective-permute-done.3.refs_2_
  58.9 0.7 copy-done.20
  59.5 4.1 %all-to-all-done.2.refs_0_ = bf16[32,40,128]{2,1,0:T(8,128)(2,1)S(1)} async-done(((bf16[32,40,128]{2,1,0:T(8,128)(2,1)}), bf16[32,40,128]{2,1,0:T(8,128)(2,1)S(1)}, u32[]{:S(2)}, u32[]{:S(2)}) %all-to-all-start.2) | async-done | bytes 327712 | tf_op jit(solution)/shard_map/all_to_all | solution.py:517
  63.7 1.4 %copy-done.3 = bf16[6144,128]{1,0:T(8,128)(2,1)S(1)} copy-done((bf16[6144,128]{1,0:T(8,128)(2,1)S(1)}, bf16[6144,128]{1,0:T(8,128)(2,1)}, u32[]{:S(2)}) %copy-start.3) | copy-done | bytes 1572888
  65.1 1.0 %copy-done.7 = bf16[256,768]{1,0:T(8,128)(2,1)S(1)} copy-done((bf16[256,768]{1,0:T(8,128)(2,1)S(1)}, bf16[256,768]{1,0:T(8,128)(2,1)}, u32[]{:S(2)}) %copy-start.7) | copy-done | bytes 393240
  66.1 1.0 %copy-done.8 = bf16[384,512]{1,0:T(8,128)(2,1)S(1)} copy-done((bf16[384,512]{1,0:T(8,128)(2,1)S(1)}, bf16[384,512]{1,0:T(8,128)(2,1)}, u32[]{:S(2)}) %copy-start.8) | copy-done | bytes 393240
  67.1 1.9 %unmix_kernel.1 = (bf16[32,40,128]{2,1,0:T(8,128)(2,1)}, bf16[384,128]{1,0:T(8,128)(2,1)S(1)}) custom-call(bf16[32,40,128]{2,1,0:T(8,128)(2,1)S(1)} %all-to-all-done.2.refs_0_, bf16[384,512]{1,0:T(8,128)(2,1)S(1)} %copy-done.8, bf16[6144,128]{1,0:T(8,128)(2,1)S(1)} %copy-done.3, bf16[256,768]{1,0:T(8,128)(2,1)S(1)} %copy-done.7), custom_call_target="tpu_custom_call" | custom-call | flops 400000000 | bytes 3112960 | tf_op jit(solution)/shard_map/unmix_kernel/pallas_call | solution.py:502
  69.0 4.6 %all-to-all-start.3 = ((bf16[32,40,128]{2,1,0:T(8,128)(2,1)}), bf16[32,40,128]{2,1,0:T(8,128)(2,1)S(1)}, u32[]{:S(2)}, u32[]{:S(2)}) async-start(bf16[32,40,128]{2,1,0:T(8,128)(2,1)} %get-tuple-element.50), calls=%async_computation.3 | async-start | bytes 655360 | tf_op jit(solution)/shard_map/all_to_all | solution.py:517
  73.6 0.9 %copy-done.13 = bf16[384,256]{1,0:T(8,128)(2,1)S(1)} copy-done((bf16[384,256]{1,0:T(8,128)(2,1)S(1)}, bf16[384,256]{1,0:T(8,128)(2,1)}, u32[]{:S(2)}) %copy-start.13) | copy-done | bytes 196632
  74.6 0.0 copy-start.4
  74.6 3.7 %weight_kernel.1 = f32[12288,64]{1,0:T(8,128)} custom-call(bf16[384,256]{1,0:T(8,128)(2,1)S(1)} %copy-done.13, bf16[384,128]{1,0:T(8,128)(2,1)S(1)} %get-tuple-element.56.refs_1_), custom_call_target="tpu_custom_call" | custom-call | flops 400000000 | bytes 3440640 | tf_op jit(solution)/shard_map/weight_kernel/pallas_call | solution.py:502
  78.3 1.1 %local_grad_kernel.1.refs_2_ = f32[1024,128]{1,0:T(8,128)S(1)} custom-call(bf16[1024,128]{1,0:T(8,128)(2,1)S(1)} %copy-done.35, bf16[512,128]{1,0:T(8,128)(2,1)S(1)} %copy-done.19, bf16[512,128]{1,0:T(8,128)(2,1)S(1)} %copy-done.21, bf16[27,64,64]{2,1,0:T(8,128)(2,1)S(1)} %bitcast.19), custom_call_target="tpu_custom_call" | custom-call | flops 700000000 | bytes 1269760 | tf_op jit(solution)/shard_map/local_grad_kernel/pallas_call | solution.py:502
  79.4 5.9 %all-to-all-done.3.refs_0_ = bf16[32,40,128]{2,1,0:T(8,128)(2,1)S(1)} async-done(((bf16[32,40,128]{2,1,0:T(8,128)(2,1)}), bf16[32,40,128]{2,1,0:T(8,128)(2,1)S(1)}, u32[]{:S(2)}, u32[]{:S(2)}) %all-to-all-start.3) | async-done | bytes 327712 | tf_op jit(solution)/shard_map/all_to_all | solution.py:517
  85.3 1.5 %finish_kernel.1 = (bf16[64,2,1024]{2,1,0:T(2,128)(2,1)}, f32[27,64,64]{2,1,0:T(8,128)}) custom-call(bf16[32,40,128]{2,1,0:T(8,128)(2,1)S(1)} %all-to-all-done.3.refs_0_, bf16[1024,256]{1,0:T(8,128)(2,1)S(1)} %copy-done.4, f32[1024,128]{1,0:T(8,128)S(1)} %local_grad_kernel.1.refs_2_), custom_call_target="tpu_custom_call" | custom-call | flops 100000000 | bytes 2080768 | tf_op jit(solution)/shard_map/finish_kernel/pallas_call | solution.py:502
  (35 shorter events, 0.1 us)
Async XLA Ops:
  0.6 17.3 %copy-start.5 = (bf16[256,768]{1,0:T(8,128)(2,1)S(1)}, bf16[256,768]{1,0:T(8,128)(2,1)}, u32[]{:S(2)}) copy-start(bf16[256,768]{1,0:T(8,128)(2,1)} %constant.18.clone.refs_3_) | copy-start | bytes 1179652
  3.2 14.7 %all-to-all-start = ((bf16[32,8,128]{2,1,0:T(8,128)(2,1)}), bf16[32,8,128]{2,1,0:T(8,128)(2,1)S(1)}, u32[]{:S(2)}, u32[]{:S(2)}) async-start(bf16[32,8,128]{2,1,0:T(8,128)(2,1)} %bitcast.24), calls=%async_computation | async-start | bytes 131072 | tf_op jit(solution)/shard_map/all_to_all | solution.py:517
  10.5 16.6 %collective-permute-start = (bf16[512,128]{1,0:T(8,128)(2,1)}, bf16[512,128]{1,0:T(8,128)(2,1)S(1)}, u32[]{:S(2)}, u32[]{:S(2)}) collective-permute-start(bf16[512,128]{1,0:T(8,128)(2,1)} %get-tuple-element.36), channel_id=1, source_target_pairs={{0,1},{1,2},{2,3},{3,4},{4,5},{5,6},{6,7},{7,8},{8,9},{9,10},{10,1... | collective-permute-start | bytes 393224 | tf_op jit(solution)/shard_map/ppermute | solution.py:522
  12.7 15.1 %collective-permute-start.1 = (bf16[512,128]{1,0:T(8,128)(2,1)}, bf16[512,128]{1,0:T(8,128)(2,1)S(1)}, u32[]{:S(2)}, u32[]{:S(2)}) collective-permute-start(bf16[512,128]{1,0:T(8,128)(2,1)} %get-tuple-element.37), channel_id=1, source_target_pairs={{1,0},{2,1},{3,2},{4,3},{5,4},{6,5},{7,6},{8,7},{9,8},{10,9},{11,1... | collective-permute-start | bytes 393224 | tf_op jit(solution)/shard_map/ppermute | solution.py:523
  14.0 1.9 %copy-start = (bf16[8,1,24,64,64]{4,3,2,1,0:T(8,128)(2,1)S(1)}, bf16[8,1,24,64,64]{4,3,2,1,0:T(8,128)(2,1)}, u32[]{:S(2)}) copy-start(bf16[8,1,24,64,64]{4,3,2,1,0:T(8,128)(2,1)} %param.14) | copy-start | bytes 4718596
  15.9 2.1 %copy-start.6 = (bf16[384,512]{1,0:T(8,128)(2,1)S(1)}, bf16[384,512]{1,0:T(8,128)(2,1)}, u32[]{:S(2)}) copy-start(bf16[384,512]{1,0:T(8,128)(2,1)} %constant.17.clone.refs_1_) | copy-start | bytes 1179652
  19.6 0.7 copy-start.12
  20.2 15.7 %all-to-all-start.1 = ((bf16[32,8,128]{2,1,0:T(8,128)(2,1)}), bf16[32,8,128]{2,1,0:T(8,128)(2,1)S(1)}, u32[]{:S(2)}, u32[]{:S(2)}) async-start(bf16[32,8,128]{2,1,0:T(8,128)(2,1)} %bitcast.4), calls=%async_computation.1 | async-start | bytes 131072 | tf_op jit(solution)/shard_map/all_to_all | solution.py:517
  27.1 0.7 copy-start.22
  27.8 0.7 copy-start.24
  28.4 1.0 %copy-start.14 = (bf16[3,3,3,64,64]{4,3,2,1,0:T(8,128)(2,1)S(1)}, bf16[3,3,3,64,64]{4,3,2,1,0:T(8,128)(2,1)}, u32[]{:S(2)}) copy-start(bf16[3,3,3,64,64]{4,3,2,1,0:T(8,128)(2,1)} %param.15) | copy-start | bytes 663556
  29.5 0.9 %copy-start.16 = (bf16[1,64,2,1024]{3,2,1,0:T(2,128)(2,1)S(1)}, bf16[1,64,2,1024]{3,2,1,0:T(2,128)(2,1)}, u32[]{:S(2)}) copy-start(bf16[1,64,2,1024]{3,2,1,0:T(2,128)(2,1)} %param.13) | copy-start | bytes 786436
  30.4 0.9 %copy-start.17 = (bf16[1024,128]{1,0:T(8,128)(2,1)S(1)}, bf16[1024,128]{1,0:T(8,128)(2,1)}, u32[]{:S(2)}) copy-start(bf16[1024,128]{1,0:T(8,128)(2,1)} %get-tuple-element.35.refs_0_) | copy-start | bytes 786436
  31.4 0.9 %copy-start.23 = (bf16[512,128]{1,0:T(8,128)(2,1)S(1)}, bf16[512,128]{1,0:T(8,128)(2,1)}, u32[]{:S(2)}) copy-start(bf16[512,128]{1,0:T(8,128)(2,1)} %copy-done.22) | copy-start | bytes 393220
  32.3 0.9 %copy-start.25 = (bf16[512,128]{1,0:T(8,128)(2,1)S(1)}, bf16[512,128]{1,0:T(8,128)(2,1)}, u32[]{:S(2)}) copy-start(bf16[512,128]{1,0:T(8,128)(2,1)} %copy-done.24) | copy-start | bytes 393220
  33.2 22.4 %copy-start.1 = (bf16[8,1,24,64,64]{4,3,2,1,0:T(8,128)(2,1)S(1)}, bf16[8,1,24,64,64]{4,3,2,1,0:T(8,128)(2,1)}, u32[]{:S(2)}) copy-start(bf16[8,1,24,64,64]{4,3,2,1,0:T(8,128)(2,1)} %param.14) | copy-start | bytes 4718596
  34.4 0.8 copy-start.30
  35.1 0.8 copy-start.32
  35.9 1.0 %copy-start.28 = (bf16[256,1024]{1,0:T(8,128)(2,1)S(1)}, bf16[256,1024]{1,0:T(8,128)(2,1)}, u32[]{:S(2)}) copy-start(bf16[256,1024]{1,0:T(8,128)(2,1)} %constant.20.clone.refs_2_) | copy-start | bytes 1572868
  37.0 1.0 %copy-start.29 = (bf16[1024,256]{1,0:T(8,128)(2,1)S(1)}, bf16[1024,256]{1,0:T(8,128)(2,1)}, u32[]{:S(2)}) copy-start(bf16[1024,256]{1,0:T(8,128)(2,1)} %constant.19.clone.refs_1_) | copy-start | bytes 1572868
  38.0 1.0 %copy-start.31 = (f32[1024,128]{1,0:T(8,128)S(1)}, f32[1024,128]{1,0:T(8,128)}, u32[]{:S(2)}) copy-start(f32[1024,128]{1,0:T(8,128)} %copy-done.30) | copy-start | bytes 1572868
  39.1 1.0 %copy-start.33 = (bf16[256,1024]{1,0:T(8,128)(2,1)S(1)}, bf16[256,1024]{1,0:T(8,128)(2,1)}, u32[]{:S(2)}) copy-start(bf16[256,1024]{1,0:T(8,128)(2,1)} %copy-done.32) | copy-start | bytes 1572868
  42.7 0.7 copy-start.9
  43.4 0.7 copy-start.10
  44.1 0.7 copy-start.26
  44.8 0.6 copy-start.27
  45.4 0.7 copy-start.34
  46.2 17.5 %all-to-all-start.2 = ((bf16[32,40,128]{2,1,0:T(8,128)(2,1)}), bf16[32,40,128]{2,1,0:T(8,128)(2,1)S(1)}, u32[]{:S(2)}, u32[]{:S(2)}) async-start(bf16[32,40,128]{2,1,0:T(8,128)(2,1)} %copy-done.9), calls=%async_computation.2 | async-start | bytes 655360 | tf_op jit(solution)/shard_map/all_to_all | solution.py:517
  52.0 5.2 %copy-start.11 = (bf16[1024,128]{1,0:T(8,128)(2,1)S(1)}, bf16[1024,128]{1,0:T(8,128)(2,1)}, u32[]{:S(2)}) copy-start(bf16[1024,128]{1,0:T(8,128)(2,1)} %copy-done.10) | copy-start | bytes 786436
  52.0 6.2 %collective-permute-start.2 = (bf16[512,128]{1,0:T(8,128)(2,1)}, bf16[512,128]{1,0:T(8,128)(2,1)S(1)}, u32[]{:S(2)}, u32[]{:S(2)}) collective-permute-start(bf16[512,128]{1,0:T(8,128)(2,1)} %copy-done.27), channel_id=1, source_target_pairs={{0,1},{1,2},{2,3},{3,4},{4,5},{5,6},{6,7},{7,8},{8,9},{9,10},{10,1... | collective-permute-start | bytes 393224 | tf_op jit(solution)/shard_map/ppermute | solution.py:522
  54.3 4.6 %collective-permute-start.3 = (bf16[512,128]{1,0:T(8,128)(2,1)}, bf16[512,128]{1,0:T(8,128)(2,1)S(1)}, u32[]{:S(2)}, u32[]{:S(2)}) collective-permute-start(bf16[512,128]{1,0:T(8,128)(2,1)} %copy-done.26), channel_id=1, source_target_pairs={{1,0},{2,1},{3,2},{4,3},{5,4},{6,5},{7,6},{8,7},{9,8},{10,9},{11,1... | collective-permute-start | bytes 393224 | tf_op jit(solution)/shard_map/ppermute | solution.py:523
  56.1 1.1 %copy-start.2 = (bf16[6144,128]{1,0:T(8,128)(2,1)}, bf16[6144,128]{1,0:T(8,128)(2,1)S(1)}, u32[]{:S(2)}) copy-start(bf16[6144,128]{1,0:T(8,128)(2,1)S(1)} %pack_kernel.3.refs_2_) | copy-start | bytes 4718596
  58.2 0.7 copy-start.18
  58.9 0.7 copy-start.20
  63.7 1.4 %copy-start.3 = (bf16[6144,128]{1,0:T(8,128)(2,1)S(1)}, bf16[6144,128]{1,0:T(8,128)(2,1)}, u32[]{:S(2)}) copy-start(bf16[6144,128]{1,0:T(8,128)(2,1)} %copy-done.2) | copy-start | bytes 4718596
  65.1 1.0 %copy-start.7 = (bf16[256,768]{1,0:T(8,128)(2,1)S(1)}, bf16[256,768]{1,0:T(8,128)(2,1)}, u32[]{:S(2)}) copy-start(bf16[256,768]{1,0:T(8,128)(2,1)} %constant.22.clone.refs_3_) | copy-start | bytes 1179652
  66.1 1.0 %copy-start.8 = (bf16[384,512]{1,0:T(8,128)(2,1)S(1)}, bf16[384,512]{1,0:T(8,128)(2,1)}, u32[]{:S(2)}) copy-start(bf16[384,512]{1,0:T(8,128)(2,1)} %constant.21.clone.refs_1_) | copy-start | bytes 1179652
  69.0 16.3 %all-to-all-start.3 = ((bf16[32,40,128]{2,1,0:T(8,128)(2,1)}), bf16[32,40,128]{2,1,0:T(8,128)(2,1)S(1)}, u32[]{:S(2)}, u32[]{:S(2)}) async-start(bf16[32,40,128]{2,1,0:T(8,128)(2,1)} %get-tuple-element.50), calls=%async_computation.3 | async-start | bytes 655360 | tf_op jit(solution)/shard_map/all_to_all | solution.py:517
  73.6 0.9 %copy-start.13 = (bf16[384,256]{1,0:T(8,128)(2,1)S(1)}, bf16[384,256]{1,0:T(8,128)(2,1)}, u32[]{:S(2)}) copy-start(bf16[384,256]{1,0:T(8,128)(2,1)} %copy-done.12) | copy-start | bytes 589828
  74.5 3.8 %copy-start.15 = (bf16[3,3,3,64,64]{4,3,2,1,0:T(8,128)(2,1)S(1)}, bf16[3,3,3,64,64]{4,3,2,1,0:T(8,128)(2,1)}, u32[]{:S(2)}) copy-start(bf16[3,3,3,64,64]{4,3,2,1,0:T(8,128)(2,1)} %param.15) | copy-start | bytes 663556
  74.5 3.8 %copy-start.19 = (bf16[512,128]{1,0:T(8,128)(2,1)S(1)}, bf16[512,128]{1,0:T(8,128)(2,1)}, u32[]{:S(2)}) copy-start(bf16[512,128]{1,0:T(8,128)(2,1)} %copy-done.18) | copy-start | bytes 393220
  74.5 3.8 %copy-start.21 = (bf16[512,128]{1,0:T(8,128)(2,1)S(1)}, bf16[512,128]{1,0:T(8,128)(2,1)}, u32[]{:S(2)}) copy-start(bf16[512,128]{1,0:T(8,128)(2,1)} %copy-done.20) | copy-start | bytes 393220
  74.5 3.8 %copy-start.35 = (bf16[1024,128]{1,0:T(8,128)(2,1)S(1)}, bf16[1024,128]{1,0:T(8,128)(2,1)}, u32[]{:S(2)}) copy-start(bf16[1024,128]{1,0:T(8,128)(2,1)} %copy-done.34) | copy-start | bytes 786436
  74.6 10.8 %copy-start.4 = (bf16[1024,256]{1,0:T(8,128)(2,1)S(1)}, bf16[1024,256]{1,0:T(8,128)(2,1)}, u32[]{:S(2)}) copy-start(bf16[1024,256]{1,0:T(8,128)(2,1)} %constant.23.clone.refs_1_) | copy-start | bytes 1572868

commit v7 on v6

--- a/solution.py
+++ b/solution.py
@@ -21,7 +21,10 @@
 OFFSETS = 27
 TERM_ROWS = 1024
 VMEM_BYTES = 40 * 1024 * 1024
+LOADER_VMEM = 60 * 1024 * 1024
 WHOLE_VMEM = 65000 * 1024
+HBM_ROWS = 20480
+TABLE_ROWS = 2560
 
 F32 = jnp.float32
 BF16 = jnp.bfloat16
@@ -68,6 +71,44 @@
         return full.reshape(-1, layers * count).astype(ml_dtypes.bfloat16)
 
     return gathered(analysis), scattered(synthesis), gathered(synthesis), scattered(analysis)
+
+
+class Piece:
+    def __init__(self, row, column, values):
+        self.index = (slice(row, row + values.shape[0]), slice(column, column + values.shape[1]))
+        self.values = values
+
+
+def join_tables(batches, slabs, layers, modes):
+    analysis, synthesis = plane_tables(batches, slabs)
+    gather, scatter, gather_back, scatter_back = depth_tables(batches, slabs, layers, modes)
+    parts = {}
+    rows = [0]
+
+    def shelf(**named):
+        column = 0
+        for name, values in named.items():
+            parts[name] = Piece(rows[0], column, values)
+            column += values.shape[1]
+        rows[0] += max(values.shape[0] for values in named.values())
+
+    shelf(analysis=analysis)
+    shelf(synthesis=synthesis)
+    shelf(
+        synthesis_cells=synthesis.T,
+        analysis_cells=analysis.T,
+        gather=np.concatenate([gather, gather_back], axis=0),
+    )
+    both = parts.pop("gather")
+    first, column = both.index[0].start, both.index[1].start
+    parts["gather"] = Piece(first, column, gather)
+    parts["gather_back"] = Piece(first + gather.shape[0], column, gather_back)
+    shelf(scatter=scatter)
+    shelf(scatter_back=scatter_back)
+    joined = np.zeros((max(rows[0], TABLE_ROWS), 1024), ml_dtypes.bfloat16)
+    for part in parts.values():
+        joined[part.index] = part.values
+    return joined, parts
 
 
 def dot(left, right, contract=(1, 0)):
@@ -232,12 +273,13 @@
     cotangent_out[...] = to_cells(cotangent[...]).astype(BF16)
 
 
-def pack_kernel(weights, out):
+def pack_kernel(weights, out, kept):
     rows = GROUP * LANES // 4
     for g in range(out.shape[0] // rows):
         first = weights[2 * g * rows : (2 * g + 1) * rows, :]
         second = weights[(2 * g + 1) * rows : (2 * g + 2) * rows, :]
         out[g * rows : (g + 1) * rows, :] = jnp.concatenate([first, second], axis=1)
+    kept[...] = out[...]
 
 
 def mode_in_group(rows, lanes, snaps):
@@ -425,6 +467,11 @@
         stencil_out[k] = terms[row : row + half, lane : lane + half]
 
 
+def part_shape(source, index):
+    dims = [part.stop - part.start for part in index]
+    return jax.ShapeDtypeStruct((*dims, *source.shape[len(dims) :]), source.dtype)
+
+
 def shape(dims, dtype):
     return jax.ShapeDtypeStruct(dims, dtype)
 
@@ -455,15 +502,21 @@
         self.buffer[index] = value
         self.copy.start()
 
+    def __getitem__(self, index):
+        return self.buffer[index]
+
     @property
     def shape(self):
         return self.buffer.shape
 
 
-def run(body, outs, *operands, staged=(), sent=(), scratch=(), flops=0, limit=VMEM_BYTES):
+def run(
+    body, outs, *operands, staged=(), sent=(), loads=(), scratch=(), flops=0, limit=VMEM_BYTES
+):
     given = [k for k, operand in enumerate(operands) if operand is not None]
     made = [k for k, out in enumerate(outs) if out is not None]
-    sent = [k for k in made if k in sent]
+    sent = {k: sent[k] if isinstance(sent, dict) else None for k in made if k in sent}
+    copies = len(staged) + len(sent)
 
     def kernel(*refs):
         refs = list(refs)
@@ -474,12 +527,22 @@
             return taken
 
         filled = dict(zip(given, take(len(given))))
+        sources = take(len(loads))
         kept = dict(zip(made, take(len(made))))
+        loaded = [
+            pltpu.make_async_copy(source.at[index], target, refs[-1].at[copies + place])
+            for place, (source, (_, index), target) in enumerate(
+                zip(sources, loads, take(len(loads)))
+            )
+        ]
+        for copy in loaded:
+            copy.start()
         own = take(len(scratch))
         for place, (k, buffer) in enumerate(zip(staged, take(len(staged)))):
             filled[k] = Staged(filled[k], buffer, refs[-1].at[place])
         for place, (k, buffer) in enumerate(zip(sent, take(len(sent)))):
-            kept[k] = Sent(kept[k], buffer, refs[-1].at[len(staged) + place])
+            target = kept[k].at[0 : buffer.shape[0]] if outs[k].shape != buffer.shape else kept[k]
+            kept[k] = Sent(target, buffer, refs[-1].at[len(staged) + place])
         body(
             *[filled.get(k) for k in range(len(operands))],
             *[kept.get(k) for k in range(len(outs))],
@@ -489,28 +552,34 @@
             filled[k].load()
         for k in sent:
             kept[k].copy.wait()
+        for copy in loaded:
+            copy.wait()
 
     arrays = [operands[k] for k in given]
     results = [outs[k] for k in made]
     size = sum(x.size * x.dtype.itemsize for x in (*arrays, *results))
     in_vmem = pl.BlockSpec(memory_space=pltpu.VMEM)
     in_hbm = pl.BlockSpec(memory_space=pltpu.HBM)
-    buffers = [operands[k] for k in staged] + [outs[k] for k in sent]
-    buffers = [pltpu.VMEM(x.shape, x.dtype) for x in buffers]
-    if buffers:
-        buffers.append(pltpu.SemaphoreType.DMA((len(buffers),)))
+    buffers = [pltpu.VMEM(operands[k].shape, operands[k].dtype) for k in staged]
+    for k in sent:
+        rows = sent[k] or outs[k].shape[0]
+        buffers.append(pltpu.VMEM((rows, *outs[k].shape[1:]), outs[k].dtype))
+    if copies + len(loads) > 0:
+        buffers.append(pltpu.SemaphoreType.DMA((copies + len(loads),)))
+    results += [part_shape(source, index) for source, index in loads]
     results = pl.pallas_call(
         kernel,
         out_shape=results,
-        in_specs=[in_hbm if k in staged else in_vmem for k in given],
-        out_specs=[in_hbm if k in sent else in_vmem for k in made],
+        in_specs=[in_hbm if k in staged else in_vmem for k in given] + [in_hbm] * len(loads),
+        out_specs=[in_hbm if k in sent else in_vmem for k in made] + [in_vmem] * len(loads),
         scratch_shapes=[*scratch, *buffers],
         compiler_params=pltpu.CompilerParams(vmem_limit_bytes=limit),
         cost_estimate=pl.CostEstimate(flops=flops, bytes_accessed=size, transcendentals=0),
         name=body.__name__ if hasattr(body, "__name__") else body.func.__name__,
-    )(*arrays)
+    )(*arrays, *[source for source, _ in loads])
+    loaded = list(results[len(made) :])
     results = dict(zip(made, results))
-    return [results.get(k) for k in range(len(outs))]
+    return [results.get(k) for k in range(len(outs))] + loaded
 
 
 def exchange(values):
@@ -536,8 +605,12 @@
     count = modes * 2 * KZ * batches
     in_slab = modes == 8 and devices * 32 == TERM_ROWS
 
-    analysis, synthesis = plane_tables(batches, slabs)
-    gather, scatter, gather_back, scatter_back = depth_tables(batches, slabs, layers, modes)
+    tables, parts = join_tables(batches, slabs, layers, modes)
+    tables = jnp.asarray(tables)
+
+    def table(name):
+        return tables, parts[name].index
+
     weights = mode_weight.reshape(modes * 2 * KZ * channels, channels)
     taps = conv_weight.reshape(OFFSETS, channels, channels)
     field = shape((channels, layers, plane), BF16)
@@ -553,7 +626,7 @@
         analyse_kernel,
         [wide, plane_modes, edge, edge],
         snapshots.reshape(field.shape),
-        analysis,
+        parts["analysis"].values,
         staged=(0, 1),
         sent=(0, 1, 2, 3),
         limit=WHOLE_VMEM,
@@ -562,9 +635,17 @@
     packed = shape((weights.shape[0] // 2, LANES), BF16)
     weights, coef = lax.optimization_barrier((weights, coef))
     coef = send(coef)
-    (packed_weights,) = run(pack_kernel, [packed], weights)
+    packed_rows = packed.shape[0]
+    packed_weights, kept_weights, gather, scatter = run(
+        pack_kernel,
+        [packed, shape((max(packed_rows, HBM_ROWS), LANES), BF16)],
+        weights,
+        sent={1: packed_rows},
+        loads=[table("gather"), table("scatter")],
+        limit=LOADER_VMEM,
+    )
     before, after = neighbours(first, last)
-    local, lanes, outer_cells = run(
+    local, lanes, outer_cells, synthesis_cells, synthesis = run(
         local_kernel,
         [shape((CELLS, LANES), F32), shape((2 * LANES, CELLS), BF16), wide],
         cells,
@@ -572,6 +653,8 @@
         after,
         cotangent.reshape(field.shape),
         taps,
+        loads=[table("synthesis_cells"), table("synthesis")],
+        limit=LOADER_VMEM,
         scratch=[padded, pltpu.VMEM((3, 2 * LANES, 3 * LANES), BF16)],
         flops=7 * 10**8,
     )
@@ -582,7 +665,7 @@
         gather,
         packed_weights,
         scatter,
-        sent=(0,),
+        sent=(0, 1),
         flops=4 * 10**8,
     )
     back = send(back)
@@ -598,7 +681,7 @@
             None if in_slab else shape((TERM_ROWS, LANES), BF16),
         ],
         back,
-        np.ascontiguousarray(synthesis.T),
+        synthesis_cells,
         synthesis,
         local,
         outer_cells,
@@ -607,23 +690,25 @@
         scratch=[pltpu.VMEM((CELLS + 2 * NY, 3 * LANES), BF16)],
         flops=10**9,
     )
-    weights, back = lax.optimization_barrier((weights, back))
-    (packed_weights,) = run(pack_kernel, [packed], weights)
     if in_slab:
         back = exchange(back)
     else:
         back = send(back)
         terms = exchange(terms.reshape(devices, TERM_ROWS // devices, LANES))
     before, after = neighbours(first, last)
-    (activated,) = run(
+    activated, packed_weights, gather_back, scatter_back = run(
         output_kernel,
         [field],
         activated,
+        loads=[
+            (kept_weights, (slice(0, packed_rows),)),
+            table("gather_back"),
+            table("scatter_back"),
+        ],
+        limit=LOADER_VMEM,
         flops=10**8,
     )
-    back, before, after, activated, packed_weights = lax.optimization_barrier(
-        (back, before, after, activated, packed_weights)
-    )
+    back, before, after = lax.optimization_barrier((back, before, after))
     scale = 1.0 / math.sqrt(batches * slabs * layers * plane)
     grad_modes, mixed_grad, sums = run(
         functools.partial(unmix_kernel, batches, scale),
@@ -645,13 +730,15 @@
     else:
         grad_modes = send(grad_modes)
         sums = lax.all_gather(sums, ("batch", "space"), axis=0, tiled=True)
-    (local,) = run(
+    local, analysis_cells = run(
         local_grad_kernel,
         [shape((CELLS, LANES), F32)],
         grad,
         before,
         after,
         taps,
+        loads=[table("analysis_cells")],
+        limit=LOADER_VMEM,
         scratch=[padded, pltpu.VMEM((3, 3 * LANES, 2 * LANES), BF16)],
         flops=7 * 10**8,
     )
@@ -667,7 +754,7 @@
         [field, shape((OFFSETS, channels, channels), F32)],
         grad_modes,
         sums,
-        np.ascontiguousarray(analysis.T),
+        analysis_cells,
         local,
         flops=10**8,
     )

time: 87.8 us -> 90 us (1.025)
  Pallas kernels: 18 us -> 31.2 us
  local copies, waits for them, and re-layouts: 24.6 us -> 16.1 us
  starting transfers between devices: 31.7 us -> 29.1 us
    pallas_call x11 -> x10, Pallas kernels: 18 us -> 31.2 us  [run(): pl.pallas_call(kernel, out_shape=results, in_specs=[in_hbm if k in staged...]
    unnamed x72 -> x38, local copies, waits for them, and re-layouts: 24.6 us -> 16.1 us
    all_to_all x4, starting transfers between devices: 24.6 us -> 22.2 us  [exchange(): lax.all_to_all(values, ('batch', 'space'), split_axis=0, concat_axis=0, t...]
  transfers between devices with their start and end apart: 8 -> 8, of which waited for: 3 -> 3; matrix products, arithmetic and copies ran while one was open for 0% -> 0% of each run, Pallas kernels for 11% -> 25%
where the time goes in v7:
time: 90 us; the launch traced here: 88.8 us
  Pallas kernels  31.2 us (35%)
  starting transfers between devices  29.1 us (32%)
  local copies, waits for them, and re-layouts  16.1 us (18%)
  waiting for transfers between devices  11.6 us (13%)
    pallas_call x10, Pallas kernels, run(): pl.pallas_call(kernel, out_shape=results, in_specs=[in_hbm if k in staged...  31.2 us
    all_to_all x4, starting transfers between devices, exchange(): lax.all_to_all(values, ('batch', 'space'), split_axis=0, concat_axis=0, t...  22.2 us
    unnamed x38, local copies, waits for them, and re-layouts  16.1 us
    all_to_all x4, waiting for transfers between devices, exchange(): lax.all_to_all(values, ('batch', 'space'), split_axis=0, concat_axis=0, t...  11.6 us
    ppermute x2, starting transfers between devices, neighbours(): before = lax.ppermute(last, 'space', [(i, i + 1) for i in range(ends)])  4.32 us
    ppermute x2, starting transfers between devices, neighbours(): after = lax.ppermute(first, 'space', [(i + 1, i) for i in range(ends)])  2.58 us
  transfers between devices with their start and end apart: 8, of which 3 were waited for; matrix products, arithmetic and copies ran while one was open for 0% of the time, Pallas kernels for 25%

profile of v7, /device:TPU:0, one launch (start us, length us, event | category | flops | bytes accessed | tf_op | source)
XLA Modules:
  0.0 88.8 jit_solution(10092273570920788475)
XLA Ops:
  0.6 2.5 %analyse_kernel.1 = (bf16[1024,128]{1,0:T(8,128)(2,1)}, bf16[256,128]{1,0:T(8,128)(2,1)}, bf16[512,128]{1,0:T(8,128)(2,1)}, bf16[512,128]{1,0:T(8,128)(2,1)}) custom-call(bf16[64,2,1024]{2,1,0:T(2,128)(2,1)} %bitcast.20, bf16[256,1024]{1,0:T(8,128)(2,1)} %constant.5.clone.refs_1_), custom_call_target="tpu_custom_call" | custom-call | flops 100000000 | bytes 1376256 | tf_op jit(solution)/shard_map/analyse_kernel/pallas_call | solution.py:570
  3.1 7.3 %all-to-all-start = ((bf16[32,8,128]{2,1,0:T(8,128)(2,1)}), bf16[32,8,128]{2,1,0:T(8,128)(2,1)S(1)}, u32[]{:S(2)}, u32[]{:S(2)}) async-start(bf16[32,8,128]{2,1,0:T(8,128)(2,1)} %bitcast.22), calls=%async_computation | async-start | bytes 131072 | tf_op jit(solution)/shard_map/all_to_all | solution.py:586
  10.4 2.2 %collective-permute-start = (bf16[512,128]{1,0:T(8,128)(2,1)}, bf16[512,128]{1,0:T(8,128)(2,1)S(1)}, u32[]{:S(2)}, u32[]{:S(2)}) collective-permute-start(bf16[512,128]{1,0:T(8,128)(2,1)} %get-tuple-element.47), channel_id=1, source_target_pairs={{0,1},{1,2},{2,3},{3,4},{4,5},{5,6},{6,7},{7,8},{8,9},{9,10},{10,1... | collective-permute-start | bytes 393224 | tf_op jit(solution)/shard_map/ppermute | solution.py:591
  12.6 1.3 %collective-permute-start.1 = (bf16[512,128]{1,0:T(8,128)(2,1)}, bf16[512,128]{1,0:T(8,128)(2,1)S(1)}, u32[]{:S(2)}, u32[]{:S(2)}) collective-permute-start(bf16[512,128]{1,0:T(8,128)(2,1)} %get-tuple-element.48), channel_id=1, source_target_pairs={{1,0},{2,1},{3,2},{4,3},{5,4},{6,5},{7,6},{8,7},{9,8},{10,9},{11,1... | collective-permute-start | bytes 393224 | tf_op jit(solution)/shard_map/ppermute | solution.py:592
  13.9 5.1 %pack_kernel.1 = (bf16[6144,128]{1,0:T(8,128)(2,1)}, bf16[20480,128]{1,0:T(8,128)(2,1)}, bf16[384,512]{1,0:T(8,128)(2,1)}, bf16[256,768]{1,0:T(8,128)(2,1)}) custom-call(bf16[12288,64]{1,0:T(8,128)(2,1)} %bitcast.17, bf16[2560,1024]{1,0:T(8,128)(2,1)} %constant.4.clone.refs_1_.refs_2_.refs_5_.refs_6_.refs_3_.refs_4_, ...), custom_call_target="tpu_custom_call" | custom-call | bytes 8388608 | tf_op jit(solution)/shard_map/pack_kernel/pallas_call | solution.py:570
  19.0 0.0 all-to-all-done
  19.0 0.0 copy-start
  19.0 1.4 %copy-done = bf16[6144,128]{1,0:T(8,128)(2,1)S(1)} copy-done((bf16[6144,128]{1,0:T(8,128)(2,1)S(1)}, bf16[6144,128]{1,0:T(8,128)(2,1)}, u32[]{:S(2)}) %copy-start) | copy-done | bytes 1572888
  20.4 0.0 copy-start.4
  20.4 1.0 %copy-done.4 = bf16[384,512]{1,0:T(8,128)(2,1)S(1)} copy-done((bf16[384,512]{1,0:T(8,128)(2,1)S(1)}, bf16[384,512]{1,0:T(8,128)(2,1)}, u32[]{:S(2)}) %copy-start.4) | copy-done | bytes 393240
  21.4 0.0 copy-start.5
  21.4 1.0 %copy-done.5 = bf16[256,768]{1,0:T(8,128)(2,1)S(1)} copy-done((bf16[256,768]{1,0:T(8,128)(2,1)S(1)}, bf16[256,768]{1,0:T(8,128)(2,1)}, u32[]{:S(2)}) %copy-start.5) | copy-done | bytes 393240
  22.4 2.0 %mix_kernel.1 = (bf16[256,128]{1,0:T(8,128)(2,1)}, bf16[384,256]{1,0:T(8,128)(2,1)S(1)}) custom-call(bf16[256,128]{1,0:T(8,128)(2,1)S(1)} %bitcast.14, bf16[384,512]{1,0:T(8,128)(2,1)S(1)} %copy-done.4, bf16[6144,128]{1,0:T(8,128)(2,1)S(1)} %copy-done, bf16[256,768]{1,0:T(8,128)(2,1)S(1)} %copy-done.5), custom_call_target="tpu_custom_call" | custom-call | flops 400000000 | bytes 2686976 | tf_op jit(solution)/shard_map/mix_kernel/pallas_call | solution.py:570
  24.4 7.9 %all-to-all-start.1 = ((bf16[32,8,128]{2,1,0:T(8,128)(2,1)}), bf16[32,8,128]{2,1,0:T(8,128)(2,1)S(1)}, u32[]{:S(2)}, u32[]{:S(2)}) async-start(bf16[32,8,128]{2,1,0:T(8,128)(2,1)} %bitcast.4), calls=%async_computation.1 | async-start | bytes 131072 | tf_op jit(solution)/shard_map/all_to_all | solution.py:586
  32.4 0.0 collective-permute-done.refs_1_
  32.4 0.0 copy-start.15
  32.4 0.0 collective-permute-done.1.refs_2_
  32.4 0.0 copy-start.16
  32.4 0.6 copy-done.15
  33.1 0.0 copy-done.16
  33.1 3.9 %local_kernel.1 = (f32[1024,128]{1,0:T(8,128)}, bf16[256,1024]{1,0:T(8,128)(2,1)}, bf16[1024,128]{1,0:T(8,128)(2,1)}, bf16[1024,256]{1,0:T(8,128)(2,1)}, bf16[256,1024]{1,0:T(8,128)(2,1)}) custom-call(bf16[1024,128]{1,0:T(8,128)(2,1)} %get-tuple-element.46.refs_0_, bf16[512,128]{1,0:T(8,128)(2,1)} %copy-done.15, bf16[512,128]{1,0:T(8,128)(2,1)} %copy-done.16, ...), custom_call_target="tpu_custom_call" | custom-call | flops 700000000 | bytes 2318336 | tf_op jit(solution)/shard_map/local_kernel/pallas_call | solution.py:570
  37.0 2.8 %all-to-all-done.1 = bf16[32,8,128]{2,1,0:T(8,128)(2,1)S(1)} async-done(((bf16[32,8,128]{2,1,0:T(8,128)(2,1)}), bf16[32,8,128]{2,1,0:T(8,128)(2,1)S(1)}, u32[]{:S(2)}, u32[]{:S(2)}) %all-to-all-start.1) | async-done | bytes 65568 | tf_op jit(solution)/shard_map/all_to_all | solution.py:586
  39.8 0.0 copy-start.10
  39.8 1.0 %copy-done.10 = f32[1024,128]{1,0:T(8,128)S(1)} copy-done((f32[1024,128]{1,0:T(8,128)S(1)}, f32[1024,128]{1,0:T(8,128)}, u32[]{:S(2)}) %copy-start.10) | copy-done | bytes 524312
  40.8 0.0 copy-start.11
  40.8 1.0 %copy-done.11 = bf16[256,1024]{1,0:T(8,128)(2,1)S(1)} copy-done((bf16[256,1024]{1,0:T(8,128)(2,1)S(1)}, bf16[256,1024]{1,0:T(8,128)(2,1)}, u32[]{:S(2)}) %copy-start.11) | copy-done | bytes 524312
  41.9 0.0 copy-start.12
  41.9 1.0 %copy-done.12 = bf16[1024,256]{1,0:T(8,128)(2,1)S(1)} copy-done((bf16[1024,256]{1,0:T(8,128)(2,1)S(1)}, bf16[1024,256]{1,0:T(8,128)(2,1)}, u32[]{:S(2)}) %copy-start.12) | copy-done | bytes 524312
  42.9 0.0 copy-start.13
  42.9 1.0 %copy-done.13 = bf16[256,1024]{1,0:T(8,128)(2,1)S(1)} copy-done((bf16[256,1024]{1,0:T(8,128)(2,1)S(1)}, bf16[256,1024]{1,0:T(8,128)(2,1)}, u32[]{:S(2)}) %copy-start.13) | copy-done | bytes 524312
  44.0 0.0 copy-start.14
  44.0 0.9 %copy-done.14 = bf16[1024,128]{1,0:T(8,128)(2,1)S(1)} copy-done((bf16[1024,128]{1,0:T(8,128)(2,1)S(1)}, bf16[1024,128]{1,0:T(8,128)(2,1)}, u32[]{:S(2)}) %copy-start.14) | copy-done | bytes 262168
  44.9 3.2 %activate_kernel.1 = (bf16[1024,128]{1,0:T(8,128)(2,1)S(1)}, bf16[1024,128]{1,0:T(8,128)(2,1)S(1)}, bf16[512,128]{1,0:T(8,128)(2,1)S(1)}, bf16[512,128]{1,0:T(8,128)(2,1)S(1)}, bf16[32,40,128]{2,1,0:T(8,128)(2,1)}) custom-call(bf16[256,128]{1,0:T(8,128)(2,1)S(1)} %bitcast.15, bf16[1024,256]{1,0:T(8,128)(2,1)S(1)} %copy-done.12, ...), custom_call_target="tpu_custom_call" | custom-call | flops 1000000000 | bytes 3538944 | tf_op jit(solution)/shard_map/activate_kernel/pallas_call | solution.py:570
  48.1 0.0 copy-start.8
  48.1 0.7 copy-done.8
  48.8 0.0 copy-start.9
  48.8 0.7 copy-done.9
  49.6 3.1 %all-to-all-start.2 = ((bf16[32,40,128]{2,1,0:T(8,128)(2,1)}), bf16[32,40,128]{2,1,0:T(8,128)(2,1)S(1)}, u32[]{:S(2)}, u32[]{:S(2)}) async-start(bf16[32,40,128]{2,1,0:T(8,128)(2,1)} %get-tuple-element.57), calls=%async_computation.2 | async-start | bytes 655360 | tf_op jit(solution)/shard_map/all_to_all | solution.py:586
  52.6 2.2 %collective-permute-start.2 = (bf16[512,128]{1,0:T(8,128)(2,1)S(1)}, bf16[512,128]{1,0:T(8,128)(2,1)S(1)}, u32[]{:S(2)}, u32[]{:S(2)}) collective-permute-start(bf16[512,128]{1,0:T(8,128)(2,1)S(1)} %get-tuple-element.58), channel_id=1, source_target_pairs={{0,1},{1,2},{2,3},{3,4},{4,5},{5,6},{6,7},{7,8},{8,9},{9,10},{10,1... | collective-permute-start | bytes 393224 | tf_op jit(solution)/shard_map/ppermute | solution.py:591
  54.8 1.3 %collective-permute-start.3 = (bf16[512,128]{1,0:T(8,128)(2,1)S(1)}, bf16[512,128]{1,0:T(8,128)(2,1)S(1)}, u32[]{:S(2)}, u32[]{:S(2)}) collective-permute-start(bf16[512,128]{1,0:T(8,128)(2,1)S(1)} %get-tuple-element.59), channel_id=1, source_target_pairs={{1,0},{2,1},{3,2},{4,3},{5,4},{6,5},{7,6},{8,7},{9,8},{10,9},{11,1... | collective-permute-start | bytes 393224 | tf_op jit(solution)/shard_map/ppermute | solution.py:592
  56.1 4.0 %output_kernel.1 = (bf16[64,2,1024]{2,1,0:T(2,128)(2,1)}, bf16[6144,128]{1,0:T(8,128)(2,1)}, bf16[384,512]{1,0:T(8,128)(2,1)}, bf16[256,768]{1,0:T(8,128)(2,1)}) custom-call(bf16[1024,128]{1,0:T(8,128)(2,1)} %copy-done.8, bf16[20480,128]{1,0:T(8,128)(2,1)} %get-tuple-element.55.refs_1_, ...), custom_call_target="tpu_custom_call" | custom-call | flops 100000000 | bytes 524288 | tf_op jit(solution)/shard_map/output_kernel/pallas_call | solution.py:570
  60.2 0.0 collective-permute-done.2.refs_1_
  60.2 0.0 copy-start.17
  60.2 0.0 collective-permute-done.3.refs_2_
  60.2 0.0 copy-start.18
  60.2 4.1 %all-to-all-done.2.refs_0_ = bf16[32,40,128]{2,1,0:T(8,128)(2,1)S(1)} async-done(((bf16[32,40,128]{2,1,0:T(8,128)(2,1)}), bf16[32,40,128]{2,1,0:T(8,128)(2,1)S(1)}, u32[]{:S(2)}, u32[]{:S(2)}) %all-to-all-start.2) | async-done | bytes 327712 | tf_op jit(solution)/shard_map/all_to_all | solution.py:586
  64.3 0.0 copy-start.1
  64.3 1.4 %copy-done.1 = bf16[6144,128]{1,0:T(8,128)(2,1)S(1)} copy-done((bf16[6144,128]{1,0:T(8,128)(2,1)S(1)}, bf16[6144,128]{1,0:T(8,128)(2,1)}, u32[]{:S(2)}) %copy-start.1) | copy-done | bytes 1572888
  65.7 0.0 copy-start.6
  65.7 1.0 %copy-done.6 = bf16[384,512]{1,0:T(8,128)(2,1)S(1)} copy-done((bf16[384,512]{1,0:T(8,128)(2,1)S(1)}, bf16[384,512]{1,0:T(8,128)(2,1)}, u32[]{:S(2)}) %copy-start.6) | copy-done | bytes 393240
  66.7 0.0 copy-start.7
  66.7 1.0 %copy-done.7 = bf16[256,768]{1,0:T(8,128)(2,1)S(1)} copy-done((bf16[256,768]{1,0:T(8,128)(2,1)S(1)}, bf16[256,768]{1,0:T(8,128)(2,1)}, u32[]{:S(2)}) %copy-start.7) | copy-done | bytes 393240
  67.7 1.9 %unmix_kernel.1 = (bf16[32,40,128]{2,1,0:T(8,128)(2,1)}, bf16[384,128]{1,0:T(8,128)(2,1)S(1)}) custom-call(bf16[32,40,128]{2,1,0:T(8,128)(2,1)S(1)} %all-to-all-done.2.refs_0_, bf16[384,512]{1,0:T(8,128)(2,1)S(1)} %copy-done.6, bf16[6144,128]{1,0:T(8,128)(2,1)S(1)} %copy-done.1, bf16[256,768]{1,0:T(8,128)(2,1)S(1)} %copy-done.7), custom_call_target="tpu_custom_call" | custom-call | flops 400000000 | bytes 3112960 | tf_op jit(solution)/shard_map/unmix_kernel/pallas_call | solution.py:570
  69.6 3.9 %all-to-all-start.3 = ((bf16[32,40,128]{2,1,0:T(8,128)(2,1)}), bf16[32,40,128]{2,1,0:T(8,128)(2,1)S(1)}, u32[]{:S(2)}, u32[]{:S(2)}) async-start(bf16[32,40,128]{2,1,0:T(8,128)(2,1)} %get-tuple-element.64), calls=%async_computation.3 | async-start | bytes 655360 | tf_op jit(solution)/shard_map/all_to_all | solution.py:586
  73.6 3.7 %weight_kernel.1 = f32[12288,64]{1,0:T(8,128)} custom-call(bf16[384,256]{1,0:T(8,128)(2,1)S(1)} %get-tuple-element.71.refs_0_, bf16[384,128]{1,0:T(8,128)(2,1)S(1)} %get-tuple-element.72.refs_1_), custom_call_target="tpu_custom_call" | custom-call | flops 400000000 | bytes 3440640 | tf_op jit(solution)/shard_map/weight_kernel/pallas_call | solution.py:570
  77.3 0.0 copy-done.17
  77.3 0.0 copy-done.18
  77.3 3.3 %local_grad_kernel.1 = (f32[1024,128]{1,0:T(8,128)}, bf16[1024,256]{1,0:T(8,128)(2,1)}) custom-call(bf16[1024,128]{1,0:T(8,128)(2,1)} %copy-done.9, bf16[512,128]{1,0:T(8,128)(2,1)} %copy-done.17, bf16[512,128]{1,0:T(8,128)(2,1)} %copy-done.18, bf16[27,64,64]{2,1,0:T(8,128)(2,1)} %bitcast.19, ...), custom_call_target="tpu_custom_call" | custom-call | flops 700000000 | bytes 1269760 | tf_op jit(solution)/shard_map/local_grad_kernel/pallas_call | solution.py:570
  80.6 4.7 %all-to-all-done.3.refs_0_ = bf16[32,40,128]{2,1,0:T(8,128)(2,1)S(1)} async-done(((bf16[32,40,128]{2,1,0:T(8,128)(2,1)}), bf16[32,40,128]{2,1,0:T(8,128)(2,1)S(1)}, u32[]{:S(2)}, u32[]{:S(2)}) %all-to-all-start.3) | async-done | bytes 327712 | tf_op jit(solution)/shard_map/all_to_all | solution.py:586
  85.3 0.0 copy-start.2
  85.3 1.0 %copy-done.2 = f32[1024,128]{1,0:T(8,128)S(1)} copy-done((f32[1024,128]{1,0:T(8,128)S(1)}, f32[1024,128]{1,0:T(8,128)}, u32[]{:S(2)}) %copy-start.2) | copy-done | bytes 524312
  86.3 0.0 copy-start.3
  86.3 1.0 %copy-done.3 = bf16[1024,256]{1,0:T(8,128)(2,1)S(1)} copy-done((bf16[1024,256]{1,0:T(8,128)(2,1)S(1)}, bf16[1024,256]{1,0:T(8,128)(2,1)}, u32[]{:S(2)}) %copy-start.3) | copy-done | bytes 524312
  87.3 1.5 %finish_kernel.1 = (bf16[64,2,1024]{2,1,0:T(2,128)(2,1)}, f32[27,64,64]{2,1,0:T(8,128)}) custom-call(bf16[32,40,128]{2,1,0:T(8,128)(2,1)S(1)} %all-to-all-done.3.refs_0_, bf16[1024,256]{1,0:T(8,128)(2,1)S(1)} %copy-done.3, f32[1024,128]{1,0:T(8,128)S(1)} %copy-done.2), custom_call_target="tpu_custom_call" | custom-call | flops 100000000 | bytes 2080768 | tf_op jit(solution)/shard_map/finish_kernel/pallas_call | solution.py:570
Async XLA Ops:
  3.1 15.9 %all-to-all-start = ((bf16[32,8,128]{2,1,0:T(8,128)(2,1)}), bf16[32,8,128]{2,1,0:T(8,128)(2,1)S(1)}, u32[]{:S(2)}, u32[]{:S(2)}) async-start(bf16[32,8,128]{2,1,0:T(8,128)(2,1)} %bitcast.22), calls=%async_computation | async-start | bytes 131072 | tf_op jit(solution)/shard_map/all_to_all | solution.py:586
  10.4 22.0 %collective-permute-start = (bf16[512,128]{1,0:T(8,128)(2,1)}, bf16[512,128]{1,0:T(8,128)(2,1)S(1)}, u32[]{:S(2)}, u32[]{:S(2)}) collective-permute-start(bf16[512,128]{1,0:T(8,128)(2,1)} %get-tuple-element.47), channel_id=1, source_target_pairs={{0,1},{1,2},{2,3},{3,4},{4,5},{5,6},{6,7},{7,8},{8,9},{9,10},{10,1... | collective-permute-start | bytes 393224 | tf_op jit(solution)/shard_map/ppermute | solution.py:591
  12.6 19.8 %collective-permute-start.1 = (bf16[512,128]{1,0:T(8,128)(2,1)}, bf16[512,128]{1,0:T(8,128)(2,1)S(1)}, u32[]{:S(2)}, u32[]{:S(2)}) collective-permute-start(bf16[512,128]{1,0:T(8,128)(2,1)} %get-tuple-element.48), channel_id=1, source_target_pairs={{1,0},{2,1},{3,2},{4,3},{5,4},{6,5},{7,6},{8,7},{9,8},{10,9},{11,1... | collective-permute-start | bytes 393224 | tf_op jit(solution)/shard_map/ppermute | solution.py:592
  19.0 1.4 %copy-start = (bf16[6144,128]{1,0:T(8,128)(2,1)S(1)}, bf16[6144,128]{1,0:T(8,128)(2,1)}, u32[]{:S(2)}) copy-start(bf16[6144,128]{1,0:T(8,128)(2,1)} %get-tuple-element.43.refs_2_) | copy-start | bytes 4718596
  20.4 1.0 %copy-start.4 = (bf16[384,512]{1,0:T(8,128)(2,1)S(1)}, bf16[384,512]{1,0:T(8,128)(2,1)}, u32[]{:S(2)}) copy-start(bf16[384,512]{1,0:T(8,128)(2,1)} %get-tuple-element.42.refs_1_) | copy-start | bytes 1179652
  21.4 1.0 %copy-start.5 = (bf16[256,768]{1,0:T(8,128)(2,1)S(1)}, bf16[256,768]{1,0:T(8,128)(2,1)}, u32[]{:S(2)}) copy-start(bf16[256,768]{1,0:T(8,128)(2,1)} %get-tuple-element.44.refs_3_) | copy-start | bytes 1179652
  24.4 15.4 %all-to-all-start.1 = ((bf16[32,8,128]{2,1,0:T(8,128)(2,1)}), bf16[32,8,128]{2,1,0:T(8,128)(2,1)S(1)}, u32[]{:S(2)}, u32[]{:S(2)}) async-start(bf16[32,8,128]{2,1,0:T(8,128)(2,1)} %bitcast.4), calls=%async_computation.1 | async-start | bytes 131072 | tf_op jit(solution)/shard_map/all_to_all | solution.py:586
  32.4 0.6 copy-start.15
  32.4 0.7 copy-start.16
  39.8 1.0 %copy-start.10 = (f32[1024,128]{1,0:T(8,128)S(1)}, f32[1024,128]{1,0:T(8,128)}, u32[]{:S(2)}) copy-start(f32[1024,128]{1,0:T(8,128)} %get-tuple-element.51.refs_3_) | copy-start | bytes 1572868
  40.8 1.0 %copy-start.11 = (bf16[256,1024]{1,0:T(8,128)(2,1)S(1)}, bf16[256,1024]{1,0:T(8,128)(2,1)}, u32[]{:S(2)}) copy-start(bf16[256,1024]{1,0:T(8,128)(2,1)} %get-tuple-element.53.refs_5_) | copy-start | bytes 1572868
  41.9 1.0 %copy-start.12 = (bf16[1024,256]{1,0:T(8,128)(2,1)S(1)}, bf16[1024,256]{1,0:T(8,128)(2,1)}, u32[]{:S(2)}) copy-start(bf16[1024,256]{1,0:T(8,128)(2,1)} %get-tuple-element.49.refs_1_) | copy-start | bytes 1572868
  42.9 1.0 %copy-start.13 = (bf16[256,1024]{1,0:T(8,128)(2,1)S(1)}, bf16[256,1024]{1,0:T(8,128)(2,1)}, u32[]{:S(2)}) copy-start(bf16[256,1024]{1,0:T(8,128)(2,1)} %get-tuple-element.50.refs_2_) | copy-start | bytes 1572868
  44.0 0.9 %copy-start.14 = (bf16[1024,128]{1,0:T(8,128)(2,1)S(1)}, bf16[1024,128]{1,0:T(8,128)(2,1)}, u32[]{:S(2)}) copy-start(bf16[1024,128]{1,0:T(8,128)(2,1)} %get-tuple-element.52.refs_4_) | copy-start | bytes 786436
  48.1 0.7 copy-start.8
  48.8 0.7 copy-start.9
  49.6 14.8 %all-to-all-start.2 = ((bf16[32,40,128]{2,1,0:T(8,128)(2,1)}), bf16[32,40,128]{2,1,0:T(8,128)(2,1)S(1)}, u32[]{:S(2)}, u32[]{:S(2)}) async-start(bf16[32,40,128]{2,1,0:T(8,128)(2,1)} %get-tuple-element.57), calls=%async_computation.2 | async-start | bytes 655360 | tf_op jit(solution)/shard_map/all_to_all | solution.py:586
  52.6 7.5 %collective-permute-start.2 = (bf16[512,128]{1,0:T(8,128)(2,1)S(1)}, bf16[512,128]{1,0:T(8,128)(2,1)S(1)}, u32[]{:S(2)}, u32[]{:S(2)}) collective-permute-start(bf16[512,128]{1,0:T(8,128)(2,1)S(1)} %get-tuple-element.58), channel_id=1, source_target_pairs={{0,1},{1,2},{2,3},{3,4},{4,5},{5,6},{6,7},{7,8},{8,9},{9,10},{10,1... | collective-permute-start | bytes 393224 | tf_op jit(solution)/shard_map/ppermute | solution.py:591
  54.8 5.4 %collective-permute-start.3 = (bf16[512,128]{1,0:T(8,128)(2,1)S(1)}, bf16[512,128]{1,0:T(8,128)(2,1)S(1)}, u32[]{:S(2)}, u32[]{:S(2)}) collective-permute-start(bf16[512,128]{1,0:T(8,128)(2,1)S(1)} %get-tuple-element.59), channel_id=1, source_target_pairs={{1,0},{2,1},{3,2},{4,3},{5,4},{6,5},{7,6},{8,7},{9,8},{10,9},{11,1... | collective-permute-start | bytes 393224 | tf_op jit(solution)/shard_map/ppermute | solution.py:592
  60.2 17.2 %copy-start.17 = (bf16[512,128]{1,0:T(8,128)(2,1)}, bf16[512,128]{1,0:T(8,128)(2,1)S(1)}, u32[]{:S(2)}) copy-start(bf16[512,128]{1,0:T(8,128)(2,1)S(1)} %collective-permute-done.2.refs_1_) | copy-start | bytes 393220
  60.2 17.1 %copy-start.18 = (bf16[512,128]{1,0:T(8,128)(2,1)}, bf16[512,128]{1,0:T(8,128)(2,1)S(1)}, u32[]{:S(2)}) copy-start(bf16[512,128]{1,0:T(8,128)(2,1)S(1)} %collective-permute-done.3.refs_2_) | copy-start | bytes 393220
  64.3 1.4 %copy-start.1 = (bf16[6144,128]{1,0:T(8,128)(2,1)S(1)}, bf16[6144,128]{1,0:T(8,128)(2,1)}, u32[]{:S(2)}) copy-start(bf16[6144,128]{1,0:T(8,128)(2,1)} %get-tuple-element.62.refs_2_) | copy-start | bytes 4718596
  65.7 1.0 %copy-start.6 = (bf16[384,512]{1,0:T(8,128)(2,1)S(1)}, bf16[384,512]{1,0:T(8,128)(2,1)}, u32[]{:S(2)}) copy-start(bf16[384,512]{1,0:T(8,128)(2,1)} %get-tuple-element.61.refs_1_) | copy-start | bytes 1179652
  66.7 1.0 %copy-start.7 = (bf16[256,768]{1,0:T(8,128)(2,1)S(1)}, bf16[256,768]{1,0:T(8,128)(2,1)}, u32[]{:S(2)}) copy-start(bf16[256,768]{1,0:T(8,128)(2,1)} %get-tuple-element.63.refs_3_) | copy-start | bytes 1179652
  69.6 15.6 %all-to-all-start.3 = ((bf16[32,40,128]{2,1,0:T(8,128)(2,1)}), bf16[32,40,128]{2,1,0:T(8,128)(2,1)S(1)}, u32[]{:S(2)}, u32[]{:S(2)}) async-start(bf16[32,40,128]{2,1,0:T(8,128)(2,1)} %get-tuple-element.64), calls=%async_computation.3 | async-start | bytes 655360 | tf_op jit(solution)/shard_map/all_to_all | solution.py:586
  85.3 1.0 %copy-start.2 = (f32[1024,128]{1,0:T(8,128)S(1)}, f32[1024,128]{1,0:T(8,128)}, u32[]{:S(2)}) copy-start(f32[1024,128]{1,0:T(8,128)} %get-tuple-element.69.refs_2_) | copy-start | bytes 1572868
  86.3 1.0 %copy-start.3 = (bf16[1024,256]{1,0:T(8,128)(2,1)S(1)}, bf16[1024,256]{1,0:T(8,128)(2,1)}, u32[]{:S(2)}) copy-start(bf16[1024,256]{1,0:T(8,128)(2,1)} %get-tuple-element.68.refs_1_) | copy-start | bytes 1572868

commit v8 on v6

--- a/solution.py
+++ b/solution.py
@@ -22,6 +22,7 @@
 TERM_ROWS = 1024
 VMEM_BYTES = 40 * 1024 * 1024
 WHOLE_VMEM = 65000 * 1024
+HBM_ROWS = 163840
 
 F32 = jnp.float32
 BF16 = jnp.bfloat16
@@ -48,24 +49,21 @@
     return analysis, synthesis
 
 
-def depth_tables(batches, slabs, layers, modes):
+def depth_tables(slabs, layers, modes):
     rows = basis_rows(KZ, slabs * layers)
     analysis = (rows * np.float32(math.sqrt(2.0 / (slabs * layers)))).astype(ml_dtypes.bfloat16)
     synthesis = (rows * np.float32(math.sqrt(2.0 / (2 * KZ)))).astype(ml_dtypes.bfloat16)
 
-    def spread(table):
+    def spread(table, order):
         table = table.astype(np.float32).reshape(2 * KZ, slabs, layers)
-        full = np.einsum("psz,bc,mn->mpbzcsn", table, np.eye(batches), np.eye(modes))
-        return full.reshape(modes * 2 * KZ * batches, layers * batches * slabs * modes)
+        full = np.einsum("psz,mn->" + order, table, np.eye(modes, dtype=np.float32))
+        return full.astype(ml_dtypes.bfloat16)
 
     def gathered(table):
-        return spread(table).astype(ml_dtypes.bfloat16)
+        return spread(table, "mpzsn").reshape(modes * 2 * KZ, layers * slabs * modes)
 
     def scattered(table):
-        full = spread(table)
-        count = full.shape[0]
-        full = full.reshape(count, layers, -1).transpose(2, 1, 0)
-        return full.reshape(-1, layers * count).astype(ml_dtypes.bfloat16)
+        return spread(table, "snzmp").reshape(slabs * modes, layers * modes * 2 * KZ)
 
     return gathered(analysis), scattered(synthesis), gathered(synthesis), scattered(analysis)
 
@@ -232,48 +230,72 @@
     cotangent_out[...] = to_cells(cotangent[...]).astype(BF16)
 
 
-def pack_kernel(weights, out):
+def pack_kernel(weights, out, kept):
     rows = GROUP * LANES // 4
     for g in range(out.shape[0] // rows):
         first = weights[2 * g * rows : (2 * g + 1) * rows, :]
         second = weights[(2 * g + 1) * rows : (2 * g + 2) * rows, :]
         out[g * rows : (g + 1) * rows, :] = jnp.concatenate([first, second], axis=1)
-
-
-def mode_in_group(rows, lanes, snaps):
-    return (lax.broadcasted_iota(jnp.int32, (rows, lanes), 0) // snaps) % GROUP
-
-
-def own_block(rows, snaps):
+    kept[...] = out[...]
+
+
+def mode_in_group(rows, lanes):
+    return lax.broadcasted_iota(jnp.int32, (rows, lanes), 0) % GROUP
+
+
+def own_block(rows):
     width = GROUP * LANES // 4
     lane = lax.broadcasted_iota(jnp.int32, (rows, width), 1)
-    return mode_in_group(rows, width, snaps) % (GROUP // 2) == lane // (LANES // 2)
-
-
-def own_half(rows, snaps):
-    return (mode_in_group(rows, LANES, snaps) < GROUP // 2) == low_lanes(rows)
+    return mode_in_group(rows, width) % (GROUP // 2) == lane // (LANES // 2)
+
+
+def own_half(rows):
+    return (mode_in_group(rows, LANES) < GROUP // 2) == low_lanes(rows)
+
+
+def to_depth(modes, table, snaps):
+    rows = modes.shape[0] // snaps
+    both = [doubled(modes[b * rows : (b + 1) * rows]) for b in range(snaps)]
+    result = dot(table, jnp.concatenate(both, axis=1).astype(BF16))
+    return jnp.concatenate(
+        [
+            result[g : g + GROUP, b * LANES : (b + 1) * LANES]
+            for g in range(0, result.shape[0], GROUP)
+            for b in range(snaps)
+        ],
+        axis=0,
+    )
+
+
+def from_depth(modes, table, snaps):
+    count = modes.shape[0] // GROUP
+    both = []
+    for b in range(snaps):
+        own = [modes[g * GROUP : (g + 1) * GROUP] for g in range(b, count, snaps)]
+        both.append(halved(jnp.concatenate(own, axis=0)))
+    result = dot(table, jnp.concatenate(both, axis=1).astype(BF16))
+    return jnp.concatenate(
+        [result[:, b * LANES : (b + 1) * LANES] for b in range(snaps)], axis=0
+    )
 
 
 def mix_kernel(snaps, received, gather, weights, scatter, back_out, diagonal_out):
-    both = doubled(received[...].astype(F32)).astype(BF16)
-    coef = dot(gather[...], both)
+    coef = to_depth(received[...].astype(F32), gather[...], snaps)
     count = coef.shape[0]
     wide = jnp.concatenate([coef] * (GROUP // 4), axis=1)
-    diagonal_out[...] = jnp.where(own_block(count, snaps), wide, 0.0).astype(BF16)
+    diagonal = jnp.where(own_block(count), wide, 0.0).astype(BF16)
+    diagonal_out[...] = diagonal
     rows = GROUP * snaps
     depth = GROUP * LANES // 4
     mixed = jnp.concatenate(
         [
-            dot(
-                diagonal_out[g * rows : (g + 1) * rows, :],
-                weights[g * depth : (g + 1) * depth, :],
-            )
+            dot(diagonal[g * rows : (g + 1) * rows, :], weights[g * depth : (g + 1) * depth, :])
             for g in range(count // rows)
         ],
         axis=0,
     )
-    mixed = jnp.where(own_half(count, snaps), mixed, swap_halves(mixed))
-    back_out[...] = dot(scatter[...], halved(mixed).astype(BF16)).astype(BF16)
+    mixed = jnp.where(own_half(count), mixed, swap_halves(mixed))
+    back_out[...] = from_depth(mixed, scatter[...], snaps).astype(BF16)
 
 
 def activate_kernel(
@@ -353,14 +375,14 @@
         modes, terms = slab_load(received)
     else:
         modes, terms = received[...].astype(F32), terms[...].astype(F32)
-    mixed = dot(gather[...], doubled(modes).astype(BF16))
+    mixed = to_depth(modes, gather[...], snaps)
     mixed_out[...] = mixed.astype(BF16)
     count = mixed.shape[0]
     rows = GROUP * snaps
     depth = GROUP * LANES // 4
     sums = jnp.sum(terms, axis=0) * scale
-    own = own_block(rows, snaps)
-    placed = jnp.where(own_half(count, snaps), mixed, 0.0).astype(BF16)
+    own = own_block(rows)
+    placed = jnp.where(own_half(count), mixed, 0.0).astype(BF16)
     pieces = []
     for g in range(count // rows):
         full = dot(
@@ -370,7 +392,7 @@
         pieces.append(sum(full[:, k : k + LANES] for k in range(0, depth, LANES)))
     coef = jnp.concatenate(pieces, axis=0)
     coef = coef + swap_halves(coef)
-    grad = dot(scatter[...], halved(coef).astype(BF16))
+    grad = from_depth(coef, scatter[...], snaps)
     if in_slab:
         owners = received.shape[0]
         share = sums.shape[0]
@@ -386,7 +408,7 @@
     rows = GROUP * snaps
     depth = GROUP * LANES // 4
     half = LANES // 2
-    first = mode_in_group(rows, depth, snaps) < GROUP // 2
+    first = mode_in_group(rows, depth) < GROUP // 2
     for g in range(diagonal.shape[0] // rows):
         span = slice(g * rows, (g + 1) * rows)
         blocks = diagonal[span, :].astype(F32)
@@ -455,6 +477,9 @@
         self.buffer[index] = value
         self.copy.start()
 
+    def __getitem__(self, index):
+        return self.buffer[index]
+
     @property
     def shape(self):
         return self.buffer.shape
@@ -463,7 +488,13 @@
 def run(body, outs, *operands, staged=(), sent=(), scratch=(), flops=0, limit=VMEM_BYTES):
     given = [k for k, operand in enumerate(operands) if operand is not None]
     made = [k for k, out in enumerate(outs) if out is not None]
-    sent = [k for k in made if k in sent]
+
+    def rows_of(chosen, places, arrays):
+        chosen = {k: chosen[k] if isinstance(chosen, dict) else None for k in places if k in chosen}
+        return {k: rows or arrays[k].shape[0] for k, rows in chosen.items()}
+
+    staged = rows_of(staged, given, operands)
+    sent = rows_of(sent, made, outs)
 
     def kernel(*refs):
         refs = list(refs)
@@ -473,13 +504,16 @@
             del refs[:count]
             return taken
 
+        def part(ref, rows):
+            return ref if ref.shape[0] == rows else ref.at[0:rows]
+
         filled = dict(zip(given, take(len(given))))
         kept = dict(zip(made, take(len(made))))
         own = take(len(scratch))
         for place, (k, buffer) in enumerate(zip(staged, take(len(staged)))):
-            filled[k] = Staged(filled[k], buffer, refs[-1].at[place])
+            filled[k] = Staged(part(filled[k], staged[k]), buffer, refs[-1].at[place])
         for place, (k, buffer) in enumerate(zip(sent, take(len(sent)))):
-            kept[k] = Sent(kept[k], buffer, refs[-1].at[len(staged) + place])
+            kept[k] = Sent(part(kept[k], sent[k]), buffer, refs[-1].at[len(staged) + place])
         body(
             *[filled.get(k) for k in range(len(operands))],
             *[kept.get(k) for k in range(len(outs))],
@@ -495,8 +529,9 @@
     size = sum(x.size * x.dtype.itemsize for x in (*arrays, *results))
     in_vmem = pl.BlockSpec(memory_space=pltpu.VMEM)
     in_hbm = pl.BlockSpec(memory_space=pltpu.HBM)
-    buffers = [operands[k] for k in staged] + [outs[k] for k in sent]
-    buffers = [pltpu.VMEM(x.shape, x.dtype) for x in buffers]
+    buffers = [(operands[k], rows) for k, rows in staged.items()]
+    buffers += [(outs[k], rows) for k, rows in sent.items()]
+    buffers = [pltpu.VMEM((rows, *x.shape[1:]), x.dtype) for x, rows in buffers]
     if buffers:
         buffers.append(pltpu.SemaphoreType.DMA((len(buffers),)))
     results = pl.pallas_call(
@@ -537,7 +572,7 @@
     in_slab = modes == 8 and devices * 32 == TERM_ROWS
 
     analysis, synthesis = plane_tables(batches, slabs)
-    gather, scatter, gather_back, scatter_back = depth_tables(batches, slabs, layers, modes)
+    gather, scatter, gather_back, scatter_back = depth_tables(slabs, layers, modes)
     weights = mode_weight.reshape(modes * 2 * KZ * channels, channels)
     taps = conv_weight.reshape(OFFSETS, channels, channels)
     field = shape((channels, layers, plane), BF16)
@@ -562,7 +597,13 @@
     packed = shape((weights.shape[0] // 2, LANES), BF16)
     weights, coef = lax.optimization_barrier((weights, coef))
     coef = send(coef)
-    (packed_weights,) = run(pack_kernel, [packed], weights)
+    packed_rows = packed.shape[0]
+    packed_weights, kept_weights = run(
+        pack_kernel,
+        [packed, shape((max(packed_rows, HBM_ROWS), LANES), BF16)],
+        weights,
+        sent={1: packed_rows},
+    )
     before, after = neighbours(first, last)
     local, lanes, outer_cells = run(
         local_kernel,
@@ -582,7 +623,7 @@
         gather,
         packed_weights,
         scatter,
-        sent=(0,),
+        sent=(0, 1),
         flops=4 * 10**8,
     )
     back = send(back)
@@ -603,12 +644,10 @@
         local,
         outer_cells,
         lanes,
-        sent=(0, 1, 2, 3, 4),
+        sent=(2, 3, 4),
         scratch=[pltpu.VMEM((CELLS + 2 * NY, 3 * LANES), BF16)],
         flops=10**9,
     )
-    weights, back = lax.optimization_barrier((weights, back))
-    (packed_weights,) = run(pack_kernel, [packed], weights)
     if in_slab:
         back = exchange(back)
     else:
@@ -621,9 +660,7 @@
         activated,
         flops=10**8,
     )
-    back, before, after, activated, packed_weights = lax.optimization_barrier(
-        (back, before, after, activated, packed_weights)
-    )
+    back, before, after, activated = lax.optimization_barrier((back, before, after, activated))
     scale = 1.0 / math.sqrt(batches * slabs * layers * plane)
     grad_modes, mixed_grad, sums = run(
         functools.partial(unmix_kernel, batches, scale),
@@ -635,8 +672,9 @@
         back,
         None if in_slab else terms,
         gather_back,
-        packed_weights,
+        kept_weights,
         scatter_back,
+        staged={3: packed_rows},
         sent=(0,),
         flops=4 * 10**8,
     )

time: 87.8 us -> 76.8 us (0.87)
  local copies, waits for them, and re-layouts: 24.6 us -> 9.14 us
  waiting for transfers between devices: 11.7 us -> 16.8 us
  starting transfers between devices: 31.7 us -> 28.9 us
  Pallas kernels: 18 us -> 20.5 us
    unnamed x72 -> x32, local copies, waits for them, and re-layouts: 24.6 us -> 9.14 us
    all_to_all x4, waiting for transfers between devices: 11.6 us -> 14.6 us  [exchange(): lax.all_to_all(values, ('batch', 'space'), split_axis=0, concat_axis=0, t...]
    all_to_all x4, starting transfers between devices: 24.6 us -> 22 us  [exchange(): lax.all_to_all(values, ('batch', 'space'), split_axis=0, concat_axis=0, t...]
    pallas_call x11 -> x10, Pallas kernels: 18 us -> 20.5 us  [run(): pl.pallas_call(kernel, out_shape=results, in_specs=[in_hbm if k in staged...]
    ppermute x2, waiting for transfers between devices: 0.05 us -> 2.13 us  [neighbours(): after = lax.ppermute(first, 'space', [(i + 1, i) for i in range(ends)])]
  transfers between devices with their start and end apart: 8 -> 8, of which waited for: 3 -> 5; matrix products, arithmetic and copies ran while one was open for 0% -> 0% of each run, Pallas kernels for 11% -> 14%
where the time goes in v8:
time: 76.8 us; the launch traced here: 76.1 us
  starting transfers between devices  28.9 us (38%)
  Pallas kernels  20.5 us (27%)
  waiting for transfers between devices  16.8 us (22%)
  local copies, waits for them, and re-layouts  9.14 us (12%)
  between operations  0.84 us (1%)
    all_to_all x4, starting transfers between devices, exchange(): lax.all_to_all(values, ('batch', 'space'), split_axis=0, concat_axis=0, t...  22 us
    pallas_call x10, Pallas kernels, run(): pl.pallas_call(kernel, out_shape=results, in_specs=[in_hbm if k in staged...  20.5 us
    all_to_all x4, waiting for transfers between devices, exchange(): lax.all_to_all(values, ('batch', 'space'), split_axis=0, concat_axis=0, t...  14.6 us
    unnamed x32, local copies, waits for them, and re-layouts  9.14 us
    ppermute x2, starting transfers between devices, neighbours(): before = lax.ppermute(last, 'space', [(i, i + 1) for i in range(ends)])  4.32 us
    ppermute x2, starting transfers between devices, neighbours(): after = lax.ppermute(first, 'space', [(i + 1, i) for i in range(ends)])  2.58 us
    ppermute x2, waiting for transfers between devices, neighbours(): after = lax.ppermute(first, 'space', [(i + 1, i) for i in range(ends)])  2.13 us
  transfers between devices with their start and end apart: 8, of which 5 were waited for; matrix products, arithmetic and copies ran while one was open for 0% of the time, Pallas kernels for 14%

profile of v8, /device:TPU:0, one launch (start us, length us, event | category | flops | bytes accessed | tf_op | source)
XLA Modules:
  0.0 76.1 jit_solution(11196900844849004046)
XLA Ops:
  0.6 2.5 %analyse_kernel.1 = (bf16[1024,128]{1,0:T(8,128)(2,1)}, bf16[256,128]{1,0:T(8,128)(2,1)}, bf16[512,128]{1,0:T(8,128)(2,1)}, bf16[512,128]{1,0:T(8,128)(2,1)}) custom-call(bf16[64,2,1024]{2,1,0:T(2,128)(2,1)} %bitcast.21, bf16[256,1024]{1,0:T(8,128)(2,1)} %constant.16.clone.refs_1_), custom_call_target="tpu_custom_call" | custom-call | flops 100000000 | bytes 1376256 | tf_op jit(solution)/shard_map/analyse_kernel/pallas_call | solution.py:537
  3.1 7.3 %all-to-all-start = ((bf16[32,8,128]{2,1,0:T(8,128)(2,1)}), bf16[32,8,128]{2,1,0:T(8,128)(2,1)S(1)}, u32[]{:S(2)}, u32[]{:S(2)}) async-start(bf16[32,8,128]{2,1,0:T(8,128)(2,1)} %bitcast.23), calls=%async_computation | async-start | bytes 131072 | tf_op jit(solution)/shard_map/all_to_all | solution.py:552
  10.4 2.2 %collective-permute-start = (bf16[512,128]{1,0:T(8,128)(2,1)}, bf16[512,128]{1,0:T(8,128)(2,1)S(1)}, u32[]{:S(2)}, u32[]{:S(2)}) collective-permute-start(bf16[512,128]{1,0:T(8,128)(2,1)} %get-tuple-element.36), channel_id=1, source_target_pairs={{0,1},{1,2},{2,3},{3,4},{4,5},{5,6},{6,7},{7,8},{8,9},{9,10},{10,1... | collective-permute-start | bytes 393224 | tf_op jit(solution)/shard_map/ppermute | solution.py:557
  12.6 1.3 %collective-permute-start.1 = (bf16[512,128]{1,0:T(8,128)(2,1)}, bf16[512,128]{1,0:T(8,128)(2,1)S(1)}, u32[]{:S(2)}, u32[]{:S(2)}) collective-permute-start(bf16[512,128]{1,0:T(8,128)(2,1)} %get-tuple-element.37), channel_id=1, source_target_pairs={{1,0},{2,1},{3,2},{4,3},{5,4},{6,5},{7,6},{8,7},{9,8},{10,9},{11,1... | collective-permute-start | bytes 393224 | tf_op jit(solution)/shard_map/ppermute | solution.py:558
  13.9 0.0 copy-start
  13.9 1.9 %copy-done = bf16[8,1,24,64,64]{4,3,2,1,0:T(8,128)(2,1)S(1)} copy-done((bf16[8,1,24,64,64]{4,3,2,1,0:T(8,128)(2,1)S(1)}, bf16[8,1,24,64,64]{4,3,2,1,0:T(8,128)(2,1)}, u32[]{:S(2)}) %copy-start) | copy-done | bytes 1572888
  15.8 0.0 copy-start.10
  15.8 0.0 copy-start.11
  15.8 0.0 copy-start.4
  15.8 0.0 copy-start.5
  15.8 1.9 %pack_kernel.1 = (bf16[6144,128]{1,0:T(8,128)(2,1)S(1)}, bf16[163840,128]{1,0:T(8,128)(2,1)}) custom-call(bf16[12288,64]{1,0:T(8,128)(2,1)S(1)} %bitcast.14), custom_call_target="tpu_custom_call" | custom-call | bytes 45088768 | tf_op jit(solution)/shard_map/pack_kernel/pallas_call | solution.py:537
  17.7 0.1 all-to-all-done
  17.8 0.0 copy-start.2
  17.8 0.9 %copy-done.2 = bf16[192,256]{1,0:T(8,128)(2,1)S(1)} copy-done((bf16[192,256]{1,0:T(8,128)(2,1)S(1)}, bf16[192,256]{1,0:T(8,128)(2,1)}, u32[]{:S(2)}) %copy-start.2) | copy-done | bytes 98328
  18.7 0.0 copy-start.3
  18.7 0.9 %copy-done.3 = bf16[128,384]{1,0:T(8,128)(2,1)S(1)} copy-done((bf16[128,384]{1,0:T(8,128)(2,1)S(1)}, bf16[128,384]{1,0:T(8,128)(2,1)}, u32[]{:S(2)}) %copy-start.3) | copy-done | bytes 98328
  19.6 1.8 %mix_kernel.1 = (bf16[256,128]{1,0:T(8,128)(2,1)}, bf16[384,256]{1,0:T(8,128)(2,1)S(1)}) custom-call(bf16[256,128]{1,0:T(8,128)(2,1)S(1)} %bitcast.15, bf16[192,256]{1,0:T(8,128)(2,1)S(1)} %copy-done.2, bf16[6144,128]{1,0:T(8,128)(2,1)S(1)} %get-tuple-element.33.refs_2_, bf16[128,384]{1,0:T(8,128)(2,1)S(1)} %copy-done.3), custom_call_target="tpu_custom_call" | custom-call | flops 400000000 | bytes 2097152 | tf_op jit(solution)/shard_map/mix_kernel/pallas_call | solution.py:537
  21.4 7.8 %all-to-all-start.1 = ((bf16[32,8,128]{2,1,0:T(8,128)(2,1)}), bf16[32,8,128]{2,1,0:T(8,128)(2,1)S(1)}, u32[]{:S(2)}, u32[]{:S(2)}) async-start(bf16[32,8,128]{2,1,0:T(8,128)(2,1)} %bitcast.4), calls=%async_computation.1 | async-start | bytes 131072 | tf_op jit(solution)/shard_map/all_to_all | solution.py:552
  29.2 0.0 collective-permute-done.refs_1_
  29.2 0.0 collective-permute-done.1.refs_2_
  29.3 0.0 copy-start.6
  29.3 1.0 %copy-done.6 = bf16[3,3,3,64,64]{4,3,2,1,0:T(8,128)(2,1)S(1)} copy-done((bf16[3,3,3,64,64]{4,3,2,1,0:T(8,128)(2,1)S(1)}, bf16[3,3,3,64,64]{4,3,2,1,0:T(8,128)(2,1)}, u32[]{:S(2)}) %copy-start.6) | copy-done | bytes 221208
  30.3 0.0 copy-start.8
  30.3 0.9 %copy-done.8 = bf16[1,64,2,1024]{3,2,1,0:T(2,128)(2,1)S(1)} copy-done((bf16[1,64,2,1024]{3,2,1,0:T(2,128)(2,1)S(1)}, bf16[1,64,2,1024]{3,2,1,0:T(2,128)(2,1)}, u32[]{:S(2)}) %copy-start.8) | copy-done | bytes 262168
  31.2 0.0 copy-start.9
  31.2 0.9 %copy-done.9 = bf16[1024,128]{1,0:T(8,128)(2,1)S(1)} copy-done((bf16[1024,128]{1,0:T(8,128)(2,1)S(1)}, bf16[1024,128]{1,0:T(8,128)(2,1)}, u32[]{:S(2)}) %copy-start.9) | copy-done | bytes 262168
  32.2 1.2 %local_kernel.1 = (f32[1024,128]{1,0:T(8,128)S(1)}, bf16[256,1024]{1,0:T(8,128)(2,1)S(1)}, bf16[1024,128]{1,0:T(8,128)(2,1)S(1)}) custom-call(bf16[1024,128]{1,0:T(8,128)(2,1)S(1)} %copy-done.9, bf16[512,128]{1,0:T(8,128)(2,1)S(1)} %collective-permute-done.refs_1_, bf16[512,128]{1,0:T(8,128)(2,1)S(1)} %collective-permute-done.1.refs_2_, ...), custom_call_target="tpu_custom_call" | custom-call | flops 700000000 | bytes 2318336 | tf_op jit(solution)/shard_map/local_kernel/pallas_call | solution.py:537
  33.4 0.0 copy-start.12
  33.4 0.8 %copy-done.12 = bf16[256,1024]{1,0:T(8,128)(2,1)} copy-done((bf16[256,1024]{1,0:T(8,128)(2,1)}, bf16[256,1024]{1,0:T(8,128)(2,1)S(1)}, u32[]{:S(2)}) %copy-start.12) | copy-done | bytes 524312
  34.2 2.5 %all-to-all-done.1 = bf16[32,8,128]{2,1,0:T(8,128)(2,1)S(1)} async-done(((bf16[32,8,128]{2,1,0:T(8,128)(2,1)}), bf16[32,8,128]{2,1,0:T(8,128)(2,1)S(1)}, u32[]{:S(2)}, u32[]{:S(2)}) %all-to-all-start.1) | async-done | bytes 65568 | tf_op jit(solution)/shard_map/all_to_all | solution.py:552
  36.6 0.0 copy-done.10
  36.6 0.0 copy-done.11
  36.7 0.0 copy-start.13
  36.7 1.0 %copy-done.13 = bf16[256,1024]{1,0:T(8,128)(2,1)S(1)} copy-done((bf16[256,1024]{1,0:T(8,128)(2,1)S(1)}, bf16[256,1024]{1,0:T(8,128)(2,1)}, u32[]{:S(2)}) %copy-start.13) | copy-done | bytes 524312
  37.7 2.9 %activate_kernel.1 = (bf16[1024,128]{1,0:T(8,128)(2,1)S(1)}, bf16[1024,128]{1,0:T(8,128)(2,1)S(1)}, bf16[512,128]{1,0:T(8,128)(2,1)S(1)}, bf16[512,128]{1,0:T(8,128)(2,1)S(1)}, bf16[32,40,128]{2,1,0:T(8,128)(2,1)}) custom-call(bf16[256,128]{1,0:T(8,128)(2,1)S(1)} %bitcast.16, bf16[1024,256]{1,0:T(8,128)(2,1)S(1)} %copy-done.10, ...), custom_call_target="tpu_custom_call" | custom-call | flops 1000000000 | bytes 3538944 | tf_op jit(solution)/shard_map/activate_kernel/pallas_call | solution.py:537
  40.6 0.0 copy-start.14
  40.6 0.7 copy-done.14
  41.3 3.3 %all-to-all-start.2 = ((bf16[32,40,128]{2,1,0:T(8,128)(2,1)}), bf16[32,40,128]{2,1,0:T(8,128)(2,1)S(1)}, u32[]{:S(2)}, u32[]{:S(2)}) async-start(bf16[32,40,128]{2,1,0:T(8,128)(2,1)} %get-tuple-element.41), calls=%async_computation.2 | async-start | bytes 655360 | tf_op jit(solution)/shard_map/all_to_all | solution.py:552
  44.7 2.2 %collective-permute-start.2 = (bf16[512,128]{1,0:T(8,128)(2,1)S(1)}, bf16[512,128]{1,0:T(8,128)(2,1)S(1)}, u32[]{:S(2)}, u32[]{:S(2)}) collective-permute-start(bf16[512,128]{1,0:T(8,128)(2,1)S(1)} %get-tuple-element.42), channel_id=1, source_target_pairs={{0,1},{1,2},{2,3},{3,4},{4,5},{5,6},{6,7},{7,8},{8,9},{9,10},{10,1... | collective-permute-start | bytes 393224 | tf_op jit(solution)/shard_map/ppermute | solution.py:557
  46.8 1.3 %collective-permute-start.3 = (bf16[512,128]{1,0:T(8,128)(2,1)S(1)}, bf16[512,128]{1,0:T(8,128)(2,1)S(1)}, u32[]{:S(2)}, u32[]{:S(2)}) collective-permute-start(bf16[512,128]{1,0:T(8,128)(2,1)S(1)} %get-tuple-element.43), channel_id=1, source_target_pairs={{1,0},{2,1},{3,2},{4,3},{5,4},{6,5},{7,6},{8,7},{9,8},{10,9},{11,1... | collective-permute-start | bytes 393224 | tf_op jit(solution)/shard_map/ppermute | solution.py:558
  48.1 0.9 %output_kernel.1 = bf16[64,2,1024]{2,1,0:T(2,128)(2,1)} custom-call(bf16[1024,128]{1,0:T(8,128)(2,1)S(1)} %get-tuple-element.44.refs_0_), custom_call_target="tpu_custom_call" | custom-call | flops 100000000 | bytes 524288 | tf_op jit(solution)/shard_map/output_kernel/pallas_call | solution.py:537
  49.1 0.0 collective-permute-done.2.refs_1_
  49.1 2.1 %collective-permute-done.3.refs_2_ = bf16[512,128]{1,0:T(8,128)(2,1)S(1)} collective-permute-done((bf16[512,128]{1,0:T(8,128)(2,1)S(1)}, bf16[512,128]{1,0:T(8,128)(2,1)S(1)}, u32[]{:S(2)}, u32[]{:S(2)}) %collective-permute-start.3) | collective-permute-done | bytes 131104 | tf_op jit(solution)/shard_map/ppermute | solution.py:558
  51.2 5.1 %all-to-all-done.2.refs_0_ = bf16[32,40,128]{2,1,0:T(8,128)(2,1)S(1)} async-done(((bf16[32,40,128]{2,1,0:T(8,128)(2,1)}), bf16[32,40,128]{2,1,0:T(8,128)(2,1)S(1)}, u32[]{:S(2)}, u32[]{:S(2)}) %all-to-all-start.2) | async-done | bytes 327712 | tf_op jit(solution)/shard_map/all_to_all | solution.py:552
  56.3 0.0 copy-done.4
  56.3 0.0 copy-done.5
  56.3 3.0 %unmix_kernel.1 = (bf16[32,40,128]{2,1,0:T(8,128)(2,1)}, bf16[384,128]{1,0:T(8,128)(2,1)S(1)}) custom-call(bf16[32,40,128]{2,1,0:T(8,128)(2,1)S(1)} %all-to-all-done.2.refs_0_, bf16[192,256]{1,0:T(8,128)(2,1)S(1)} %copy-done.4, bf16[163840,128]{1,0:T(8,128)(2,1)} %get-tuple-element.47.refs_2_, bf16[128,384]{1,0:T(8,128)(2,1)S(1)} %copy-done.5), custom_call_target="tpu_custom_call" | custom-call | flops 400000000 | bytes 42893312 | tf_op jit(solution)/shard_map/unmix_kernel/pallas_call | solution.py:537
  59.4 0.0 copy-start.7
  59.4 0.0 copy-start.15
  59.4 0.0 copy-start.1
  59.4 3.5 %all-to-all-start.3 = ((bf16[32,40,128]{2,1,0:T(8,128)(2,1)}), bf16[32,40,128]{2,1,0:T(8,128)(2,1)S(1)}, u32[]{:S(2)}, u32[]{:S(2)}) async-start(bf16[32,40,128]{2,1,0:T(8,128)(2,1)} %get-tuple-element.48), calls=%async_computation.3 | async-start | bytes 655360 | tf_op jit(solution)/shard_map/all_to_all | solution.py:552
  62.9 3.7 %weight_kernel.1 = f32[12288,64]{1,0:T(8,128)} custom-call(bf16[384,256]{1,0:T(8,128)(2,1)S(1)} %get-tuple-element.53.refs_0_, bf16[384,128]{1,0:T(8,128)(2,1)S(1)} %get-tuple-element.54.refs_1_), custom_call_target="tpu_custom_call" | custom-call | flops 400000000 | bytes 3440640 | tf_op jit(solution)/shard_map/weight_kernel/pallas_call | solution.py:537
  66.7 0.0 copy-done.7
  66.7 0.0 copy-done.15
  66.7 1.1 %local_grad_kernel.1.refs_2_ = f32[1024,128]{1,0:T(8,128)S(1)} custom-call(bf16[1024,128]{1,0:T(8,128)(2,1)S(1)} %copy-done.15, bf16[512,128]{1,0:T(8,128)(2,1)S(1)} %collective-permute-done.2.refs_1_, bf16[512,128]{1,0:T(8,128)(2,1)S(1)} %collective-permute-done.3.refs_2_, bf16[27,64,64]{2,1,0:T(8,128)(2,1)S(1)} %bitcast.18), custom_call_target="tpu_custom_call" | custom-call | flops 700000000 | bytes 1269760 | tf_op jit(solution)/shard_map/local_grad_kernel/pallas_call | solution.py:537
  67.7 6.9 %all-to-all-done.3.refs_0_ = bf16[32,40,128]{2,1,0:T(8,128)(2,1)S(1)} async-done(((bf16[32,40,128]{2,1,0:T(8,128)(2,1)}), bf16[32,40,128]{2,1,0:T(8,128)(2,1)S(1)}, u32[]{:S(2)}, u32[]{:S(2)}) %all-to-all-start.3) | async-done | bytes 327712 | tf_op jit(solution)/shard_map/all_to_all | solution.py:552
  74.6 0.0 copy-done.1
  74.6 1.5 %finish_kernel.1 = (bf16[64,2,1024]{2,1,0:T(2,128)(2,1)}, f32[27,64,64]{2,1,0:T(8,128)}) custom-call(bf16[32,40,128]{2,1,0:T(8,128)(2,1)S(1)} %all-to-all-done.3.refs_0_, bf16[1024,256]{1,0:T(8,128)(2,1)S(1)} %copy-done.1, f32[1024,128]{1,0:T(8,128)S(1)} %local_grad_kernel.1.refs_2_), custom_call_target="tpu_custom_call" | custom-call | flops 100000000 | bytes 2080768 | tf_op jit(solution)/shard_map/finish_kernel/pallas_call | solution.py:537
Async XLA Ops:
  3.1 14.7 %all-to-all-start = ((bf16[32,8,128]{2,1,0:T(8,128)(2,1)}), bf16[32,8,128]{2,1,0:T(8,128)(2,1)S(1)}, u32[]{:S(2)}, u32[]{:S(2)}) async-start(bf16[32,8,128]{2,1,0:T(8,128)(2,1)} %bitcast.23), calls=%async_computation | async-start | bytes 131072 | tf_op jit(solution)/shard_map/all_to_all | solution.py:552
  10.4 18.8 %collective-permute-start = (bf16[512,128]{1,0:T(8,128)(2,1)}, bf16[512,128]{1,0:T(8,128)(2,1)S(1)}, u32[]{:S(2)}, u32[]{:S(2)}) collective-permute-start(bf16[512,128]{1,0:T(8,128)(2,1)} %get-tuple-element.36), channel_id=1, source_target_pairs={{0,1},{1,2},{2,3},{3,4},{4,5},{5,6},{6,7},{7,8},{8,9},{9,10},{10,1... | collective-permute-start | bytes 393224 | tf_op jit(solution)/shard_map/ppermute | solution.py:557
  12.6 16.7 %collective-permute-start.1 = (bf16[512,128]{1,0:T(8,128)(2,1)}, bf16[512,128]{1,0:T(8,128)(2,1)S(1)}, u32[]{:S(2)}, u32[]{:S(2)}) collective-permute-start(bf16[512,128]{1,0:T(8,128)(2,1)} %get-tuple-element.37), channel_id=1, source_target_pairs={{1,0},{2,1},{3,2},{4,3},{5,4},{6,5},{7,6},{8,7},{9,8},{10,9},{11,1... | collective-permute-start | bytes 393224 | tf_op jit(solution)/shard_map/ppermute | solution.py:558
  13.9 1.9 %copy-start = (bf16[8,1,24,64,64]{4,3,2,1,0:T(8,128)(2,1)S(1)}, bf16[8,1,24,64,64]{4,3,2,1,0:T(8,128)(2,1)}, u32[]{:S(2)}) copy-start(bf16[8,1,24,64,64]{4,3,2,1,0:T(8,128)(2,1)} %param.14) | copy-start | bytes 4718596
  15.8 20.9 %copy-start.10 = (bf16[1024,256]{1,0:T(8,128)(2,1)S(1)}, bf16[1024,256]{1,0:T(8,128)(2,1)}, u32[]{:S(2)}) copy-start(bf16[1024,256]{1,0:T(8,128)(2,1)} %constant.19.clone.refs_1_) | copy-start | bytes 1572868
  15.8 20.9 %copy-start.11 = (bf16[256,1024]{1,0:T(8,128)(2,1)S(1)}, bf16[256,1024]{1,0:T(8,128)(2,1)}, u32[]{:S(2)}) copy-start(bf16[256,1024]{1,0:T(8,128)(2,1)} %constant.20.clone.refs_2_) | copy-start | bytes 1572868
  15.8 40.5 %copy-start.4 = (bf16[192,256]{1,0:T(8,128)(2,1)S(1)}, bf16[192,256]{1,0:T(8,128)(2,1)}, u32[]{:S(2)}) copy-start(bf16[192,256]{1,0:T(8,128)(2,1)} %constant.21.clone.refs_1_) | copy-start | bytes 294916
  15.8 40.6 %copy-start.5 = (bf16[128,384]{1,0:T(8,128)(2,1)S(1)}, bf16[128,384]{1,0:T(8,128)(2,1)}, u32[]{:S(2)}) copy-start(bf16[128,384]{1,0:T(8,128)(2,1)} %constant.22.clone.refs_3_) | copy-start | bytes 294916
  17.8 0.9 %copy-start.2 = (bf16[192,256]{1,0:T(8,128)(2,1)S(1)}, bf16[192,256]{1,0:T(8,128)(2,1)}, u32[]{:S(2)}) copy-start(bf16[192,256]{1,0:T(8,128)(2,1)} %constant.17.clone.refs_1_) | copy-start | bytes 294916
  18.7 0.9 %copy-start.3 = (bf16[128,384]{1,0:T(8,128)(2,1)S(1)}, bf16[128,384]{1,0:T(8,128)(2,1)}, u32[]{:S(2)}) copy-start(bf16[128,384]{1,0:T(8,128)(2,1)} %constant.18.clone.refs_3_) | copy-start | bytes 294916
  21.4 15.2 %all-to-all-start.1 = ((bf16[32,8,128]{2,1,0:T(8,128)(2,1)}), bf16[32,8,128]{2,1,0:T(8,128)(2,1)S(1)}, u32[]{:S(2)}, u32[]{:S(2)}) async-start(bf16[32,8,128]{2,1,0:T(8,128)(2,1)} %bitcast.4), calls=%async_computation.1 | async-start | bytes 131072 | tf_op jit(solution)/shard_map/all_to_all | solution.py:552
  29.3 1.0 %copy-start.6 = (bf16[3,3,3,64,64]{4,3,2,1,0:T(8,128)(2,1)S(1)}, bf16[3,3,3,64,64]{4,3,2,1,0:T(8,128)(2,1)}, u32[]{:S(2)}) copy-start(bf16[3,3,3,64,64]{4,3,2,1,0:T(8,128)(2,1)} %param.15) | copy-start | bytes 663556
  30.3 0.9 %copy-start.8 = (bf16[1,64,2,1024]{3,2,1,0:T(2,128)(2,1)S(1)}, bf16[1,64,2,1024]{3,2,1,0:T(2,128)(2,1)}, u32[]{:S(2)}) copy-start(bf16[1,64,2,1024]{3,2,1,0:T(2,128)(2,1)} %param.13) | copy-start | bytes 786436
  31.2 0.9 %copy-start.9 = (bf16[1024,128]{1,0:T(8,128)(2,1)S(1)}, bf16[1024,128]{1,0:T(8,128)(2,1)}, u32[]{:S(2)}) copy-start(bf16[1024,128]{1,0:T(8,128)(2,1)} %get-tuple-element.35.refs_0_) | copy-start | bytes 786436
  33.4 0.8 %copy-start.12 = (bf16[256,1024]{1,0:T(8,128)(2,1)}, bf16[256,1024]{1,0:T(8,128)(2,1)S(1)}, u32[]{:S(2)}) copy-start(bf16[256,1024]{1,0:T(8,128)(2,1)S(1)} %get-tuple-element.40.refs_5_) | copy-start | bytes 1572868
  36.7 1.0 %copy-start.13 = (bf16[256,1024]{1,0:T(8,128)(2,1)S(1)}, bf16[256,1024]{1,0:T(8,128)(2,1)}, u32[]{:S(2)}) copy-start(bf16[256,1024]{1,0:T(8,128)(2,1)} %copy-done.12) | copy-start | bytes 1572868
  40.6 0.7 copy-start.14
  41.3 15.0 %all-to-all-start.2 = ((bf16[32,40,128]{2,1,0:T(8,128)(2,1)}), bf16[32,40,128]{2,1,0:T(8,128)(2,1)S(1)}, u32[]{:S(2)}, u32[]{:S(2)}) async-start(bf16[32,40,128]{2,1,0:T(8,128)(2,1)} %get-tuple-element.41), calls=%async_computation.2 | async-start | bytes 655360 | tf_op jit(solution)/shard_map/all_to_all | solution.py:552
  44.7 4.4 %collective-permute-start.2 = (bf16[512,128]{1,0:T(8,128)(2,1)S(1)}, bf16[512,128]{1,0:T(8,128)(2,1)S(1)}, u32[]{:S(2)}, u32[]{:S(2)}) collective-permute-start(bf16[512,128]{1,0:T(8,128)(2,1)S(1)} %get-tuple-element.42), channel_id=1, source_target_pairs={{0,1},{1,2},{2,3},{3,4},{4,5},{5,6},{6,7},{7,8},{8,9},{9,10},{10,1... | collective-permute-start | bytes 393224 | tf_op jit(solution)/shard_map/ppermute | solution.py:557
  46.8 4.4 %collective-permute-start.3 = (bf16[512,128]{1,0:T(8,128)(2,1)S(1)}, bf16[512,128]{1,0:T(8,128)(2,1)S(1)}, u32[]{:S(2)}, u32[]{:S(2)}) collective-permute-start(bf16[512,128]{1,0:T(8,128)(2,1)S(1)} %get-tuple-element.43), channel_id=1, source_target_pairs={{1,0},{2,1},{3,2},{4,3},{5,4},{6,5},{7,6},{8,7},{9,8},{10,9},{11,1... | collective-permute-start | bytes 393224 | tf_op jit(solution)/shard_map/ppermute | solution.py:558
  59.4 7.3 %copy-start.7 = (bf16[3,3,3,64,64]{4,3,2,1,0:T(8,128)(2,1)S(1)}, bf16[3,3,3,64,64]{4,3,2,1,0:T(8,128)(2,1)}, u32[]{:S(2)}) copy-start(bf16[3,3,3,64,64]{4,3,2,1,0:T(8,128)(2,1)} %param.15) | copy-start | bytes 663556
  59.4 7.3 %copy-start.15 = (bf16[1024,128]{1,0:T(8,128)(2,1)S(1)}, bf16[1024,128]{1,0:T(8,128)(2,1)}, u32[]{:S(2)}) copy-start(bf16[1024,128]{1,0:T(8,128)(2,1)} %copy-done.14) | copy-start | bytes 786436
  59.4 15.2 %copy-start.1 = (bf16[1024,256]{1,0:T(8,128)(2,1)S(1)}, bf16[1024,256]{1,0:T(8,128)(2,1)}, u32[]{:S(2)}) copy-start(bf16[1024,256]{1,0:T(8,128)(2,1)} %constant.23.clone.refs_1_) | copy-start | bytes 1572868
  59.4 15.2 %all-to-all-start.3 = ((bf16[32,40,128]{2,1,0:T(8,128)(2,1)}), bf16[32,40,128]{2,1,0:T(8,128)(2,1)S(1)}, u32[]{:S(2)}, u32[]{:S(2)}) async-start(bf16[32,40,128]{2,1,0:T(8,128)(2,1)} %get-tuple-element.48), calls=%async_computation.3 | async-start | bytes 655360 | tf_op jit(solution)/shard_map/all_to_all | solution.py:552

commit v9 on v8

--- a/solution.py
+++ b/solution.py
@@ -22,7 +22,7 @@
 TERM_ROWS = 1024
 VMEM_BYTES = 40 * 1024 * 1024
 WHOLE_VMEM = 65000 * 1024
-HBM_ROWS = 163840
+HBM_BYTES = 100 * 1024 * 256
 
 F32 = jnp.float32
 BF16 = jnp.bfloat16
@@ -230,13 +230,12 @@
     cotangent_out[...] = to_cells(cotangent[...]).astype(BF16)
 
 
-def pack_kernel(weights, out, kept):
+def pack_kernel(weights, out):
     rows = GROUP * LANES // 4
     for g in range(out.shape[0] // rows):
         first = weights[2 * g * rows : (2 * g + 1) * rows, :]
         second = weights[(2 * g + 1) * rows : (2 * g + 2) * rows, :]
         out[g * rows : (g + 1) * rows, :] = jnp.concatenate([first, second], axis=1)
-    kept[...] = out[...]
 
 
 def mode_in_group(rows, lanes):
@@ -485,7 +484,9 @@
         return self.buffer.shape
 
 
-def run(body, outs, *operands, staged=(), sent=(), scratch=(), flops=0, limit=VMEM_BYTES):
+def run(
+    body, outs, *operands, staged=(), sent=(), moved=(), scratch=(), flops=0, limit=VMEM_BYTES
+):
     given = [k for k, operand in enumerate(operands) if operand is not None]
     made = [k for k, out in enumerate(outs) if out is not None]
 
@@ -510,19 +511,31 @@
         filled = dict(zip(given, take(len(given))))
         kept = dict(zip(made, take(len(made))))
         own = take(len(scratch))
+        copies = [
+            pltpu.make_async_copy(
+                filled.pop(k),
+                part(kept.pop(out), operands[k].shape[0]),
+                refs[-1].at[len(staged) + len(sent) + place],
+            )
+            for place, (k, out) in enumerate(dict(moved).items())
+        ]
         for place, (k, buffer) in enumerate(zip(staged, take(len(staged)))):
             filled[k] = Staged(part(filled[k], staged[k]), buffer, refs[-1].at[place])
         for place, (k, buffer) in enumerate(zip(sent, take(len(sent)))):
             kept[k] = Sent(part(kept[k], sent[k]), buffer, refs[-1].at[len(staged) + place])
+        for copy in copies:
+            copy.start()
         body(
-            *[filled.get(k) for k in range(len(operands))],
-            *[kept.get(k) for k in range(len(outs))],
+            *[filled.get(k) for k in range(len(operands)) if k not in dict(moved)],
+            *[kept.get(k) for k in range(len(outs)) if k not in dict(moved).values()],
             *own,
         )
         for k in staged:
             filled[k].load()
         for k in sent:
             kept[k].copy.wait()
+        for copy in copies:
+            copy.wait()
 
     arrays = [operands[k] for k in given]
     results = [outs[k] for k in made]
@@ -532,13 +545,13 @@
     buffers = [(operands[k], rows) for k, rows in staged.items()]
     buffers += [(outs[k], rows) for k, rows in sent.items()]
     buffers = [pltpu.VMEM((rows, *x.shape[1:]), x.dtype) for x, rows in buffers]
-    if buffers:
-        buffers.append(pltpu.SemaphoreType.DMA((len(buffers),)))
+    if len(buffers) + len(moved) > 0:
+        buffers.append(pltpu.SemaphoreType.DMA((len(buffers) + len(moved),)))
     results = pl.pallas_call(
         kernel,
         out_shape=results,
-        in_specs=[in_hbm if k in staged else in_vmem for k in given],
-        out_specs=[in_hbm if k in sent else in_vmem for k in made],
+        in_specs=[in_hbm if k in staged or k in moved else in_vmem for k in given],
+        out_specs=[in_hbm if k in sent or k in dict(moved).values() else in_vmem for k in made],
         scratch_shapes=[*scratch, *buffers],
         compiler_params=pltpu.CompilerParams(vmem_limit_bytes=limit),
         cost_estimate=pl.CostEstimate(flops=flops, bytes_accessed=size, transcendentals=0),
@@ -584,35 +597,37 @@
     def send(values):
         return exchange(values.reshape(devices, modes, LANES)).reshape(plane_rows, LANES)
 
-    cells, coef, first, last = run(
+    cells, coef, first, last, weights = run(
         analyse_kernel,
-        [wide, plane_modes, edge, edge],
+        [wide, plane_modes, edge, edge, shape((HBM_BYTES // (2 * LANES), channels), BF16)],
         snapshots.reshape(field.shape),
         analysis,
+        weights,
         staged=(0, 1),
         sent=(0, 1, 2, 3),
+        moved={2: 4},
         limit=WHOLE_VMEM,
         flops=10**8,
     )
-    packed = shape((weights.shape[0] // 2, LANES), BF16)
-    weights, coef = lax.optimization_barrier((weights, coef))
+    rows = count * channels // batches
+
+    def pack(weights, first):
+        weights, first = lax.optimization_barrier((weights, first))
+        packed = shape((rows // 2, LANES), BF16)
+        return run(pack_kernel, [packed], weights, staged={0: rows})[0], first
+
+    packed_weights, coef = pack(weights, coef)
     coef = send(coef)
-    packed_rows = packed.shape[0]
-    packed_weights, kept_weights = run(
-        pack_kernel,
-        [packed, shape((max(packed_rows, HBM_ROWS), LANES), BF16)],
-        weights,
-        sent={1: packed_rows},
-    )
     before, after = neighbours(first, last)
     local, lanes, outer_cells = run(
         local_kernel,
-        [shape((CELLS, LANES), F32), shape((2 * LANES, CELLS), BF16), wide],
+        [shape((CELLS, LANES), F32), shape((HBM_BYTES // (2 * CELLS), CELLS), BF16), wide],
         cells,
         before,
         after,
         cotangent.reshape(field.shape),
         taps,
+        sent={1: 2 * LANES},
         scratch=[padded, pltpu.VMEM((3, 2 * LANES, 3 * LANES), BF16)],
         flops=7 * 10**8,
     )
@@ -632,7 +647,7 @@
         functools.partial(activate_kernel, in_slab),
         [
             wide,
-            wide,
+            shape((HBM_BYTES // (2 * LANES), LANES), BF16),
             edge,
             edge,
             slab if in_slab else plane_modes,
@@ -644,10 +659,12 @@
         local,
         outer_cells,
         lanes,
-        sent=(2, 3, 4),
+        staged={5: 2 * LANES},
+        sent={1: CELLS, 2: None, 3: None, 4: None},
         scratch=[pltpu.VMEM((CELLS + 2 * NY, 3 * LANES), BF16)],
         flops=10**9,
     )
+    packed_weights, back = pack(weights, back)
     if in_slab:
         back = exchange(back)
     else:
@@ -660,7 +677,9 @@
         activated,
         flops=10**8,
     )
-    back, before, after, activated = lax.optimization_barrier((back, before, after, activated))
+    back, before, after, activated, packed_weights = lax.optimization_barrier(
+        (back, before, after, activated, packed_weights)
+    )
     scale = 1.0 / math.sqrt(batches * slabs * layers * plane)
     grad_modes, mixed_grad, sums = run(
         functools.partial(unmix_kernel, batches, scale),
@@ -672,9 +691,8 @@
         back,
         None if in_slab else terms,
         gather_back,
-        kept_weights,
+        packed_weights,
         scatter_back,
-        staged={3: packed_rows},
         sent=(0,),
         flops=4 * 10**8,
     )
@@ -690,6 +708,7 @@
         before,
         after,
         taps,
+        staged={0: CELLS},
         scratch=[padded, pltpu.VMEM((3, 3 * LANES, 2 * LANES), BF16)],
         flops=7 * 10**8,
     )

time: 76.8 us -> 166 us (2.16)
  Pallas kernels: 20.5 us -> 119 us
  local copies, waits for them, and re-layouts: 9.14 us -> 2.55 us
  waiting for transfers between devices: 16.8 us -> 13.9 us
    pallas_call x10 -> x11, Pallas kernels: 20.5 us -> 119 us  [run(): pl.pallas_call(kernel, out_shape=results, in_specs=[in_hbm if k in staged...]
    unnamed x32 -> x22, local copies, waits for them, and re-layouts: 9.14 us -> 2.55 us
    ppermute x2, waiting for transfers between devices: 2.13 us -> 0.01 us  [neighbours(): after = lax.ppermute(first, 'space', [(i + 1, i) for i in range(ends)])]
  transfers between devices with their start and end apart: 8 -> 8, of which waited for: 5 -> 4; matrix products, arithmetic and copies ran while one was open for 0% -> 0% of each run, Pallas kernels for 14% -> 9%
where the time goes in v9:
time: 166 us; the launch traced here: 165 us
  Pallas kernels  119 us (72%)
  starting transfers between devices  28.9 us (17%)
  waiting for transfers between devices  13.9 us (8%)
  local copies, waits for them, and re-layouts  2.55 us (2%)
    pallas_call x11, Pallas kernels, run(): pl.pallas_call(kernel, out_shape=results, in_specs=[in_hbm if k in staged...  119 us
    all_to_all x4, starting transfers between devices, exchange(): lax.all_to_all(values, ('batch', 'space'), split_axis=0, concat_axis=0, t...  21.1 us
    all_to_all x4, waiting for transfers between devices, exchange(): lax.all_to_all(values, ('batch', 'space'), split_axis=0, concat_axis=0, t...  13.9 us
    ppermute x2, starting transfers between devices, neighbours(): before = lax.ppermute(last, 'space', [(i, i + 1) for i in range(ends)])  4.98 us
  transfers between devices with their start and end apart: 8, of which 4 were waited for; matrix products, arithmetic and copies ran while one was open for 0% of the time, Pallas kernels for 9%

profile of v9, /device:TPU:0, one launch (start us, length us, event | category | flops | bytes accessed | tf_op | source)
XLA Modules:
  0.0 165.4 jit_solution(15833011150859385180)
XLA Ops:
  0.6 96.5 %analyse_kernel.1 = (bf16[1024,128]{1,0:T(8,128)(2,1)}, bf16[256,128]{1,0:T(8,128)(2,1)}, bf16[512,128]{1,0:T(8,128)(2,1)}, bf16[512,128]{1,0:T(8,128)(2,1)}, bf16[102400,64]{1,0:T(8,128)(2,1)}) custom-call(bf16[64,2,1024]{2,1,0:T(2,128)(2,1)} %bitcast.23, bf16[256,1024]{1,0:T(8,128)(2,1)} %constant.16.clone.refs_1_, bf16[12288,64]{1,0:T(8,128)(2,1)} %bitcast.21), custom_call_target="tpu_custom_call" | custom-call | flops 100000000 | bytes 16056320 | tf_op jit(solution)/shard_map/analyse_kernel/pallas_call | solution.py:550
  97.1 7.3 %all-to-all-start = ((bf16[32,8,128]{2,1,0:T(8,128)(2,1)}), bf16[32,8,128]{2,1,0:T(8,128)(2,1)S(1)}, u32[]{:S(2)}, u32[]{:S(2)}) async-start(bf16[32,8,128]{2,1,0:T(8,128)(2,1)} %bitcast.24), calls=%async_computation | async-start | bytes 131072 | tf_op jit(solution)/shard_map/all_to_all | solution.py:565
  104.4 2.8 %collective-permute-start = (bf16[512,128]{1,0:T(8,128)(2,1)}, bf16[512,128]{1,0:T(8,128)(2,1)}, u32[]{:S(2)}, u32[]{:S(2)}) collective-permute-start(bf16[512,128]{1,0:T(8,128)(2,1)} %get-tuple-element.38), channel_id=1, source_target_pairs={{0,1},{1,2},{2,3},{3,4},{4,5},{5,6},{6,7},{7,8},{8,9},{9,10},{10,1... | collective-permute-start | bytes 393224 | tf_op jit(solution)/shard_map/ppermute | solution.py:570
  107.2 0.0 copy-start.6
  107.2 0.0 copy-start.7
  107.2 0.0 copy-start.3
  107.2 0.0 copy-start
  107.2 0.0 copy-start.1
  107.2 1.4 collective-permute-start.1
  108.7 2.4 %pack_kernel.2.refs_2_ = bf16[6144,128]{1,0:T(8,128)(2,1)S(1)} custom-call(bf16[102400,64]{1,0:T(8,128)(2,1)} %get-tuple-element.48.refs_0_), custom_call_target="tpu_custom_call" | custom-call | bytes 14680064 | tf_op jit(solution)/shard_map/pack_kernel/pallas_call | solution.py:550
  111.1 0.8 all-to-all-done
  111.8 0.0 copy-done.6
  111.8 0.0 copy-done.7
  111.8 1.2 mix_kernel.1
  113.1 0.0 copy-start.8
  113.1 0.6 copy-done.8
  113.7 6.6 %all-to-all-start.1 = ((bf16[32,8,128]{2,1,0:T(8,128)(2,1)}), bf16[32,8,128]{2,1,0:T(8,128)(2,1)S(1)}, u32[]{:S(2)}, u32[]{:S(2)}) async-start(bf16[32,8,128]{2,1,0:T(8,128)(2,1)} %bitcast.18), calls=%async_computation.1 | async-start | bytes 131072 | tf_op jit(solution)/shard_map/all_to_all | solution.py:565
  120.3 0.0 collective-permute-done.refs_1_
  120.3 0.0 collective-permute-done.1.refs_2_
  120.3 0.0 copy-done.3
  120.4 0.0 copy-start.9
  120.4 0.9 copy-done.9
  121.3 0.0 copy-start.10
  121.3 0.9 copy-done.10
  122.3 2.9 %local_kernel.1 = (f32[1024,128]{1,0:T(8,128)S(1)}, bf16[12800,1024]{1,0:T(8,128)(2,1)}, bf16[1024,128]{1,0:T(8,128)(2,1)S(1)}) custom-call(bf16[1024,128]{1,0:T(8,128)(2,1)S(1)} %copy-done.10, bf16[512,128]{1,0:T(8,128)(2,1)} %collective-permute-done.refs_1_, bf16[512,128]{1,0:T(8,128)(2,1)} %collective-permute-done.1.refs_2_, ...), custom_call_target="tpu_custom_call" | custom-call | flops 700000000 | bytes 28008448 | tf_op jit(solution)/shard_map/local_kernel/pallas_call | solution.py:550
  125.2 2.6 %all-to-all-done.1 = bf16[32,8,128]{2,1,0:T(8,128)(2,1)S(1)} async-done(((bf16[32,8,128]{2,1,0:T(8,128)(2,1)}), bf16[32,8,128]{2,1,0:T(8,128)(2,1)S(1)}, u32[]{:S(2)}, u32[]{:S(2)}) %all-to-all-start.1) | async-done | bytes 65568 | tf_op jit(solution)/shard_map/all_to_all | solution.py:565
  127.7 0.0 copy-done
  127.7 0.0 copy-done.1
  127.7 3.8 %activate_kernel.1 = (bf16[1024,128]{1,0:T(8,128)(2,1)S(1)}, bf16[102400,128]{1,0:T(8,128)(2,1)}, bf16[512,128]{1,0:T(8,128)(2,1)}, bf16[512,128]{1,0:T(8,128)(2,1)}, bf16[32,40,128]{2,1,0:T(8,128)(2,1)}) custom-call(bf16[256,128]{1,0:T(8,128)(2,1)S(1)} %bitcast.16, bf16[1024,256]{1,0:T(8,128)(2,1)S(1)} %copy-done.1, bf16[256,1024]{1,0:T(8,128)(2,1)S(1)} %copy-done, ...), custom_call_target="tpu_custom_call" | custom-call | flops 1000000000 | bytes 55181312 | tf_op jit(solution)/shard_map/activate_kernel/pallas_call | solution.py:550
  131.5 3.3 %all-to-all-start.2 = ((bf16[32,40,128]{2,1,0:T(8,128)(2,1)}), bf16[32,40,128]{2,1,0:T(8,128)(2,1)S(1)}, u32[]{:S(2)}, u32[]{:S(2)}) async-start(bf16[32,40,128]{2,1,0:T(8,128)(2,1)} %get-tuple-element.44), calls=%async_computation.2 | async-start | bytes 655360 | tf_op jit(solution)/shard_map/all_to_all | solution.py:565
  134.8 2.2 %collective-permute-start.2 = (bf16[512,128]{1,0:T(8,128)(2,1)}, bf16[512,128]{1,0:T(8,128)(2,1)S(1)}, u32[]{:S(2)}, u32[]{:S(2)}) collective-permute-start(bf16[512,128]{1,0:T(8,128)(2,1)} %get-tuple-element.45), channel_id=1, source_target_pairs={{0,1},{1,2},{2,3},{3,4},{4,5},{5,6},{6,7},{7,8},{8,9},{9,10},{10,1... | collective-permute-start | bytes 393224 | tf_op jit(solution)/shard_map/ppermute | solution.py:570
  137.0 0.0 copy-start.4
  137.0 0.0 copy-start.5
  137.0 1.4 collective-permute-start.3
  138.5 2.4 %pack_kernel.3.refs_2_ = bf16[6144,128]{1,0:T(8,128)(2,1)S(1)} custom-call(bf16[102400,64]{1,0:T(8,128)(2,1)} %get-tuple-element.48.refs_0_), custom_call_target="tpu_custom_call" | custom-call | bytes 14680064 | tf_op jit(solution)/shard_map/pack_kernel/pallas_call | solution.py:550
  140.8 0.9 output_kernel.1
  141.8 0.0 collective-permute-done.2.refs_1_
  141.8 0.0 collective-permute-done.3.refs_2_
  141.8 4.7 %all-to-all-done.2.refs_0_ = bf16[32,40,128]{2,1,0:T(8,128)(2,1)S(1)} async-done(((bf16[32,40,128]{2,1,0:T(8,128)(2,1)}), bf16[32,40,128]{2,1,0:T(8,128)(2,1)S(1)}, u32[]{:S(2)}, u32[]{:S(2)}) %all-to-all-start.2) | async-done | bytes 327712 | tf_op jit(solution)/shard_map/all_to_all | solution.py:565
  146.5 0.0 copy-done.4
  146.5 0.0 copy-done.5
  146.5 1.8 %unmix_kernel.1 = (bf16[32,40,128]{2,1,0:T(8,128)(2,1)}, bf16[384,128]{1,0:T(8,128)(2,1)S(1)}) custom-call(bf16[32,40,128]{2,1,0:T(8,128)(2,1)S(1)} %all-to-all-done.2.refs_0_, bf16[192,256]{1,0:T(8,128)(2,1)S(1)} %copy-done.5, bf16[6144,128]{1,0:T(8,128)(2,1)S(1)} %pack_kernel.3.refs_2_, bf16[128,384]{1,0:T(8,128)(2,1)S(1)} %copy-done.4), custom_call_target="tpu_custom_call" | custom-call | flops 400000000 | bytes 2523136 | tf_op jit(solution)/shard_map/unmix_kernel/pallas_call | solution.py:550
  148.3 3.9 %all-to-all-start.3 = ((bf16[32,40,128]{2,1,0:T(8,128)(2,1)}), bf16[32,40,128]{2,1,0:T(8,128)(2,1)S(1)}, u32[]{:S(2)}, u32[]{:S(2)}) async-start(bf16[32,40,128]{2,1,0:T(8,128)(2,1)} %get-tuple-element.52), calls=%async_computation.3 | async-start | bytes 655360 | tf_op jit(solution)/shard_map/all_to_all | solution.py:565
  152.2 3.7 %weight_kernel.1 = f32[12288,64]{1,0:T(8,128)} custom-call(bf16[384,256]{1,0:T(8,128)(2,1)S(1)} %get-tuple-element.57.refs_0_, bf16[384,128]{1,0:T(8,128)(2,1)S(1)} %get-tuple-element.58.refs_1_), custom_call_target="tpu_custom_call" | custom-call | flops 400000000 | bytes 3440640 | tf_op jit(solution)/shard_map/weight_kernel/pallas_call | solution.py:550
  155.9 0.0 copy-start.2
  155.9 2.1 %local_grad_kernel.1.refs_2_ = f32[1024,128]{1,0:T(8,128)S(1)} custom-call(bf16[102400,128]{1,0:T(8,128)(2,1)} %get-tuple-element.53.refs_0_, bf16[512,128]{1,0:T(8,128)(2,1)S(1)} %collective-permute-done.2.refs_1_, bf16[512,128]{1,0:T(8,128)(2,1)S(1)} %collective-permute-done.3.refs_2_, bf16[27,64,64]{2,1,0:T(8,128)(2,1)S(1)} %bitcast.15), custom_call_target="tpu_custom_call" | custom-call | flops 700000000 | bytes 27222016 | tf_op jit(solution)/shard_map/local_grad_kernel/pallas_call | solution.py:550
  158.0 5.9 %all-to-all-done.3.refs_0_ = bf16[32,40,128]{2,1,0:T(8,128)(2,1)S(1)} async-done(((bf16[32,40,128]{2,1,0:T(8,128)(2,1)}), bf16[32,40,128]{2,1,0:T(8,128)(2,1)S(1)}, u32[]{:S(2)}, u32[]{:S(2)}) %all-to-all-start.3) | async-done | bytes 327712 | tf_op jit(solution)/shard_map/all_to_all | solution.py:565
  163.9 0.0 copy-done.2
  163.9 1.5 finish_kernel.1
Async XLA Ops:
  97.1 14.7 %all-to-all-start = ((bf16[32,8,128]{2,1,0:T(8,128)(2,1)}), bf16[32,8,128]{2,1,0:T(8,128)(2,1)S(1)}, u32[]{:S(2)}, u32[]{:S(2)}) async-start(bf16[32,8,128]{2,1,0:T(8,128)(2,1)} %bitcast.24), calls=%async_computation | async-start | bytes 131072 | tf_op jit(solution)/shard_map/all_to_all | solution.py:565
  104.4 15.9 %collective-permute-start = (bf16[512,128]{1,0:T(8,128)(2,1)}, bf16[512,128]{1,0:T(8,128)(2,1)}, u32[]{:S(2)}, u32[]{:S(2)}) collective-permute-start(bf16[512,128]{1,0:T(8,128)(2,1)} %get-tuple-element.38), channel_id=1, source_target_pairs={{0,1},{1,2},{2,3},{3,4},{4,5},{5,6},{6,7},{7,8},{8,9},{9,10},{10,1... | collective-permute-start | bytes 393224 | tf_op jit(solution)/shard_map/ppermute | solution.py:570
  107.2 4.6 %copy-start.6 = (bf16[128,384]{1,0:T(8,128)(2,1)S(1)}, bf16[128,384]{1,0:T(8,128)(2,1)}, u32[]{:S(2)}) copy-start(bf16[128,384]{1,0:T(8,128)(2,1)} %constant.18.clone.refs_3_) | copy-start | bytes 294916
  107.2 4.6 %copy-start.7 = (bf16[192,256]{1,0:T(8,128)(2,1)S(1)}, bf16[192,256]{1,0:T(8,128)(2,1)}, u32[]{:S(2)}) copy-start(bf16[192,256]{1,0:T(8,128)(2,1)} %constant.17.clone.refs_1_) | copy-start | bytes 294916
  107.2 13.1 %copy-start.3 = (bf16[3,3,3,64,64]{4,3,2,1,0:T(8,128)(2,1)S(1)}, bf16[3,3,3,64,64]{4,3,2,1,0:T(8,128)(2,1)}, u32[]{:S(2)}) copy-start(bf16[3,3,3,64,64]{4,3,2,1,0:T(8,128)(2,1)} %param.15) | copy-start | bytes 663556
  107.2 20.5 %copy-start = (bf16[256,1024]{1,0:T(8,128)(2,1)S(1)}, bf16[256,1024]{1,0:T(8,128)(2,1)}, u32[]{:S(2)}) copy-start(bf16[256,1024]{1,0:T(8,128)(2,1)} %constant.20.clone.refs_2_) | copy-start | bytes 1572868
  107.2 20.5 %copy-start.1 = (bf16[1024,256]{1,0:T(8,128)(2,1)S(1)}, bf16[1024,256]{1,0:T(8,128)(2,1)}, u32[]{:S(2)}) copy-start(bf16[1024,256]{1,0:T(8,128)(2,1)} %constant.19.clone.refs_1_) | copy-start | bytes 1572868
  107.2 13.1 %collective-permute-start.1 = (bf16[512,128]{1,0:T(8,128)(2,1)}, bf16[512,128]{1,0:T(8,128)(2,1)}, u32[]{:S(2)}, u32[]{:S(2)}) collective-permute-start(bf16[512,128]{1,0:T(8,128)(2,1)} %get-tuple-element.39), channel_id=1, source_target_pairs={{1,0},{2,1},{3,2},{4,3},{5,4},{6,5},{7,6},{8,7},{9,8},{10,9},{11,1... | collective-permute-start | bytes 393224 | tf_op jit(solution)/shard_map/ppermute | solution.py:571
  113.1 0.6 copy-start.8
  113.7 14.0 %all-to-all-start.1 = ((bf16[32,8,128]{2,1,0:T(8,128)(2,1)}), bf16[32,8,128]{2,1,0:T(8,128)(2,1)S(1)}, u32[]{:S(2)}, u32[]{:S(2)}) async-start(bf16[32,8,128]{2,1,0:T(8,128)(2,1)} %bitcast.18), calls=%async_computation.1 | async-start | bytes 131072 | tf_op jit(solution)/shard_map/all_to_all | solution.py:565
  120.4 1.0 copy-start.9
  121.3 0.9 copy-start.10
  131.5 15.0 %all-to-all-start.2 = ((bf16[32,40,128]{2,1,0:T(8,128)(2,1)}), bf16[32,40,128]{2,1,0:T(8,128)(2,1)S(1)}, u32[]{:S(2)}, u32[]{:S(2)}) async-start(bf16[32,40,128]{2,1,0:T(8,128)(2,1)} %get-tuple-element.44), calls=%async_computation.2 | async-start | bytes 655360 | tf_op jit(solution)/shard_map/all_to_all | solution.py:565
  134.8 7.0 %collective-permute-start.2 = (bf16[512,128]{1,0:T(8,128)(2,1)}, bf16[512,128]{1,0:T(8,128)(2,1)S(1)}, u32[]{:S(2)}, u32[]{:S(2)}) collective-permute-start(bf16[512,128]{1,0:T(8,128)(2,1)} %get-tuple-element.45), channel_id=1, source_target_pairs={{0,1},{1,2},{2,3},{3,4},{4,5},{5,6},{6,7},{7,8},{8,9},{9,10},{10,1... | collective-permute-start | bytes 393224 | tf_op jit(solution)/shard_map/ppermute | solution.py:570
  137.0 9.5 %copy-start.4 = (bf16[128,384]{1,0:T(8,128)(2,1)S(1)}, bf16[128,384]{1,0:T(8,128)(2,1)}, u32[]{:S(2)}) copy-start(bf16[128,384]{1,0:T(8,128)(2,1)} %constant.22.clone.refs_3_) | copy-start | bytes 294916
  137.0 9.5 %copy-start.5 = (bf16[192,256]{1,0:T(8,128)(2,1)S(1)}, bf16[192,256]{1,0:T(8,128)(2,1)}, u32[]{:S(2)}) copy-start(bf16[192,256]{1,0:T(8,128)(2,1)} %constant.21.clone.refs_1_) | copy-start | bytes 294916
  137.0 4.8 %collective-permute-start.3 = (bf16[512,128]{1,0:T(8,128)(2,1)}, bf16[512,128]{1,0:T(8,128)(2,1)S(1)}, u32[]{:S(2)}, u32[]{:S(2)}) collective-permute-start(bf16[512,128]{1,0:T(8,128)(2,1)} %get-tuple-element.46), channel_id=1, source_target_pairs={{1,0},{2,1},{3,2},{4,3},{5,4},{6,5},{7,6},{8,7},{9,8},{10,9},{11,1... | collective-permute-start | bytes 393224 | tf_op jit(solution)/shard_map/ppermute | solution.py:571
  148.3 15.6 %all-to-all-start.3 = ((bf16[32,40,128]{2,1,0:T(8,128)(2,1)}), bf16[32,40,128]{2,1,0:T(8,128)(2,1)S(1)}, u32[]{:S(2)}, u32[]{:S(2)}) async-start(bf16[32,40,128]{2,1,0:T(8,128)(2,1)} %get-tuple-element.52), calls=%async_computation.3 | async-start | bytes 655360 | tf_op jit(solution)/shard_map/all_to_all | solution.py:565
  155.9 8.0 %copy-start.2 = (bf16[1024,256]{1,0:T(8,128)(2,1)S(1)}, bf16[1024,256]{1,0:T(8,128)(2,1)}, u32[]{:S(2)}) copy-start(bf16[1024,256]{1,0:T(8,128)(2,1)} %constant.23.clone.refs_1_) | copy-start | bytes 1572868

commit v10 on v9

--- a/solution.py
+++ b/solution.py
@@ -204,7 +204,9 @@
                     )
 
 
-def analyse_kernel(field, analysis, cells_out, coef_out, first_out, last_out):
+def analyse_kernel(
+    field, analysis, weights, cells_out, coef_out, first_out, last_out, packed_out
+):
     cells = to_cells(field[...])
     rounded = cells.astype(BF16)
     coef_out[...] = dot(analysis[...], rounded).astype(BF16)
@@ -212,6 +214,12 @@
     first, last = edge_layers(cells)
     first_out[...] = first
     last_out[...] = last
+    weights.load()
+    rows = GROUP * LANES // 4
+    for g in range(packed_out.shape[0] // rows):
+        pair = [weights[k * rows : (k + 1) * rows, :] for k in (2 * g, 2 * g + 1)]
+        packed_out.buffer[g * rows : (g + 1) * rows, :] = jnp.concatenate(pair, axis=1)
+    packed_out.copy.start()
 
 
 def local_kernel(
@@ -230,12 +238,8 @@
     cotangent_out[...] = to_cells(cotangent[...]).astype(BF16)
 
 
-def pack_kernel(weights, out):
-    rows = GROUP * LANES // 4
-    for g in range(out.shape[0] // rows):
-        first = weights[2 * g * rows : (2 * g + 1) * rows, :]
-        second = weights[(2 * g + 1) * rows : (2 * g + 2) * rows, :]
-        out[g * rows : (g + 1) * rows, :] = jnp.concatenate([first, second], axis=1)
+def fetch_kernel():
+    pass
 
 
 def mode_in_group(rows, lanes):
@@ -494,6 +498,7 @@
         chosen = {k: chosen[k] if isinstance(chosen, dict) else None for k in places if k in chosen}
         return {k: rows or arrays[k].shape[0] for k, rows in chosen.items()}
 
+    moved = dict(moved)
     staged = rows_of(staged, given, operands)
     sent = rows_of(sent, made, outs)
 
@@ -511,14 +516,14 @@
         filled = dict(zip(given, take(len(given))))
         kept = dict(zip(made, take(len(made))))
         own = take(len(scratch))
-        copies = [
-            pltpu.make_async_copy(
-                filled.pop(k),
-                part(kept.pop(out), operands[k].shape[0]),
-                refs[-1].at[len(staged) + len(sent) + place],
+        copies = []
+        for place, (k, out) in enumerate(moved.items()):
+            source, target = filled.pop(k), kept.pop(out)
+            rows = min(source.shape[0], target.shape[0])
+            semaphore = refs[-1].at[len(staged) + len(sent) + place]
+            copies.append(
+                pltpu.make_async_copy(part(source, rows), part(target, rows), semaphore)
             )
-            for place, (k, out) in enumerate(dict(moved).items())
-        ]
         for place, (k, buffer) in enumerate(zip(staged, take(len(staged)))):
             filled[k] = Staged(part(filled[k], staged[k]), buffer, refs[-1].at[place])
         for place, (k, buffer) in enumerate(zip(sent, take(len(sent)))):
@@ -526,8 +531,8 @@
         for copy in copies:
             copy.start()
         body(
-            *[filled.get(k) for k in range(len(operands)) if k not in dict(moved)],
-            *[kept.get(k) for k in range(len(outs)) if k not in dict(moved).values()],
+            *[filled.get(k) for k in range(len(operands)) if k not in moved],
+            *[kept.get(k) for k in range(len(outs)) if k not in moved.values()],
             *own,
         )
         for k in staged:
@@ -551,7 +556,7 @@
         kernel,
         out_shape=results,
         in_specs=[in_hbm if k in staged or k in moved else in_vmem for k in given],
-        out_specs=[in_hbm if k in sent or k in dict(moved).values() else in_vmem for k in made],
+        out_specs=[in_hbm if k in sent else in_vmem for k in made],
         scratch_shapes=[*scratch, *buffers],
         compiler_params=pltpu.CompilerParams(vmem_limit_bytes=limit),
         cost_estimate=pl.CostEstimate(flops=flops, bytes_accessed=size, transcendentals=0),
@@ -597,27 +602,20 @@
     def send(values):
         return exchange(values.reshape(devices, modes, LANES)).reshape(plane_rows, LANES)
 
-    cells, coef, first, last, weights = run(
+    packed = shape((weights.shape[0] // 2, LANES), BF16)
+    cells, coef, first, last, kept_weights = run(
         analyse_kernel,
-        [wide, plane_modes, edge, edge, shape((HBM_BYTES // (2 * LANES), channels), BF16)],
+        [wide, plane_modes, edge, edge, shape((HBM_BYTES // (2 * LANES), LANES), BF16)],
         snapshots.reshape(field.shape),
         analysis,
         weights,
-        staged=(0, 1),
-        sent=(0, 1, 2, 3),
-        moved={2: 4},
+        staged=(0, 1, 2),
+        sent={0: None, 1: None, 2: None, 3: None, 4: packed.shape[0]},
         limit=WHOLE_VMEM,
         flops=10**8,
     )
-    rows = count * channels // batches
-
-    def pack(weights, first):
-        weights, first = lax.optimization_barrier((weights, first))
-        packed = shape((rows // 2, LANES), BF16)
-        return run(pack_kernel, [packed], weights, staged={0: rows})[0], first
-
-    packed_weights, coef = pack(weights, coef)
     coef = send(coef)
+    (packed_weights,) = run(fetch_kernel, [packed], kept_weights, moved={0: 0})
     before, after = neighbours(first, last)
     local, lanes, outer_cells = run(
         local_kernel,
@@ -664,17 +662,18 @@
         scratch=[pltpu.VMEM((CELLS + 2 * NY, 3 * LANES), BF16)],
         flops=10**9,
     )
-    packed_weights, back = pack(weights, back)
     if in_slab:
         back = exchange(back)
     else:
         back = send(back)
         terms = exchange(terms.reshape(devices, TERM_ROWS // devices, LANES))
     before, after = neighbours(first, last)
-    (activated,) = run(
+    activated, packed_weights = run(
         output_kernel,
-        [field],
+        [field, packed],
         activated,
+        kept_weights,
+        moved={1: 1},
         flops=10**8,
     )
     back, before, after, activated, packed_weights = lax.optimization_barrier(

time: 166 us -> 72.3 us (0.44)
  Pallas kernels: 119 us -> 24.6 us
  waiting for transfers between devices: 13.9 us -> 16.1 us
    pallas_call x11 -> x10, Pallas kernels: 119 us -> 24.6 us  [run(): pl.pallas_call(kernel, out_shape=results, in_specs=[in_hbm if k in staged...]
  transfers between devices with their start and end apart: 8 -> 8, of which waited for: 4 -> 5; matrix products, arithmetic and copies ran while one was open for 0% -> 0% of each run, Pallas kernels for 9% -> 19%
where the time goes in v10:
time: 72.3 us; the launch traced here: 71.7 us
  starting transfers between devices  27.5 us (38%)
  Pallas kernels  24.6 us (34%)
  waiting for transfers between devices  16.1 us (22%)
  local copies, waits for them, and re-layouts  2.57 us (4%)
  between operations  0.86 us (1%)
    pallas_call x10, Pallas kernels, run(): pl.pallas_call(kernel, out_shape=results, in_specs=[in_hbm if k in staged...  24.6 us
    all_to_all x4, starting transfers between devices, exchange(): lax.all_to_all(values, ('batch', 'space'), split_axis=0, concat_axis=0, t...  20 us
    all_to_all x4, waiting for transfers between devices, exchange(): lax.all_to_all(values, ('batch', 'space'), split_axis=0, concat_axis=0, t...  15.1 us
    ppermute x2, starting transfers between devices, neighbours(): before = lax.ppermute(last, 'space', [(i, i + 1) for i in range(ends)])  4.97 us
    ppermute x2, starting transfers between devices, neighbours(): after = lax.ppermute(first, 'space', [(i + 1, i) for i in range(ends)])  2.57 us
    unnamed x22, local copies, waits for them, and re-layouts  2.57 us
  transfers between devices with their start and end apart: 8, of which 5 were waited for; matrix products, arithmetic and copies ran while one was open for 0% of the time, Pallas kernels for 19%

profile of v10, /device:TPU:0, one launch (start us, length us, event | category | flops | bytes accessed | tf_op | source)
XLA Modules:
  0.0 71.7 jit_solution(2371607929080532789)
XLA Ops:
  0.6 3.9 %analyse_kernel.1 = (bf16[1024,128]{1,0:T(8,128)(2,1)}, bf16[256,128]{1,0:T(8,128)(2,1)}, bf16[512,128]{1,0:T(8,128)(2,1)}, bf16[512,128]{1,0:T(8,128)(2,1)}, bf16[102400,128]{1,0:T(8,128)(2,1)}) custom-call(bf16[64,2,1024]{2,1,0:T(2,128)(2,1)} %bitcast.22, bf16[256,1024]{1,0:T(8,128)(2,1)} %constant.16.clone.refs_1_, bf16[12288,64]{1,0:T(8,128)(2,1)} %bitcast.21), custom_call_target="tpu_custom_call" | custom-call | flops 100000000 | bytes 29163520 | tf_op jit(solution)/shard_map/analyse_kernel/pallas_call | solution.py:555
  4.5 7.3 %all-to-all-start = ((bf16[32,8,128]{2,1,0:T(8,128)(2,1)}), bf16[32,8,128]{2,1,0:T(8,128)(2,1)S(1)}, u32[]{:S(2)}, u32[]{:S(2)}) async-start(bf16[32,8,128]{2,1,0:T(8,128)(2,1)} %bitcast.23), calls=%async_computation | async-start | bytes 131072 | tf_op jit(solution)/shard_map/all_to_all | solution.py:570
  11.8 2.8 %collective-permute-start = (bf16[512,128]{1,0:T(8,128)(2,1)}, bf16[512,128]{1,0:T(8,128)(2,1)}, u32[]{:S(2)}, u32[]{:S(2)}) collective-permute-start(bf16[512,128]{1,0:T(8,128)(2,1)} %get-tuple-element.34), channel_id=1, source_target_pairs={{0,1},{1,2},{2,3},{3,4},{4,5},{5,6},{6,7},{7,8},{8,9},{9,10},{10,1... | collective-permute-start | bytes 393224 | tf_op jit(solution)/shard_map/ppermute | solution.py:575
  14.6 1.3 %collective-permute-start.1 = (bf16[512,128]{1,0:T(8,128)(2,1)}, bf16[512,128]{1,0:T(8,128)(2,1)}, u32[]{:S(2)}, u32[]{:S(2)}) collective-permute-start(bf16[512,128]{1,0:T(8,128)(2,1)} %get-tuple-element.35), channel_id=1, source_target_pairs={{1,0},{2,1},{3,2},{4,3},{5,4},{6,5},{7,6},{8,7},{9,8},{10,9},{11,1... | collective-permute-start | bytes 393224 | tf_op jit(solution)/shard_map/ppermute | solution.py:576
  15.9 0.0 copy-start.6
  15.9 0.0 copy-start.7
  16.0 0.0 copy-start.3
  16.0 0.0 copy-start
  16.0 0.0 copy-start.1
  16.0 1.5 %fetch_kernel.1.refs_2_ = bf16[6144,128]{1,0:T(8,128)(2,1)S(1)} custom-call(bf16[102400,128]{1,0:T(8,128)(2,1)} %get-tuple-element.31.refs_0_.refs_1_), custom_call_target="tpu_custom_call" | custom-call | bytes 27787264 | tf_op jit(solution)/shard_map/fetch_kernel/pallas_call | solution.py:555
  17.5 1.7 %all-to-all-done = bf16[32,8,128]{2,1,0:T(8,128)(2,1)S(1)} async-done(((bf16[32,8,128]{2,1,0:T(8,128)(2,1)}), bf16[32,8,128]{2,1,0:T(8,128)(2,1)S(1)}, u32[]{:S(2)}, u32[]{:S(2)}) %all-to-all-start) | async-done | bytes 65568 | tf_op jit(solution)/shard_map/all_to_all | solution.py:570
  19.2 0.0 copy-done.6
  19.2 0.0 copy-done.7
  19.2 1.2 %mix_kernel.1 = (bf16[256,128]{1,0:T(8,128)(2,1)S(1)}, bf16[384,256]{1,0:T(8,128)(2,1)S(1)}) custom-call(bf16[256,128]{1,0:T(8,128)(2,1)S(1)} %bitcast.17, bf16[192,256]{1,0:T(8,128)(2,1)S(1)} %copy-done.7, bf16[6144,128]{1,0:T(8,128)(2,1)S(1)} %fetch_kernel.1.refs_2_, bf16[128,384]{1,0:T(8,128)(2,1)S(1)} %copy-done.6), custom_call_target="tpu_custom_call" | custom-call | flops 400000000 | bytes 2097152 | tf_op jit(solution)/shard_map/mix_kernel/pallas_call | solution.py:555
  20.5 0.0 copy-start.8
  20.5 0.6 copy-done.8
  21.1 5.6 %all-to-all-start.1 = ((bf16[32,8,128]{2,1,0:T(8,128)(2,1)}), bf16[32,8,128]{2,1,0:T(8,128)(2,1)S(1)}, u32[]{:S(2)}, u32[]{:S(2)}) async-start(bf16[32,8,128]{2,1,0:T(8,128)(2,1)} %bitcast.18), calls=%async_computation.1 | async-start | bytes 131072 | tf_op jit(solution)/shard_map/all_to_all | solution.py:570
  26.8 0.0 collective-permute-done.refs_1_
  26.8 0.0 collective-permute-done.1.refs_2_
  26.8 0.0 copy-done.3
  26.8 0.0 copy-start.9
  26.8 0.9 %copy-done.9 = bf16[1,64,2,1024]{3,2,1,0:T(2,128)(2,1)S(1)} copy-done((bf16[1,64,2,1024]{3,2,1,0:T(2,128)(2,1)S(1)}, bf16[1,64,2,1024]{3,2,1,0:T(2,128)(2,1)}, u32[]{:S(2)}) %copy-start.9) | copy-done | bytes 262168
  27.8 0.0 copy-start.10
  27.8 0.9 %copy-done.10 = bf16[1024,128]{1,0:T(8,128)(2,1)S(1)} copy-done((bf16[1024,128]{1,0:T(8,128)(2,1)S(1)}, bf16[1024,128]{1,0:T(8,128)(2,1)}, u32[]{:S(2)}) %copy-start.10) | copy-done | bytes 262168
  28.7 2.9 %local_kernel.1 = (f32[1024,128]{1,0:T(8,128)S(1)}, bf16[12800,1024]{1,0:T(8,128)(2,1)}, bf16[1024,128]{1,0:T(8,128)(2,1)S(1)}) custom-call(bf16[1024,128]{1,0:T(8,128)(2,1)S(1)} %copy-done.10, bf16[512,128]{1,0:T(8,128)(2,1)} %collective-permute-done.refs_1_, bf16[512,128]{1,0:T(8,128)(2,1)} %collective-permute-done.1.refs_2_, ...), custom_call_target="tpu_custom_call" | custom-call | flops 700000000 | bytes 28008448 | tf_op jit(solution)/shard_map/local_kernel/pallas_call | solution.py:555
  31.6 2.6 %all-to-all-done.1 = bf16[32,8,128]{2,1,0:T(8,128)(2,1)S(1)} async-done(((bf16[32,8,128]{2,1,0:T(8,128)(2,1)}), bf16[32,8,128]{2,1,0:T(8,128)(2,1)S(1)}, u32[]{:S(2)}, u32[]{:S(2)}) %all-to-all-start.1) | async-done | bytes 65568 | tf_op jit(solution)/shard_map/all_to_all | solution.py:570
  34.2 0.0 copy-done
  34.2 0.0 copy-done.1
  34.2 3.8 %activate_kernel.1 = (bf16[1024,128]{1,0:T(8,128)(2,1)S(1)}, bf16[102400,128]{1,0:T(8,128)(2,1)}, bf16[512,128]{1,0:T(8,128)(2,1)}, bf16[512,128]{1,0:T(8,128)(2,1)}, bf16[32,40,128]{2,1,0:T(8,128)(2,1)}) custom-call(bf16[256,128]{1,0:T(8,128)(2,1)S(1)} %bitcast.16, bf16[1024,256]{1,0:T(8,128)(2,1)S(1)} %copy-done.1, bf16[256,1024]{1,0:T(8,128)(2,1)S(1)} %copy-done, ...), custom_call_target="tpu_custom_call" | custom-call | flops 1000000000 | bytes 55181312 | tf_op jit(solution)/shard_map/activate_kernel/pallas_call | solution.py:555
  38.0 3.3 %all-to-all-start.2 = ((bf16[32,40,128]{2,1,0:T(8,128)(2,1)}), bf16[32,40,128]{2,1,0:T(8,128)(2,1)S(1)}, u32[]{:S(2)}, u32[]{:S(2)}) async-start(bf16[32,40,128]{2,1,0:T(8,128)(2,1)} %get-tuple-element.39), calls=%async_computation.2 | async-start | bytes 655360 | tf_op jit(solution)/shard_map/all_to_all | solution.py:570
  41.3 2.2 %collective-permute-start.2 = (bf16[512,128]{1,0:T(8,128)(2,1)}, bf16[512,128]{1,0:T(8,128)(2,1)S(1)}, u32[]{:S(2)}, u32[]{:S(2)}) collective-permute-start(bf16[512,128]{1,0:T(8,128)(2,1)} %get-tuple-element.40), channel_id=1, source_target_pairs={{0,1},{1,2},{2,3},{3,4},{4,5},{5,6},{6,7},{7,8},{8,9},{9,10},{10,1... | collective-permute-start | bytes 393224 | tf_op jit(solution)/shard_map/ppermute | solution.py:575
  43.4 1.3 %collective-permute-start.3 = (bf16[512,128]{1,0:T(8,128)(2,1)}, bf16[512,128]{1,0:T(8,128)(2,1)S(1)}, u32[]{:S(2)}, u32[]{:S(2)}) collective-permute-start(bf16[512,128]{1,0:T(8,128)(2,1)} %get-tuple-element.41), channel_id=1, source_target_pairs={{1,0},{2,1},{3,2},{4,3},{5,4},{6,5},{7,6},{8,7},{9,8},{10,9},{11,1... | collective-permute-start | bytes 393224 | tf_op jit(solution)/shard_map/ppermute | solution.py:576
  44.7 0.0 copy-start.4
  44.7 0.0 copy-start.5
  44.8 2.2 %output_kernel.1 = (bf16[64,2,1024]{2,1,0:T(2,128)(2,1)}, bf16[6144,128]{1,0:T(8,128)(2,1)S(1)}) custom-call(bf16[1024,128]{1,0:T(8,128)(2,1)S(1)} %get-tuple-element.42.refs_0_, bf16[102400,128]{1,0:T(8,128)(2,1)} %get-tuple-element.31.refs_0_.refs_1_), custom_call_target="tpu_custom_call" | custom-call | flops 100000000 | bytes 28311552 | tf_op jit(solution)/shard_map/output_kernel/pallas_call | solution.py:555
  47.0 0.0 collective-permute-done.2.refs_1_
  47.0 1.1 %collective-permute-done.3.refs_2_ = bf16[512,128]{1,0:T(8,128)(2,1)S(1)} collective-permute-done((bf16[512,128]{1,0:T(8,128)(2,1)}, bf16[512,128]{1,0:T(8,128)(2,1)S(1)}, u32[]{:S(2)}, u32[]{:S(2)}) %collective-permute-start.3) | collective-permute-done | bytes 131104 | tf_op jit(solution)/shard_map/ppermute | solution.py:576
  48.0 4.9 %all-to-all-done.2.refs_0_ = bf16[32,40,128]{2,1,0:T(8,128)(2,1)S(1)} async-done(((bf16[32,40,128]{2,1,0:T(8,128)(2,1)}), bf16[32,40,128]{2,1,0:T(8,128)(2,1)S(1)}, u32[]{:S(2)}, u32[]{:S(2)}) %all-to-all-start.2) | async-done | bytes 327712 | tf_op jit(solution)/shard_map/all_to_all | solution.py:570
  53.0 0.0 copy-done.4
  53.0 0.0 copy-done.5
  53.0 1.8 %unmix_kernel.1 = (bf16[32,40,128]{2,1,0:T(8,128)(2,1)}, bf16[384,128]{1,0:T(8,128)(2,1)S(1)}) custom-call(bf16[32,40,128]{2,1,0:T(8,128)(2,1)S(1)} %all-to-all-done.2.refs_0_, bf16[192,256]{1,0:T(8,128)(2,1)S(1)} %copy-done.5, bf16[6144,128]{1,0:T(8,128)(2,1)S(1)} %get-tuple-element.47.refs_2_, bf16[128,384]{1,0:T(8,128)(2,1)S(1)} %copy-done.4), custom_call_target="tpu_custom_call" | custom-call | flops 400000000 | bytes 2523136 | tf_op jit(solution)/shard_map/unmix_kernel/pallas_call | solution.py:555
  54.8 3.7 %all-to-all-start.3 = ((bf16[32,40,128]{2,1,0:T(8,128)(2,1)}), bf16[32,40,128]{2,1,0:T(8,128)(2,1)S(1)}, u32[]{:S(2)}, u32[]{:S(2)}) async-start(bf16[32,40,128]{2,1,0:T(8,128)(2,1)} %get-tuple-element.48), calls=%async_computation.3 | async-start | bytes 655360 | tf_op jit(solution)/shard_map/all_to_all | solution.py:570
  58.5 3.7 %weight_kernel.1 = f32[12288,64]{1,0:T(8,128)} custom-call(bf16[384,256]{1,0:T(8,128)(2,1)S(1)} %get-tuple-element.53.refs_0_, bf16[384,128]{1,0:T(8,128)(2,1)S(1)} %get-tuple-element.54.refs_1_), custom_call_target="tpu_custom_call" | custom-call | flops 400000000 | bytes 3440640 | tf_op jit(solution)/shard_map/weight_kernel/pallas_call | solution.py:555
  62.2 0.0 copy-start.2
  62.2 2.1 %local_grad_kernel.1.refs_2_ = f32[1024,128]{1,0:T(8,128)S(1)} custom-call(bf16[102400,128]{1,0:T(8,128)(2,1)} %get-tuple-element.49.refs_0_, bf16[512,128]{1,0:T(8,128)(2,1)S(1)} %collective-permute-done.2.refs_1_, bf16[512,128]{1,0:T(8,128)(2,1)S(1)} %collective-permute-done.3.refs_2_, bf16[27,64,64]{2,1,0:T(8,128)(2,1)S(1)} %bitcast.15), custom_call_target="tpu_custom_call" | custom-call | flops 700000000 | bytes 27222016 | tf_op jit(solution)/shard_map/local_grad_kernel/pallas_call | solution.py:555
  64.3 5.9 %all-to-all-done.3.refs_0_ = bf16[32,40,128]{2,1,0:T(8,128)(2,1)S(1)} async-done(((bf16[32,40,128]{2,1,0:T(8,128)(2,1)}), bf16[32,40,128]{2,1,0:T(8,128)(2,1)S(1)}, u32[]{:S(2)}, u32[]{:S(2)}) %all-to-all-start.3) | async-done | bytes 327712 | tf_op jit(solution)/shard_map/all_to_all | solution.py:570
  70.2 0.0 copy-done.2
  70.2 1.5 %finish_kernel.1 = (bf16[64,2,1024]{2,1,0:T(2,128)(2,1)}, f32[27,64,64]{2,1,0:T(8,128)}) custom-call(bf16[32,40,128]{2,1,0:T(8,128)(2,1)S(1)} %all-to-all-done.3.refs_0_, bf16[1024,256]{1,0:T(8,128)(2,1)S(1)} %copy-done.2, f32[1024,128]{1,0:T(8,128)S(1)} %local_grad_kernel.1.refs_2_), custom_call_target="tpu_custom_call" | custom-call | flops 100000000 | bytes 2080768 | tf_op jit(solution)/shard_map/finish_kernel/pallas_call | solution.py:555
Async XLA Ops:
  4.5 14.7 %all-to-all-start = ((bf16[32,8,128]{2,1,0:T(8,128)(2,1)}), bf16[32,8,128]{2,1,0:T(8,128)(2,1)S(1)}, u32[]{:S(2)}, u32[]{:S(2)}) async-start(bf16[32,8,128]{2,1,0:T(8,128)(2,1)} %bitcast.23), calls=%async_computation | async-start | bytes 131072 | tf_op jit(solution)/shard_map/all_to_all | solution.py:570
  11.8 14.9 %collective-permute-start = (bf16[512,128]{1,0:T(8,128)(2,1)}, bf16[512,128]{1,0:T(8,128)(2,1)}, u32[]{:S(2)}, u32[]{:S(2)}) collective-permute-start(bf16[512,128]{1,0:T(8,128)(2,1)} %get-tuple-element.34), channel_id=1, source_target_pairs={{0,1},{1,2},{2,3},{3,4},{4,5},{5,6},{6,7},{7,8},{8,9},{9,10},{10,1... | collective-permute-start | bytes 393224 | tf_op jit(solution)/shard_map/ppermute | solution.py:575
  14.6 12.1 %collective-permute-start.1 = (bf16[512,128]{1,0:T(8,128)(2,1)}, bf16[512,128]{1,0:T(8,128)(2,1)}, u32[]{:S(2)}, u32[]{:S(2)}) collective-permute-start(bf16[512,128]{1,0:T(8,128)(2,1)} %get-tuple-element.35), channel_id=1, source_target_pairs={{1,0},{2,1},{3,2},{4,3},{5,4},{6,5},{7,6},{8,7},{9,8},{10,9},{11,1... | collective-permute-start | bytes 393224 | tf_op jit(solution)/shard_map/ppermute | solution.py:576
  15.9 3.3 %copy-start.6 = (bf16[128,384]{1,0:T(8,128)(2,1)S(1)}, bf16[128,384]{1,0:T(8,128)(2,1)}, u32[]{:S(2)}) copy-start(bf16[128,384]{1,0:T(8,128)(2,1)} %constant.18.clone.refs_3_) | copy-start | bytes 294916
  15.9 3.3 %copy-start.7 = (bf16[192,256]{1,0:T(8,128)(2,1)S(1)}, bf16[192,256]{1,0:T(8,128)(2,1)}, u32[]{:S(2)}) copy-start(bf16[192,256]{1,0:T(8,128)(2,1)} %constant.17.clone.refs_1_) | copy-start | bytes 294916
  16.0 10.8 %copy-start.3 = (bf16[3,3,3,64,64]{4,3,2,1,0:T(8,128)(2,1)S(1)}, bf16[3,3,3,64,64]{4,3,2,1,0:T(8,128)(2,1)}, u32[]{:S(2)}) copy-start(bf16[3,3,3,64,64]{4,3,2,1,0:T(8,128)(2,1)} %param.15) | copy-start | bytes 663556
  16.0 18.2 %copy-start = (bf16[256,1024]{1,0:T(8,128)(2,1)S(1)}, bf16[256,1024]{1,0:T(8,128)(2,1)}, u32[]{:S(2)}) copy-start(bf16[256,1024]{1,0:T(8,128)(2,1)} %constant.20.clone.refs_2_) | copy-start | bytes 1572868
  16.0 18.2 %copy-start.1 = (bf16[1024,256]{1,0:T(8,128)(2,1)S(1)}, bf16[1024,256]{1,0:T(8,128)(2,1)}, u32[]{:S(2)}) copy-start(bf16[1024,256]{1,0:T(8,128)(2,1)} %constant.19.clone.refs_1_) | copy-start | bytes 1572868
  20.5 0.6 copy-start.8
  21.1 13.1 %all-to-all-start.1 = ((bf16[32,8,128]{2,1,0:T(8,128)(2,1)}), bf16[32,8,128]{2,1,0:T(8,128)(2,1)S(1)}, u32[]{:S(2)}, u32[]{:S(2)}) async-start(bf16[32,8,128]{2,1,0:T(8,128)(2,1)} %bitcast.18), calls=%async_computation.1 | async-start | bytes 131072 | tf_op jit(solution)/shard_map/all_to_all | solution.py:570
  26.8 1.0 %copy-start.9 = (bf16[1,64,2,1024]{3,2,1,0:T(2,128)(2,1)S(1)}, bf16[1,64,2,1024]{3,2,1,0:T(2,128)(2,1)}, u32[]{:S(2)}) copy-start(bf16[1,64,2,1024]{3,2,1,0:T(2,128)(2,1)} %param.13) | copy-start | bytes 786436
  27.8 0.9 %copy-start.10 = (bf16[1024,128]{1,0:T(8,128)(2,1)S(1)}, bf16[1024,128]{1,0:T(8,128)(2,1)}, u32[]{:S(2)}) copy-start(bf16[1024,128]{1,0:T(8,128)(2,1)} %get-tuple-element.33.refs_0_) | copy-start | bytes 786436
  38.0 15.0 %all-to-all-start.2 = ((bf16[32,40,128]{2,1,0:T(8,128)(2,1)}), bf16[32,40,128]{2,1,0:T(8,128)(2,1)S(1)}, u32[]{:S(2)}, u32[]{:S(2)}) async-start(bf16[32,40,128]{2,1,0:T(8,128)(2,1)} %get-tuple-element.39), calls=%async_computation.2 | async-start | bytes 655360 | tf_op jit(solution)/shard_map/all_to_all | solution.py:570
  41.3 5.7 %collective-permute-start.2 = (bf16[512,128]{1,0:T(8,128)(2,1)}, bf16[512,128]{1,0:T(8,128)(2,1)S(1)}, u32[]{:S(2)}, u32[]{:S(2)}) collective-permute-start(bf16[512,128]{1,0:T(8,128)(2,1)} %get-tuple-element.40), channel_id=1, source_target_pairs={{0,1},{1,2},{2,3},{3,4},{4,5},{5,6},{6,7},{7,8},{8,9},{9,10},{10,1... | collective-permute-start | bytes 393224 | tf_op jit(solution)/shard_map/ppermute | solution.py:575
  43.4 4.6 %collective-permute-start.3 = (bf16[512,128]{1,0:T(8,128)(2,1)}, bf16[512,128]{1,0:T(8,128)(2,1)S(1)}, u32[]{:S(2)}, u32[]{:S(2)}) collective-permute-start(bf16[512,128]{1,0:T(8,128)(2,1)} %get-tuple-element.41), channel_id=1, source_target_pairs={{1,0},{2,1},{3,2},{4,3},{5,4},{6,5},{7,6},{8,7},{9,8},{10,9},{11,1... | collective-permute-start | bytes 393224 | tf_op jit(solution)/shard_map/ppermute | solution.py:576
  44.7 8.2 %copy-start.4 = (bf16[128,384]{1,0:T(8,128)(2,1)S(1)}, bf16[128,384]{1,0:T(8,128)(2,1)}, u32[]{:S(2)}) copy-start(bf16[128,384]{1,0:T(8,128)(2,1)} %constant.22.clone.refs_3_) | copy-start | bytes 294916
  44.7 8.2 %copy-start.5 = (bf16[192,256]{1,0:T(8,128)(2,1)S(1)}, bf16[192,256]{1,0:T(8,128)(2,1)}, u32[]{:S(2)}) copy-start(bf16[192,256]{1,0:T(8,128)(2,1)} %constant.21.clone.refs_1_) | copy-start | bytes 294916
  54.8 15.4 %all-to-all-start.3 = ((bf16[32,40,128]{2,1,0:T(8,128)(2,1)}), bf16[32,40,128]{2,1,0:T(8,128)(2,1)S(1)}, u32[]{:S(2)}, u32[]{:S(2)}) async-start(bf16[32,40,128]{2,1,0:T(8,128)(2,1)} %get-tuple-element.48), calls=%async_computation.3 | async-start | bytes 655360 | tf_op jit(solution)/shard_map/all_to_all | solution.py:570
  62.2 7.9 %copy-start.2 = (bf16[1024,256]{1,0:T(8,128)(2,1)S(1)}, bf16[1024,256]{1,0:T(8,128)(2,1)}, u32[]{:S(2)}) copy-start(bf16[1024,256]{1,0:T(8,128)(2,1)} %constant.23.clone.refs_1_) | copy-start | bytes 1572868

commit v11 on v10

--- a/solution.py
+++ b/solution.py
@@ -20,6 +20,7 @@
 GROUP = 8
 OFFSETS = 27
 TERM_ROWS = 1024
+CHUNKS = 3
 VMEM_BYTES = 40 * 1024 * 1024
 WHOLE_VMEM = 65000 * 1024
 HBM_BYTES = 100 * 1024 * 256
@@ -204,9 +205,9 @@
                     )
 
 
-def analyse_kernel(
-    field, analysis, weights, cells_out, coef_out, first_out, last_out, packed_out
-):
+def analyse_kernel(field, analysis, *refs):
+    weights = refs[:CHUNKS]
+    cells_out, coef_out, first_out, last_out, packed_out, buffer, semaphores = refs[CHUNKS:]
     cells = to_cells(field[...])
     rounded = cells.astype(BF16)
     coef_out[...] = dot(analysis[...], rounded).astype(BF16)
@@ -214,12 +215,21 @@
     first, last = edge_layers(cells)
     first_out[...] = first
     last_out[...] = last
-    weights.load()
     rows = GROUP * LANES // 4
-    for g in range(packed_out.shape[0] // rows):
-        pair = [weights[k * rows : (k + 1) * rows, :] for k in (2 * g, 2 * g + 1)]
-        packed_out.buffer[g * rows : (g + 1) * rows, :] = jnp.concatenate(pair, axis=1)
-    packed_out.copy.start()
+    share = buffer.shape[0] // CHUNKS
+    copies = []
+    for place, part in enumerate(weights):
+        for g in range(share // rows):
+            pair = [part[k * rows : (k + 1) * rows, :] for k in (2 * g, 2 * g + 1)]
+            row = place * share + g * rows
+            buffer[row : row + rows, :] = jnp.concatenate(pair, axis=1)
+        span = slice(place * share, (place + 1) * share)
+        copies.append(
+            pltpu.make_async_copy(buffer.at[span], packed_out.at[span], semaphores.at[place])
+        )
+        copies[-1].start()
+    for copy in copies:
+        copy.wait()
 
 
 def local_kernel(
@@ -298,7 +308,8 @@
         axis=0,
     )
     mixed = jnp.where(own_half(count), mixed, swap_halves(mixed))
-    back_out[...] = from_depth(mixed, scatter[...], snaps).astype(BF16)
+    back = from_depth(mixed, scatter[...], snaps).astype(BF16)
+    back_out[...] = back.reshape(back_out.shape)
 
 
 def activate_kernel(
@@ -441,13 +452,15 @@
         terms = terms.reshape(TERM_ROWS, LANES)
     else:
         modes, terms = received[...], sums[...].astype(F32)
-    cells = (dot(synthesis[...], modes.astype(BF16)) + local[...]).astype(BF16)
-    grad_out[...] = to_field(cells)
     half = LANES // 2
+    blocks = []
     for k in range(OFFSETS):
         row = (k // 2) * half
         lane = (k % 2) * half
-        stencil_out[k] = terms[row : row + half, lane : lane + half]
+        blocks.append(terms[row : row + half, lane : lane + half])
+    stencil_out[...] = jnp.stack(blocks, axis=0)
+    cells = (dot(synthesis[...], modes.astype(BF16)) + local[...]).astype(BF16)
+    grad_out[...] = to_field(cells)
 
 
 def shape(dims, dtype):
@@ -488,8 +501,12 @@
         return self.buffer.shape
 
 
+def row_count(rows):
+    return rows.stop - rows.start if isinstance(rows, slice) else rows
+
+
 def run(
-    body, outs, *operands, staged=(), sent=(), moved=(), scratch=(), flops=0, limit=VMEM_BYTES
+    body, outs, *operands, staged=(), sent=(), moved=(), plain=(), scratch=(), flops=0, limit=VMEM_BYTES
 ):
     given = [k for k, operand in enumerate(operands) if operand is not None]
     made = [k for k, out in enumerate(outs) if out is not None]
@@ -511,6 +528,8 @@
             return taken
 
         def part(ref, rows):
+            if isinstance(rows, slice):
+                return ref.at[rows]
             return ref if ref.shape[0] == rows else ref.at[0:rows]
 
         filled = dict(zip(given, take(len(given))))
@@ -549,14 +568,14 @@
     in_hbm = pl.BlockSpec(memory_space=pltpu.HBM)
     buffers = [(operands[k], rows) for k, rows in staged.items()]
     buffers += [(outs[k], rows) for k, rows in sent.items()]
-    buffers = [pltpu.VMEM((rows, *x.shape[1:]), x.dtype) for x, rows in buffers]
+    buffers = [pltpu.VMEM((row_count(rows), *x.shape[1:]), x.dtype) for x, rows in buffers]
     if len(buffers) + len(moved) > 0:
         buffers.append(pltpu.SemaphoreType.DMA((len(buffers) + len(moved),)))
     results = pl.pallas_call(
         kernel,
         out_shape=results,
         in_specs=[in_hbm if k in staged or k in moved else in_vmem for k in given],
-        out_specs=[in_hbm if k in sent else in_vmem for k in made],
+        out_specs=[in_hbm if k in sent or k in plain else in_vmem for k in made],
         scratch_shapes=[*scratch, *buffers],
         compiler_params=pltpu.CompilerParams(vmem_limit_bytes=limit),
         cost_estimate=pl.CostEstimate(flops=flops, bytes_accessed=size, transcendentals=0),
@@ -603,14 +622,17 @@
         return exchange(values.reshape(devices, modes, LANES)).reshape(plane_rows, LANES)
 
     packed = shape((weights.shape[0] // 2, LANES), BF16)
+    share = weights.shape[0] // CHUNKS
     cells, coef, first, last, kept_weights = run(
         analyse_kernel,
         [wide, plane_modes, edge, edge, shape((HBM_BYTES // (2 * LANES), LANES), BF16)],
         snapshots.reshape(field.shape),
         analysis,
-        weights,
-        staged=(0, 1, 2),
-        sent={0: None, 1: None, 2: None, 3: None, 4: packed.shape[0]},
+        *[weights] * CHUNKS,
+        staged={0: None, 1: None} | {2 + k: slice(k * share, (k + 1) * share) for k in range(CHUNKS)},
+        sent=(0, 1, 2, 3),
+        plain=(4,),
+        scratch=[pltpu.VMEM(packed.shape, BF16), pltpu.SemaphoreType.DMA((CHUNKS,))],
         limit=WHOLE_VMEM,
         flops=10**8,
     )
@@ -631,7 +653,10 @@
     )
     back, diagonal = run(
         functools.partial(mix_kernel, batches),
-        [plane_modes, shape((count, GROUP * half // 2), BF16)],
+        [
+            shape((devices, modes, LANES), BF16) if modes % 8 == 0 else plane_modes,
+            shape((count, GROUP * half // 2), BF16),
+        ],
         coef,
         gather,
         packed_weights,
@@ -725,6 +750,7 @@
         sums,
         np.ascontiguousarray(analysis.T),
         local,
+        sent=(1,),
         flops=10**8,
     )
     return (

time: 72.3 us -> 72.2 us (level)
  no operation moved by 1% of the time
where the time goes in v11:
time: 72.2 us; the launch traced here: 71.6 us
  starting transfers between devices  27.5 us (38%)
  Pallas kernels  24.6 us (34%)
  waiting for transfers between devices  16.1 us (22%)
  local copies, waits for them, and re-layouts  2.57 us (4%)
  between operations  0.86 us (1%)
    pallas_call x10, Pallas kernels, run(): pl.pallas_call(kernel, out_shape=results, in_specs=[in_hbm if k in staged...  24.6 us
    all_to_all x4, starting transfers between devices, exchange(): lax.all_to_all(values, ('batch', 'space'), split_axis=0, concat_axis=0, t...  20 us
    all_to_all x4, waiting for transfers between devices, exchange(): lax.all_to_all(values, ('batch', 'space'), split_axis=0, concat_axis=0, t...  15.1 us
    ppermute x2, starting transfers between devices, neighbours(): before = lax.ppermute(last, 'space', [(i, i + 1) for i in range(ends)])  4.97 us
    ppermute x2, starting transfers between devices, neighbours(): after = lax.ppermute(first, 'space', [(i + 1, i) for i in range(ends)])  2.57 us
    unnamed x22, local copies, waits for them, and re-layouts  2.57 us
  transfers between devices with their start and end apart: 8, of which 5 were waited for; matrix products, arithmetic and copies ran while one was open for 0% of the time, Pallas kernels for 19%

profile of v11, /device:TPU:0, one launch (start us, length us, event | category | flops | bytes accessed | tf_op | source)
XLA Modules:
  0.0 71.6 jit_solution(4271813361501025865)
XLA Ops:
  0.6 3.2 %analyse_kernel.1 = (bf16[1024,128]{1,0:T(8,128)(2,1)}, bf16[256,128]{1,0:T(8,128)(2,1)}, bf16[512,128]{1,0:T(8,128)(2,1)}, bf16[512,128]{1,0:T(8,128)(2,1)}, bf16[102400,128]{1,0:T(8,128)(2,1)}) custom-call(bf16[64,2,1024]{2,1,0:T(2,128)(2,1)} %bitcast.22, bf16[256,1024]{1,0:T(8,128)(2,1)} %constant.16.clone.refs_1_, bf16[12288,64]{1,0:T(8,128)(2,1)} %bitcast.18, ...), custom_call_target="tpu_custom_call" | custom-call | flops 100000000 | bytes 32309248 | tf_op jit(solution)/shard_map/analyse_kernel/pallas_call | solution.py:574
  3.9 7.3 %all-to-all-start = ((bf16[32,8,128]{2,1,0:T(8,128)(2,1)}), bf16[32,8,128]{2,1,0:T(8,128)(2,1)S(1)}, u32[]{:S(2)}, u32[]{:S(2)}) async-start(bf16[32,8,128]{2,1,0:T(8,128)(2,1)} %bitcast.23), calls=%async_computation | async-start | bytes 131072 | tf_op jit(solution)/shard_map/all_to_all | solution.py:589
  11.2 2.8 %collective-permute-start = (bf16[512,128]{1,0:T(8,128)(2,1)}, bf16[512,128]{1,0:T(8,128)(2,1)}, u32[]{:S(2)}, u32[]{:S(2)}) collective-permute-start(bf16[512,128]{1,0:T(8,128)(2,1)} %get-tuple-element.34), channel_id=1, source_target_pairs={{0,1},{1,2},{2,3},{3,4},{4,5},{5,6},{6,7},{7,8},{8,9},{9,10},{10,1... | collective-permute-start | bytes 393224 | tf_op jit(solution)/shard_map/ppermute | solution.py:594
  14.0 1.3 %collective-permute-start.1 = (bf16[512,128]{1,0:T(8,128)(2,1)}, bf16[512,128]{1,0:T(8,128)(2,1)}, u32[]{:S(2)}, u32[]{:S(2)}) collective-permute-start(bf16[512,128]{1,0:T(8,128)(2,1)} %get-tuple-element.35), channel_id=1, source_target_pairs={{1,0},{2,1},{3,2},{4,3},{5,4},{6,5},{7,6},{8,7},{9,8},{10,9},{11,1... | collective-permute-start | bytes 393224 | tf_op jit(solution)/shard_map/ppermute | solution.py:595
  15.3 0.0 copy-start.6
  15.3 0.0 copy-start.7
  15.3 0.0 copy-start.3
  15.3 0.0 copy-start
  15.3 0.0 copy-start.1
  15.3 1.5 %fetch_kernel.1.refs_2_ = bf16[6144,128]{1,0:T(8,128)(2,1)S(1)} custom-call(bf16[102400,128]{1,0:T(8,128)(2,1)} %get-tuple-element.31.refs_0_.refs_1_), custom_call_target="tpu_custom_call" | custom-call | bytes 27787264 | tf_op jit(solution)/shard_map/fetch_kernel/pallas_call | solution.py:574
  16.9 1.7 %all-to-all-done = bf16[32,8,128]{2,1,0:T(8,128)(2,1)S(1)} async-done(((bf16[32,8,128]{2,1,0:T(8,128)(2,1)}), bf16[32,8,128]{2,1,0:T(8,128)(2,1)S(1)}, u32[]{:S(2)}, u32[]{:S(2)}) %all-to-all-start) | async-done | bytes 65568 | tf_op jit(solution)/shard_map/all_to_all | solution.py:589
  18.6 0.0 copy-done.6
  18.6 0.0 copy-done.7
  18.6 1.2 %mix_kernel.1 = (bf16[32,8,128]{2,1,0:T(8,128)(2,1)S(1)}, bf16[384,256]{1,0:T(8,128)(2,1)S(1)}) custom-call(bf16[256,128]{1,0:T(8,128)(2,1)S(1)} %bitcast.16, bf16[192,256]{1,0:T(8,128)(2,1)S(1)} %copy-done.7, bf16[6144,128]{1,0:T(8,128)(2,1)S(1)} %fetch_kernel.1.refs_2_, bf16[128,384]{1,0:T(8,128)(2,1)S(1)} %copy-done.6), custom_call_target="tpu_custom_call" | custom-call | flops 400000000 | bytes 2097152 | tf_op jit(solution)/shard_map/mix_kernel/pallas_call | solution.py:574
  19.8 0.0 copy-start.8
  19.9 0.6 copy-done.8
  20.5 5.6 %all-to-all-start.1 = ((bf16[32,8,128]{2,1,0:T(8,128)(2,1)}), bf16[32,8,128]{2,1,0:T(8,128)(2,1)S(1)}, u32[]{:S(2)}, u32[]{:S(2)}) async-start(bf16[32,8,128]{2,1,0:T(8,128)(2,1)} %copy-done.8), calls=%async_computation.1 | async-start | bytes 131072 | tf_op jit(solution)/shard_map/all_to_all | solution.py:589
  26.1 0.0 collective-permute-done.refs_1_
  26.1 0.0 collective-permute-done.1.refs_2_
  26.1 0.0 copy-done.3
  26.1 0.0 copy-start.9
  26.2 0.9 %copy-done.9 = bf16[1,64,2,1024]{3,2,1,0:T(2,128)(2,1)S(1)} copy-done((bf16[1,64,2,1024]{3,2,1,0:T(2,128)(2,1)S(1)}, bf16[1,64,2,1024]{3,2,1,0:T(2,128)(2,1)}, u32[]{:S(2)}) %copy-start.9) | copy-done | bytes 262168
  27.1 0.0 copy-start.10
  27.1 0.9 %copy-done.10 = bf16[1024,128]{1,0:T(8,128)(2,1)S(1)} copy-done((bf16[1024,128]{1,0:T(8,128)(2,1)S(1)}, bf16[1024,128]{1,0:T(8,128)(2,1)}, u32[]{:S(2)}) %copy-start.10) | copy-done | bytes 262168
  28.1 2.9 %local_kernel.1 = (f32[1024,128]{1,0:T(8,128)S(1)}, bf16[12800,1024]{1,0:T(8,128)(2,1)}, bf16[1024,128]{1,0:T(8,128)(2,1)S(1)}) custom-call(bf16[1024,128]{1,0:T(8,128)(2,1)S(1)} %copy-done.10, bf16[512,128]{1,0:T(8,128)(2,1)} %collective-permute-done.refs_1_, bf16[512,128]{1,0:T(8,128)(2,1)} %collective-permute-done.1.refs_2_, ...), custom_call_target="tpu_custom_call" | custom-call | flops 700000000 | bytes 28008448 | tf_op jit(solution)/shard_map/local_kernel/pallas_call | solution.py:574
  31.0 2.6 %all-to-all-done.1 = bf16[32,8,128]{2,1,0:T(8,128)(2,1)S(1)} async-done(((bf16[32,8,128]{2,1,0:T(8,128)(2,1)}), bf16[32,8,128]{2,1,0:T(8,128)(2,1)S(1)}, u32[]{:S(2)}, u32[]{:S(2)}) %all-to-all-start.1) | async-done | bytes 65568 | tf_op jit(solution)/shard_map/all_to_all | solution.py:589
  33.5 0.0 copy-done
  33.5 0.0 copy-done.1
  33.5 3.8 %activate_kernel.1 = (bf16[1024,128]{1,0:T(8,128)(2,1)S(1)}, bf16[102400,128]{1,0:T(8,128)(2,1)}, bf16[512,128]{1,0:T(8,128)(2,1)}, bf16[512,128]{1,0:T(8,128)(2,1)}, bf16[32,40,128]{2,1,0:T(8,128)(2,1)}) custom-call(bf16[256,128]{1,0:T(8,128)(2,1)S(1)} %bitcast.15, bf16[1024,256]{1,0:T(8,128)(2,1)S(1)} %copy-done.1, bf16[256,1024]{1,0:T(8,128)(2,1)S(1)} %copy-done, ...), custom_call_target="tpu_custom_call" | custom-call | flops 1000000000 | bytes 55181312 | tf_op jit(solution)/shard_map/activate_kernel/pallas_call | solution.py:574
  37.3 3.3 %all-to-all-start.2 = ((bf16[32,40,128]{2,1,0:T(8,128)(2,1)}), bf16[32,40,128]{2,1,0:T(8,128)(2,1)S(1)}, u32[]{:S(2)}, u32[]{:S(2)}) async-start(bf16[32,40,128]{2,1,0:T(8,128)(2,1)} %get-tuple-element.39), calls=%async_computation.2 | async-start | bytes 655360 | tf_op jit(solution)/shard_map/all_to_all | solution.py:589
  40.6 2.2 %collective-permute-start.2 = (bf16[512,128]{1,0:T(8,128)(2,1)}, bf16[512,128]{1,0:T(8,128)(2,1)S(1)}, u32[]{:S(2)}, u32[]{:S(2)}) collective-permute-start(bf16[512,128]{1,0:T(8,128)(2,1)} %get-tuple-element.40), channel_id=1, source_target_pairs={{0,1},{1,2},{2,3},{3,4},{4,5},{5,6},{6,7},{7,8},{8,9},{9,10},{10,1... | collective-permute-start | bytes 393224 | tf_op jit(solution)/shard_map/ppermute | solution.py:594
  42.8 1.3 %collective-permute-start.3 = (bf16[512,128]{1,0:T(8,128)(2,1)}, bf16[512,128]{1,0:T(8,128)(2,1)S(1)}, u32[]{:S(2)}, u32[]{:S(2)}) collective-permute-start(bf16[512,128]{1,0:T(8,128)(2,1)} %get-tuple-element.41), channel_id=1, source_target_pairs={{1,0},{2,1},{3,2},{4,3},{5,4},{6,5},{7,6},{8,7},{9,8},{10,9},{11,1... | collective-permute-start | bytes 393224 | tf_op jit(solution)/shard_map/ppermute | solution.py:595
  44.1 0.0 copy-start.4
  44.1 0.0 copy-start.5
  44.1 2.2 %output_kernel.1 = (bf16[64,2,1024]{2,1,0:T(2,128)(2,1)}, bf16[6144,128]{1,0:T(8,128)(2,1)S(1)}) custom-call(bf16[1024,128]{1,0:T(8,128)(2,1)S(1)} %get-tuple-element.42.refs_0_, bf16[102400,128]{1,0:T(8,128)(2,1)} %get-tuple-element.31.refs_0_.refs_1_), custom_call_target="tpu_custom_call" | custom-call | flops 100000000 | bytes 28311552 | tf_op jit(solution)/shard_map/output_kernel/pallas_call | solution.py:574
  46.3 0.0 collective-permute-done.2.refs_1_
  46.3 1.1 %collective-permute-done.3.refs_2_ = bf16[512,128]{1,0:T(8,128)(2,1)S(1)} collective-permute-done((bf16[512,128]{1,0:T(8,128)(2,1)}, bf16[512,128]{1,0:T(8,128)(2,1)S(1)}, u32[]{:S(2)}, u32[]{:S(2)}) %collective-permute-start.3) | collective-permute-done | bytes 131104 | tf_op jit(solution)/shard_map/ppermute | solution.py:595
  47.4 4.9 %all-to-all-done.2.refs_0_ = bf16[32,40,128]{2,1,0:T(8,128)(2,1)S(1)} async-done(((bf16[32,40,128]{2,1,0:T(8,128)(2,1)}), bf16[32,40,128]{2,1,0:T(8,128)(2,1)S(1)}, u32[]{:S(2)}, u32[]{:S(2)}) %all-to-all-start.2) | async-done | bytes 327712 | tf_op jit(solution)/shard_map/all_to_all | solution.py:589
  52.3 0.0 copy-done.4
  52.3 0.0 copy-done.5
  52.3 1.8 %unmix_kernel.1 = (bf16[32,40,128]{2,1,0:T(8,128)(2,1)}, bf16[384,128]{1,0:T(8,128)(2,1)S(1)}) custom-call(bf16[32,40,128]{2,1,0:T(8,128)(2,1)S(1)} %all-to-all-done.2.refs_0_, bf16[192,256]{1,0:T(8,128)(2,1)S(1)} %copy-done.5, bf16[6144,128]{1,0:T(8,128)(2,1)S(1)} %get-tuple-element.47.refs_2_, bf16[128,384]{1,0:T(8,128)(2,1)S(1)} %copy-done.4), custom_call_target="tpu_custom_call" | custom-call | flops 400000000 | bytes 2523136 | tf_op jit(solution)/shard_map/unmix_kernel/pallas_call | solution.py:574
  54.1 3.7 %all-to-all-start.3 = ((bf16[32,40,128]{2,1,0:T(8,128)(2,1)}), bf16[32,40,128]{2,1,0:T(8,128)(2,1)S(1)}, u32[]{:S(2)}, u32[]{:S(2)}) async-start(bf16[32,40,128]{2,1,0:T(8,128)(2,1)} %get-tuple-element.48), calls=%async_computation.3 | async-start | bytes 655360 | tf_op jit(solution)/shard_map/all_to_all | solution.py:589
  57.8 3.7 %weight_kernel.1 = f32[12288,64]{1,0:T(8,128)} custom-call(bf16[384,256]{1,0:T(8,128)(2,1)S(1)} %get-tuple-element.53.refs_0_, bf16[384,128]{1,0:T(8,128)(2,1)S(1)} %get-tuple-element.54.refs_1_), custom_call_target="tpu_custom_call" | custom-call | flops 400000000 | bytes 3440640 | tf_op jit(solution)/shard_map/weight_kernel/pallas_call | solution.py:574
  61.6 0.0 copy-start.2
  61.6 2.1 %local_grad_kernel.1.refs_2_ = f32[1024,128]{1,0:T(8,128)S(1)} custom-call(bf16[102400,128]{1,0:T(8,128)(2,1)} %get-tuple-element.49.refs_0_, bf16[512,128]{1,0:T(8,128)(2,1)S(1)} %collective-permute-done.2.refs_1_, bf16[512,128]{1,0:T(8,128)(2,1)S(1)} %collective-permute-done.3.refs_2_, bf16[27,64,64]{2,1,0:T(8,128)(2,1)S(1)} %bitcast.14), custom_call_target="tpu_custom_call" | custom-call | flops 700000000 | bytes 27222016 | tf_op jit(solution)/shard_map/local_grad_kernel/pallas_call | solution.py:574
  63.6 5.9 %all-to-all-done.3.refs_0_ = bf16[32,40,128]{2,1,0:T(8,128)(2,1)S(1)} async-done(((bf16[32,40,128]{2,1,0:T(8,128)(2,1)}), bf16[32,40,128]{2,1,0:T(8,128)(2,1)S(1)}, u32[]{:S(2)}, u32[]{:S(2)}) %all-to-all-start.3) | async-done | bytes 327712 | tf_op jit(solution)/shard_map/all_to_all | solution.py:589
  69.5 0.0 copy-done.2
  69.5 2.1 %finish_kernel.1 = (bf16[64,2,1024]{2,1,0:T(2,128)(2,1)}, f32[27,64,64]{2,1,0:T(8,128)}) custom-call(bf16[32,40,128]{2,1,0:T(8,128)(2,1)S(1)} %all-to-all-done.3.refs_0_, bf16[1024,256]{1,0:T(8,128)(2,1)S(1)} %copy-done.2, f32[1024,128]{1,0:T(8,128)S(1)} %local_grad_kernel.1.refs_2_), custom_call_target="tpu_custom_call" | custom-call | flops 100000000 | bytes 2080768 | tf_op jit(solution)/shard_map/finish_kernel/pallas_call | solution.py:574
Async XLA Ops:
  3.9 14.7 %all-to-all-start = ((bf16[32,8,128]{2,1,0:T(8,128)(2,1)}), bf16[32,8,128]{2,1,0:T(8,128)(2,1)S(1)}, u32[]{:S(2)}, u32[]{:S(2)}) async-start(bf16[32,8,128]{2,1,0:T(8,128)(2,1)} %bitcast.23), calls=%async_computation | async-start | bytes 131072 | tf_op jit(solution)/shard_map/all_to_all | solution.py:589
  11.2 14.9 %collective-permute-start = (bf16[512,128]{1,0:T(8,128)(2,1)}, bf16[512,128]{1,0:T(8,128)(2,1)}, u32[]{:S(2)}, u32[]{:S(2)}) collective-permute-start(bf16[512,128]{1,0:T(8,128)(2,1)} %get-tuple-element.34), channel_id=1, source_target_pairs={{0,1},{1,2},{2,3},{3,4},{4,5},{5,6},{6,7},{7,8},{8,9},{9,10},{10,1... | collective-permute-start | bytes 393224 | tf_op jit(solution)/shard_map/ppermute | solution.py:594
  14.0 12.1 %collective-permute-start.1 = (bf16[512,128]{1,0:T(8,128)(2,1)}, bf16[512,128]{1,0:T(8,128)(2,1)}, u32[]{:S(2)}, u32[]{:S(2)}) collective-permute-start(bf16[512,128]{1,0:T(8,128)(2,1)} %get-tuple-element.35), channel_id=1, source_target_pairs={{1,0},{2,1},{3,2},{4,3},{5,4},{6,5},{7,6},{8,7},{9,8},{10,9},{11,1... | collective-permute-start | bytes 393224 | tf_op jit(solution)/shard_map/ppermute | solution.py:595
  15.3 3.3 %copy-start.6 = (bf16[128,384]{1,0:T(8,128)(2,1)S(1)}, bf16[128,384]{1,0:T(8,128)(2,1)}, u32[]{:S(2)}) copy-start(bf16[128,384]{1,0:T(8,128)(2,1)} %constant.18.clone.refs_3_) | copy-start | bytes 294916
  15.3 3.3 %copy-start.7 = (bf16[192,256]{1,0:T(8,128)(2,1)S(1)}, bf16[192,256]{1,0:T(8,128)(2,1)}, u32[]{:S(2)}) copy-start(bf16[192,256]{1,0:T(8,128)(2,1)} %constant.17.clone.refs_1_) | copy-start | bytes 294916
  15.3 10.8 %copy-start.3 = (bf16[3,3,3,64,64]{4,3,2,1,0:T(8,128)(2,1)S(1)}, bf16[3,3,3,64,64]{4,3,2,1,0:T(8,128)(2,1)}, u32[]{:S(2)}) copy-start(bf16[3,3,3,64,64]{4,3,2,1,0:T(8,128)(2,1)} %param.15) | copy-start | bytes 663556
  15.3 18.2 %copy-start = (bf16[256,1024]{1,0:T(8,128)(2,1)S(1)}, bf16[256,1024]{1,0:T(8,128)(2,1)}, u32[]{:S(2)}) copy-start(bf16[256,1024]{1,0:T(8,128)(2,1)} %constant.20.clone.refs_2_) | copy-start | bytes 1572868
  15.3 18.2 %copy-start.1 = (bf16[1024,256]{1,0:T(8,128)(2,1)S(1)}, bf16[1024,256]{1,0:T(8,128)(2,1)}, u32[]{:S(2)}) copy-start(bf16[1024,256]{1,0:T(8,128)(2,1)} %constant.19.clone.refs_1_) | copy-start | bytes 1572868
  19.8 0.6 copy-start.8
  20.5 13.1 %all-to-all-start.1 = ((bf16[32,8,128]{2,1,0:T(8,128)(2,1)}), bf16[32,8,128]{2,1,0:T(8,128)(2,1)S(1)}, u32[]{:S(2)}, u32[]{:S(2)}) async-start(bf16[32,8,128]{2,1,0:T(8,128)(2,1)} %copy-done.8), calls=%async_computation.1 | async-start | bytes 131072 | tf_op jit(solution)/shard_map/all_to_all | solution.py:589
  26.1 1.0 %copy-start.9 = (bf16[1,64,2,1024]{3,2,1,0:T(2,128)(2,1)S(1)}, bf16[1,64,2,1024]{3,2,1,0:T(2,128)(2,1)}, u32[]{:S(2)}) copy-start(bf16[1,64,2,1024]{3,2,1,0:T(2,128)(2,1)} %param.13) | copy-start | bytes 786436
  27.1 0.9 %copy-start.10 = (bf16[1024,128]{1,0:T(8,128)(2,1)S(1)}, bf16[1024,128]{1,0:T(8,128)(2,1)}, u32[]{:S(2)}) copy-start(bf16[1024,128]{1,0:T(8,128)(2,1)} %get-tuple-element.33.refs_0_) | copy-start | bytes 786436
  37.3 15.0 %all-to-all-start.2 = ((bf16[32,40,128]{2,1,0:T(8,128)(2,1)}), bf16[32,40,128]{2,1,0:T(8,128)(2,1)S(1)}, u32[]{:S(2)}, u32[]{:S(2)}) async-start(bf16[32,40,128]{2,1,0:T(8,128)(2,1)} %get-tuple-element.39), calls=%async_computation.2 | async-start | bytes 655360 | tf_op jit(solution)/shard_map/all_to_all | solution.py:589
  40.6 5.7 %collective-permute-start.2 = (bf16[512,128]{1,0:T(8,128)(2,1)}, bf16[512,128]{1,0:T(8,128)(2,1)S(1)}, u32[]{:S(2)}, u32[]{:S(2)}) collective-permute-start(bf16[512,128]{1,0:T(8,128)(2,1)} %get-tuple-element.40), channel_id=1, source_target_pairs={{0,1},{1,2},{2,3},{3,4},{4,5},{5,6},{6,7},{7,8},{8,9},{9,10},{10,1... | collective-permute-start | bytes 393224 | tf_op jit(solution)/shard_map/ppermute | solution.py:594
  42.8 4.6 %collective-permute-start.3 = (bf16[512,128]{1,0:T(8,128)(2,1)}, bf16[512,128]{1,0:T(8,128)(2,1)S(1)}, u32[]{:S(2)}, u32[]{:S(2)}) collective-permute-start(bf16[512,128]{1,0:T(8,128)(2,1)} %get-tuple-element.41), channel_id=1, source_target_pairs={{1,0},{2,1},{3,2},{4,3},{5,4},{6,5},{7,6},{8,7},{9,8},{10,9},{11,1... | collective-permute-start | bytes 393224 | tf_op jit(solution)/shard_map/ppermute | solution.py:595
  44.1 8.2 %copy-start.4 = (bf16[128,384]{1,0:T(8,128)(2,1)S(1)}, bf16[128,384]{1,0:T(8,128)(2,1)}, u32[]{:S(2)}) copy-start(bf16[128,384]{1,0:T(8,128)(2,1)} %constant.22.clone.refs_3_) | copy-start | bytes 294916
  44.1 8.2 %copy-start.5 = (bf16[192,256]{1,0:T(8,128)(2,1)S(1)}, bf16[192,256]{1,0:T(8,128)(2,1)}, u32[]{:S(2)}) copy-start(bf16[192,256]{1,0:T(8,128)(2,1)} %constant.21.clone.refs_1_) | copy-start | bytes 294916
  54.1 15.4 %all-to-all-start.3 = ((bf16[32,40,128]{2,1,0:T(8,128)(2,1)}), bf16[32,40,128]{2,1,0:T(8,128)(2,1)S(1)}, u32[]{:S(2)}, u32[]{:S(2)}) async-start(bf16[32,40,128]{2,1,0:T(8,128)(2,1)} %get-tuple-element.48), calls=%async_computation.3 | async-start | bytes 655360 | tf_op jit(solution)/shard_map/all_to_all | solution.py:589
  61.6 8.0 %copy-start.2 = (bf16[1024,256]{1,0:T(8,128)(2,1)S(1)}, bf16[1024,256]{1,0:T(8,128)(2,1)}, u32[]{:S(2)}) copy-start(bf16[1024,256]{1,0:T(8,128)(2,1)} %constant.23.clone.refs_1_) | copy-start | bytes 1572868

commit v12 on v11

--- a/solution.py
+++ b/solution.py
@@ -44,7 +44,7 @@
         2 * KX, 2 * KY, CELLS
     )
     outer = outer.reshape(batches, 2 * KX // batches, slabs, 2 * KY // slabs, CELLS)
-    outer = outer.transpose(0, 2, 1, 3, 4).reshape(4 * KX * KY, CELLS)
+    outer = outer.transpose(2, 0, 1, 3, 4).reshape(4 * KX * KY, CELLS)
     analysis = (outer * np.float32(2.0 / math.sqrt(CELLS))).astype(ml_dtypes.bfloat16)
     synthesis = (outer * np.float32(2.0 / math.sqrt(4 * KX * KY))).astype(ml_dtypes.bfloat16)
     return analysis, synthesis
@@ -266,9 +266,9 @@
     return (mode_in_group(rows, LANES) < GROUP // 2) == low_lanes(rows)
 
 
-def to_depth(modes, table, snaps):
-    rows = modes.shape[0] // snaps
-    both = [doubled(modes[b * rows : (b + 1) * rows]) for b in range(snaps)]
+def to_depth(modes, table, snaps, slabs):
+    modes = modes.reshape(slabs, snaps, -1, LANES)
+    both = [doubled(modes[:, b].reshape(-1, LANES)) for b in range(snaps)]
     result = dot(table, jnp.concatenate(both, axis=1).astype(BF16))
     return jnp.concatenate(
         [
@@ -280,20 +280,21 @@
     )
 
 
-def from_depth(modes, table, snaps):
+def from_depth(modes, table, snaps, slabs):
     count = modes.shape[0] // GROUP
     both = []
     for b in range(snaps):
         own = [modes[g * GROUP : (g + 1) * GROUP] for g in range(b, count, snaps)]
         both.append(halved(jnp.concatenate(own, axis=0)))
     result = dot(table, jnp.concatenate(both, axis=1).astype(BF16))
-    return jnp.concatenate(
-        [result[:, b * LANES : (b + 1) * LANES] for b in range(snaps)], axis=0
-    )
-
-
-def mix_kernel(snaps, received, gather, weights, scatter, back_out, diagonal_out):
-    coef = to_depth(received[...].astype(F32), gather[...], snaps)
+    own = [
+        result[:, b * LANES : (b + 1) * LANES].reshape(slabs, -1, LANES) for b in range(snaps)
+    ]
+    return jnp.stack(own, axis=1).reshape(-1, LANES)
+
+
+def mix_kernel(snaps, slabs, received, gather, weights, scatter, back_out, diagonal_out):
+    coef = to_depth(received[...].astype(F32), gather[...], snaps, slabs)
     count = coef.shape[0]
     wide = jnp.concatenate([coef] * (GROUP // 4), axis=1)
     diagonal = jnp.where(own_block(count), wide, 0.0).astype(BF16)
@@ -308,7 +309,7 @@
         axis=0,
     )
     mixed = jnp.where(own_half(count), mixed, swap_halves(mixed))
-    back = from_depth(mixed, scatter[...], snaps).astype(BF16)
+    back = from_depth(mixed, scatter[...], snaps, slabs).astype(BF16)
     back_out[...] = back.reshape(back_out.shape)
 
 
@@ -383,13 +384,13 @@
     return whole[:, 0:8, :].reshape(-1, LANES), whole[:, 8:, :]
 
 
-def unmix_kernel(snaps, scale, received, terms, gather, weights, scatter, grad_out, mixed_out, sums_out):
+def unmix_kernel(snaps, slabs, scale, received, terms, gather, weights, scatter, grad_out, mixed_out, sums_out):
     in_slab = terms is None
     if in_slab:
         modes, terms = slab_load(received)
     else:
         modes, terms = received[...].astype(F32), terms[...].astype(F32)
-    mixed = to_depth(modes, gather[...], snaps)
+    mixed = to_depth(modes, gather[...], snaps, slabs)
     mixed_out[...] = mixed.astype(BF16)
     count = mixed.shape[0]
     rows = GROUP * snaps
@@ -406,7 +407,7 @@
         pieces.append(sum(full[:, k : k + LANES] for k in range(0, depth, LANES)))
     coef = jnp.concatenate(pieces, axis=0)
     coef = coef + swap_halves(coef)
-    grad = from_depth(coef, scatter[...], snaps)
+    grad = from_depth(coef, scatter[...], snaps, slabs)
     if in_slab:
         owners = received.shape[0]
         share = sums.shape[0]
@@ -452,15 +453,13 @@
         terms = terms.reshape(TERM_ROWS, LANES)
     else:
         modes, terms = received[...], sums[...].astype(F32)
+    cells = (dot(synthesis[...], modes.astype(BF16)) + local[...]).astype(BF16)
+    grad_out[...] = to_field(cells)
     half = LANES // 2
-    blocks = []
     for k in range(OFFSETS):
         row = (k // 2) * half
         lane = (k % 2) * half
-        blocks.append(terms[row : row + half, lane : lane + half])
-    stencil_out[...] = jnp.stack(blocks, axis=0)
-    cells = (dot(synthesis[...], modes.astype(BF16)) + local[...]).astype(BF16)
-    grad_out[...] = to_field(cells)
+        stencil_out[k] = terms[row : row + half, lane : lane + half]
 
 
 def shape(dims, dtype):
@@ -586,7 +585,7 @@
 
 
 def exchange(values):
-    return lax.all_to_all(values, ("batch", "space"), split_axis=0, concat_axis=0, tiled=True)
+    return lax.all_to_all(values, ("space", "batch"), split_axis=0, concat_axis=0, tiled=True)
 
 
 def neighbours(first, last):
@@ -652,7 +651,7 @@
         flops=7 * 10**8,
     )
     back, diagonal = run(
-        functools.partial(mix_kernel, batches),
+        functools.partial(mix_kernel, batches, slabs),
         [
             shape((devices, modes, LANES), BF16) if modes % 8 == 0 else plane_modes,
             shape((count, GROUP * half // 2), BF16),
@@ -706,7 +705,7 @@
     )
     scale = 1.0 / math.sqrt(batches * slabs * layers * plane)
     grad_modes, mixed_grad, sums = run(
-        functools.partial(unmix_kernel, batches, scale),
+        functools.partial(unmix_kernel, batches, slabs, scale),
         [
             slab if in_slab else plane_modes,
             shape((count, LANES), BF16),
@@ -724,7 +723,7 @@
         grad_modes = exchange(grad_modes)
     else:
         grad_modes = send(grad_modes)
-        sums = lax.all_gather(sums, ("batch", "space"), axis=0, tiled=True)
+        sums = lax.all_gather(sums, ("space", "batch"), axis=0, tiled=True)
     (local,) = run(
         local_grad_kernel,
         [shape((CELLS, LANES), F32)],
@@ -750,7 +749,6 @@
         sums,
         np.ascontiguousarray(analysis.T),
         local,
-        sent=(1,),
         flops=10**8,
     )
     return (

time: 72.2 us -> 71.7 us (level)
  no operation moved by 1% of the time
where the time goes in v12:
time: 71.7 us; the launch traced here: 71 us
  starting transfers between devices  27.1 us (38%)
  Pallas kernels  23.9 us (33%)
  waiting for transfers between devices  16.6 us (23%)
  local copies, waits for them, and re-layouts  2.57 us (4%)
  between operations  0.86 us (1%)
    pallas_call x10, Pallas kernels, run(): pl.pallas_call(kernel, out_shape=results, in_specs=[in_hbm if k in staged...  23.9 us
    all_to_all x4, starting transfers between devices, exchange(): lax.all_to_all(values, ('space', 'batch'), split_axis=0, concat_axis=0, t...  19.5 us
    all_to_all x4, waiting for transfers between devices, exchange(): lax.all_to_all(values, ('space', 'batch'), split_axis=0, concat_axis=0, t...  15.6 us
    ppermute x2, starting transfers between devices, neighbours(): before = lax.ppermute(last, 'space', [(i, i + 1) for i in range(ends)])  4.97 us
    ppermute x2, starting transfers between devices, neighbours(): after = lax.ppermute(first, 'space', [(i + 1, i) for i in range(ends)])  2.57 us
    unnamed x22, local copies, waits for them, and re-layouts  2.57 us
  transfers between devices with their start and end apart: 8, of which 5 were waited for; matrix products, arithmetic and copies ran while one was open for 0% of the time, Pallas kernels for 19%

profile of v12, /device:TPU:0, one launch (start us, length us, event | category | flops | bytes accessed | tf_op | source)
XLA Modules:
  0.0 71.0 jit_solution(13472321410637012978)
XLA Ops:
  0.6 3.2 %analyse_kernel.1 = (bf16[1024,128]{1,0:T(8,128)(2,1)}, bf16[256,128]{1,0:T(8,128)(2,1)}, bf16[512,128]{1,0:T(8,128)(2,1)}, bf16[512,128]{1,0:T(8,128)(2,1)}, bf16[102400,128]{1,0:T(8,128)(2,1)}) custom-call(bf16[64,2,1024]{2,1,0:T(2,128)(2,1)} %bitcast.22, bf16[256,1024]{1,0:T(8,128)(2,1)} %constant.16.clone.refs_1_, bf16[12288,64]{1,0:T(8,128)(2,1)} %bitcast.18, ...), custom_call_target="tpu_custom_call" | custom-call | flops 100000000 | bytes 32309248 | tf_op jit(solution)/shard_map/analyse_kernel/pallas_call | solution.py:573
  3.9 7.3 %all-to-all-start = ((bf16[32,8,128]{2,1,0:T(8,128)(2,1)}), bf16[32,8,128]{2,1,0:T(8,128)(2,1)S(1)}, u32[]{:S(2)}, u32[]{:S(2)}) async-start(bf16[32,8,128]{2,1,0:T(8,128)(2,1)} %bitcast.23), calls=%async_computation | async-start | bytes 131072 | tf_op jit(solution)/shard_map/all_to_all | solution.py:588
  11.2 2.8 %collective-permute-start = (bf16[512,128]{1,0:T(8,128)(2,1)}, bf16[512,128]{1,0:T(8,128)(2,1)}, u32[]{:S(2)}, u32[]{:S(2)}) collective-permute-start(bf16[512,128]{1,0:T(8,128)(2,1)} %get-tuple-element.34), channel_id=1, source_target_pairs={{0,1},{1,2},{2,3},{3,4},{4,5},{5,6},{6,7},{7,8},{8,9},{9,10},{10,1... | collective-permute-start | bytes 393224 | tf_op jit(solution)/shard_map/ppermute | solution.py:593
  14.0 1.3 %collective-permute-start.1 = (bf16[512,128]{1,0:T(8,128)(2,1)}, bf16[512,128]{1,0:T(8,128)(2,1)}, u32[]{:S(2)}, u32[]{:S(2)}) collective-permute-start(bf16[512,128]{1,0:T(8,128)(2,1)} %get-tuple-element.35), channel_id=1, source_target_pairs={{1,0},{2,1},{3,2},{4,3},{5,4},{6,5},{7,6},{8,7},{9,8},{10,9},{11,1... | collective-permute-start | bytes 393224 | tf_op jit(solution)/shard_map/ppermute | solution.py:594
  15.3 0.0 copy-start.6
  15.3 0.0 copy-start.7
  15.3 0.0 copy-start.3
  15.3 0.0 copy-start
  15.3 0.0 copy-start.1
  15.3 1.5 %fetch_kernel.1.refs_2_ = bf16[6144,128]{1,0:T(8,128)(2,1)S(1)} custom-call(bf16[102400,128]{1,0:T(8,128)(2,1)} %get-tuple-element.31.refs_0_.refs_1_), custom_call_target="tpu_custom_call" | custom-call | bytes 27787264 | tf_op jit(solution)/shard_map/fetch_kernel/pallas_call | solution.py:573
  16.9 1.9 %all-to-all-done = bf16[32,8,128]{2,1,0:T(8,128)(2,1)S(1)} async-done(((bf16[32,8,128]{2,1,0:T(8,128)(2,1)}), bf16[32,8,128]{2,1,0:T(8,128)(2,1)S(1)}, u32[]{:S(2)}, u32[]{:S(2)}) %all-to-all-start) | async-done | bytes 65568 | tf_op jit(solution)/shard_map/all_to_all | solution.py:588
  18.8 0.0 copy-done.6
  18.8 0.0 copy-done.7
  18.8 1.2 %mix_kernel.1 = (bf16[32,8,128]{2,1,0:T(8,128)(2,1)S(1)}, bf16[384,256]{1,0:T(8,128)(2,1)S(1)}) custom-call(bf16[256,128]{1,0:T(8,128)(2,1)S(1)} %bitcast.16, bf16[192,256]{1,0:T(8,128)(2,1)S(1)} %copy-done.7, bf16[6144,128]{1,0:T(8,128)(2,1)S(1)} %fetch_kernel.1.refs_2_, bf16[128,384]{1,0:T(8,128)(2,1)S(1)} %copy-done.6), custom_call_target="tpu_custom_call" | custom-call | flops 400000000 | bytes 2097152 | tf_op jit(solution)/shard_map/mix_kernel/pallas_call | solution.py:573
  20.0 0.0 copy-start.8
  20.0 0.6 copy-done.8
  20.7 5.4 %all-to-all-start.1 = ((bf16[32,8,128]{2,1,0:T(8,128)(2,1)}), bf16[32,8,128]{2,1,0:T(8,128)(2,1)S(1)}, u32[]{:S(2)}, u32[]{:S(2)}) async-start(bf16[32,8,128]{2,1,0:T(8,128)(2,1)} %copy-done.8), calls=%async_computation.1 | async-start | bytes 131072 | tf_op jit(solution)/shard_map/all_to_all | solution.py:588
  26.1 0.0 collective-permute-done.refs_1_
  26.1 0.0 collective-permute-done.1.refs_2_
  26.1 0.0 copy-done.3
  26.1 0.0 copy-start.9
  26.2 0.9 %copy-done.9 = bf16[1,64,2,1024]{3,2,1,0:T(2,128)(2,1)S(1)} copy-done((bf16[1,64,2,1024]{3,2,1,0:T(2,128)(2,1)S(1)}, bf16[1,64,2,1024]{3,2,1,0:T(2,128)(2,1)}, u32[]{:S(2)}) %copy-start.9) | copy-done | bytes 262168
  27.1 0.0 copy-start.10
  27.1 0.9 %copy-done.10 = bf16[1024,128]{1,0:T(8,128)(2,1)S(1)} copy-done((bf16[1024,128]{1,0:T(8,128)(2,1)S(1)}, bf16[1024,128]{1,0:T(8,128)(2,1)}, u32[]{:S(2)}) %copy-start.10) | copy-done | bytes 262168
  28.1 2.9 %local_kernel.1 = (f32[1024,128]{1,0:T(8,128)S(1)}, bf16[12800,1024]{1,0:T(8,128)(2,1)}, bf16[1024,128]{1,0:T(8,128)(2,1)S(1)}) custom-call(bf16[1024,128]{1,0:T(8,128)(2,1)S(1)} %copy-done.10, bf16[512,128]{1,0:T(8,128)(2,1)} %collective-permute-done.refs_1_, bf16[512,128]{1,0:T(8,128)(2,1)} %collective-permute-done.1.refs_2_, ...), custom_call_target="tpu_custom_call" | custom-call | flops 700000000 | bytes 28008448 | tf_op jit(solution)/shard_map/local_kernel/pallas_call | solution.py:573
  31.0 2.8 %all-to-all-done.1 = bf16[32,8,128]{2,1,0:T(8,128)(2,1)S(1)} async-done(((bf16[32,8,128]{2,1,0:T(8,128)(2,1)}), bf16[32,8,128]{2,1,0:T(8,128)(2,1)S(1)}, u32[]{:S(2)}, u32[]{:S(2)}) %all-to-all-start.1) | async-done | bytes 65568 | tf_op jit(solution)/shard_map/all_to_all | solution.py:588
  33.7 0.0 copy-done
  33.7 0.0 copy-done.1
  33.7 3.8 %activate_kernel.1 = (bf16[1024,128]{1,0:T(8,128)(2,1)S(1)}, bf16[102400,128]{1,0:T(8,128)(2,1)}, bf16[512,128]{1,0:T(8,128)(2,1)}, bf16[512,128]{1,0:T(8,128)(2,1)}, bf16[32,40,128]{2,1,0:T(8,128)(2,1)}) custom-call(bf16[256,128]{1,0:T(8,128)(2,1)S(1)} %bitcast.15, bf16[1024,256]{1,0:T(8,128)(2,1)S(1)} %copy-done.1, bf16[256,1024]{1,0:T(8,128)(2,1)S(1)} %copy-done, ...), custom_call_target="tpu_custom_call" | custom-call | flops 1000000000 | bytes 55181312 | tf_op jit(solution)/shard_map/activate_kernel/pallas_call | solution.py:573
  37.5 3.1 %all-to-all-start.2 = ((bf16[32,40,128]{2,1,0:T(8,128)(2,1)}), bf16[32,40,128]{2,1,0:T(8,128)(2,1)S(1)}, u32[]{:S(2)}, u32[]{:S(2)}) async-start(bf16[32,40,128]{2,1,0:T(8,128)(2,1)} %get-tuple-element.39), calls=%async_computation.2 | async-start | bytes 655360 | tf_op jit(solution)/shard_map/all_to_all | solution.py:588
  40.6 2.2 %collective-permute-start.2 = (bf16[512,128]{1,0:T(8,128)(2,1)}, bf16[512,128]{1,0:T(8,128)(2,1)S(1)}, u32[]{:S(2)}, u32[]{:S(2)}) collective-permute-start(bf16[512,128]{1,0:T(8,128)(2,1)} %get-tuple-element.40), channel_id=1, source_target_pairs={{0,1},{1,2},{2,3},{3,4},{4,5},{5,6},{6,7},{7,8},{8,9},{9,10},{10,1... | collective-permute-start | bytes 393224 | tf_op jit(solution)/shard_map/ppermute | solution.py:593
  42.8 1.3 %collective-permute-start.3 = (bf16[512,128]{1,0:T(8,128)(2,1)}, bf16[512,128]{1,0:T(8,128)(2,1)S(1)}, u32[]{:S(2)}, u32[]{:S(2)}) collective-permute-start(bf16[512,128]{1,0:T(8,128)(2,1)} %get-tuple-element.41), channel_id=1, source_target_pairs={{1,0},{2,1},{3,2},{4,3},{5,4},{6,5},{7,6},{8,7},{9,8},{10,9},{11,1... | collective-permute-start | bytes 393224 | tf_op jit(solution)/shard_map/ppermute | solution.py:594
  44.1 0.0 copy-start.4
  44.1 0.0 copy-start.5
  44.1 2.2 %output_kernel.1 = (bf16[64,2,1024]{2,1,0:T(2,128)(2,1)}, bf16[6144,128]{1,0:T(8,128)(2,1)S(1)}) custom-call(bf16[1024,128]{1,0:T(8,128)(2,1)S(1)} %get-tuple-element.42.refs_0_, bf16[102400,128]{1,0:T(8,128)(2,1)} %get-tuple-element.31.refs_0_.refs_1_), custom_call_target="tpu_custom_call" | custom-call | flops 100000000 | bytes 28311552 | tf_op jit(solution)/shard_map/output_kernel/pallas_call | solution.py:573
  46.3 0.0 collective-permute-done.2.refs_1_
  46.3 1.1 %collective-permute-done.3.refs_2_ = bf16[512,128]{1,0:T(8,128)(2,1)S(1)} collective-permute-done((bf16[512,128]{1,0:T(8,128)(2,1)}, bf16[512,128]{1,0:T(8,128)(2,1)S(1)}, u32[]{:S(2)}, u32[]{:S(2)}) %collective-permute-start.3) | collective-permute-done | bytes 131104 | tf_op jit(solution)/shard_map/ppermute | solution.py:594
  47.4 5.0 %all-to-all-done.2.refs_0_ = bf16[32,40,128]{2,1,0:T(8,128)(2,1)S(1)} async-done(((bf16[32,40,128]{2,1,0:T(8,128)(2,1)}), bf16[32,40,128]{2,1,0:T(8,128)(2,1)S(1)}, u32[]{:S(2)}, u32[]{:S(2)}) %all-to-all-start.2) | async-done | bytes 327712 | tf_op jit(solution)/shard_map/all_to_all | solution.py:588
  52.3 0.0 copy-done.4
  52.3 0.0 copy-done.5
  52.3 1.8 %unmix_kernel.1 = (bf16[32,40,128]{2,1,0:T(8,128)(2,1)}, bf16[384,128]{1,0:T(8,128)(2,1)S(1)}) custom-call(bf16[32,40,128]{2,1,0:T(8,128)(2,1)S(1)} %all-to-all-done.2.refs_0_, bf16[192,256]{1,0:T(8,128)(2,1)S(1)} %copy-done.5, bf16[6144,128]{1,0:T(8,128)(2,1)S(1)} %get-tuple-element.47.refs_2_, bf16[128,384]{1,0:T(8,128)(2,1)S(1)} %copy-done.4), custom_call_target="tpu_custom_call" | custom-call | flops 400000000 | bytes 2523136 | tf_op jit(solution)/shard_map/unmix_kernel/pallas_call | solution.py:573
  54.1 3.7 %all-to-all-start.3 = ((bf16[32,40,128]{2,1,0:T(8,128)(2,1)}), bf16[32,40,128]{2,1,0:T(8,128)(2,1)S(1)}, u32[]{:S(2)}, u32[]{:S(2)}) async-start(bf16[32,40,128]{2,1,0:T(8,128)(2,1)} %get-tuple-element.48), calls=%async_computation.3 | async-start | bytes 655360 | tf_op jit(solution)/shard_map/all_to_all | solution.py:588
  57.8 3.7 %weight_kernel.1 = f32[12288,64]{1,0:T(8,128)} custom-call(bf16[384,256]{1,0:T(8,128)(2,1)S(1)} %get-tuple-element.53.refs_0_, bf16[384,128]{1,0:T(8,128)(2,1)S(1)} %get-tuple-element.54.refs_1_), custom_call_target="tpu_custom_call" | custom-call | flops 400000000 | bytes 3440640 | tf_op jit(solution)/shard_map/weight_kernel/pallas_call | solution.py:573
  61.6 0.0 copy-start.2
  61.6 2.1 %local_grad_kernel.1.refs_2_ = f32[1024,128]{1,0:T(8,128)S(1)} custom-call(bf16[102400,128]{1,0:T(8,128)(2,1)} %get-tuple-element.49.refs_0_, bf16[512,128]{1,0:T(8,128)(2,1)S(1)} %collective-permute-done.2.refs_1_, bf16[512,128]{1,0:T(8,128)(2,1)S(1)} %collective-permute-done.3.refs_2_, bf16[27,64,64]{2,1,0:T(8,128)(2,1)S(1)} %bitcast.14), custom_call_target="tpu_custom_call" | custom-call | flops 700000000 | bytes 27222016 | tf_op jit(solution)/shard_map/local_grad_kernel/pallas_call | solution.py:573
  63.6 5.9 %all-to-all-done.3.refs_0_ = bf16[32,40,128]{2,1,0:T(8,128)(2,1)S(1)} async-done(((bf16[32,40,128]{2,1,0:T(8,128)(2,1)}), bf16[32,40,128]{2,1,0:T(8,128)(2,1)S(1)}, u32[]{:S(2)}, u32[]{:S(2)}) %all-to-all-start.3) | async-done | bytes 327712 | tf_op jit(solution)/shard_map/all_to_all | solution.py:588
  69.6 0.0 copy-done.2
  69.6 1.5 %finish_kernel.1 = (bf16[64,2,1024]{2,1,0:T(2,128)(2,1)}, f32[27,64,64]{2,1,0:T(8,128)}) custom-call(bf16[32,40,128]{2,1,0:T(8,128)(2,1)S(1)} %all-to-all-done.3.refs_0_, bf16[1024,256]{1,0:T(8,128)(2,1)S(1)} %copy-done.2, f32[1024,128]{1,0:T(8,128)S(1)} %local_grad_kernel.1.refs_2_), custom_call_target="tpu_custom_call" | custom-call | flops 100000000 | bytes 2080768 | tf_op jit(solution)/shard_map/finish_kernel/pallas_call | solution.py:573
Async XLA Ops:
  3.9 14.9 %all-to-all-start = ((bf16[32,8,128]{2,1,0:T(8,128)(2,1)}), bf16[32,8,128]{2,1,0:T(8,128)(2,1)S(1)}, u32[]{:S(2)}, u32[]{:S(2)}) async-start(bf16[32,8,128]{2,1,0:T(8,128)(2,1)} %bitcast.23), calls=%async_computation | async-start | bytes 131072 | tf_op jit(solution)/shard_map/all_to_all | solution.py:588
  11.2 14.9 %collective-permute-start = (bf16[512,128]{1,0:T(8,128)(2,1)}, bf16[512,128]{1,0:T(8,128)(2,1)}, u32[]{:S(2)}, u32[]{:S(2)}) collective-permute-start(bf16[512,128]{1,0:T(8,128)(2,1)} %get-tuple-element.34), channel_id=1, source_target_pairs={{0,1},{1,2},{2,3},{3,4},{4,5},{5,6},{6,7},{7,8},{8,9},{9,10},{10,1... | collective-permute-start | bytes 393224 | tf_op jit(solution)/shard_map/ppermute | solution.py:593
  14.0 12.1 %collective-permute-start.1 = (bf16[512,128]{1,0:T(8,128)(2,1)}, bf16[512,128]{1,0:T(8,128)(2,1)}, u32[]{:S(2)}, u32[]{:S(2)}) collective-permute-start(bf16[512,128]{1,0:T(8,128)(2,1)} %get-tuple-element.35), channel_id=1, source_target_pairs={{1,0},{2,1},{3,2},{4,3},{5,4},{6,5},{7,6},{8,7},{9,8},{10,9},{11,1... | collective-permute-start | bytes 393224 | tf_op jit(solution)/shard_map/ppermute | solution.py:594
  15.3 3.5 %copy-start.6 = (bf16[128,384]{1,0:T(8,128)(2,1)S(1)}, bf16[128,384]{1,0:T(8,128)(2,1)}, u32[]{:S(2)}) copy-start(bf16[128,384]{1,0:T(8,128)(2,1)} %constant.18.clone.refs_3_) | copy-start | bytes 294916
  15.3 3.5 %copy-start.7 = (bf16[192,256]{1,0:T(8,128)(2,1)S(1)}, bf16[192,256]{1,0:T(8,128)(2,1)}, u32[]{:S(2)}) copy-start(bf16[192,256]{1,0:T(8,128)(2,1)} %constant.17.clone.refs_1_) | copy-start | bytes 294916
  15.3 10.8 %copy-start.3 = (bf16[3,3,3,64,64]{4,3,2,1,0:T(8,128)(2,1)S(1)}, bf16[3,3,3,64,64]{4,3,2,1,0:T(8,128)(2,1)}, u32[]{:S(2)}) copy-start(bf16[3,3,3,64,64]{4,3,2,1,0:T(8,128)(2,1)} %param.15) | copy-start | bytes 663556
  15.3 18.4 %copy-start = (bf16[256,1024]{1,0:T(8,128)(2,1)S(1)}, bf16[256,1024]{1,0:T(8,128)(2,1)}, u32[]{:S(2)}) copy-start(bf16[256,1024]{1,0:T(8,128)(2,1)} %constant.20.clone.refs_2_) | copy-start | bytes 1572868
  15.3 18.4 %copy-start.1 = (bf16[1024,256]{1,0:T(8,128)(2,1)S(1)}, bf16[1024,256]{1,0:T(8,128)(2,1)}, u32[]{:S(2)}) copy-start(bf16[1024,256]{1,0:T(8,128)(2,1)} %constant.19.clone.refs_1_) | copy-start | bytes 1572868
  20.0 0.6 copy-start.8
  20.7 13.1 %all-to-all-start.1 = ((bf16[32,8,128]{2,1,0:T(8,128)(2,1)}), bf16[32,8,128]{2,1,0:T(8,128)(2,1)S(1)}, u32[]{:S(2)}, u32[]{:S(2)}) async-start(bf16[32,8,128]{2,1,0:T(8,128)(2,1)} %copy-done.8), calls=%async_computation.1 | async-start | bytes 131072 | tf_op jit(solution)/shard_map/all_to_all | solution.py:588
  26.1 1.0 %copy-start.9 = (bf16[1,64,2,1024]{3,2,1,0:T(2,128)(2,1)S(1)}, bf16[1,64,2,1024]{3,2,1,0:T(2,128)(2,1)}, u32[]{:S(2)}) copy-start(bf16[1,64,2,1024]{3,2,1,0:T(2,128)(2,1)} %param.13) | copy-start | bytes 786436
  27.1 0.9 %copy-start.10 = (bf16[1024,128]{1,0:T(8,128)(2,1)S(1)}, bf16[1024,128]{1,0:T(8,128)(2,1)}, u32[]{:S(2)}) copy-start(bf16[1024,128]{1,0:T(8,128)(2,1)} %get-tuple-element.33.refs_0_) | copy-start | bytes 786436
  37.5 14.8 %all-to-all-start.2 = ((bf16[32,40,128]{2,1,0:T(8,128)(2,1)}), bf16[32,40,128]{2,1,0:T(8,128)(2,1)S(1)}, u32[]{:S(2)}, u32[]{:S(2)}) async-start(bf16[32,40,128]{2,1,0:T(8,128)(2,1)} %get-tuple-element.39), calls=%async_computation.2 | async-start | bytes 655360 | tf_op jit(solution)/shard_map/all_to_all | solution.py:588
  40.6 5.7 %collective-permute-start.2 = (bf16[512,128]{1,0:T(8,128)(2,1)}, bf16[512,128]{1,0:T(8,128)(2,1)S(1)}, u32[]{:S(2)}, u32[]{:S(2)}) collective-permute-start(bf16[512,128]{1,0:T(8,128)(2,1)} %get-tuple-element.40), channel_id=1, source_target_pairs={{0,1},{1,2},{2,3},{3,4},{4,5},{5,6},{6,7},{7,8},{8,9},{9,10},{10,1... | collective-permute-start | bytes 393224 | tf_op jit(solution)/shard_map/ppermute | solution.py:593
  42.8 4.6 %collective-permute-start.3 = (bf16[512,128]{1,0:T(8,128)(2,1)}, bf16[512,128]{1,0:T(8,128)(2,1)S(1)}, u32[]{:S(2)}, u32[]{:S(2)}) collective-permute-start(bf16[512,128]{1,0:T(8,128)(2,1)} %get-tuple-element.41), channel_id=1, source_target_pairs={{1,0},{2,1},{3,2},{4,3},{5,4},{6,5},{7,6},{8,7},{9,8},{10,9},{11,1... | collective-permute-start | bytes 393224 | tf_op jit(solution)/shard_map/ppermute | solution.py:594
  44.1 8.3 %copy-start.4 = (bf16[128,384]{1,0:T(8,128)(2,1)S(1)}, bf16[128,384]{1,0:T(8,128)(2,1)}, u32[]{:S(2)}) copy-start(bf16[128,384]{1,0:T(8,128)(2,1)} %constant.22.clone.refs_3_) | copy-start | bytes 294916
  44.1 8.2 %copy-start.5 = (bf16[192,256]{1,0:T(8,128)(2,1)S(1)}, bf16[192,256]{1,0:T(8,128)(2,1)}, u32[]{:S(2)}) copy-start(bf16[192,256]{1,0:T(8,128)(2,1)} %constant.21.clone.refs_1_) | copy-start | bytes 294916
  54.1 15.4 %all-to-all-start.3 = ((bf16[32,40,128]{2,1,0:T(8,128)(2,1)}), bf16[32,40,128]{2,1,0:T(8,128)(2,1)S(1)}, u32[]{:S(2)}, u32[]{:S(2)}) async-start(bf16[32,40,128]{2,1,0:T(8,128)(2,1)} %get-tuple-element.48), calls=%async_computation.3 | async-start | bytes 655360 | tf_op jit(solution)/shard_map/all_to_all | solution.py:588
  61.6 8.0 %copy-start.2 = (bf16[1024,256]{1,0:T(8,128)(2,1)S(1)}, bf16[1024,256]{1,0:T(8,128)(2,1)}, u32[]{:S(2)}) copy-start(bf16[1024,256]{1,0:T(8,128)(2,1)} %constant.23.clone.refs_1_) | copy-start | bytes 1572868

commit v13 on v12

--- a/solution.py
+++ b/solution.py
@@ -207,7 +207,7 @@
 
 def analyse_kernel(field, analysis, *refs):
     weights = refs[:CHUNKS]
-    cells_out, coef_out, first_out, last_out, packed_out, buffer, semaphores = refs[CHUNKS:]
+    cells_out, coef_out, first_out, last_out, packed_out, _, buffer, semaphores = refs[CHUNKS:]
     cells = to_cells(field[...])
     rounded = cells.astype(BF16)
     coef_out[...] = dot(analysis[...], rounded).astype(BF16)
@@ -334,12 +334,10 @@
     density = jnp.exp(-0.5 * pre * pre) * inv_root_two_pi
     activated_out[...] = (pre * cdf).astype(BF16)
     grad = (cotangent[...].astype(F32) * (cdf + pre * density)).astype(BF16)
-    grad_out[...] = grad
     back = dot(synthesis_rows[...], grad)
+    rounded = grad
     grad = grad.astype(F32)
     first, last = edge_layers(grad)
-    first_out[...] = first
-    last_out[...] = last
     spread[0:NY, :] = jnp.zeros((NY, 3 * LANES), BF16)
     spread[NY + CELLS : 2 * NY + CELLS, :] = jnp.zeros((NY, 3 * LANES), BF16)
     spread[NY : NY + CELLS, 0:LANES] = from_above(grad).astype(BF16)
@@ -370,6 +368,9 @@
     else:
         back_out[...] = back.astype(BF16)
         terms_out[...] = terms.astype(BF16)
+    grad_out[...] = rounded
+    first_out[...] = first
+    last_out[...] = last
 
 
 def slab_store(slab, modes, terms):
@@ -505,7 +506,7 @@
 
 
 def run(
-    body, outs, *operands, staged=(), sent=(), moved=(), plain=(), scratch=(), flops=0, limit=VMEM_BYTES
+    body, outs, *operands, staged=(), sent=(), moved=(), plain=(), slots=(), scratch=(), flops=0, limit=VMEM_BYTES
 ):
     given = [k for k, operand in enumerate(operands) if operand is not None]
     made = [k for k, out in enumerate(outs) if out is not None]
@@ -515,6 +516,7 @@
         return {k: rows or arrays[k].shape[0] for k, rows in chosen.items()}
 
     moved = dict(moved)
+    slots = dict(slots)
     staged = rows_of(staged, given, operands)
     sent = rows_of(sent, made, outs)
 
@@ -532,6 +534,7 @@
             return ref if ref.shape[0] == rows else ref.at[0:rows]
 
         filled = dict(zip(given, take(len(given))))
+        take(len(slots))
         kept = dict(zip(made, take(len(made))))
         own = take(len(scratch))
         copies = []
@@ -573,13 +576,15 @@
     results = pl.pallas_call(
         kernel,
         out_shape=results,
-        in_specs=[in_hbm if k in staged or k in moved else in_vmem for k in given],
+        in_specs=[in_hbm if k in staged or k in moved else in_vmem for k in given]
+        + [in_hbm] * len(slots),
         out_specs=[in_hbm if k in sent or k in plain else in_vmem for k in made],
+        input_output_aliases={len(given) + at: made.index(k) for at, k in enumerate(slots)},
         scratch_shapes=[*scratch, *buffers],
         compiler_params=pltpu.CompilerParams(vmem_limit_bytes=limit),
         cost_estimate=pl.CostEstimate(flops=flops, bytes_accessed=size, transcendentals=0),
         name=body.__name__ if hasattr(body, "__name__") else body.func.__name__,
-    )(*arrays)
+    )(*arrays, *slots.values())
     results = dict(zip(made, results))
     return [results.get(k) for k in range(len(outs))]
 
@@ -622,15 +627,23 @@
 
     packed = shape((weights.shape[0] // 2, LANES), BF16)
     share = weights.shape[0] // CHUNKS
-    cells, coef, first, last, kept_weights = run(
+    to_send = shape((devices, modes, LANES), BF16) if modes % 8 == 0 else plane_modes
+    cells, coef, first, last, kept_weights, slot = run(
         analyse_kernel,
-        [wide, plane_modes, edge, edge, shape((HBM_BYTES // (2 * LANES), LANES), BF16)],
+        [
+            wide,
+            plane_modes,
+            edge,
+            edge,
+            shape((HBM_BYTES // (2 * LANES), LANES), BF16),
+            to_send,
+        ],
         snapshots.reshape(field.shape),
         analysis,
         *[weights] * CHUNKS,
         staged={0: None, 1: None} | {2 + k: slice(k * share, (k + 1) * share) for k in range(CHUNKS)},
         sent=(0, 1, 2, 3),
-        plain=(4,),
+        plain=(4, 5),
         scratch=[pltpu.VMEM(packed.shape, BF16), pltpu.SemaphoreType.DMA((CHUNKS,))],
         limit=WHOLE_VMEM,
         flops=10**8,
@@ -652,15 +665,13 @@
     )
     back, diagonal = run(
         functools.partial(mix_kernel, batches, slabs),
-        [
-            shape((devices, modes, LANES), BF16) if modes % 8 == 0 else plane_modes,
-            shape((count, GROUP * half // 2), BF16),
-        ],
+        [to_send, shape((count, GROUP * half // 2), BF16)],
         coef,
         gather,
         packed_weights,
         scatter,
         sent=(0, 1),
+        slots={0: slot},
         flops=4 * 10**8,
     )
     back = send(back)

time: 71.7 us -> 71.6 us (level)
    unnamed x22 -> x20, local copies, waits for them, and re-layouts: 2.57 us -> 1.95 us
  transfers between devices with their start and end apart: 8 -> 8, of which waited for: 5 -> 5; matrix products, arithmetic and copies ran while one was open for 0% -> 0% of each run, Pallas kernels for 19% -> 20%
where the time goes in v13:
time: 71.6 us; the launch traced here: 71 us
  starting transfers between devices  27.1 us (38%)
  Pallas kernels  24.5 us (34%)
  waiting for transfers between devices  16.6 us (23%)
  local copies, waits for them, and re-layouts  1.95 us (3%)
  between operations  0.85 us (1%)
    pallas_call x10, Pallas kernels, run(): pl.pallas_call(kernel, out_shape=results, in_specs=[in_hbm if k in staged...  24.5 us
    all_to_all x4, starting transfers between devices, exchange(): lax.all_to_all(values, ('space', 'batch'), split_axis=0, concat_axis=0, t...  19.5 us
    all_to_all x4, waiting for transfers between devices, exchange(): lax.all_to_all(values, ('space', 'batch'), split_axis=0, concat_axis=0, t...  15.5 us
    ppermute x2, starting transfers between devices, neighbours(): before = lax.ppermute(last, 'space', [(i, i + 1) for i in range(ends)])  4.98 us
    ppermute x2, starting transfers between devices, neighbours(): after = lax.ppermute(first, 'space', [(i + 1, i) for i in range(ends)])  2.57 us
    unnamed x20, local copies, waits for them, and re-layouts  1.95 us
  transfers between devices with their start and end apart: 8, of which 5 were waited for; matrix products, arithmetic and copies ran while one was open for 0% of the time, Pallas kernels for 20%

profile of v13, /device:TPU:0, one launch (start us, length us, event | category | flops | bytes accessed | tf_op | source)
XLA Modules:
  0.0 71.0 jit_solution(8301694879680003416)
XLA Ops:
  0.6 3.2 %analyse_kernel.1 = (bf16[1024,128]{1,0:T(8,128)(2,1)}, bf16[256,128]{1,0:T(8,128)(2,1)}, bf16[512,128]{1,0:T(8,128)(2,1)}, bf16[512,128]{1,0:T(8,128)(2,1)}, bf...) custom-call(bf16[64,2,1024]{2,1,0:T(2,128)(2,1)} %bitcast.22, bf16[256,1024]{1,0:T(8,128)(2,1)} %constant.16.clone.refs_1_, ...), custom_call_target="tpu_custom_call" | custom-call | flops 100000000 | bytes 32374784 | tf_op jit(solution)/shard_map/analyse_kernel/pallas_call | solution.py:576
  3.8 7.3 %all-to-all-start = ((bf16[32,8,128]{2,1,0:T(8,128)(2,1)}), bf16[32,8,128]{2,1,0:T(8,128)(2,1)S(1)}, u32[]{:S(2)}, u32[]{:S(2)}) async-start(bf16[32,8,128]{2,1,0:T(8,128)(2,1)} %bitcast.23), calls=%async_computation | async-start | bytes 131072 | tf_op jit(solution)/shard_map/all_to_all | solution.py:593
  11.2 2.8 %collective-permute-start = (bf16[512,128]{1,0:T(8,128)(2,1)}, bf16[512,128]{1,0:T(8,128)(2,1)}, u32[]{:S(2)}, u32[]{:S(2)}) collective-permute-start(bf16[512,128]{1,0:T(8,128)(2,1)} %get-tuple-element.36), channel_id=1, source_target_pairs={{0,1},{1,2},{2,3},{3,4},{4,5},{5,6},{6,7},{7,8},{8,9},{9,10},{10,1... | collective-permute-start | bytes 393224 | tf_op jit(solution)/shard_map/ppermute | solution.py:598
  14.0 1.3 %collective-permute-start.1 = (bf16[512,128]{1,0:T(8,128)(2,1)}, bf16[512,128]{1,0:T(8,128)(2,1)}, u32[]{:S(2)}, u32[]{:S(2)}) collective-permute-start(bf16[512,128]{1,0:T(8,128)(2,1)} %get-tuple-element.37), channel_id=1, source_target_pairs={{1,0},{2,1},{3,2},{4,3},{5,4},{6,5},{7,6},{8,7},{9,8},{10,9},{11,1... | collective-permute-start | bytes 393224 | tf_op jit(solution)/shard_map/ppermute | solution.py:599
  15.3 0.0 copy-start.6
  15.3 0.0 copy-start.7
  15.3 0.0 copy-start.3
  15.3 0.0 copy-start
  15.3 0.0 copy-start.1
  15.3 1.5 %fetch_kernel.1.refs_2_ = bf16[6144,128]{1,0:T(8,128)(2,1)S(1)} custom-call(bf16[102400,128]{1,0:T(8,128)(2,1)} %get-tuple-element.32.refs_0_.refs_1_), custom_call_target="tpu_custom_call" | custom-call | bytes 27787264 | tf_op jit(solution)/shard_map/fetch_kernel/pallas_call | solution.py:576
  16.9 1.9 %all-to-all-done = bf16[32,8,128]{2,1,0:T(8,128)(2,1)S(1)} async-done(((bf16[32,8,128]{2,1,0:T(8,128)(2,1)}), bf16[32,8,128]{2,1,0:T(8,128)(2,1)S(1)}, u32[]{:S(2)}, u32[]{:S(2)}) %all-to-all-start) | async-done | bytes 65568 | tf_op jit(solution)/shard_map/all_to_all | solution.py:593
  18.8 0.0 copy-done.6
  18.8 0.0 copy-done.7
  18.8 1.8 %mix_kernel.1 = (bf16[32,8,128]{2,1,0:T(8,128)(2,1)}, bf16[384,256]{1,0:T(8,128)(2,1)S(1)}) custom-call(bf16[256,128]{1,0:T(8,128)(2,1)S(1)} %bitcast.16, bf16[192,256]{1,0:T(8,128)(2,1)S(1)} %copy-done.7, bf16[6144,128]{1,0:T(8,128)(2,1)S(1)} %fetch_kernel.1.refs_2_, bf16[128,384]{1,0:T(8,128)(2,1)S(1)} %copy-done.6, ...), custom_call_target="tpu_custom_call", output_to_operand_aliasing={{0}: (4, {})} | custom-call | flops 400000000 | bytes 2097152 | tf_op jit(solution)/shard_map/mix_kernel/pallas_call | solution.py:576
  20.6 5.4 %all-to-all-start.1 = ((bf16[32,8,128]{2,1,0:T(8,128)(2,1)}), bf16[32,8,128]{2,1,0:T(8,128)(2,1)S(1)}, u32[]{:S(2)}, u32[]{:S(2)}) async-start(bf16[32,8,128]{2,1,0:T(8,128)(2,1)} %get-tuple-element.34), calls=%async_computation.1 | async-start | bytes 131072 | tf_op jit(solution)/shard_map/all_to_all | solution.py:593
  26.0 0.0 collective-permute-done.refs_1_
  26.0 0.0 collective-permute-done.1.refs_2_
  26.0 0.0 copy-done.3
  26.0 0.0 copy-start.8
  26.1 0.9 %copy-done.8 = bf16[1,64,2,1024]{3,2,1,0:T(2,128)(2,1)S(1)} copy-done((bf16[1,64,2,1024]{3,2,1,0:T(2,128)(2,1)S(1)}, bf16[1,64,2,1024]{3,2,1,0:T(2,128)(2,1)}, u32[]{:S(2)}) %copy-start.8) | copy-done | bytes 262168
  27.0 0.0 copy-start.9
  27.0 0.9 %copy-done.9 = bf16[1024,128]{1,0:T(8,128)(2,1)S(1)} copy-done((bf16[1024,128]{1,0:T(8,128)(2,1)S(1)}, bf16[1024,128]{1,0:T(8,128)(2,1)}, u32[]{:S(2)}) %copy-start.9) | copy-done | bytes 262168
  27.9 2.9 %local_kernel.1 = (f32[1024,128]{1,0:T(8,128)S(1)}, bf16[12800,1024]{1,0:T(8,128)(2,1)}, bf16[1024,128]{1,0:T(8,128)(2,1)S(1)}) custom-call(bf16[1024,128]{1,0:T(8,128)(2,1)S(1)} %copy-done.9, bf16[512,128]{1,0:T(8,128)(2,1)} %collective-permute-done.refs_1_, bf16[512,128]{1,0:T(8,128)(2,1)} %collective-permute-done.1.refs_2_, ...), custom_call_target="tpu_custom_call" | custom-call | flops 700000000 | bytes 28008448 | tf_op jit(solution)/shard_map/local_kernel/pallas_call | solution.py:576
  30.9 2.8 %all-to-all-done.1 = bf16[32,8,128]{2,1,0:T(8,128)(2,1)S(1)} async-done(((bf16[32,8,128]{2,1,0:T(8,128)(2,1)}), bf16[32,8,128]{2,1,0:T(8,128)(2,1)S(1)}, u32[]{:S(2)}, u32[]{:S(2)}) %all-to-all-start.1) | async-done | bytes 65568 | tf_op jit(solution)/shard_map/all_to_all | solution.py:593
  33.6 0.0 copy-done
  33.6 0.0 copy-done.1
  33.6 3.8 %activate_kernel.1 = (bf16[1024,128]{1,0:T(8,128)(2,1)S(1)}, bf16[102400,128]{1,0:T(8,128)(2,1)}, bf16[512,128]{1,0:T(8,128)(2,1)}, bf16[512,128]{1,0:T(8,128)(2,1)}, bf16[32,40,128]{2,1,0:T(8,128)(2,1)}) custom-call(bf16[256,128]{1,0:T(8,128)(2,1)S(1)} %bitcast.15, bf16[1024,256]{1,0:T(8,128)(2,1)S(1)} %copy-done.1, bf16[256,1024]{1,0:T(8,128)(2,1)S(1)} %copy-done, ...), custom_call_target="tpu_custom_call" | custom-call | flops 1000000000 | bytes 55181312 | tf_op jit(solution)/shard_map/activate_kernel/pallas_call | solution.py:576
  37.4 3.1 %all-to-all-start.2 = ((bf16[32,40,128]{2,1,0:T(8,128)(2,1)}), bf16[32,40,128]{2,1,0:T(8,128)(2,1)S(1)}, u32[]{:S(2)}, u32[]{:S(2)}) async-start(bf16[32,40,128]{2,1,0:T(8,128)(2,1)} %get-tuple-element.41), calls=%async_computation.2 | async-start | bytes 655360 | tf_op jit(solution)/shard_map/all_to_all | solution.py:593
  40.5 2.2 %collective-permute-start.2 = (bf16[512,128]{1,0:T(8,128)(2,1)}, bf16[512,128]{1,0:T(8,128)(2,1)S(1)}, u32[]{:S(2)}, u32[]{:S(2)}) collective-permute-start(bf16[512,128]{1,0:T(8,128)(2,1)} %get-tuple-element.42), channel_id=1, source_target_pairs={{0,1},{1,2},{2,3},{3,4},{4,5},{5,6},{6,7},{7,8},{8,9},{9,10},{10,1... | collective-permute-start | bytes 393224 | tf_op jit(solution)/shard_map/ppermute | solution.py:598
  42.7 1.3 %collective-permute-start.3 = (bf16[512,128]{1,0:T(8,128)(2,1)}, bf16[512,128]{1,0:T(8,128)(2,1)S(1)}, u32[]{:S(2)}, u32[]{:S(2)}) collective-permute-start(bf16[512,128]{1,0:T(8,128)(2,1)} %get-tuple-element.43), channel_id=1, source_target_pairs={{1,0},{2,1},{3,2},{4,3},{5,4},{6,5},{7,6},{8,7},{9,8},{10,9},{11,1... | collective-permute-start | bytes 393224 | tf_op jit(solution)/shard_map/ppermute | solution.py:599
  44.0 0.0 copy-start.4
  44.0 0.0 copy-start.5
  44.0 2.2 %output_kernel.1 = (bf16[64,2,1024]{2,1,0:T(2,128)(2,1)}, bf16[6144,128]{1,0:T(8,128)(2,1)S(1)}) custom-call(bf16[1024,128]{1,0:T(8,128)(2,1)S(1)} %get-tuple-element.44.refs_0_, bf16[102400,128]{1,0:T(8,128)(2,1)} %get-tuple-element.32.refs_0_.refs_1_), custom_call_target="tpu_custom_call" | custom-call | flops 100000000 | bytes 28311552 | tf_op jit(solution)/shard_map/output_kernel/pallas_call | solution.py:576
  46.2 0.0 collective-permute-done.2.refs_1_
  46.2 1.1 %collective-permute-done.3.refs_2_ = bf16[512,128]{1,0:T(8,128)(2,1)S(1)} collective-permute-done((bf16[512,128]{1,0:T(8,128)(2,1)}, bf16[512,128]{1,0:T(8,128)(2,1)S(1)}, u32[]{:S(2)}, u32[]{:S(2)}) %collective-permute-start.3) | collective-permute-done | bytes 131104 | tf_op jit(solution)/shard_map/ppermute | solution.py:599
  47.3 5.0 %all-to-all-done.2.refs_0_ = bf16[32,40,128]{2,1,0:T(8,128)(2,1)S(1)} async-done(((bf16[32,40,128]{2,1,0:T(8,128)(2,1)}), bf16[32,40,128]{2,1,0:T(8,128)(2,1)S(1)}, u32[]{:S(2)}, u32[]{:S(2)}) %all-to-all-start.2) | async-done | bytes 327712 | tf_op jit(solution)/shard_map/all_to_all | solution.py:593
  52.3 0.0 copy-done.4
  52.3 0.0 copy-done.5
  52.3 1.8 %unmix_kernel.1 = (bf16[32,40,128]{2,1,0:T(8,128)(2,1)}, bf16[384,128]{1,0:T(8,128)(2,1)S(1)}) custom-call(bf16[32,40,128]{2,1,0:T(8,128)(2,1)S(1)} %all-to-all-done.2.refs_0_, bf16[192,256]{1,0:T(8,128)(2,1)S(1)} %copy-done.5, bf16[6144,128]{1,0:T(8,128)(2,1)S(1)} %get-tuple-element.49.refs_2_, bf16[128,384]{1,0:T(8,128)(2,1)S(1)} %copy-done.4), custom_call_target="tpu_custom_call" | custom-call | flops 400000000 | bytes 2523136 | tf_op jit(solution)/shard_map/unmix_kernel/pallas_call | solution.py:576
  54.1 3.7 %all-to-all-start.3 = ((bf16[32,40,128]{2,1,0:T(8,128)(2,1)}), bf16[32,40,128]{2,1,0:T(8,128)(2,1)S(1)}, u32[]{:S(2)}, u32[]{:S(2)}) async-start(bf16[32,40,128]{2,1,0:T(8,128)(2,1)} %get-tuple-element.50), calls=%async_computation.3 | async-start | bytes 655360 | tf_op jit(solution)/shard_map/all_to_all | solution.py:593
  57.8 3.7 %weight_kernel.1 = f32[12288,64]{1,0:T(8,128)} custom-call(bf16[384,256]{1,0:T(8,128)(2,1)S(1)} %get-tuple-element.55.refs_0_, bf16[384,128]{1,0:T(8,128)(2,1)S(1)} %get-tuple-element.56.refs_1_), custom_call_target="tpu_custom_call" | custom-call | flops 400000000 | bytes 3440640 | tf_op jit(solution)/shard_map/weight_kernel/pallas_call | solution.py:576
  61.5 0.0 copy-start.2
  61.5 2.1 %local_grad_kernel.1.refs_2_ = f32[1024,128]{1,0:T(8,128)S(1)} custom-call(bf16[102400,128]{1,0:T(8,128)(2,1)} %get-tuple-element.51.refs_0_, bf16[512,128]{1,0:T(8,128)(2,1)S(1)} %collective-permute-done.2.refs_1_, bf16[512,128]{1,0:T(8,128)(2,1)S(1)} %collective-permute-done.3.refs_2_, bf16[27,64,64]{2,1,0:T(8,128)(2,1)S(1)} %bitcast.14), custom_call_target="tpu_custom_call" | custom-call | flops 700000000 | bytes 27222016 | tf_op jit(solution)/shard_map/local_grad_kernel/pallas_call | solution.py:576
  63.6 5.9 %all-to-all-done.3.refs_0_ = bf16[32,40,128]{2,1,0:T(8,128)(2,1)S(1)} async-done(((bf16[32,40,128]{2,1,0:T(8,128)(2,1)}), bf16[32,40,128]{2,1,0:T(8,128)(2,1)S(1)}, u32[]{:S(2)}, u32[]{:S(2)}) %all-to-all-start.3) | async-done | bytes 327712 | tf_op jit(solution)/shard_map/all_to_all | solution.py:593
  69.5 0.0 copy-done.2
  69.5 1.5 %finish_kernel.1 = (bf16[64,2,1024]{2,1,0:T(2,128)(2,1)}, f32[27,64,64]{2,1,0:T(8,128)}) custom-call(bf16[32,40,128]{2,1,0:T(8,128)(2,1)S(1)} %all-to-all-done.3.refs_0_, bf16[1024,256]{1,0:T(8,128)(2,1)S(1)} %copy-done.2, f32[1024,128]{1,0:T(8,128)S(1)} %local_grad_kernel.1.refs_2_), custom_call_target="tpu_custom_call" | custom-call | flops 100000000 | bytes 2080768 | tf_op jit(solution)/shard_map/finish_kernel/pallas_call | solution.py:576
Async XLA Ops:
  3.8 14.9 %all-to-all-start = ((bf16[32,8,128]{2,1,0:T(8,128)(2,1)}), bf16[32,8,128]{2,1,0:T(8,128)(2,1)S(1)}, u32[]{:S(2)}, u32[]{:S(2)}) async-start(bf16[32,8,128]{2,1,0:T(8,128)(2,1)} %bitcast.23), calls=%async_computation | async-start | bytes 131072 | tf_op jit(solution)/shard_map/all_to_all | solution.py:593
  11.2 14.9 %collective-permute-start = (bf16[512,128]{1,0:T(8,128)(2,1)}, bf16[512,128]{1,0:T(8,128)(2,1)}, u32[]{:S(2)}, u32[]{:S(2)}) collective-permute-start(bf16[512,128]{1,0:T(8,128)(2,1)} %get-tuple-element.36), channel_id=1, source_target_pairs={{0,1},{1,2},{2,3},{3,4},{4,5},{5,6},{6,7},{7,8},{8,9},{9,10},{10,1... | collective-permute-start | bytes 393224 | tf_op jit(solution)/shard_map/ppermute | solution.py:598
  14.0 12.0 %collective-permute-start.1 = (bf16[512,128]{1,0:T(8,128)(2,1)}, bf16[512,128]{1,0:T(8,128)(2,1)}, u32[]{:S(2)}, u32[]{:S(2)}) collective-permute-start(bf16[512,128]{1,0:T(8,128)(2,1)} %get-tuple-element.37), channel_id=1, source_target_pairs={{1,0},{2,1},{3,2},{4,3},{5,4},{6,5},{7,6},{8,7},{9,8},{10,9},{11,1... | collective-permute-start | bytes 393224 | tf_op jit(solution)/shard_map/ppermute | solution.py:599
  15.3 3.5 %copy-start.6 = (bf16[128,384]{1,0:T(8,128)(2,1)S(1)}, bf16[128,384]{1,0:T(8,128)(2,1)}, u32[]{:S(2)}) copy-start(bf16[128,384]{1,0:T(8,128)(2,1)} %constant.18.clone.refs_3_) | copy-start | bytes 294916
  15.3 3.5 %copy-start.7 = (bf16[192,256]{1,0:T(8,128)(2,1)S(1)}, bf16[192,256]{1,0:T(8,128)(2,1)}, u32[]{:S(2)}) copy-start(bf16[192,256]{1,0:T(8,128)(2,1)} %constant.17.clone.refs_1_) | copy-start | bytes 294916
  15.3 10.7 %copy-start.3 = (bf16[3,3,3,64,64]{4,3,2,1,0:T(8,128)(2,1)S(1)}, bf16[3,3,3,64,64]{4,3,2,1,0:T(8,128)(2,1)}, u32[]{:S(2)}) copy-start(bf16[3,3,3,64,64]{4,3,2,1,0:T(8,128)(2,1)} %param.15) | copy-start | bytes 663556
  15.3 18.3 %copy-start = (bf16[256,1024]{1,0:T(8,128)(2,1)S(1)}, bf16[256,1024]{1,0:T(8,128)(2,1)}, u32[]{:S(2)}) copy-start(bf16[256,1024]{1,0:T(8,128)(2,1)} %constant.20.clone.refs_2_) | copy-start | bytes 1572868
  15.3 18.3 %copy-start.1 = (bf16[1024,256]{1,0:T(8,128)(2,1)S(1)}, bf16[1024,256]{1,0:T(8,128)(2,1)}, u32[]{:S(2)}) copy-start(bf16[1024,256]{1,0:T(8,128)(2,1)} %constant.19.clone.refs_1_) | copy-start | bytes 1572868
  20.6 13.1 %all-to-all-start.1 = ((bf16[32,8,128]{2,1,0:T(8,128)(2,1)}), bf16[32,8,128]{2,1,0:T(8,128)(2,1)S(1)}, u32[]{:S(2)}, u32[]{:S(2)}) async-start(bf16[32,8,128]{2,1,0:T(8,128)(2,1)} %get-tuple-element.34), calls=%async_computation.1 | async-start | bytes 131072 | tf_op jit(solution)/shard_map/all_to_all | solution.py:593
  26.0 1.0 %copy-start.8 = (bf16[1,64,2,1024]{3,2,1,0:T(2,128)(2,1)S(1)}, bf16[1,64,2,1024]{3,2,1,0:T(2,128)(2,1)}, u32[]{:S(2)}) copy-start(bf16[1,64,2,1024]{3,2,1,0:T(2,128)(2,1)} %param.13) | copy-start | bytes 786436
  27.0 0.9 %copy-start.9 = (bf16[1024,128]{1,0:T(8,128)(2,1)S(1)}, bf16[1024,128]{1,0:T(8,128)(2,1)}, u32[]{:S(2)}) copy-start(bf16[1024,128]{1,0:T(8,128)(2,1)} %get-tuple-element.35.refs_0_) | copy-start | bytes 786436
  37.4 14.8 %all-to-all-start.2 = ((bf16[32,40,128]{2,1,0:T(8,128)(2,1)}), bf16[32,40,128]{2,1,0:T(8,128)(2,1)S(1)}, u32[]{:S(2)}, u32[]{:S(2)}) async-start(bf16[32,40,128]{2,1,0:T(8,128)(2,1)} %get-tuple-element.41), calls=%async_computation.2 | async-start | bytes 655360 | tf_op jit(solution)/shard_map/all_to_all | solution.py:593
  40.5 5.7 %collective-permute-start.2 = (bf16[512,128]{1,0:T(8,128)(2,1)}, bf16[512,128]{1,0:T(8,128)(2,1)S(1)}, u32[]{:S(2)}, u32[]{:S(2)}) collective-permute-start(bf16[512,128]{1,0:T(8,128)(2,1)} %get-tuple-element.42), channel_id=1, source_target_pairs={{0,1},{1,2},{2,3},{3,4},{4,5},{5,6},{6,7},{7,8},{8,9},{9,10},{10,1... | collective-permute-start | bytes 393224 | tf_op jit(solution)/shard_map/ppermute | solution.py:598
  42.7 4.6 %collective-permute-start.3 = (bf16[512,128]{1,0:T(8,128)(2,1)}, bf16[512,128]{1,0:T(8,128)(2,1)S(1)}, u32[]{:S(2)}, u32[]{:S(2)}) collective-permute-start(bf16[512,128]{1,0:T(8,128)(2,1)} %get-tuple-element.43), channel_id=1, source_target_pairs={{1,0},{2,1},{3,2},{4,3},{5,4},{6,5},{7,6},{8,7},{9,8},{10,9},{11,1... | collective-permute-start | bytes 393224 | tf_op jit(solution)/shard_map/ppermute | solution.py:599
  44.0 8.3 %copy-start.4 = (bf16[128,384]{1,0:T(8,128)(2,1)S(1)}, bf16[128,384]{1,0:T(8,128)(2,1)}, u32[]{:S(2)}) copy-start(bf16[128,384]{1,0:T(8,128)(2,1)} %constant.22.clone.refs_3_) | copy-start | bytes 294916
  44.0 8.2 %copy-start.5 = (bf16[192,256]{1,0:T(8,128)(2,1)S(1)}, bf16[192,256]{1,0:T(8,128)(2,1)}, u32[]{:S(2)}) copy-start(bf16[192,256]{1,0:T(8,128)(2,1)} %constant.21.clone.refs_1_) | copy-start | bytes 294916
  54.1 15.4 %all-to-all-start.3 = ((bf16[32,40,128]{2,1,0:T(8,128)(2,1)}), bf16[32,40,128]{2,1,0:T(8,128)(2,1)S(1)}, u32[]{:S(2)}, u32[]{:S(2)}) async-start(bf16[32,40,128]{2,1,0:T(8,128)(2,1)} %get-tuple-element.50), calls=%async_computation.3 | async-start | bytes 655360 | tf_op jit(solution)/shard_map/all_to_all | solution.py:593
  61.5 8.0 %copy-start.2 = (bf16[1024,256]{1,0:T(8,128)(2,1)S(1)}, bf16[1024,256]{1,0:T(8,128)(2,1)}, u32[]{:S(2)}) copy-start(bf16[1024,256]{1,0:T(8,128)(2,1)} %constant.23.clone.refs_1_) | copy-start | bytes 1572868

commit v14 on v13

--- a/solution.py
+++ b/solution.py
@@ -207,11 +207,10 @@
 
 def analyse_kernel(field, analysis, *refs):
     weights = refs[:CHUNKS]
-    cells_out, coef_out, first_out, last_out, packed_out, _, buffer, semaphores = refs[CHUNKS:]
+    coef_out, first_out, last_out, packed_out, _, buffer, semaphores = refs[CHUNKS:]
     cells = to_cells(field[...])
     rounded = cells.astype(BF16)
     coef_out[...] = dot(analysis[...], rounded).astype(BF16)
-    cells_out[...] = rounded
     first, last = edge_layers(cells)
     first_out[...] = first
     last_out[...] = last
@@ -233,17 +232,18 @@
 
 
 def local_kernel(
-    cells, before, after, cotangent, weights, local_out, lanes_out, cotangent_out, padded, table
+    first, last, before, after, cotangent, weights, local_out, lanes_out, cotangent_out, padded, table
 ):
     banded_forward(weights, table)
     beside = beside_layers(before[...], after[...])
-    pad_cells(padded, cells[...], beside)
+    own = beside_layers(first[...], last[...])
+    pad_cells(padded, own, beside)
 
     def store(start, result):
         local_out[start : start + STEP, :] = result
 
     stencil(padded, table, False, store)
-    whole = jnp.concatenate([cells[...].astype(F32), beside.astype(F32)], axis=1)
+    whole = jnp.concatenate([own.astype(F32), beside.astype(F32)], axis=1)
     lanes_out[...] = whole.T.astype(BF16)
     cotangent_out[...] = to_cells(cotangent[...]).astype(BF16)
 
@@ -322,7 +322,6 @@
     cotangent,
     lanes,
     activated_out,
-    grad_out,
     first_out,
     last_out,
     back_out,
@@ -335,7 +334,6 @@
     activated_out[...] = (pre * cdf).astype(BF16)
     grad = (cotangent[...].astype(F32) * (cdf + pre * density)).astype(BF16)
     back = dot(synthesis_rows[...], grad)
-    rounded = grad
     grad = grad.astype(F32)
     first, last = edge_layers(grad)
     spread[0:NY, :] = jnp.zeros((NY, 3 * LANES), BF16)
@@ -368,7 +366,6 @@
     else:
         back_out[...] = back.astype(BF16)
         terms_out[...] = terms.astype(BF16)
-    grad_out[...] = rounded
     first_out[...] = first
     last_out[...] = last
 
@@ -437,9 +434,10 @@
     out[...] = to_field(cells[...])
 
 
-def local_grad_kernel(grad, before, after, weights, out, padded, table):
+def local_grad_kernel(first, last, before, after, weights, out, padded, table):
     banded_backward(weights, table)
-    pad_cells(padded, grad[...], beside_layers(before[...], after[...]))
+    own = beside_layers(first[...], last[...])
+    pad_cells(padded, own, beside_layers(before[...], after[...]))
 
     def store(start, result):
         out[start : start + STEP, :] = result
@@ -628,10 +626,9 @@
     packed = shape((weights.shape[0] // 2, LANES), BF16)
     share = weights.shape[0] // CHUNKS
     to_send = shape((devices, modes, LANES), BF16) if modes % 8 == 0 else plane_modes
-    cells, coef, first, last, kept_weights, slot = run(
+    coef, first, last, kept_weights, slot = run(
         analyse_kernel,
         [
-            wide,
             plane_modes,
             edge,
             edge,
@@ -642,8 +639,8 @@
         analysis,
         *[weights] * CHUNKS,
         staged={0: None, 1: None} | {2 + k: slice(k * share, (k + 1) * share) for k in range(CHUNKS)},
-        sent=(0, 1, 2, 3),
-        plain=(4, 5),
+        sent=(0, 1, 2),
+        plain=(3, 4),
         scratch=[pltpu.VMEM(packed.shape, BF16), pltpu.SemaphoreType.DMA((CHUNKS,))],
         limit=WHOLE_VMEM,
         flops=10**8,
@@ -654,7 +651,8 @@
     local, lanes, outer_cells = run(
         local_kernel,
         [shape((CELLS, LANES), F32), shape((HBM_BYTES // (2 * CELLS), CELLS), BF16), wide],
-        cells,
+        first,
+        last,
         before,
         after,
         cotangent.reshape(field.shape),
@@ -676,11 +674,10 @@
     )
     back = send(back)
     slab = shape((devices, 8 + TERM_ROWS // devices, LANES), BF16)
-    activated, grad, first, last, back, terms = run(
+    activated, first, last, back, terms = run(
         functools.partial(activate_kernel, in_slab),
         [
             wide,
-            shape((HBM_BYTES // (2 * LANES), LANES), BF16),
             edge,
             edge,
             slab if in_slab else plane_modes,
@@ -693,7 +690,7 @@
         outer_cells,
         lanes,
         staged={5: 2 * LANES},
-        sent={1: CELLS, 2: None, 3: None, 4: None},
+        sent=(1, 2, 3),
         scratch=[pltpu.VMEM((CELLS + 2 * NY, 3 * LANES), BF16)],
         flops=10**9,
     )
@@ -738,11 +735,11 @@
     (local,) = run(
         local_grad_kernel,
         [shape((CELLS, LANES), F32)],
-        grad,
+        first,
+        last,
         before,
         after,
         taps,
-        staged={0: CELLS},
         scratch=[padded, pltpu.VMEM((3, 3 * LANES, 2 * LANES), BF16)],
         flops=7 * 10**8,
     )

time: 71.6 us -> 72.9 us (1.018)
  waiting for transfers between devices: 16.6 us -> 13.6 us
  starting transfers between devices: 27.1 us -> 29.4 us
  local copies, waits for them, and re-layouts: 1.95 us -> 4.09 us
    all_to_all x4, waiting for transfers between devices: 15.5 us -> 13.2 us  [exchange(): lax.all_to_all(values, ('space', 'batch'), split_axis=0, concat_axis=0, t...]
    unnamed x20 -> x30, local copies, waits for them, and re-layouts: 1.95 us -> 4.09 us
    all_to_all x4, starting transfers between devices: 19.5 us -> 21 us  [exchange(): lax.all_to_all(values, ('space', 'batch'), split_axis=0, concat_axis=0, t...]
    ppermute x2, starting transfers between devices: 4.98 us -> 5.86 us  [neighbours(): before = lax.ppermute(last, 'space', [(i, i + 1) for i in range(ends)])]
where the time goes in v14:
time: 72.9 us; the launch traced here: 72.3 us
  starting transfers between devices  29.4 us (40%)
  Pallas kernels  24.4 us (33%)
  waiting for transfers between devices  13.6 us (19%)
  local copies, waits for them, and re-layouts  4.09 us (6%)
  between operations  0.85 us (1%)
    pallas_call x10, Pallas kernels, run(): pl.pallas_call(kernel, out_shape=results, in_specs=[in_hbm if k in staged...  24.4 us
    all_to_all x4, starting transfers between devices, exchange(): lax.all_to_all(values, ('space', 'batch'), split_axis=0, concat_axis=0, t...  21 us
    all_to_all x4, waiting for transfers between devices, exchange(): lax.all_to_all(values, ('space', 'batch'), split_axis=0, concat_axis=0, t...  13.2 us
    ppermute x2, starting transfers between devices, neighbours(): before = lax.ppermute(last, 'space', [(i, i + 1) for i in range(ends)])  5.86 us
    unnamed x30, local copies, waits for them, and re-layouts  4.09 us
    ppermute x2, starting transfers between devices, neighbours(): after = lax.ppermute(first, 'space', [(i + 1, i) for i in range(ends)])  2.58 us
  transfers between devices with their start and end apart: 8, of which 5 were waited for; matrix products, arithmetic and copies ran while one was open for 0% of the time, Pallas kernels for 20%

profile of v14, /device:TPU:0, one launch (start us, length us, event | category | flops | bytes accessed | tf_op | source)
XLA Modules:
  0.0 72.3 jit_solution(12745852321110375710)
XLA Ops:
  0.6 3.2 %analyse_kernel.1 = (bf16[256,128]{1,0:T(8,128)(2,1)}, bf16[512,128]{1,0:T(8,128)(2,1)}, bf16[512,128]{1,0:T(8,128)(2,1)}, bf16[102400,128]{1,0:T(8,128)(2,1)}, bf16[32,8,128]{2,1,0:T(8,128)(2,1)}) custom-call(bf16[64,2,1024]{2,1,0:T(2,128)(2,1)} %bitcast.22, bf16[256,1024]{1,0:T(8,128)(2,1)} %constant.16.clone.refs_1_, bf16[12288,64]{1,0:T(8,128)(2,1)} %bitcast.18, ...), custom_call_target="tpu_custom_call" | custom-call | flops 100000000 | bytes 32112640 | tf_op jit(solution)/shard_map/analyse_kernel/pallas_call | solution.py:574
  3.8 7.3 %all-to-all-start = ((bf16[32,8,128]{2,1,0:T(8,128)(2,1)}), bf16[32,8,128]{2,1,0:T(8,128)(2,1)S(1)}, u32[]{:S(2)}, u32[]{:S(2)}) async-start(bf16[32,8,128]{2,1,0:T(8,128)(2,1)} %bitcast.23), calls=%async_computation | async-start | bytes 131072 | tf_op jit(solution)/shard_map/all_to_all | solution.py:591
  11.2 1.3 %collective-permute-start.1 = (bf16[512,128]{1,0:T(8,128)(2,1)}, bf16[512,128]{1,0:T(8,128)(2,1)}, u32[]{:S(2)}, u32[]{:S(2)}) collective-permute-start(bf16[512,128]{1,0:T(8,128)(2,1)} %get-tuple-element.33.refs_0_), channel_id=1, source_target_pairs={{1,0},{2,1},{3,2},{4,3},{5,4},{6,5},{7,6},{8,7},{9,8},{10,9},{11,1... | collective-permute-start | bytes 393224 | tf_op jit(solution)/shard_map/ppermute | solution.py:597
  12.5 3.7 %collective-permute-start = (bf16[512,128]{1,0:T(8,128)(2,1)}, bf16[512,128]{1,0:T(8,128)(2,1)}, u32[]{:S(2)}, u32[]{:S(2)}) collective-permute-start(bf16[512,128]{1,0:T(8,128)(2,1)} %get-tuple-element.34.refs_1_), channel_id=1, source_target_pairs={{0,1},{1,2},{2,3},{3,4},{4,5},{5,6},{6,7},{7,8},{8,9},{9,10},{10,1... | collective-permute-start | bytes 393224 | tf_op jit(solution)/shard_map/ppermute | solution.py:596
  16.2 0.0 copy-start.5
  16.2 0.0 copy-start.6
  16.2 0.0 copy-start.7
  16.2 0.0 copy-start
  16.2 0.0 copy-start.1
  16.2 1.5 %fetch_kernel.1.refs_2_ = bf16[6144,128]{1,0:T(8,128)(2,1)S(1)} custom-call(bf16[102400,128]{1,0:T(8,128)(2,1)} %get-tuple-element.30.refs_0_.refs_1_), custom_call_target="tpu_custom_call" | custom-call | bytes 27787264 | tf_op jit(solution)/shard_map/fetch_kernel/pallas_call | solution.py:574
  17.7 1.0 %all-to-all-done = bf16[32,8,128]{2,1,0:T(8,128)(2,1)S(1)} async-done(((bf16[32,8,128]{2,1,0:T(8,128)(2,1)}), bf16[32,8,128]{2,1,0:T(8,128)(2,1)S(1)}, u32[]{:S(2)}, u32[]{:S(2)}) %all-to-all-start) | async-done | bytes 65568 | tf_op jit(solution)/shard_map/all_to_all | solution.py:591
  18.8 0.0 copy-done.5
  18.8 0.0 copy-done.6
  18.8 1.8 %mix_kernel.1 = (bf16[32,8,128]{2,1,0:T(8,128)(2,1)}, bf16[384,256]{1,0:T(8,128)(2,1)S(1)}) custom-call(bf16[256,128]{1,0:T(8,128)(2,1)S(1)} %bitcast.14, bf16[192,256]{1,0:T(8,128)(2,1)S(1)} %copy-done.6, bf16[6144,128]{1,0:T(8,128)(2,1)S(1)} %fetch_kernel.1.refs_2_, bf16[128,384]{1,0:T(8,128)(2,1)S(1)} %copy-done.5, ...), custom_call_target="tpu_custom_call", output_to_operand_aliasing={{0}: (4, {})} | custom-call | flops 400000000 | bytes 2097152 | tf_op jit(solution)/shard_map/mix_kernel/pallas_call | solution.py:574
  20.6 5.1 %all-to-all-start.1 = ((bf16[32,8,128]{2,1,0:T(8,128)(2,1)}), bf16[32,8,128]{2,1,0:T(8,128)(2,1)S(1)}, u32[]{:S(2)}, u32[]{:S(2)}) async-start(bf16[32,8,128]{2,1,0:T(8,128)(2,1)} %get-tuple-element.32), calls=%async_computation.1 | async-start | bytes 131072 | tf_op jit(solution)/shard_map/all_to_all | solution.py:591
  25.7 0.0 collective-permute-done.1.refs_3_
  25.7 0.0 collective-permute-done.refs_2_
  25.7 0.0 copy-done.7
  25.7 0.0 copy-start.8
  25.8 0.9 %copy-done.8 = bf16[1,64,2,1024]{3,2,1,0:T(2,128)(2,1)S(1)} copy-done((bf16[1,64,2,1024]{3,2,1,0:T(2,128)(2,1)S(1)}, bf16[1,64,2,1024]{3,2,1,0:T(2,128)(2,1)}, u32[]{:S(2)}) %copy-start.8) | copy-done | bytes 262168
  26.7 0.0 copy-start.9
  26.7 0.9 %copy-done.9 = bf16[512,128]{1,0:T(8,128)(2,1)S(1)} copy-done((bf16[512,128]{1,0:T(8,128)(2,1)S(1)}, bf16[512,128]{1,0:T(8,128)(2,1)}, u32[]{:S(2)}) %copy-start.9) | copy-done | bytes 131096
  27.6 0.0 copy-start.10
  27.6 0.9 %copy-done.10 = bf16[512,128]{1,0:T(8,128)(2,1)S(1)} copy-done((bf16[512,128]{1,0:T(8,128)(2,1)S(1)}, bf16[512,128]{1,0:T(8,128)(2,1)}, u32[]{:S(2)}) %copy-start.10) | copy-done | bytes 131096
  28.5 2.9 %local_kernel.1 = (f32[1024,128]{1,0:T(8,128)S(1)}, bf16[12800,1024]{1,0:T(8,128)(2,1)}, bf16[1024,128]{1,0:T(8,128)(2,1)S(1)}) custom-call(bf16[512,128]{1,0:T(8,128)(2,1)S(1)} %copy-done.9, bf16[512,128]{1,0:T(8,128)(2,1)S(1)} %copy-done.10, bf16[512,128]{1,0:T(8,128)(2,1)} %collective-permute-done.refs_2_, ...), custom_call_target="tpu_custom_call" | custom-call | flops 700000000 | bytes 28008448 | tf_op jit(solution)/shard_map/local_kernel/pallas_call | solution.py:574
  31.4 1.9 %all-to-all-done.1 = bf16[32,8,128]{2,1,0:T(8,128)(2,1)S(1)} async-done(((bf16[32,8,128]{2,1,0:T(8,128)(2,1)}), bf16[32,8,128]{2,1,0:T(8,128)(2,1)S(1)}, u32[]{:S(2)}, u32[]{:S(2)}) %all-to-all-start.1) | async-done | bytes 65568 | tf_op jit(solution)/shard_map/all_to_all | solution.py:591
  33.3 0.0 copy-done
  33.3 0.0 copy-done.1
  33.3 3.7 %activate_kernel.1 = (bf16[1024,128]{1,0:T(8,128)(2,1)S(1)}, bf16[512,128]{1,0:T(8,128)(2,1)}, bf16[512,128]{1,0:T(8,128)(2,1)}, bf16[32,40,128]{2,1,0:T(8,128)(2,1)}) custom-call(bf16[256,128]{1,0:T(8,128)(2,1)S(1)} %bitcast.13, bf16[1024,256]{1,0:T(8,128)(2,1)S(1)} %copy-done.1, bf16[256,1024]{1,0:T(8,128)(2,1)S(1)} %copy-done, ...), custom_call_target="tpu_custom_call" | custom-call | flops 1000000000 | bytes 28966912 | tf_op jit(solution)/shard_map/activate_kernel/pallas_call | solution.py:574
  37.0 4.0 %all-to-all-start.2 = ((bf16[32,40,128]{2,1,0:T(8,128)(2,1)}), bf16[32,40,128]{2,1,0:T(8,128)(2,1)S(1)}, u32[]{:S(2)}, u32[]{:S(2)}) async-start(bf16[32,40,128]{2,1,0:T(8,128)(2,1)} %get-tuple-element.38), calls=%async_computation.2 | async-start | bytes 655360 | tf_op jit(solution)/shard_map/all_to_all | solution.py:591
  41.0 2.2 %collective-permute-start.2 = (bf16[512,128]{1,0:T(8,128)(2,1)}, bf16[512,128]{1,0:T(8,128)(2,1)S(1)}, u32[]{:S(2)}, u32[]{:S(2)}) collective-permute-start(bf16[512,128]{1,0:T(8,128)(2,1)} %get-tuple-element.39.refs_1_), channel_id=1, source_target_pairs={{0,1},{1,2},{2,3},{3,4},{4,5},{5,6},{6,7},{7,8},{8,9},{9,10},{10,1... | collective-permute-start | bytes 393224 | tf_op jit(solution)/shard_map/ppermute | solution.py:596
  43.2 1.3 %collective-permute-start.3 = (bf16[512,128]{1,0:T(8,128)(2,1)}, bf16[512,128]{1,0:T(8,128)(2,1)S(1)}, u32[]{:S(2)}, u32[]{:S(2)}) collective-permute-start(bf16[512,128]{1,0:T(8,128)(2,1)} %get-tuple-element.40.refs_0_), channel_id=1, source_target_pairs={{1,0},{2,1},{3,2},{4,3},{5,4},{6,5},{7,6},{8,7},{9,8},{10,9},{11,1... | collective-permute-start | bytes 393224 | tf_op jit(solution)/shard_map/ppermute | solution.py:597
  44.5 0.0 copy-start.3
  44.5 0.0 copy-start.4
  44.5 2.2 %output_kernel.1 = (bf16[64,2,1024]{2,1,0:T(2,128)(2,1)}, bf16[6144,128]{1,0:T(8,128)(2,1)S(1)}) custom-call(bf16[1024,128]{1,0:T(8,128)(2,1)S(1)} %get-tuple-element.41.refs_0_, bf16[102400,128]{1,0:T(8,128)(2,1)} %get-tuple-element.30.refs_0_.refs_1_), custom_call_target="tpu_custom_call" | custom-call | flops 100000000 | bytes 28311552 | tf_op jit(solution)/shard_map/output_kernel/pallas_call | solution.py:574
  46.7 0.0 copy-start.2
  46.7 0.0 collective-permute-done.2.refs_2_
  46.7 0.0 copy-start.11
  46.7 0.6 copy-done.11
  47.4 0.4 collective-permute-done.3.refs_3_
  47.8 0.0 copy-start.13
  47.8 0.6 copy-done.13
  48.4 0.0 copy-start.12
  48.4 4.3 %all-to-all-done.2.refs_0_ = bf16[32,40,128]{2,1,0:T(8,128)(2,1)S(1)} async-done(((bf16[32,40,128]{2,1,0:T(8,128)(2,1)}), bf16[32,40,128]{2,1,0:T(8,128)(2,1)S(1)}, u32[]{:S(2)}, u32[]{:S(2)}) %all-to-all-start.2) | async-done | bytes 327712 | tf_op jit(solution)/shard_map/all_to_all | solution.py:591
  52.7 0.0 copy-done.3
  52.7 0.0 copy-done.4
  52.7 1.8 %unmix_kernel.1 = (bf16[32,40,128]{2,1,0:T(8,128)(2,1)}, bf16[384,128]{1,0:T(8,128)(2,1)S(1)}) custom-call(bf16[32,40,128]{2,1,0:T(8,128)(2,1)S(1)} %all-to-all-done.2.refs_0_, bf16[192,256]{1,0:T(8,128)(2,1)S(1)} %copy-done.4, bf16[6144,128]{1,0:T(8,128)(2,1)S(1)} %get-tuple-element.46.refs_2_, bf16[128,384]{1,0:T(8,128)(2,1)S(1)} %copy-done.3), custom_call_target="tpu_custom_call" | custom-call | flops 400000000 | bytes 2523136 | tf_op jit(solution)/shard_map/unmix_kernel/pallas_call | solution.py:574
  54.5 0.0 copy-start.14
  54.6 4.6 %all-to-all-start.3 = ((bf16[32,40,128]{2,1,0:T(8,128)(2,1)}), bf16[32,40,128]{2,1,0:T(8,128)(2,1)S(1)}, u32[]{:S(2)}, u32[]{:S(2)}) async-start(bf16[32,40,128]{2,1,0:T(8,128)(2,1)} %get-tuple-element.47), calls=%async_computation.3 | async-start | bytes 655360 | tf_op jit(solution)/shard_map/all_to_all | solution.py:591
  59.1 3.7 %weight_kernel.1 = f32[12288,64]{1,0:T(8,128)} custom-call(bf16[384,256]{1,0:T(8,128)(2,1)S(1)} %get-tuple-element.51.refs_0_, bf16[384,128]{1,0:T(8,128)(2,1)S(1)} %get-tuple-element.52.refs_1_), custom_call_target="tpu_custom_call" | custom-call | flops 400000000 | bytes 3440640 | tf_op jit(solution)/shard_map/weight_kernel/pallas_call | solution.py:574
  62.9 0.0 copy-done.12
  62.9 0.0 copy-done.14
  62.9 2.1 %local_grad_kernel.1.refs_2_ = f32[1024,128]{1,0:T(8,128)S(1)} custom-call(bf16[512,128]{1,0:T(8,128)(2,1)} %get-tuple-element.40.refs_0_, bf16[512,128]{1,0:T(8,128)(2,1)} %get-tuple-element.39.refs_1_, bf16[512,128]{1,0:T(8,128)(2,1)S(1)} %copy-done.12, bf16[512,128]{1,0:T(8,128)(2,1)S(1)} %copy-done.14, bf16[27,64,64]{2,1,0:T(8,128)(2,1)S(1)} %bitcast.16), custom_call_target="tpu_custom_call" | custom-call | flops 700000000 | bytes 1269760 | tf_op jit(solution)/shard_map/local_grad_kernel/pallas_call | solution.py:574
  64.9 5.9 %all-to-all-done.3.refs_0_ = bf16[32,40,128]{2,1,0:T(8,128)(2,1)S(1)} async-done(((bf16[32,40,128]{2,1,0:T(8,128)(2,1)}), bf16[32,40,128]{2,1,0:T(8,128)(2,1)S(1)}, u32[]{:S(2)}, u32[]{:S(2)}) %all-to-all-start.3) | async-done | bytes 327712 | tf_op jit(solution)/shard_map/all_to_all | solution.py:591
  70.9 0.0 copy-done.2
  70.9 1.5 %finish_kernel.1 = (bf16[64,2,1024]{2,1,0:T(2,128)(2,1)}, f32[27,64,64]{2,1,0:T(8,128)}) custom-call(bf16[32,40,128]{2,1,0:T(8,128)(2,1)S(1)} %all-to-all-done.3.refs_0_, bf16[1024,256]{1,0:T(8,128)(2,1)S(1)} %copy-done.2, f32[1024,128]{1,0:T(8,128)S(1)} %local_grad_kernel.1.refs_2_), custom_call_target="tpu_custom_call" | custom-call | flops 100000000 | bytes 2080768 | tf_op jit(solution)/shard_map/finish_kernel/pallas_call | solution.py:574
Async XLA Ops:
  3.8 14.9 %all-to-all-start = ((bf16[32,8,128]{2,1,0:T(8,128)(2,1)}), bf16[32,8,128]{2,1,0:T(8,128)(2,1)S(1)}, u32[]{:S(2)}, u32[]{:S(2)}) async-start(bf16[32,8,128]{2,1,0:T(8,128)(2,1)} %bitcast.23), calls=%async_computation | async-start | bytes 131072 | tf_op jit(solution)/shard_map/all_to_all | solution.py:591
  11.2 14.6 %collective-permute-start.1 = (bf16[512,128]{1,0:T(8,128)(2,1)}, bf16[512,128]{1,0:T(8,128)(2,1)}, u32[]{:S(2)}, u32[]{:S(2)}) collective-permute-start(bf16[512,128]{1,0:T(8,128)(2,1)} %get-tuple-element.33.refs_0_), channel_id=1, source_target_pairs={{1,0},{2,1},{3,2},{4,3},{5,4},{6,5},{7,6},{8,7},{9,8},{10,9},{11,1... | collective-permute-start | bytes 393224 | tf_op jit(solution)/shard_map/ppermute | solution.py:597
  12.5 13.3 %collective-permute-start = (bf16[512,128]{1,0:T(8,128)(2,1)}, bf16[512,128]{1,0:T(8,128)(2,1)}, u32[]{:S(2)}, u32[]{:S(2)}) collective-permute-start(bf16[512,128]{1,0:T(8,128)(2,1)} %get-tuple-element.34.refs_1_), channel_id=1, source_target_pairs={{0,1},{1,2},{2,3},{3,4},{4,5},{5,6},{6,7},{7,8},{8,9},{9,10},{10,1... | collective-permute-start | bytes 393224 | tf_op jit(solution)/shard_map/ppermute | solution.py:596
  16.2 2.6 %copy-start.5 = (bf16[128,384]{1,0:T(8,128)(2,1)S(1)}, bf16[128,384]{1,0:T(8,128)(2,1)}, u32[]{:S(2)}) copy-start(bf16[128,384]{1,0:T(8,128)(2,1)} %constant.18.clone.refs_3_) | copy-start | bytes 294916
  16.2 2.6 %copy-start.6 = (bf16[192,256]{1,0:T(8,128)(2,1)S(1)}, bf16[192,256]{1,0:T(8,128)(2,1)}, u32[]{:S(2)}) copy-start(bf16[192,256]{1,0:T(8,128)(2,1)} %constant.17.clone.refs_1_) | copy-start | bytes 294916
  16.2 9.6 %copy-start.7 = (bf16[3,3,3,64,64]{4,3,2,1,0:T(8,128)(2,1)S(1)}, bf16[3,3,3,64,64]{4,3,2,1,0:T(8,128)(2,1)}, u32[]{:S(2)}) copy-start(bf16[3,3,3,64,64]{4,3,2,1,0:T(8,128)(2,1)} %param.15) | copy-start | bytes 663556
  16.2 17.2 %copy-start = (bf16[256,1024]{1,0:T(8,128)(2,1)S(1)}, bf16[256,1024]{1,0:T(8,128)(2,1)}, u32[]{:S(2)}) copy-start(bf16[256,1024]{1,0:T(8,128)(2,1)} %constant.20.clone.refs_2_) | copy-start | bytes 1572868
  16.2 17.2 %copy-start.1 = (bf16[1024,256]{1,0:T(8,128)(2,1)S(1)}, bf16[1024,256]{1,0:T(8,128)(2,1)}, u32[]{:S(2)}) copy-start(bf16[1024,256]{1,0:T(8,128)(2,1)} %constant.19.clone.refs_1_) | copy-start | bytes 1572868
  20.6 12.8 %all-to-all-start.1 = ((bf16[32,8,128]{2,1,0:T(8,128)(2,1)}), bf16[32,8,128]{2,1,0:T(8,128)(2,1)S(1)}, u32[]{:S(2)}, u32[]{:S(2)}) async-start(bf16[32,8,128]{2,1,0:T(8,128)(2,1)} %get-tuple-element.32), calls=%async_computation.1 | async-start | bytes 131072 | tf_op jit(solution)/shard_map/all_to_all | solution.py:591
  25.7 1.0 %copy-start.8 = (bf16[1,64,2,1024]{3,2,1,0:T(2,128)(2,1)S(1)}, bf16[1,64,2,1024]{3,2,1,0:T(2,128)(2,1)}, u32[]{:S(2)}) copy-start(bf16[1,64,2,1024]{3,2,1,0:T(2,128)(2,1)} %param.13) | copy-start | bytes 786436
  26.7 0.9 %copy-start.9 = (bf16[512,128]{1,0:T(8,128)(2,1)S(1)}, bf16[512,128]{1,0:T(8,128)(2,1)}, u32[]{:S(2)}) copy-start(bf16[512,128]{1,0:T(8,128)(2,1)} %get-tuple-element.33.refs_0_) | copy-start | bytes 393220
  27.6 0.9 %copy-start.10 = (bf16[512,128]{1,0:T(8,128)(2,1)S(1)}, bf16[512,128]{1,0:T(8,128)(2,1)}, u32[]{:S(2)}) copy-start(bf16[512,128]{1,0:T(8,128)(2,1)} %get-tuple-element.34.refs_1_) | copy-start | bytes 393220
  37.0 15.7 %all-to-all-start.2 = ((bf16[32,40,128]{2,1,0:T(8,128)(2,1)}), bf16[32,40,128]{2,1,0:T(8,128)(2,1)S(1)}, u32[]{:S(2)}, u32[]{:S(2)}) async-start(bf16[32,40,128]{2,1,0:T(8,128)(2,1)} %get-tuple-element.38), calls=%async_computation.2 | async-start | bytes 655360 | tf_op jit(solution)/shard_map/all_to_all | solution.py:591
  41.0 5.7 %collective-permute-start.2 = (bf16[512,128]{1,0:T(8,128)(2,1)}, bf16[512,128]{1,0:T(8,128)(2,1)S(1)}, u32[]{:S(2)}, u32[]{:S(2)}) collective-permute-start(bf16[512,128]{1,0:T(8,128)(2,1)} %get-tuple-element.39.refs_1_), channel_id=1, source_target_pairs={{0,1},{1,2},{2,3},{3,4},{4,5},{5,6},{6,7},{7,8},{8,9},{9,10},{10,1... | collective-permute-start | bytes 393224 | tf_op jit(solution)/shard_map/ppermute | solution.py:596
  43.2 4.6 %collective-permute-start.3 = (bf16[512,128]{1,0:T(8,128)(2,1)}, bf16[512,128]{1,0:T(8,128)(2,1)S(1)}, u32[]{:S(2)}, u32[]{:S(2)}) collective-permute-start(bf16[512,128]{1,0:T(8,128)(2,1)} %get-tuple-element.40.refs_0_), channel_id=1, source_target_pairs={{1,0},{2,1},{3,2},{4,3},{5,4},{6,5},{7,6},{8,7},{9,8},{10,9},{11,1... | collective-permute-start | bytes 393224 | tf_op jit(solution)/shard_map/ppermute | solution.py:597
  44.5 8.3 %copy-start.3 = (bf16[128,384]{1,0:T(8,128)(2,1)S(1)}, bf16[128,384]{1,0:T(8,128)(2,1)}, u32[]{:S(2)}) copy-start(bf16[128,384]{1,0:T(8,128)(2,1)} %constant.22.clone.refs_3_) | copy-start | bytes 294916
  44.5 8.2 %copy-start.4 = (bf16[192,256]{1,0:T(8,128)(2,1)S(1)}, bf16[192,256]{1,0:T(8,128)(2,1)}, u32[]{:S(2)}) copy-start(bf16[192,256]{1,0:T(8,128)(2,1)} %constant.21.clone.refs_1_) | copy-start | bytes 294916
  46.7 24.1 %copy-start.2 = (bf16[1024,256]{1,0:T(8,128)(2,1)S(1)}, bf16[1024,256]{1,0:T(8,128)(2,1)}, u32[]{:S(2)}) copy-start(bf16[1024,256]{1,0:T(8,128)(2,1)} %constant.23.clone.refs_1_) | copy-start | bytes 1572868
  46.7 0.7 copy-start.11
  47.8 0.6 copy-start.13
  48.4 14.5 %copy-start.12 = (bf16[512,128]{1,0:T(8,128)(2,1)S(1)}, bf16[512,128]{1,0:T(8,128)(2,1)}, u32[]{:S(2)}) copy-start(bf16[512,128]{1,0:T(8,128)(2,1)} %copy-done.11) | copy-start | bytes 393220
  54.5 8.3 %copy-start.14 = (bf16[512,128]{1,0:T(8,128)(2,1)S(1)}, bf16[512,128]{1,0:T(8,128)(2,1)}, u32[]{:S(2)}) copy-start(bf16[512,128]{1,0:T(8,128)(2,1)} %copy-done.13) | copy-start | bytes 393220
  54.6 16.3 %all-to-all-start.3 = ((bf16[32,40,128]{2,1,0:T(8,128)(2,1)}), bf16[32,40,128]{2,1,0:T(8,128)(2,1)S(1)}, u32[]{:S(2)}, u32[]{:S(2)}) async-start(bf16[32,40,128]{2,1,0:T(8,128)(2,1)} %get-tuple-element.47), calls=%async_computation.3 | async-start | bytes 655360 | tf_op jit(solution)/shard_map/all_to_all | solution.py:591

commit v15 on v13

--- a/solution.py
+++ b/solution.py
@@ -317,7 +317,6 @@
     terms_in_slab,
     received,
     synthesis,
-    synthesis_rows,
     local,
     cotangent,
     lanes,
@@ -334,7 +333,7 @@
     density = jnp.exp(-0.5 * pre * pre) * inv_root_two_pi
     activated_out[...] = (pre * cdf).astype(BF16)
     grad = (cotangent[...].astype(F32) * (cdf + pre * density)).astype(BF16)
-    back = dot(synthesis_rows[...], grad)
+    back = dot(synthesis[...], grad, (0, 0))
     rounded = grad
     grad = grad.astype(F32)
     first, last = edge_layers(grad)
@@ -653,13 +652,12 @@
     before, after = neighbours(first, last)
     local, lanes, outer_cells = run(
         local_kernel,
-        [shape((CELLS, LANES), F32), shape((HBM_BYTES // (2 * CELLS), CELLS), BF16), wide],
+        [shape((CELLS, LANES), F32), shape((2 * LANES, CELLS), BF16), wide],
         cells,
         before,
         after,
         cotangent.reshape(field.shape),
         taps,
-        sent={1: 2 * LANES},
         scratch=[padded, pltpu.VMEM((3, 2 * LANES, 3 * LANES), BF16)],
         flops=7 * 10**8,
     )
@@ -688,11 +686,9 @@
         ],
         back,
         np.ascontiguousarray(synthesis.T),
-        synthesis,
         local,
         outer_cells,
         lanes,
-        staged={5: 2 * LANES},
         sent={1: CELLS, 2: None, 3: None, 4: None},
         scratch=[pltpu.VMEM((CELLS + 2 * NY, 3 * LANES), BF16)],
         flops=10**9,

time: 71.6 us -> 70.7 us (0.987)
  waiting for transfers between devices: 16.6 us -> 21 us
  Pallas kernels: 24.5 us -> 21.6 us
  starting transfers between devices: 27.1 us -> 25.6 us
  local copies, waits for them, and re-layouts: 1.95 us -> 1.09 us
    all_to_all x4, waiting for transfers between devices: 15.5 us -> 20.1 us  [exchange(): lax.all_to_all(values, ('space', 'batch'), split_axis=0, concat_axis=0, t...]
    pallas_call x10, Pallas kernels: 24.5 us -> 21.6 us  [run(): pl.pallas_call(kernel, out_shape=results, in_specs=[in_hbm if k in staged...]
    unnamed x20 -> x18, local copies, waits for them, and re-layouts: 1.95 us -> 1.09 us
    ppermute x2, starting transfers between devices: 4.98 us -> 4.19 us  [neighbours(): before = lax.ppermute(last, 'space', [(i, i + 1) for i in range(ends)])]
    all_to_all x4, starting transfers between devices: 19.5 us -> 18.8 us  [exchange(): lax.all_to_all(values, ('space', 'batch'), split_axis=0, concat_axis=0, t...]
  transfers between devices with their start and end apart: 8 -> 8, of which waited for: 5 -> 5; matrix products, arithmetic and copies ran while one was open for 0% -> 0% of each run, Pallas kernels for 20% -> 18%
where the time goes in v15:
time: 70.7 us; the launch traced here: 70.1 us
  starting transfers between devices  25.6 us (36%)
  Pallas kernels  21.6 us (31%)
  waiting for transfers between devices  21 us (30%)
  local copies, waits for them, and re-layouts  1.09 us (2%)
  between operations  0.87 us (1%)
    pallas_call x10, Pallas kernels, run(): pl.pallas_call(kernel, out_shape=results, in_specs=[in_hbm if k in staged...  21.6 us
    all_to_all x4, waiting for transfers between devices, exchange(): lax.all_to_all(values, ('space', 'batch'), split_axis=0, concat_axis=0, t...  20.1 us
    all_to_all x4, starting transfers between devices, exchange(): lax.all_to_all(values, ('space', 'batch'), split_axis=0, concat_axis=0, t...  18.8 us
    ppermute x2, starting transfers between devices, neighbours(): before = lax.ppermute(last, 'space', [(i, i + 1) for i in range(ends)])  4.19 us
    ppermute x2, starting transfers between devices, neighbours(): after = lax.ppermute(first, 'space', [(i + 1, i) for i in range(ends)])  2.58 us
  transfers between devices with their start and end apart: 8, of which 5 were waited for; matrix products, arithmetic and copies ran while one was open for 0% of the time, Pallas kernels for 18%

profile of v15, /device:TPU:0, one launch (start us, length us, event | category | flops | bytes accessed | tf_op | source)
XLA Modules:
  0.0 70.1 jit_solution(16255777325897417375)
XLA Ops:
  0.6 3.2 %analyse_kernel.1 = (bf16[1024,128]{1,0:T(8,128)(2,1)}, bf16[256,128]{1,0:T(8,128)(2,1)}, bf16[512,128]{1,0:T(8,128)(2,1)}, bf16[512,128]{1,0:T(8,128)(2,1)}, bf...) custom-call(bf16[64,2,1024]{2,1,0:T(2,128)(2,1)} %bitcast.22, bf16[256,1024]{1,0:T(8,128)(2,1)} %constant.14.clone.refs_1_, ...), custom_call_target="tpu_custom_call" | custom-call | flops 100000000 | bytes 32374784 | tf_op jit(solution)/shard_map/analyse_kernel/pallas_call | solution.py:575
  3.9 7.3 %all-to-all-start = ((bf16[32,8,128]{2,1,0:T(8,128)(2,1)}), bf16[32,8,128]{2,1,0:T(8,128)(2,1)S(1)}, u32[]{:S(2)}, u32[]{:S(2)}) async-start(bf16[32,8,128]{2,1,0:T(8,128)(2,1)} %bitcast.23), calls=%async_computation | async-start | bytes 131072 | tf_op jit(solution)/shard_map/all_to_all | solution.py:592
  11.2 2.2 %collective-permute-start = (bf16[512,128]{1,0:T(8,128)(2,1)}, bf16[512,128]{1,0:T(8,128)(2,1)S(1)}, u32[]{:S(2)}, u32[]{:S(2)}) collective-permute-start(bf16[512,128]{1,0:T(8,128)(2,1)} %get-tuple-element.36), channel_id=1, source_target_pairs={{0,1},{1,2},{2,3},{3,4},{4,5},{5,6},{6,7},{7,8},{8,9},{9,10},{10,1... | collective-permute-start | bytes 393224 | tf_op jit(solution)/shard_map/ppermute | solution.py:597
  13.3 1.3 %collective-permute-start.1 = (bf16[512,128]{1,0:T(8,128)(2,1)}, bf16[512,128]{1,0:T(8,128)(2,1)S(1)}, u32[]{:S(2)}, u32[]{:S(2)}) collective-permute-start(bf16[512,128]{1,0:T(8,128)(2,1)} %get-tuple-element.37), channel_id=1, source_target_pairs={{1,0},{2,1},{3,2},{4,3},{5,4},{6,5},{7,6},{8,7},{9,8},{10,9},{11,1... | collective-permute-start | bytes 393224 | tf_op jit(solution)/shard_map/ppermute | solution.py:598
  14.6 0.0 copy-start.4
  14.7 0.0 copy-start.5
  14.7 0.0 copy-start.1
  14.7 0.0 copy-start.6
  14.7 0.0 copy-start.7
  14.7 1.5 %fetch_kernel.1.refs_2_ = bf16[6144,128]{1,0:T(8,128)(2,1)S(1)} custom-call(bf16[102400,128]{1,0:T(8,128)(2,1)} %get-tuple-element.32.refs_0_.refs_1_), custom_call_target="tpu_custom_call" | custom-call | bytes 27787264 | tf_op jit(solution)/shard_map/fetch_kernel/pallas_call | solution.py:575
  16.2 2.6 %all-to-all-done = bf16[32,8,128]{2,1,0:T(8,128)(2,1)S(1)} async-done(((bf16[32,8,128]{2,1,0:T(8,128)(2,1)}), bf16[32,8,128]{2,1,0:T(8,128)(2,1)S(1)}, u32[]{:S(2)}, u32[]{:S(2)}) %all-to-all-start) | async-done | bytes 65568 | tf_op jit(solution)/shard_map/all_to_all | solution.py:592
  18.8 0.0 copy-done.4
  18.8 0.0 copy-done.5
  18.8 1.8 %mix_kernel.1 = (bf16[32,8,128]{2,1,0:T(8,128)(2,1)}, bf16[384,256]{1,0:T(8,128)(2,1)S(1)}) custom-call(bf16[256,128]{1,0:T(8,128)(2,1)S(1)} %bitcast.15, bf16[192,256]{1,0:T(8,128)(2,1)S(1)} %copy-done.5, bf16[6144,128]{1,0:T(8,128)(2,1)S(1)} %fetch_kernel.1.refs_2_, bf16[128,384]{1,0:T(8,128)(2,1)S(1)} %copy-done.4, ...), custom_call_target="tpu_custom_call", output_to_operand_aliasing={{0}: (4, {})} | custom-call | flops 400000000 | bytes 2097152 | tf_op jit(solution)/shard_map/mix_kernel/pallas_call | solution.py:575
  20.6 5.4 %all-to-all-start.1 = ((bf16[32,8,128]{2,1,0:T(8,128)(2,1)}), bf16[32,8,128]{2,1,0:T(8,128)(2,1)S(1)}, u32[]{:S(2)}, u32[]{:S(2)}) async-start(bf16[32,8,128]{2,1,0:T(8,128)(2,1)} %get-tuple-element.34), calls=%async_computation.1 | async-start | bytes 131072 | tf_op jit(solution)/shard_map/all_to_all | solution.py:592
  26.0 0.0 collective-permute-done.refs_1_
  26.0 0.0 collective-permute-done.1.refs_2_
  26.0 0.0 copy-done.1
  26.0 0.0 copy-done.6
  26.0 0.0 copy-done.7
  26.0 1.2 %local_kernel.1 = (f32[1024,128]{1,0:T(8,128)S(1)}, bf16[256,1024]{1,0:T(8,128)(2,1)S(1)}, bf16[1024,128]{1,0:T(8,128)(2,1)S(1)}) custom-call(bf16[1024,128]{1,0:T(8,128)(2,1)S(1)} %copy-done.7, bf16[512,128]{1,0:T(8,128)(2,1)S(1)} %collective-permute-done.refs_1_, bf16[512,128]{1,0:T(8,128)(2,1)S(1)} %collective-permute-done.1.refs_2_, ...), custom_call_target="tpu_custom_call" | custom-call | flops 700000000 | bytes 2318336 | tf_op jit(solution)/shard_map/local_kernel/pallas_call | solution.py:575
  27.2 6.4 %all-to-all-done.1 = bf16[32,8,128]{2,1,0:T(8,128)(2,1)S(1)} async-done(((bf16[32,8,128]{2,1,0:T(8,128)(2,1)}), bf16[32,8,128]{2,1,0:T(8,128)(2,1)S(1)}, u32[]{:S(2)}, u32[]{:S(2)}) %all-to-all-start.1) | async-done | bytes 65568 | tf_op jit(solution)/shard_map/all_to_all | solution.py:592
  33.6 0.0 copy-start.8
  33.6 1.0 %copy-done.8 = bf16[1024,256]{1,0:T(8,128)(2,1)S(1)} copy-done((bf16[1024,256]{1,0:T(8,128)(2,1)S(1)}, bf16[1024,256]{1,0:T(8,128)(2,1)}, u32[]{:S(2)}) %copy-start.8) | copy-done | bytes 524312
  34.6 2.6 %activate_kernel.1 = (bf16[1024,128]{1,0:T(8,128)(2,1)S(1)}, bf16[102400,128]{1,0:T(8,128)(2,1)}, bf16[512,128]{1,0:T(8,128)(2,1)S(1)}, bf16[512,128]{1,0:T(8,128)(2,1)S(1)}, bf16[32,40,128]{2,1,0:T(8,128)(2,1)}) custom-call(bf16[256,128]{1,0:T(8,128)(2,1)S(1)} %bitcast.16, bf16[1024,256]{1,0:T(8,128)(2,1)S(1)} %copy-done.8, ...), custom_call_target="tpu_custom_call" | custom-call | flops 1000000000 | bytes 28966912 | tf_op jit(solution)/shard_map/activate_kernel/pallas_call | solution.py:575
  37.3 2.6 %all-to-all-start.2 = ((bf16[32,40,128]{2,1,0:T(8,128)(2,1)}), bf16[32,40,128]{2,1,0:T(8,128)(2,1)S(1)}, u32[]{:S(2)}, u32[]{:S(2)}) async-start(bf16[32,40,128]{2,1,0:T(8,128)(2,1)} %get-tuple-element.41), calls=%async_computation.2 | async-start | bytes 655360 | tf_op jit(solution)/shard_map/all_to_all | solution.py:592
  39.9 2.0 %collective-permute-start.2 = (bf16[512,128]{1,0:T(8,128)(2,1)S(1)}, bf16[512,128]{1,0:T(8,128)(2,1)S(1)}, u32[]{:S(2)}, u32[]{:S(2)}) collective-permute-start(bf16[512,128]{1,0:T(8,128)(2,1)S(1)} %get-tuple-element.42), channel_id=1, source_target_pairs={{0,1},{1,2},{2,3},{3,4},{4,5},{5,6},{6,7},{7,8},{8,9},{9,10},{10,1... | collective-permute-start | bytes 393224 | tf_op jit(solution)/shard_map/ppermute | solution.py:597
  41.9 1.3 %collective-permute-start.3 = (bf16[512,128]{1,0:T(8,128)(2,1)S(1)}, bf16[512,128]{1,0:T(8,128)(2,1)S(1)}, u32[]{:S(2)}, u32[]{:S(2)}) collective-permute-start(bf16[512,128]{1,0:T(8,128)(2,1)S(1)} %get-tuple-element.43), channel_id=1, source_target_pairs={{1,0},{2,1},{3,2},{4,3},{5,4},{6,5},{7,6},{8,7},{9,8},{10,9},{11,1... | collective-permute-start | bytes 393224 | tf_op jit(solution)/shard_map/ppermute | solution.py:598
  43.2 0.0 copy-start.2
  43.2 0.0 copy-start.3
  43.3 2.2 %output_kernel.1 = (bf16[64,2,1024]{2,1,0:T(2,128)(2,1)}, bf16[6144,128]{1,0:T(8,128)(2,1)S(1)}) custom-call(bf16[1024,128]{1,0:T(8,128)(2,1)S(1)} %get-tuple-element.44.refs_0_, bf16[102400,128]{1,0:T(8,128)(2,1)} %get-tuple-element.32.refs_0_.refs_1_), custom_call_target="tpu_custom_call" | custom-call | flops 100000000 | bytes 28311552 | tf_op jit(solution)/shard_map/output_kernel/pallas_call | solution.py:575
  45.4 0.0 collective-permute-done.2.refs_1_
  45.5 0.9 %collective-permute-done.3.refs_2_ = bf16[512,128]{1,0:T(8,128)(2,1)S(1)} collective-permute-done((bf16[512,128]{1,0:T(8,128)(2,1)S(1)}, bf16[512,128]{1,0:T(8,128)(2,1)S(1)}, u32[]{:S(2)}, u32[]{:S(2)}) %collective-permute-start.3) | collective-permute-done | bytes 131104 | tf_op jit(solution)/shard_map/ppermute | solution.py:598
  46.3 5.3 %all-to-all-done.2.refs_0_ = bf16[32,40,128]{2,1,0:T(8,128)(2,1)S(1)} async-done(((bf16[32,40,128]{2,1,0:T(8,128)(2,1)}), bf16[32,40,128]{2,1,0:T(8,128)(2,1)S(1)}, u32[]{:S(2)}, u32[]{:S(2)}) %all-to-all-start.2) | async-done | bytes 327712 | tf_op jit(solution)/shard_map/all_to_all | solution.py:592
  51.6 0.0 copy-done.2
  51.6 0.0 copy-done.3
  51.6 1.8 %unmix_kernel.1 = (bf16[32,40,128]{2,1,0:T(8,128)(2,1)}, bf16[384,128]{1,0:T(8,128)(2,1)S(1)}) custom-call(bf16[32,40,128]{2,1,0:T(8,128)(2,1)S(1)} %all-to-all-done.2.refs_0_, bf16[192,256]{1,0:T(8,128)(2,1)S(1)} %copy-done.3, bf16[6144,128]{1,0:T(8,128)(2,1)S(1)} %get-tuple-element.49.refs_2_, bf16[128,384]{1,0:T(8,128)(2,1)S(1)} %copy-done.2), custom_call_target="tpu_custom_call" | custom-call | flops 400000000 | bytes 2523136 | tf_op jit(solution)/shard_map/unmix_kernel/pallas_call | solution.py:575
  53.4 3.5 %all-to-all-start.3 = ((bf16[32,40,128]{2,1,0:T(8,128)(2,1)}), bf16[32,40,128]{2,1,0:T(8,128)(2,1)S(1)}, u32[]{:S(2)}, u32[]{:S(2)}) async-start(bf16[32,40,128]{2,1,0:T(8,128)(2,1)} %get-tuple-element.50), calls=%async_computation.3 | async-start | bytes 655360 | tf_op jit(solution)/shard_map/all_to_all | solution.py:592
  56.9 3.7 %weight_kernel.1 = f32[12288,64]{1,0:T(8,128)} custom-call(bf16[384,256]{1,0:T(8,128)(2,1)S(1)} %get-tuple-element.55.refs_0_, bf16[384,128]{1,0:T(8,128)(2,1)S(1)} %get-tuple-element.56.refs_1_), custom_call_target="tpu_custom_call" | custom-call | flops 400000000 | bytes 3440640 | tf_op jit(solution)/shard_map/weight_kernel/pallas_call | solution.py:575
  60.7 0.0 copy-start
  60.7 2.1 %local_grad_kernel.1.refs_2_ = f32[1024,128]{1,0:T(8,128)S(1)} custom-call(bf16[102400,128]{1,0:T(8,128)(2,1)} %get-tuple-element.51.refs_0_, bf16[512,128]{1,0:T(8,128)(2,1)S(1)} %collective-permute-done.2.refs_1_, bf16[512,128]{1,0:T(8,128)(2,1)S(1)} %collective-permute-done.3.refs_2_, bf16[27,64,64]{2,1,0:T(8,128)(2,1)S(1)} %bitcast.14), custom_call_target="tpu_custom_call" | custom-call | flops 700000000 | bytes 27222016 | tf_op jit(solution)/shard_map/local_grad_kernel/pallas_call | solution.py:575
  62.7 5.9 %all-to-all-done.3.refs_0_ = bf16[32,40,128]{2,1,0:T(8,128)(2,1)S(1)} async-done(((bf16[32,40,128]{2,1,0:T(8,128)(2,1)}), bf16[32,40,128]{2,1,0:T(8,128)(2,1)S(1)}, u32[]{:S(2)}, u32[]{:S(2)}) %all-to-all-start.3) | async-done | bytes 327712 | tf_op jit(solution)/shard_map/all_to_all | solution.py:592
  68.6 0.0 copy-done
  68.6 1.5 %finish_kernel.1 = (bf16[64,2,1024]{2,1,0:T(2,128)(2,1)}, f32[27,64,64]{2,1,0:T(8,128)}) custom-call(bf16[32,40,128]{2,1,0:T(8,128)(2,1)S(1)} %all-to-all-done.3.refs_0_, bf16[1024,256]{1,0:T(8,128)(2,1)S(1)} %copy-done, f32[1024,128]{1,0:T(8,128)S(1)} %local_grad_kernel.1.refs_2_), custom_call_target="tpu_custom_call" | custom-call | flops 100000000 | bytes 2080768 | tf_op jit(solution)/shard_map/finish_kernel/pallas_call | solution.py:575
Async XLA Ops:
  3.9 14.9 %all-to-all-start = ((bf16[32,8,128]{2,1,0:T(8,128)(2,1)}), bf16[32,8,128]{2,1,0:T(8,128)(2,1)S(1)}, u32[]{:S(2)}, u32[]{:S(2)}) async-start(bf16[32,8,128]{2,1,0:T(8,128)(2,1)} %bitcast.23), calls=%async_computation | async-start | bytes 131072 | tf_op jit(solution)/shard_map/all_to_all | solution.py:592
  11.2 14.8 %collective-permute-start = (bf16[512,128]{1,0:T(8,128)(2,1)}, bf16[512,128]{1,0:T(8,128)(2,1)S(1)}, u32[]{:S(2)}, u32[]{:S(2)}) collective-permute-start(bf16[512,128]{1,0:T(8,128)(2,1)} %get-tuple-element.36), channel_id=1, source_target_pairs={{0,1},{1,2},{2,3},{3,4},{4,5},{5,6},{6,7},{7,8},{8,9},{9,10},{10,1... | collective-permute-start | bytes 393224 | tf_op jit(solution)/shard_map/ppermute | solution.py:597
  13.3 12.7 %collective-permute-start.1 = (bf16[512,128]{1,0:T(8,128)(2,1)}, bf16[512,128]{1,0:T(8,128)(2,1)S(1)}, u32[]{:S(2)}, u32[]{:S(2)}) collective-permute-start(bf16[512,128]{1,0:T(8,128)(2,1)} %get-tuple-element.37), channel_id=1, source_target_pairs={{1,0},{2,1},{3,2},{4,3},{5,4},{6,5},{7,6},{8,7},{9,8},{10,9},{11,1... | collective-permute-start | bytes 393224 | tf_op jit(solution)/shard_map/ppermute | solution.py:598
  14.6 4.1 %copy-start.4 = (bf16[128,384]{1,0:T(8,128)(2,1)S(1)}, bf16[128,384]{1,0:T(8,128)(2,1)}, u32[]{:S(2)}) copy-start(bf16[128,384]{1,0:T(8,128)(2,1)} %constant.16.clone.refs_3_) | copy-start | bytes 294916
  14.7 4.1 %copy-start.5 = (bf16[192,256]{1,0:T(8,128)(2,1)S(1)}, bf16[192,256]{1,0:T(8,128)(2,1)}, u32[]{:S(2)}) copy-start(bf16[192,256]{1,0:T(8,128)(2,1)} %constant.15.clone.refs_1_) | copy-start | bytes 294916
  14.7 11.3 %copy-start.1 = (bf16[3,3,3,64,64]{4,3,2,1,0:T(8,128)(2,1)S(1)}, bf16[3,3,3,64,64]{4,3,2,1,0:T(8,128)(2,1)}, u32[]{:S(2)}) copy-start(bf16[3,3,3,64,64]{4,3,2,1,0:T(8,128)(2,1)} %param.14) | copy-start | bytes 663556
  14.7 11.3 %copy-start.6 = (bf16[1,64,2,1024]{3,2,1,0:T(2,128)(2,1)S(1)}, bf16[1,64,2,1024]{3,2,1,0:T(2,128)(2,1)}, u32[]{:S(2)}) copy-start(bf16[1,64,2,1024]{3,2,1,0:T(2,128)(2,1)} %param.12) | copy-start | bytes 786436
  14.7 11.3 %copy-start.7 = (bf16[1024,128]{1,0:T(8,128)(2,1)S(1)}, bf16[1024,128]{1,0:T(8,128)(2,1)}, u32[]{:S(2)}) copy-start(bf16[1024,128]{1,0:T(8,128)(2,1)} %get-tuple-element.35.refs_0_) | copy-start | bytes 786436
  20.6 13.0 %all-to-all-start.1 = ((bf16[32,8,128]{2,1,0:T(8,128)(2,1)}), bf16[32,8,128]{2,1,0:T(8,128)(2,1)S(1)}, u32[]{:S(2)}, u32[]{:S(2)}) async-start(bf16[32,8,128]{2,1,0:T(8,128)(2,1)} %get-tuple-element.34), calls=%async_computation.1 | async-start | bytes 131072 | tf_op jit(solution)/shard_map/all_to_all | solution.py:592
  33.6 1.0 %copy-start.8 = (bf16[1024,256]{1,0:T(8,128)(2,1)S(1)}, bf16[1024,256]{1,0:T(8,128)(2,1)}, u32[]{:S(2)}) copy-start(bf16[1024,256]{1,0:T(8,128)(2,1)} %constant.17.clone.refs_1_) | copy-start | bytes 1572868
  37.3 14.3 %all-to-all-start.2 = ((bf16[32,40,128]{2,1,0:T(8,128)(2,1)}), bf16[32,40,128]{2,1,0:T(8,128)(2,1)S(1)}, u32[]{:S(2)}, u32[]{:S(2)}) async-start(bf16[32,40,128]{2,1,0:T(8,128)(2,1)} %get-tuple-element.41), calls=%async_computation.2 | async-start | bytes 655360 | tf_op jit(solution)/shard_map/all_to_all | solution.py:592
  39.9 5.6 %collective-permute-start.2 = (bf16[512,128]{1,0:T(8,128)(2,1)S(1)}, bf16[512,128]{1,0:T(8,128)(2,1)S(1)}, u32[]{:S(2)}, u32[]{:S(2)}) collective-permute-start(bf16[512,128]{1,0:T(8,128)(2,1)S(1)} %get-tuple-element.42), channel_id=1, source_target_pairs={{0,1},{1,2},{2,3},{3,4},{4,5},{5,6},{6,7},{7,8},{8,9},{9,10},{10,1... | collective-permute-start | bytes 393224 | tf_op jit(solution)/shard_map/ppermute | solution.py:597
  41.9 4.4 %collective-permute-start.3 = (bf16[512,128]{1,0:T(8,128)(2,1)S(1)}, bf16[512,128]{1,0:T(8,128)(2,1)S(1)}, u32[]{:S(2)}, u32[]{:S(2)}) collective-permute-start(bf16[512,128]{1,0:T(8,128)(2,1)S(1)} %get-tuple-element.43), channel_id=1, source_target_pairs={{1,0},{2,1},{3,2},{4,3},{5,4},{6,5},{7,6},{8,7},{9,8},{10,9},{11,1... | collective-permute-start | bytes 393224 | tf_op jit(solution)/shard_map/ppermute | solution.py:598
  43.2 8.4 %copy-start.2 = (bf16[128,384]{1,0:T(8,128)(2,1)S(1)}, bf16[128,384]{1,0:T(8,128)(2,1)}, u32[]{:S(2)}) copy-start(bf16[128,384]{1,0:T(8,128)(2,1)} %constant.19.clone.refs_3_) | copy-start | bytes 294916
  43.2 8.4 %copy-start.3 = (bf16[192,256]{1,0:T(8,128)(2,1)S(1)}, bf16[192,256]{1,0:T(8,128)(2,1)}, u32[]{:S(2)}) copy-start(bf16[192,256]{1,0:T(8,128)(2,1)} %constant.18.clone.refs_1_) | copy-start | bytes 294916
  53.4 15.2 %all-to-all-start.3 = ((bf16[32,40,128]{2,1,0:T(8,128)(2,1)}), bf16[32,40,128]{2,1,0:T(8,128)(2,1)S(1)}, u32[]{:S(2)}, u32[]{:S(2)}) async-start(bf16[32,40,128]{2,1,0:T(8,128)(2,1)} %get-tuple-element.50), calls=%async_computation.3 | async-start | bytes 655360 | tf_op jit(solution)/shard_map/all_to_all | solution.py:592
  60.7 8.0 %copy-start = (bf16[1024,256]{1,0:T(8,128)(2,1)S(1)}, bf16[1024,256]{1,0:T(8,128)(2,1)}, u32[]{:S(2)}) copy-start(bf16[1024,256]{1,0:T(8,128)(2,1)} %constant.20.clone.refs_1_) | copy-start | bytes 1572868

commit v16 on v15

--- a/solution.py
+++ b/solution.py
@@ -659,7 +659,7 @@
         cotangent.reshape(field.shape),
         taps,
         scratch=[padded, pltpu.VMEM((3, 2 * LANES, 3 * LANES), BF16)],
-        flops=7 * 10**8,
+        flops=8 * 10**9,
     )
     back, diagonal = run(
         functools.partial(mix_kernel, batches, slabs),

time: 70.7 us -> 69.6 us (0.984)
  local copies, waits for them, and re-layouts: 1.09 us -> 0.06 us
    unnamed x18, local copies, waits for them, and re-layouts: 1.09 us -> 0.06 us
where the time goes in v16:
time: 69.6 us; the launch traced here: 69.1 us
  starting transfers between devices  25.6 us (37%)
  Pallas kernels  21.6 us (31%)
  waiting for transfers between devices  21 us (30%)
  between operations  0.87 us (1%)
    pallas_call x10, Pallas kernels, run(): pl.pallas_call(kernel, out_shape=results, in_specs=[in_hbm if k in staged...  21.6 us
    all_to_all x4, waiting for transfers between devices, exchange(): lax.all_to_all(values, ('space', 'batch'), split_axis=0, concat_axis=0, t...  20.1 us
    all_to_all x4, starting transfers between devices, exchange(): lax.all_to_all(values, ('space', 'batch'), split_axis=0, concat_axis=0, t...  18.8 us
    ppermute x2, starting transfers between devices, neighbours(): before = lax.ppermute(last, 'space', [(i, i + 1) for i in range(ends)])  4.19 us
    ppermute x2, starting transfers between devices, neighbours(): after = lax.ppermute(first, 'space', [(i + 1, i) for i in range(ends)])  2.58 us
  transfers between devices with their start and end apart: 8, of which 5 were waited for; matrix products, arithmetic and copies ran while one was open for 0% of the time, Pallas kernels for 18%

profile of v16, /device:TPU:0, one launch (start us, length us, event | category | flops | bytes accessed | tf_op | source)
XLA Modules:
  0.0 69.1 jit_solution(8986627286718303520)
XLA Ops:
  0.6 3.2 %analyse_kernel.1 = (bf16[1024,128]{1,0:T(8,128)(2,1)}, bf16[256,128]{1,0:T(8,128)(2,1)}, bf16[512,128]{1,0:T(8,128)(2,1)}, bf16[512,128]{1,0:T(8,128)(2,1)}, bf...) custom-call(bf16[64,2,1024]{2,1,0:T(2,128)(2,1)} %bitcast.22, bf16[256,1024]{1,0:T(8,128)(2,1)} %constant.14.clone.refs_1_, ...), custom_call_target="tpu_custom_call" | custom-call | flops 100000000 | bytes 32374784 | tf_op jit(solution)/shard_map/analyse_kernel/pallas_call | solution.py:575
  3.9 7.3 %all-to-all-start = ((bf16[32,8,128]{2,1,0:T(8,128)(2,1)}), bf16[32,8,128]{2,1,0:T(8,128)(2,1)S(1)}, u32[]{:S(2)}, u32[]{:S(2)}) async-start(bf16[32,8,128]{2,1,0:T(8,128)(2,1)} %bitcast.23), calls=%async_computation | async-start | bytes 131072 | tf_op jit(solution)/shard_map/all_to_all | solution.py:592
  11.2 2.2 %collective-permute-start = (bf16[512,128]{1,0:T(8,128)(2,1)}, bf16[512,128]{1,0:T(8,128)(2,1)S(1)}, u32[]{:S(2)}, u32[]{:S(2)}) collective-permute-start(bf16[512,128]{1,0:T(8,128)(2,1)} %get-tuple-element.36), channel_id=1, source_target_pairs={{0,1},{1,2},{2,3},{3,4},{4,5},{5,6},{6,7},{7,8},{8,9},{9,10},{10,1... | collective-permute-start | bytes 393224 | tf_op jit(solution)/shard_map/ppermute | solution.py:597
  13.3 1.3 %collective-permute-start.1 = (bf16[512,128]{1,0:T(8,128)(2,1)}, bf16[512,128]{1,0:T(8,128)(2,1)S(1)}, u32[]{:S(2)}, u32[]{:S(2)}) collective-permute-start(bf16[512,128]{1,0:T(8,128)(2,1)} %get-tuple-element.37), channel_id=1, source_target_pairs={{1,0},{2,1},{3,2},{4,3},{5,4},{6,5},{7,6},{8,7},{9,8},{10,9},{11,1... | collective-permute-start | bytes 393224 | tf_op jit(solution)/shard_map/ppermute | solution.py:598
  14.6 0.0 copy-start.4
  14.7 0.0 copy-start.5
  14.7 0.0 copy-start.1
  14.7 0.0 copy-start.6
  14.7 0.0 copy-start.7
  14.7 1.5 %fetch_kernel.1.refs_2_ = bf16[6144,128]{1,0:T(8,128)(2,1)S(1)} custom-call(bf16[102400,128]{1,0:T(8,128)(2,1)} %get-tuple-element.32.refs_0_.refs_1_), custom_call_target="tpu_custom_call" | custom-call | bytes 27787264 | tf_op jit(solution)/shard_map/fetch_kernel/pallas_call | solution.py:575
  16.2 2.6 %all-to-all-done = bf16[32,8,128]{2,1,0:T(8,128)(2,1)S(1)} async-done(((bf16[32,8,128]{2,1,0:T(8,128)(2,1)}), bf16[32,8,128]{2,1,0:T(8,128)(2,1)S(1)}, u32[]{:S(2)}, u32[]{:S(2)}) %all-to-all-start) | async-done | bytes 65568 | tf_op jit(solution)/shard_map/all_to_all | solution.py:592
  18.8 0.0 copy-done.4
  18.8 0.0 copy-done.5
  18.8 1.8 %mix_kernel.1 = (bf16[32,8,128]{2,1,0:T(8,128)(2,1)}, bf16[384,256]{1,0:T(8,128)(2,1)S(1)}) custom-call(bf16[256,128]{1,0:T(8,128)(2,1)S(1)} %bitcast.15, bf16[192,256]{1,0:T(8,128)(2,1)S(1)} %copy-done.5, bf16[6144,128]{1,0:T(8,128)(2,1)S(1)} %fetch_kernel.1.refs_2_, bf16[128,384]{1,0:T(8,128)(2,1)S(1)} %copy-done.4, ...), custom_call_target="tpu_custom_call", output_to_operand_aliasing={{0}: (4, {})} | custom-call | flops 400000000 | bytes 2097152 | tf_op jit(solution)/shard_map/mix_kernel/pallas_call | solution.py:575
  20.6 5.4 %all-to-all-start.1 = ((bf16[32,8,128]{2,1,0:T(8,128)(2,1)}), bf16[32,8,128]{2,1,0:T(8,128)(2,1)S(1)}, u32[]{:S(2)}, u32[]{:S(2)}) async-start(bf16[32,8,128]{2,1,0:T(8,128)(2,1)} %get-tuple-element.34), calls=%async_computation.1 | async-start | bytes 131072 | tf_op jit(solution)/shard_map/all_to_all | solution.py:592
  26.0 0.0 collective-permute-done.refs_1_
  26.0 0.0 collective-permute-done.1.refs_2_
  26.0 0.0 copy-done.1
  26.0 0.0 copy-done.6
  26.0 0.0 copy-done.7
  26.0 0.0 copy-start.8
  26.0 1.2 %local_kernel.1 = (f32[1024,128]{1,0:T(8,128)S(1)}, bf16[256,1024]{1,0:T(8,128)(2,1)S(1)}, bf16[1024,128]{1,0:T(8,128)(2,1)S(1)}) custom-call(bf16[1024,128]{1,0:T(8,128)(2,1)S(1)} %copy-done.7, bf16[512,128]{1,0:T(8,128)(2,1)S(1)} %collective-permute-done.refs_1_, bf16[512,128]{1,0:T(8,128)(2,1)S(1)} %collective-permute-done.1.refs_2_, ...), custom_call_target="tpu_custom_call" | custom-call | flops 8000000000 | bytes 2318336 | tf_op jit(solution)/shard_map/local_kernel/pallas_call | solution.py:575
  27.2 6.4 %all-to-all-done.1 = bf16[32,8,128]{2,1,0:T(8,128)(2,1)S(1)} async-done(((bf16[32,8,128]{2,1,0:T(8,128)(2,1)}), bf16[32,8,128]{2,1,0:T(8,128)(2,1)S(1)}, u32[]{:S(2)}, u32[]{:S(2)}) %all-to-all-start.1) | async-done | bytes 65568 | tf_op jit(solution)/shard_map/all_to_all | solution.py:592
  33.6 0.0 copy-done.8
  33.6 2.6 %activate_kernel.1 = (bf16[1024,128]{1,0:T(8,128)(2,1)S(1)}, bf16[102400,128]{1,0:T(8,128)(2,1)}, bf16[512,128]{1,0:T(8,128)(2,1)S(1)}, bf16[512,128]{1,0:T(8,128)(2,1)S(1)}, bf16[32,40,128]{2,1,0:T(8,128)(2,1)}) custom-call(bf16[256,128]{1,0:T(8,128)(2,1)S(1)} %bitcast.16, bf16[1024,256]{1,0:T(8,128)(2,1)S(1)} %copy-done.8, ...), custom_call_target="tpu_custom_call" | custom-call | flops 1000000000 | bytes 28966912 | tf_op jit(solution)/shard_map/activate_kernel/pallas_call | solution.py:575
  36.2 2.6 %all-to-all-start.2 = ((bf16[32,40,128]{2,1,0:T(8,128)(2,1)}), bf16[32,40,128]{2,1,0:T(8,128)(2,1)S(1)}, u32[]{:S(2)}, u32[]{:S(2)}) async-start(bf16[32,40,128]{2,1,0:T(8,128)(2,1)} %get-tuple-element.41), calls=%async_computation.2 | async-start | bytes 655360 | tf_op jit(solution)/shard_map/all_to_all | solution.py:592
  38.9 2.0 %collective-permute-start.2 = (bf16[512,128]{1,0:T(8,128)(2,1)S(1)}, bf16[512,128]{1,0:T(8,128)(2,1)S(1)}, u32[]{:S(2)}, u32[]{:S(2)}) collective-permute-start(bf16[512,128]{1,0:T(8,128)(2,1)S(1)} %get-tuple-element.42), channel_id=1, source_target_pairs={{0,1},{1,2},{2,3},{3,4},{4,5},{5,6},{6,7},{7,8},{8,9},{9,10},{10,1... | collective-permute-start | bytes 393224 | tf_op jit(solution)/shard_map/ppermute | solution.py:597
  40.9 1.3 %collective-permute-start.3 = (bf16[512,128]{1,0:T(8,128)(2,1)S(1)}, bf16[512,128]{1,0:T(8,128)(2,1)S(1)}, u32[]{:S(2)}, u32[]{:S(2)}) collective-permute-start(bf16[512,128]{1,0:T(8,128)(2,1)S(1)} %get-tuple-element.43), channel_id=1, source_target_pairs={{1,0},{2,1},{3,2},{4,3},{5,4},{6,5},{7,6},{8,7},{9,8},{10,9},{11,1... | collective-permute-start | bytes 393224 | tf_op jit(solution)/shard_map/ppermute | solution.py:598
  42.2 0.0 copy-start.2
  42.2 0.0 copy-start.3
  42.2 2.2 %output_kernel.1 = (bf16[64,2,1024]{2,1,0:T(2,128)(2,1)}, bf16[6144,128]{1,0:T(8,128)(2,1)S(1)}) custom-call(bf16[1024,128]{1,0:T(8,128)(2,1)S(1)} %get-tuple-element.44.refs_0_, bf16[102400,128]{1,0:T(8,128)(2,1)} %get-tuple-element.32.refs_0_.refs_1_), custom_call_target="tpu_custom_call" | custom-call | flops 100000000 | bytes 28311552 | tf_op jit(solution)/shard_map/output_kernel/pallas_call | solution.py:575
  44.4 0.0 collective-permute-done.2.refs_1_
  44.4 0.9 %collective-permute-done.3.refs_2_ = bf16[512,128]{1,0:T(8,128)(2,1)S(1)} collective-permute-done((bf16[512,128]{1,0:T(8,128)(2,1)S(1)}, bf16[512,128]{1,0:T(8,128)(2,1)S(1)}, u32[]{:S(2)}, u32[]{:S(2)}) %collective-permute-start.3) | collective-permute-done | bytes 131104 | tf_op jit(solution)/shard_map/ppermute | solution.py:598
  45.3 5.3 %all-to-all-done.2.refs_0_ = bf16[32,40,128]{2,1,0:T(8,128)(2,1)S(1)} async-done(((bf16[32,40,128]{2,1,0:T(8,128)(2,1)}), bf16[32,40,128]{2,1,0:T(8,128)(2,1)S(1)}, u32[]{:S(2)}, u32[]{:S(2)}) %all-to-all-start.2) | async-done | bytes 327712 | tf_op jit(solution)/shard_map/all_to_all | solution.py:592
  50.6 0.0 copy-done.2
  50.6 0.0 copy-done.3
  50.6 1.8 %unmix_kernel.1 = (bf16[32,40,128]{2,1,0:T(8,128)(2,1)}, bf16[384,128]{1,0:T(8,128)(2,1)S(1)}) custom-call(bf16[32,40,128]{2,1,0:T(8,128)(2,1)S(1)} %all-to-all-done.2.refs_0_, bf16[192,256]{1,0:T(8,128)(2,1)S(1)} %copy-done.3, bf16[6144,128]{1,0:T(8,128)(2,1)S(1)} %get-tuple-element.49.refs_2_, bf16[128,384]{1,0:T(8,128)(2,1)S(1)} %copy-done.2), custom_call_target="tpu_custom_call" | custom-call | flops 400000000 | bytes 2523136 | tf_op jit(solution)/shard_map/unmix_kernel/pallas_call | solution.py:575
  52.4 3.5 %all-to-all-start.3 = ((bf16[32,40,128]{2,1,0:T(8,128)(2,1)}), bf16[32,40,128]{2,1,0:T(8,128)(2,1)S(1)}, u32[]{:S(2)}, u32[]{:S(2)}) async-start(bf16[32,40,128]{2,1,0:T(8,128)(2,1)} %get-tuple-element.50), calls=%async_computation.3 | async-start | bytes 655360 | tf_op jit(solution)/shard_map/all_to_all | solution.py:592
  55.9 3.7 %weight_kernel.1 = f32[12288,64]{1,0:T(8,128)} custom-call(bf16[384,256]{1,0:T(8,128)(2,1)S(1)} %get-tuple-element.55.refs_0_, bf16[384,128]{1,0:T(8,128)(2,1)S(1)} %get-tuple-element.56.refs_1_), custom_call_target="tpu_custom_call" | custom-call | flops 400000000 | bytes 3440640 | tf_op jit(solution)/shard_map/weight_kernel/pallas_call | solution.py:575
  59.6 0.0 copy-start
  59.6 2.1 %local_grad_kernel.1.refs_2_ = f32[1024,128]{1,0:T(8,128)S(1)} custom-call(bf16[102400,128]{1,0:T(8,128)(2,1)} %get-tuple-element.51.refs_0_, bf16[512,128]{1,0:T(8,128)(2,1)S(1)} %collective-permute-done.2.refs_1_, bf16[512,128]{1,0:T(8,128)(2,1)S(1)} %collective-permute-done.3.refs_2_, bf16[27,64,64]{2,1,0:T(8,128)(2,1)S(1)} %bitcast.14), custom_call_target="tpu_custom_call" | custom-call | flops 700000000 | bytes 27222016 | tf_op jit(solution)/shard_map/local_grad_kernel/pallas_call | solution.py:575
  61.7 5.9 %all-to-all-done.3.refs_0_ = bf16[32,40,128]{2,1,0:T(8,128)(2,1)S(1)} async-done(((bf16[32,40,128]{2,1,0:T(8,128)(2,1)}), bf16[32,40,128]{2,1,0:T(8,128)(2,1)S(1)}, u32[]{:S(2)}, u32[]{:S(2)}) %all-to-all-start.3) | async-done | bytes 327712 | tf_op jit(solution)/shard_map/all_to_all | solution.py:592
  67.6 0.0 copy-done
  67.6 1.5 %finish_kernel.1 = (bf16[64,2,1024]{2,1,0:T(2,128)(2,1)}, f32[27,64,64]{2,1,0:T(8,128)}) custom-call(bf16[32,40,128]{2,1,0:T(8,128)(2,1)S(1)} %all-to-all-done.3.refs_0_, bf16[1024,256]{1,0:T(8,128)(2,1)S(1)} %copy-done, f32[1024,128]{1,0:T(8,128)S(1)} %local_grad_kernel.1.refs_2_), custom_call_target="tpu_custom_call" | custom-call | flops 100000000 | bytes 2080768 | tf_op jit(solution)/shard_map/finish_kernel/pallas_call | solution.py:575
Async XLA Ops:
  3.9 14.9 %all-to-all-start = ((bf16[32,8,128]{2,1,0:T(8,128)(2,1)}), bf16[32,8,128]{2,1,0:T(8,128)(2,1)S(1)}, u32[]{:S(2)}, u32[]{:S(2)}) async-start(bf16[32,8,128]{2,1,0:T(8,128)(2,1)} %bitcast.23), calls=%async_computation | async-start | bytes 131072 | tf_op jit(solution)/shard_map/all_to_all | solution.py:592
  11.2 14.8 %collective-permute-start = (bf16[512,128]{1,0:T(8,128)(2,1)}, bf16[512,128]{1,0:T(8,128)(2,1)S(1)}, u32[]{:S(2)}, u32[]{:S(2)}) collective-permute-start(bf16[512,128]{1,0:T(8,128)(2,1)} %get-tuple-element.36), channel_id=1, source_target_pairs={{0,1},{1,2},{2,3},{3,4},{4,5},{5,6},{6,7},{7,8},{8,9},{9,10},{10,1... | collective-permute-start | bytes 393224 | tf_op jit(solution)/shard_map/ppermute | solution.py:597
  13.3 12.7 %collective-permute-start.1 = (bf16[512,128]{1,0:T(8,128)(2,1)}, bf16[512,128]{1,0:T(8,128)(2,1)S(1)}, u32[]{:S(2)}, u32[]{:S(2)}) collective-permute-start(bf16[512,128]{1,0:T(8,128)(2,1)} %get-tuple-element.37), channel_id=1, source_target_pairs={{1,0},{2,1},{3,2},{4,3},{5,4},{6,5},{7,6},{8,7},{9,8},{10,9},{11,1... | collective-permute-start | bytes 393224 | tf_op jit(solution)/shard_map/ppermute | solution.py:598
  14.6 4.1 %copy-start.4 = (bf16[128,384]{1,0:T(8,128)(2,1)S(1)}, bf16[128,384]{1,0:T(8,128)(2,1)}, u32[]{:S(2)}) copy-start(bf16[128,384]{1,0:T(8,128)(2,1)} %constant.16.clone.refs_3_) | copy-start | bytes 294916
  14.7 4.1 %copy-start.5 = (bf16[192,256]{1,0:T(8,128)(2,1)S(1)}, bf16[192,256]{1,0:T(8,128)(2,1)}, u32[]{:S(2)}) copy-start(bf16[192,256]{1,0:T(8,128)(2,1)} %constant.15.clone.refs_1_) | copy-start | bytes 294916
  14.7 11.3 %copy-start.1 = (bf16[3,3,3,64,64]{4,3,2,1,0:T(8,128)(2,1)S(1)}, bf16[3,3,3,64,64]{4,3,2,1,0:T(8,128)(2,1)}, u32[]{:S(2)}) copy-start(bf16[3,3,3,64,64]{4,3,2,1,0:T(8,128)(2,1)} %param.14) | copy-start | bytes 663556
  14.7 11.3 %copy-start.6 = (bf16[1,64,2,1024]{3,2,1,0:T(2,128)(2,1)S(1)}, bf16[1,64,2,1024]{3,2,1,0:T(2,128)(2,1)}, u32[]{:S(2)}) copy-start(bf16[1,64,2,1024]{3,2,1,0:T(2,128)(2,1)} %param.12) | copy-start | bytes 786436
  14.7 11.3 %copy-start.7 = (bf16[1024,128]{1,0:T(8,128)(2,1)S(1)}, bf16[1024,128]{1,0:T(8,128)(2,1)}, u32[]{:S(2)}) copy-start(bf16[1024,128]{1,0:T(8,128)(2,1)} %get-tuple-element.35.refs_0_) | copy-start | bytes 786436
  20.6 13.0 %all-to-all-start.1 = ((bf16[32,8,128]{2,1,0:T(8,128)(2,1)}), bf16[32,8,128]{2,1,0:T(8,128)(2,1)S(1)}, u32[]{:S(2)}, u32[]{:S(2)}) async-start(bf16[32,8,128]{2,1,0:T(8,128)(2,1)} %get-tuple-element.34), calls=%async_computation.1 | async-start | bytes 131072 | tf_op jit(solution)/shard_map/all_to_all | solution.py:592
  26.0 7.6 %copy-start.8 = (bf16[1024,256]{1,0:T(8,128)(2,1)S(1)}, bf16[1024,256]{1,0:T(8,128)(2,1)}, u32[]{:S(2)}) copy-start(bf16[1024,256]{1,0:T(8,128)(2,1)} %constant.17.clone.refs_1_) | copy-start | bytes 1572868
  36.2 14.3 %all-to-all-start.2 = ((bf16[32,40,128]{2,1,0:T(8,128)(2,1)}), bf16[32,40,128]{2,1,0:T(8,128)(2,1)S(1)}, u32[]{:S(2)}, u32[]{:S(2)}) async-start(bf16[32,40,128]{2,1,0:T(8,128)(2,1)} %get-tuple-element.41), calls=%async_computation.2 | async-start | bytes 655360 | tf_op jit(solution)/shard_map/all_to_all | solution.py:592
  38.9 5.6 %collective-permute-start.2 = (bf16[512,128]{1,0:T(8,128)(2,1)S(1)}, bf16[512,128]{1,0:T(8,128)(2,1)S(1)}, u32[]{:S(2)}, u32[]{:S(2)}) collective-permute-start(bf16[512,128]{1,0:T(8,128)(2,1)S(1)} %get-tuple-element.42), channel_id=1, source_target_pairs={{0,1},{1,2},{2,3},{3,4},{4,5},{5,6},{6,7},{7,8},{8,9},{9,10},{10,1... | collective-permute-start | bytes 393224 | tf_op jit(solution)/shard_map/ppermute | solution.py:597
  40.9 4.4 %collective-permute-start.3 = (bf16[512,128]{1,0:T(8,128)(2,1)S(1)}, bf16[512,128]{1,0:T(8,128)(2,1)S(1)}, u32[]{:S(2)}, u32[]{:S(2)}) collective-permute-start(bf16[512,128]{1,0:T(8,128)(2,1)S(1)} %get-tuple-element.43), channel_id=1, source_target_pairs={{1,0},{2,1},{3,2},{4,3},{5,4},{6,5},{7,6},{8,7},{9,8},{10,9},{11,1... | collective-permute-start | bytes 393224 | tf_op jit(solution)/shard_map/ppermute | solution.py:598
  42.2 8.4 %copy-start.2 = (bf16[128,384]{1,0:T(8,128)(2,1)S(1)}, bf16[128,384]{1,0:T(8,128)(2,1)}, u32[]{:S(2)}) copy-start(bf16[128,384]{1,0:T(8,128)(2,1)} %constant.19.clone.refs_3_) | copy-start | bytes 294916
  42.2 8.4 %copy-start.3 = (bf16[192,256]{1,0:T(8,128)(2,1)S(1)}, bf16[192,256]{1,0:T(8,128)(2,1)}, u32[]{:S(2)}) copy-start(bf16[192,256]{1,0:T(8,128)(2,1)} %constant.18.clone.refs_1_) | copy-start | bytes 294916
  52.4 15.2 %all-to-all-start.3 = ((bf16[32,40,128]{2,1,0:T(8,128)(2,1)}), bf16[32,40,128]{2,1,0:T(8,128)(2,1)S(1)}, u32[]{:S(2)}, u32[]{:S(2)}) async-start(bf16[32,40,128]{2,1,0:T(8,128)(2,1)} %get-tuple-element.50), calls=%async_computation.3 | async-start | bytes 655360 | tf_op jit(solution)/shard_map/all_to_all | solution.py:592
  59.6 8.0 %copy-start = (bf16[1024,256]{1,0:T(8,128)(2,1)S(1)}, bf16[1024,256]{1,0:T(8,128)(2,1)}, u32[]{:S(2)}) copy-start(bf16[1024,256]{1,0:T(8,128)(2,1)} %constant.20.clone.refs_1_) | copy-start | bytes 1572868

commit v17 on v16

--- a/solution.py
+++ b/solution.py
@@ -22,6 +22,7 @@
 TERM_ROWS = 1024
 CHUNKS = 3
 VMEM_BYTES = 40 * 1024 * 1024
+LARGE_VMEM = 60 * 1024 * 1024
 WHOLE_VMEM = 65000 * 1024
 HBM_BYTES = 100 * 1024 * 256
 
@@ -205,9 +206,7 @@
                     )
 
 
-def analyse_kernel(field, analysis, *refs):
-    weights = refs[:CHUNKS]
-    cells_out, coef_out, first_out, last_out, packed_out, _, buffer, semaphores = refs[CHUNKS:]
+def analyse_kernel(field, analysis, cells_out, coef_out, first_out, last_out, _):
     cells = to_cells(field[...])
     rounded = cells.astype(BF16)
     coef_out[...] = dot(analysis[...], rounded).astype(BF16)
@@ -215,6 +214,11 @@
     first, last = edge_layers(cells)
     first_out[...] = first
     last_out[...] = last
+
+
+def pack_kernel(*refs):
+    weights = refs[:CHUNKS]
+    packed_out, buffer, semaphores = refs[CHUNKS:]
     rows = GROUP * LANES // 4
     share = buffer.shape[0] // CHUNKS
     copies = []
@@ -453,13 +457,14 @@
         terms = terms.reshape(TERM_ROWS, LANES)
     else:
         modes, terms = received[...], sums[...].astype(F32)
-    cells = (dot(synthesis[...], modes.astype(BF16)) + local[...]).astype(BF16)
-    grad_out[...] = to_field(cells)
     half = LANES // 2
     for k in range(OFFSETS):
         row = (k // 2) * half
         lane = (k % 2) * half
-        stencil_out[k] = terms[row : row + half, lane : lane + half]
+        stencil_out.buffer[k] = terms[row : row + half, lane : lane + half]
+    stencil_out.copy.start()
+    cells = (dot(synthesis[...], modes.astype(BF16)) + local[...]).astype(BF16)
+    grad_out[...] = to_field(cells)
 
 
 def shape(dims, dtype):
@@ -625,29 +630,30 @@
         return exchange(values.reshape(devices, modes, LANES)).reshape(plane_rows, LANES)
 
     packed = shape((weights.shape[0] // 2, LANES), BF16)
-    share = weights.shape[0] // CHUNKS
     to_send = shape((devices, modes, LANES), BF16) if modes % 8 == 0 else plane_modes
-    cells, coef, first, last, kept_weights, slot = run(
+    cells, coef, first, last, slot = run(
         analyse_kernel,
-        [
-            wide,
-            plane_modes,
-            edge,
-            edge,
-            shape((HBM_BYTES // (2 * LANES), LANES), BF16),
-            to_send,
-        ],
+        [wide, plane_modes, edge, edge, to_send],
         snapshots.reshape(field.shape),
         analysis,
-        *[weights] * CHUNKS,
-        staged={0: None, 1: None} | {2 + k: slice(k * share, (k + 1) * share) for k in range(CHUNKS)},
+        staged=(0, 1),
         sent=(0, 1, 2, 3),
-        plain=(4, 5),
-        scratch=[pltpu.VMEM(packed.shape, BF16), pltpu.SemaphoreType.DMA((CHUNKS,))],
+        plain=(4,),
         limit=WHOLE_VMEM,
         flops=10**8,
     )
+    weights, coef = lax.optimization_barrier((weights, coef))
     coef = send(coef)
+    share = weights.shape[0] // CHUNKS
+    (kept_weights,) = run(
+        pack_kernel,
+        [shape((HBM_BYTES // (2 * LANES), LANES), BF16)],
+        *[weights] * CHUNKS,
+        staged={k: slice(k * share, (k + 1) * share) for k in range(CHUNKS)},
+        plain=(0,),
+        scratch=[pltpu.VMEM(packed.shape, BF16), pltpu.SemaphoreType.DMA((CHUNKS,))],
+        limit=LARGE_VMEM,
+    )
     (packed_weights,) = run(fetch_kernel, [packed], kept_weights, moved={0: 0})
     before, after = neighbours(first, last)
     local, lanes, outer_cells = run(
@@ -756,6 +762,7 @@
         sums,
         np.ascontiguousarray(analysis.T),
         local,
+        sent=(1,),
         flops=10**8,
     )
     return (

time: 69.6 us -> 72.4 us (1.040)
  Pallas kernels: 21.6 us -> 24.4 us
  waiting for transfers between devices: 21 us -> 18.4 us
  starting transfers between devices: 25.6 us -> 28.1 us
    pallas_call x10 -> x11, Pallas kernels: 21.6 us -> 24.4 us  [run(): pl.pallas_call(kernel, out_shape=results, in_specs=[in_hbm if k in staged...]
    all_to_all x4, waiting for transfers between devices: 20.1 us -> 17.6 us  [exchange(): lax.all_to_all(values, ('space', 'batch'), split_axis=0, concat_axis=0, t...]
    all_to_all x4, starting transfers between devices: 18.8 us -> 21.3 us  [exchange(): lax.all_to_all(values, ('space', 'batch'), split_axis=0, concat_axis=0, t...]
  transfers between devices with their start and end apart: 8 -> 8, of which waited for: 5 -> 4; matrix products, arithmetic and copies ran while one was open for 0% -> 0% of each run, Pallas kernels for 18% -> 21%
where the time goes in v17:
time: 72.4 us; the launch traced here: 71.9 us
  starting transfers between devices  28.1 us (39%)
  Pallas kernels  24.4 us (34%)
  waiting for transfers between devices  18.4 us (25%)
  between operations  0.9 us (1%)
    pallas_call x11, Pallas kernels, run(): pl.pallas_call(kernel, out_shape=results, in_specs=[in_hbm if k in staged...  24.4 us
    all_to_all x4, starting transfers between devices, exchange(): lax.all_to_all(values, ('space', 'batch'), split_axis=0, concat_axis=0, t...  21.3 us
    all_to_all x4, waiting for transfers between devices, exchange(): lax.all_to_all(values, ('space', 'batch'), split_axis=0, concat_axis=0, t...  17.6 us
    ppermute x2, starting transfers between devices, neighbours(): before = lax.ppermute(last, 'space', [(i, i + 1) for i in range(ends)])  4.19 us
    ppermute x2, starting transfers between devices, neighbours(): after = lax.ppermute(first, 'space', [(i + 1, i) for i in range(ends)])  2.58 us
  transfers between devices with their start and end apart: 8, of which 4 were waited for; matrix products, arithmetic and copies ran while one was open for 0% of the time, Pallas kernels for 21%

profile of v17, /device:TPU:0, one launch (start us, length us, event | category | flops | bytes accessed | tf_op | source)
XLA Modules:
  0.0 71.9 jit_solution(9027437867795794160)
XLA Ops:
  0.6 2.5 %analyse_kernel.1 = (bf16[1024,128]{1,0:T(8,128)(2,1)}, bf16[256,128]{1,0:T(8,128)(2,1)}, bf16[512,128]{1,0:T(8,128)(2,1)}, bf16[512,128]{1,0:T(8,128)(2,1)}, bf16[32,8,128]{2,1,0:T(8,128)(2,1)}) custom-call(bf16[64,2,1024]{2,1,0:T(2,128)(2,1)} %bitcast.22, bf16[256,1024]{1,0:T(8,128)(2,1)} %constant.14.clone.refs_1_), custom_call_target="tpu_custom_call" | custom-call | flops 100000000 | bytes 1441792 | tf_op jit(solution)/shard_map/analyse_kernel/pallas_call | solution.py:580
  3.1 7.3 %all-to-all-start = ((bf16[32,8,128]{2,1,0:T(8,128)(2,1)}), bf16[32,8,128]{2,1,0:T(8,128)(2,1)S(1)}, u32[]{:S(2)}, u32[]{:S(2)}) async-start(bf16[32,8,128]{2,1,0:T(8,128)(2,1)} %bitcast.23), calls=%async_computation | async-start | bytes 131072 | tf_op jit(solution)/shard_map/all_to_all | solution.py:597
  10.4 2.2 %collective-permute-start = (bf16[512,128]{1,0:T(8,128)(2,1)}, bf16[512,128]{1,0:T(8,128)(2,1)S(1)}, u32[]{:S(2)}, u32[]{:S(2)}) collective-permute-start(bf16[512,128]{1,0:T(8,128)(2,1)} %get-tuple-element.38), channel_id=1, source_target_pairs={{0,1},{1,2},{2,3},{3,4},{4,5},{5,6},{6,7},{7,8},{8,9},{9,10},{10,1... | collective-permute-start | bytes 393224 | tf_op jit(solution)/shard_map/ppermute | solution.py:602
  12.6 1.3 %collective-permute-start.1 = (bf16[512,128]{1,0:T(8,128)(2,1)}, bf16[512,128]{1,0:T(8,128)(2,1)S(1)}, u32[]{:S(2)}, u32[]{:S(2)}) collective-permute-start(bf16[512,128]{1,0:T(8,128)(2,1)} %get-tuple-element.39), channel_id=1, source_target_pairs={{1,0},{2,1},{3,2},{4,3},{5,4},{6,5},{7,6},{8,7},{9,8},{10,9},{11,1... | collective-permute-start | bytes 393224 | tf_op jit(solution)/shard_map/ppermute | solution.py:603
  13.9 2.9 %pack_kernel.1.refs_0_.refs_1_ = bf16[102400,128]{1,0:T(8,128)(2,1)} custom-call(bf16[12288,64]{1,0:T(8,128)(2,1)} %bitcast.18, bf16[12288,64]{1,0:T(8,128)(2,1)} %bitcast.19, bf16[12288,64]{1,0:T(8,128)(2,1)} %bitcast.20), custom_call_target="tpu_custom_call" | custom-call | bytes 30932992 | tf_op jit(solution)/shard_map/pack_kernel/pallas_call | solution.py:580
  16.8 0.0 copy-start.4
  16.8 0.0 copy-start.5
  16.8 0.0 copy-start.1
  16.9 0.0 copy-start.6
  16.9 0.0 copy-start.7
  16.9 1.5 %fetch_kernel.1.refs_2_ = bf16[6144,128]{1,0:T(8,128)(2,1)S(1)} custom-call(bf16[102400,128]{1,0:T(8,128)(2,1)} %pack_kernel.1.refs_0_.refs_1_), custom_call_target="tpu_custom_call" | custom-call | bytes 27787264 | tf_op jit(solution)/shard_map/fetch_kernel/pallas_call | solution.py:580
  18.4 0.0 all-to-all-done
  18.4 0.0 copy-done.4
  18.4 0.0 copy-done.5
  18.4 1.8 %mix_kernel.1 = (bf16[32,8,128]{2,1,0:T(8,128)(2,1)}, bf16[384,256]{1,0:T(8,128)(2,1)S(1)}) custom-call(bf16[256,128]{1,0:T(8,128)(2,1)S(1)} %bitcast.15, bf16[192,256]{1,0:T(8,128)(2,1)S(1)} %copy-done.5, bf16[6144,128]{1,0:T(8,128)(2,1)S(1)} %fetch_kernel.1.refs_2_, bf16[128,384]{1,0:T(8,128)(2,1)S(1)} %copy-done.4, ...), custom_call_target="tpu_custom_call", output_to_operand_aliasing={{0}: (4, {})} | custom-call | flops 400000000 | bytes 2097152 | tf_op jit(solution)/shard_map/mix_kernel/pallas_call | solution.py:580
  20.2 7.9 %all-to-all-start.1 = ((bf16[32,8,128]{2,1,0:T(8,128)(2,1)}), bf16[32,8,128]{2,1,0:T(8,128)(2,1)S(1)}, u32[]{:S(2)}, u32[]{:S(2)}) async-start(bf16[32,8,128]{2,1,0:T(8,128)(2,1)} %get-tuple-element.36), calls=%async_computation.1 | async-start | bytes 131072 | tf_op jit(solution)/shard_map/all_to_all | solution.py:597
  28.2 0.0 collective-permute-done.refs_1_
  28.2 0.0 collective-permute-done.1.refs_2_
  28.2 0.0 copy-done.1
  28.2 0.0 copy-done.6
  28.2 0.0 copy-done.7
  28.2 0.0 copy-start.8
  28.2 1.2 %local_kernel.1 = (f32[1024,128]{1,0:T(8,128)S(1)}, bf16[256,1024]{1,0:T(8,128)(2,1)S(1)}, bf16[1024,128]{1,0:T(8,128)(2,1)S(1)}) custom-call(bf16[1024,128]{1,0:T(8,128)(2,1)S(1)} %copy-done.7, bf16[512,128]{1,0:T(8,128)(2,1)S(1)} %collective-permute-done.refs_1_, bf16[512,128]{1,0:T(8,128)(2,1)S(1)} %collective-permute-done.1.refs_2_, ...), custom_call_target="tpu_custom_call" | custom-call | flops 8000000000 | bytes 2318336 | tf_op jit(solution)/shard_map/local_kernel/pallas_call | solution.py:580
  29.4 6.4 %all-to-all-done.1 = bf16[32,8,128]{2,1,0:T(8,128)(2,1)S(1)} async-done(((bf16[32,8,128]{2,1,0:T(8,128)(2,1)}), bf16[32,8,128]{2,1,0:T(8,128)(2,1)S(1)}, u32[]{:S(2)}, u32[]{:S(2)}) %all-to-all-start.1) | async-done | bytes 65568 | tf_op jit(solution)/shard_map/all_to_all | solution.py:597
  35.8 0.0 copy-done.8
  35.8 2.6 %activate_kernel.1 = (bf16[1024,128]{1,0:T(8,128)(2,1)S(1)}, bf16[102400,128]{1,0:T(8,128)(2,1)}, bf16[512,128]{1,0:T(8,128)(2,1)S(1)}, bf16[512,128]{1,0:T(8,128)(2,1)S(1)}, bf16[32,40,128]{2,1,0:T(8,128)(2,1)}) custom-call(bf16[256,128]{1,0:T(8,128)(2,1)S(1)} %bitcast.16, bf16[1024,256]{1,0:T(8,128)(2,1)S(1)} %copy-done.8, ...), custom_call_target="tpu_custom_call" | custom-call | flops 1000000000 | bytes 28966912 | tf_op jit(solution)/shard_map/activate_kernel/pallas_call | solution.py:580
  38.4 2.6 %all-to-all-start.2 = ((bf16[32,40,128]{2,1,0:T(8,128)(2,1)}), bf16[32,40,128]{2,1,0:T(8,128)(2,1)S(1)}, u32[]{:S(2)}, u32[]{:S(2)}) async-start(bf16[32,40,128]{2,1,0:T(8,128)(2,1)} %get-tuple-element.43), calls=%async_computation.2 | async-start | bytes 655360 | tf_op jit(solution)/shard_map/all_to_all | solution.py:597
  41.0 2.0 %collective-permute-start.2 = (bf16[512,128]{1,0:T(8,128)(2,1)S(1)}, bf16[512,128]{1,0:T(8,128)(2,1)S(1)}, u32[]{:S(2)}, u32[]{:S(2)}) collective-permute-start(bf16[512,128]{1,0:T(8,128)(2,1)S(1)} %get-tuple-element.44), channel_id=1, source_target_pairs={{0,1},{1,2},{2,3},{3,4},{4,5},{5,6},{6,7},{7,8},{8,9},{9,10},{10,1... | collective-permute-start | bytes 393224 | tf_op jit(solution)/shard_map/ppermute | solution.py:602
  43.1 1.3 %collective-permute-start.3 = (bf16[512,128]{1,0:T(8,128)(2,1)S(1)}, bf16[512,128]{1,0:T(8,128)(2,1)S(1)}, u32[]{:S(2)}, u32[]{:S(2)}) collective-permute-start(bf16[512,128]{1,0:T(8,128)(2,1)S(1)} %get-tuple-element.45), channel_id=1, source_target_pairs={{1,0},{2,1},{3,2},{4,3},{5,4},{6,5},{7,6},{8,7},{9,8},{10,9},{11,1... | collective-permute-start | bytes 393224 | tf_op jit(solution)/shard_map/ppermute | solution.py:603
  44.4 0.0 copy-start.2
  44.4 0.0 copy-start.3
  44.4 2.2 %output_kernel.1 = (bf16[64,2,1024]{2,1,0:T(2,128)(2,1)}, bf16[6144,128]{1,0:T(8,128)(2,1)S(1)}) custom-call(bf16[1024,128]{1,0:T(8,128)(2,1)S(1)} %get-tuple-element.46.refs_0_, bf16[102400,128]{1,0:T(8,128)(2,1)} %pack_kernel.1.refs_0_.refs_1_), custom_call_target="tpu_custom_call" | custom-call | flops 100000000 | bytes 28311552 | tf_op jit(solution)/shard_map/output_kernel/pallas_call | solution.py:580
  46.6 0.0 collective-permute-done.2.refs_1_
  46.6 0.9 %collective-permute-done.3.refs_2_ = bf16[512,128]{1,0:T(8,128)(2,1)S(1)} collective-permute-done((bf16[512,128]{1,0:T(8,128)(2,1)S(1)}, bf16[512,128]{1,0:T(8,128)(2,1)S(1)}, u32[]{:S(2)}, u32[]{:S(2)}) %collective-permute-start.3) | collective-permute-done | bytes 131104 | tf_op jit(solution)/shard_map/ppermute | solution.py:603
  47.5 5.3 %all-to-all-done.2.refs_0_ = bf16[32,40,128]{2,1,0:T(8,128)(2,1)S(1)} async-done(((bf16[32,40,128]{2,1,0:T(8,128)(2,1)}), bf16[32,40,128]{2,1,0:T(8,128)(2,1)S(1)}, u32[]{:S(2)}, u32[]{:S(2)}) %all-to-all-start.2) | async-done | bytes 327712 | tf_op jit(solution)/shard_map/all_to_all | solution.py:597
  52.8 0.0 copy-done.2
  52.8 0.0 copy-done.3
  52.8 1.8 %unmix_kernel.1 = (bf16[32,40,128]{2,1,0:T(8,128)(2,1)}, bf16[384,128]{1,0:T(8,128)(2,1)S(1)}) custom-call(bf16[32,40,128]{2,1,0:T(8,128)(2,1)S(1)} %all-to-all-done.2.refs_0_, bf16[192,256]{1,0:T(8,128)(2,1)S(1)} %copy-done.3, bf16[6144,128]{1,0:T(8,128)(2,1)S(1)} %get-tuple-element.51.refs_2_, bf16[128,384]{1,0:T(8,128)(2,1)S(1)} %copy-done.2), custom_call_target="tpu_custom_call" | custom-call | flops 400000000 | bytes 2523136 | tf_op jit(solution)/shard_map/unmix_kernel/pallas_call | solution.py:580
  54.6 3.5 %all-to-all-start.3 = ((bf16[32,40,128]{2,1,0:T(8,128)(2,1)}), bf16[32,40,128]{2,1,0:T(8,128)(2,1)S(1)}, u32[]{:S(2)}, u32[]{:S(2)}) async-start(bf16[32,40,128]{2,1,0:T(8,128)(2,1)} %get-tuple-element.52), calls=%async_computation.3 | async-start | bytes 655360 | tf_op jit(solution)/shard_map/all_to_all | solution.py:597
  58.1 3.7 %weight_kernel.1 = f32[12288,64]{1,0:T(8,128)} custom-call(bf16[384,256]{1,0:T(8,128)(2,1)S(1)} %get-tuple-element.57.refs_0_, bf16[384,128]{1,0:T(8,128)(2,1)S(1)} %get-tuple-element.58.refs_1_), custom_call_target="tpu_custom_call" | custom-call | flops 400000000 | bytes 3440640 | tf_op jit(solution)/shard_map/weight_kernel/pallas_call | solution.py:580
  61.8 0.0 copy-start
  61.8 2.1 %local_grad_kernel.1.refs_2_ = f32[1024,128]{1,0:T(8,128)S(1)} custom-call(bf16[102400,128]{1,0:T(8,128)(2,1)} %get-tuple-element.53.refs_0_, bf16[512,128]{1,0:T(8,128)(2,1)S(1)} %collective-permute-done.2.refs_1_, bf16[512,128]{1,0:T(8,128)(2,1)S(1)} %collective-permute-done.3.refs_2_, bf16[27,64,64]{2,1,0:T(8,128)(2,1)S(1)} %bitcast.14), custom_call_target="tpu_custom_call" | custom-call | flops 700000000 | bytes 27222016 | tf_op jit(solution)/shard_map/local_grad_kernel/pallas_call | solution.py:580
  63.9 5.9 %all-to-all-done.3.refs_0_ = bf16[32,40,128]{2,1,0:T(8,128)(2,1)S(1)} async-done(((bf16[32,40,128]{2,1,0:T(8,128)(2,1)}), bf16[32,40,128]{2,1,0:T(8,128)(2,1)S(1)}, u32[]{:S(2)}, u32[]{:S(2)}) %all-to-all-start.3) | async-done | bytes 327712 | tf_op jit(solution)/shard_map/all_to_all | solution.py:597
  69.8 0.0 copy-done
  69.8 2.1 %finish_kernel.1 = (bf16[64,2,1024]{2,1,0:T(2,128)(2,1)}, f32[27,64,64]{2,1,0:T(8,128)}) custom-call(bf16[32,40,128]{2,1,0:T(8,128)(2,1)S(1)} %all-to-all-done.3.refs_0_, bf16[1024,256]{1,0:T(8,128)(2,1)S(1)} %copy-done, f32[1024,128]{1,0:T(8,128)S(1)} %local_grad_kernel.1.refs_2_), custom_call_target="tpu_custom_call" | custom-call | flops 100000000 | bytes 2080768 | tf_op jit(solution)/shard_map/finish_kernel/pallas_call | solution.py:580
Async XLA Ops:
  3.1 15.3 %all-to-all-start = ((bf16[32,8,128]{2,1,0:T(8,128)(2,1)}), bf16[32,8,128]{2,1,0:T(8,128)(2,1)S(1)}, u32[]{:S(2)}, u32[]{:S(2)}) async-start(bf16[32,8,128]{2,1,0:T(8,128)(2,1)} %bitcast.23), calls=%async_computation | async-start | bytes 131072 | tf_op jit(solution)/shard_map/all_to_all | solution.py:597
  10.4 17.7 %collective-permute-start = (bf16[512,128]{1,0:T(8,128)(2,1)}, bf16[512,128]{1,0:T(8,128)(2,1)S(1)}, u32[]{:S(2)}, u32[]{:S(2)}) collective-permute-start(bf16[512,128]{1,0:T(8,128)(2,1)} %get-tuple-element.38), channel_id=1, source_target_pairs={{0,1},{1,2},{2,3},{3,4},{4,5},{5,6},{6,7},{7,8},{8,9},{9,10},{10,1... | collective-permute-start | bytes 393224 | tf_op jit(solution)/shard_map/ppermute | solution.py:602
  12.6 15.6 %collective-permute-start.1 = (bf16[512,128]{1,0:T(8,128)(2,1)}, bf16[512,128]{1,0:T(8,128)(2,1)S(1)}, u32[]{:S(2)}, u32[]{:S(2)}) collective-permute-start(bf16[512,128]{1,0:T(8,128)(2,1)} %get-tuple-element.39), channel_id=1, source_target_pairs={{1,0},{2,1},{3,2},{4,3},{5,4},{6,5},{7,6},{8,7},{9,8},{10,9},{11,1... | collective-permute-start | bytes 393224 | tf_op jit(solution)/shard_map/ppermute | solution.py:603
  16.8 1.6 %copy-start.4 = (bf16[128,384]{1,0:T(8,128)(2,1)S(1)}, bf16[128,384]{1,0:T(8,128)(2,1)}, u32[]{:S(2)}) copy-start(bf16[128,384]{1,0:T(8,128)(2,1)} %constant.16.clone.refs_3_) | copy-start | bytes 294916
  16.8 1.6 %copy-start.5 = (bf16[192,256]{1,0:T(8,128)(2,1)S(1)}, bf16[192,256]{1,0:T(8,128)(2,1)}, u32[]{:S(2)}) copy-start(bf16[192,256]{1,0:T(8,128)(2,1)} %constant.15.clone.refs_1_) | copy-start | bytes 294916
  16.8 11.3 %copy-start.1 = (bf16[3,3,3,64,64]{4,3,2,1,0:T(8,128)(2,1)S(1)}, bf16[3,3,3,64,64]{4,3,2,1,0:T(8,128)(2,1)}, u32[]{:S(2)}) copy-start(bf16[3,3,3,64,64]{4,3,2,1,0:T(8,128)(2,1)} %param.14) | copy-start | bytes 663556
  16.9 11.3 %copy-start.6 = (bf16[1,64,2,1024]{3,2,1,0:T(2,128)(2,1)S(1)}, bf16[1,64,2,1024]{3,2,1,0:T(2,128)(2,1)}, u32[]{:S(2)}) copy-start(bf16[1,64,2,1024]{3,2,1,0:T(2,128)(2,1)} %param.12) | copy-start | bytes 786436
  16.9 11.3 %copy-start.7 = (bf16[1024,128]{1,0:T(8,128)(2,1)S(1)}, bf16[1024,128]{1,0:T(8,128)(2,1)}, u32[]{:S(2)}) copy-start(bf16[1024,128]{1,0:T(8,128)(2,1)} %get-tuple-element.37.refs_0_) | copy-start | bytes 786436
  20.2 15.6 %all-to-all-start.1 = ((bf16[32,8,128]{2,1,0:T(8,128)(2,1)}), bf16[32,8,128]{2,1,0:T(8,128)(2,1)S(1)}, u32[]{:S(2)}, u32[]{:S(2)}) async-start(bf16[32,8,128]{2,1,0:T(8,128)(2,1)} %get-tuple-element.36), calls=%async_computation.1 | async-start | bytes 131072 | tf_op jit(solution)/shard_map/all_to_all | solution.py:597
  28.2 7.6 %copy-start.8 = (bf16[1024,256]{1,0:T(8,128)(2,1)S(1)}, bf16[1024,256]{1,0:T(8,128)(2,1)}, u32[]{:S(2)}) copy-start(bf16[1024,256]{1,0:T(8,128)(2,1)} %constant.17.clone.refs_1_) | copy-start | bytes 1572868
  38.4 14.3 %all-to-all-start.2 = ((bf16[32,40,128]{2,1,0:T(8,128)(2,1)}), bf16[32,40,128]{2,1,0:T(8,128)(2,1)S(1)}, u32[]{:S(2)}, u32[]{:S(2)}) async-start(bf16[32,40,128]{2,1,0:T(8,128)(2,1)} %get-tuple-element.43), calls=%async_computation.2 | async-start | bytes 655360 | tf_op jit(solution)/shard_map/all_to_all | solution.py:597
  41.0 5.6 %collective-permute-start.2 = (bf16[512,128]{1,0:T(8,128)(2,1)S(1)}, bf16[512,128]{1,0:T(8,128)(2,1)S(1)}, u32[]{:S(2)}, u32[]{:S(2)}) collective-permute-start(bf16[512,128]{1,0:T(8,128)(2,1)S(1)} %get-tuple-element.44), channel_id=1, source_target_pairs={{0,1},{1,2},{2,3},{3,4},{4,5},{5,6},{6,7},{7,8},{8,9},{9,10},{10,1... | collective-permute-start | bytes 393224 | tf_op jit(solution)/shard_map/ppermute | solution.py:602
  43.1 4.4 %collective-permute-start.3 = (bf16[512,128]{1,0:T(8,128)(2,1)S(1)}, bf16[512,128]{1,0:T(8,128)(2,1)S(1)}, u32[]{:S(2)}, u32[]{:S(2)}) collective-permute-start(bf16[512,128]{1,0:T(8,128)(2,1)S(1)} %get-tuple-element.45), channel_id=1, source_target_pairs={{1,0},{2,1},{3,2},{4,3},{5,4},{6,5},{7,6},{8,7},{9,8},{10,9},{11,1... | collective-permute-start | bytes 393224 | tf_op jit(solution)/shard_map/ppermute | solution.py:603
  44.4 8.4 %copy-start.2 = (bf16[128,384]{1,0:T(8,128)(2,1)S(1)}, bf16[128,384]{1,0:T(8,128)(2,1)}, u32[]{:S(2)}) copy-start(bf16[128,384]{1,0:T(8,128)(2,1)} %constant.19.clone.refs_3_) | copy-start | bytes 294916
  44.4 8.4 %copy-start.3 = (bf16[192,256]{1,0:T(8,128)(2,1)S(1)}, bf16[192,256]{1,0:T(8,128)(2,1)}, u32[]{:S(2)}) copy-start(bf16[192,256]{1,0:T(8,128)(2,1)} %constant.18.clone.refs_1_) | copy-start | bytes 294916
  54.6 15.2 %all-to-all-start.3 = ((bf16[32,40,128]{2,1,0:T(8,128)(2,1)}), bf16[32,40,128]{2,1,0:T(8,128)(2,1)S(1)}, u32[]{:S(2)}, u32[]{:S(2)}) async-start(bf16[32,40,128]{2,1,0:T(8,128)(2,1)} %get-tuple-element.52), calls=%async_computation.3 | async-start | bytes 655360 | tf_op jit(solution)/shard_map/all_to_all | solution.py:597
  61.8 8.0 %copy-start = (bf16[1024,256]{1,0:T(8,128)(2,1)S(1)}, bf16[1024,256]{1,0:T(8,128)(2,1)}, u32[]{:S(2)}) copy-start(bf16[1024,256]{1,0:T(8,128)(2,1)} %constant.20.clone.refs_1_) | copy-start | bytes 1572868

commit v18 on v17

--- a/solution.py
+++ b/solution.py
@@ -457,14 +457,13 @@
         terms = terms.reshape(TERM_ROWS, LANES)
     else:
         modes, terms = received[...], sums[...].astype(F32)
+    cells = (dot(synthesis[...], modes.astype(BF16)) + local[...]).astype(BF16)
+    grad_out[...] = to_field(cells)
     half = LANES // 2
     for k in range(OFFSETS):
         row = (k // 2) * half
         lane = (k % 2) * half
-        stencil_out.buffer[k] = terms[row : row + half, lane : lane + half]
-    stencil_out.copy.start()
-    cells = (dot(synthesis[...], modes.astype(BF16)) + local[...]).astype(BF16)
-    grad_out[...] = to_field(cells)
+        stencil_out[k] = terms[row : row + half, lane : lane + half]
 
 
 def shape(dims, dtype):
@@ -655,6 +654,19 @@
         limit=LARGE_VMEM,
     )
     (packed_weights,) = run(fetch_kernel, [packed], kept_weights, moved={0: 0})
+    back, diagonal = run(
+        functools.partial(mix_kernel, batches, slabs),
+        [to_send, shape((count, GROUP * half // 2), BF16)],
+        coef,
+        gather,
+        packed_weights,
+        scatter,
+        sent=(0, 1),
+        slots={0: slot},
+        flops=4 * 10**8,
+    )
+    back, first, last = lax.optimization_barrier((back, first, last))
+    back = send(back)
     before, after = neighbours(first, last)
     local, lanes, outer_cells = run(
         local_kernel,
@@ -667,18 +679,6 @@
         scratch=[padded, pltpu.VMEM((3, 2 * LANES, 3 * LANES), BF16)],
         flops=8 * 10**9,
     )
-    back, diagonal = run(
-        functools.partial(mix_kernel, batches, slabs),
-        [to_send, shape((count, GROUP * half // 2), BF16)],
-        coef,
-        gather,
-        packed_weights,
-        scatter,
-        sent=(0, 1),
-        slots={0: slot},
-        flops=4 * 10**8,
-    )
-    back = send(back)
     slab = shape((devices, 8 + TERM_ROWS // devices, LANES), BF16)
     activated, grad, first, last, back, terms = run(
         functools.partial(activate_kernel, in_slab),
@@ -762,7 +762,6 @@
         sums,
         np.ascontiguousarray(analysis.T),
         local,
-        sent=(1,),
         flops=10**8,
     )
     return (

time: 72.4 us -> 72.9 us (level)
  starting transfers between devices: 28.1 us -> 25.1 us
  waiting for transfers between devices: 18.4 us -> 20.8 us
  local copies, waits for them, and re-layouts: 0.06 us -> 1.72 us
    all_to_all x4, starting transfers between devices: 21.3 us -> 18.9 us  [exchange(): lax.all_to_all(values, ('space', 'batch'), split_axis=0, concat_axis=0, t...]
    all_to_all x4, waiting for transfers between devices: 17.6 us -> 19.9 us  [exchange(): lax.all_to_all(values, ('space', 'batch'), split_axis=0, concat_axis=0, t...]
    unnamed x18 -> x26, local copies, waits for them, and re-layouts: 0.06 us -> 1.72 us
  transfers between devices with their start and end apart: 8 -> 8, of which waited for: 4 -> 5; matrix products, arithmetic and copies ran while one was open for 0% -> 0% of each run, Pallas kernels for 21% -> 19%
where the time goes in v18:
time: 72.9 us; the launch traced here: 72.3 us
  starting transfers between devices  25.1 us (34%)
  Pallas kernels  23.8 us (33%)
  waiting for transfers between devices  20.8 us (29%)
  local copies, waits for them, and re-layouts  1.72 us (2%)
  between operations  0.92 us (1%)
    pallas_call x11, Pallas kernels, run(): pl.pallas_call(kernel, out_shape=results, in_specs=[in_hbm if k in staged...  23.8 us
    all_to_all x4, waiting for transfers between devices, exchange(): lax.all_to_all(values, ('space', 'batch'), split_axis=0, concat_axis=0, t...  19.9 us
    all_to_all x4, starting transfers between devices, exchange(): lax.all_to_all(values, ('space', 'batch'), split_axis=0, concat_axis=0, t...  18.9 us
    ppermute x2, starting transfers between devices, neighbours(): before = lax.ppermute(last, 'space', [(i, i + 1) for i in range(ends)])  3.62 us
    ppermute x2, starting transfers between devices, neighbours(): after = lax.ppermute(first, 'space', [(i + 1, i) for i in range(ends)])  2.58 us
    unnamed x26, local copies, waits for them, and re-layouts  1.72 us
  transfers between devices with their start and end apart: 8, of which 5 were waited for; matrix products, arithmetic and copies ran while one was open for 0% of the time, Pallas kernels for 19%

profile of v18, /device:TPU:0, one launch (start us, length us, event | category | flops | bytes accessed | tf_op | source)
XLA Modules:
  0.0 72.3 jit_solution(16039421917747138288)
XLA Ops:
  0.6 2.5 %analyse_kernel.1 = (bf16[1024,128]{1,0:T(8,128)(2,1)}, bf16[256,128]{1,0:T(8,128)(2,1)}, bf16[512,128]{1,0:T(8,128)(2,1)}, bf16[512,128]{1,0:T(8,128)(2,1)}, bf16[32,8,128]{2,1,0:T(8,128)(2,1)}) custom-call(bf16[64,2,1024]{2,1,0:T(2,128)(2,1)} %bitcast.22, bf16[256,1024]{1,0:T(8,128)(2,1)} %constant.14.clone.refs_1_), custom_call_target="tpu_custom_call" | custom-call | flops 100000000 | bytes 1441792 | tf_op jit(solution)/shard_map/analyse_kernel/pallas_call | solution.py:579
  3.1 7.3 %all-to-all-start = ((bf16[32,8,128]{2,1,0:T(8,128)(2,1)}), bf16[32,8,128]{2,1,0:T(8,128)(2,1)S(1)}, u32[]{:S(2)}, u32[]{:S(2)}) async-start(bf16[32,8,128]{2,1,0:T(8,128)(2,1)} %bitcast.23), calls=%async_computation | async-start | bytes 131072 | tf_op jit(solution)/shard_map/all_to_all | solution.py:596
  10.4 2.9 %pack_kernel.1.refs_0_.refs_1_ = bf16[102400,128]{1,0:T(8,128)(2,1)} custom-call(bf16[12288,64]{1,0:T(8,128)(2,1)} %bitcast.18, bf16[12288,64]{1,0:T(8,128)(2,1)} %bitcast.19, bf16[12288,64]{1,0:T(8,128)(2,1)} %bitcast.20), custom_call_target="tpu_custom_call" | custom-call | bytes 30932992 | tf_op jit(solution)/shard_map/pack_kernel/pallas_call | solution.py:579
  13.4 0.0 copy-start.4
  13.4 0.0 copy-start.5
  13.4 0.0 copy-start.12
  13.4 0.0 copy-start.11
  13.4 0.0 copy-start.1
  13.4 0.0 copy-start.6
  13.4 0.0 copy-start.7
  13.4 1.5 %fetch_kernel.1.refs_2_ = bf16[6144,128]{1,0:T(8,128)(2,1)S(1)} custom-call(bf16[102400,128]{1,0:T(8,128)(2,1)} %pack_kernel.1.refs_0_.refs_1_), custom_call_target="tpu_custom_call" | custom-call | bytes 27787264 | tf_op jit(solution)/shard_map/fetch_kernel/pallas_call | solution.py:579
  15.0 3.0 %all-to-all-done = bf16[32,8,128]{2,1,0:T(8,128)(2,1)S(1)} async-done(((bf16[32,8,128]{2,1,0:T(8,128)(2,1)}), bf16[32,8,128]{2,1,0:T(8,128)(2,1)S(1)}, u32[]{:S(2)}, u32[]{:S(2)}) %all-to-all-start) | async-done | bytes 65568 | tf_op jit(solution)/shard_map/all_to_all | solution.py:596
  18.0 0.0 copy-done.4
  18.0 0.0 copy-done.5
  18.0 1.8 %mix_kernel.1 = (bf16[32,8,128]{2,1,0:T(8,128)(2,1)}, bf16[384,256]{1,0:T(8,128)(2,1)S(1)}) custom-call(bf16[256,128]{1,0:T(8,128)(2,1)S(1)} %bitcast.15, bf16[192,256]{1,0:T(8,128)(2,1)S(1)} %copy-done.5, bf16[6144,128]{1,0:T(8,128)(2,1)S(1)} %fetch_kernel.1.refs_2_, bf16[128,384]{1,0:T(8,128)(2,1)S(1)} %copy-done.4, ...), custom_call_target="tpu_custom_call", output_to_operand_aliasing={{0}: (4, {})} | custom-call | flops 400000000 | bytes 2097152 | tf_op jit(solution)/shard_map/mix_kernel/pallas_call | solution.py:579
  19.8 0.0 copy-done.12
  19.8 1.6 %collective-permute-start = (bf16[512,128]{1,0:T(8,128)(2,1)S(1)}, bf16[512,128]{1,0:T(8,128)(2,1)S(1)}, u32[]{:S(2)}, u32[]{:S(2)}) collective-permute-start(bf16[512,128]{1,0:T(8,128)(2,1)S(1)} %copy-done.12), channel_id=1, source_target_pairs={{0,1},{1,2},{2,3},{3,4},{4,5},{5,6},{6,7},{7,8},{8,9},{9,10},{10,1... | collective-permute-start | bytes 393224 | tf_op jit(solution)/shard_map/ppermute | solution.py:601
  21.4 0.0 copy-done.11
  21.4 1.3 %collective-permute-start.1 = (bf16[512,128]{1,0:T(8,128)(2,1)S(1)}, bf16[512,128]{1,0:T(8,128)(2,1)S(1)}, u32[]{:S(2)}, u32[]{:S(2)}) collective-permute-start(bf16[512,128]{1,0:T(8,128)(2,1)S(1)} %copy-done.11), channel_id=1, source_target_pairs={{1,0},{2,1},{3,2},{4,3},{5,4},{6,5},{7,6},{8,7},{9,8},{10,9},{11,1... | collective-permute-start | bytes 393224 | tf_op jit(solution)/shard_map/ppermute | solution.py:602
  22.7 5.5 %all-to-all-start.1 = ((bf16[32,8,128]{2,1,0:T(8,128)(2,1)}), bf16[32,8,128]{2,1,0:T(8,128)(2,1)S(1)}, u32[]{:S(2)}, u32[]{:S(2)}) async-start(bf16[32,8,128]{2,1,0:T(8,128)(2,1)} %get-tuple-element.42), calls=%async_computation.1 | async-start | bytes 131072 | tf_op jit(solution)/shard_map/all_to_all | solution.py:596
  28.2 0.0 collective-permute-done.refs_1_
  28.3 0.0 collective-permute-done.1.refs_2_
  28.3 0.0 copy-done.1
  28.3 0.0 copy-done.6
  28.3 0.0 copy-done.7
  28.3 0.0 copy-start.8
  28.3 1.2 %local_kernel.1 = (f32[1024,128]{1,0:T(8,128)S(1)}, bf16[256,1024]{1,0:T(8,128)(2,1)S(1)}, bf16[1024,128]{1,0:T(8,128)(2,1)S(1)}) custom-call(bf16[1024,128]{1,0:T(8,128)(2,1)S(1)} %copy-done.7, bf16[512,128]{1,0:T(8,128)(2,1)S(1)} %collective-permute-done.refs_1_, bf16[512,128]{1,0:T(8,128)(2,1)S(1)} %collective-permute-done.1.refs_2_, ...), custom_call_target="tpu_custom_call" | custom-call | flops 8000000000 | bytes 2318336 | tf_op jit(solution)/shard_map/local_kernel/pallas_call | solution.py:579
  29.5 0.0 copy-start.9
  29.5 0.7 copy-done.9
  30.2 5.7 %all-to-all-done.1 = bf16[32,8,128]{2,1,0:T(8,128)(2,1)S(1)} async-done(((bf16[32,8,128]{2,1,0:T(8,128)(2,1)}), bf16[32,8,128]{2,1,0:T(8,128)(2,1)S(1)}, u32[]{:S(2)}, u32[]{:S(2)}) %all-to-all-start.1) | async-done | bytes 65568 | tf_op jit(solution)/shard_map/all_to_all | solution.py:596
  35.9 0.0 copy-done.8
  35.9 0.0 copy-start.10
  35.9 0.9 %copy-done.10 = bf16[1024,128]{1,0:T(8,128)(2,1)S(1)} copy-done((bf16[1024,128]{1,0:T(8,128)(2,1)S(1)}, bf16[1024,128]{1,0:T(8,128)(2,1)}, u32[]{:S(2)}) %copy-start.10) | copy-done | bytes 262168
  36.8 2.6 %activate_kernel.1 = (bf16[1024,128]{1,0:T(8,128)(2,1)S(1)}, bf16[102400,128]{1,0:T(8,128)(2,1)}, bf16[512,128]{1,0:T(8,128)(2,1)S(1)}, bf16[512,128]{1,0:T(8,128)(2,1)S(1)}, bf16[32,40,128]{2,1,0:T(8,128)(2,1)}) custom-call(bf16[256,128]{1,0:T(8,128)(2,1)S(1)} %bitcast.16, bf16[1024,256]{1,0:T(8,128)(2,1)S(1)} %copy-done.8, ...), custom_call_target="tpu_custom_call" | custom-call | flops 1000000000 | bytes 28966912 | tf_op jit(solution)/shard_map/activate_kernel/pallas_call | solution.py:579
  39.5 2.6 %all-to-all-start.2 = ((bf16[32,40,128]{2,1,0:T(8,128)(2,1)}), bf16[32,40,128]{2,1,0:T(8,128)(2,1)S(1)}, u32[]{:S(2)}, u32[]{:S(2)}) async-start(bf16[32,40,128]{2,1,0:T(8,128)(2,1)} %get-tuple-element.49), calls=%async_computation.2 | async-start | bytes 655360 | tf_op jit(solution)/shard_map/all_to_all | solution.py:596
  42.1 2.0 %collective-permute-start.2 = (bf16[512,128]{1,0:T(8,128)(2,1)S(1)}, bf16[512,128]{1,0:T(8,128)(2,1)S(1)}, u32[]{:S(2)}, u32[]{:S(2)}) collective-permute-start(bf16[512,128]{1,0:T(8,128)(2,1)S(1)} %get-tuple-element.50), channel_id=1, source_target_pairs={{0,1},{1,2},{2,3},{3,4},{4,5},{5,6},{6,7},{7,8},{8,9},{9,10},{10,1... | collective-permute-start | bytes 393224 | tf_op jit(solution)/shard_map/ppermute | solution.py:601
  44.1 1.3 %collective-permute-start.3 = (bf16[512,128]{1,0:T(8,128)(2,1)S(1)}, bf16[512,128]{1,0:T(8,128)(2,1)S(1)}, u32[]{:S(2)}, u32[]{:S(2)}) collective-permute-start(bf16[512,128]{1,0:T(8,128)(2,1)S(1)} %get-tuple-element.51), channel_id=1, source_target_pairs={{1,0},{2,1},{3,2},{4,3},{5,4},{6,5},{7,6},{8,7},{9,8},{10,9},{11,1... | collective-permute-start | bytes 393224 | tf_op jit(solution)/shard_map/ppermute | solution.py:602
  45.4 0.0 copy-start.2
  45.4 0.0 copy-start.3
  45.4 2.2 %output_kernel.1 = (bf16[64,2,1024]{2,1,0:T(2,128)(2,1)}, bf16[6144,128]{1,0:T(8,128)(2,1)S(1)}) custom-call(bf16[1024,128]{1,0:T(8,128)(2,1)S(1)} %get-tuple-element.52.refs_0_, bf16[102400,128]{1,0:T(8,128)(2,1)} %pack_kernel.1.refs_0_.refs_1_), custom_call_target="tpu_custom_call" | custom-call | flops 100000000 | bytes 28311552 | tf_op jit(solution)/shard_map/output_kernel/pallas_call | solution.py:579
  47.6 0.0 collective-permute-done.2.refs_1_
  47.6 0.9 %collective-permute-done.3.refs_2_ = bf16[512,128]{1,0:T(8,128)(2,1)S(1)} collective-permute-done((bf16[512,128]{1,0:T(8,128)(2,1)S(1)}, bf16[512,128]{1,0:T(8,128)(2,1)S(1)}, u32[]{:S(2)}, u32[]{:S(2)}) %collective-permute-start.3) | collective-permute-done | bytes 131104 | tf_op jit(solution)/shard_map/ppermute | solution.py:602
  48.5 5.3 %all-to-all-done.2.refs_0_ = bf16[32,40,128]{2,1,0:T(8,128)(2,1)S(1)} async-done(((bf16[32,40,128]{2,1,0:T(8,128)(2,1)}), bf16[32,40,128]{2,1,0:T(8,128)(2,1)S(1)}, u32[]{:S(2)}, u32[]{:S(2)}) %all-to-all-start.2) | async-done | bytes 327712 | tf_op jit(solution)/shard_map/all_to_all | solution.py:596
  53.8 0.0 copy-done.2
  53.8 0.0 copy-done.3
  53.8 1.8 %unmix_kernel.1 = (bf16[32,40,128]{2,1,0:T(8,128)(2,1)}, bf16[384,128]{1,0:T(8,128)(2,1)S(1)}) custom-call(bf16[32,40,128]{2,1,0:T(8,128)(2,1)S(1)} %all-to-all-done.2.refs_0_, bf16[192,256]{1,0:T(8,128)(2,1)S(1)} %copy-done.3, bf16[6144,128]{1,0:T(8,128)(2,1)S(1)} %get-tuple-element.57.refs_2_, bf16[128,384]{1,0:T(8,128)(2,1)S(1)} %copy-done.2), custom_call_target="tpu_custom_call" | custom-call | flops 400000000 | bytes 2523136 | tf_op jit(solution)/shard_map/unmix_kernel/pallas_call | solution.py:579
  55.6 3.5 %all-to-all-start.3 = ((bf16[32,40,128]{2,1,0:T(8,128)(2,1)}), bf16[32,40,128]{2,1,0:T(8,128)(2,1)S(1)}, u32[]{:S(2)}, u32[]{:S(2)}) async-start(bf16[32,40,128]{2,1,0:T(8,128)(2,1)} %get-tuple-element.58), calls=%async_computation.3 | async-start | bytes 655360 | tf_op jit(solution)/shard_map/all_to_all | solution.py:596
  59.1 3.7 %weight_kernel.1 = f32[12288,64]{1,0:T(8,128)} custom-call(bf16[384,256]{1,0:T(8,128)(2,1)S(1)} %get-tuple-element.63.refs_0_, bf16[384,128]{1,0:T(8,128)(2,1)S(1)} %get-tuple-element.64.refs_1_), custom_call_target="tpu_custom_call" | custom-call | flops 400000000 | bytes 3440640 | tf_op jit(solution)/shard_map/weight_kernel/pallas_call | solution.py:579
  62.8 0.0 copy-start
  62.8 2.1 %local_grad_kernel.1.refs_2_ = f32[1024,128]{1,0:T(8,128)S(1)} custom-call(bf16[102400,128]{1,0:T(8,128)(2,1)} %get-tuple-element.59.refs_0_, bf16[512,128]{1,0:T(8,128)(2,1)S(1)} %collective-permute-done.2.refs_1_, bf16[512,128]{1,0:T(8,128)(2,1)S(1)} %collective-permute-done.3.refs_2_, bf16[27,64,64]{2,1,0:T(8,128)(2,1)S(1)} %bitcast.14), custom_call_target="tpu_custom_call" | custom-call | flops 700000000 | bytes 27222016 | tf_op jit(solution)/shard_map/local_grad_kernel/pallas_call | solution.py:579
  64.9 5.9 %all-to-all-done.3.refs_0_ = bf16[32,40,128]{2,1,0:T(8,128)(2,1)S(1)} async-done(((bf16[32,40,128]{2,1,0:T(8,128)(2,1)}), bf16[32,40,128]{2,1,0:T(8,128)(2,1)S(1)}, u32[]{:S(2)}, u32[]{:S(2)}) %all-to-all-start.3) | async-done | bytes 327712 | tf_op jit(solution)/shard_map/all_to_all | solution.py:596
  70.8 0.0 copy-done
  70.8 1.5 %finish_kernel.1 = (bf16[64,2,1024]{2,1,0:T(2,128)(2,1)}, f32[27,64,64]{2,1,0:T(8,128)}) custom-call(bf16[32,40,128]{2,1,0:T(8,128)(2,1)S(1)} %all-to-all-done.3.refs_0_, bf16[1024,256]{1,0:T(8,128)(2,1)S(1)} %copy-done, f32[1024,128]{1,0:T(8,128)S(1)} %local_grad_kernel.1.refs_2_), custom_call_target="tpu_custom_call" | custom-call | flops 100000000 | bytes 2080768 | tf_op jit(solution)/shard_map/finish_kernel/pallas_call | solution.py:579
Async XLA Ops:
  3.1 14.9 %all-to-all-start = ((bf16[32,8,128]{2,1,0:T(8,128)(2,1)}), bf16[32,8,128]{2,1,0:T(8,128)(2,1)S(1)}, u32[]{:S(2)}, u32[]{:S(2)}) async-start(bf16[32,8,128]{2,1,0:T(8,128)(2,1)} %bitcast.23), calls=%async_computation | async-start | bytes 131072 | tf_op jit(solution)/shard_map/all_to_all | solution.py:596
  13.4 4.7 %copy-start.4 = (bf16[128,384]{1,0:T(8,128)(2,1)S(1)}, bf16[128,384]{1,0:T(8,128)(2,1)}, u32[]{:S(2)}) copy-start(bf16[128,384]{1,0:T(8,128)(2,1)} %constant.16.clone.refs_3_) | copy-start | bytes 294916
  13.4 4.7 %copy-start.5 = (bf16[192,256]{1,0:T(8,128)(2,1)S(1)}, bf16[192,256]{1,0:T(8,128)(2,1)}, u32[]{:S(2)}) copy-start(bf16[192,256]{1,0:T(8,128)(2,1)} %constant.15.clone.refs_1_) | copy-start | bytes 294916
  13.4 6.4 %copy-start.12 = (bf16[512,128]{1,0:T(8,128)(2,1)S(1)}, bf16[512,128]{1,0:T(8,128)(2,1)}, u32[]{:S(2)}) copy-start(bf16[512,128]{1,0:T(8,128)(2,1)} %get-tuple-element.44) | copy-start | bytes 393220
  13.4 8.0 %copy-start.11 = (bf16[512,128]{1,0:T(8,128)(2,1)S(1)}, bf16[512,128]{1,0:T(8,128)(2,1)}, u32[]{:S(2)}) copy-start(bf16[512,128]{1,0:T(8,128)(2,1)} %get-tuple-element.45) | copy-start | bytes 393220
  13.4 14.9 %copy-start.1 = (bf16[3,3,3,64,64]{4,3,2,1,0:T(8,128)(2,1)S(1)}, bf16[3,3,3,64,64]{4,3,2,1,0:T(8,128)(2,1)}, u32[]{:S(2)}) copy-start(bf16[3,3,3,64,64]{4,3,2,1,0:T(8,128)(2,1)} %param.14) | copy-start | bytes 663556
  13.4 14.9 %copy-start.6 = (bf16[1,64,2,1024]{3,2,1,0:T(2,128)(2,1)S(1)}, bf16[1,64,2,1024]{3,2,1,0:T(2,128)(2,1)}, u32[]{:S(2)}) copy-start(bf16[1,64,2,1024]{3,2,1,0:T(2,128)(2,1)} %param.12) | copy-start | bytes 786436
  13.4 14.9 %copy-start.7 = (bf16[1024,128]{1,0:T(8,128)(2,1)S(1)}, bf16[1024,128]{1,0:T(8,128)(2,1)}, u32[]{:S(2)}) copy-start(bf16[1024,128]{1,0:T(8,128)(2,1)} %get-tuple-element.43.refs_0_) | copy-start | bytes 786436
  19.8 8.4 %collective-permute-start = (bf16[512,128]{1,0:T(8,128)(2,1)S(1)}, bf16[512,128]{1,0:T(8,128)(2,1)S(1)}, u32[]{:S(2)}, u32[]{:S(2)}) collective-permute-start(bf16[512,128]{1,0:T(8,128)(2,1)S(1)} %copy-done.12), channel_id=1, source_target_pairs={{0,1},{1,2},{2,3},{3,4},{4,5},{5,6},{6,7},{7,8},{8,9},{9,10},{10,1... | collective-permute-start | bytes 393224 | tf_op jit(solution)/shard_map/ppermute | solution.py:601
  21.4 6.8 %collective-permute-start.1 = (bf16[512,128]{1,0:T(8,128)(2,1)S(1)}, bf16[512,128]{1,0:T(8,128)(2,1)S(1)}, u32[]{:S(2)}, u32[]{:S(2)}) collective-permute-start(bf16[512,128]{1,0:T(8,128)(2,1)S(1)} %copy-done.11), channel_id=1, source_target_pairs={{1,0},{2,1},{3,2},{4,3},{5,4},{6,5},{7,6},{8,7},{9,8},{10,9},{11,1... | collective-permute-start | bytes 393224 | tf_op jit(solution)/shard_map/ppermute | solution.py:602
  22.7 13.1 %all-to-all-start.1 = ((bf16[32,8,128]{2,1,0:T(8,128)(2,1)}), bf16[32,8,128]{2,1,0:T(8,128)(2,1)S(1)}, u32[]{:S(2)}, u32[]{:S(2)}) async-start(bf16[32,8,128]{2,1,0:T(8,128)(2,1)} %get-tuple-element.42), calls=%async_computation.1 | async-start | bytes 131072 | tf_op jit(solution)/shard_map/all_to_all | solution.py:596
  28.3 7.6 %copy-start.8 = (bf16[1024,256]{1,0:T(8,128)(2,1)S(1)}, bf16[1024,256]{1,0:T(8,128)(2,1)}, u32[]{:S(2)}) copy-start(bf16[1024,256]{1,0:T(8,128)(2,1)} %constant.17.clone.refs_1_) | copy-start | bytes 1572868
  29.5 0.7 copy-start.9
  35.9 1.0 %copy-start.10 = (bf16[1024,128]{1,0:T(8,128)(2,1)S(1)}, bf16[1024,128]{1,0:T(8,128)(2,1)}, u32[]{:S(2)}) copy-start(bf16[1024,128]{1,0:T(8,128)(2,1)} %copy-done.9) | copy-start | bytes 786436
  39.5 14.3 %all-to-all-start.2 = ((bf16[32,40,128]{2,1,0:T(8,128)(2,1)}), bf16[32,40,128]{2,1,0:T(8,128)(2,1)S(1)}, u32[]{:S(2)}, u32[]{:S(2)}) async-start(bf16[32,40,128]{2,1,0:T(8,128)(2,1)} %get-tuple-element.49), calls=%async_computation.2 | async-start | bytes 655360 | tf_op jit(solution)/shard_map/all_to_all | solution.py:596
  42.1 5.6 %collective-permute-start.2 = (bf16[512,128]{1,0:T(8,128)(2,1)S(1)}, bf16[512,128]{1,0:T(8,128)(2,1)S(1)}, u32[]{:S(2)}, u32[]{:S(2)}) collective-permute-start(bf16[512,128]{1,0:T(8,128)(2,1)S(1)} %get-tuple-element.50), channel_id=1, source_target_pairs={{0,1},{1,2},{2,3},{3,4},{4,5},{5,6},{6,7},{7,8},{8,9},{9,10},{10,1... | collective-permute-start | bytes 393224 | tf_op jit(solution)/shard_map/ppermute | solution.py:601
  44.1 4.4 %collective-permute-start.3 = (bf16[512,128]{1,0:T(8,128)(2,1)S(1)}, bf16[512,128]{1,0:T(8,128)(2,1)S(1)}, u32[]{:S(2)}, u32[]{:S(2)}) collective-permute-start(bf16[512,128]{1,0:T(8,128)(2,1)S(1)} %get-tuple-element.51), channel_id=1, source_target_pairs={{1,0},{2,1},{3,2},{4,3},{5,4},{6,5},{7,6},{8,7},{9,8},{10,9},{11,1... | collective-permute-start | bytes 393224 | tf_op jit(solution)/shard_map/ppermute | solution.py:602
  45.4 8.4 %copy-start.2 = (bf16[128,384]{1,0:T(8,128)(2,1)S(1)}, bf16[128,384]{1,0:T(8,128)(2,1)}, u32[]{:S(2)}) copy-start(bf16[128,384]{1,0:T(8,128)(2,1)} %constant.19.clone.refs_3_) | copy-start | bytes 294916
  45.4 8.4 %copy-start.3 = (bf16[192,256]{1,0:T(8,128)(2,1)S(1)}, bf16[192,256]{1,0:T(8,128)(2,1)}, u32[]{:S(2)}) copy-start(bf16[192,256]{1,0:T(8,128)(2,1)} %constant.18.clone.refs_1_) | copy-start | bytes 294916
  55.6 15.2 %all-to-all-start.3 = ((bf16[32,40,128]{2,1,0:T(8,128)(2,1)}), bf16[32,40,128]{2,1,0:T(8,128)(2,1)S(1)}, u32[]{:S(2)}, u32[]{:S(2)}) async-start(bf16[32,40,128]{2,1,0:T(8,128)(2,1)} %get-tuple-element.58), calls=%async_computation.3 | async-start | bytes 655360 | tf_op jit(solution)/shard_map/all_to_all | solution.py:596
  62.8 8.0 %copy-start = (bf16[1024,256]{1,0:T(8,128)(2,1)S(1)}, bf16[1024,256]{1,0:T(8,128)(2,1)}, u32[]{:S(2)}) copy-start(bf16[1024,256]{1,0:T(8,128)(2,1)} %constant.20.clone.refs_1_) | copy-start | bytes 1572868

commit v19 on v18

--- a/solution.py
+++ b/solution.py
@@ -40,15 +40,23 @@
     return np.where(row < half_count, np.cos(phases), np.sin(phases)).astype(np.float32)
 
 
-def plane_tables(batches, slabs):
-    outer = (basis_rows(KX, NX)[:, None, :, None] * basis_rows(KY, NY)[None, :, None, :]).reshape(
-        2 * KX, 2 * KY, CELLS
-    )
-    outer = outer.reshape(batches, 2 * KX // batches, slabs, 2 * KY // slabs, CELLS)
-    outer = outer.transpose(2, 0, 1, 3, 4).reshape(4 * KX * KY, CELLS)
-    analysis = (outer * np.float32(2.0 / math.sqrt(CELLS))).astype(ml_dtypes.bfloat16)
-    synthesis = (outer * np.float32(2.0 / math.sqrt(4 * KX * KY))).astype(ml_dtypes.bfloat16)
-    return analysis, synthesis
+def plane_factors(batches, slabs):
+    modes_x, modes_y = 2 * KX, 2 * KY
+
+    def columns(values, cells):
+        values = np.broadcast_to(values, (modes_x, modes_y, cells))
+        values = values.reshape(batches, modes_x // batches, slabs, modes_y // slabs, cells)
+        values = values.transpose(2, 0, 1, 3, 4).reshape(modes_x * modes_y, cells)
+        return np.ascontiguousarray(values.T)
+
+    across = columns(basis_rows(KX, NX)[:, None, :], NX)
+    along_y = columns(basis_rows(KY, NY)[None, :, :], NY)
+    return across, along_y
+
+
+def plane_analysis(across, along_y):
+    outer = (across[:, None, :] * along_y[None, :, :]).reshape(CELLS, -1).T
+    return (outer * np.float32(2.0 / math.sqrt(CELLS))).astype(ml_dtypes.bfloat16)
 
 
 def depth_tables(slabs, layers, modes):
@@ -237,8 +245,24 @@
 
 
 def local_kernel(
-    cells, before, after, cotangent, weights, local_out, lanes_out, cotangent_out, padded, table
+    cells,
+    before,
+    after,
+    cotangent,
+    weights,
+    across,
+    along_y,
+    local_out,
+    lanes_out,
+    cotangent_out,
+    synthesis_out,
+    padded,
+    table,
 ):
+    scale = 2.0 / math.sqrt(4 * KX * KY)
+    for x in range(NX):
+        rows = across[x : x + 1, :] * along_y[...] * scale
+        synthesis_out[x * NY : (x + 1) * NY, :] = rows.astype(BF16)
     banded_forward(weights, table)
     beside = beside_layers(before[...], after[...])
     pad_cells(padded, cells[...], beside)
@@ -615,7 +639,8 @@
     count = modes * 2 * KZ * batches
     in_slab = modes == 8 and devices * 32 == TERM_ROWS
 
-    analysis, synthesis = plane_tables(batches, slabs)
+    across, along_y = plane_factors(batches, slabs)
+    analysis = np.ascontiguousarray(plane_analysis(across, along_y))
     gather, scatter, gather_back, scatter_back = depth_tables(slabs, layers, modes)
     weights = mode_weight.reshape(modes * 2 * KZ * channels, channels)
     taps = conv_weight.reshape(OFFSETS, channels, channels)
@@ -668,16 +693,23 @@
     back, first, last = lax.optimization_barrier((back, first, last))
     back = send(back)
     before, after = neighbours(first, last)
-    local, lanes, outer_cells = run(
+    local, lanes, outer_cells, synthesis = run(
         local_kernel,
-        [shape((CELLS, LANES), F32), shape((2 * LANES, CELLS), BF16), wide],
+        [
+            shape((CELLS, LANES), F32),
+            shape((2 * LANES, CELLS), BF16),
+            wide,
+            shape((CELLS, plane_rows), BF16),
+        ],
         cells,
         before,
         after,
         cotangent.reshape(field.shape),
         taps,
+        across,
+        along_y,
         scratch=[padded, pltpu.VMEM((3, 2 * LANES, 3 * LANES), BF16)],
-        flops=8 * 10**9,
+        flops=7 * 10**8,
     )
     slab = shape((devices, 8 + TERM_ROWS // devices, LANES), BF16)
     activated, grad, first, last, back, terms = run(
@@ -691,7 +723,7 @@
             None if in_slab else shape((TERM_ROWS, LANES), BF16),
         ],
         back,
-        np.ascontiguousarray(synthesis.T),
+        synthesis,
         local,
         outer_cells,
         lanes,

time: 72.9 us -> 74 us (1.015)
  local copies, waits for them, and re-layouts: 1.72 us -> 3.56 us
  waiting for transfers between devices: 20.8 us -> 19.9 us
    unnamed x26 -> x32, local copies, waits for them, and re-layouts: 1.72 us -> 3.56 us
    all_to_all x4, waiting for transfers between devices: 19.9 us -> 19 us  [exchange(): lax.all_to_all(values, ('space', 'batch'), split_axis=0, concat_axis=0, t...]
where the time goes in v19:
time: 74 us; the launch traced here: 73.4 us
  starting transfers between devices  25.1 us (34%)
  Pallas kernels  23.9 us (32%)
  waiting for transfers between devices  19.9 us (27%)
  local copies, waits for them, and re-layouts  3.56 us (5%)
  between operations  0.95 us (1%)
    pallas_call x11, Pallas kernels, run(): pl.pallas_call(kernel, out_shape=results, in_specs=[in_hbm if k in staged...  23.9 us
    all_to_all x4, waiting for transfers between devices, exchange(): lax.all_to_all(values, ('space', 'batch'), split_axis=0, concat_axis=0, t...  19 us
    all_to_all x4, starting transfers between devices, exchange(): lax.all_to_all(values, ('space', 'batch'), split_axis=0, concat_axis=0, t...  18.9 us
    ppermute x2, starting transfers between devices, neighbours(): before = lax.ppermute(last, 'space', [(i, i + 1) for i in range(ends)])  3.62 us
    unnamed x32, local copies, waits for them, and re-layouts  3.56 us
    ppermute x2, starting transfers between devices, neighbours(): after = lax.ppermute(first, 'space', [(i + 1, i) for i in range(ends)])  2.58 us
  transfers between devices with their start and end apart: 8, of which 5 were waited for; matrix products, arithmetic and copies ran while one was open for 0% of the time, Pallas kernels for 19%

profile of v19, /device:TPU:0, one launch (start us, length us, event | category | flops | bytes accessed | tf_op | source)
XLA Modules:
  0.0 73.4 jit_solution(13229456839474329541)
XLA Ops:
  0.6 2.5 %analyse_kernel.1 = (bf16[1024,128]{1,0:T(8,128)(2,1)}, bf16[256,128]{1,0:T(8,128)(2,1)}, bf16[512,128]{1,0:T(8,128)(2,1)}, bf16[512,128]{1,0:T(8,128)(2,1)}, bf16[32,8,128]{2,1,0:T(8,128)(2,1)}) custom-call(bf16[64,2,1024]{2,1,0:T(2,128)(2,1)} %bitcast.22, bf16[256,1024]{1,0:T(8,128)(2,1)} %constant.16.clone.refs_1_), custom_call_target="tpu_custom_call" | custom-call | flops 100000000 | bytes 1441792 | tf_op jit(solution)/shard_map/analyse_kernel/pallas_call | solution.py:603
  3.1 7.3 %all-to-all-start = ((bf16[32,8,128]{2,1,0:T(8,128)(2,1)}), bf16[32,8,128]{2,1,0:T(8,128)(2,1)S(1)}, u32[]{:S(2)}, u32[]{:S(2)}) async-start(bf16[32,8,128]{2,1,0:T(8,128)(2,1)} %bitcast.23), calls=%async_computation | async-start | bytes 131072 | tf_op jit(solution)/shard_map/all_to_all | solution.py:620
  10.4 2.9 %pack_kernel.1.refs_0_.refs_1_ = bf16[102400,128]{1,0:T(8,128)(2,1)} custom-call(bf16[12288,64]{1,0:T(8,128)(2,1)} %bitcast.18, bf16[12288,64]{1,0:T(8,128)(2,1)} %bitcast.19, bf16[12288,64]{1,0:T(8,128)(2,1)} %bitcast.20), custom_call_target="tpu_custom_call" | custom-call | bytes 30932992 | tf_op jit(solution)/shard_map/pack_kernel/pallas_call | solution.py:603
  13.4 0.0 copy-start.4
  13.4 0.0 copy-start.5
  13.4 0.0 copy-start.15
  13.4 0.0 copy-start.14
  13.4 0.0 copy-start.1
  13.4 0.0 copy-start.6
  13.4 0.0 copy-start.7
  13.4 0.0 copy-start.8
  13.4 0.0 copy-start.9
  13.5 1.6 %fetch_kernel.1.refs_2_ = bf16[6144,128]{1,0:T(8,128)(2,1)S(1)} custom-call(bf16[102400,128]{1,0:T(8,128)(2,1)} %pack_kernel.1.refs_0_.refs_1_), custom_call_target="tpu_custom_call" | custom-call | bytes 27787264 | tf_op jit(solution)/shard_map/fetch_kernel/pallas_call | solution.py:603
  15.0 3.0 %all-to-all-done = bf16[32,8,128]{2,1,0:T(8,128)(2,1)S(1)} async-done(((bf16[32,8,128]{2,1,0:T(8,128)(2,1)}), bf16[32,8,128]{2,1,0:T(8,128)(2,1)S(1)}, u32[]{:S(2)}, u32[]{:S(2)}) %all-to-all-start) | async-done | bytes 65568 | tf_op jit(solution)/shard_map/all_to_all | solution.py:620
  18.0 0.0 copy-done.4
  18.0 0.0 copy-done.5
  18.0 1.8 %mix_kernel.1 = (bf16[32,8,128]{2,1,0:T(8,128)(2,1)}, bf16[384,256]{1,0:T(8,128)(2,1)S(1)}) custom-call(bf16[256,128]{1,0:T(8,128)(2,1)S(1)} %bitcast.15, bf16[192,256]{1,0:T(8,128)(2,1)S(1)} %copy-done.5, bf16[6144,128]{1,0:T(8,128)(2,1)S(1)} %fetch_kernel.1.refs_2_, bf16[128,384]{1,0:T(8,128)(2,1)S(1)} %copy-done.4, ...), custom_call_target="tpu_custom_call", output_to_operand_aliasing={{0}: (4, {})} | custom-call | flops 400000000 | bytes 2097152 | tf_op jit(solution)/shard_map/mix_kernel/pallas_call | solution.py:603
  19.8 0.0 copy-done.15
  19.8 1.6 %collective-permute-start = (bf16[512,128]{1,0:T(8,128)(2,1)S(1)}, bf16[512,128]{1,0:T(8,128)(2,1)S(1)}, u32[]{:S(2)}, u32[]{:S(2)}) collective-permute-start(bf16[512,128]{1,0:T(8,128)(2,1)S(1)} %copy-done.15), channel_id=1, source_target_pairs={{0,1},{1,2},{2,3},{3,4},{4,5},{5,6},{6,7},{7,8},{8,9},{9,10},{10,1... | collective-permute-start | bytes 393224 | tf_op jit(solution)/shard_map/ppermute | solution.py:625
  21.4 0.0 copy-done.14
  21.5 1.3 %collective-permute-start.1 = (bf16[512,128]{1,0:T(8,128)(2,1)S(1)}, bf16[512,128]{1,0:T(8,128)(2,1)S(1)}, u32[]{:S(2)}, u32[]{:S(2)}) collective-permute-start(bf16[512,128]{1,0:T(8,128)(2,1)S(1)} %copy-done.14), channel_id=1, source_target_pairs={{1,0},{2,1},{3,2},{4,3},{5,4},{6,5},{7,6},{8,7},{9,8},{10,9},{11,1... | collective-permute-start | bytes 393224 | tf_op jit(solution)/shard_map/ppermute | solution.py:626
  22.8 5.5 %all-to-all-start.1 = ((bf16[32,8,128]{2,1,0:T(8,128)(2,1)}), bf16[32,8,128]{2,1,0:T(8,128)(2,1)S(1)}, u32[]{:S(2)}, u32[]{:S(2)}) async-start(bf16[32,8,128]{2,1,0:T(8,128)(2,1)} %get-tuple-element.43), calls=%async_computation.1 | async-start | bytes 131072 | tf_op jit(solution)/shard_map/all_to_all | solution.py:620
  28.3 0.0 collective-permute-done.refs_1_
  28.3 0.0 collective-permute-done.1.refs_2_
  28.3 0.0 copy-done.1
  28.3 0.0 copy-done.6
  28.3 0.0 copy-done.7
  28.3 0.0 copy-done.8
  28.3 0.0 copy-done.9
  28.4 1.2 %local_kernel.1 = (f32[1024,128]{1,0:T(8,128)S(1)}, bf16[256,1024]{1,0:T(8,128)(2,1)S(1)}, bf16[1024,128]{1,0:T(8,128)(2,1)S(1)}, bf16[1024,256]{1,0:T(8,128)(2,1)S(1)}) custom-call(bf16[1024,128]{1,0:T(8,128)(2,1)S(1)} %copy-done.7, bf16[512,128]{1,0:T(8,128)(2,1)S(1)} %collective-permute-done.refs_1_, bf16[512,128]{1,0:T(8,128)(2,1)S(1)} %collective-permute-done.1.refs_2_, ...), custom_call_target="tpu_custom_call" | custom-call | flops 700000000 | bytes 2908160 | tf_op jit(solution)/shard_map/local_kernel/pallas_call | solution.py:603
  29.6 0.0 copy-start.10
  29.6 0.8 %copy-done.10 = bf16[1024,256]{1,0:T(8,128)(2,1)} copy-done((bf16[1024,256]{1,0:T(8,128)(2,1)}, bf16[1024,256]{1,0:T(8,128)(2,1)S(1)}, u32[]{:S(2)}) %copy-start.10) | copy-done | bytes 524312
  30.4 0.0 copy-start.12
  30.4 0.7 copy-done.12
  31.1 4.8 %all-to-all-done.1 = bf16[32,8,128]{2,1,0:T(8,128)(2,1)S(1)} async-done(((bf16[32,8,128]{2,1,0:T(8,128)(2,1)}), bf16[32,8,128]{2,1,0:T(8,128)(2,1)S(1)}, u32[]{:S(2)}, u32[]{:S(2)}) %all-to-all-start.1) | async-done | bytes 65568 | tf_op jit(solution)/shard_map/all_to_all | solution.py:620
  35.9 0.0 copy-start.11
  35.9 1.0 %copy-done.11 = bf16[1024,256]{1,0:T(8,128)(2,1)S(1)} copy-done((bf16[1024,256]{1,0:T(8,128)(2,1)S(1)}, bf16[1024,256]{1,0:T(8,128)(2,1)}, u32[]{:S(2)}) %copy-start.11) | copy-done | bytes 524312
  36.9 0.0 copy-start.13
  36.9 0.9 %copy-done.13 = bf16[1024,128]{1,0:T(8,128)(2,1)S(1)} copy-done((bf16[1024,128]{1,0:T(8,128)(2,1)S(1)}, bf16[1024,128]{1,0:T(8,128)(2,1)}, u32[]{:S(2)}) %copy-start.13) | copy-done | bytes 262168
  37.9 2.6 %activate_kernel.1 = (bf16[1024,128]{1,0:T(8,128)(2,1)S(1)}, bf16[102400,128]{1,0:T(8,128)(2,1)}, bf16[512,128]{1,0:T(8,128)(2,1)S(1)}, bf16[512,128]{1,0:T(8,128)(2,1)S(1)}, bf16[32,40,128]{2,1,0:T(8,128)(2,1)}) custom-call(bf16[256,128]{1,0:T(8,128)(2,1)S(1)} %bitcast.16, bf16[1024,256]{1,0:T(8,128)(2,1)S(1)} %copy-done.11, ...), custom_call_target="tpu_custom_call" | custom-call | flops 1000000000 | bytes 28966912 | tf_op jit(solution)/shard_map/activate_kernel/pallas_call | solution.py:603
  40.5 2.6 %all-to-all-start.2 = ((bf16[32,40,128]{2,1,0:T(8,128)(2,1)}), bf16[32,40,128]{2,1,0:T(8,128)(2,1)S(1)}, u32[]{:S(2)}, u32[]{:S(2)}) async-start(bf16[32,40,128]{2,1,0:T(8,128)(2,1)} %get-tuple-element.51), calls=%async_computation.2 | async-start | bytes 655360 | tf_op jit(solution)/shard_map/all_to_all | solution.py:620
  43.2 2.0 %collective-permute-start.2 = (bf16[512,128]{1,0:T(8,128)(2,1)S(1)}, bf16[512,128]{1,0:T(8,128)(2,1)S(1)}, u32[]{:S(2)}, u32[]{:S(2)}) collective-permute-start(bf16[512,128]{1,0:T(8,128)(2,1)S(1)} %get-tuple-element.52), channel_id=1, source_target_pairs={{0,1},{1,2},{2,3},{3,4},{4,5},{5,6},{6,7},{7,8},{8,9},{9,10},{10,1... | collective-permute-start | bytes 393224 | tf_op jit(solution)/shard_map/ppermute | solution.py:625
  45.2 1.3 %collective-permute-start.3 = (bf16[512,128]{1,0:T(8,128)(2,1)S(1)}, bf16[512,128]{1,0:T(8,128)(2,1)S(1)}, u32[]{:S(2)}, u32[]{:S(2)}) collective-permute-start(bf16[512,128]{1,0:T(8,128)(2,1)S(1)} %get-tuple-element.53), channel_id=1, source_target_pairs={{1,0},{2,1},{3,2},{4,3},{5,4},{6,5},{7,6},{8,7},{9,8},{10,9},{11,1... | collective-permute-start | bytes 393224 | tf_op jit(solution)/shard_map/ppermute | solution.py:626
  46.5 0.0 copy-start.2
  46.5 0.0 copy-start.3
  46.5 2.2 %output_kernel.1 = (bf16[64,2,1024]{2,1,0:T(2,128)(2,1)}, bf16[6144,128]{1,0:T(8,128)(2,1)S(1)}) custom-call(bf16[1024,128]{1,0:T(8,128)(2,1)S(1)} %get-tuple-element.54.refs_0_, bf16[102400,128]{1,0:T(8,128)(2,1)} %pack_kernel.1.refs_0_.refs_1_), custom_call_target="tpu_custom_call" | custom-call | flops 100000000 | bytes 28311552 | tf_op jit(solution)/shard_map/output_kernel/pallas_call | solution.py:603
  48.7 0.0 collective-permute-done.2.refs_1_
  48.7 0.9 %collective-permute-done.3.refs_2_ = bf16[512,128]{1,0:T(8,128)(2,1)S(1)} collective-permute-done((bf16[512,128]{1,0:T(8,128)(2,1)S(1)}, bf16[512,128]{1,0:T(8,128)(2,1)S(1)}, u32[]{:S(2)}, u32[]{:S(2)}) %collective-permute-start.3) | collective-permute-done | bytes 131104 | tf_op jit(solution)/shard_map/ppermute | solution.py:626
  49.6 5.3 %all-to-all-done.2.refs_0_ = bf16[32,40,128]{2,1,0:T(8,128)(2,1)S(1)} async-done(((bf16[32,40,128]{2,1,0:T(8,128)(2,1)}), bf16[32,40,128]{2,1,0:T(8,128)(2,1)S(1)}, u32[]{:S(2)}, u32[]{:S(2)}) %all-to-all-start.2) | async-done | bytes 327712 | tf_op jit(solution)/shard_map/all_to_all | solution.py:620
  54.9 0.0 copy-done.2
  54.9 0.0 copy-done.3
  54.9 1.8 %unmix_kernel.1 = (bf16[32,40,128]{2,1,0:T(8,128)(2,1)}, bf16[384,128]{1,0:T(8,128)(2,1)S(1)}) custom-call(bf16[32,40,128]{2,1,0:T(8,128)(2,1)S(1)} %all-to-all-done.2.refs_0_, bf16[192,256]{1,0:T(8,128)(2,1)S(1)} %copy-done.3, bf16[6144,128]{1,0:T(8,128)(2,1)S(1)} %get-tuple-element.59.refs_2_, bf16[128,384]{1,0:T(8,128)(2,1)S(1)} %copy-done.2), custom_call_target="tpu_custom_call" | custom-call | flops 400000000 | bytes 2523136 | tf_op jit(solution)/shard_map/unmix_kernel/pallas_call | solution.py:603
  56.7 3.5 %all-to-all-start.3 = ((bf16[32,40,128]{2,1,0:T(8,128)(2,1)}), bf16[32,40,128]{2,1,0:T(8,128)(2,1)S(1)}, u32[]{:S(2)}, u32[]{:S(2)}) async-start(bf16[32,40,128]{2,1,0:T(8,128)(2,1)} %get-tuple-element.60), calls=%async_computation.3 | async-start | bytes 655360 | tf_op jit(solution)/shard_map/all_to_all | solution.py:620
  60.2 3.7 %weight_kernel.1 = f32[12288,64]{1,0:T(8,128)} custom-call(bf16[384,256]{1,0:T(8,128)(2,1)S(1)} %get-tuple-element.65.refs_0_, bf16[384,128]{1,0:T(8,128)(2,1)S(1)} %get-tuple-element.66.refs_1_), custom_call_target="tpu_custom_call" | custom-call | flops 400000000 | bytes 3440640 | tf_op jit(solution)/shard_map/weight_kernel/pallas_call | solution.py:603
  63.9 0.0 copy-start
  63.9 2.1 %local_grad_kernel.1.refs_2_ = f32[1024,128]{1,0:T(8,128)S(1)} custom-call(bf16[102400,128]{1,0:T(8,128)(2,1)} %get-tuple-element.61.refs_0_, bf16[512,128]{1,0:T(8,128)(2,1)S(1)} %collective-permute-done.2.refs_1_, bf16[512,128]{1,0:T(8,128)(2,1)S(1)} %collective-permute-done.3.refs_2_, bf16[27,64,64]{2,1,0:T(8,128)(2,1)S(1)} %bitcast.14), custom_call_target="tpu_custom_call" | custom-call | flops 700000000 | bytes 27222016 | tf_op jit(solution)/shard_map/local_grad_kernel/pallas_call | solution.py:603
  66.0 5.9 %all-to-all-done.3.refs_0_ = bf16[32,40,128]{2,1,0:T(8,128)(2,1)S(1)} async-done(((bf16[32,40,128]{2,1,0:T(8,128)(2,1)}), bf16[32,40,128]{2,1,0:T(8,128)(2,1)S(1)}, u32[]{:S(2)}, u32[]{:S(2)}) %all-to-all-start.3) | async-done | bytes 327712 | tf_op jit(solution)/shard_map/all_to_all | solution.py:620
  71.9 0.0 copy-done
  71.9 1.5 %finish_kernel.1 = (bf16[64,2,1024]{2,1,0:T(2,128)(2,1)}, f32[27,64,64]{2,1,0:T(8,128)}) custom-call(bf16[32,40,128]{2,1,0:T(8,128)(2,1)S(1)} %all-to-all-done.3.refs_0_, bf16[1024,256]{1,0:T(8,128)(2,1)S(1)} %copy-done, f32[1024,128]{1,0:T(8,128)S(1)} %local_grad_kernel.1.refs_2_), custom_call_target="tpu_custom_call" | custom-call | flops 100000000 | bytes 2080768 | tf_op jit(solution)/shard_map/finish_kernel/pallas_call | solution.py:603
Async XLA Ops:
  3.1 14.9 %all-to-all-start = ((bf16[32,8,128]{2,1,0:T(8,128)(2,1)}), bf16[32,8,128]{2,1,0:T(8,128)(2,1)S(1)}, u32[]{:S(2)}, u32[]{:S(2)}) async-start(bf16[32,8,128]{2,1,0:T(8,128)(2,1)} %bitcast.23), calls=%async_computation | async-start | bytes 131072 | tf_op jit(solution)/shard_map/all_to_all | solution.py:620
  13.4 4.7 %copy-start.4 = (bf16[128,384]{1,0:T(8,128)(2,1)S(1)}, bf16[128,384]{1,0:T(8,128)(2,1)}, u32[]{:S(2)}) copy-start(bf16[128,384]{1,0:T(8,128)(2,1)} %constant.18.clone.refs_3_) | copy-start | bytes 294916
  13.4 4.7 %copy-start.5 = (bf16[192,256]{1,0:T(8,128)(2,1)S(1)}, bf16[192,256]{1,0:T(8,128)(2,1)}, u32[]{:S(2)}) copy-start(bf16[192,256]{1,0:T(8,128)(2,1)} %constant.17.clone.refs_1_) | copy-start | bytes 294916
  13.4 6.5 %copy-start.15 = (bf16[512,128]{1,0:T(8,128)(2,1)S(1)}, bf16[512,128]{1,0:T(8,128)(2,1)}, u32[]{:S(2)}) copy-start(bf16[512,128]{1,0:T(8,128)(2,1)} %get-tuple-element.45) | copy-start | bytes 393220
  13.4 8.1 %copy-start.14 = (bf16[512,128]{1,0:T(8,128)(2,1)S(1)}, bf16[512,128]{1,0:T(8,128)(2,1)}, u32[]{:S(2)}) copy-start(bf16[512,128]{1,0:T(8,128)(2,1)} %get-tuple-element.46) | copy-start | bytes 393220
  13.4 14.9 %copy-start.1 = (bf16[3,3,3,64,64]{4,3,2,1,0:T(8,128)(2,1)S(1)}, bf16[3,3,3,64,64]{4,3,2,1,0:T(8,128)(2,1)}, u32[]{:S(2)}) copy-start(bf16[3,3,3,64,64]{4,3,2,1,0:T(8,128)(2,1)} %param.15) | copy-start | bytes 663556
  13.4 14.9 %copy-start.6 = (bf16[1,64,2,1024]{3,2,1,0:T(2,128)(2,1)S(1)}, bf16[1,64,2,1024]{3,2,1,0:T(2,128)(2,1)}, u32[]{:S(2)}) copy-start(bf16[1,64,2,1024]{3,2,1,0:T(2,128)(2,1)} %param.13) | copy-start | bytes 786436
  13.4 14.9 %copy-start.7 = (bf16[1024,128]{1,0:T(8,128)(2,1)S(1)}, bf16[1024,128]{1,0:T(8,128)(2,1)}, u32[]{:S(2)}) copy-start(bf16[1024,128]{1,0:T(8,128)(2,1)} %get-tuple-element.44.refs_0_) | copy-start | bytes 786436
  13.4 14.9 %copy-start.8 = (f32[32,256]{1,0:T(8,128)S(1)}, f32[32,256]{1,0:T(8,128)}, u32[]{:S(2)}) copy-start(f32[32,256]{1,0:T(8,128)} %constant.20.clone.refs_6_) | copy-start | bytes 98308
  13.4 14.9 %copy-start.9 = (f32[32,256]{1,0:T(8,128)S(1)}, f32[32,256]{1,0:T(8,128)}, u32[]{:S(2)}) copy-start(f32[32,256]{1,0:T(8,128)} %constant.19.clone.refs_5_) | copy-start | bytes 98308
  19.8 8.4 %collective-permute-start = (bf16[512,128]{1,0:T(8,128)(2,1)S(1)}, bf16[512,128]{1,0:T(8,128)(2,1)S(1)}, u32[]{:S(2)}, u32[]{:S(2)}) collective-permute-start(bf16[512,128]{1,0:T(8,128)(2,1)S(1)} %copy-done.15), channel_id=1, source_target_pairs={{0,1},{1,2},{2,3},{3,4},{4,5},{5,6},{6,7},{7,8},{8,9},{9,10},{10,1... | collective-permute-start | bytes 393224 | tf_op jit(solution)/shard_map/ppermute | solution.py:625
  21.5 6.8 %collective-permute-start.1 = (bf16[512,128]{1,0:T(8,128)(2,1)S(1)}, bf16[512,128]{1,0:T(8,128)(2,1)S(1)}, u32[]{:S(2)}, u32[]{:S(2)}) collective-permute-start(bf16[512,128]{1,0:T(8,128)(2,1)S(1)} %copy-done.14), channel_id=1, source_target_pairs={{1,0},{2,1},{3,2},{4,3},{5,4},{6,5},{7,6},{8,7},{9,8},{10,9},{11,1... | collective-permute-start | bytes 393224 | tf_op jit(solution)/shard_map/ppermute | solution.py:626
  22.8 13.1 %all-to-all-start.1 = ((bf16[32,8,128]{2,1,0:T(8,128)(2,1)}), bf16[32,8,128]{2,1,0:T(8,128)(2,1)S(1)}, u32[]{:S(2)}, u32[]{:S(2)}) async-start(bf16[32,8,128]{2,1,0:T(8,128)(2,1)} %get-tuple-element.43), calls=%async_computation.1 | async-start | bytes 131072 | tf_op jit(solution)/shard_map/all_to_all | solution.py:620
  29.6 0.8 %copy-start.10 = (bf16[1024,256]{1,0:T(8,128)(2,1)}, bf16[1024,256]{1,0:T(8,128)(2,1)S(1)}, u32[]{:S(2)}) copy-start(bf16[1024,256]{1,0:T(8,128)(2,1)S(1)} %get-tuple-element.47.refs_1_) | copy-start | bytes 1572868
  30.4 0.7 copy-start.12
  35.9 1.0 %copy-start.11 = (bf16[1024,256]{1,0:T(8,128)(2,1)S(1)}, bf16[1024,256]{1,0:T(8,128)(2,1)}, u32[]{:S(2)}) copy-start(bf16[1024,256]{1,0:T(8,128)(2,1)} %copy-done.10) | copy-start | bytes 1572868
  36.9 0.9 %copy-start.13 = (bf16[1024,128]{1,0:T(8,128)(2,1)S(1)}, bf16[1024,128]{1,0:T(8,128)(2,1)}, u32[]{:S(2)}) copy-start(bf16[1024,128]{1,0:T(8,128)(2,1)} %copy-done.12) | copy-start | bytes 786436
  40.5 14.3 %all-to-all-start.2 = ((bf16[32,40,128]{2,1,0:T(8,128)(2,1)}), bf16[32,40,128]{2,1,0:T(8,128)(2,1)S(1)}, u32[]{:S(2)}, u32[]{:S(2)}) async-start(bf16[32,40,128]{2,1,0:T(8,128)(2,1)} %get-tuple-element.51), calls=%async_computation.2 | async-start | bytes 655360 | tf_op jit(solution)/shard_map/all_to_all | solution.py:620
  43.2 5.6 %collective-permute-start.2 = (bf16[512,128]{1,0:T(8,128)(2,1)S(1)}, bf16[512,128]{1,0:T(8,128)(2,1)S(1)}, u32[]{:S(2)}, u32[]{:S(2)}) collective-permute-start(bf16[512,128]{1,0:T(8,128)(2,1)S(1)} %get-tuple-element.52), channel_id=1, source_target_pairs={{0,1},{1,2},{2,3},{3,4},{4,5},{5,6},{6,7},{7,8},{8,9},{9,10},{10,1... | collective-permute-start | bytes 393224 | tf_op jit(solution)/shard_map/ppermute | solution.py:625
  45.2 4.4 %collective-permute-start.3 = (bf16[512,128]{1,0:T(8,128)(2,1)S(1)}, bf16[512,128]{1,0:T(8,128)(2,1)S(1)}, u32[]{:S(2)}, u32[]{:S(2)}) collective-permute-start(bf16[512,128]{1,0:T(8,128)(2,1)S(1)} %get-tuple-element.53), channel_id=1, source_target_pairs={{1,0},{2,1},{3,2},{4,3},{5,4},{6,5},{7,6},{8,7},{9,8},{10,9},{11,1... | collective-permute-start | bytes 393224 | tf_op jit(solution)/shard_map/ppermute | solution.py:626
  46.5 8.4 %copy-start.2 = (bf16[128,384]{1,0:T(8,128)(2,1)S(1)}, bf16[128,384]{1,0:T(8,128)(2,1)}, u32[]{:S(2)}) copy-start(bf16[128,384]{1,0:T(8,128)(2,1)} %constant.22.clone.refs_3_) | copy-start | bytes 294916
  46.5 8.4 %copy-start.3 = (bf16[192,256]{1,0:T(8,128)(2,1)S(1)}, bf16[192,256]{1,0:T(8,128)(2,1)}, u32[]{:S(2)}) copy-start(bf16[192,256]{1,0:T(8,128)(2,1)} %constant.21.clone.refs_1_) | copy-start | bytes 294916
  56.7 15.2 %all-to-all-start.3 = ((bf16[32,40,128]{2,1,0:T(8,128)(2,1)}), bf16[32,40,128]{2,1,0:T(8,128)(2,1)S(1)}, u32[]{:S(2)}, u32[]{:S(2)}) async-start(bf16[32,40,128]{2,1,0:T(8,128)(2,1)} %get-tuple-element.60), calls=%async_computation.3 | async-start | bytes 655360 | tf_op jit(solution)/shard_map/all_to_all | solution.py:620
  63.9 8.0 %copy-start = (bf16[1024,256]{1,0:T(8,128)(2,1)S(1)}, bf16[1024,256]{1,0:T(8,128)(2,1)}, u32[]{:S(2)}) copy-start(bf16[1024,256]{1,0:T(8,128)(2,1)} %constant.23.clone.refs_1_) | copy-start | bytes 1572868

commit v20 on v17

--- a/solution.py
+++ b/solution.py
@@ -252,8 +252,9 @@
     cotangent_out[...] = to_cells(cotangent[...]).astype(BF16)
 
 
-def fetch_kernel():
-    pass
+def tables_kernel(gather, scatter, _, gather_out, scatter_out):
+    gather_out[...] = gather[...]
+    scatter_out[...] = scatter[...]
 
 
 def mode_in_group(rows, lanes):
@@ -297,6 +298,13 @@
     return jnp.stack(own, axis=1).reshape(-1, LANES)
 
 
+def wide_blocks(diagonal, snaps):
+    first = mode_in_group(*diagonal.shape) < GROUP // 2
+    blocks = diagonal.astype(F32)
+    blocks = [jnp.where(first, blocks, 0.0), jnp.where(first, 0.0, blocks)]
+    return jnp.concatenate(blocks, axis=1).astype(BF16)
+
+
 def mix_kernel(snaps, slabs, received, gather, weights, scatter, back_out, diagonal_out):
     coef = to_depth(received[...].astype(F32), gather[...], snaps, slabs)
     count = coef.shape[0]
@@ -304,15 +312,16 @@
     diagonal = jnp.where(own_block(count), wide, 0.0).astype(BF16)
     diagonal_out[...] = diagonal
     rows = GROUP * snaps
-    depth = GROUP * LANES // 4
+    depth = GROUP * LANES // 2
+    wide = wide_blocks(diagonal, snaps)
     mixed = jnp.concatenate(
         [
-            dot(diagonal[g * rows : (g + 1) * rows, :], weights[g * depth : (g + 1) * depth, :])
+            dot(wide[g * rows : (g + 1) * rows, :], weights[g * depth : (g + 1) * depth, :])
             for g in range(count // rows)
         ],
         axis=0,
     )
-    mixed = jnp.where(own_half(count), mixed, swap_halves(mixed))
+    mixed = jnp.concatenate([mixed, mixed], axis=1)
     back = from_depth(mixed, scatter[...], snaps, slabs).astype(BF16)
     back_out[...] = back.reshape(back_out.shape)
 
@@ -457,14 +466,13 @@
         terms = terms.reshape(TERM_ROWS, LANES)
     else:
         modes, terms = received[...], sums[...].astype(F32)
+    cells = (dot(synthesis[...], modes.astype(BF16)) + local[...]).astype(BF16)
+    grad_out[...] = to_field(cells)
     half = LANES // 2
     for k in range(OFFSETS):
         row = (k // 2) * half
         lane = (k % 2) * half
-        stencil_out.buffer[k] = terms[row : row + half, lane : lane + half]
-    stencil_out.copy.start()
-    cells = (dot(synthesis[...], modes.astype(BF16)) + local[...]).astype(BF16)
-    grad_out[...] = to_field(cells)
+        stencil_out[k] = terms[row : row + half, lane : lane + half]
 
 
 def shape(dims, dtype):
@@ -642,19 +650,15 @@
         limit=WHOLE_VMEM,
         flops=10**8,
     )
-    weights, coef = lax.optimization_barrier((weights, coef))
+    ahead = first
     coef = send(coef)
-    share = weights.shape[0] // CHUNKS
-    (kept_weights,) = run(
-        pack_kernel,
-        [shape((HBM_BYTES // (2 * LANES), LANES), BF16)],
-        *[weights] * CHUNKS,
-        staged={k: slice(k * share, (k + 1) * share) for k in range(CHUNKS)},
-        plain=(0,),
-        scratch=[pltpu.VMEM(packed.shape, BF16), pltpu.SemaphoreType.DMA((CHUNKS,))],
-        limit=LARGE_VMEM,
-    )
-    (packed_weights,) = run(fetch_kernel, [packed], kept_weights, moved={0: 0})
+    gather, scatter = run(
+        tables_kernel,
+        [shape(gather.shape, BF16), shape(scatter.shape, BF16)],
+        gather,
+        scatter,
+        ahead,
+    )
     before, after = neighbours(first, last)
     local, lanes, outer_cells = run(
         local_kernel,
@@ -672,13 +676,24 @@
         [to_send, shape((count, GROUP * half // 2), BF16)],
         coef,
         gather,
-        packed_weights,
+        weights,
         scatter,
         sent=(0, 1),
         slots={0: slot},
         flops=4 * 10**8,
     )
+    weights, back = lax.optimization_barrier((weights, back))
     back = send(back)
+    share = weights.shape[0] // CHUNKS
+    (kept_weights,) = run(
+        pack_kernel,
+        [shape((HBM_BYTES // (2 * LANES), LANES), BF16)],
+        *[weights] * CHUNKS,
+        staged={k: slice(k * share, (k + 1) * share) for k in range(CHUNKS)},
+        plain=(0,),
+        scratch=[pltpu.VMEM(packed.shape, BF16), pltpu.SemaphoreType.DMA((CHUNKS,))],
+        limit=LARGE_VMEM,
+    )
     slab = shape((devices, 8 + TERM_ROWS // devices, LANES), BF16)
     activated, grad, first, last, back, terms = run(
         functools.partial(activate_kernel, in_slab),
@@ -762,7 +777,6 @@
         sums,
         np.ascontiguousarray(analysis.T),
         local,
-        sent=(1,),
         flops=10**8,
     )
     return (

time: 72.4 us -> 74.7 us (1.032)
  local copies, waits for them, and re-layouts: 0.06 us -> 8.97 us
  waiting for transfers between devices: 18.4 us -> 14 us
  Pallas kernels: 24.4 us -> 21.9 us
    unnamed x18 -> x28, local copies, waits for them, and re-layouts: 0.06 us -> 8.97 us
    all_to_all x4, waiting for transfers between devices: 17.6 us -> 14 us  [exchange(): lax.all_to_all(values, ('space', 'batch'), split_axis=0, concat_axis=0, t...]
    pallas_call x11, Pallas kernels: 24.4 us -> 21.9 us  [run(): pl.pallas_call(kernel, out_shape=results, in_specs=[in_hbm if k in staged...]
    ppermute x2, waiting for transfers between devices: 0.87 us -> 0.01 us  [neighbours(): after = lax.ppermute(first, 'space', [(i + 1, i) for i in range(ends)])]
  transfers between devices with their start and end apart: 8 -> 8, of which waited for: 4 -> 4; matrix products, arithmetic and copies ran while one was open for 0% -> 0% of each run, Pallas kernels for 21% -> 18%
where the time goes in v20:
time: 74.7 us; the launch traced here: 73.9 us
  starting transfers between devices  28.1 us (38%)
  Pallas kernels  21.9 us (29%)
  waiting for transfers between devices  14 us (19%)
  local copies, waits for them, and re-layouts  8.97 us (12%)
  between operations  0.85 us (1%)
    pallas_call x11, Pallas kernels, run(): pl.pallas_call(kernel, out_shape=results, in_specs=[in_hbm if k in staged...  21.9 us
    all_to_all x4, starting transfers between devices, exchange(): lax.all_to_all(values, ('space', 'batch'), split_axis=0, concat_axis=0, t...  21.4 us
    all_to_all x4, waiting for transfers between devices, exchange(): lax.all_to_all(values, ('space', 'batch'), split_axis=0, concat_axis=0, t...  14 us
    unnamed x28, local copies, waits for them, and re-layouts  8.97 us
    ppermute x2, starting transfers between devices, neighbours(): before = lax.ppermute(last, 'space', [(i, i + 1) for i in range(ends)])  4.19 us
    ppermute x2, starting transfers between devices, neighbours(): after = lax.ppermute(first, 'space', [(i + 1, i) for i in range(ends)])  2.58 us
  transfers between devices with their start and end apart: 8, of which 4 were waited for; matrix products, arithmetic and copies ran while one was open for 0% of the time, Pallas kernels for 18%

profile of v20, /device:TPU:0, one launch (start us, length us, event | category | flops | bytes accessed | tf_op | source)
XLA Modules:
  0.0 73.9 jit_solution(15308153631233657343)
XLA Ops:
  0.6 2.5 %analyse_kernel.1 = (bf16[1024,128]{1,0:T(8,128)(2,1)}, bf16[256,128]{1,0:T(8,128)(2,1)}, bf16[512,128]{1,0:T(8,128)(2,1)}, bf16[512,128]{1,0:T(8,128)(2,1)}, bf16[32,8,128]{2,1,0:T(8,128)(2,1)}) custom-call(bf16[64,2,1024]{2,1,0:T(2,128)(2,1)} %bitcast.23, bf16[256,1024]{1,0:T(8,128)(2,1)} %constant.14.clone.refs_1_), custom_call_target="tpu_custom_call" | custom-call | flops 100000000 | bytes 1441792 | tf_op jit(solution)/shard_map/analyse_kernel/pallas_call | solution.py:588
  3.1 7.3 %all-to-all-start = ((bf16[32,8,128]{2,1,0:T(8,128)(2,1)}), bf16[32,8,128]{2,1,0:T(8,128)(2,1)S(1)}, u32[]{:S(2)}, u32[]{:S(2)}) async-start(bf16[32,8,128]{2,1,0:T(8,128)(2,1)} %bitcast.24), calls=%async_computation | async-start | bytes 131072 | tf_op jit(solution)/shard_map/all_to_all | solution.py:605
  10.4 2.2 %collective-permute-start = (bf16[512,128]{1,0:T(8,128)(2,1)}, bf16[512,128]{1,0:T(8,128)(2,1)S(1)}, u32[]{:S(2)}, u32[]{:S(2)}) collective-permute-start(bf16[512,128]{1,0:T(8,128)(2,1)} %get-tuple-element.42), channel_id=1, source_target_pairs={{0,1},{1,2},{2,3},{3,4},{4,5},{5,6},{6,7},{7,8},{8,9},{9,10},{10,1... | collective-permute-start | bytes 393224 | tf_op jit(solution)/shard_map/ppermute | solution.py:610
  12.6 1.3 %collective-permute-start.1 = (bf16[512,128]{1,0:T(8,128)(2,1)}, bf16[512,128]{1,0:T(8,128)(2,1)S(1)}, u32[]{:S(2)}, u32[]{:S(2)}) collective-permute-start(bf16[512,128]{1,0:T(8,128)(2,1)} %get-tuple-element.35.refs_2_), channel_id=1, source_target_pairs={{1,0},{2,1},{3,2},{4,3},{5,4},{6,5},{7,6},{8,7},{9,8},{10,9},{11,1... | collective-permute-start | bytes 393224 | tf_op jit(solution)/shard_map/ppermute | solution.py:611
  13.9 0.0 copy-start.6
  13.9 0.9 %copy-done.6 = bf16[512,128]{1,0:T(8,128)(2,1)S(1)} copy-done((bf16[512,128]{1,0:T(8,128)(2,1)S(1)}, bf16[512,128]{1,0:T(8,128)(2,1)}, u32[]{:S(2)}) %copy-start.6) | copy-done | bytes 131096
  14.8 0.0 copy-start.9
  14.8 0.9 %copy-done.9 = bf16[128,384]{1,0:T(8,128)(2,1)S(1)} copy-done((bf16[128,384]{1,0:T(8,128)(2,1)S(1)}, bf16[128,384]{1,0:T(8,128)(2,1)}, u32[]{:S(2)}) %copy-start.9) | copy-done | bytes 98328
  15.7 0.0 copy-start.10
  15.7 0.9 %copy-done.10 = bf16[192,256]{1,0:T(8,128)(2,1)S(1)} copy-done((bf16[192,256]{1,0:T(8,128)(2,1)S(1)}, bf16[192,256]{1,0:T(8,128)(2,1)}, u32[]{:S(2)}) %copy-start.10) | copy-done | bytes 98328
  16.6 1.4 %all-to-all-done = bf16[32,8,128]{2,1,0:T(8,128)(2,1)S(1)} async-done(((bf16[32,8,128]{2,1,0:T(8,128)(2,1)}), bf16[32,8,128]{2,1,0:T(8,128)(2,1)S(1)}, u32[]{:S(2)}, u32[]{:S(2)}) %all-to-all-start) | async-done | bytes 65568 | tf_op jit(solution)/shard_map/all_to_all | solution.py:605
  18.0 0.0 copy-start
  18.0 1.9 %copy-done = bf16[8,1,24,64,64]{4,3,2,1,0:T(8,128)(2,1)S(1)} copy-done((bf16[8,1,24,64,64]{4,3,2,1,0:T(8,128)(2,1)S(1)}, bf16[8,1,24,64,64]{4,3,2,1,0:T(8,128)(2,1)}, u32[]{:S(2)}) %copy-start) | copy-done | bytes 1572888
  19.9 0.0 copy-start.4
  19.9 0.8 %copy-done.4 = bf16[32,8,128]{2,1,0:T(8,128)(2,1)S(1)} copy-done((bf16[32,8,128]{2,1,0:T(8,128)(2,1)S(1)}, bf16[32,8,128]{2,1,0:T(8,128)(2,1)}, u32[]{:S(2)}) %copy-start.4) | copy-done | bytes 65560
  20.8 1.4 %mix_kernel.1 = (bf16[32,8,128]{2,1,0:T(8,128)(2,1)S(1)}, bf16[384,256]{1,0:T(8,128)(2,1)S(1)}) custom-call(bf16[256,128]{1,0:T(8,128)(2,1)S(1)} %bitcast.19, bf16[192,256]{1,0:T(8,128)(2,1)S(1)} %get-tuple-element.36.refs_1_, bf16[12288,64]{1,0:T(8,128)(2,1)S(1)} %bitcast.16, ...), custom_call_target="tpu_custom_call", output_to_operand_aliasing={{0}: (4, {})} | custom-call | flops 400000000 | bytes 2097152 | tf_op jit(solution)/shard_map/mix_kernel/pallas_call | solution.py:588
  22.2 0.0 copy-start.5
  22.2 0.6 copy-done.5
  22.8 6.5 %all-to-all-start.1 = ((bf16[32,8,128]{2,1,0:T(8,128)(2,1)}), bf16[32,8,128]{2,1,0:T(8,128)(2,1)S(1)}, u32[]{:S(2)}, u32[]{:S(2)}) async-start(bf16[32,8,128]{2,1,0:T(8,128)(2,1)} %copy-done.5), calls=%async_computation.1 | async-start | bytes 131072 | tf_op jit(solution)/shard_map/all_to_all | solution.py:605
  29.4 0.0 collective-permute-done.refs_1_
  29.4 0.0 collective-permute-done.1.refs_2_
  29.4 0.0 copy-start.2
  29.4 1.0 %copy-done.2 = bf16[3,3,3,64,64]{4,3,2,1,0:T(8,128)(2,1)S(1)} copy-done((bf16[3,3,3,64,64]{4,3,2,1,0:T(8,128)(2,1)S(1)}, bf16[3,3,3,64,64]{4,3,2,1,0:T(8,128)(2,1)}, u32[]{:S(2)}) %copy-start.2) | copy-done | bytes 221208
  30.4 0.0 copy-start.11
  30.4 0.9 %copy-done.11 = bf16[1,64,2,1024]{3,2,1,0:T(2,128)(2,1)S(1)} copy-done((bf16[1,64,2,1024]{3,2,1,0:T(2,128)(2,1)S(1)}, bf16[1,64,2,1024]{3,2,1,0:T(2,128)(2,1)}, u32[]{:S(2)}) %copy-start.11) | copy-done | bytes 262168
  31.4 0.0 copy-start.12
  31.4 0.9 %copy-done.12 = bf16[1024,128]{1,0:T(8,128)(2,1)S(1)} copy-done((bf16[1024,128]{1,0:T(8,128)(2,1)S(1)}, bf16[1024,128]{1,0:T(8,128)(2,1)}, u32[]{:S(2)}) %copy-start.12) | copy-done | bytes 262168
  32.3 0.0 copy-start.13
  32.3 1.2 %local_kernel.1 = (f32[1024,128]{1,0:T(8,128)S(1)}, bf16[256,1024]{1,0:T(8,128)(2,1)S(1)}, bf16[1024,128]{1,0:T(8,128)(2,1)S(1)}) custom-call(bf16[1024,128]{1,0:T(8,128)(2,1)S(1)} %copy-done.12, bf16[512,128]{1,0:T(8,128)(2,1)S(1)} %collective-permute-done.refs_1_, bf16[512,128]{1,0:T(8,128)(2,1)S(1)} %collective-permute-done.1.refs_2_, ...), custom_call_target="tpu_custom_call" | custom-call | flops 8000000000 | bytes 2318336 | tf_op jit(solution)/shard_map/local_kernel/pallas_call | solution.py:588
  33.5 3.5 %all-to-all-done.1 = bf16[32,8,128]{2,1,0:T(8,128)(2,1)S(1)} async-done(((bf16[32,8,128]{2,1,0:T(8,128)(2,1)}), bf16[32,8,128]{2,1,0:T(8,128)(2,1)S(1)}, u32[]{:S(2)}, u32[]{:S(2)}) %all-to-all-start.1) | async-done | bytes 65568 | tf_op jit(solution)/shard_map/all_to_all | solution.py:605
  37.0 0.0 copy-done.13
  37.0 2.6 %activate_kernel.1 = (bf16[1024,128]{1,0:T(8,128)(2,1)S(1)}, bf16[102400,128]{1,0:T(8,128)(2,1)}, bf16[512,128]{1,0:T(8,128)(2,1)S(1)}, bf16[512,128]{1,0:T(8,128)(2,1)S(1)}, bf16[32,40,128]{2,1,0:T(8,128)(2,1)}) custom-call(bf16[256,128]{1,0:T(8,128)(2,1)S(1)} %bitcast.20, bf16[1024,256]{1,0:T(8,128)(2,1)S(1)} %copy-done.13, ...), custom_call_target="tpu_custom_call" | custom-call | flops 1000000000 | bytes 28966912 | tf_op jit(solution)/shard_map/activate_kernel/pallas_call | solution.py:588
  39.6 2.6 %all-to-all-start.2 = ((bf16[32,40,128]{2,1,0:T(8,128)(2,1)}), bf16[32,40,128]{2,1,0:T(8,128)(2,1)S(1)}, u32[]{:S(2)}, u32[]{:S(2)}) async-start(bf16[32,40,128]{2,1,0:T(8,128)(2,1)} %get-tuple-element.46), calls=%async_computation.2 | async-start | bytes 655360 | tf_op jit(solution)/shard_map/all_to_all | solution.py:605
  42.2 2.0 %collective-permute-start.2 = (bf16[512,128]{1,0:T(8,128)(2,1)S(1)}, bf16[512,128]{1,0:T(8,128)(2,1)S(1)}, u32[]{:S(2)}, u32[]{:S(2)}) collective-permute-start(bf16[512,128]{1,0:T(8,128)(2,1)S(1)} %get-tuple-element.47), channel_id=1, source_target_pairs={{0,1},{1,2},{2,3},{3,4},{4,5},{5,6},{6,7},{7,8},{8,9},{9,10},{10,1... | collective-permute-start | bytes 393224 | tf_op jit(solution)/shard_map/ppermute | solution.py:610
  44.3 1.3 %collective-permute-start.3 = (bf16[512,128]{1,0:T(8,128)(2,1)S(1)}, bf16[512,128]{1,0:T(8,128)(2,1)S(1)}, u32[]{:S(2)}, u32[]{:S(2)}) collective-permute-start(bf16[512,128]{1,0:T(8,128)(2,1)S(1)} %get-tuple-element.48), channel_id=1, source_target_pairs={{1,0},{2,1},{3,2},{4,3},{5,4},{6,5},{7,6},{8,7},{9,8},{10,9},{11,1... | collective-permute-start | bytes 393224 | tf_op jit(solution)/shard_map/ppermute | solution.py:611
  45.6 2.9 %pack_kernel.1.refs_1_ = bf16[102400,128]{1,0:T(8,128)(2,1)} custom-call(bf16[12288,64]{1,0:T(8,128)(2,1)} %bitcast.13, bf16[12288,64]{1,0:T(8,128)(2,1)} %bitcast.14, bf16[12288,64]{1,0:T(8,128)(2,1)} %bitcast.15), custom_call_target="tpu_custom_call" | custom-call | bytes 30932992 | tf_op jit(solution)/shard_map/pack_kernel/pallas_call | solution.py:588
  48.5 0.0 copy-start.7
  48.5 0.0 copy-start.8
  48.5 2.2 %output_kernel.1 = (bf16[64,2,1024]{2,1,0:T(2,128)(2,1)}, bf16[6144,128]{1,0:T(8,128)(2,1)S(1)}) custom-call(bf16[1024,128]{1,0:T(8,128)(2,1)S(1)} %get-tuple-element.49.refs_0_, bf16[102400,128]{1,0:T(8,128)(2,1)} %pack_kernel.1.refs_1_), custom_call_target="tpu_custom_call" | custom-call | flops 100000000 | bytes 28311552 | tf_op jit(solution)/shard_map/output_kernel/pallas_call | solution.py:588
  50.7 0.0 copy-start.3
  50.7 0.0 collective-permute-done.2.refs_1_
  50.8 0.0 collective-permute-done.3.refs_2_
  50.8 3.2 %all-to-all-done.2.refs_0_ = bf16[32,40,128]{2,1,0:T(8,128)(2,1)S(1)} async-done(((bf16[32,40,128]{2,1,0:T(8,128)(2,1)}), bf16[32,40,128]{2,1,0:T(8,128)(2,1)S(1)}, u32[]{:S(2)}, u32[]{:S(2)}) %all-to-all-start.2) | async-done | bytes 327712 | tf_op jit(solution)/shard_map/all_to_all | solution.py:605
  54.0 0.0 copy-done.7
  54.0 0.0 copy-done.8
  54.0 1.8 %unmix_kernel.1 = (bf16[32,40,128]{2,1,0:T(8,128)(2,1)}, bf16[384,128]{1,0:T(8,128)(2,1)S(1)}) custom-call(bf16[32,40,128]{2,1,0:T(8,128)(2,1)S(1)} %all-to-all-done.2.refs_0_, bf16[192,256]{1,0:T(8,128)(2,1)S(1)} %copy-done.8, bf16[6144,128]{1,0:T(8,128)(2,1)S(1)} %get-tuple-element.55.refs_2_, bf16[128,384]{1,0:T(8,128)(2,1)S(1)} %copy-done.7), custom_call_target="tpu_custom_call" | custom-call | flops 400000000 | bytes 2523136 | tf_op jit(solution)/shard_map/unmix_kernel/pallas_call | solution.py:588
  55.8 4.9 %all-to-all-start.3 = ((bf16[32,40,128]{2,1,0:T(8,128)(2,1)}), bf16[32,40,128]{2,1,0:T(8,128)(2,1)S(1)}, u32[]{:S(2)}, u32[]{:S(2)}) async-start(bf16[32,40,128]{2,1,0:T(8,128)(2,1)} %get-tuple-element.56), calls=%async_computation.3 | async-start | bytes 655360 | tf_op jit(solution)/shard_map/all_to_all | solution.py:605
  60.7 3.7 %weight_kernel.1 = f32[12288,64]{1,0:T(8,128)} custom-call(bf16[384,256]{1,0:T(8,128)(2,1)S(1)} %get-tuple-element.61.refs_0_, bf16[384,128]{1,0:T(8,128)(2,1)S(1)} %get-tuple-element.62.refs_1_), custom_call_target="tpu_custom_call" | custom-call | flops 400000000 | bytes 3440640 | tf_op jit(solution)/shard_map/weight_kernel/pallas_call | solution.py:588
  64.4 0.0 copy-done.3
  64.4 0.0 copy-start.1
  64.4 2.1 %local_grad_kernel.1.refs_2_ = f32[1024,128]{1,0:T(8,128)S(1)} custom-call(bf16[102400,128]{1,0:T(8,128)(2,1)} %get-tuple-element.57.refs_0_, bf16[512,128]{1,0:T(8,128)(2,1)S(1)} %collective-permute-done.2.refs_1_, bf16[512,128]{1,0:T(8,128)(2,1)S(1)} %collective-permute-done.3.refs_2_, bf16[27,64,64]{2,1,0:T(8,128)(2,1)S(1)} %bitcast.18), custom_call_target="tpu_custom_call" | custom-call | flops 700000000 | bytes 27222016 | tf_op jit(solution)/shard_map/local_grad_kernel/pallas_call | solution.py:588
  66.5 5.9 %all-to-all-done.3.refs_0_ = bf16[32,40,128]{2,1,0:T(8,128)(2,1)S(1)} async-done(((bf16[32,40,128]{2,1,0:T(8,128)(2,1)}), bf16[32,40,128]{2,1,0:T(8,128)(2,1)S(1)}, u32[]{:S(2)}, u32[]{:S(2)}) %all-to-all-start.3) | async-done | bytes 327712 | tf_op jit(solution)/shard_map/all_to_all | solution.py:605
  72.4 0.0 copy-done.1
  72.4 1.5 %finish_kernel.1 = (bf16[64,2,1024]{2,1,0:T(2,128)(2,1)}, f32[27,64,64]{2,1,0:T(8,128)}) custom-call(bf16[32,40,128]{2,1,0:T(8,128)(2,1)S(1)} %all-to-all-done.3.refs_0_, bf16[1024,256]{1,0:T(8,128)(2,1)S(1)} %copy-done.1, f32[1024,128]{1,0:T(8,128)S(1)} %local_grad_kernel.1.refs_2_), custom_call_target="tpu_custom_call" | custom-call | flops 100000000 | bytes 2080768 | tf_op jit(solution)/shard_map/finish_kernel/pallas_call | solution.py:588
  (1 shorter events, 0.0 us)
Async XLA Ops:
  3.1 14.9 %all-to-all-start = ((bf16[32,8,128]{2,1,0:T(8,128)(2,1)}), bf16[32,8,128]{2,1,0:T(8,128)(2,1)S(1)}, u32[]{:S(2)}, u32[]{:S(2)}) async-start(bf16[32,8,128]{2,1,0:T(8,128)(2,1)} %bitcast.24), calls=%async_computation | async-start | bytes 131072 | tf_op jit(solution)/shard_map/all_to_all | solution.py:605
  10.4 19.0 %collective-permute-start = (bf16[512,128]{1,0:T(8,128)(2,1)}, bf16[512,128]{1,0:T(8,128)(2,1)S(1)}, u32[]{:S(2)}, u32[]{:S(2)}) collective-permute-start(bf16[512,128]{1,0:T(8,128)(2,1)} %get-tuple-element.42), channel_id=1, source_target_pairs={{0,1},{1,2},{2,3},{3,4},{4,5},{5,6},{6,7},{7,8},{8,9},{9,10},{10,1... | collective-permute-start | bytes 393224 | tf_op jit(solution)/shard_map/ppermute | solution.py:610
  12.6 16.8 %collective-permute-start.1 = (bf16[512,128]{1,0:T(8,128)(2,1)}, bf16[512,128]{1,0:T(8,128)(2,1)S(1)}, u32[]{:S(2)}, u32[]{:S(2)}) collective-permute-start(bf16[512,128]{1,0:T(8,128)(2,1)} %get-tuple-element.35.refs_2_), channel_id=1, source_target_pairs={{1,0},{2,1},{3,2},{4,3},{5,4},{6,5},{7,6},{8,7},{9,8},{10,9},{11,1... | collective-permute-start | bytes 393224 | tf_op jit(solution)/shard_map/ppermute | solution.py:611
  13.9 0.9 %copy-start.6 = (bf16[512,128]{1,0:T(8,128)(2,1)S(1)}, bf16[512,128]{1,0:T(8,128)(2,1)}, u32[]{:S(2)}) copy-start(bf16[512,128]{1,0:T(8,128)(2,1)} %get-tuple-element.35.refs_2_) | copy-start | bytes 393220
  14.8 0.9 %copy-start.9 = (bf16[128,384]{1,0:T(8,128)(2,1)S(1)}, bf16[128,384]{1,0:T(8,128)(2,1)}, u32[]{:S(2)}) copy-start(bf16[128,384]{1,0:T(8,128)(2,1)} %constant.16.clone.refs_1_) | copy-start | bytes 294916
  15.7 0.9 %copy-start.10 = (bf16[192,256]{1,0:T(8,128)(2,1)S(1)}, bf16[192,256]{1,0:T(8,128)(2,1)}, u32[]{:S(2)}) copy-start(bf16[192,256]{1,0:T(8,128)(2,1)} %constant.15.clone.refs_0_) | copy-start | bytes 294916
  18.0 1.9 %copy-start = (bf16[8,1,24,64,64]{4,3,2,1,0:T(8,128)(2,1)S(1)}, bf16[8,1,24,64,64]{4,3,2,1,0:T(8,128)(2,1)}, u32[]{:S(2)}) copy-start(bf16[8,1,24,64,64]{4,3,2,1,0:T(8,128)(2,1)} %param.13) | copy-start | bytes 4718596
  19.9 0.8 %copy-start.4 = (bf16[32,8,128]{2,1,0:T(8,128)(2,1)S(1)}, bf16[32,8,128]{2,1,0:T(8,128)(2,1)}, u32[]{:S(2)}) copy-start(bf16[32,8,128]{2,1,0:T(8,128)(2,1)} %get-tuple-element.38.refs_4_) | copy-start | bytes 196612
  22.2 0.6 copy-start.5
  22.8 14.2 %all-to-all-start.1 = ((bf16[32,8,128]{2,1,0:T(8,128)(2,1)}), bf16[32,8,128]{2,1,0:T(8,128)(2,1)S(1)}, u32[]{:S(2)}, u32[]{:S(2)}) async-start(bf16[32,8,128]{2,1,0:T(8,128)(2,1)} %copy-done.5), calls=%async_computation.1 | async-start | bytes 131072 | tf_op jit(solution)/shard_map/all_to_all | solution.py:605
  29.4 1.0 %copy-start.2 = (bf16[3,3,3,64,64]{4,3,2,1,0:T(8,128)(2,1)S(1)}, bf16[3,3,3,64,64]{4,3,2,1,0:T(8,128)(2,1)}, u32[]{:S(2)}) copy-start(bf16[3,3,3,64,64]{4,3,2,1,0:T(8,128)(2,1)} %param.14) | copy-start | bytes 663556
  30.4 0.9 %copy-start.11 = (bf16[1,64,2,1024]{3,2,1,0:T(2,128)(2,1)S(1)}, bf16[1,64,2,1024]{3,2,1,0:T(2,128)(2,1)}, u32[]{:S(2)}) copy-start(bf16[1,64,2,1024]{3,2,1,0:T(2,128)(2,1)} %param.12) | copy-start | bytes 786436
  31.4 0.9 %copy-start.12 = (bf16[1024,128]{1,0:T(8,128)(2,1)S(1)}, bf16[1024,128]{1,0:T(8,128)(2,1)}, u32[]{:S(2)}) copy-start(bf16[1024,128]{1,0:T(8,128)(2,1)} %get-tuple-element.41.refs_0_) | copy-start | bytes 786436
  32.3 4.7 %copy-start.13 = (bf16[1024,256]{1,0:T(8,128)(2,1)S(1)}, bf16[1024,256]{1,0:T(8,128)(2,1)}, u32[]{:S(2)}) copy-start(bf16[1024,256]{1,0:T(8,128)(2,1)} %constant.17.clone.refs_1_) | copy-start | bytes 1572868
  39.6 14.3 %all-to-all-start.2 = ((bf16[32,40,128]{2,1,0:T(8,128)(2,1)}), bf16[32,40,128]{2,1,0:T(8,128)(2,1)S(1)}, u32[]{:S(2)}, u32[]{:S(2)}) async-start(bf16[32,40,128]{2,1,0:T(8,128)(2,1)} %get-tuple-element.46), calls=%async_computation.2 | async-start | bytes 655360 | tf_op jit(solution)/shard_map/all_to_all | solution.py:605
  42.2 8.5 %collective-permute-start.2 = (bf16[512,128]{1,0:T(8,128)(2,1)S(1)}, bf16[512,128]{1,0:T(8,128)(2,1)S(1)}, u32[]{:S(2)}, u32[]{:S(2)}) collective-permute-start(bf16[512,128]{1,0:T(8,128)(2,1)S(1)} %get-tuple-element.47), channel_id=1, source_target_pairs={{0,1},{1,2},{2,3},{3,4},{4,5},{5,6},{6,7},{7,8},{8,9},{9,10},{10,1... | collective-permute-start | bytes 393224 | tf_op jit(solution)/shard_map/ppermute | solution.py:610
  44.3 6.5 %collective-permute-start.3 = (bf16[512,128]{1,0:T(8,128)(2,1)S(1)}, bf16[512,128]{1,0:T(8,128)(2,1)S(1)}, u32[]{:S(2)}, u32[]{:S(2)}) collective-permute-start(bf16[512,128]{1,0:T(8,128)(2,1)S(1)} %get-tuple-element.48), channel_id=1, source_target_pairs={{1,0},{2,1},{3,2},{4,3},{5,4},{6,5},{7,6},{8,7},{9,8},{10,9},{11,1... | collective-permute-start | bytes 393224 | tf_op jit(solution)/shard_map/ppermute | solution.py:611
  48.5 5.5 %copy-start.7 = (bf16[128,384]{1,0:T(8,128)(2,1)S(1)}, bf16[128,384]{1,0:T(8,128)(2,1)}, u32[]{:S(2)}) copy-start(bf16[128,384]{1,0:T(8,128)(2,1)} %constant.19.clone.refs_3_) | copy-start | bytes 294916
  48.5 5.5 %copy-start.8 = (bf16[192,256]{1,0:T(8,128)(2,1)S(1)}, bf16[192,256]{1,0:T(8,128)(2,1)}, u32[]{:S(2)}) copy-start(bf16[192,256]{1,0:T(8,128)(2,1)} %constant.18.clone.refs_1_) | copy-start | bytes 294916
  50.7 13.7 %copy-start.3 = (bf16[3,3,3,64,64]{4,3,2,1,0:T(8,128)(2,1)S(1)}, bf16[3,3,3,64,64]{4,3,2,1,0:T(8,128)(2,1)}, u32[]{:S(2)}) copy-start(bf16[3,3,3,64,64]{4,3,2,1,0:T(8,128)(2,1)} %param.14) | copy-start | bytes 663556
  55.8 16.6 %all-to-all-start.3 = ((bf16[32,40,128]{2,1,0:T(8,128)(2,1)}), bf16[32,40,128]{2,1,0:T(8,128)(2,1)S(1)}, u32[]{:S(2)}, u32[]{:S(2)}) async-start(bf16[32,40,128]{2,1,0:T(8,128)(2,1)} %get-tuple-element.56), calls=%async_computation.3 | async-start | bytes 655360 | tf_op jit(solution)/shard_map/all_to_all | solution.py:605
  64.4 8.0 %copy-start.1 = (bf16[1024,256]{1,0:T(8,128)(2,1)S(1)}, bf16[1024,256]{1,0:T(8,128)(2,1)}, u32[]{:S(2)}) copy-start(bf16[1024,256]{1,0:T(8,128)(2,1)} %constant.20.clone.refs_1_) | copy-start | bytes 1572868

commit v21 on v16

--- a/solution.py
+++ b/solution.py
@@ -327,21 +327,31 @@
     back_out,
     terms_out,
     spread,
+    before_grad,
 ):
-    pre = dot(synthesis[...], received[...]) + local[...]
-    cdf = 0.5 * (1.0 + lax.erf(pre * inv_root_two))
-    density = jnp.exp(-0.5 * pre * pre) * inv_root_two_pi
-    activated_out[...] = (pre * cdf).astype(BF16)
-    grad = (cotangent[...].astype(F32) * (cdf + pre * density)).astype(BF16)
-    back = dot(synthesis[...], grad, (0, 0))
-    rounded = grad
-    grad = grad.astype(F32)
-    first, last = edge_layers(grad)
+    before_grad[...] = dot(synthesis[...], received[...]) + local[...]
     spread[0:NY, :] = jnp.zeros((NY, 3 * LANES), BF16)
     spread[NY + CELLS : 2 * NY + CELLS, :] = jnp.zeros((NY, 3 * LANES), BF16)
-    spread[NY : NY + CELLS, 0:LANES] = from_above(grad).astype(BF16)
-    spread[NY : NY + CELLS, LANES : 2 * LANES] = grad.astype(BF16)
-    spread[NY : NY + CELLS, 2 * LANES :] = from_below(grad).astype(BF16)
+
+    def block(k, carry):
+        rows = pl.ds(pl.multiple_of(k * STEP, STEP), STEP)
+        pre = before_grad[rows, :]
+        cdf = 0.5 * (1.0 + lax.erf(pre * inv_root_two))
+        density = jnp.exp(-0.5 * pre * pre) * inv_root_two_pi
+        activated_out[rows, :] = (pre * cdf).astype(BF16)
+        rounded = (cotangent[rows, :].astype(F32) * (cdf + pre * density)).astype(BF16)
+        grad_out.buffer[rows, :] = rounded
+        grad = rounded.astype(F32)
+        rows = pl.ds(pl.multiple_of(k * STEP + NY, NY), STEP)
+        spread[rows, 0:LANES] = from_above(grad).astype(BF16)
+        spread[rows, LANES : 2 * LANES] = rounded
+        spread[rows, 2 * LANES : 3 * LANES] = from_below(grad).astype(BF16)
+        return carry
+
+    lax.fori_loop(0, CELLS // STEP, block, None)
+    grad_out.copy.start()
+    back = dot(synthesis[...], grad_out.buffer[...], (0, 0))
+    first, last = edge_layers(grad_out.buffer[...].astype(F32))
     half = LANES // 2
     low = low_lanes(half)
     twice = {}
@@ -367,7 +377,6 @@
     else:
         back_out[...] = back.astype(BF16)
         terms_out[...] = terms.astype(BF16)
-    grad_out[...] = rounded
     first_out[...] = first
     last_out[...] = last
 
@@ -690,7 +699,7 @@
         outer_cells,
         lanes,
         sent={1: CELLS, 2: None, 3: None, 4: None},
-        scratch=[pltpu.VMEM((CELLS + 2 * NY, 3 * LANES), BF16)],
+        scratch=[pltpu.VMEM((CELLS + 2 * NY, 3 * LANES), BF16), pltpu.VMEM((CELLS, LANES), F32)],
         flops=10**9,
     )
     if in_slab:

time: 69.6 us -> 69.9 us (level)
  no operation moved by 1% of the time
where the time goes in v21:
time: 69.9 us; the launch traced here: 69.4 us
  starting transfers between devices  25.6 us (37%)
  Pallas kernels  21.9 us (31%)
  waiting for transfers between devices  21 us (30%)
  between operations  0.87 us (1%)
    pallas_call x10, Pallas kernels, run(): pl.pallas_call(kernel, out_shape=results, in_specs=[in_hbm if k in staged...  21.9 us
    all_to_all x4, waiting for transfers between devices, exchange(): lax.all_to_all(values, ('space', 'batch'), split_axis=0, concat_axis=0, t...  20.1 us
    all_to_all x4, starting transfers between devices, exchange(): lax.all_to_all(values, ('space', 'batch'), split_axis=0, concat_axis=0, t...  18.8 us
    ppermute x2, starting transfers between devices, neighbours(): before = lax.ppermute(last, 'space', [(i, i + 1) for i in range(ends)])  4.19 us
    ppermute x2, starting transfers between devices, neighbours(): after = lax.ppermute(first, 'space', [(i + 1, i) for i in range(ends)])  2.58 us
  transfers between devices with their start and end apart: 8, of which 5 were waited for; matrix products, arithmetic and copies ran while one was open for 0% of the time, Pallas kernels for 18%

profile of v21, /device:TPU:0, one launch (start us, length us, event | category | flops | bytes accessed | tf_op | source)
XLA Modules:
  0.0 69.4 jit_solution(2794432852179302508)
XLA Ops:
  0.6 3.2 %analyse_kernel.1 = (bf16[1024,128]{1,0:T(8,128)(2,1)}, bf16[256,128]{1,0:T(8,128)(2,1)}, bf16[512,128]{1,0:T(8,128)(2,1)}, bf16[512,128]{1,0:T(8,128)(2,1)}, bf...) custom-call(bf16[64,2,1024]{2,1,0:T(2,128)(2,1)} %bitcast.22, bf16[256,1024]{1,0:T(8,128)(2,1)} %constant.14.clone.refs_1_, ...), custom_call_target="tpu_custom_call" | custom-call | flops 100000000 | bytes 32374784 | tf_op jit(solution)/shard_map/analyse_kernel/pallas_call | solution.py:584
  3.9 7.3 %all-to-all-start = ((bf16[32,8,128]{2,1,0:T(8,128)(2,1)}), bf16[32,8,128]{2,1,0:T(8,128)(2,1)S(1)}, u32[]{:S(2)}, u32[]{:S(2)}) async-start(bf16[32,8,128]{2,1,0:T(8,128)(2,1)} %bitcast.23), calls=%async_computation | async-start | bytes 131072 | tf_op jit(solution)/shard_map/all_to_all | solution.py:601
  11.2 2.2 %collective-permute-start = (bf16[512,128]{1,0:T(8,128)(2,1)}, bf16[512,128]{1,0:T(8,128)(2,1)S(1)}, u32[]{:S(2)}, u32[]{:S(2)}) collective-permute-start(bf16[512,128]{1,0:T(8,128)(2,1)} %get-tuple-element.36), channel_id=1, source_target_pairs={{0,1},{1,2},{2,3},{3,4},{4,5},{5,6},{6,7},{7,8},{8,9},{9,10},{10,1... | collective-permute-start | bytes 393224 | tf_op jit(solution)/shard_map/ppermute | solution.py:606
  13.3 1.3 %collective-permute-start.1 = (bf16[512,128]{1,0:T(8,128)(2,1)}, bf16[512,128]{1,0:T(8,128)(2,1)S(1)}, u32[]{:S(2)}, u32[]{:S(2)}) collective-permute-start(bf16[512,128]{1,0:T(8,128)(2,1)} %get-tuple-element.37), channel_id=1, source_target_pairs={{1,0},{2,1},{3,2},{4,3},{5,4},{6,5},{7,6},{8,7},{9,8},{10,9},{11,1... | collective-permute-start | bytes 393224 | tf_op jit(solution)/shard_map/ppermute | solution.py:607
  14.6 0.0 copy-start.4
  14.7 0.0 copy-start.5
  14.7 0.0 copy-start.1
  14.7 0.0 copy-start.6
  14.7 0.0 copy-start.7
  14.7 1.5 %fetch_kernel.1.refs_2_ = bf16[6144,128]{1,0:T(8,128)(2,1)S(1)} custom-call(bf16[102400,128]{1,0:T(8,128)(2,1)} %get-tuple-element.32.refs_0_.refs_1_), custom_call_target="tpu_custom_call" | custom-call | bytes 27787264 | tf_op jit(solution)/shard_map/fetch_kernel/pallas_call | solution.py:584
  16.2 2.6 %all-to-all-done = bf16[32,8,128]{2,1,0:T(8,128)(2,1)S(1)} async-done(((bf16[32,8,128]{2,1,0:T(8,128)(2,1)}), bf16[32,8,128]{2,1,0:T(8,128)(2,1)S(1)}, u32[]{:S(2)}, u32[]{:S(2)}) %all-to-all-start) | async-done | bytes 65568 | tf_op jit(solution)/shard_map/all_to_all | solution.py:601
  18.8 0.0 copy-done.4
  18.8 0.0 copy-done.5
  18.8 1.8 %mix_kernel.1 = (bf16[32,8,128]{2,1,0:T(8,128)(2,1)}, bf16[384,256]{1,0:T(8,128)(2,1)S(1)}) custom-call(bf16[256,128]{1,0:T(8,128)(2,1)S(1)} %bitcast.15, bf16[192,256]{1,0:T(8,128)(2,1)S(1)} %copy-done.5, bf16[6144,128]{1,0:T(8,128)(2,1)S(1)} %fetch_kernel.1.refs_2_, bf16[128,384]{1,0:T(8,128)(2,1)S(1)} %copy-done.4, ...), custom_call_target="tpu_custom_call", output_to_operand_aliasing={{0}: (4, {})} | custom-call | flops 400000000 | bytes 2097152 | tf_op jit(solution)/shard_map/mix_kernel/pallas_call | solution.py:584
  20.6 5.4 %all-to-all-start.1 = ((bf16[32,8,128]{2,1,0:T(8,128)(2,1)}), bf16[32,8,128]{2,1,0:T(8,128)(2,1)S(1)}, u32[]{:S(2)}, u32[]{:S(2)}) async-start(bf16[32,8,128]{2,1,0:T(8,128)(2,1)} %get-tuple-element.34), calls=%async_computation.1 | async-start | bytes 131072 | tf_op jit(solution)/shard_map/all_to_all | solution.py:601
  26.0 0.0 collective-permute-done.refs_1_
  26.0 0.0 collective-permute-done.1.refs_2_
  26.0 0.0 copy-done.1
  26.0 0.0 copy-done.6
  26.0 0.0 copy-done.7
  26.0 0.0 copy-start.8
  26.0 1.2 %local_kernel.1 = (f32[1024,128]{1,0:T(8,128)S(1)}, bf16[256,1024]{1,0:T(8,128)(2,1)S(1)}, bf16[1024,128]{1,0:T(8,128)(2,1)S(1)}) custom-call(bf16[1024,128]{1,0:T(8,128)(2,1)S(1)} %copy-done.7, bf16[512,128]{1,0:T(8,128)(2,1)S(1)} %collective-permute-done.refs_1_, bf16[512,128]{1,0:T(8,128)(2,1)S(1)} %collective-permute-done.1.refs_2_, ...), custom_call_target="tpu_custom_call" | custom-call | flops 8000000000 | bytes 2318336 | tf_op jit(solution)/shard_map/local_kernel/pallas_call | solution.py:584
  27.2 6.4 %all-to-all-done.1 = bf16[32,8,128]{2,1,0:T(8,128)(2,1)S(1)} async-done(((bf16[32,8,128]{2,1,0:T(8,128)(2,1)}), bf16[32,8,128]{2,1,0:T(8,128)(2,1)S(1)}, u32[]{:S(2)}, u32[]{:S(2)}) %all-to-all-start.1) | async-done | bytes 65568 | tf_op jit(solution)/shard_map/all_to_all | solution.py:601
  33.6 0.0 copy-done.8
  33.6 3.0 %activate_kernel.1 = (bf16[1024,128]{1,0:T(8,128)(2,1)S(1)}, bf16[102400,128]{1,0:T(8,128)(2,1)}, bf16[512,128]{1,0:T(8,128)(2,1)S(1)}, bf16[512,128]{1,0:T(8,128)(2,1)S(1)}, bf16[32,40,128]{2,1,0:T(8,128)(2,1)}) custom-call(bf16[256,128]{1,0:T(8,128)(2,1)S(1)} %bitcast.16, bf16[1024,256]{1,0:T(8,128)(2,1)S(1)} %copy-done.8, ...), custom_call_target="tpu_custom_call" | custom-call | flops 1000000000 | bytes 28966912 | tf_op jit(solution)/shard_map/activate_kernel/pallas_call | solution.py:584
  36.6 2.6 %all-to-all-start.2 = ((bf16[32,40,128]{2,1,0:T(8,128)(2,1)}), bf16[32,40,128]{2,1,0:T(8,128)(2,1)S(1)}, u32[]{:S(2)}, u32[]{:S(2)}) async-start(bf16[32,40,128]{2,1,0:T(8,128)(2,1)} %get-tuple-element.41), calls=%async_computation.2 | async-start | bytes 655360 | tf_op jit(solution)/shard_map/all_to_all | solution.py:601
  39.2 2.0 %collective-permute-start.2 = (bf16[512,128]{1,0:T(8,128)(2,1)S(1)}, bf16[512,128]{1,0:T(8,128)(2,1)S(1)}, u32[]{:S(2)}, u32[]{:S(2)}) collective-permute-start(bf16[512,128]{1,0:T(8,128)(2,1)S(1)} %get-tuple-element.42), channel_id=1, source_target_pairs={{0,1},{1,2},{2,3},{3,4},{4,5},{5,6},{6,7},{7,8},{8,9},{9,10},{10,1... | collective-permute-start | bytes 393224 | tf_op jit(solution)/shard_map/ppermute | solution.py:606
  41.2 1.3 %collective-permute-start.3 = (bf16[512,128]{1,0:T(8,128)(2,1)S(1)}, bf16[512,128]{1,0:T(8,128)(2,1)S(1)}, u32[]{:S(2)}, u32[]{:S(2)}) collective-permute-start(bf16[512,128]{1,0:T(8,128)(2,1)S(1)} %get-tuple-element.43), channel_id=1, source_target_pairs={{1,0},{2,1},{3,2},{4,3},{5,4},{6,5},{7,6},{8,7},{9,8},{10,9},{11,1... | collective-permute-start | bytes 393224 | tf_op jit(solution)/shard_map/ppermute | solution.py:607
  42.5 0.0 copy-start.2
  42.5 0.0 copy-start.3
  42.5 2.2 %output_kernel.1 = (bf16[64,2,1024]{2,1,0:T(2,128)(2,1)}, bf16[6144,128]{1,0:T(8,128)(2,1)S(1)}) custom-call(bf16[1024,128]{1,0:T(8,128)(2,1)S(1)} %get-tuple-element.44.refs_0_, bf16[102400,128]{1,0:T(8,128)(2,1)} %get-tuple-element.32.refs_0_.refs_1_), custom_call_target="tpu_custom_call" | custom-call | flops 100000000 | bytes 28311552 | tf_op jit(solution)/shard_map/output_kernel/pallas_call | solution.py:584
  44.7 0.0 collective-permute-done.2.refs_1_
  44.7 0.9 %collective-permute-done.3.refs_2_ = bf16[512,128]{1,0:T(8,128)(2,1)S(1)} collective-permute-done((bf16[512,128]{1,0:T(8,128)(2,1)S(1)}, bf16[512,128]{1,0:T(8,128)(2,1)S(1)}, u32[]{:S(2)}, u32[]{:S(2)}) %collective-permute-start.3) | collective-permute-done | bytes 131104 | tf_op jit(solution)/shard_map/ppermute | solution.py:607
  45.6 5.3 %all-to-all-done.2.refs_0_ = bf16[32,40,128]{2,1,0:T(8,128)(2,1)S(1)} async-done(((bf16[32,40,128]{2,1,0:T(8,128)(2,1)}), bf16[32,40,128]{2,1,0:T(8,128)(2,1)S(1)}, u32[]{:S(2)}, u32[]{:S(2)}) %all-to-all-start.2) | async-done | bytes 327712 | tf_op jit(solution)/shard_map/all_to_all | solution.py:601
  50.9 0.0 copy-done.2
  50.9 0.0 copy-done.3
  50.9 1.8 %unmix_kernel.1 = (bf16[32,40,128]{2,1,0:T(8,128)(2,1)}, bf16[384,128]{1,0:T(8,128)(2,1)S(1)}) custom-call(bf16[32,40,128]{2,1,0:T(8,128)(2,1)S(1)} %all-to-all-done.2.refs_0_, bf16[192,256]{1,0:T(8,128)(2,1)S(1)} %copy-done.3, bf16[6144,128]{1,0:T(8,128)(2,1)S(1)} %get-tuple-element.49.refs_2_, bf16[128,384]{1,0:T(8,128)(2,1)S(1)} %copy-done.2), custom_call_target="tpu_custom_call" | custom-call | flops 400000000 | bytes 2523136 | tf_op jit(solution)/shard_map/unmix_kernel/pallas_call | solution.py:584
  52.7 3.5 %all-to-all-start.3 = ((bf16[32,40,128]{2,1,0:T(8,128)(2,1)}), bf16[32,40,128]{2,1,0:T(8,128)(2,1)S(1)}, u32[]{:S(2)}, u32[]{:S(2)}) async-start(bf16[32,40,128]{2,1,0:T(8,128)(2,1)} %get-tuple-element.50), calls=%async_computation.3 | async-start | bytes 655360 | tf_op jit(solution)/shard_map/all_to_all | solution.py:601
  56.2 3.7 %weight_kernel.1 = f32[12288,64]{1,0:T(8,128)} custom-call(bf16[384,256]{1,0:T(8,128)(2,1)S(1)} %get-tuple-element.55.refs_0_, bf16[384,128]{1,0:T(8,128)(2,1)S(1)} %get-tuple-element.56.refs_1_), custom_call_target="tpu_custom_call" | custom-call | flops 400000000 | bytes 3440640 | tf_op jit(solution)/shard_map/weight_kernel/pallas_call | solution.py:584
  59.9 0.0 copy-start
  59.9 2.1 %local_grad_kernel.1.refs_2_ = f32[1024,128]{1,0:T(8,128)S(1)} custom-call(bf16[102400,128]{1,0:T(8,128)(2,1)} %get-tuple-element.51.refs_0_, bf16[512,128]{1,0:T(8,128)(2,1)S(1)} %collective-permute-done.2.refs_1_, bf16[512,128]{1,0:T(8,128)(2,1)S(1)} %collective-permute-done.3.refs_2_, bf16[27,64,64]{2,1,0:T(8,128)(2,1)S(1)} %bitcast.14), custom_call_target="tpu_custom_call" | custom-call | flops 700000000 | bytes 27222016 | tf_op jit(solution)/shard_map/local_grad_kernel/pallas_call | solution.py:584
  62.0 5.9 %all-to-all-done.3.refs_0_ = bf16[32,40,128]{2,1,0:T(8,128)(2,1)S(1)} async-done(((bf16[32,40,128]{2,1,0:T(8,128)(2,1)}), bf16[32,40,128]{2,1,0:T(8,128)(2,1)S(1)}, u32[]{:S(2)}, u32[]{:S(2)}) %all-to-all-start.3) | async-done | bytes 327712 | tf_op jit(solution)/shard_map/all_to_all | solution.py:601
  67.9 0.0 copy-done
  67.9 1.5 %finish_kernel.1 = (bf16[64,2,1024]{2,1,0:T(2,128)(2,1)}, f32[27,64,64]{2,1,0:T(8,128)}) custom-call(bf16[32,40,128]{2,1,0:T(8,128)(2,1)S(1)} %all-to-all-done.3.refs_0_, bf16[1024,256]{1,0:T(8,128)(2,1)S(1)} %copy-done, f32[1024,128]{1,0:T(8,128)S(1)} %local_grad_kernel.1.refs_2_), custom_call_target="tpu_custom_call" | custom-call | flops 100000000 | bytes 2080768 | tf_op jit(solution)/shard_map/finish_kernel/pallas_call | solution.py:584
Async XLA Ops:
  3.9 14.9 %all-to-all-start = ((bf16[32,8,128]{2,1,0:T(8,128)(2,1)}), bf16[32,8,128]{2,1,0:T(8,128)(2,1)S(1)}, u32[]{:S(2)}, u32[]{:S(2)}) async-start(bf16[32,8,128]{2,1,0:T(8,128)(2,1)} %bitcast.23), calls=%async_computation | async-start | bytes 131072 | tf_op jit(solution)/shard_map/all_to_all | solution.py:601
  11.2 14.8 %collective-permute-start = (bf16[512,128]{1,0:T(8,128)(2,1)}, bf16[512,128]{1,0:T(8,128)(2,1)S(1)}, u32[]{:S(2)}, u32[]{:S(2)}) collective-permute-start(bf16[512,128]{1,0:T(8,128)(2,1)} %get-tuple-element.36), channel_id=1, source_target_pairs={{0,1},{1,2},{2,3},{3,4},{4,5},{5,6},{6,7},{7,8},{8,9},{9,10},{10,1... | collective-permute-start | bytes 393224 | tf_op jit(solution)/shard_map/ppermute | solution.py:606
  13.3 12.7 %collective-permute-start.1 = (bf16[512,128]{1,0:T(8,128)(2,1)}, bf16[512,128]{1,0:T(8,128)(2,1)S(1)}, u32[]{:S(2)}, u32[]{:S(2)}) collective-permute-start(bf16[512,128]{1,0:T(8,128)(2,1)} %get-tuple-element.37), channel_id=1, source_target_pairs={{1,0},{2,1},{3,2},{4,3},{5,4},{6,5},{7,6},{8,7},{9,8},{10,9},{11,1... | collective-permute-start | bytes 393224 | tf_op jit(solution)/shard_map/ppermute | solution.py:607
  14.6 4.1 %copy-start.4 = (bf16[128,384]{1,0:T(8,128)(2,1)S(1)}, bf16[128,384]{1,0:T(8,128)(2,1)}, u32[]{:S(2)}) copy-start(bf16[128,384]{1,0:T(8,128)(2,1)} %constant.16.clone.refs_3_) | copy-start | bytes 294916
  14.7 4.1 %copy-start.5 = (bf16[192,256]{1,0:T(8,128)(2,1)S(1)}, bf16[192,256]{1,0:T(8,128)(2,1)}, u32[]{:S(2)}) copy-start(bf16[192,256]{1,0:T(8,128)(2,1)} %constant.15.clone.refs_1_) | copy-start | bytes 294916
  14.7 11.3 %copy-start.1 = (bf16[3,3,3,64,64]{4,3,2,1,0:T(8,128)(2,1)S(1)}, bf16[3,3,3,64,64]{4,3,2,1,0:T(8,128)(2,1)}, u32[]{:S(2)}) copy-start(bf16[3,3,3,64,64]{4,3,2,1,0:T(8,128)(2,1)} %param.14) | copy-start | bytes 663556
  14.7 11.3 %copy-start.6 = (bf16[1,64,2,1024]{3,2,1,0:T(2,128)(2,1)S(1)}, bf16[1,64,2,1024]{3,2,1,0:T(2,128)(2,1)}, u32[]{:S(2)}) copy-start(bf16[1,64,2,1024]{3,2,1,0:T(2,128)(2,1)} %param.12) | copy-start | bytes 786436
  14.7 11.3 %copy-start.7 = (bf16[1024,128]{1,0:T(8,128)(2,1)S(1)}, bf16[1024,128]{1,0:T(8,128)(2,1)}, u32[]{:S(2)}) copy-start(bf16[1024,128]{1,0:T(8,128)(2,1)} %get-tuple-element.35.refs_0_) | copy-start | bytes 786436
  20.6 13.0 %all-to-all-start.1 = ((bf16[32,8,128]{2,1,0:T(8,128)(2,1)}), bf16[32,8,128]{2,1,0:T(8,128)(2,1)S(1)}, u32[]{:S(2)}, u32[]{:S(2)}) async-start(bf16[32,8,128]{2,1,0:T(8,128)(2,1)} %get-tuple-element.34), calls=%async_computation.1 | async-start | bytes 131072 | tf_op jit(solution)/shard_map/all_to_all | solution.py:601
  26.0 7.6 %copy-start.8 = (bf16[1024,256]{1,0:T(8,128)(2,1)S(1)}, bf16[1024,256]{1,0:T(8,128)(2,1)}, u32[]{:S(2)}) copy-start(bf16[1024,256]{1,0:T(8,128)(2,1)} %constant.17.clone.refs_1_) | copy-start | bytes 1572868
  36.6 14.3 %all-to-all-start.2 = ((bf16[32,40,128]{2,1,0:T(8,128)(2,1)}), bf16[32,40,128]{2,1,0:T(8,128)(2,1)S(1)}, u32[]{:S(2)}, u32[]{:S(2)}) async-start(bf16[32,40,128]{2,1,0:T(8,128)(2,1)} %get-tuple-element.41), calls=%async_computation.2 | async-start | bytes 655360 | tf_op jit(solution)/shard_map/all_to_all | solution.py:601
  39.2 5.6 %collective-permute-start.2 = (bf16[512,128]{1,0:T(8,128)(2,1)S(1)}, bf16[512,128]{1,0:T(8,128)(2,1)S(1)}, u32[]{:S(2)}, u32[]{:S(2)}) collective-permute-start(bf16[512,128]{1,0:T(8,128)(2,1)S(1)} %get-tuple-element.42), channel_id=1, source_target_pairs={{0,1},{1,2},{2,3},{3,4},{4,5},{5,6},{6,7},{7,8},{8,9},{9,10},{10,1... | collective-permute-start | bytes 393224 | tf_op jit(solution)/shard_map/ppermute | solution.py:606
  41.2 4.4 %collective-permute-start.3 = (bf16[512,128]{1,0:T(8,128)(2,1)S(1)}, bf16[512,128]{1,0:T(8,128)(2,1)S(1)}, u32[]{:S(2)}, u32[]{:S(2)}) collective-permute-start(bf16[512,128]{1,0:T(8,128)(2,1)S(1)} %get-tuple-element.43), channel_id=1, source_target_pairs={{1,0},{2,1},{3,2},{4,3},{5,4},{6,5},{7,6},{8,7},{9,8},{10,9},{11,1... | collective-permute-start | bytes 393224 | tf_op jit(solution)/shard_map/ppermute | solution.py:607
  42.5 8.4 %copy-start.2 = (bf16[128,384]{1,0:T(8,128)(2,1)S(1)}, bf16[128,384]{1,0:T(8,128)(2,1)}, u32[]{:S(2)}) copy-start(bf16[128,384]{1,0:T(8,128)(2,1)} %constant.19.clone.refs_3_) | copy-start | bytes 294916
  42.5 8.4 %copy-start.3 = (bf16[192,256]{1,0:T(8,128)(2,1)S(1)}, bf16[192,256]{1,0:T(8,128)(2,1)}, u32[]{:S(2)}) copy-start(bf16[192,256]{1,0:T(8,128)(2,1)} %constant.18.clone.refs_1_) | copy-start | bytes 294916
  52.7 15.2 %all-to-all-start.3 = ((bf16[32,40,128]{2,1,0:T(8,128)(2,1)}), bf16[32,40,128]{2,1,0:T(8,128)(2,1)S(1)}, u32[]{:S(2)}, u32[]{:S(2)}) async-start(bf16[32,40,128]{2,1,0:T(8,128)(2,1)} %get-tuple-element.50), calls=%async_computation.3 | async-start | bytes 655360 | tf_op jit(solution)/shard_map/all_to_all | solution.py:601
  59.9 8.0 %copy-start = (bf16[1024,256]{1,0:T(8,128)(2,1)S(1)}, bf16[1024,256]{1,0:T(8,128)(2,1)}, u32[]{:S(2)}) copy-start(bf16[1024,256]{1,0:T(8,128)(2,1)} %constant.20.clone.refs_1_) | copy-start | bytes 1572868

commit v22 on v18

--- a/solution.py
+++ b/solution.py
@@ -206,14 +206,15 @@
                     )
 
 
-def analyse_kernel(field, analysis, cells_out, coef_out, first_out, last_out, _):
+def analyse_kernel(field, analysis, cells_out, coef_out, _):
     cells = to_cells(field[...])
     rounded = cells.astype(BF16)
     coef_out[...] = dot(analysis[...], rounded).astype(BF16)
     cells_out[...] = rounded
-    first, last = edge_layers(cells)
-    first_out[...] = first
-    last_out[...] = last
+
+
+def edges_kernel(cells, first_out, last_out):
+    first_out[...], last_out[...] = edge_layers(cells[...].astype(F32))
 
 
 def pack_kernel(*refs):
@@ -630,14 +631,14 @@
 
     packed = shape((weights.shape[0] // 2, LANES), BF16)
     to_send = shape((devices, modes, LANES), BF16) if modes % 8 == 0 else plane_modes
-    cells, coef, first, last, slot = run(
+    cells, coef, slot = run(
         analyse_kernel,
-        [wide, plane_modes, edge, edge, to_send],
+        [wide, plane_modes, to_send],
         snapshots.reshape(field.shape),
         analysis,
         staged=(0, 1),
-        sent=(0, 1, 2, 3),
-        plain=(4,),
+        sent=(0, 1),
+        plain=(2,),
         limit=WHOLE_VMEM,
         flops=10**8,
     )
@@ -665,8 +666,9 @@
         slots={0: slot},
         flops=4 * 10**8,
     )
-    back, first, last = lax.optimization_barrier((back, first, last))
+    back, cells = lax.optimization_barrier((back, cells))
     back = send(back)
+    first, last = run(edges_kernel, [edge, edge], cells)
     before, after = neighbours(first, last)
     local, lanes, outer_cells = run(
         local_kernel,

time: 72.9 us -> 72.9 us (level)
    pallas_call x11 -> x12, Pallas kernels: 23.8 us -> 23.8 us  [run(): pl.pallas_call(kernel, out_shape=results, in_specs=[in_hbm if k in staged...]
    unnamed x26 -> x22, local copies, waits for them, and re-layouts: 1.72 us -> 1.7 us
where the time goes in v22:
time: 72.9 us; the launch traced here: 72.3 us
  starting transfers between devices  25 us (34%)
  Pallas kernels  23.8 us (33%)
  waiting for transfers between devices  20.8 us (29%)
  local copies, waits for them, and re-layouts  1.7 us (2%)
  between operations  0.9 us (1%)
    pallas_call x12, Pallas kernels, run(): pl.pallas_call(kernel, out_shape=results, in_specs=[in_hbm if k in staged...  23.8 us
    all_to_all x4, waiting for transfers between devices, exchange(): lax.all_to_all(values, ('space', 'batch'), split_axis=0, concat_axis=0, t...  20 us
    all_to_all x4, starting transfers between devices, exchange(): lax.all_to_all(values, ('space', 'batch'), split_axis=0, concat_axis=0, t...  18.8 us
    ppermute x2, starting transfers between devices, neighbours(): before = lax.ppermute(last, 'space', [(i, i + 1) for i in range(ends)])  3.63 us
    ppermute x2, starting transfers between devices, neighbours(): after = lax.ppermute(first, 'space', [(i + 1, i) for i in range(ends)])  2.58 us
    unnamed x22, local copies, waits for them, and re-layouts  1.7 us
  transfers between devices with their start and end apart: 8, of which 5 were waited for; matrix products, arithmetic and copies ran while one was open for 0% of the time, Pallas kernels for 19%

profile of v22, /device:TPU:0, one launch (start us, length us, event | category | flops | bytes accessed | tf_op | source)
XLA Modules:
  0.0 72.3 jit_solution(4446713526132633524)
XLA Ops:
  0.6 2.4 %analyse_kernel.1 = (bf16[1024,128]{1,0:T(8,128)(2,1)}, bf16[256,128]{1,0:T(8,128)(2,1)}, bf16[32,8,128]{2,1,0:T(8,128)(2,1)}) custom-call(bf16[64,2,1024]{2,1,0:T(2,128)(2,1)} %bitcast.22, bf16[256,1024]{1,0:T(8,128)(2,1)} %constant.14.clone.refs_1_), custom_call_target="tpu_custom_call" | custom-call | flops 100000000 | bytes 1179648 | tf_op jit(solution)/shard_map/analyse_kernel/pallas_call | solution.py:580
  3.0 7.3 %all-to-all-start = ((bf16[32,8,128]{2,1,0:T(8,128)(2,1)}), bf16[32,8,128]{2,1,0:T(8,128)(2,1)S(1)}, u32[]{:S(2)}, u32[]{:S(2)}) async-start(bf16[32,8,128]{2,1,0:T(8,128)(2,1)} %bitcast.23), calls=%async_computation | async-start | bytes 131072 | tf_op jit(solution)/shard_map/all_to_all | solution.py:597
  10.3 2.9 %pack_kernel.1.refs_0_.refs_1_ = bf16[102400,128]{1,0:T(8,128)(2,1)} custom-call(bf16[12288,64]{1,0:T(8,128)(2,1)} %bitcast.18, bf16[12288,64]{1,0:T(8,128)(2,1)} %bitcast.19, bf16[12288,64]{1,0:T(8,128)(2,1)} %bitcast.20), custom_call_target="tpu_custom_call" | custom-call | bytes 30932992 | tf_op jit(solution)/shard_map/pack_kernel/pallas_call | solution.py:580
  13.3 0.0 copy-start.5
  13.3 0.0 copy-start.6
  13.3 0.0 copy-start.2
  13.3 0.0 copy-start.1
  13.3 0.0 copy-start.7
  13.3 1.5 %fetch_kernel.1.refs_2_ = bf16[6144,128]{1,0:T(8,128)(2,1)S(1)} custom-call(bf16[102400,128]{1,0:T(8,128)(2,1)} %pack_kernel.1.refs_0_.refs_1_), custom_call_target="tpu_custom_call" | custom-call | bytes 27787264 | tf_op jit(solution)/shard_map/fetch_kernel/pallas_call | solution.py:580
  14.9 3.1 %all-to-all-done = bf16[32,8,128]{2,1,0:T(8,128)(2,1)S(1)} async-done(((bf16[32,8,128]{2,1,0:T(8,128)(2,1)}), bf16[32,8,128]{2,1,0:T(8,128)(2,1)S(1)}, u32[]{:S(2)}, u32[]{:S(2)}) %all-to-all-start) | async-done | bytes 65568 | tf_op jit(solution)/shard_map/all_to_all | solution.py:597
  17.9 0.0 copy-done.5
  17.9 0.0 copy-done.6
  17.9 1.8 %mix_kernel.1 = (bf16[32,8,128]{2,1,0:T(8,128)(2,1)}, bf16[384,256]{1,0:T(8,128)(2,1)S(1)}) custom-call(bf16[256,128]{1,0:T(8,128)(2,1)S(1)} %bitcast.15, bf16[192,256]{1,0:T(8,128)(2,1)S(1)} %copy-done.6, bf16[6144,128]{1,0:T(8,128)(2,1)S(1)} %fetch_kernel.1.refs_2_, bf16[128,384]{1,0:T(8,128)(2,1)S(1)} %copy-done.5, ...), custom_call_target="tpu_custom_call", output_to_operand_aliasing={{0}: (4, {})} | custom-call | flops 400000000 | bytes 2097152 | tf_op jit(solution)/shard_map/mix_kernel/pallas_call | solution.py:580
  19.7 0.0 copy-done.2
  19.7 0.1 edges_kernel.1
  19.9 1.6 %collective-permute-start = (bf16[512,128]{1,0:T(8,128)(2,1)S(1)}, bf16[512,128]{1,0:T(8,128)(2,1)S(1)}, u32[]{:S(2)}, u32[]{:S(2)}) collective-permute-start(bf16[512,128]{1,0:T(8,128)(2,1)S(1)} %get-tuple-element.42), channel_id=1, source_target_pairs={{0,1},{1,2},{2,3},{3,4},{4,5},{5,6},{6,7},{7,8},{8,9},{9,10},{10,1... | collective-permute-start | bytes 393224 | tf_op jit(solution)/shard_map/ppermute | solution.py:602
  21.5 1.3 %collective-permute-start.1 = (bf16[512,128]{1,0:T(8,128)(2,1)S(1)}, bf16[512,128]{1,0:T(8,128)(2,1)S(1)}, u32[]{:S(2)}, u32[]{:S(2)}) collective-permute-start(bf16[512,128]{1,0:T(8,128)(2,1)S(1)} %get-tuple-element.43), channel_id=1, source_target_pairs={{1,0},{2,1},{3,2},{4,3},{5,4},{6,5},{7,6},{8,7},{9,8},{10,9},{11,1... | collective-permute-start | bytes 393224 | tf_op jit(solution)/shard_map/ppermute | solution.py:603
  22.8 5.5 %all-to-all-start.1 = ((bf16[32,8,128]{2,1,0:T(8,128)(2,1)}), bf16[32,8,128]{2,1,0:T(8,128)(2,1)S(1)}, u32[]{:S(2)}, u32[]{:S(2)}) async-start(bf16[32,8,128]{2,1,0:T(8,128)(2,1)} %get-tuple-element.40), calls=%async_computation.1 | async-start | bytes 131072 | tf_op jit(solution)/shard_map/all_to_all | solution.py:597
  28.3 0.0 collective-permute-done.refs_1_
  28.3 0.0 collective-permute-done.1.refs_2_
  28.3 0.0 copy-done.1
  28.3 0.0 copy-done.7
  28.3 0.0 copy-start.8
  28.3 1.2 %local_kernel.1 = (f32[1024,128]{1,0:T(8,128)S(1)}, bf16[256,1024]{1,0:T(8,128)(2,1)S(1)}, bf16[1024,128]{1,0:T(8,128)(2,1)S(1)}) custom-call(bf16[1024,128]{1,0:T(8,128)(2,1)S(1)} %copy-done.2, bf16[512,128]{1,0:T(8,128)(2,1)S(1)} %collective-permute-done.refs_1_, bf16[512,128]{1,0:T(8,128)(2,1)S(1)} %collective-permute-done.1.refs_2_, ...), custom_call_target="tpu_custom_call" | custom-call | flops 8000000000 | bytes 2318336 | tf_op jit(solution)/shard_map/local_kernel/pallas_call | solution.py:580
  29.5 0.0 copy-start.9
  29.5 0.7 copy-done.9
  30.2 5.7 %all-to-all-done.1 = bf16[32,8,128]{2,1,0:T(8,128)(2,1)S(1)} async-done(((bf16[32,8,128]{2,1,0:T(8,128)(2,1)}), bf16[32,8,128]{2,1,0:T(8,128)(2,1)S(1)}, u32[]{:S(2)}, u32[]{:S(2)}) %all-to-all-start.1) | async-done | bytes 65568 | tf_op jit(solution)/shard_map/all_to_all | solution.py:597
  35.9 0.0 copy-done.8
  35.9 0.0 copy-start.10
  35.9 0.9 %copy-done.10 = bf16[1024,128]{1,0:T(8,128)(2,1)S(1)} copy-done((bf16[1024,128]{1,0:T(8,128)(2,1)S(1)}, bf16[1024,128]{1,0:T(8,128)(2,1)}, u32[]{:S(2)}) %copy-start.10) | copy-done | bytes 262168
  36.8 2.6 %activate_kernel.1 = (bf16[1024,128]{1,0:T(8,128)(2,1)S(1)}, bf16[102400,128]{1,0:T(8,128)(2,1)}, bf16[512,128]{1,0:T(8,128)(2,1)S(1)}, bf16[512,128]{1,0:T(8,128)(2,1)S(1)}, bf16[32,40,128]{2,1,0:T(8,128)(2,1)}) custom-call(bf16[256,128]{1,0:T(8,128)(2,1)S(1)} %bitcast.16, bf16[1024,256]{1,0:T(8,128)(2,1)S(1)} %copy-done.8, ...), custom_call_target="tpu_custom_call" | custom-call | flops 1000000000 | bytes 28966912 | tf_op jit(solution)/shard_map/activate_kernel/pallas_call | solution.py:580
  39.5 2.6 %all-to-all-start.2 = ((bf16[32,40,128]{2,1,0:T(8,128)(2,1)}), bf16[32,40,128]{2,1,0:T(8,128)(2,1)S(1)}, u32[]{:S(2)}, u32[]{:S(2)}) async-start(bf16[32,40,128]{2,1,0:T(8,128)(2,1)} %get-tuple-element.47), calls=%async_computation.2 | async-start | bytes 655360 | tf_op jit(solution)/shard_map/all_to_all | solution.py:597
  42.1 2.0 %collective-permute-start.2 = (bf16[512,128]{1,0:T(8,128)(2,1)S(1)}, bf16[512,128]{1,0:T(8,128)(2,1)S(1)}, u32[]{:S(2)}, u32[]{:S(2)}) collective-permute-start(bf16[512,128]{1,0:T(8,128)(2,1)S(1)} %get-tuple-element.48), channel_id=1, source_target_pairs={{0,1},{1,2},{2,3},{3,4},{4,5},{5,6},{6,7},{7,8},{8,9},{9,10},{10,1... | collective-permute-start | bytes 393224 | tf_op jit(solution)/shard_map/ppermute | solution.py:602
  44.1 1.3 %collective-permute-start.3 = (bf16[512,128]{1,0:T(8,128)(2,1)S(1)}, bf16[512,128]{1,0:T(8,128)(2,1)S(1)}, u32[]{:S(2)}, u32[]{:S(2)}) collective-permute-start(bf16[512,128]{1,0:T(8,128)(2,1)S(1)} %get-tuple-element.49), channel_id=1, source_target_pairs={{1,0},{2,1},{3,2},{4,3},{5,4},{6,5},{7,6},{8,7},{9,8},{10,9},{11,1... | collective-permute-start | bytes 393224 | tf_op jit(solution)/shard_map/ppermute | solution.py:603
  45.4 0.0 copy-start.3
  45.4 0.0 copy-start.4
  45.4 2.2 %output_kernel.1 = (bf16[64,2,1024]{2,1,0:T(2,128)(2,1)}, bf16[6144,128]{1,0:T(8,128)(2,1)S(1)}) custom-call(bf16[1024,128]{1,0:T(8,128)(2,1)S(1)} %get-tuple-element.50.refs_0_, bf16[102400,128]{1,0:T(8,128)(2,1)} %pack_kernel.1.refs_0_.refs_1_), custom_call_target="tpu_custom_call" | custom-call | flops 100000000 | bytes 28311552 | tf_op jit(solution)/shard_map/output_kernel/pallas_call | solution.py:580
  47.6 0.0 collective-permute-done.2.refs_1_
  47.6 0.9 %collective-permute-done.3.refs_2_ = bf16[512,128]{1,0:T(8,128)(2,1)S(1)} collective-permute-done((bf16[512,128]{1,0:T(8,128)(2,1)S(1)}, bf16[512,128]{1,0:T(8,128)(2,1)S(1)}, u32[]{:S(2)}, u32[]{:S(2)}) %collective-permute-start.3) | collective-permute-done | bytes 131104 | tf_op jit(solution)/shard_map/ppermute | solution.py:603
  48.5 5.3 %all-to-all-done.2.refs_0_ = bf16[32,40,128]{2,1,0:T(8,128)(2,1)S(1)} async-done(((bf16[32,40,128]{2,1,0:T(8,128)(2,1)}), bf16[32,40,128]{2,1,0:T(8,128)(2,1)S(1)}, u32[]{:S(2)}, u32[]{:S(2)}) %all-to-all-start.2) | async-done | bytes 327712 | tf_op jit(solution)/shard_map/all_to_all | solution.py:597
  53.8 0.0 copy-done.3
  53.8 0.0 copy-done.4
  53.8 1.8 %unmix_kernel.1 = (bf16[32,40,128]{2,1,0:T(8,128)(2,1)}, bf16[384,128]{1,0:T(8,128)(2,1)S(1)}) custom-call(bf16[32,40,128]{2,1,0:T(8,128)(2,1)S(1)} %all-to-all-done.2.refs_0_, bf16[192,256]{1,0:T(8,128)(2,1)S(1)} %copy-done.4, bf16[6144,128]{1,0:T(8,128)(2,1)S(1)} %get-tuple-element.55.refs_2_, bf16[128,384]{1,0:T(8,128)(2,1)S(1)} %copy-done.3), custom_call_target="tpu_custom_call" | custom-call | flops 400000000 | bytes 2523136 | tf_op jit(solution)/shard_map/unmix_kernel/pallas_call | solution.py:580
  55.6 3.5 %all-to-all-start.3 = ((bf16[32,40,128]{2,1,0:T(8,128)(2,1)}), bf16[32,40,128]{2,1,0:T(8,128)(2,1)S(1)}, u32[]{:S(2)}, u32[]{:S(2)}) async-start(bf16[32,40,128]{2,1,0:T(8,128)(2,1)} %get-tuple-element.56), calls=%async_computation.3 | async-start | bytes 655360 | tf_op jit(solution)/shard_map/all_to_all | solution.py:597
  59.1 3.7 %weight_kernel.1 = f32[12288,64]{1,0:T(8,128)} custom-call(bf16[384,256]{1,0:T(8,128)(2,1)S(1)} %get-tuple-element.61.refs_0_, bf16[384,128]{1,0:T(8,128)(2,1)S(1)} %get-tuple-element.62.refs_1_), custom_call_target="tpu_custom_call" | custom-call | flops 400000000 | bytes 3440640 | tf_op jit(solution)/shard_map/weight_kernel/pallas_call | solution.py:580
  62.8 0.0 copy-start
  62.8 2.1 %local_grad_kernel.1.refs_2_ = f32[1024,128]{1,0:T(8,128)S(1)} custom-call(bf16[102400,128]{1,0:T(8,128)(2,1)} %get-tuple-element.57.refs_0_, bf16[512,128]{1,0:T(8,128)(2,1)S(1)} %collective-permute-done.2.refs_1_, bf16[512,128]{1,0:T(8,128)(2,1)S(1)} %collective-permute-done.3.refs_2_, bf16[27,64,64]{2,1,0:T(8,128)(2,1)S(1)} %bitcast.14), custom_call_target="tpu_custom_call" | custom-call | flops 700000000 | bytes 27222016 | tf_op jit(solution)/shard_map/local_grad_kernel/pallas_call | solution.py:580
  64.9 5.9 %all-to-all-done.3.refs_0_ = bf16[32,40,128]{2,1,0:T(8,128)(2,1)S(1)} async-done(((bf16[32,40,128]{2,1,0:T(8,128)(2,1)}), bf16[32,40,128]{2,1,0:T(8,128)(2,1)S(1)}, u32[]{:S(2)}, u32[]{:S(2)}) %all-to-all-start.3) | async-done | bytes 327712 | tf_op jit(solution)/shard_map/all_to_all | solution.py:597
  70.8 0.0 copy-done
  70.8 1.5 %finish_kernel.1 = (bf16[64,2,1024]{2,1,0:T(2,128)(2,1)}, f32[27,64,64]{2,1,0:T(8,128)}) custom-call(bf16[32,40,128]{2,1,0:T(8,128)(2,1)S(1)} %all-to-all-done.3.refs_0_, bf16[1024,256]{1,0:T(8,128)(2,1)S(1)} %copy-done, f32[1024,128]{1,0:T(8,128)S(1)} %local_grad_kernel.1.refs_2_), custom_call_target="tpu_custom_call" | custom-call | flops 100000000 | bytes 2080768 | tf_op jit(solution)/shard_map/finish_kernel/pallas_call | solution.py:580
Async XLA Ops:
  3.0 14.9 %all-to-all-start = ((bf16[32,8,128]{2,1,0:T(8,128)(2,1)}), bf16[32,8,128]{2,1,0:T(8,128)(2,1)S(1)}, u32[]{:S(2)}, u32[]{:S(2)}) async-start(bf16[32,8,128]{2,1,0:T(8,128)(2,1)} %bitcast.23), calls=%async_computation | async-start | bytes 131072 | tf_op jit(solution)/shard_map/all_to_all | solution.py:597
  13.3 4.7 %copy-start.5 = (bf16[128,384]{1,0:T(8,128)(2,1)S(1)}, bf16[128,384]{1,0:T(8,128)(2,1)}, u32[]{:S(2)}) copy-start(bf16[128,384]{1,0:T(8,128)(2,1)} %constant.16.clone.refs_3_) | copy-start | bytes 294916
  13.3 4.7 %copy-start.6 = (bf16[192,256]{1,0:T(8,128)(2,1)S(1)}, bf16[192,256]{1,0:T(8,128)(2,1)}, u32[]{:S(2)}) copy-start(bf16[192,256]{1,0:T(8,128)(2,1)} %constant.15.clone.refs_1_) | copy-start | bytes 294916
  13.3 6.4 %copy-start.2 = (bf16[1024,128]{1,0:T(8,128)(2,1)S(1)}, bf16[1024,128]{1,0:T(8,128)(2,1)}, u32[]{:S(2)}) copy-start(bf16[1024,128]{1,0:T(8,128)(2,1)} %get-tuple-element.41.refs_0_) | copy-start | bytes 786436
  13.3 15.0 %copy-start.1 = (bf16[3,3,3,64,64]{4,3,2,1,0:T(8,128)(2,1)S(1)}, bf16[3,3,3,64,64]{4,3,2,1,0:T(8,128)(2,1)}, u32[]{:S(2)}) copy-start(bf16[3,3,3,64,64]{4,3,2,1,0:T(8,128)(2,1)} %param.14) | copy-start | bytes 663556
  13.3 15.0 %copy-start.7 = (bf16[1,64,2,1024]{3,2,1,0:T(2,128)(2,1)S(1)}, bf16[1,64,2,1024]{3,2,1,0:T(2,128)(2,1)}, u32[]{:S(2)}) copy-start(bf16[1,64,2,1024]{3,2,1,0:T(2,128)(2,1)} %param.12) | copy-start | bytes 786436
  19.9 8.4 %collective-permute-start = (bf16[512,128]{1,0:T(8,128)(2,1)S(1)}, bf16[512,128]{1,0:T(8,128)(2,1)S(1)}, u32[]{:S(2)}, u32[]{:S(2)}) collective-permute-start(bf16[512,128]{1,0:T(8,128)(2,1)S(1)} %get-tuple-element.42), channel_id=1, source_target_pairs={{0,1},{1,2},{2,3},{3,4},{4,5},{5,6},{6,7},{7,8},{8,9},{9,10},{10,1... | collective-permute-start | bytes 393224 | tf_op jit(solution)/shard_map/ppermute | solution.py:602
  21.5 6.8 %collective-permute-start.1 = (bf16[512,128]{1,0:T(8,128)(2,1)S(1)}, bf16[512,128]{1,0:T(8,128)(2,1)S(1)}, u32[]{:S(2)}, u32[]{:S(2)}) collective-permute-start(bf16[512,128]{1,0:T(8,128)(2,1)S(1)} %get-tuple-element.43), channel_id=1, source_target_pairs={{1,0},{2,1},{3,2},{4,3},{5,4},{6,5},{7,6},{8,7},{9,8},{10,9},{11,1... | collective-permute-start | bytes 393224 | tf_op jit(solution)/shard_map/ppermute | solution.py:603
  22.8 13.1 %all-to-all-start.1 = ((bf16[32,8,128]{2,1,0:T(8,128)(2,1)}), bf16[32,8,128]{2,1,0:T(8,128)(2,1)S(1)}, u32[]{:S(2)}, u32[]{:S(2)}) async-start(bf16[32,8,128]{2,1,0:T(8,128)(2,1)} %get-tuple-element.40), calls=%async_computation.1 | async-start | bytes 131072 | tf_op jit(solution)/shard_map/all_to_all | solution.py:597
  28.3 7.6 %copy-start.8 = (bf16[1024,256]{1,0:T(8,128)(2,1)S(1)}, bf16[1024,256]{1,0:T(8,128)(2,1)}, u32[]{:S(2)}) copy-start(bf16[1024,256]{1,0:T(8,128)(2,1)} %constant.17.clone.refs_1_) | copy-start | bytes 1572868
  29.5 0.7 copy-start.9
  35.9 1.0 %copy-start.10 = (bf16[1024,128]{1,0:T(8,128)(2,1)S(1)}, bf16[1024,128]{1,0:T(8,128)(2,1)}, u32[]{:S(2)}) copy-start(bf16[1024,128]{1,0:T(8,128)(2,1)} %copy-done.9) | copy-start | bytes 786436
  39.5 14.3 %all-to-all-start.2 = ((bf16[32,40,128]{2,1,0:T(8,128)(2,1)}), bf16[32,40,128]{2,1,0:T(8,128)(2,1)S(1)}, u32[]{:S(2)}, u32[]{:S(2)}) async-start(bf16[32,40,128]{2,1,0:T(8,128)(2,1)} %get-tuple-element.47), calls=%async_computation.2 | async-start | bytes 655360 | tf_op jit(solution)/shard_map/all_to_all | solution.py:597
  42.1 5.6 %collective-permute-start.2 = (bf16[512,128]{1,0:T(8,128)(2,1)S(1)}, bf16[512,128]{1,0:T(8,128)(2,1)S(1)}, u32[]{:S(2)}, u32[]{:S(2)}) collective-permute-start(bf16[512,128]{1,0:T(8,128)(2,1)S(1)} %get-tuple-element.48), channel_id=1, source_target_pairs={{0,1},{1,2},{2,3},{3,4},{4,5},{5,6},{6,7},{7,8},{8,9},{9,10},{10,1... | collective-permute-start | bytes 393224 | tf_op jit(solution)/shard_map/ppermute | solution.py:602
  44.1 4.4 %collective-permute-start.3 = (bf16[512,128]{1,0:T(8,128)(2,1)S(1)}, bf16[512,128]{1,0:T(8,128)(2,1)S(1)}, u32[]{:S(2)}, u32[]{:S(2)}) collective-permute-start(bf16[512,128]{1,0:T(8,128)(2,1)S(1)} %get-tuple-element.49), channel_id=1, source_target_pairs={{1,0},{2,1},{3,2},{4,3},{5,4},{6,5},{7,6},{8,7},{9,8},{10,9},{11,1... | collective-permute-start | bytes 393224 | tf_op jit(solution)/shard_map/ppermute | solution.py:603
  45.4 8.4 %copy-start.3 = (bf16[128,384]{1,0:T(8,128)(2,1)S(1)}, bf16[128,384]{1,0:T(8,128)(2,1)}, u32[]{:S(2)}) copy-start(bf16[128,384]{1,0:T(8,128)(2,1)} %constant.19.clone.refs_3_) | copy-start | bytes 294916
  45.4 8.4 %copy-start.4 = (bf16[192,256]{1,0:T(8,128)(2,1)S(1)}, bf16[192,256]{1,0:T(8,128)(2,1)}, u32[]{:S(2)}) copy-start(bf16[192,256]{1,0:T(8,128)(2,1)} %constant.18.clone.refs_1_) | copy-start | bytes 294916
  55.6 15.2 %all-to-all-start.3 = ((bf16[32,40,128]{2,1,0:T(8,128)(2,1)}), bf16[32,40,128]{2,1,0:T(8,128)(2,1)S(1)}, u32[]{:S(2)}, u32[]{:S(2)}) async-start(bf16[32,40,128]{2,1,0:T(8,128)(2,1)} %get-tuple-element.56), calls=%async_computation.3 | async-start | bytes 655360 | tf_op jit(solution)/shard_map/all_to_all | solution.py:597
  62.8 8.0 %copy-start = (bf16[1024,256]{1,0:T(8,128)(2,1)S(1)}, bf16[1024,256]{1,0:T(8,128)(2,1)}, u32[]{:S(2)}) copy-start(bf16[1024,256]{1,0:T(8,128)(2,1)} %constant.20.clone.refs_1_) | copy-start | bytes 1572868

commit v23 on v16

--- a/solution.py
+++ b/solution.py
@@ -372,15 +372,19 @@
     last_out[...] = last
 
 
+def slab_owners(slab):
+    return (slab.shape[0] - TERM_ROWS) // 8
+
+
 def slab_store(slab, modes, terms):
-    owners = slab.shape[0]
+    owners = slab_owners(slab)
     modes = modes.reshape(owners, 8, LANES)
     terms = terms.reshape(owners, -1, LANES)
-    slab[...] = jnp.concatenate([modes, terms], axis=1).astype(BF16)
+    slab[...] = jnp.concatenate([modes, terms], axis=1).reshape(-1, LANES).astype(BF16)
 
 
 def slab_load(slab):
-    whole = slab[...].astype(F32)
+    whole = slab[...].astype(F32).reshape(slab_owners(slab), -1, LANES)
     return whole[:, 0:8, :].reshape(-1, LANES), whole[:, 8:, :]
 
 
@@ -409,7 +413,7 @@
     coef = coef + swap_halves(coef)
     grad = from_depth(coef, scatter[...], snaps, slabs)
     if in_slab:
-        owners = received.shape[0]
+        owners = slab_owners(received)
         share = sums.shape[0]
         slab_store(
             grad_out, grad, jnp.broadcast_to(sums[None], (owners, share, LANES)).reshape(-1, LANES)
@@ -626,7 +630,6 @@
 
     packed = shape((weights.shape[0] // 2, LANES), BF16)
     share = weights.shape[0] // CHUNKS
-    to_send = shape((devices, modes, LANES), BF16) if modes % 8 == 0 else plane_modes
     cells, coef, first, last, kept_weights, slot = run(
         analyse_kernel,
         [
@@ -635,7 +638,7 @@
             edge,
             edge,
             shape((HBM_BYTES // (2 * LANES), LANES), BF16),
-            to_send,
+            plane_modes,
         ],
         snapshots.reshape(field.shape),
         analysis,
@@ -663,7 +666,7 @@
     )
     back, diagonal = run(
         functools.partial(mix_kernel, batches, slabs),
-        [to_send, shape((count, GROUP * half // 2), BF16)],
+        [plane_modes, shape((count, GROUP * half // 2), BF16)],
         coef,
         gather,
         packed_weights,
@@ -673,7 +676,7 @@
         flops=4 * 10**8,
     )
     back = send(back)
-    slab = shape((devices, 8 + TERM_ROWS // devices, LANES), BF16)
+    slab = shape((devices * 8 + TERM_ROWS, LANES), BF16)
     activated, grad, first, last, back, terms = run(
         functools.partial(activate_kernel, in_slab),
         [
@@ -694,7 +697,7 @@
         flops=10**9,
     )
     if in_slab:
-        back = exchange(back)
+        back = exchange(back.reshape(devices, -1, LANES)).reshape(-1, LANES)
     else:
         back = send(back)
         terms = exchange(terms.reshape(devices, TERM_ROWS // devices, LANES))
@@ -727,7 +730,7 @@
         flops=4 * 10**8,
     )
     if in_slab:
-        grad_modes = exchange(grad_modes)
+        grad_modes = exchange(grad_modes.reshape(devices, -1, LANES)).reshape(-1, LANES)
     else:
         grad_modes = send(grad_modes)
         sums = lax.all_gather(sums, ("space", "batch"), axis=0, tiled=True)

time: 69.6 us -> 69.6 us (level)
  no operation moved by 1% of the time
where the time goes in v23:
time: 69.6 us; the launch traced here: 69.1 us
  starting transfers between devices  25.6 us (37%)
  Pallas kernels  21.6 us (31%)
  waiting for transfers between devices  21 us (30%)
  between operations  0.87 us (1%)
    pallas_call x10, Pallas kernels, run(): pl.pallas_call(kernel, out_shape=results, in_specs=[in_hbm if k in staged...  21.6 us
    all_to_all x4, waiting for transfers between devices, exchange(): lax.all_to_all(values, ('space', 'batch'), split_axis=0, concat_axis=0, t...  20.1 us
    all_to_all x4, starting transfers between devices, exchange(): lax.all_to_all(values, ('space', 'batch'), split_axis=0, concat_axis=0, t...  18.8 us
    ppermute x2, starting transfers between devices, neighbours(): before = lax.ppermute(last, 'space', [(i, i + 1) for i in range(ends)])  4.19 us
    ppermute x2, starting transfers between devices, neighbours(): after = lax.ppermute(first, 'space', [(i + 1, i) for i in range(ends)])  2.58 us
  transfers between devices with their start and end apart: 8, of which 5 were waited for; matrix products, arithmetic and copies ran while one was open for 0% of the time, Pallas kernels for 18%

profile of v23, /device:TPU:0, one launch (start us, length us, event | category | flops | bytes accessed | tf_op | source)
XLA Modules:
  0.0 69.1 jit_solution(8458114023648349336)
XLA Ops:
  0.6 3.2 %analyse_kernel.1 = (bf16[1024,128]{1,0:T(8,128)(2,1)}, bf16[256,128]{1,0:T(8,128)(2,1)}, bf16[512,128]{1,0:T(8,128)(2,1)}, bf16[512,128]{1,0:T(8,128)(2,1)}, bf...) custom-call(bf16[64,2,1024]{2,1,0:T(2,128)(2,1)} %bitcast.29, bf16[256,1024]{1,0:T(8,128)(2,1)} %constant.14.clone.refs_1_, ...), custom_call_target="tpu_custom_call" | custom-call | flops 100000000 | bytes 32374784 | tf_op jit(solution)/shard_map/analyse_kernel/pallas_call | solution.py:579
  3.9 7.3 %all-to-all-start = ((bf16[32,8,128]{2,1,0:T(8,128)(2,1)}), bf16[32,8,128]{2,1,0:T(8,128)(2,1)S(1)}, u32[]{:S(2)}, u32[]{:S(2)}) async-start(bf16[32,8,128]{2,1,0:T(8,128)(2,1)} %bitcast.30), calls=%async_computation | async-start | bytes 131072 | tf_op jit(solution)/shard_map/all_to_all | solution.py:596
  11.2 2.2 %collective-permute-start = (bf16[512,128]{1,0:T(8,128)(2,1)}, bf16[512,128]{1,0:T(8,128)(2,1)S(1)}, u32[]{:S(2)}, u32[]{:S(2)}) collective-permute-start(bf16[512,128]{1,0:T(8,128)(2,1)} %get-tuple-element.36), channel_id=1, source_target_pairs={{0,1},{1,2},{2,3},{3,4},{4,5},{5,6},{6,7},{7,8},{8,9},{9,10},{10,1... | collective-permute-start | bytes 393224 | tf_op jit(solution)/shard_map/ppermute | solution.py:601
  13.3 1.3 %collective-permute-start.1 = (bf16[512,128]{1,0:T(8,128)(2,1)}, bf16[512,128]{1,0:T(8,128)(2,1)S(1)}, u32[]{:S(2)}, u32[]{:S(2)}) collective-permute-start(bf16[512,128]{1,0:T(8,128)(2,1)} %get-tuple-element.37), channel_id=1, source_target_pairs={{1,0},{2,1},{3,2},{4,3},{5,4},{6,5},{7,6},{8,7},{9,8},{10,9},{11,1... | collective-permute-start | bytes 393224 | tf_op jit(solution)/shard_map/ppermute | solution.py:602
  14.6 0.0 copy-start.4
  14.7 0.0 copy-start.5
  14.7 0.0 copy-start.1
  14.7 0.0 copy-start.6
  14.7 0.0 copy-start.7
  14.7 1.5 %fetch_kernel.1.refs_2_ = bf16[6144,128]{1,0:T(8,128)(2,1)S(1)} custom-call(bf16[102400,128]{1,0:T(8,128)(2,1)} %get-tuple-element.32.refs_0_.refs_1_), custom_call_target="tpu_custom_call" | custom-call | bytes 27787264 | tf_op jit(solution)/shard_map/fetch_kernel/pallas_call | solution.py:579
  16.2 2.6 %all-to-all-done = bf16[32,8,128]{2,1,0:T(8,128)(2,1)S(1)} async-done(((bf16[32,8,128]{2,1,0:T(8,128)(2,1)}), bf16[32,8,128]{2,1,0:T(8,128)(2,1)S(1)}, u32[]{:S(2)}, u32[]{:S(2)}) %all-to-all-start) | async-done | bytes 65568 | tf_op jit(solution)/shard_map/all_to_all | solution.py:596
  18.8 0.0 copy-done.4
  18.8 0.0 copy-done.5
  18.8 1.8 %mix_kernel.1 = (bf16[256,128]{1,0:T(8,128)(2,1)}, bf16[384,256]{1,0:T(8,128)(2,1)S(1)}) custom-call(bf16[256,128]{1,0:T(8,128)(2,1)S(1)} %bitcast.22, bf16[192,256]{1,0:T(8,128)(2,1)S(1)} %copy-done.5, bf16[6144,128]{1,0:T(8,128)(2,1)S(1)} %fetch_kernel.1.refs_2_, bf16[128,384]{1,0:T(8,128)(2,1)S(1)} %copy-done.4, ...), custom_call_target="tpu_custom_call", output_to_operand_aliasing={{0}: (4, {})} | custom-call | flops 400000000 | bytes 2097152 | tf_op jit(solution)/shard_map/mix_kernel/pallas_call | solution.py:579
  20.6 5.4 %all-to-all-start.1 = ((bf16[32,8,128]{2,1,0:T(8,128)(2,1)}), bf16[32,8,128]{2,1,0:T(8,128)(2,1)S(1)}, u32[]{:S(2)}, u32[]{:S(2)}) async-start(bf16[32,8,128]{2,1,0:T(8,128)(2,1)} %bitcast.4), calls=%async_computation.1 | async-start | bytes 131072 | tf_op jit(solution)/shard_map/all_to_all | solution.py:596
  26.0 0.0 collective-permute-done.refs_1_
  26.0 0.0 collective-permute-done.1.refs_2_
  26.0 0.0 copy-done.1
  26.0 0.0 copy-done.6
  26.0 0.0 copy-done.7
  26.0 0.0 copy-start.8
  26.0 1.2 %local_kernel.1 = (f32[1024,128]{1,0:T(8,128)S(1)}, bf16[256,1024]{1,0:T(8,128)(2,1)S(1)}, bf16[1024,128]{1,0:T(8,128)(2,1)S(1)}) custom-call(bf16[1024,128]{1,0:T(8,128)(2,1)S(1)} %copy-done.7, bf16[512,128]{1,0:T(8,128)(2,1)S(1)} %collective-permute-done.refs_1_, bf16[512,128]{1,0:T(8,128)(2,1)S(1)} %collective-permute-done.1.refs_2_, ...), custom_call_target="tpu_custom_call" | custom-call | flops 8000000000 | bytes 2318336 | tf_op jit(solution)/shard_map/local_kernel/pallas_call | solution.py:579
  27.2 6.4 %all-to-all-done.1 = bf16[32,8,128]{2,1,0:T(8,128)(2,1)S(1)} async-done(((bf16[32,8,128]{2,1,0:T(8,128)(2,1)}), bf16[32,8,128]{2,1,0:T(8,128)(2,1)S(1)}, u32[]{:S(2)}, u32[]{:S(2)}) %all-to-all-start.1) | async-done | bytes 65568 | tf_op jit(solution)/shard_map/all_to_all | solution.py:596
  33.6 0.0 copy-done.8
  33.6 2.6 %activate_kernel.1 = (bf16[1024,128]{1,0:T(8,128)(2,1)S(1)}, bf16[102400,128]{1,0:T(8,128)(2,1)}, bf16[512,128]{1,0:T(8,128)(2,1)S(1)}, bf16[512,128]{1,0:T(8,128)(2,1)S(1)}, bf16[1280,128]{1,0:T(8,128)(2,1)}) custom-call(bf16[256,128]{1,0:T(8,128)(2,1)S(1)} %bitcast.23, bf16[1024,256]{1,0:T(8,128)(2,1)S(1)} %copy-done.8, ...), custom_call_target="tpu_custom_call" | custom-call | flops 1000000000 | bytes 28966912 | tf_op jit(solution)/shard_map/activate_kernel/pallas_call | solution.py:579
  36.2 2.6 %all-to-all-start.2 = ((bf16[32,40,128]{2,1,0:T(8,128)(2,1)}), bf16[32,40,128]{2,1,0:T(8,128)(2,1)S(1)}, u32[]{:S(2)}, u32[]{:S(2)}) async-start(bf16[32,40,128]{2,1,0:T(8,128)(2,1)} %bitcast.8), calls=%async_computation.2 | async-start | bytes 655360 | tf_op jit(solution)/shard_map/all_to_all | solution.py:596
  38.9 2.0 %collective-permute-start.2 = (bf16[512,128]{1,0:T(8,128)(2,1)S(1)}, bf16[512,128]{1,0:T(8,128)(2,1)S(1)}, u32[]{:S(2)}, u32[]{:S(2)}) collective-permute-start(bf16[512,128]{1,0:T(8,128)(2,1)S(1)} %get-tuple-element.42), channel_id=1, source_target_pairs={{0,1},{1,2},{2,3},{3,4},{4,5},{5,6},{6,7},{7,8},{8,9},{9,10},{10,1... | collective-permute-start | bytes 393224 | tf_op jit(solution)/shard_map/ppermute | solution.py:601
  40.9 1.3 %collective-permute-start.3 = (bf16[512,128]{1,0:T(8,128)(2,1)S(1)}, bf16[512,128]{1,0:T(8,128)(2,1)S(1)}, u32[]{:S(2)}, u32[]{:S(2)}) collective-permute-start(bf16[512,128]{1,0:T(8,128)(2,1)S(1)} %get-tuple-element.43), channel_id=1, source_target_pairs={{1,0},{2,1},{3,2},{4,3},{5,4},{6,5},{7,6},{8,7},{9,8},{10,9},{11,1... | collective-permute-start | bytes 393224 | tf_op jit(solution)/shard_map/ppermute | solution.py:602
  42.2 0.0 copy-start.2
  42.2 0.0 copy-start.3
  42.2 2.2 %output_kernel.1 = (bf16[64,2,1024]{2,1,0:T(2,128)(2,1)}, bf16[6144,128]{1,0:T(8,128)(2,1)S(1)}) custom-call(bf16[1024,128]{1,0:T(8,128)(2,1)S(1)} %get-tuple-element.44.refs_0_, bf16[102400,128]{1,0:T(8,128)(2,1)} %get-tuple-element.32.refs_0_.refs_1_), custom_call_target="tpu_custom_call" | custom-call | flops 100000000 | bytes 28311552 | tf_op jit(solution)/shard_map/output_kernel/pallas_call | solution.py:579
  44.4 0.0 collective-permute-done.2.refs_1_
  44.4 0.9 %collective-permute-done.3.refs_2_ = bf16[512,128]{1,0:T(8,128)(2,1)S(1)} collective-permute-done((bf16[512,128]{1,0:T(8,128)(2,1)S(1)}, bf16[512,128]{1,0:T(8,128)(2,1)S(1)}, u32[]{:S(2)}, u32[]{:S(2)}) %collective-permute-start.3) | collective-permute-done | bytes 131104 | tf_op jit(solution)/shard_map/ppermute | solution.py:602
  45.3 5.3 %all-to-all-done.2 = bf16[32,40,128]{2,1,0:T(8,128)(2,1)S(1)} async-done(((bf16[32,40,128]{2,1,0:T(8,128)(2,1)}), bf16[32,40,128]{2,1,0:T(8,128)(2,1)S(1)}, u32[]{:S(2)}, u32[]{:S(2)}) %all-to-all-start.2) | async-done | bytes 327712 | tf_op jit(solution)/shard_map/all_to_all | solution.py:596
  50.6 0.0 copy-done.2
  50.6 0.0 copy-done.3
  50.6 1.8 %unmix_kernel.1 = (bf16[1280,128]{1,0:T(8,128)(2,1)}, bf16[384,128]{1,0:T(8,128)(2,1)S(1)}) custom-call(bf16[1280,128]{1,0:T(8,128)(2,1)S(1)} %bitcast.19, bf16[192,256]{1,0:T(8,128)(2,1)S(1)} %copy-done.3, bf16[6144,128]{1,0:T(8,128)(2,1)S(1)} %get-tuple-element.49.refs_2_, bf16[128,384]{1,0:T(8,128)(2,1)S(1)} %copy-done.2), custom_call_target="tpu_custom_call" | custom-call | flops 400000000 | bytes 2523136 | tf_op jit(solution)/shard_map/unmix_kernel/pallas_call | solution.py:579
  52.4 3.5 %all-to-all-start.3 = ((bf16[32,40,128]{2,1,0:T(8,128)(2,1)}), bf16[32,40,128]{2,1,0:T(8,128)(2,1)S(1)}, u32[]{:S(2)}, u32[]{:S(2)}) async-start(bf16[32,40,128]{2,1,0:T(8,128)(2,1)} %bitcast.11), calls=%async_computation.3 | async-start | bytes 655360 | tf_op jit(solution)/shard_map/all_to_all | solution.py:596
  55.9 3.7 %weight_kernel.1 = f32[12288,64]{1,0:T(8,128)} custom-call(bf16[384,256]{1,0:T(8,128)(2,1)S(1)} %get-tuple-element.55.refs_0_, bf16[384,128]{1,0:T(8,128)(2,1)S(1)} %get-tuple-element.56.refs_1_), custom_call_target="tpu_custom_call" | custom-call | flops 400000000 | bytes 3440640 | tf_op jit(solution)/shard_map/weight_kernel/pallas_call | solution.py:579
  59.6 0.0 copy-start
  59.6 2.1 %local_grad_kernel.1.refs_2_ = f32[1024,128]{1,0:T(8,128)S(1)} custom-call(bf16[102400,128]{1,0:T(8,128)(2,1)} %get-tuple-element.51.refs_0_, bf16[512,128]{1,0:T(8,128)(2,1)S(1)} %collective-permute-done.2.refs_1_, bf16[512,128]{1,0:T(8,128)(2,1)S(1)} %collective-permute-done.3.refs_2_, bf16[27,64,64]{2,1,0:T(8,128)(2,1)S(1)} %bitcast.21), custom_call_target="tpu_custom_call" | custom-call | flops 700000000 | bytes 27222016 | tf_op jit(solution)/shard_map/local_grad_kernel/pallas_call | solution.py:579
  61.7 5.9 %all-to-all-done.3 = bf16[32,40,128]{2,1,0:T(8,128)(2,1)S(1)} async-done(((bf16[32,40,128]{2,1,0:T(8,128)(2,1)}), bf16[32,40,128]{2,1,0:T(8,128)(2,1)S(1)}, u32[]{:S(2)}, u32[]{:S(2)}) %all-to-all-start.3) | async-done | bytes 327712 | tf_op jit(solution)/shard_map/all_to_all | solution.py:596
  67.6 0.0 copy-done
  67.6 1.5 %finish_kernel.1 = (bf16[64,2,1024]{2,1,0:T(2,128)(2,1)}, f32[27,64,64]{2,1,0:T(8,128)}) custom-call(bf16[1280,128]{1,0:T(8,128)(2,1)S(1)} %bitcast.18, bf16[1024,256]{1,0:T(8,128)(2,1)S(1)} %copy-done, f32[1024,128]{1,0:T(8,128)S(1)} %local_grad_kernel.1.refs_2_), custom_call_target="tpu_custom_call" | custom-call | flops 100000000 | bytes 2080768 | tf_op jit(solution)/shard_map/finish_kernel/pallas_call | solution.py:579
Async XLA Ops:
  3.9 14.9 %all-to-all-start = ((bf16[32,8,128]{2,1,0:T(8,128)(2,1)}), bf16[32,8,128]{2,1,0:T(8,128)(2,1)S(1)}, u32[]{:S(2)}, u32[]{:S(2)}) async-start(bf16[32,8,128]{2,1,0:T(8,128)(2,1)} %bitcast.30), calls=%async_computation | async-start | bytes 131072 | tf_op jit(solution)/shard_map/all_to_all | solution.py:596
  11.2 14.8 %collective-permute-start = (bf16[512,128]{1,0:T(8,128)(2,1)}, bf16[512,128]{1,0:T(8,128)(2,1)S(1)}, u32[]{:S(2)}, u32[]{:S(2)}) collective-permute-start(bf16[512,128]{1,0:T(8,128)(2,1)} %get-tuple-element.36), channel_id=1, source_target_pairs={{0,1},{1,2},{2,3},{3,4},{4,5},{5,6},{6,7},{7,8},{8,9},{9,10},{10,1... | collective-permute-start | bytes 393224 | tf_op jit(solution)/shard_map/ppermute | solution.py:601
  13.3 12.7 %collective-permute-start.1 = (bf16[512,128]{1,0:T(8,128)(2,1)}, bf16[512,128]{1,0:T(8,128)(2,1)S(1)}, u32[]{:S(2)}, u32[]{:S(2)}) collective-permute-start(bf16[512,128]{1,0:T(8,128)(2,1)} %get-tuple-element.37), channel_id=1, source_target_pairs={{1,0},{2,1},{3,2},{4,3},{5,4},{6,5},{7,6},{8,7},{9,8},{10,9},{11,1... | collective-permute-start | bytes 393224 | tf_op jit(solution)/shard_map/ppermute | solution.py:602
  14.6 4.1 %copy-start.4 = (bf16[128,384]{1,0:T(8,128)(2,1)S(1)}, bf16[128,384]{1,0:T(8,128)(2,1)}, u32[]{:S(2)}) copy-start(bf16[128,384]{1,0:T(8,128)(2,1)} %constant.16.clone.refs_3_) | copy-start | bytes 294916
  14.7 4.1 %copy-start.5 = (bf16[192,256]{1,0:T(8,128)(2,1)S(1)}, bf16[192,256]{1,0:T(8,128)(2,1)}, u32[]{:S(2)}) copy-start(bf16[192,256]{1,0:T(8,128)(2,1)} %constant.15.clone.refs_1_) | copy-start | bytes 294916
  14.7 11.3 %copy-start.1 = (bf16[3,3,3,64,64]{4,3,2,1,0:T(8,128)(2,1)S(1)}, bf16[3,3,3,64,64]{4,3,2,1,0:T(8,128)(2,1)}, u32[]{:S(2)}) copy-start(bf16[3,3,3,64,64]{4,3,2,1,0:T(8,128)(2,1)} %param.14) | copy-start | bytes 663556
  14.7 11.3 %copy-start.6 = (bf16[1,64,2,1024]{3,2,1,0:T(2,128)(2,1)S(1)}, bf16[1,64,2,1024]{3,2,1,0:T(2,128)(2,1)}, u32[]{:S(2)}) copy-start(bf16[1,64,2,1024]{3,2,1,0:T(2,128)(2,1)} %param.12) | copy-start | bytes 786436
  14.7 11.3 %copy-start.7 = (bf16[1024,128]{1,0:T(8,128)(2,1)S(1)}, bf16[1024,128]{1,0:T(8,128)(2,1)}, u32[]{:S(2)}) copy-start(bf16[1024,128]{1,0:T(8,128)(2,1)} %get-tuple-element.35.refs_0_) | copy-start | bytes 786436
  20.6 13.0 %all-to-all-start.1 = ((bf16[32,8,128]{2,1,0:T(8,128)(2,1)}), bf16[32,8,128]{2,1,0:T(8,128)(2,1)S(1)}, u32[]{:S(2)}, u32[]{:S(2)}) async-start(bf16[32,8,128]{2,1,0:T(8,128)(2,1)} %bitcast.4), calls=%async_computation.1 | async-start | bytes 131072 | tf_op jit(solution)/shard_map/all_to_all | solution.py:596
  26.0 7.6 %copy-start.8 = (bf16[1024,256]{1,0:T(8,128)(2,1)S(1)}, bf16[1024,256]{1,0:T(8,128)(2,1)}, u32[]{:S(2)}) copy-start(bf16[1024,256]{1,0:T(8,128)(2,1)} %constant.17.clone.refs_1_) | copy-start | bytes 1572868
  36.2 14.3 %all-to-all-start.2 = ((bf16[32,40,128]{2,1,0:T(8,128)(2,1)}), bf16[32,40,128]{2,1,0:T(8,128)(2,1)S(1)}, u32[]{:S(2)}, u32[]{:S(2)}) async-start(bf16[32,40,128]{2,1,0:T(8,128)(2,1)} %bitcast.8), calls=%async_computation.2 | async-start | bytes 655360 | tf_op jit(solution)/shard_map/all_to_all | solution.py:596
  38.9 5.6 %collective-permute-start.2 = (bf16[512,128]{1,0:T(8,128)(2,1)S(1)}, bf16[512,128]{1,0:T(8,128)(2,1)S(1)}, u32[]{:S(2)}, u32[]{:S(2)}) collective-permute-start(bf16[512,128]{1,0:T(8,128)(2,1)S(1)} %get-tuple-element.42), channel_id=1, source_target_pairs={{0,1},{1,2},{2,3},{3,4},{4,5},{5,6},{6,7},{7,8},{8,9},{9,10},{10,1... | collective-permute-start | bytes 393224 | tf_op jit(solution)/shard_map/ppermute | solution.py:601
  40.9 4.4 %collective-permute-start.3 = (bf16[512,128]{1,0:T(8,128)(2,1)S(1)}, bf16[512,128]{1,0:T(8,128)(2,1)S(1)}, u32[]{:S(2)}, u32[]{:S(2)}) collective-permute-start(bf16[512,128]{1,0:T(8,128)(2,1)S(1)} %get-tuple-element.43), channel_id=1, source_target_pairs={{1,0},{2,1},{3,2},{4,3},{5,4},{6,5},{7,6},{8,7},{9,8},{10,9},{11,1... | collective-permute-start | bytes 393224 | tf_op jit(solution)/shard_map/ppermute | solution.py:602
  42.2 8.4 %copy-start.2 = (bf16[128,384]{1,0:T(8,128)(2,1)S(1)}, bf16[128,384]{1,0:T(8,128)(2,1)}, u32[]{:S(2)}) copy-start(bf16[128,384]{1,0:T(8,128)(2,1)} %constant.19.clone.refs_3_) | copy-start | bytes 294916
  42.2 8.4 %copy-start.3 = (bf16[192,256]{1,0:T(8,128)(2,1)S(1)}, bf16[192,256]{1,0:T(8,128)(2,1)}, u32[]{:S(2)}) copy-start(bf16[192,256]{1,0:T(8,128)(2,1)} %constant.18.clone.refs_1_) | copy-start | bytes 294916
  52.4 15.2 %all-to-all-start.3 = ((bf16[32,40,128]{2,1,0:T(8,128)(2,1)}), bf16[32,40,128]{2,1,0:T(8,128)(2,1)S(1)}, u32[]{:S(2)}, u32[]{:S(2)}) async-start(bf16[32,40,128]{2,1,0:T(8,128)(2,1)} %bitcast.11), calls=%async_computation.3 | async-start | bytes 655360 | tf_op jit(solution)/shard_map/all_to_all | solution.py:596
  59.6 8.0 %copy-start = (bf16[1024,256]{1,0:T(8,128)(2,1)S(1)}, bf16[1024,256]{1,0:T(8,128)(2,1)}, u32[]{:S(2)}) copy-start(bf16[1024,256]{1,0:T(8,128)(2,1)} %constant.20.clone.refs_1_) | copy-start | bytes 1572868

commit v24 on v23

--- a/solution.py
+++ b/solution.py
@@ -20,7 +20,7 @@
 GROUP = 8
 OFFSETS = 27
 TERM_ROWS = 1024
-CHUNKS = 3
+CHUNKS = 6
 VMEM_BYTES = 40 * 1024 * 1024
 WHOLE_VMEM = 65000 * 1024
 HBM_BYTES = 100 * 1024 * 256
@@ -205,9 +205,9 @@
                     )
 
 
-def analyse_kernel(field, analysis, *refs):
-    weights = refs[:CHUNKS]
-    cells_out, coef_out, first_out, last_out, packed_out, _, buffer, semaphores = refs[CHUNKS:]
+def analyse_kernel(chunks, field, analysis, *refs):
+    weights = refs[:chunks]
+    cells_out, coef_out, first_out, last_out, packed_out, _, buffer, semaphores = refs[chunks:]
     cells = to_cells(field[...])
     rounded = cells.astype(BF16)
     coef_out[...] = dot(analysis[...], rounded).astype(BF16)
@@ -216,7 +216,7 @@
     first_out[...] = first
     last_out[...] = last
     rows = GROUP * LANES // 4
-    share = buffer.shape[0] // CHUNKS
+    share = buffer.shape[0] // chunks
     copies = []
     for place, part in enumerate(weights):
         for g in range(share // rows):
@@ -629,9 +629,10 @@
         return exchange(values.reshape(devices, modes, LANES)).reshape(plane_rows, LANES)
 
     packed = shape((weights.shape[0] // 2, LANES), BF16)
-    share = weights.shape[0] // CHUNKS
+    chunks = math.gcd(CHUNKS, weights.shape[0] // (GROUP * channels))
+    share = weights.shape[0] // chunks
     cells, coef, first, last, kept_weights, slot = run(
-        analyse_kernel,
+        functools.partial(analyse_kernel, chunks),
         [
             wide,
             plane_modes,
@@ -642,11 +643,11 @@
         ],
         snapshots.reshape(field.shape),
         analysis,
-        *[weights] * CHUNKS,
-        staged={0: None, 1: None} | {2 + k: slice(k * share, (k + 1) * share) for k in range(CHUNKS)},
+        *[weights] * chunks,
+        staged={0: None, 1: None} | {2 + k: slice(k * share, (k + 1) * share) for k in range(chunks)},
         sent=(0, 1, 2, 3),
         plain=(4, 5),
-        scratch=[pltpu.VMEM(packed.shape, BF16), pltpu.SemaphoreType.DMA((CHUNKS,))],
+        scratch=[pltpu.VMEM(packed.shape, BF16), pltpu.SemaphoreType.DMA((chunks,))],
         limit=WHOLE_VMEM,
         flops=10**8,
     )

time: 69.6 us -> 69.7 us (level)
  no operation moved by 1% of the time
where the time goes in v24:
time: 69.7 us; the launch traced here: 69.2 us
  starting transfers between devices  25.6 us (37%)
  Pallas kernels  21.7 us (31%)
  waiting for transfers between devices  21 us (30%)
  between operations  0.87 us (1%)
    pallas_call x10, Pallas kernels, run(): pl.pallas_call(kernel, out_shape=results, in_specs=[in_hbm if k in staged...  21.7 us
    all_to_all x4, waiting for transfers between devices, exchange(): lax.all_to_all(values, ('space', 'batch'), split_axis=0, concat_axis=0, t...  20.1 us
    all_to_all x4, starting transfers between devices, exchange(): lax.all_to_all(values, ('space', 'batch'), split_axis=0, concat_axis=0, t...  18.8 us
    ppermute x2, starting transfers between devices, neighbours(): before = lax.ppermute(last, 'space', [(i, i + 1) for i in range(ends)])  4.19 us
    ppermute x2, starting transfers between devices, neighbours(): after = lax.ppermute(first, 'space', [(i + 1, i) for i in range(ends)])  2.58 us
  transfers between devices with their start and end apart: 8, of which 5 were waited for; matrix products, arithmetic and copies ran while one was open for 0% of the time, Pallas kernels for 18%

profile of v24, /device:TPU:0, one launch (start us, length us, event | category | flops | bytes accessed | tf_op | source)
XLA Modules:
  0.0 69.2 jit_solution(1062806151298664201)
XLA Ops:
  0.6 3.3 %analyse_kernel.1 = (bf16[1024,128]{1,0:T(8,128)(2,1)}, bf16[256,128]{1,0:T(8,128)(2,1)}, bf16[512,128]{1,0:T(8,128)(2,1)}, bf16[512,128]{1,0:T(8,128)(2,1)}, bf...) custom-call(bf16[64,2,1024]{2,1,0:T(2,128)(2,1)} %bitcast.32, bf16[256,1024]{1,0:T(8,128)(2,1)} %constant.14.clone.refs_1_, ...), custom_call_target="tpu_custom_call" | custom-call | flops 100000000 | bytes 37093376 | tf_op jit(solution)/shard_map/analyse_kernel/pallas_call | solution.py:579
  4.0 7.3 %all-to-all-start = ((bf16[32,8,128]{2,1,0:T(8,128)(2,1)}), bf16[32,8,128]{2,1,0:T(8,128)(2,1)S(1)}, u32[]{:S(2)}, u32[]{:S(2)}) async-start(bf16[32,8,128]{2,1,0:T(8,128)(2,1)} %bitcast.33), calls=%async_computation | async-start | bytes 131072 | tf_op jit(solution)/shard_map/all_to_all | solution.py:596
  11.3 2.2 %collective-permute-start = (bf16[512,128]{1,0:T(8,128)(2,1)}, bf16[512,128]{1,0:T(8,128)(2,1)S(1)}, u32[]{:S(2)}, u32[]{:S(2)}) collective-permute-start(bf16[512,128]{1,0:T(8,128)(2,1)} %get-tuple-element.36), channel_id=1, source_target_pairs={{0,1},{1,2},{2,3},{3,4},{4,5},{5,6},{6,7},{7,8},{8,9},{9,10},{10,1... | collective-permute-start | bytes 393224 | tf_op jit(solution)/shard_map/ppermute | solution.py:601
  13.4 1.3 %collective-permute-start.1 = (bf16[512,128]{1,0:T(8,128)(2,1)}, bf16[512,128]{1,0:T(8,128)(2,1)S(1)}, u32[]{:S(2)}, u32[]{:S(2)}) collective-permute-start(bf16[512,128]{1,0:T(8,128)(2,1)} %get-tuple-element.37), channel_id=1, source_target_pairs={{1,0},{2,1},{3,2},{4,3},{5,4},{6,5},{7,6},{8,7},{9,8},{10,9},{11,1... | collective-permute-start | bytes 393224 | tf_op jit(solution)/shard_map/ppermute | solution.py:602
  14.7 0.0 copy-start.4
  14.7 0.0 copy-start.5
  14.8 0.0 copy-start.1
  14.8 0.0 copy-start.6
  14.8 0.0 copy-start.7
  14.8 1.5 %fetch_kernel.1.refs_2_ = bf16[6144,128]{1,0:T(8,128)(2,1)S(1)} custom-call(bf16[102400,128]{1,0:T(8,128)(2,1)} %get-tuple-element.32.refs_0_.refs_1_), custom_call_target="tpu_custom_call" | custom-call | bytes 27787264 | tf_op jit(solution)/shard_map/fetch_kernel/pallas_call | solution.py:579
  16.3 2.6 %all-to-all-done = bf16[32,8,128]{2,1,0:T(8,128)(2,1)S(1)} async-done(((bf16[32,8,128]{2,1,0:T(8,128)(2,1)}), bf16[32,8,128]{2,1,0:T(8,128)(2,1)S(1)}, u32[]{:S(2)}, u32[]{:S(2)}) %all-to-all-start) | async-done | bytes 65568 | tf_op jit(solution)/shard_map/all_to_all | solution.py:596
  18.9 0.0 copy-done.4
  18.9 0.0 copy-done.5
  18.9 1.8 %mix_kernel.1 = (bf16[256,128]{1,0:T(8,128)(2,1)}, bf16[384,256]{1,0:T(8,128)(2,1)S(1)}) custom-call(bf16[256,128]{1,0:T(8,128)(2,1)S(1)} %bitcast.22, bf16[192,256]{1,0:T(8,128)(2,1)S(1)} %copy-done.5, bf16[6144,128]{1,0:T(8,128)(2,1)S(1)} %fetch_kernel.1.refs_2_, bf16[128,384]{1,0:T(8,128)(2,1)S(1)} %copy-done.4, ...), custom_call_target="tpu_custom_call", output_to_operand_aliasing={{0}: (4, {})} | custom-call | flops 400000000 | bytes 2097152 | tf_op jit(solution)/shard_map/mix_kernel/pallas_call | solution.py:579
  20.7 5.4 %all-to-all-start.1 = ((bf16[32,8,128]{2,1,0:T(8,128)(2,1)}), bf16[32,8,128]{2,1,0:T(8,128)(2,1)S(1)}, u32[]{:S(2)}, u32[]{:S(2)}) async-start(bf16[32,8,128]{2,1,0:T(8,128)(2,1)} %bitcast.4), calls=%async_computation.1 | async-start | bytes 131072 | tf_op jit(solution)/shard_map/all_to_all | solution.py:596
  26.1 0.0 collective-permute-done.refs_1_
  26.1 0.0 collective-permute-done.1.refs_2_
  26.1 0.0 copy-done.1
  26.1 0.0 copy-done.6
  26.1 0.0 copy-done.7
  26.1 0.0 copy-start.8
  26.1 1.2 %local_kernel.1 = (f32[1024,128]{1,0:T(8,128)S(1)}, bf16[256,1024]{1,0:T(8,128)(2,1)S(1)}, bf16[1024,128]{1,0:T(8,128)(2,1)S(1)}) custom-call(bf16[1024,128]{1,0:T(8,128)(2,1)S(1)} %copy-done.7, bf16[512,128]{1,0:T(8,128)(2,1)S(1)} %collective-permute-done.refs_1_, bf16[512,128]{1,0:T(8,128)(2,1)S(1)} %collective-permute-done.1.refs_2_, ...), custom_call_target="tpu_custom_call" | custom-call | flops 8000000000 | bytes 2318336 | tf_op jit(solution)/shard_map/local_kernel/pallas_call | solution.py:579
  27.3 6.4 %all-to-all-done.1 = bf16[32,8,128]{2,1,0:T(8,128)(2,1)S(1)} async-done(((bf16[32,8,128]{2,1,0:T(8,128)(2,1)}), bf16[32,8,128]{2,1,0:T(8,128)(2,1)S(1)}, u32[]{:S(2)}, u32[]{:S(2)}) %all-to-all-start.1) | async-done | bytes 65568 | tf_op jit(solution)/shard_map/all_to_all | solution.py:596
  33.7 0.0 copy-done.8
  33.7 2.6 %activate_kernel.1 = (bf16[1024,128]{1,0:T(8,128)(2,1)S(1)}, bf16[102400,128]{1,0:T(8,128)(2,1)}, bf16[512,128]{1,0:T(8,128)(2,1)S(1)}, bf16[512,128]{1,0:T(8,128)(2,1)S(1)}, bf16[1280,128]{1,0:T(8,128)(2,1)}) custom-call(bf16[256,128]{1,0:T(8,128)(2,1)S(1)} %bitcast.23, bf16[1024,256]{1,0:T(8,128)(2,1)S(1)} %copy-done.8, ...), custom_call_target="tpu_custom_call" | custom-call | flops 1000000000 | bytes 28966912 | tf_op jit(solution)/shard_map/activate_kernel/pallas_call | solution.py:579
  36.3 2.6 %all-to-all-start.2 = ((bf16[32,40,128]{2,1,0:T(8,128)(2,1)}), bf16[32,40,128]{2,1,0:T(8,128)(2,1)S(1)}, u32[]{:S(2)}, u32[]{:S(2)}) async-start(bf16[32,40,128]{2,1,0:T(8,128)(2,1)} %bitcast.8), calls=%async_computation.2 | async-start | bytes 655360 | tf_op jit(solution)/shard_map/all_to_all | solution.py:596
  39.0 2.0 %collective-permute-start.2 = (bf16[512,128]{1,0:T(8,128)(2,1)S(1)}, bf16[512,128]{1,0:T(8,128)(2,1)S(1)}, u32[]{:S(2)}, u32[]{:S(2)}) collective-permute-start(bf16[512,128]{1,0:T(8,128)(2,1)S(1)} %get-tuple-element.42), channel_id=1, source_target_pairs={{0,1},{1,2},{2,3},{3,4},{4,5},{5,6},{6,7},{7,8},{8,9},{9,10},{10,1... | collective-permute-start | bytes 393224 | tf_op jit(solution)/shard_map/ppermute | solution.py:601
  41.0 1.3 %collective-permute-start.3 = (bf16[512,128]{1,0:T(8,128)(2,1)S(1)}, bf16[512,128]{1,0:T(8,128)(2,1)S(1)}, u32[]{:S(2)}, u32[]{:S(2)}) collective-permute-start(bf16[512,128]{1,0:T(8,128)(2,1)S(1)} %get-tuple-element.43), channel_id=1, source_target_pairs={{1,0},{2,1},{3,2},{4,3},{5,4},{6,5},{7,6},{8,7},{9,8},{10,9},{11,1... | collective-permute-start | bytes 393224 | tf_op jit(solution)/shard_map/ppermute | solution.py:602
  42.3 0.0 copy-start.2
  42.3 0.0 copy-start.3
  42.3 2.2 %output_kernel.1 = (bf16[64,2,1024]{2,1,0:T(2,128)(2,1)}, bf16[6144,128]{1,0:T(8,128)(2,1)S(1)}) custom-call(bf16[1024,128]{1,0:T(8,128)(2,1)S(1)} %get-tuple-element.44.refs_0_, bf16[102400,128]{1,0:T(8,128)(2,1)} %get-tuple-element.32.refs_0_.refs_1_), custom_call_target="tpu_custom_call" | custom-call | flops 100000000 | bytes 28311552 | tf_op jit(solution)/shard_map/output_kernel/pallas_call | solution.py:579
  44.5 0.0 collective-permute-done.2.refs_1_
  44.5 0.9 %collective-permute-done.3.refs_2_ = bf16[512,128]{1,0:T(8,128)(2,1)S(1)} collective-permute-done((bf16[512,128]{1,0:T(8,128)(2,1)S(1)}, bf16[512,128]{1,0:T(8,128)(2,1)S(1)}, u32[]{:S(2)}, u32[]{:S(2)}) %collective-permute-start.3) | collective-permute-done | bytes 131104 | tf_op jit(solution)/shard_map/ppermute | solution.py:602
  45.4 5.3 %all-to-all-done.2 = bf16[32,40,128]{2,1,0:T(8,128)(2,1)S(1)} async-done(((bf16[32,40,128]{2,1,0:T(8,128)(2,1)}), bf16[32,40,128]{2,1,0:T(8,128)(2,1)S(1)}, u32[]{:S(2)}, u32[]{:S(2)}) %all-to-all-start.2) | async-done | bytes 327712 | tf_op jit(solution)/shard_map/all_to_all | solution.py:596
  50.7 0.0 copy-done.2
  50.7 0.0 copy-done.3
  50.7 1.8 %unmix_kernel.1 = (bf16[1280,128]{1,0:T(8,128)(2,1)}, bf16[384,128]{1,0:T(8,128)(2,1)S(1)}) custom-call(bf16[1280,128]{1,0:T(8,128)(2,1)S(1)} %bitcast.19, bf16[192,256]{1,0:T(8,128)(2,1)S(1)} %copy-done.3, bf16[6144,128]{1,0:T(8,128)(2,1)S(1)} %get-tuple-element.49.refs_2_, bf16[128,384]{1,0:T(8,128)(2,1)S(1)} %copy-done.2), custom_call_target="tpu_custom_call" | custom-call | flops 400000000 | bytes 2523136 | tf_op jit(solution)/shard_map/unmix_kernel/pallas_call | solution.py:579
  52.5 3.5 %all-to-all-start.3 = ((bf16[32,40,128]{2,1,0:T(8,128)(2,1)}), bf16[32,40,128]{2,1,0:T(8,128)(2,1)S(1)}, u32[]{:S(2)}, u32[]{:S(2)}) async-start(bf16[32,40,128]{2,1,0:T(8,128)(2,1)} %bitcast.11), calls=%async_computation.3 | async-start | bytes 655360 | tf_op jit(solution)/shard_map/all_to_all | solution.py:596
  56.0 3.7 %weight_kernel.1 = f32[12288,64]{1,0:T(8,128)} custom-call(bf16[384,256]{1,0:T(8,128)(2,1)S(1)} %get-tuple-element.55.refs_0_, bf16[384,128]{1,0:T(8,128)(2,1)S(1)} %get-tuple-element.56.refs_1_), custom_call_target="tpu_custom_call" | custom-call | flops 400000000 | bytes 3440640 | tf_op jit(solution)/shard_map/weight_kernel/pallas_call | solution.py:579
  59.7 0.0 copy-start
  59.7 2.1 %local_grad_kernel.1.refs_2_ = f32[1024,128]{1,0:T(8,128)S(1)} custom-call(bf16[102400,128]{1,0:T(8,128)(2,1)} %get-tuple-element.51.refs_0_, bf16[512,128]{1,0:T(8,128)(2,1)S(1)} %collective-permute-done.2.refs_1_, bf16[512,128]{1,0:T(8,128)(2,1)S(1)} %collective-permute-done.3.refs_2_, bf16[27,64,64]{2,1,0:T(8,128)(2,1)S(1)} %bitcast.21), custom_call_target="tpu_custom_call" | custom-call | flops 700000000 | bytes 27222016 | tf_op jit(solution)/shard_map/local_grad_kernel/pallas_call | solution.py:579
  61.8 5.9 %all-to-all-done.3 = bf16[32,40,128]{2,1,0:T(8,128)(2,1)S(1)} async-done(((bf16[32,40,128]{2,1,0:T(8,128)(2,1)}), bf16[32,40,128]{2,1,0:T(8,128)(2,1)S(1)}, u32[]{:S(2)}, u32[]{:S(2)}) %all-to-all-start.3) | async-done | bytes 327712 | tf_op jit(solution)/shard_map/all_to_all | solution.py:596
  67.7 0.0 copy-done
  67.7 1.5 %finish_kernel.1 = (bf16[64,2,1024]{2,1,0:T(2,128)(2,1)}, f32[27,64,64]{2,1,0:T(8,128)}) custom-call(bf16[1280,128]{1,0:T(8,128)(2,1)S(1)} %bitcast.18, bf16[1024,256]{1,0:T(8,128)(2,1)S(1)} %copy-done, f32[1024,128]{1,0:T(8,128)S(1)} %local_grad_kernel.1.refs_2_), custom_call_target="tpu_custom_call" | custom-call | flops 100000000 | bytes 2080768 | tf_op jit(solution)/shard_map/finish_kernel/pallas_call | solution.py:579
Async XLA Ops:
  4.0 14.9 %all-to-all-start = ((bf16[32,8,128]{2,1,0:T(8,128)(2,1)}), bf16[32,8,128]{2,1,0:T(8,128)(2,1)S(1)}, u32[]{:S(2)}, u32[]{:S(2)}) async-start(bf16[32,8,128]{2,1,0:T(8,128)(2,1)} %bitcast.33), calls=%async_computation | async-start | bytes 131072 | tf_op jit(solution)/shard_map/all_to_all | solution.py:596
  11.3 14.8 %collective-permute-start = (bf16[512,128]{1,0:T(8,128)(2,1)}, bf16[512,128]{1,0:T(8,128)(2,1)S(1)}, u32[]{:S(2)}, u32[]{:S(2)}) collective-permute-start(bf16[512,128]{1,0:T(8,128)(2,1)} %get-tuple-element.36), channel_id=1, source_target_pairs={{0,1},{1,2},{2,3},{3,4},{4,5},{5,6},{6,7},{7,8},{8,9},{9,10},{10,1... | collective-permute-start | bytes 393224 | tf_op jit(solution)/shard_map/ppermute | solution.py:601
  13.4 12.7 %collective-permute-start.1 = (bf16[512,128]{1,0:T(8,128)(2,1)}, bf16[512,128]{1,0:T(8,128)(2,1)S(1)}, u32[]{:S(2)}, u32[]{:S(2)}) collective-permute-start(bf16[512,128]{1,0:T(8,128)(2,1)} %get-tuple-element.37), channel_id=1, source_target_pairs={{1,0},{2,1},{3,2},{4,3},{5,4},{6,5},{7,6},{8,7},{9,8},{10,9},{11,1... | collective-permute-start | bytes 393224 | tf_op jit(solution)/shard_map/ppermute | solution.py:602
  14.7 4.1 %copy-start.4 = (bf16[128,384]{1,0:T(8,128)(2,1)S(1)}, bf16[128,384]{1,0:T(8,128)(2,1)}, u32[]{:S(2)}) copy-start(bf16[128,384]{1,0:T(8,128)(2,1)} %constant.16.clone.refs_3_) | copy-start | bytes 294916
  14.7 4.1 %copy-start.5 = (bf16[192,256]{1,0:T(8,128)(2,1)S(1)}, bf16[192,256]{1,0:T(8,128)(2,1)}, u32[]{:S(2)}) copy-start(bf16[192,256]{1,0:T(8,128)(2,1)} %constant.15.clone.refs_1_) | copy-start | bytes 294916
  14.8 11.3 %copy-start.1 = (bf16[3,3,3,64,64]{4,3,2,1,0:T(8,128)(2,1)S(1)}, bf16[3,3,3,64,64]{4,3,2,1,0:T(8,128)(2,1)}, u32[]{:S(2)}) copy-start(bf16[3,3,3,64,64]{4,3,2,1,0:T(8,128)(2,1)} %param.14) | copy-start | bytes 663556
  14.8 11.3 %copy-start.6 = (bf16[1,64,2,1024]{3,2,1,0:T(2,128)(2,1)S(1)}, bf16[1,64,2,1024]{3,2,1,0:T(2,128)(2,1)}, u32[]{:S(2)}) copy-start(bf16[1,64,2,1024]{3,2,1,0:T(2,128)(2,1)} %param.12) | copy-start | bytes 786436
  14.8 11.3 %copy-start.7 = (bf16[1024,128]{1,0:T(8,128)(2,1)S(1)}, bf16[1024,128]{1,0:T(8,128)(2,1)}, u32[]{:S(2)}) copy-start(bf16[1024,128]{1,0:T(8,128)(2,1)} %get-tuple-element.35.refs_0_) | copy-start | bytes 786436
  20.7 13.0 %all-to-all-start.1 = ((bf16[32,8,128]{2,1,0:T(8,128)(2,1)}), bf16[32,8,128]{2,1,0:T(8,128)(2,1)S(1)}, u32[]{:S(2)}, u32[]{:S(2)}) async-start(bf16[32,8,128]{2,1,0:T(8,128)(2,1)} %bitcast.4), calls=%async_computation.1 | async-start | bytes 131072 | tf_op jit(solution)/shard_map/all_to_all | solution.py:596
  26.1 7.6 %copy-start.8 = (bf16[1024,256]{1,0:T(8,128)(2,1)S(1)}, bf16[1024,256]{1,0:T(8,128)(2,1)}, u32[]{:S(2)}) copy-start(bf16[1024,256]{1,0:T(8,128)(2,1)} %constant.17.clone.refs_1_) | copy-start | bytes 1572868
  36.3 14.3 %all-to-all-start.2 = ((bf16[32,40,128]{2,1,0:T(8,128)(2,1)}), bf16[32,40,128]{2,1,0:T(8,128)(2,1)S(1)}, u32[]{:S(2)}, u32[]{:S(2)}) async-start(bf16[32,40,128]{2,1,0:T(8,128)(2,1)} %bitcast.8), calls=%async_computation.2 | async-start | bytes 655360 | tf_op jit(solution)/shard_map/all_to_all | solution.py:596
  39.0 5.6 %collective-permute-start.2 = (bf16[512,128]{1,0:T(8,128)(2,1)S(1)}, bf16[512,128]{1,0:T(8,128)(2,1)S(1)}, u32[]{:S(2)}, u32[]{:S(2)}) collective-permute-start(bf16[512,128]{1,0:T(8,128)(2,1)S(1)} %get-tuple-element.42), channel_id=1, source_target_pairs={{0,1},{1,2},{2,3},{3,4},{4,5},{5,6},{6,7},{7,8},{8,9},{9,10},{10,1... | collective-permute-start | bytes 393224 | tf_op jit(solution)/shard_map/ppermute | solution.py:601
  41.0 4.4 %collective-permute-start.3 = (bf16[512,128]{1,0:T(8,128)(2,1)S(1)}, bf16[512,128]{1,0:T(8,128)(2,1)S(1)}, u32[]{:S(2)}, u32[]{:S(2)}) collective-permute-start(bf16[512,128]{1,0:T(8,128)(2,1)S(1)} %get-tuple-element.43), channel_id=1, source_target_pairs={{1,0},{2,1},{3,2},{4,3},{5,4},{6,5},{7,6},{8,7},{9,8},{10,9},{11,1... | collective-permute-start | bytes 393224 | tf_op jit(solution)/shard_map/ppermute | solution.py:602
  42.3 8.4 %copy-start.2 = (bf16[128,384]{1,0:T(8,128)(2,1)S(1)}, bf16[128,384]{1,0:T(8,128)(2,1)}, u32[]{:S(2)}) copy-start(bf16[128,384]{1,0:T(8,128)(2,1)} %constant.19.clone.refs_3_) | copy-start | bytes 294916
  42.3 8.4 %copy-start.3 = (bf16[192,256]{1,0:T(8,128)(2,1)S(1)}, bf16[192,256]{1,0:T(8,128)(2,1)}, u32[]{:S(2)}) copy-start(bf16[192,256]{1,0:T(8,128)(2,1)} %constant.18.clone.refs_1_) | copy-start | bytes 294916
  52.5 15.2 %all-to-all-start.3 = ((bf16[32,40,128]{2,1,0:T(8,128)(2,1)}), bf16[32,40,128]{2,1,0:T(8,128)(2,1)S(1)}, u32[]{:S(2)}, u32[]{:S(2)}) async-start(bf16[32,40,128]{2,1,0:T(8,128)(2,1)} %bitcast.11), calls=%async_computation.3 | async-start | bytes 655360 | tf_op jit(solution)/shard_map/all_to_all | solution.py:596
  59.7 8.0 %copy-start = (bf16[1024,256]{1,0:T(8,128)(2,1)S(1)}, bf16[1024,256]{1,0:T(8,128)(2,1)}, u32[]{:S(2)}) copy-start(bf16[1024,256]{1,0:T(8,128)(2,1)} %constant.20.clone.refs_1_) | copy-start | bytes 1572868
